TPU v7x, 32 devices: a whole 2x2x4 slice. The times are simulated.
32 devices in a mesh: section: 4 (over z), expert: 4 (over y, core), dp: 2 (over x).
Axes of the slice: x: 2, y: 2, z: 4, core: 2. Of those that a mesh axis runs over, the one named last changes fastest.
Arguments:
- tokens: bfloat16 [4096, 5120], P(('section', 'expert', 'dp')), may hold values from -6 to 6
- cotangent: bfloat16 [4096, 5120], P(('section', 'expert', 'dp')), may hold values from -6 to 6
- w_gate: bfloat16 [4, 5120, 2048], P('section', None, 'expert'), may hold values from -0.078125 to 0.078125
- w_up: bfloat16 [4, 5120, 2048], P('section', None, 'expert'), may hold values from -0.078125 to 0.078125
- w_down: bfloat16 [4, 2048, 5120], P('section', 'expert'), may hold values from -0.125 to 0.125
- routes: int32 [2, 4096, 4], P(None, ('section', 'expert', 'dp')), may hold values from 0 to 63, as said below
- gates: float32 [2, 4096, 4], P(None, ('section', 'expert', 'dp')), may hold values from 0.2 to 1
Outputs:
- tokens_grad: bfloat16 [4096, 5120], P(('section', 'expert', 'dp'))
- final_state: bfloat16 [4096, 5120], P(('section', 'expert', 'dp'))
- gate_grad: bfloat16 [4, 5120, 2048], P('section', None, 'expert')
- up_grad: bfloat16 [4, 5120, 2048], P('section', None, 'expert')
- down_grad: bfloat16 [4, 2048, 5120], P('section', 'expert')
Inputs may be any that keep to these rules, and one draw needn't show every extreme that they name: `routes`: each row names 4 different experts. In each tick the 128 rows of one device name each expert below 1 in 1 to 10 rows, and for every tick and such expert all devices of some section and dp index name it in exactly 10 rows.
All inputs are finite; a program needn't handle non-finite values.
Results may differ from a plain program's by a relative error of at most 0.0095.
Values may be sent and summed in bfloat16 or wider, within the bound.
No kernel may reach another device: no remote copies, remote signals or barrier semaphores. Data moves between devices by JAX's collectives and lax.ppermute only.
A program may use at most 128 MiB of HBM per device.

v0:
```python
import jax
import jax.numpy as jnp
from jax import lax
from jax.sharding import PartitionSpec as P

EXP_W = 1
CAP = 10
TICKS = 2


EPSILON = 1e-06


def shifted(block, axis, distance):
    devices = range(lax.axis_size(axis))
    route = [((i - distance) % len(devices), i) for i in devices]
    return lax.ppermute(block, axis, route)


def routing(route_ids, gate_vals):
    experts_here = jnp.arange(EXP_W, dtype=jnp.int32)
    matches = route_ids[..., None, :, :] == experts_here[:, None, None]
    marked = jnp.any(matches, axis=-1)
    weights = jnp.sum(jnp.where(matches, gate_vals[..., None, :, :], 0.0), axis=-1)
    places = jnp.cumsum(marked.astype(jnp.int32), axis=-1, dtype=jnp.int32) - 1
    capacity = jnp.arange(CAP, dtype=jnp.int32)
    select = (places[..., None, :] == capacity[:, None]) & marked[..., None, :]
    return (select.astype(jnp.float32), weights)


def normalize(current):
    values = current.astype(jnp.float32)
    inv_rms = lax.rsqrt(jnp.mean(values * values, axis=-1, keepdims=True) + EPSILON)
    return (values, inv_rms, (values * inv_rms).astype(jnp.bfloat16))


def shards(tokens, cotangent, w_gate, w_up, w_down, routes, gates):
    gate_mat = w_gate[0]
    up_mat = w_up[0]
    down_mat = w_down[0]
    group_size = lax.axis_size("expert") // EXP_W
    current = tokens
    history = []
    stored = []
    for tick_index in range(TICKS):
        select, weights = routing(routes[tick_index], gates[tick_index])
        values, inv_rms, normed = normalize(current)
        select_half = select.astype(jnp.bfloat16)
        buffer = jnp.einsum(
            "jcr,rx->jcx", select_half, normed, preferred_element_type=jnp.float32
        ).astype(jnp.bfloat16)
        outgoing = jnp.repeat(buffer, group_size, axis=0)
        arrived = lax.all_to_all(outgoing, "expert", split_axis=0, concat_axis=0, tiled=True)
        expert_flat_rows = arrived.reshape(-1, arrived.shape[2])
        pre_gate = jnp.dot(expert_flat_rows, gate_mat, preferred_element_type=jnp.float32)
        pre_up = jnp.dot(expert_flat_rows, up_mat, preferred_element_type=jnp.float32)
        expert_gate_sig = jax.nn.sigmoid(pre_gate)
        expert_activated = (pre_gate * expert_gate_sig * pre_up).astype(jnp.bfloat16)
        partial_out = jnp.dot(
            expert_activated, down_mat, preferred_element_type=jnp.float32
        ).astype(jnp.bfloat16)
        partial_out = partial_out.reshape(arrived.shape)
        returned = lax.all_to_all(partial_out, "expert", split_axis=0, concat_axis=0, tiled=True)
        hidden_shape = (arrived.shape[0], arrived.shape[1], pre_gate.shape[1])
        returned, arrived, pre_gate, pre_up = (
            returned,
            arrived,
            pre_gate.reshape(hidden_shape),
            pre_up.reshape(hidden_shape),
        )
        summed = returned.reshape(EXP_W, group_size, CAP, -1).astype(jnp.float32).sum(axis=1)
        moved_back = jnp.einsum("jcr,jcx->jrx", select, summed, precision=lax.Precision.HIGHEST)
        updated = (values + jnp.sum(weights[:, :, None] * moved_back, axis=0)).astype(jnp.bfloat16)
        history.append((select, weights, values, inv_rms, normed))
        stored.append((arrived, pre_gate, pre_up))
        current = shifted(updated, "section", 1)
    total_gate = jnp.zeros(gate_mat.shape, jnp.float32)
    total_up = jnp.zeros(up_mat.shape, jnp.float32)
    total_down = jnp.zeros(down_mat.shape, jnp.float32)
    carried = cotangent
    for tick_index in reversed(range(TICKS)):
        carried = shifted(carried, "section", -1)
        select, weights, values, inv_rms, normed = history[tick_index]
        select_half = select.astype(jnp.bfloat16)
        scaled = (weights[:, :, None] * carried.astype(jnp.float32)[None]).astype(jnp.bfloat16)
        grad_buffer = jnp.einsum(
            "jcr,jrx->jcx", select_half, scaled, preferred_element_type=jnp.float32
        ).astype(jnp.bfloat16)
        grad_outgoing = jnp.repeat(grad_buffer, group_size, axis=0)
        buffer = jnp.einsum(
            "jcr,rx->jcx", select_half, normed, preferred_element_type=jnp.float32
        ).astype(jnp.bfloat16)
        arrived, grad_arrived = (
            lax.all_to_all(
                jnp.repeat(buffer, group_size, axis=0),
                "expert",
                split_axis=0,
                concat_axis=0,
                tiled=True,
            ),
            lax.all_to_all(grad_outgoing, "expert", split_axis=0, concat_axis=0, tiled=True),
        )
        flat_rows = arrived.reshape(-1, arrived.shape[2])
        pre_gate = jnp.dot(flat_rows, gate_mat, preferred_element_type=jnp.float32)
        pre_up = jnp.dot(flat_rows, up_mat, preferred_element_type=jnp.float32)
        grad_slots = grad_arrived.reshape(-1, grad_arrived.shape[2])
        gate_sig = jax.nn.sigmoid(pre_gate)
        silu_value = pre_gate * gate_sig
        activated = (silu_value * pre_up).astype(jnp.bfloat16)
        grad_act = jnp.einsum("sx,hx->sh", grad_slots, down_mat, preferred_element_type=jnp.float32)
        grad_gate = (grad_act * pre_up * gate_sig * (1.0 + pre_gate * (1.0 - gate_sig))).astype(
            jnp.bfloat16
        )
        grad_up = (grad_act * silu_value).astype(jnp.bfloat16)
        total_down = total_down + jnp.einsum(
            "sh,sx->hx", activated, grad_slots, preferred_element_type=jnp.float32
        )
        total_gate = total_gate + jnp.einsum(
            "sx,sh->xh", flat_rows, grad_gate, preferred_element_type=jnp.float32
        )
        total_up = total_up + jnp.einsum(
            "sx,sh->xh", flat_rows, grad_up, preferred_element_type=jnp.float32
        )
        back_share = jnp.einsum(
            "sh,xh->sx", grad_gate, gate_mat, preferred_element_type=jnp.float32
        )
        back_share = back_share + jnp.einsum(
            "sh,xh->sx", grad_up, up_mat, preferred_element_type=jnp.float32
        )
        back_share = back_share.astype(jnp.bfloat16).reshape(grad_arrived.shape)
        returned = lax.all_to_all(back_share, "expert", split_axis=0, concat_axis=0, tiled=True)
        summed = returned.reshape(EXP_W, group_size, CAP, -1).astype(jnp.float32).sum(axis=1)
        grad_norm = jnp.einsum("jcr,jcx->rx", select, summed, precision=lax.Precision.HIGHEST)
        inner = jnp.mean(grad_norm * values, axis=-1, keepdims=True)
        carried = (
            carried.astype(jnp.float32) + inv_rms * grad_norm - inv_rms**3 * values * inner
        ).astype(jnp.bfloat16)
    reduced = (
        lax.psum(total_gate.astype(jnp.bfloat16), "dp").astype(jnp.float32),
        lax.psum(total_up.astype(jnp.bfloat16), "dp").astype(jnp.float32),
        lax.psum(total_down.astype(jnp.bfloat16), "dp").astype(jnp.float32),
    )
    gate_out = reduced[0].astype(jnp.bfloat16)
    up_out = reduced[1].astype(jnp.bfloat16)
    down_out = reduced[2].astype(jnp.bfloat16)
    return (carried, current, gate_out[None], up_out[None], down_out[None])


def solution(mesh):
    return jax.shard_map(
        shards,
        mesh=mesh,
        in_specs=(
            P(("section", "expert", "dp"), None),
            P(("section", "expert", "dp"), None),
            P("section", None, "expert"),
            P("section", None, "expert"),
            P("section", "expert", None),
            P(None, ("section", "expert", "dp"), None),
            P(None, ("section", "expert", "dp"), None),
        ),
        out_specs=(
            P(("section", "expert", "dp"), None),
            P(("section", "expert", "dp"), None),
            P("section", None, "expert"),
            P("section", None, "expert"),
            P("section", "expert", None),
        ),
        check_vma=False,
    )
```

profile of v0, /device:TPU:0, one launch (start us, length us, event | category | flops | bytes accessed | tf_op | source)
XLA Modules:
  0.0 604.5 jit_solution(13398669955394330754)
XLA Ops:
  7.2 1.7 fusion.35
  8.8 0.5 multiply_multiply_fusion
  9.4 0.7 fusion.77
  10.1 0.7 select_reduce_fusion
  11.2 1.7 convolution_convert_fusion.5
  13.0 14.3 %all_to_all.42 = bf16[4,10,5120]{2,1,0:T(8,128)(2,1)S(1)} all-to-all(bf16[4,10,5120]{2,1,0:T(8,128)(2,1)S(1)} %reshape.381), channel_id=1, replica_groups=mesh['section'=4,'expert'=4,'dp'=2] {'expert'}, dimensions={0} | all-to-all | bytes 819200 | tf_op jit(solution)/shard_map/all_to_all | solution.py:53
  27.5 3.6 fusion.27
  31.1 4.1 multiply_convert_fusion.5
  35.3 1.0 convolution_convert_fusion.1
  36.3 1.0 reshape.383
  37.3 3.5 all-to-all-start.1
  40.8 3.7 collective-permute-start
  44.5 6.6 %all-to-all-done.1 = bf16[4,10,5120]{2,1,0:T(8,128)(2,1)S(1)} async-done(((bf16[4,10,5120]{2,1,0:T(8,128)(2,1)}), bf16[4,10,5120]{2,1,0:T(8,128)(2,1)S(1)}, u32[]{:S(2)}, u32[]{:S(2)}) %all-to-all-start.1) | async-done | bytes 409632 | tf_op jit(solution)/shard_map/all_to_all | solution.py:63
  51.1 2.4 fusion.6
  53.6 1.6 collective-permute-start.1
  55.6 18.4 %collective-permute-done = bf16[128,5120]{1,0:T(8,128)(2,1)} collective-permute-done((bf16[128,5120]{1,0:T(8,128)(2,1)}, bf16[128,5120]{1,0:T(8,128)(2,1)}, u32[]{:S(2)}, u32[]{:S(2)}) %collective-permute-start) | collective-permute-done | bytes 1310752 | tf_op jit(solution)/shard_map/ppermute | solution.py:17
  73.9 1.7 convolution_convert_fusion.4
  75.7 13.3 %all_to_all.43 = bf16[4,10,5120]{2,1,0:T(8,128)(2,1)S(1)} all-to-all(bf16[4,10,5120]{2,1,0:T(8,128)(2,1)S(1)} %reshape.384), channel_id=1, replica_groups=mesh['section'=4,'expert'=4,'dp'=2] {'expert'}, dimensions={0} | all-to-all | bytes 819200 | tf_op jit(solution)/shard_map/all_to_all | solution.py:101
  89.2 13.2 %collective-permute-done.1 = bf16[128,5120]{1,0:T(8,128)(2,1)} collective-permute-done((bf16[128,5120]{1,0:T(8,128)(2,1)}, bf16[128,5120]{1,0:T(8,128)(2,1)}, u32[]{:S(2)}, u32[]{:S(2)}) %collective-permute-start.1) | collective-permute-done | bytes 1310752 | tf_op jit(solution)/shard_map/ppermute | solution.py:17
  102.4 1.7 fusion.39
  104.1 1.7 convolution_convert_fusion.3
  105.8 0.9 reshape.386
  106.7 4.2 all-to-all-start.3
  110.9 4.2 fusion.12
  115.0 6.1 %all-to-all-done.3 = bf16[4,10,5120]{2,1,0:T(8,128)(2,1)} async-done(((bf16[4,10,5120]{2,1,0:T(8,128)(2,1)}), bf16[4,10,5120]{2,1,0:T(8,128)(2,1)}, u32[]{:S(2)}, u32[]{:S(2)}) %all-to-all-start.3) | async-done | bytes 409632 | tf_op jit(solution)/shard_map/all_to_all | solution.py:94
  121.2 1.3 reshape.387
  122.5 3.6 fusion.25
  126.2 3.8 multiply_convert_fusion
  130.0 1.6 fusion.23
  131.7 2.4 fusion.7
  134.1 1.2 reshape.388
  135.2 12.7 %all_to_all.44 = bf16[4,10,5120]{2,1,0:T(8,128)(2,1)S(1)} all-to-all(bf16[4,10,5120]{2,1,0:T(8,128)(2,1)S(1)} %reshape.388), channel_id=1, replica_groups=mesh['section'=4,'expert'=4,'dp'=2] {'expert'}, dimensions={0} | all-to-all | bytes 819200 | tf_op jit(solution)/shard_map/all_to_all | solution.py:131
  148.0 2.8 fusion.42
  150.8 2.7 fusion.31
  153.5 3.4 collective-permute-start.2
  156.9 5.4 fusion.79
  162.3 5.6 fusion.78
  167.9 16.7 %collective-permute-done.2 = bf16[128,5120]{1,0:T(8,128)(2,1)S(1)} collective-permute-done((bf16[128,5120]{1,0:T(8,128)(2,1)S(1)}, bf16[128,5120]{1,0:T(8,128)(2,1)S(1)}, u32[]{:S(2)}, u32[]{:S(2)}) %collective-permute-start.2) | collective-permute-done | bytes 1310752 | tf_op jit(solution)/shard_map/ppermute | solution.py:17
  184.6 1.1 copy-done.2
  186.1 0.9 reshape.389
  186.9 3.5 all-to-all-start.5
  190.5 5.5 fusion.80
  196.0 4.6 all-to-all-done.5
  200.8 4.2 multiply_convert_fusion.1
  205.0 8.0 %fusion.2 = bf16[1,512,5120]{2,1,0:T(8,128)(2,1)} fusion(f32[512,5120]{1,0:T(8,128)} %fusion.80, bf16[40,512]{1,0:T(8,128)(2,1)S(1)} %get-tuple-element.22, bf16[40,5120]{1,0:T(8,128)(2,1)S(1)} %reshape.390), kind=kOutput, calls=%fused_computation.5 | convolution fusion | flops 214958080 | bytes 16179200 | tf_op jit(solution)/shard_map/sh,sx->hx/dot_general | solution.py:115
  213.1 8.1 %fusion.1 = bf16[1,5120,512]{2,1,0:T(8,128)(2,1)} fusion(f32[5120,512]{1,0:T(8,128)} %fusion.79, bf16[40,5120]{1,0:T(8,128)(2,1)S(1)} %reshape.382, bf16[40,512]{1,0:T(8,128)(2,1)S(1)} %get-tuple-element.16), kind=kOutput, calls=%fused_computation.4 | convolution fusion | flops 214958080 | bytes 16179200 | tf_op jit(solution)/shard_map/sx,sh->xh/dot_general | solution.py:121
  221.2 3.9 fusion
  225.1 3.6 convolution_convert_fusion
  228.9 12.7 %all_to_all.45 = bf16[4,10,5120]{2,1,0:T(8,128)(2,1)S(1)} all-to-all(bf16[4,10,5120]{2,1,0:T(8,128)(2,1)S(1)} %reshape.392), channel_id=1, replica_groups=mesh['section'=4,'expert'=4,'dp'=2] {'expert'}, dimensions={0} | all-to-all | bytes 819200 | tf_op jit(solution)/shard_map/all_to_all | solution.py:63
  241.7 3.9 fusion.5
  245.6 0.7 collective-permute-start.3
  246.4 4.2 fusion.21
  250.6 1.6 fusion.8
  252.3 1.0 reshape.391
  253.3 3.7 all-to-all-start.6
  257.0 22.0 %collective-permute-done.3 = bf16[128,5120]{1,0:T(8,128)(2,1)} collective-permute-done((bf16[128,5120]{1,0:T(8,128)(2,1)}, bf16[128,5120]{1,0:T(8,128)(2,1)}, u32[]{:S(2)}, u32[]{:S(2)}) %collective-permute-start.3) | collective-permute-done | bytes 1310752 | tf_op jit(solution)/shard_map/ppermute | solution.py:17
  279.2 1.4 fusion.38
  280.6 3.4 fusion.34
  284.0 299.4 %all-reduce.3.cloned.1.call-done = (bf16[1,5120,512]{2,1,0:T(8,128)(2,1)}, bf16[1,5120,512]{2,1,0:T(8,128)(2,1)}, bf16[1,512,5120]{2,1,0:T(8,128)(2,1)}) async-done(((bf16[1,5120,512]{2,1,0:T(8,128)(2,1)}, bf16[1,5120,512]{2,1,0:T(8,128)(2,1)}, bf16[1,512,5120]{2,1,0:T(8,128)(2,1)}), (bf16[1,5120,512]{2,1,0:T(8,128)(2,1)}, bf16[1,5120,512]{2,1,0:T(8,128)(2,1)}, ...) | async-done | bytes 15728656 | tf_op jit(solution)/shard_map/psum | solution.py:139
  583.4 2.5 copy.20
  585.8 5.7 copy.21
  591.5 2.7 copy.22
  594.3 1.0 slice-done.12
  595.3 2.4 copy.23
  (86 shorter events, 2.8 us)
Async XLA Ops:
  9.4 21.8 %copy-start.12 = (f32[128]{0:T(128)}, f32[128]{0:T(128)S(1)}, u32[]{:S(2)}) copy-start(f32[128]{0:T(128)S(1)} %get-tuple-element.19) | copy-start | bytes 1540
  10.1 138.0 %copy-start.6 = (pred[128]{0:T(512)(128)(4,1)}, pred[128]{0:T(512)(128)(4,1)S(1)}, u32[]{:S(2)}) copy-start(pred[128]{0:T(512)(128)(4,1)S(1)} %get-tuple-element.10) | copy-start | bytes 388
  10.8 63.1 %copy-start.10 = (f32[128]{0:T(128)}, f32[128]{0:T(128)S(1)}, u32[]{:S(2)}) copy-start(f32[128]{0:T(128)S(1)} %get-tuple-element.5) | copy-start | bytes 1540
  10.8 173.8 %copy-start.8 = (pred[128]{0:T(512)(128)(4,1)}, pred[128]{0:T(512)(128)(4,1)S(1)}, u32[]{:S(2)}) copy-start(pred[128]{0:T(512)(128)(4,1)S(1)} %reduce_or.18) | copy-start | bytes 388
  27.3 8.0 %slice-start = ((s8[5242880]{0:T(1024)(128)(4,1)}), s8[1048576]{0:T(1024)(128)(4,1)S(1)}, s32[]{:S(2)}) async-start(s8[5242880]{0:T(1024)(128)(4,1)} %bitcast.71), calls=%async_computation.9 | async-start | bytes 2097152
  27.5 7.8 %slice-start.1 = ((s8[5242880]{0:T(1024)(128)(4,1)}), s8[4194304]{0:T(1024)(128)(4,1)S(1)}, s32[]{:S(2)}) async-start(s8[5242880]{0:T(1024)(128)(4,1)} %bitcast.71), calls=%async_computation.10 | async-start | bytes 8388608
  36.3 14.8 %copy-start = (bf16[128,5120]{1,0:T(8,128)(2,1)S(1)}, bf16[128,5120]{1,0:T(8,128)(2,1)}, u32[]{:S(2)}) copy-start(bf16[128,5120]{1,0:T(8,128)(2,1)} %param.7) | copy-start | bytes 3932164
  37.3 13.7 %all-to-all-start.1 = ((bf16[4,10,5120]{2,1,0:T(8,128)(2,1)}), bf16[4,10,5120]{2,1,0:T(8,128)(2,1)S(1)}, u32[]{:S(2)}, u32[]{:S(2)}) async-start(bf16[4,10,5120]{2,1,0:T(8,128)(2,1)} %reshape.383), calls=%async_computation.1 | async-start | bytes 1310720 | tf_op jit(solution)/shard_map/all_to_all | solution.py:63
  40.8 33.1 %collective-permute-start = (bf16[128,5120]{1,0:T(8,128)(2,1)}, bf16[128,5120]{1,0:T(8,128)(2,1)}, u32[]{:S(2)}, u32[]{:S(2)}) collective-permute-start(bf16[128,5120]{1,0:T(8,128)(2,1)} %param.8), channel_id=1, source_target_pairs={{8,0},{16,8},{24,16},{0,24},{9,1},{17,9},{25,17},{1,25},{10,2},{18... | collective-permute-start | bytes 3932168 | tf_op jit(solution)/shard_map/ppermute | solution.py:17
  53.6 48.8 %collective-permute-start.1 = (bf16[128,5120]{1,0:T(8,128)(2,1)}, bf16[128,5120]{1,0:T(8,128)(2,1)}, u32[]{:S(2)}, u32[]{:S(2)}) collective-permute-start(bf16[128,5120]{1,0:T(8,128)(2,1)} %fusion.6), channel_id=1, source_target_pairs={{24,0},{0,8},{8,16},{16,24},{25,1},{1,9},{9,17},{17,25},{26,2},{2,... | collective-permute-start | bytes 3932168 | tf_op jit(solution)/shard_map/ppermute | solution.py:17
  89.2 25.9 %copy-start.3 = (bf16[40,5120]{1,0:T(8,128)(2,1)}, bf16[40,5120]{1,0:T(8,128)(2,1)S(1)}, u32[]{:S(2)}) copy-start(bf16[40,5120]{1,0:T(8,128)(2,1)S(1)} %reshape.385) | copy-start | bytes 1228804
  106.7 14.5 %all-to-all-start.3 = ((bf16[4,10,5120]{2,1,0:T(8,128)(2,1)}), bf16[4,10,5120]{2,1,0:T(8,128)(2,1)}, u32[]{:S(2)}, u32[]{:S(2)}) async-start(bf16[4,10,5120]{2,1,0:T(8,128)(2,1)} %reshape.386), calls=%async_computation.3 | async-start | bytes 1310720 | tf_op jit(solution)/shard_map/all_to_all | solution.py:94
  121.2 8.8 %slice-start.2 = ((s8[5242880]{0:T(1024)(128)(4,1)}), s8[1048576]{0:T(1024)(128)(4,1)S(1)}, s32[]{:S(2)}) async-start(s8[5242880]{0:T(1024)(128)(4,1)} %bitcast.73), calls=%async_computation.11 | async-start | bytes 2097152
  122.5 7.5 %slice-start.3 = ((s8[5242880]{0:T(1024)(128)(4,1)}), s8[4194304]{0:T(1024)(128)(4,1)S(1)}, s32[]{:S(2)}) async-start(s8[5242880]{0:T(1024)(128)(4,1)} %bitcast.73), calls=%async_computation.12 | async-start | bytes 8388608
  122.5 9.1 %slice-start.4 = ((s8[5242880]{0:T(1024)(128)(4,1)}), s8[4194304]{0:T(1024)(128)(4,1)S(1)}, s32[]{:S(2)}) async-start(s8[5242880]{0:T(1024)(128)(4,1)} %bitcast.75), calls=%async_computation.13 | async-start | bytes 8388608
  126.2 5.5 slice-start.5
  153.5 31.1 %collective-permute-start.2 = (bf16[128,5120]{1,0:T(8,128)(2,1)S(1)}, bf16[128,5120]{1,0:T(8,128)(2,1)S(1)}, u32[]{:S(2)}, u32[]{:S(2)}) collective-permute-start(bf16[128,5120]{1,0:T(8,128)(2,1)S(1)} %fusion.31), channel_id=1, source_target_pairs={{8,0},{16,8},{24,16},{0,24},{9,1},{17,9},{25,17},{1,25},{10,2},{18... | collective-permute-start | bytes 3932168 | tf_op jit(solution)/shard_map/ppermute | solution.py:17
  167.9 22.6 %copy-start.4 = (bf16[40,5120]{1,0:T(8,128)(2,1)S(1)}, bf16[40,5120]{1,0:T(8,128)(2,1)}, u32[]{:S(2)}) copy-start(bf16[40,5120]{1,0:T(8,128)(2,1)} %copy-done.3) | copy-start | bytes 1228804
  184.6 1.1 copy-start.2
  186.9 13.7 %all-to-all-start.5 = ((bf16[4,10,5120]{2,1,0:T(8,128)(2,1)}), bf16[4,10,5120]{2,1,0:T(8,128)(2,1)S(1)}, u32[]{:S(2)}, u32[]{:S(2)}) async-start(bf16[4,10,5120]{2,1,0:T(8,128)(2,1)} %reshape.389), calls=%async_computation.5 | async-start | bytes 1310720 | tf_op jit(solution)/shard_map/all_to_all | solution.py:101
  190.4 392.9 %all-reduce.3.cloned.1.call-start = ((), (), s32[]{:S(2)}) async-start(), calls=%async_computation.8 | async-start | bytes 31457280 | tf_op jit(solution)/shard_map/psum | solution.py:139
  190.5 10.3 %copy-start.5 = (f32[40,512]{1,0:T(8,128)S(1)}, f32[40,512]{1,0:T(8,128)}, u32[]{:S(2)}) copy-start(f32[40,512]{1,0:T(8,128)} %get-tuple-element.23) | copy-start | bytes 245764
  205.0 16.1 %slice-start.8 = ((s8[10485760]{0:T(1024)(128)(4,1)}), s8[4194304]{0:T(1024)(128)(4,1)S(1)}, s32[]{:S(2)}) async-start(s8[10485760]{0:T(1024)(128)(4,1)} %bitcast.79), calls=%async_computation.17 | async-start | bytes 8388608
  205.0 16.1 %slice-start.9 = ((s8[10485760]{0:T(1024)(128)(4,1)}), s8[4194304]{0:T(1024)(128)(4,1)S(1)}, s32[]{:S(2)}) async-start(s8[10485760]{0:T(1024)(128)(4,1)} %bitcast.79), calls=%async_computation.18 | async-start | bytes 8388608
  213.1 8.1 %slice-start.10 = ((s8[10485760]{0:T(1024)(128)(4,1)}), s8[2097152]{0:T(1024)(128)(4,1)S(1)}, s32[]{:S(2)}) async-start(s8[10485760]{0:T(1024)(128)(4,1)} %bitcast.79), calls=%async_computation.19 | async-start | bytes 4194304
  225.1 25.5 %slice-start.6 = ((s8[5242880]{0:T(1024)(128)(4,1)}), s8[1048576]{0:T(1024)(128)(4,1)S(1)}, s32[]{:S(2)}) async-start(s8[5242880]{0:T(1024)(128)(4,1)} %bitcast.77), calls=%async_computation.15 | async-start | bytes 2097152
  228.7 13.0 %copy-start.7 = (pred[128]{0:T(512)(128)(4,1)S(1)}, pred[128]{0:T(512)(128)(4,1)}, u32[]{:S(2)}) copy-start(pred[128]{0:T(512)(128)(4,1)} %copy-done.6) | copy-start | bytes 388
  228.7 13.0 %copy-start.11 = (f32[128]{0:T(128)S(1)}, f32[128]{0:T(128)}, u32[]{:S(2)}) copy-start(f32[128]{0:T(128)} %copy-done.10) | copy-start | bytes 1540
  241.7 8.9 %slice-start.7 = ((s8[5242880]{0:T(1024)(128)(4,1)}), s8[4194304]{0:T(1024)(128)(4,1)S(1)}, s32[]{:S(2)}) async-start(s8[5242880]{0:T(1024)(128)(4,1)} %bitcast.77), calls=%async_computation.16 | async-start | bytes 8388608
  245.6 33.4 %collective-permute-start.3 = (bf16[128,5120]{1,0:T(8,128)(2,1)}, bf16[128,5120]{1,0:T(8,128)(2,1)}, u32[]{:S(2)}, u32[]{:S(2)}) collective-permute-start(bf16[128,5120]{1,0:T(8,128)(2,1)} %fusion.5), channel_id=1, source_target_pairs={{24,0},{0,8},{8,16},{16,24},{25,1},{1,9},{9,17},{17,25},{26,2},{2,... | collective-permute-start | bytes 3932168 | tf_op jit(solution)/shard_map/ppermute | solution.py:17
  252.2 26.9 %copy-start.9 = (pred[128]{0:T(512)(128)(4,1)S(1)}, pred[128]{0:T(512)(128)(4,1)}, u32[]{:S(2)}) copy-start(pred[128]{0:T(512)(128)(4,1)} %copy-done.8) | copy-start | bytes 388
  253.3 25.8 %all-to-all-start.6 = ((bf16[4,10,5120]{2,1,0:T(8,128)(2,1)}), bf16[4,10,5120]{2,1,0:T(8,128)(2,1)S(1)}, u32[]{:S(2)}, u32[]{:S(2)}) async-start(bf16[4,10,5120]{2,1,0:T(8,128)(2,1)} %reshape.391), calls=%async_computation.6 | async-start | bytes 1310720 | tf_op jit(solution)/shard_map/all_to_all | solution.py:131
  257.0 23.7 %copy-start.13 = (f32[128]{0:T(128)S(1)}, f32[128]{0:T(128)}, u32[]{:S(2)}) copy-start(f32[128]{0:T(128)} %copy-done.12) | copy-start | bytes 1540
  257.0 23.7 %copy-start.14 = (f32[128]{0:T(128)S(1)}, f32[128]{0:T(128)}, u32[]{:S(2)}) copy-start(f32[128]{0:T(128)} %get-tuple-element.18) | copy-start | bytes 1540
  585.8 5.7 copy-start.1
  585.8 8.5 %slice-start.11 = ((s8[5242880]{0:T(1024)(128)(4,1)}), s8[4194304]{0:T(1024)(128)(4,1)S(1)}, s32[]{:S(2)}) async-start(s8[5242880]{0:T(1024)(128)(4,1)} %bitcast.81), calls=%async_computation.20 | async-start | bytes 8388608
  591.5 3.8 slice-start.12
Sparse Core Ops, SparseCore 0:
  225.2 358.0 all-reduce.2
where the time goes:
time: 606 us; the launch traced here: 604 us
  waiting for transfers between devices  387 us (64%)
  matrix products  90.7 us (15%)
  blocking collectives  52.9 us (9%)
  starting transfers between devices  24.3 us (4%)
  local copies, waits for them, and re-layouts  22.7 us (4%)
  between operations  14.5 us (2%)
  other arithmetic  12.4 us (2%)
    psum x1, waiting for transfers between devices, shards(): lax.psum(total_gate.astype(jnp.bfloat16), 'dp').astype(jnp.float32)  299 us
    ppermute x4, waiting for transfers between devices, shifted(): return lax.ppermute(block, axis, route)  70.3 us
    unnamed x60, local copies, waits for them, and re-layouts  15.5 us
    all_to_all x1, blocking collectives, shards(): lax.all_to_all(outgoing, 'expert', split_axis=0, concat_axis=0, tiled=True)  14.3 us
    dot_general x2, matrix products, shards(): jnp.einsum('sh,sx->hx', activated, grad_slots, preferred_element_type=jnp...  13.6 us
    dot_general x2, matrix products, shards(): jnp.einsum('sx,sh->xh', flat_rows, grad_up, preferred_element_type=jnp.fl...  13.5 us
    all_to_all x1, blocking collectives, shards(): lax.all_to_all(grad_outgoing, 'expert', split_axis=0, concat_axis=0, tile...  13.3 us
    all_to_all x1, blocking collectives, shards(): lax.all_to_all(back_share, 'expert', split_axis=0, concat_axis=0, tiled=T...  12.7 us
  transfers between devices with their start and end apart: 9, of which 8 were waited for; matrix products, arithmetic and copies ran while one was open for 7% of the time, Pallas kernels for 0%

commit v1 on v0

v1 whole, which is shorter than its diff:
```python
import functools

import jax
import jax.numpy as jnp
from jax import lax
from jax.experimental import pallas as pl
from jax.experimental.pallas import tpu as pltpu
from jax.sharding import PartitionSpec as P

SLOTS = 16
TICKS = 2
EPSILON = 1e-06
F32 = jnp.float32
BF16 = jnp.bfloat16
VMEM_BIG = 48 * 1024 * 1024
VMEM_SMALL = 24 * 1024 * 1024
CHUNKS = 8


def shifted(block, axis, distance):
    size = lax.axis_size(axis)
    return lax.ppermute(block, axis, [((i - distance) % size, i) for i in range(size)])


def dot(a, b, ca=1, cb=0):
    return lax.dot_general(a, b, (((ca,), (cb,)), ((), ())), preferred_element_type=F32)


def call(kernel, outs, args, *, any_args=(), scratch=(), vmem=VMEM_SMALL, flops=0, extra=0):
    outs = [jax.ShapeDtypeStruct(s, d) for s, d in outs]
    moved = sum(a.size * a.dtype.itemsize for a in args) + sum(o.size * o.dtype.itemsize for o in outs)
    specs = [
        pl.BlockSpec(memory_space=pl.ANY if i in any_args else pltpu.VMEM) for i in range(len(args))
    ]
    return pl.pallas_call(
        kernel,
        out_shape=outs,
        in_specs=specs,
        out_specs=[pl.BlockSpec(memory_space=pltpu.VMEM) for _ in outs],
        scratch_shapes=list(scratch),
        compiler_params=pltpu.CompilerParams(vmem_limit_bytes=vmem),
        cost_estimate=pl.CostEstimate(flops=flops, bytes_accessed=moved + extra, transcendentals=0),
    )(*args)


def select_of(routes):
    hits = (routes == 0).astype(F32)
    marked = jnp.sum(hits, axis=0, keepdims=True)
    rows = routes.shape[1]
    before = lax.broadcasted_iota(jnp.int32, (rows, rows), 0) < lax.broadcasted_iota(
        jnp.int32, (rows, rows), 1
    )
    wide = jnp.broadcast_to(marked, (SLOTS, rows))
    places = dot(wide.astype(BF16), before.astype(F32).astype(BF16))
    slot = lax.broadcasted_iota(jnp.int32, (SLOTS, rows), 0).astype(F32)
    return jnp.where((places == slot) & (wide > 0.5), 1.0, 0.0), marked


def slot_gates(select, routes, gates):
    weights = jnp.sum(jnp.where(routes == 0, gates, 0.0), axis=0, keepdims=True)
    return jnp.sum(select * weights, axis=1, keepdims=True)


def pick(select, rows):
    return dot(select.astype(BF16), rows).astype(BF16)


def put(select, rows):
    return dot(select.astype(BF16), rows, 0, 0)


def inv_rms_of(values):
    return lax.rsqrt(jnp.mean(values * values, axis=-1, keepdims=True) + EPSILON)


def merged(select_to, select_from, fresh, old):
    same = dot(select_to.astype(BF16), select_from.astype(BF16), 1, 1)
    taken = jnp.sum(same, axis=1, keepdims=True)
    moved = dot(same.astype(BF16), fresh)
    return jnp.where(taken > 0.5, moved, old.astype(F32)).astype(BF16)


def first_rows_kernel(tokens, routes, raw, normed):
    select, _ = select_of(routes[0])
    rows = pick(select, tokens[...])
    raw[...] = rows
    values = rows.astype(F32)
    normed[...] = (values * inv_rms_of(values)).astype(BF16)


def other_rows_kernel(tokens, cotangent, next_routes, prev_routes, prev2_routes, t1, cot):
    t1[...] = pick(select_of(next_routes[0])[0], tokens[...])
    cot[:SLOTS] = pick(select_of(prev_routes[1])[0], cotangent[...])
    cot[SLOTS:] = pick(select_of(prev2_routes[0])[0], cotangent[...])


def scale_kernel(tick, rows, routes, gates, out):
    select, _ = select_of(routes[tick])
    weight = slot_gates(select, routes[tick], gates[tick])
    out[...] = (weight * rows[:SLOTS].astype(F32)).astype(BF16)


def norm_kernel(rows, out):
    values = rows[...].astype(F32)
    out[...] = (values * inv_rms_of(values)).astype(BF16)


def update_kernel(tick, n, *refs):
    parts, (raw, routes, gates), rest = refs[:n], refs[n : n + 3], refs[n + 3 :]
    select, _ = select_of(routes[tick])
    weight = slot_gates(select, routes[tick], gates[tick])
    total = parts[0][...].astype(F32)
    for p in parts[1:]:
        total = total + p[...].astype(F32)
    fresh = (raw[...].astype(F32) + weight * total).astype(BF16)
    if tick == 0:
        next_routes, t1, upd, onward = rest
        onward[...] = merged(select_of(next_routes[0])[0], select, fresh, t1[...])
    else:
        (upd,) = rest
    upd[...] = fresh


def state_grad(parts, h, c):
    total = parts[0][...].astype(F32)
    for p in parts[1:]:
        total = total + p[...].astype(F32)
    values = h.astype(F32)
    inv = inv_rms_of(values)
    inner = jnp.mean(total * values, axis=-1, keepdims=True)
    return (c.astype(F32) + inv * total - inv * inv * inv * values * inner).astype(BF16)


def grad1_kernel(n, *refs):
    parts, (h, cot, routes, prev_routes, upd, onward) = refs[:n], refs[n:]
    fresh = state_grad(parts, h[...], cot[:SLOTS])
    upd[...] = fresh
    onward[...] = merged(
        select_of(prev_routes[0])[0], select_of(routes[1])[0], fresh, cot[SLOTS:]
    )


def finish_grad_kernel(n, *refs):
    parts, (h, c, routes, upd1, next_routes, bulk, out) = refs[:n], refs[n:]
    fresh = state_grad(parts, h[...], c[...])
    first, _ = select_of(next_routes[0])
    second, _ = select_of(routes[0])
    place_rows(bulk, first, upd1[...], second, fresh, out)


def place_rows(bulk, first, rows1, second, rows2, out):
    ones = jnp.ones((SLOTS, 128), BF16)
    hit1 = put(first, ones)[:, :1] > 0.5
    hit2 = put(second, ones)[:, :1] > 0.5
    value = jnp.where(hit1, put(first, rows1), bulk[...].astype(F32))
    out[...] = jnp.where(hit2, put(second, rows2), value).astype(BF16)


def finish_state_kernel(bulk, upd0, prev2_routes, upd1, prev_routes, out):
    first, _ = select_of(prev2_routes[0])
    second, _ = select_of(prev_routes[1])
    place_rows(bulk, first, upd0[...], second, upd1[...], out)


def silu_grads(pre_gate, pre_up, grad_act):
    sig = jax.nn.sigmoid(pre_gate)
    grad_gate = (grad_act * pre_up * sig * (1.0 + pre_gate * (1.0 - sig))).astype(BF16)
    grad_up = (grad_act * (pre_gate * sig)).astype(BF16)
    return grad_gate, grad_up


def weight_copies(gate, up, down, gate_v, up_v, down_v, sems, rows, cols):
    out = []
    for c in range(CHUNKS):
        r = pl.ds(c * rows, rows)
        k = pl.ds(c * cols, cols)
        out.append(
            (
                pltpu.make_async_copy(gate.at[r], gate_v.at[r], sems.at[0, c]),
                pltpu.make_async_copy(up.at[r], up_v.at[r], sems.at[1, c]),
                pltpu.make_async_copy(down.at[:, k], down_v.at[:, k], sems.at[2, c]),
            )
        )
    return out


def gather_rows(blocks, whole):
    for i, b in enumerate(blocks):
        whole[i * SLOTS : (i + 1) * SLOTS] = b[...]


def spread_rows(value, blocks, cols):
    for i, b in enumerate(blocks):
        b[:, cols] = value[i * SLOTS : (i + 1) * SLOTS].astype(BF16)


def forward_kernel(n, *refs):
    blocks, (gate, up, down) = refs[:n], refs[n : n + 3]
    x, pre_gate, pre_up, act = refs[n + 3 : n + 7]
    parts = refs[n + 7 : 2 * n + 7]
    gate_v, up_v, down_v, sems = refs[2 * n + 7 :]
    width = gate.shape[0]
    step = width // CHUNKS
    copies = weight_copies(gate, up, down, gate_v, up_v, down_v, sems, step, step)
    for cg, cu, _ in copies:
        cg.start()
        cu.start()
    for _, _, cd in copies:
        cd.start()
    gather_rows(blocks, x)
    acc_g = jnp.zeros(pre_gate.shape, F32)
    acc_u = jnp.zeros(pre_up.shape, F32)
    for c, (cg, cu, _) in enumerate(copies):
        k = slice(c * step, (c + 1) * step)
        cg.wait()
        acc_g = acc_g + dot(x[:, k], gate_v[k])
        cu.wait()
        acc_u = acc_u + dot(x[:, k], up_v[k])
    pre_gate[...] = acc_g
    pre_up[...] = acc_u
    activated = (acc_g * jax.nn.sigmoid(acc_g) * acc_u).astype(BF16)
    act[...] = activated
    for c, (_, _, cd) in enumerate(copies):
        k = slice(c * step, (c + 1) * step)
        cd.wait()
        spread_rows(dot(activated, down_v[:, k]), parts, k)


def down_kernel(n, act, down, *parts):
    width = down.shape[1]
    step = width // CHUNKS
    for c in range(CHUNKS):
        k = slice(c * step, (c + 1) * step)
        spread_rows(dot(act[...], down[:, k]), parts, k)


def back_rows(gg, gu, gate_v, up_v, parts, step):
    for c in range(CHUNKS):
        k = slice(c * step, (c + 1) * step)
        spread_rows(dot(gg, gate_v[k], 1, 1) + dot(gu, up_v[k], 1, 1), parts, k)


def tick1_kernel(n, *refs):
    xs, gs, (gate, up, down) = refs[:n], refs[n : 2 * n], refs[2 * n : 2 * n + 3]
    x, g, act, grad_gate, grad_up = refs[2 * n + 3 : 2 * n + 8]
    parts = refs[2 * n + 8 : 3 * n + 8]
    gate_v, up_v, down_v, sems = refs[3 * n + 8 :]
    width = gate.shape[0]
    step = width // CHUNKS
    copies = weight_copies(gate, up, down, gate_v, up_v, down_v, sems, step, step)
    for three in copies:
        for c in three:
            c.start()
    gather_rows(xs, x)
    gather_rows(gs, g)
    acc_g = jnp.zeros(act.shape, F32)
    acc_u = jnp.zeros(act.shape, F32)
    acc_a = jnp.zeros(act.shape, F32)
    for c, (cg, cu, cd) in enumerate(copies):
        k = slice(c * step, (c + 1) * step)
        cg.wait()
        acc_g = acc_g + dot(x[:, k], gate_v[k])
        cu.wait()
        acc_u = acc_u + dot(x[:, k], up_v[k])
        cd.wait()
        acc_a = acc_a + dot(g[:, k], down_v[:, k], 1, 1)
    act[...] = (acc_g * jax.nn.sigmoid(acc_g) * acc_u).astype(BF16)
    gg, gu = silu_grads(acc_g, acc_u, acc_a)
    grad_gate[...] = gg
    grad_up[...] = gu
    back_rows(gg, gu, gate_v, up_v, parts, step)


def tick0_kernel(n, *refs):
    gs, (pre_gate, pre_up, gate, up, down) = refs[:n], refs[n : n + 5]
    g, grad_gate, grad_up = refs[n + 5 : n + 8]
    parts = refs[n + 8 : 2 * n + 8]
    gate_v, up_v, down_v, sems = refs[2 * n + 8 :]
    width = gate.shape[0]
    step = width // CHUNKS
    copies = weight_copies(gate, up, down, gate_v, up_v, down_v, sems, step, step)
    for _, _, cd in copies:
        cd.start()
    for cg, cu, _ in copies:
        cg.start()
        cu.start()
    gather_rows(gs, g)
    acc_a = jnp.zeros(pre_gate.shape, F32)
    for c, (_, _, cd) in enumerate(copies):
        k = slice(c * step, (c + 1) * step)
        cd.wait()
        acc_a = acc_a + dot(g[:, k], down_v[:, k], 1, 1)
    gg, gu = silu_grads(pre_gate[...], pre_up[...], acc_a)
    grad_gate[...] = gg
    grad_up[...] = gu
    for cg, cu, _ in copies:
        cg.wait()
        cu.wait()
    back_rows(gg, gu, gate_v, up_v, parts, step)


def weight_grad_kernel(m, *refs):
    xs, gs = refs[:m], refs[m : 2 * m]
    acts, ggs, gus = refs[2 * m : 3 * m], refs[3 * m : 4 * m], refs[4 * m : 5 * m]
    gate_out, up_out, down_out = refs[5 * m :]

    def whole(blocks):
        return jnp.concatenate([b[...] for b in blocks], axis=0)

    x_t = whole(xs).T
    gate_out[...] = dot(x_t, whole(ggs)).astype(BF16)
    up_out[...] = dot(x_t, whole(gus)).astype(BF16)
    down_out[...] = dot(whole(acts), whole(gs), 0, 0).astype(BF16)


def weight_grads(xs, gs, acts, ggs, gus):
    m = len(xs)
    rows, width = xs[0].shape
    hidden = acts[0].shape[1]
    step = width // CHUNKS
    wide = pl.BlockSpec((rows, step), lambda c: (0, c))
    narrow = pl.BlockSpec((rows, hidden), lambda c: (0, 0))
    return pl.pallas_call(
        functools.partial(weight_grad_kernel, m),
        grid=(CHUNKS,),
        out_shape=[
            jax.ShapeDtypeStruct((width, hidden), BF16),
            jax.ShapeDtypeStruct((width, hidden), BF16),
            jax.ShapeDtypeStruct((hidden, width), BF16),
        ],
        in_specs=[wide] * (2 * m) + [narrow] * (3 * m),
        out_specs=[
            pl.BlockSpec((step, hidden), lambda c: (c, 0)),
            pl.BlockSpec((step, hidden), lambda c: (c, 0)),
            pl.BlockSpec((hidden, step), lambda c: (0, c)),
        ],
        compiler_params=pltpu.CompilerParams(vmem_limit_bytes=VMEM_BIG),
        cost_estimate=pl.CostEstimate(
            flops=6 * m * rows * width * hidden,
            bytes_accessed=6 * width * hidden + 4 * m * rows * width,
            transcendentals=0,
        ),
    )(*xs, *gs, *acts, *ggs, *gus)


def from_group(block):
    n = lax.axis_size("expert")
    return [block] + [shifted(block, "expert", k) for k in range(1, n)]


def to_group(blocks):
    return [blocks[0]] + [shifted(b, "expert", -k) for k, b in enumerate(blocks) if k]


def copies_of(block):
    n = lax.axis_size("dp")
    return [block] + [shifted(block, "dp", k) for k in range(1, n)]


def shards(tokens, cotangent, w_gate, w_up, w_down, routes, gates):
    gate, up, down = w_gate[0], w_up[0], w_down[0]
    width, hidden = gate.shape
    n = lax.axis_size("expert")
    rows = n * SLOTS
    routes = jnp.transpose(routes, (0, 2, 1))
    gates = jnp.transpose(gates, (0, 2, 1))
    one = ((SLOTS, width), BF16)
    every = ((rows, width), BF16)
    wide = ((rows, hidden), BF16)
    wide32 = ((rows, hidden), F32)
    part = functools.partial
    weights_v = [
        pltpu.VMEM((width, hidden), BF16),
        pltpu.VMEM((width, hidden), BF16),
        pltpu.VMEM((hidden, width), BF16),
        pltpu.SemaphoreType.DMA((3, CHUNKS)),
    ]
    matmul = 2 * rows * width * hidden

    prev_routes = shifted(routes, "section", 1)
    next_routes = shifted(routes[1:], "section", -1)
    prev2_routes = shifted(routes[:1], "section", 2)
    bulk_state = shifted(tokens, "section", 2)
    bulk_grad = shifted(cotangent, "section", -2)

    raw0, normed0 = call(first_rows_kernel, [one, one], [tokens, routes])
    x0_blocks = from_group(normed0)
    t1, cot_rows = call(
        other_rows_kernel,
        [one, ((2 * SLOTS, width), BF16)],
        [tokens, cotangent, next_routes, prev_routes, prev2_routes],
    )
    cot_rows = shifted(cot_rows, "section", -1)
    x0, pre_gate0, pre_up0, act0, *parts = call(
        part(forward_kernel, n),
        [every, wide32, wide32, wide] + [one] * n,
        [*x0_blocks, gate, up, down],
        any_args=(n, n + 1, n + 2),
        scratch=weights_v,
        vmem=VMEM_BIG,
        flops=3 * matmul,
    )
    parts = to_group(parts)
    upd0, h1 = call(
        part(update_kernel, 0, n),
        [one, one],
        [*parts, raw0, routes, gates, next_routes, t1],
    )
    h1 = shifted(h1, "section", 1)
    upd0 = shifted(upd0, "section", 2)
    (g1_rows,) = call(part(scale_kernel, 1), [one], [cot_rows, routes, gates])
    g1_blocks = from_group(g1_rows)

    (normed1,) = call(norm_kernel, [one], [h1])
    x1_blocks = from_group(normed1)
    x1, g1, act1, gg1, gu1, *parts = call(
        part(tick1_kernel, n),
        [every, every, wide, wide, wide] + [one] * n,
        [*x1_blocks, *g1_blocks, gate, up, down],
        any_args=(2 * n, 2 * n + 1, 2 * n + 2),
        scratch=weights_v,
        vmem=VMEM_BIG,
        flops=5 * matmul,
    )
    parts = to_group(parts)
    outs1 = call(part(down_kernel, n), [one] * n, [act1, down], vmem=VMEM_BIG, flops=matmul)
    outs1 = to_group(outs1)
    cu1, c0 = call(
        part(grad1_kernel, n), [one, one], [*parts, h1, cot_rows, routes, prev_routes]
    )
    c0 = shifted(c0, "section", -1)
    cu1 = shifted(cu1, "section", -1)
    (upd1,) = call(part(update_kernel, 1, n), [one], [*outs1, h1, routes, gates])
    upd1 = shifted(upd1, "section", 1)

    (g0_rows,) = call(part(scale_kernel, 0), [one], [c0, routes, gates])
    g0_blocks = from_group(g0_rows)
    g0, gg0, gu0, *parts = call(
        part(tick0_kernel, n),
        [every, wide, wide] + [one] * n,
        [*g0_blocks, pre_gate0, pre_up0, gate, up, down],
        any_args=(n + 2, n + 3, n + 4),
        scratch=weights_v,
        vmem=VMEM_BIG,
        flops=3 * matmul,
    )
    parts = to_group(parts)
    gate_out, up_out, down_out = weight_grads(
        copies_of(x0) + copies_of(x1),
        copies_of(g0) + copies_of(g1),
        copies_of(act0) + copies_of(act1),
        copies_of(gg0) + copies_of(gg1),
        copies_of(gu0) + copies_of(gu1),
    )
    (state,) = call(
        finish_state_kernel,
        [(tokens.shape, BF16)],
        [bulk_state, upd0, prev2_routes, upd1, prev_routes],
    )
    (grad,) = call(
        part(finish_grad_kernel, n),
        [(tokens.shape, BF16)],
        [*parts, raw0, c0, routes, cu1, next_routes, bulk_grad],
    )
    return (grad, state, gate_out[None], up_out[None], down_out[None])


def solution(mesh):
    rows = P(("section", "expert", "dp"), None)
    slots = P(None, ("section", "expert", "dp"), None)
    cols = P("section", None, "expert")
    hidden = P("section", "expert", None)
    return jax.shard_map(
        shards,
        mesh=mesh,
        in_specs=(rows, rows, cols, cols, hidden, slots, slots),
        out_specs=(rows, rows, cols, cols, hidden),
        check_vma=False,
    )
```

time: 606 us -> 274 us (0.45)
  the two profiles are of different devices: /device:TPU:0 before, /device:TPU:17 now
where the time goes in v1:
time: 274 us; the launch traced here: 273 us
  waiting for transfers between devices  172 us (63%)
  starting transfers between devices  55.2 us (20%)
  Pallas kernels  42 us (15%)
  local copies, waits for them, and re-layouts  3.35 us (1%)
    ppermute x45, waiting for transfers between devices, shifted(): lax.ppermute(block, axis, [((i - distance) % size, i) for i in range(size)])  172 us
    ppermute x45, starting transfers between devices, shifted(): lax.ppermute(block, axis, [((i - distance) % size, i) for i in range(size)])  55.2 us
    pallas_call x14, Pallas kernels, call(): pl.pallas_call(kernel, out_shape=outs, in_specs=specs, out_specs=[pl.Bloc...  33.4 us
    pallas_call x1, Pallas kernels, weight_grads(): pl.pallas_call(functools.partial(weight_grad_kernel, m), grid=(CHUNKS,),...  8.66 us
  transfers between devices with their start and end apart: 45, of which 22 were waited for; matrix products, arithmetic and copies ran while one was open for 0% of the time, Pallas kernels for 9%

profile of v1, /device:TPU:17, one launch (start us, length us, event | category | flops | bytes accessed | tf_op | source)
XLA Modules:
  0.0 273.3 jit_solution(6724488477222597418)
XLA Ops:
  0.6 1.3 copy-done
  2.0 0.7 copy-done.4
  2.6 0.5 shard_map.110
  3.2 1.9 collective-permute-start
  5.7 1.3 collective-permute-start.7
  7.0 1.3 collective-permute-done.6.next_routes.refs_7_.refs_8_
  8.2 1.4 collective-permute-start.8
  9.6 2.0 collective-permute-done.8.prev2_routes
  11.6 1.3 copy-done.2
  12.9 1.0 shard_map.112
  13.8 1.7 collective-permute-start.13
  15.5 6.4 %shard_map.111 = (bf16[64,5120]{1,0:T(8,128)(2,1)S(1)}, f32[64,512]{1,0:T(8,128)S(1)}, f32[64,512]{1,0:T(8,128)S(1)}, bf16[64,512]{1,0:T(8,128)(2,1)S(1)}, bf16[...) custom-call(bf16[16,5120]{1,0:T(8,128)(2,1)S(1)} %get-tuple-element., ...), custom_call_target="tpu_custom_call" | custom-call | flops 1006632960 | bytes 18022400 | tf_op jit(solution)/shard_map/pallas_call | solution.py:35
  21.9 3.7 %collective-permute-start.3 = (bf16[16,5120]{1,0:T(8,128)(2,1)S(1)}, bf16[16,5120]{1,0:T(8,128)(2,1)S(1)}, u32[]{:S(2)}, u32[]{:S(2)}) collective-permute-start(bf16[16,5120]{1,0:T(8,128)(2,1)S(1)} %get-tuple-element.46), channel_id=1, source_target_pairs={{2,0},{4,2},{6,4},{0,6},{3,1},{5,3},{7,5},{1,7},{10,8},{12,10},{14... | collective-permute-start | bytes 491528 | tf_op jit(solution)/shard_map/ppermute | solution.py:22
  25.9 1.5 collective-permute-start.5
  27.4 2.1 collective-permute-done.3.refs_1_
  29.5 2.4 collective-permute-done.4.refs_2_
  31.9 1.5 collective-permute-done.5.refs_3_
  33.9 1.3 collective-permute-start.9
  35.4 2.8 %collective-permute-start.14 = (bf16[16,5120]{1,0:T(8,128)(2,1)S(1)}, bf16[16,5120]{1,0:T(8,128)(2,1)S(1)}, u32[]{:S(2)}, u32[]{:S(2)}) collective-permute-start(bf16[16,5120]{1,0:T(8,128)(2,1)S(1)} %shard_map.115.refs_4_), channel_id=1, source_target_pairs={{6,0},{0,2},{2,4},{4,6},{7,1},{1,3},{3,5},{5,7},{14,8},{8,10},{10,... | collective-permute-start | bytes 491528 | tf_op jit(solution)/shard_map/ppermute | solution.py:22
  38.8 3.1 %collective-permute-start.10 = (bf16[16,5120]{1,0:T(8,128)(2,1)S(1)}, bf16[16,5120]{1,0:T(8,128)(2,1)S(1)}, u32[]{:S(2)}, u32[]{:S(2)}) collective-permute-start(bf16[16,5120]{1,0:T(8,128)(2,1)S(1)} %shard_map.114.refs_0_), channel_id=1, source_target_pairs={{6,0},{0,2},{2,4},{4,6},{7,1},{1,3},{3,5},{5,7},{14,8},{8,10},{10,... | collective-permute-start | bytes 491528 | tf_op jit(solution)/shard_map/ppermute | solution.py:22
  42.1 0.8 collective-permute-start.12
  42.9 2.8 %collective-permute-done.15.refs_6_ = bf16[16,5120]{1,0:T(8,128)(2,1)S(1)} collective-permute-done((bf16[16,5120]{1,0:T(8,128)(2,1)S(1)}, bf16[16,5120]{1,0:T(8,128)(2,1)S(1)}, u32[]{:S(2)}, u32[]{:S(2)}) %collective-permute-start.15) | collective-permute-done | bytes 163872 | tf_op jit(solution)/shard_map/ppermute | solution.py:22
  45.8 1.5 collective-permute-done.16.refs_7_
  47.3 1.3 collective-permute-done.10.refs_1_
  48.6 4.2 %collective-permute-done.11.refs_2_ = bf16[16,5120]{1,0:T(8,128)(2,1)S(1)} collective-permute-done((bf16[16,5120]{1,0:T(8,128)(2,1)S(1)}, bf16[16,5120]{1,0:T(8,128)(2,1)S(1)}, u32[]{:S(2)}, u32[]{:S(2)}) %collective-permute-start.11) | collective-permute-done | bytes 163872 | tf_op jit(solution)/shard_map/ppermute | solution.py:22
  52.8 0.6 collective-permute-done.12.refs_3_
  53.4 9.4 %shard_map.116 = (bf16[64,5120]{1,0:T(8,128)(2,1)S(1)}, bf16[64,5120]{1,0:T(8,128)(2,1)S(1)}, bf16[64,512]{1,0:T(8,128)(2,1)S(1)}, bf16[64,512]{1,0:T(8,128)(2,1...) custom-call(bf16[16,5120]{1,0:T(8,128)(2,1)S(1)} %shard_map.114.refs, ...), custom_call_target="tpu_custom_call" | custom-call | flops 1677721600 | bytes 19202048 | tf_op jit(solution)/shard_map/pallas_call | solution.py:35
  62.9 1.3 collective-permute-start.18
  64.2 1.9 collective-permute-start.19
  66.1 2.1 collective-permute-start.30
  68.2 1.2 collective-permute-start.39
  69.6 1.2 collective-permute-start.40
  70.8 0.5 collective-permute-done.19.refs_3_
  71.3 0.5 shard_map.117
  71.8 1.1 collective-permute-start.20
  72.8 1.2 collective-permute-start.42
  74.0 1.0 shard_map.121
  75.4 1.9 collective-permute-start.31
  77.3 1.2 collective-permute-start.32
  78.5 1.2 collective-permute-start.44
  79.7 11.7 %collective-permute-done.44.refs_19_ = bf16[64,512]{1,0:T(8,128)(2,1)S(1)} collective-permute-done((bf16[64,512]{1,0:T(8,128)(2,1)S(1)}, bf16[64,512]{1,0:T(8,128)(2,1)S(1)}, u32[]{:S(2)}, u32[]{:S(2)}) %collective-permute-start.44) | collective-permute-done | bytes 65568 | tf_op jit(solution)/shard_map/ppermute | solution.py:22
  91.5 5.0 %collective-permute-start.29 = (bf16[128,5120]{1,0:T(8,128)(2,1)S(1)}, bf16[128,5120]{1,0:T(8,128)(2,1)S(1)}, u32[]{:S(2)}, u32[]{:S(2)}) collective-permute-start(bf16[128,5120]{1,0:T(8,128)(2,1)S(1)} %copy-done.1), channel_id=1, source_target_pairs={{16,0},{24,8},{0,16},{8,24},{17,1},{25,9},{1,17},{9,25},{18,2},{26... | collective-permute-start | bytes 3932168 | tf_op jit(solution)/shard_map/ppermute | solution.py:22
  96.8 3.2 %collective-permute-start.33 = (bf16[16,5120]{1,0:T(8,128)(2,1)S(1)}, bf16[16,5120]{1,0:T(8,128)(2,1)S(1)}, u32[]{:S(2)}, u32[]{:S(2)}) collective-permute-start(bf16[16,5120]{1,0:T(8,128)(2,1)S(1)} %get-tuple-element.70), channel_id=1, source_target_pairs={{6,0},{0,2},{2,4},{4,6},{7,1},{1,3},{3,5},{5,7},{14,8},{8,10},{10,... | collective-permute-start | bytes 491528 | tf_op jit(solution)/shard_map/ppermute | solution.py:22
  100.0 2.2 collective-permute-done.33.refs_3_
  102.2 1.2 collective-permute-start.22
  103.5 0.5 collective-permute-done.21.refs_1_
  104.0 2.4 collective-permute-start.23
  106.6 1.1 collective-permute-done.22.refs_2_
  107.9 3.4 %collective-permute-done.23.refs_3_ = bf16[16,5120]{1,0:T(8,128)(2,1)S(1)} collective-permute-done((bf16[16,5120]{1,0:T(8,128)(2,1)S(1)}, bf16[16,5120]{1,0:T(8,128)(2,1)S(1)}, u32[]{:S(2)}, u32[]{:S(2)}) %collective-permute-start.23) | collective-permute-done | bytes 163872 | tf_op jit(solution)/shard_map/ppermute | solution.py:22
  111.3 9.0 %shard_map.119 = (bf16[64,5120]{1,0:T(8,128)(2,1)S(1)}, bf16[64,512]{1,0:T(8,128)(2,1)S(1)}, bf16[64,512]{1,0:T(8,128)(2,1)S(1)}, bf16[16,5120]{1,0:T(8,128)(2,1...) custom-call(bf16[16,5120]{1,0:T(8,128)(2,1)S(1)} %shard_map.118.refs_0_, ...), custom_call_target="tpu_custom_call" | custom-call | flops 1006632960 | bytes 18087936 | tf_op jit(solution)/shard_map/pallas_call | solution.py:35
  120.3 0.7 collective-permute-start.24
  121.0 94.4 %collective-permute-done.34.upd1 = bf16[16,5120]{1,0:T(8,128)(2,1)S(1)} collective-permute-done((bf16[16,5120]{1,0:T(8,128)(2,1)S(1)}, bf16[16,5120]{1,0:T(8,128)(2,1)S(1)}, u32[]{:S(2)}, u32[]{:S(2)}) %collective-permute-start.34) | collective-permute-done | bytes 163872 | tf_op jit(solution)/shard_map/ppermute | solution.py:22
  215.4 2.9 %collective-permute-start.26 = (bf16[16,5120]{1,0:T(8,128)(2,1)S(1)}, bf16[16,5120]{1,0:T(8,128)(2,1)S(1)}, u32[]{:S(2)}, u32[]{:S(2)}) collective-permute-start(bf16[16,5120]{1,0:T(8,128)(2,1)S(1)} %get-tuple-element.63), channel_id=1, source_target_pairs={{6,0},{0,2},{2,4},{4,6},{7,1},{1,3},{3,5},{5,7},{14,8},{8,10},{10,... | collective-permute-start | bytes 491528 | tf_op jit(solution)/shard_map/ppermute | solution.py:22
  218.8 0.8 collective-permute-done.25.refs_2_
  219.6 1.0 collective-permute-start.38
  220.7 0.6 collective-permute-done.26.refs_3_
  221.2 0.9 collective-permute-start.37
  222.1 0.6 collective-permute-start.41
  222.7 0.9 collective-permute-start.43
  223.6 2.1 shard_map.123
  225.7 2.2 shard_map.120
  227.8 36.1 %collective-permute-done.41.refs_13_ = bf16[64,512]{1,0:T(8,128)(2,1)S(1)} collective-permute-done((bf16[64,512]{1,0:T(8,128)(2,1)S(1)}, bf16[64,512]{1,0:T(8,128)(2,1)S(1)}, u32[]{:S(2)}, u32[]{:S(2)}) %collective-permute-start.41) | collective-permute-done | bytes 65568 | tf_op jit(solution)/shard_map/ppermute | solution.py:22
  263.9 0.7 collective-permute-done.43.refs_17_
  264.6 8.7 %shard_map.124 = (bf16[5120,512]{1,0:T(8,128)(2,1)}, bf16[5120,512]{1,0:T(8,128)(2,1)}, bf16[512,5120]{1,0:T(8,128)(2,1)}) custom-call(bf16[64,5120]{1,0:T(8,128)(2,1)S(1)} %get-tuple-element.71.refs_0_, bf16[64,5120]{1,0:T(8,128)(2,1)S(1)} %collective-permute-done.35.refs_1_, bf16[64,5120]{1,0:T(8,128)(2,1)S(1)} %get-tuple-element.72.refs_2_, ...), custom_call_target="tpu_custom_call" | custom-call | flops 4026531840 | bytes 20971520 | tf_op jit(solution)/shard_map/pallas_call | solution.py:323
  (61 shorter events, 4.4 us)
Async XLA Ops:
  0.6 1.3 copy-start
  1.9 0.7 copy-start.4
  3.2 12.3 %collective-permute-start = (bf16[16,5120]{1,0:T(8,128)(2,1)S(1)}, bf16[16,5120]{1,0:T(8,128)(2,1)S(1)}, u32[]{:S(2)}, u32[]{:S(2)}) collective-permute-start(bf16[16,5120]{1,0:T(8,128)(2,1)S(1)} %get-tuple-element.44.refs_0_), channel_id=1, source_target_pairs={{6,0},{0,2},{2,4},{4,6},{7,1},{1,3},{3,5},{5,7},{14,8},{8,10},{10,... | collective-permute-start | bytes 491528 | tf_op jit(solution)/shard_map/ppermute | solution.py:22
  5.0 10.5 %collective-permute-start.1 = (bf16[16,5120]{1,0:T(8,128)(2,1)S(1)}, bf16[16,5120]{1,0:T(8,128)(2,1)S(1)}, u32[]{:S(2)}, u32[]{:S(2)}) collective-permute-start(bf16[16,5120]{1,0:T(8,128)(2,1)S(1)} %get-tuple-element.44.refs_0_), channel_id=1, source_target_pairs={{4,0},{6,2},{0,4},{2,6},{5,1},{7,3},{1,5},{3,7},{12,8},{14,10},{8,... | collective-permute-start | bytes 491528 | tf_op jit(solution)/shard_map/ppermute | solution.py:22
  5.2 10.3 %collective-permute-start.2 = (bf16[16,5120]{1,0:T(8,128)(2,1)S(1)}, bf16[16,5120]{1,0:T(8,128)(2,1)S(1)}, u32[]{:S(2)}, u32[]{:S(2)}) collective-permute-start(bf16[16,5120]{1,0:T(8,128)(2,1)S(1)} %get-tuple-element.44.refs_0_), channel_id=1, source_target_pairs={{2,0},{4,2},{6,4},{0,6},{3,1},{5,3},{7,5},{1,7},{10,8},{12,10},{14... | collective-permute-start | bytes 491528 | tf_op jit(solution)/shard_map/ppermute | solution.py:22
  5.5 2.7 collective-permute-start.6
  5.7 5.9 %collective-permute-start.7 = (s32[2,4,128]{2,1,0:T(4,128)S(1)}, s32[2,4,128]{2,1,0:T(4,128)S(1)}, u32[]{:S(2)}, u32[]{:S(2)}) collective-permute-start(s32[2,4,128]{2,1,0:T(4,128)S(1)} %bitcast.16), channel_id=1, source_target_pairs={{24,0},{0,8},{8,16},{16,24},{25,1},{1,9},{9,17},{17,25},{26,2},{2,... | collective-permute-start | bytes 12296 | tf_op jit(solution)/shard_map/ppermute | solution.py:22
  8.2 3.3 %collective-permute-start.8 = (s32[1,4,128]{2,1,0:T(4,128)S(1)}, s32[1,4,128]{2,1,0:T(4,128)S(1)}, u32[]{:S(2)}, u32[]{:S(2)}) collective-permute-start(s32[1,4,128]{2,1,0:T(4,128)S(1)} %get-tuple-element.83), channel_id=1, source_target_pairs={{16,0},{24,8},{0,16},{8,24},{17,1},{25,9},{1,17},{9,25},{18,2},{26... | collective-permute-start | bytes 6152 | tf_op jit(solution)/shard_map/ppermute | solution.py:22
  11.6 1.3 copy-start.2
  13.8 21.3 %collective-permute-start.13 = (bf16[32,5120]{1,0:T(8,128)(2,1)S(1)}, bf16[32,5120]{1,0:T(8,128)(2,1)S(1)}, u32[]{:S(2)}, u32[]{:S(2)}) collective-permute-start(bf16[32,5120]{1,0:T(8,128)(2,1)S(1)} %get-tuple-element.52), channel_id=1, source_target_pairs={{8,0},{16,8},{24,16},{0,24},{9,1},{17,9},{25,17},{1,25},{10,2},{18... | collective-permute-start | bytes 983048 | tf_op jit(solution)/shard_map/ppermute | solution.py:22
  15.5 18.0 %copy-start.5 = (s32[2,128,4]{1,2,0:T(4,128)S(1)}, s32[2,128,4]{1,2,0:T(4,128)}, u32[]{:S(2)}) copy-start(s32[2,128,4]{1,2,0:T(4,128)} %param.12) | copy-start | bytes 12292
  15.5 17.9 %copy-start.6 = (f32[2,128,4]{1,2,0:T(4,128)S(1)}, f32[2,128,4]{1,2,0:T(4,128)}, u32[]{:S(2)}) copy-start(f32[2,128,4]{1,2,0:T(4,128)} %param.13) | copy-start | bytes 12292
  21.9 7.5 %collective-permute-start.3 = (bf16[16,5120]{1,0:T(8,128)(2,1)S(1)}, bf16[16,5120]{1,0:T(8,128)(2,1)S(1)}, u32[]{:S(2)}, u32[]{:S(2)}) collective-permute-start(bf16[16,5120]{1,0:T(8,128)(2,1)S(1)} %get-tuple-element.46), channel_id=1, source_target_pairs={{2,0},{4,2},{6,4},{0,6},{3,1},{5,3},{7,5},{1,7},{10,8},{12,10},{14... | collective-permute-start | bytes 491528 | tf_op jit(solution)/shard_map/ppermute | solution.py:22
  25.7 6.2 %collective-permute-start.4 = (bf16[16,5120]{1,0:T(8,128)(2,1)S(1)}, bf16[16,5120]{1,0:T(8,128)(2,1)S(1)}, u32[]{:S(2)}, u32[]{:S(2)}) collective-permute-start(bf16[16,5120]{1,0:T(8,128)(2,1)S(1)} %get-tuple-element.47), channel_id=1, source_target_pairs={{4,0},{6,2},{0,4},{2,6},{5,1},{7,3},{1,5},{3,7},{12,8},{14,10},{8,... | collective-permute-start | bytes 491528 | tf_op jit(solution)/shard_map/ppermute | solution.py:22
  25.9 7.5 %collective-permute-start.5 = (bf16[16,5120]{1,0:T(8,128)(2,1)S(1)}, bf16[16,5120]{1,0:T(8,128)(2,1)S(1)}, u32[]{:S(2)}, u32[]{:S(2)}) collective-permute-start(bf16[16,5120]{1,0:T(8,128)(2,1)S(1)} %get-tuple-element.48), channel_id=1, source_target_pairs={{6,0},{0,2},{2,4},{4,6},{7,1},{1,3},{3,5},{5,7},{14,8},{8,10},{10,... | collective-permute-start | bytes 491528 | tf_op jit(solution)/shard_map/ppermute | solution.py:22
  33.9 4.8 %collective-permute-start.9 = (bf16[16,5120]{1,0:T(8,128)(2,1)S(1)}, bf16[16,5120]{1,0:T(8,128)(2,1)S(1)}, u32[]{:S(2)}, u32[]{:S(2)}) collective-permute-start(bf16[16,5120]{1,0:T(8,128)(2,1)S(1)} %get-tuple-element.51), channel_id=1, source_target_pairs={{24,0},{0,8},{8,16},{16,24},{25,1},{1,9},{9,17},{17,25},{26,2},{2,... | collective-permute-start | bytes 491528 | tf_op jit(solution)/shard_map/ppermute | solution.py:22
  35.4 6.7 %collective-permute-start.14 = (bf16[16,5120]{1,0:T(8,128)(2,1)S(1)}, bf16[16,5120]{1,0:T(8,128)(2,1)S(1)}, u32[]{:S(2)}, u32[]{:S(2)}) collective-permute-start(bf16[16,5120]{1,0:T(8,128)(2,1)S(1)} %shard_map.115.refs_4_), channel_id=1, source_target_pairs={{6,0},{0,2},{2,4},{4,6},{7,1},{1,3},{3,5},{5,7},{14,8},{8,10},{10,... | collective-permute-start | bytes 491528 | tf_op jit(solution)/shard_map/ppermute | solution.py:22
  38.2 7.6 %collective-permute-start.15 = (bf16[16,5120]{1,0:T(8,128)(2,1)S(1)}, bf16[16,5120]{1,0:T(8,128)(2,1)S(1)}, u32[]{:S(2)}, u32[]{:S(2)}) collective-permute-start(bf16[16,5120]{1,0:T(8,128)(2,1)S(1)} %shard_map.115.refs_4_), channel_id=1, source_target_pairs={{4,0},{6,2},{0,4},{2,6},{5,1},{7,3},{1,5},{3,7},{12,8},{14,10},{8,... | collective-permute-start | bytes 491528 | tf_op jit(solution)/shard_map/ppermute | solution.py:22
  38.4 8.9 %collective-permute-start.16 = (bf16[16,5120]{1,0:T(8,128)(2,1)S(1)}, bf16[16,5120]{1,0:T(8,128)(2,1)S(1)}, u32[]{:S(2)}, u32[]{:S(2)}) collective-permute-start(bf16[16,5120]{1,0:T(8,128)(2,1)S(1)} %shard_map.115.refs_4_), channel_id=1, source_target_pairs={{2,0},{4,2},{6,4},{0,6},{3,1},{5,3},{7,5},{1,7},{10,8},{12,10},{14... | collective-permute-start | bytes 491528 | tf_op jit(solution)/shard_map/ppermute | solution.py:22
  38.6 35.4 %slice-start = ((s8[5242880]{0:T(1024)(128)(4,1)}), s8[4194304]{0:T(1024)(128)(4,1)S(1)}, s32[]{:S(2)}) async-start(s8[5242880]{0:T(1024)(128)(4,1)} %bitcast.11), calls=%async_computation | async-start | bytes 8388608
  38.8 35.2 %slice-start.1 = ((s8[5242880]{0:T(1024)(128)(4,1)}), s8[1048576]{0:T(1024)(128)(4,1)S(1)}, s32[]{:S(2)}) async-start(s8[5242880]{0:T(1024)(128)(4,1)} %bitcast.11), calls=%async_computation.1 | async-start | bytes 2097152
  38.8 9.8 %collective-permute-start.10 = (bf16[16,5120]{1,0:T(8,128)(2,1)S(1)}, bf16[16,5120]{1,0:T(8,128)(2,1)S(1)}, u32[]{:S(2)}, u32[]{:S(2)}) collective-permute-start(bf16[16,5120]{1,0:T(8,128)(2,1)S(1)} %shard_map.114.refs_0_), channel_id=1, source_target_pairs={{6,0},{0,2},{2,4},{4,6},{7,1},{1,3},{3,5},{5,7},{14,8},{8,10},{10,... | collective-permute-start | bytes 491528 | tf_op jit(solution)/shard_map/ppermute | solution.py:22
  41.9 10.9 %collective-permute-start.11 = (bf16[16,5120]{1,0:T(8,128)(2,1)S(1)}, bf16[16,5120]{1,0:T(8,128)(2,1)S(1)}, u32[]{:S(2)}, u32[]{:S(2)}) collective-permute-start(bf16[16,5120]{1,0:T(8,128)(2,1)S(1)} %shard_map.114.refs_0_), channel_id=1, source_target_pairs={{4,0},{6,2},{0,4},{2,6},{5,1},{7,3},{1,5},{3,7},{12,8},{14,10},{8,... | collective-permute-start | bytes 491528 | tf_op jit(solution)/shard_map/ppermute | solution.py:22
  42.1 11.2 %collective-permute-start.12 = (bf16[16,5120]{1,0:T(8,128)(2,1)S(1)}, bf16[16,5120]{1,0:T(8,128)(2,1)S(1)}, u32[]{:S(2)}, u32[]{:S(2)}) collective-permute-start(bf16[16,5120]{1,0:T(8,128)(2,1)S(1)} %shard_map.114.refs_0_), channel_id=1, source_target_pairs={{2,0},{4,2},{6,4},{0,6},{3,1},{5,3},{7,5},{1,7},{10,8},{12,10},{14... | collective-permute-start | bytes 491528 | tf_op jit(solution)/shard_map/ppermute | solution.py:22
  62.8 28.7 %copy-start.1 = (bf16[128,5120]{1,0:T(8,128)(2,1)S(1)}, bf16[128,5120]{1,0:T(8,128)(2,1)}, u32[]{:S(2)}) copy-start(bf16[128,5120]{1,0:T(8,128)(2,1)} %tokens.3) | copy-start | bytes 3932164
  62.8 33.6 %copy-start.3 = (bf16[128,5120]{1,0:T(8,128)(2,1)S(1)}, bf16[128,5120]{1,0:T(8,128)(2,1)}, u32[]{:S(2)}) copy-start(bf16[128,5120]{1,0:T(8,128)(2,1)} %cotangent.1) | copy-start | bytes 3932164
  62.8 6.8 %collective-permute-start.17 = (bf16[16,5120]{1,0:T(8,128)(2,1)S(1)}, bf16[16,5120]{1,0:T(8,128)(2,1)S(1)}, u32[]{:S(2)}, u32[]{:S(2)}) collective-permute-start(bf16[16,5120]{1,0:T(8,128)(2,1)S(1)} %get-tuple-element.54), channel_id=1, source_target_pairs={{2,0},{4,2},{6,4},{0,6},{3,1},{5,3},{7,5},{1,7},{10,8},{12,10},{14... | collective-permute-start | bytes 491528 | tf_op jit(solution)/shard_map/ppermute | solution.py:22
  62.9 7.9 %collective-permute-start.18 = (bf16[16,5120]{1,0:T(8,128)(2,1)S(1)}, bf16[16,5120]{1,0:T(8,128)(2,1)S(1)}, u32[]{:S(2)}, u32[]{:S(2)}) collective-permute-start(bf16[16,5120]{1,0:T(8,128)(2,1)S(1)} %get-tuple-element.55), channel_id=1, source_target_pairs={{4,0},{6,2},{0,4},{2,6},{5,1},{7,3},{1,5},{3,7},{12,8},{14,10},{8,... | collective-permute-start | bytes 491528 | tf_op jit(solution)/shard_map/ppermute | solution.py:22
  64.2 7.1 %collective-permute-start.19 = (bf16[16,5120]{1,0:T(8,128)(2,1)S(1)}, bf16[16,5120]{1,0:T(8,128)(2,1)S(1)}, u32[]{:S(2)}, u32[]{:S(2)}) collective-permute-start(bf16[16,5120]{1,0:T(8,128)(2,1)S(1)} %get-tuple-element.56), channel_id=1, source_target_pairs={{6,0},{0,2},{2,4},{4,6},{7,1},{1,3},{3,5},{5,7},{14,8},{8,10},{10,... | collective-permute-start | bytes 491528 | tf_op jit(solution)/shard_map/ppermute | solution.py:22
  66.1 9.3 %collective-permute-start.30 = (bf16[16,5120]{1,0:T(8,128)(2,1)S(1)}, bf16[16,5120]{1,0:T(8,128)(2,1)S(1)}, u32[]{:S(2)}, u32[]{:S(2)}) collective-permute-start(bf16[16,5120]{1,0:T(8,128)(2,1)S(1)} %get-tuple-element.65), channel_id=1, source_target_pairs={{16,0},{24,8},{0,16},{8,24},{17,1},{25,9},{1,17},{9,25},{18,2},{26... | collective-permute-start | bytes 491528 | tf_op jit(solution)/shard_map/ppermute | solution.py:22
  68.2 6.9 %collective-permute-start.39 = (bf16[64,512]{1,0:T(8,128)(2,1)S(1)}, bf16[64,512]{1,0:T(8,128)(2,1)S(1)}, u32[]{:S(2)}, u32[]{:S(2)}) collective-permute-start(bf16[64,512]{1,0:T(8,128)(2,1)S(1)} %get-tuple-element.75.refs_8_), channel_id=1, source_target_pairs={{1,0},{0,1},{3,2},{2,3},{5,4},{4,5},{7,6},{6,7},{9,8},{8,9},{11,10... | collective-permute-start | bytes 196616 | tf_op jit(solution)/shard_map/ppermute | solution.py:22
  69.6 7.7 %collective-permute-start.40 = (bf16[64,512]{1,0:T(8,128)(2,1)S(1)}, bf16[64,512]{1,0:T(8,128)(2,1)S(1)}, u32[]{:S(2)}, u32[]{:S(2)}) collective-permute-start(bf16[64,512]{1,0:T(8,128)(2,1)S(1)} %get-tuple-element.66.act.refs_10_), channel_id=1, source_target_pairs={{1,0},{0,1},{3,2},{2,3},{5,4},{4,5},{7,6},{6,7},{9,8},{8,9},{11,10... | collective-permute-start | bytes 196616 | tf_op jit(solution)/shard_map/ppermute | solution.py:22
  71.8 24.7 %collective-permute-start.20 = (bf16[16,5120]{1,0:T(8,128)(2,1)S(1)}, bf16[16,5120]{1,0:T(8,128)(2,1)S(1)}, u32[]{:S(2)}, u32[]{:S(2)}) collective-permute-start(bf16[16,5120]{1,0:T(8,128)(2,1)S(1)} %get-tuple-element.57), channel_id=1, source_target_pairs={{8,0},{16,8},{24,16},{0,24},{9,1},{17,9},{25,17},{1,25},{10,2},{18... | collective-permute-start | bytes 491528 | tf_op jit(solution)/shard_map/ppermute | solution.py:22
  72.8 5.7 %collective-permute-start.42 = (bf16[64,512]{1,0:T(8,128)(2,1)S(1)}, bf16[64,512]{1,0:T(8,128)(2,1)S(1)}, u32[]{:S(2)}, u32[]{:S(2)}) collective-permute-start(bf16[64,512]{1,0:T(8,128)(2,1)S(1)} %get-tuple-element.77.refs_14_), channel_id=1, source_target_pairs={{1,0},{0,1},{3,2},{2,3},{5,4},{4,5},{7,6},{6,7},{9,8},{8,9},{11,10... | collective-permute-start | bytes 196616 | tf_op jit(solution)/shard_map/ppermute | solution.py:22
  75.1 45.2 %collective-permute-start.35 = (bf16[64,5120]{1,0:T(8,128)(2,1)S(1)}, bf16[64,5120]{1,0:T(8,128)(2,1)S(1)}, u32[]{:S(2)}, u32[]{:S(2)}) collective-permute-start(bf16[64,5120]{1,0:T(8,128)(2,1)S(1)} %get-tuple-element.71.refs_0_), channel_id=1, source_target_pairs={{1,0},{0,1},{3,2},{2,3},{5,4},{4,5},{7,6},{6,7},{9,8},{8,9},{11,10... | collective-permute-start | bytes 1966088 | tf_op jit(solution)/shard_map/ppermute | solution.py:22
  75.4 21.3 %collective-permute-start.31 = (bf16[16,5120]{1,0:T(8,128)(2,1)S(1)}, bf16[16,5120]{1,0:T(8,128)(2,1)S(1)}, u32[]{:S(2)}, u32[]{:S(2)}) collective-permute-start(bf16[16,5120]{1,0:T(8,128)(2,1)S(1)} %get-tuple-element.68), channel_id=1, source_target_pairs={{2,0},{4,2},{6,4},{0,6},{3,1},{5,3},{7,5},{1,7},{10,8},{12,10},{14... | collective-permute-start | bytes 491528 | tf_op jit(solution)/shard_map/ppermute | solution.py:22
  77.3 22.7 %collective-permute-start.32 = (bf16[16,5120]{1,0:T(8,128)(2,1)S(1)}, bf16[16,5120]{1,0:T(8,128)(2,1)S(1)}, u32[]{:S(2)}, u32[]{:S(2)}) collective-permute-start(bf16[16,5120]{1,0:T(8,128)(2,1)S(1)} %get-tuple-element.69), channel_id=1, source_target_pairs={{4,0},{6,2},{0,4},{2,6},{5,1},{7,3},{1,5},{3,7},{12,8},{14,10},{8,... | collective-permute-start | bytes 491528 | tf_op jit(solution)/shard_map/ppermute | solution.py:22
  78.5 12.9 %collective-permute-start.44 = (bf16[64,512]{1,0:T(8,128)(2,1)S(1)}, bf16[64,512]{1,0:T(8,128)(2,1)S(1)}, u32[]{:S(2)}, u32[]{:S(2)}) collective-permute-start(bf16[64,512]{1,0:T(8,128)(2,1)S(1)} %get-tuple-element.79.refs_18_), channel_id=1, source_target_pairs={{1,0},{0,1},{3,2},{2,3},{5,4},{4,5},{7,6},{6,7},{9,8},{8,9},{11,10... | collective-permute-start | bytes 196616 | tf_op jit(solution)/shard_map/ppermute | solution.py:22
  91.5 130.7 %collective-permute-start.29 = (bf16[128,5120]{1,0:T(8,128)(2,1)S(1)}, bf16[128,5120]{1,0:T(8,128)(2,1)S(1)}, u32[]{:S(2)}, u32[]{:S(2)}) collective-permute-start(bf16[128,5120]{1,0:T(8,128)(2,1)S(1)} %copy-done.1), channel_id=1, source_target_pairs={{16,0},{24,8},{0,16},{8,24},{17,1},{25,9},{1,17},{9,25},{18,2},{26... | collective-permute-start | bytes 3932168 | tf_op jit(solution)/shard_map/ppermute | solution.py:22
  96.4 126.3 %collective-permute-start.28 = (bf16[128,5120]{1,0:T(8,128)(2,1)S(1)}, bf16[128,5120]{1,0:T(8,128)(2,1)S(1)}, u32[]{:S(2)}, u32[]{:S(2)}) collective-permute-start(bf16[128,5120]{1,0:T(8,128)(2,1)S(1)} %copy-done.3), channel_id=1, source_target_pairs={{16,0},{24,8},{0,16},{8,24},{17,1},{25,9},{1,17},{9,25},{18,2},{26... | collective-permute-start | bytes 3932168 | tf_op jit(solution)/shard_map/ppermute | solution.py:22
  96.8 5.5 %collective-permute-start.33 = (bf16[16,5120]{1,0:T(8,128)(2,1)S(1)}, bf16[16,5120]{1,0:T(8,128)(2,1)S(1)}, u32[]{:S(2)}, u32[]{:S(2)}) collective-permute-start(bf16[16,5120]{1,0:T(8,128)(2,1)S(1)} %get-tuple-element.70), channel_id=1, source_target_pairs={{6,0},{0,2},{2,4},{4,6},{7,1},{1,3},{3,5},{5,7},{14,8},{8,10},{10,... | collective-permute-start | bytes 491528 | tf_op jit(solution)/shard_map/ppermute | solution.py:22
  100.0 4.0 %collective-permute-start.21 = (bf16[16,5120]{1,0:T(8,128)(2,1)S(1)}, bf16[16,5120]{1,0:T(8,128)(2,1)S(1)}, u32[]{:S(2)}, u32[]{:S(2)}) collective-permute-start(bf16[16,5120]{1,0:T(8,128)(2,1)S(1)} %shard_map.118.refs_0_), channel_id=1, source_target_pairs={{6,0},{0,2},{2,4},{4,6},{7,1},{1,3},{3,5},{5,7},{14,8},{8,10},{10,... | collective-permute-start | bytes 491528 | tf_op jit(solution)/shard_map/ppermute | solution.py:22
  102.2 5.5 %collective-permute-start.22 = (bf16[16,5120]{1,0:T(8,128)(2,1)S(1)}, bf16[16,5120]{1,0:T(8,128)(2,1)S(1)}, u32[]{:S(2)}, u32[]{:S(2)}) collective-permute-start(bf16[16,5120]{1,0:T(8,128)(2,1)S(1)} %shard_map.118.refs_0_), channel_id=1, source_target_pairs={{4,0},{6,2},{0,4},{2,6},{5,1},{7,3},{1,5},{3,7},{12,8},{14,10},{8,... | collective-permute-start | bytes 491528 | tf_op jit(solution)/shard_map/ppermute | solution.py:22
  104.0 7.3 %collective-permute-start.23 = (bf16[16,5120]{1,0:T(8,128)(2,1)S(1)}, bf16[16,5120]{1,0:T(8,128)(2,1)S(1)}, u32[]{:S(2)}, u32[]{:S(2)}) collective-permute-start(bf16[16,5120]{1,0:T(8,128)(2,1)S(1)} %shard_map.118.refs_0_), channel_id=1, source_target_pairs={{2,0},{4,2},{6,4},{0,6},{3,1},{5,3},{7,5},{1,7},{10,8},{12,10},{14... | collective-permute-start | bytes 491528 | tf_op jit(solution)/shard_map/ppermute | solution.py:22
  107.7 107.7 %collective-permute-start.34 = (bf16[16,5120]{1,0:T(8,128)(2,1)S(1)}, bf16[16,5120]{1,0:T(8,128)(2,1)S(1)}, u32[]{:S(2)}, u32[]{:S(2)}) collective-permute-start(bf16[16,5120]{1,0:T(8,128)(2,1)S(1)} %shard_map.122), channel_id=1, source_target_pairs={{24,0},{0,8},{8,16},{16,24},{25,1},{1,9},{9,17},{17,25},{26,2},{2,... | collective-permute-start | bytes 491528 | tf_op jit(solution)/shard_map/ppermute | solution.py:22
  111.3 104.2 %collective-permute-start.27 = (bf16[16,5120]{1,0:T(8,128)(2,1)S(1)}, bf16[16,5120]{1,0:T(8,128)(2,1)S(1)}, u32[]{:S(2)}, u32[]{:S(2)}) collective-permute-start(bf16[16,5120]{1,0:T(8,128)(2,1)S(1)} %get-tuple-element.64), channel_id=1, source_target_pairs={{8,0},{16,8},{24,16},{0,24},{9,1},{17,9},{25,17},{1,25},{10,2},{18... | collective-permute-start | bytes 491528 | tf_op jit(solution)/shard_map/ppermute | solution.py:22
  120.3 98.1 %collective-permute-start.24 = (bf16[16,5120]{1,0:T(8,128)(2,1)S(1)}, bf16[16,5120]{1,0:T(8,128)(2,1)S(1)}, u32[]{:S(2)}, u32[]{:S(2)}) collective-permute-start(bf16[16,5120]{1,0:T(8,128)(2,1)S(1)} %get-tuple-element.61), channel_id=1, source_target_pairs={{2,0},{4,2},{6,4},{0,6},{3,1},{5,3},{7,5},{1,7},{10,8},{12,10},{14... | collective-permute-start | bytes 491528 | tf_op jit(solution)/shard_map/ppermute | solution.py:22
  215.4 4.2 %collective-permute-start.25 = (bf16[16,5120]{1,0:T(8,128)(2,1)S(1)}, bf16[16,5120]{1,0:T(8,128)(2,1)S(1)}, u32[]{:S(2)}, u32[]{:S(2)}) collective-permute-start(bf16[16,5120]{1,0:T(8,128)(2,1)S(1)} %get-tuple-element.62), channel_id=1, source_target_pairs={{4,0},{6,2},{0,4},{2,6},{5,1},{7,3},{1,5},{3,7},{12,8},{14,10},{8,... | collective-permute-start | bytes 491528 | tf_op jit(solution)/shard_map/ppermute | solution.py:22
  215.4 5.8 %collective-permute-start.26 = (bf16[16,5120]{1,0:T(8,128)(2,1)S(1)}, bf16[16,5120]{1,0:T(8,128)(2,1)S(1)}, u32[]{:S(2)}, u32[]{:S(2)}) collective-permute-start(bf16[16,5120]{1,0:T(8,128)(2,1)S(1)} %get-tuple-element.63), channel_id=1, source_target_pairs={{6,0},{0,2},{2,4},{4,6},{7,1},{1,3},{3,5},{5,7},{14,8},{8,10},{10,... | collective-permute-start | bytes 491528 | tf_op jit(solution)/shard_map/ppermute | solution.py:22
  218.4 46.3 %collective-permute-start.36 = (bf16[64,5120]{1,0:T(8,128)(2,1)S(1)}, bf16[64,5120]{1,0:T(8,128)(2,1)S(1)}, u32[]{:S(2)}, u32[]{:S(2)}) collective-permute-start(bf16[64,5120]{1,0:T(8,128)(2,1)S(1)} %get-tuple-element.72.refs_2_), channel_id=1, source_target_pairs={{1,0},{0,1},{3,2},{2,3},{5,4},{4,5},{7,6},{6,7},{9,8},{8,9},{11,10... | collective-permute-start | bytes 1966088 | tf_op jit(solution)/shard_map/ppermute | solution.py:22
  219.6 45.0 %collective-permute-start.38 = (bf16[64,5120]{1,0:T(8,128)(2,1)S(1)}, bf16[64,5120]{1,0:T(8,128)(2,1)S(1)}, u32[]{:S(2)}, u32[]{:S(2)}) collective-permute-start(bf16[64,5120]{1,0:T(8,128)(2,1)S(1)} %get-tuple-element.74.refs_6_), channel_id=1, source_target_pairs={{1,0},{0,1},{3,2},{2,3},{5,4},{4,5},{7,6},{6,7},{9,8},{8,9},{11,10... | collective-permute-start | bytes 1966088 | tf_op jit(solution)/shard_map/ppermute | solution.py:22
  221.2 43.4 %collective-permute-start.37 = (bf16[64,5120]{1,0:T(8,128)(2,1)S(1)}, bf16[64,5120]{1,0:T(8,128)(2,1)S(1)}, u32[]{:S(2)}, u32[]{:S(2)}) collective-permute-start(bf16[64,5120]{1,0:T(8,128)(2,1)S(1)} %get-tuple-element.73.refs_4_), channel_id=1, source_target_pairs={{1,0},{0,1},{3,2},{2,3},{5,4},{4,5},{7,6},{6,7},{9,8},{8,9},{11,10... | collective-permute-start | bytes 1966088 | tf_op jit(solution)/shard_map/ppermute | solution.py:22
  222.1 41.8 %collective-permute-start.41 = (bf16[64,512]{1,0:T(8,128)(2,1)S(1)}, bf16[64,512]{1,0:T(8,128)(2,1)S(1)}, u32[]{:S(2)}, u32[]{:S(2)}) collective-permute-start(bf16[64,512]{1,0:T(8,128)(2,1)S(1)} %get-tuple-element.76.refs_12_), channel_id=1, source_target_pairs={{1,0},{0,1},{3,2},{2,3},{5,4},{4,5},{7,6},{6,7},{9,8},{8,9},{11,10... | collective-permute-start | bytes 196616 | tf_op jit(solution)/shard_map/ppermute | solution.py:22
  222.7 41.9 %collective-permute-start.43 = (bf16[64,512]{1,0:T(8,128)(2,1)S(1)}, bf16[64,512]{1,0:T(8,128)(2,1)S(1)}, u32[]{:S(2)}, u32[]{:S(2)}) collective-permute-start(bf16[64,512]{1,0:T(8,128)(2,1)S(1)} %get-tuple-element.78.refs_16_), channel_id=1, source_target_pairs={{1,0},{0,1},{3,2},{2,3},{5,4},{4,5},{7,6},{6,7},{9,8},{8,9},{11,10... | collective-permute-start | bytes 196616 | tf_op jit(solution)/shard_map/ppermute | solution.py:22

commit v2 on v1

v2 whole, which is shorter than its diff:
```python
import functools

import jax
import jax.numpy as jnp
from jax import lax
from jax.experimental import pallas as pl
from jax.experimental.pallas import tpu as pltpu
from jax.sharding import PartitionSpec as P

CAP = 10
PACK = 8
PACKED = CAP * PACK
FIRST = 64
SECOND = 16
EPSILON = 1e-06
F32 = jnp.float32
BF16 = jnp.bfloat16
VMEM_BIG = 48 * 1024 * 1024
VMEM_SMALL = 24 * 1024 * 1024
COST_BYTES = 1024


def shifted(block, axis, distance):
    size = lax.axis_size(axis)
    return lax.ppermute(block, axis, [((i - distance) % size, i) for i in range(size)])


def dot(a, b, ca=1, cb=0):
    return lax.dot_general(a, b, (((ca,), (cb,)), ((), ())), preferred_element_type=F32)


def call(
    kernel, outs, args, *, any_args=(), any_outs=(), scratch=(), vmem=VMEM_SMALL, flops=0
):
    outs = [jax.ShapeDtypeStruct(s, d) for s, d in outs]
    anywhere = pl.BlockSpec(memory_space=pl.ANY)
    near = pl.BlockSpec(memory_space=pltpu.VMEM)
    return pl.pallas_call(
        kernel,
        out_shape=outs,
        in_specs=[anywhere if i in any_args else near for i in range(len(args))],
        out_specs=[anywhere if i in any_outs else near for i in range(len(outs))],
        scratch_shapes=list(scratch),
        compiler_params=pltpu.CompilerParams(vmem_limit_bytes=vmem),
        cost_estimate=pl.CostEstimate(flops=flops, bytes_accessed=COST_BYTES, transcendentals=0),
    )(*args)


def packed_index(shape, dim):
    place = lax.broadcasted_iota(jnp.int32, shape, dim).astype(F32)
    chunk = jnp.floor((place + 0.5) * (1.0 / CAP))
    return place - CAP * chunk, chunk


def select_of(routes):
    hits = (routes == 0).astype(F32)
    marked = jnp.sum(hits, axis=0, keepdims=True)
    rows = routes.shape[1]
    before = lax.broadcasted_iota(jnp.int32, (rows, rows), 0) < lax.broadcasted_iota(
        jnp.int32, (rows, rows), 1
    )
    wide = jnp.broadcast_to(marked, (PACKED, rows))
    places = dot(wide.astype(BF16), before.astype(F32).astype(BF16))
    slot, _ = packed_index((PACKED, rows), 0)
    return jnp.where((places == slot) & (wide > 0.5), 1.0, 0.0)


def slot_gates(select, routes, gates):
    weights = jnp.sum(jnp.where(routes == 0, gates, 0.0), axis=0, keepdims=True)
    return jnp.sum(select * weights, axis=1, keepdims=True)


def chunk_of(select, c):
    _, chunk = packed_index(select.shape, 0)
    return jnp.where(chunk == c, select, 0.0).astype(BF16)


def columns(c, width):
    return slice(c * (width // PACK), (c + 1) * (width // PACK))


def pick(select, rows):
    total = None
    at = 0
    for block in rows:
        end = at + block.shape[0]
        for c in range(PACK):
            part = dot(chunk_of(select[:, at:end], c), block[:, columns(c, block.shape[1])])
            total = part if total is None else total + part
        at = end
    return total


def over_chunks(row_sums):
    slot_r, _ = packed_index((PACKED, PACKED), 0)
    slot_c, _ = packed_index((PACKED, PACKED), 1)
    same = jnp.where(slot_r == slot_c, 1.0, 0.0)
    wide = jnp.broadcast_to(row_sums, (PACKED, 128))
    return jnp.dot(
        same, wide, precision=lax.Precision.HIGHEST, preferred_element_type=F32
    )[:, :1]


def mean_of(values):
    return over_chunks(jnp.sum(values, axis=-1, keepdims=True)) * (1.0 / (PACK * values.shape[1]))


def inv_rms_of(values):
    return lax.rsqrt(mean_of(values * values) + EPSILON)


def merged(select_to, select_from, fresh, old):
    same = dot(select_to.astype(BF16), select_from.astype(BF16), 1, 1)
    _, chunk_r = packed_index(same.shape, 0)
    _, chunk_c = packed_index(same.shape, 1)
    same = jnp.where(chunk_r == chunk_c, same, 0.0)
    taken = jnp.sum(same, axis=1, keepdims=True)
    return jnp.where(taken > 0.5, dot(same.astype(BF16), fresh), old).astype(BF16)


def summed(parts):
    total = parts[0][...].astype(F32)
    for p in parts[1:]:
        total = total + p[...].astype(F32)
    return total


def place_rows(bulk, first, rows1, second, rows2, out):
    ones = jnp.ones((PACKED, 128), BF16)
    hit1 = dot(chunk_of(first, 0), ones, 0, 0)[:, :1] > 0.5
    hit2 = dot(chunk_of(second, 0), ones, 0, 0)[:, :1] > 0.5
    width = out.shape[1]
    for c in range(PACK):
        k = columns(c, width)
        new1 = dot(chunk_of(first, c), rows1, 0, 0)
        new2 = dot(chunk_of(second, c), rows2, 0, 0)
        at = 0
        for block in bulk:
            r = slice(at, at + block.shape[0])
            at = r.stop
            value = jnp.where(hit1[r], new1[r], block[:, k].astype(F32))
            out[r, k] = jnp.where(hit2[r], new2[r], value).astype(BF16)


def first_rows_kernel(tokens, routes, cotangent, raw, normed, piece, sem):
    copy = pltpu.make_async_copy(cotangent.at[pl.ds(0, FIRST)], piece, sem)
    copy.start()
    values = pick(select_of(routes[0]), [tokens])
    raw[...] = values.astype(BF16)
    normed[...] = (values * inv_rms_of(values)).astype(BF16)
    copy.wait()


def other_rows_kernel(tokens, cotangent, next_routes, prev_routes, t1, cot):
    t1[...] = pick(select_of(next_routes[0]), [tokens]).astype(BF16)
    cot[...] = pick(select_of(prev_routes[0]), [cotangent]).astype(BF16)


def update0_kernel(n, *refs):
    parts, (raw, routes, gates, next_routes, t1, tokens) = refs[:n], refs[n : n + 6]
    upd, onward, piece, sem = refs[n + 9 :]
    copy = pltpu.make_async_copy(tokens.at[pl.ds(0, SECOND)], piece, sem)
    copy.start()
    select = select_of(routes[0])
    weight = slot_gates(select, routes[0], gates[0])
    fresh = (raw[...].astype(F32) + weight * summed(parts)).astype(BF16)
    onward[...] = merged(select_of(next_routes[0]), select, fresh, t1[...].astype(F32))
    upd[...] = fresh
    copy.wait()


def update1_kernel(n, *refs):
    parts, (h, routes, gates, upd) = refs[:n], refs[n:]
    select = select_of(routes[1])
    weight = slot_gates(select, routes[1], gates[1])
    upd[...] = (h[...].astype(F32) + weight * summed(parts)).astype(BF16)


def enter1_kernel(h, cot, routes, gates, cotangent, _, out, piece, sem):
    rows = cotangent.shape[0]
    copy = pltpu.make_async_copy(cotangent.at[pl.ds(FIRST, rows - FIRST)], piece, sem)
    copy.start()
    values = h[...].astype(F32)
    out[:PACKED] = (values * inv_rms_of(values)).astype(BF16)
    weight = slot_gates(select_of(routes[1]), routes[1], gates[1])
    out[PACKED:] = (weight * cot[...].astype(F32)).astype(BF16)
    copy.wait()


def state_grad(parts, h, c):
    total = summed(parts)
    values = h.astype(F32)
    inv = inv_rms_of(values)
    inner = mean_of(total * values)
    return (c.astype(F32) + inv * total - inv * inv * inv * values * inner).astype(BF16)


def grad1_kernel(n, *refs):
    parts, (h, cot, tokens) = refs[:n], refs[n : n + 3]
    upd, piece, sem = refs[n + 5 :]
    copy = pltpu.make_async_copy(tokens.at[pl.ds(SECOND, SECOND)], piece, sem)
    copy.start()
    upd[...] = state_grad(parts, h[...], cot[...])
    copy.wait()


def enter0_kernel(
    upd1, next_routes, routes, gates, bulk_a, bulk_b, tokens, _, c0, out, piece, sem
):
    left = tokens.shape[0] - 2 * SECOND
    copy = pltpu.make_async_copy(tokens.at[pl.ds(2 * SECOND, left)], piece, sem)
    copy.start()
    select = select_of(routes[0])
    old = pick(select, [bulk_a, bulk_b])
    rows = merged(select, select_of(next_routes[0]), upd1[...], old)
    c0[...] = rows
    out[...] = (slot_gates(select, routes[0], gates[0]) * rows.astype(F32)).astype(BF16)
    copy.wait()


def finish_grad_kernel(n, *refs):
    parts, (h, c, routes, upd1, next_routes, bulk_a, bulk_b, out) = refs[:n], refs[n:]
    fresh = state_grad(parts, h[...], c[...])
    place_rows(
        [bulk_a, bulk_b], select_of(next_routes[0]), upd1[...], select_of(routes[0]), fresh, out
    )


def finish_state_kernel(
    bulk_a, bulk_b, bulk_c, upd0, prev2_routes, upd1, prev_routes, out
):
    place_rows(
        [bulk_a, bulk_b, bulk_c],
        select_of(prev2_routes[0]),
        upd0[...],
        select_of(prev_routes[0]),
        upd1[...],
        out,
    )


def silu_grads(pre_gate, pre_up, grad_act):
    sig = jax.nn.sigmoid(pre_gate)
    grad_gate = (grad_act * pre_up * sig * (1.0 + pre_gate * (1.0 - sig))).astype(BF16)
    grad_up = (grad_act * (pre_gate * sig)).astype(BF16)
    return grad_gate, grad_up


def weight_copies(gate, up, down, gate_v, up_v, down_v, sems):
    out = []
    step = gate.shape[0] // PACK
    for c in range(PACK):
        r = pl.ds(c * step, step)
        out.append(
            (
                pltpu.make_async_copy(gate.at[r], gate_v.at[r], sems.at[0, c]),
                pltpu.make_async_copy(up.at[r], up_v.at[r], sems.at[1, c]),
                pltpu.make_async_copy(down.at[:, r], down_v.at[:, r], sems.at[2, c]),
            )
        )
    return out


def gather_rows(blocks, first, unpacked, whole32, whole):
    width = whole.shape[1]
    used = len(blocks) * CAP
    if used < whole.shape[0]:
        whole32[used:] = jnp.zeros((whole.shape[0] - used, width), F32)
    for i, b in enumerate(blocks):
        unpacked[i] = b[first : first + PACKED].astype(F32)
        for c in range(PACK):
            whole32[i * CAP : (i + 1) * CAP, columns(c, width)] = unpacked[
                i, c * CAP : (c + 1) * CAP
            ]
    whole[...] = whole32[...].astype(BF16)


def spread_rows(value, c, n, held, unpacked):
    held[...] = value
    for i in range(n):
        unpacked[i, c * CAP : (c + 1) * CAP] = held[i * CAP : (i + 1) * CAP]


def forward_kernel(n, *refs):
    blocks, (gate, up, down, _) = refs[:n], refs[n : n + 4]
    x, pre_gate, pre_up, act = refs[n + 4 : n + 8]
    parts = refs[n + 8 : 2 * n + 8]
    gate_v, up_v, down_v, sems, unpacked, whole32, held = refs[2 * n + 8 :]
    copies = weight_copies(gate, up, down, gate_v, up_v, down_v, sems)
    for cg, cu, _ in copies:
        cg.start()
        cu.start()
    for _, _, cd in copies:
        cd.start()
    gather_rows(blocks, 0, unpacked, whole32, x)
    acc_g = jnp.zeros(pre_gate.shape, F32)
    acc_u = jnp.zeros(pre_up.shape, F32)
    width = gate.shape[0]
    for c, (cg, cu, _) in enumerate(copies):
        k = columns(c, width)
        cg.wait()
        acc_g = acc_g + dot(x[:, k], gate_v[k])
        cu.wait()
        acc_u = acc_u + dot(x[:, k], up_v[k])
    pre_gate[...] = acc_g
    pre_up[...] = acc_u
    activated = (acc_g * jax.nn.sigmoid(acc_g) * acc_u).astype(BF16)
    act[...] = activated
    for c, (_, _, cd) in enumerate(copies):
        cd.wait()
        spread_rows(dot(activated, down_v[:, columns(c, width)]), c, n, held.at[c], unpacked)
    for i, p in enumerate(parts):
        p[...] = unpacked[i].astype(BF16)


def down_kernel(n, act, down, _, *refs):
    parts, (unpacked, held) = refs[:n], refs[n:]
    hidden = down.shape[0]
    for c in range(PACK):
        value = dot(act[:, hidden : 2 * hidden], down[:, columns(c, down.shape[1])])
        spread_rows(value, c, n, held.at[c], unpacked)
    for i, p in enumerate(parts):
        p[...] = unpacked[i].astype(BF16)


def back_rows(gg, gu, gate_v, up_v, held, unpacked, parts):
    n = len(parts)
    for c in range(PACK):
        k = columns(c, gate_v.shape[0])
        value = dot(gg, gate_v[k], 1, 1) + dot(gu, up_v[k], 1, 1)
        spread_rows(value, c, n, held.at[c], unpacked)
    for i, p in enumerate(parts):
        p[...] = unpacked[i].astype(BF16)


def tick1_kernel(n, *refs):
    blocks, (act0, gate, up, down, _) = refs[:n], refs[n : n + 5]
    xg, small = refs[n + 5 : n + 7]
    parts = refs[n + 7 : 2 * n + 7]
    gate_v, up_v, down_v, sems, unpacked, whole32, held, x, g = refs[2 * n + 7 :]
    copies = weight_copies(gate, up, down, gate_v, up_v, down_v, sems)
    for three in copies:
        for c in three:
            c.start()
    gather_rows(blocks, 0, unpacked, whole32.at[0], x)
    gather_rows(blocks, PACKED, unpacked, whole32.at[1], g)
    rows, hidden = act0.shape
    xg[:rows] = x[...]
    xg[rows:] = g[...]
    width = gate.shape[0]
    acc_g = jnp.zeros(act0.shape, F32)
    acc_u = jnp.zeros(act0.shape, F32)
    acc_a = jnp.zeros(act0.shape, F32)
    for c, (cg, cu, cd) in enumerate(copies):
        k = columns(c, width)
        cg.wait()
        acc_g = acc_g + dot(x[:, k], gate_v[k])
        cu.wait()
        acc_u = acc_u + dot(x[:, k], up_v[k])
        cd.wait()
        acc_a = acc_a + dot(g[:, k], down_v[:, k], 1, 1)
    gg, gu = silu_grads(acc_g, acc_u, acc_a)
    small[:, :hidden] = act0[...]
    small[:, hidden : 2 * hidden] = (acc_g * jax.nn.sigmoid(acc_g) * acc_u).astype(BF16)
    small[:, 2 * hidden : 3 * hidden] = gg
    small[:, 3 * hidden :] = gu
    back_rows(gg, gu, gate_v, up_v, held, unpacked, parts)


def tick0_kernel(n, *refs):
    blocks, (pre_gate, pre_up, gate, up, down, _) = refs[:n], refs[n : n + 6]
    g, small = refs[n + 6 : n + 8]
    parts = refs[n + 8 : 2 * n + 8]
    gate_v, up_v, down_v, sems, unpacked, whole32, held = refs[2 * n + 8 :]
    copies = weight_copies(gate, up, down, gate_v, up_v, down_v, sems)
    for _, _, cd in copies:
        cd.start()
    for cg, cu, _ in copies:
        cg.start()
        cu.start()
    gather_rows(blocks, 0, unpacked, whole32, g)
    hidden = pre_gate.shape[1]
    acc_a = jnp.zeros(pre_gate.shape, F32)
    for c, (_, _, cd) in enumerate(copies):
        k = columns(c, gate.shape[0])
        cd.wait()
        acc_a = acc_a + dot(g[:, k], down_v[:, k], 1, 1)
    gg, gu = silu_grads(pre_gate[...], pre_up[...], acc_a)
    small[:, :hidden] = gg
    small[:, hidden:] = gu
    for cg, cu, _ in copies:
        cg.wait()
        cu.wait()
    back_rows(gg, gu, gate_v, up_v, held, unpacked, parts)


def whole_of(blocks):
    return jnp.concatenate(blocks, axis=0)


def input_grad_kernel(m, *refs):
    x0, xg, small1, small0 = (refs[i * m : (i + 1) * m] for i in range(4))
    gate_out, up_out = refs[4 * m :]
    hidden = gate_out.shape[1]
    x_t = whole_of([b[...] for b in x0] + [b[...] for b in xg]).T
    gg = [b[:, :hidden] for b in small0] + [b[:, 2 * hidden : 3 * hidden] for b in small1]
    gu = [b[:, hidden:] for b in small0] + [b[:, 3 * hidden :] for b in small1]
    gate_out[...] = dot(x_t, whole_of(gg)).astype(BF16)
    up_out[...] = dot(x_t, whole_of(gu)).astype(BF16)


def down_grad_kernel(m, *refs):
    g0, xg, small1 = (refs[i * m : (i + 1) * m] for i in range(3))
    (down_out,) = refs[3 * m :]
    hidden = down_out.shape[0]
    act = [b[:, :hidden] for b in small1] + [b[:, hidden : 2 * hidden] for b in small1]
    grads = [b[...] for b in g0] + [b[...] for b in xg]
    down_out[...] = dot(whole_of(act), whole_of(grads), 0, 0).astype(BF16)


def input_grads(x0, xg, small1, small0):
    m = len(x0)
    rows, width = x0[0].shape
    hidden = small0[0].shape[1] // 2
    step = width // PACK
    wide = pl.BlockSpec((rows, step), lambda c: (0, c))
    whole = [pl.BlockSpec(a.shape, lambda c: (0, 0)) for a in small1 + small0]
    out = pl.BlockSpec((step, hidden), lambda c: (c, 0))
    return pl.pallas_call(
        functools.partial(input_grad_kernel, m),
        grid=(PACK,),
        out_shape=[jax.ShapeDtypeStruct((width, hidden), BF16)] * 2,
        in_specs=[wide] * (2 * m) + whole,
        out_specs=[out, out],
        compiler_params=pltpu.CompilerParams(vmem_limit_bytes=VMEM_SMALL),
        cost_estimate=pl.CostEstimate(flops=0, bytes_accessed=COST_BYTES, transcendentals=0),
    )(*x0, *xg, *small1, *small0)


def down_grads(g0, xg, small1):
    m = len(g0)
    rows, width = g0[0].shape
    hidden = small1[0].shape[1] // 4
    step = width // PACK
    wide = pl.BlockSpec((rows, step), lambda c: (0, c))
    second = pl.BlockSpec((rows, step), lambda c: (1, c))
    whole = [pl.BlockSpec(a.shape, lambda c: (0, 0)) for a in small1]
    return pl.pallas_call(
        functools.partial(down_grad_kernel, m),
        grid=(PACK,),
        out_shape=[jax.ShapeDtypeStruct((hidden, width), BF16)],
        in_specs=[wide] * m + [second] * m + whole,
        out_specs=[pl.BlockSpec((hidden, step), lambda c: (0, c))],
        compiler_params=pltpu.CompilerParams(vmem_limit_bytes=VMEM_SMALL),
        cost_estimate=pl.CostEstimate(flops=0, bytes_accessed=COST_BYTES, transcendentals=0),
    )(*g0, *xg, *small1)


def from_group(block):
    n = lax.axis_size("expert")
    return [block] + [shifted(block, "expert", k) for k in range(1, n)]


def to_group(blocks):
    return [blocks[0]] + [shifted(b, "expert", -k) for k, b in enumerate(blocks) if k]


def copies_of(block):
    n = lax.axis_size("dp")
    return [block] + [shifted(block, "dp", k) for k in range(1, n)]


def shards(tokens, cotangent, w_gate, w_up, w_down, routes, gates):
    gate, up, down = w_gate[0], w_up[0], w_down[0]
    width, hidden = gate.shape
    step = width // PACK
    own = tokens.shape[0]
    n = lax.axis_size("expert")
    rows = -(-n * CAP // 16) * 16
    routes = jnp.transpose(routes, (0, 2, 1))
    gates = jnp.transpose(gates, (0, 2, 1))
    one = ((PACKED, step), BF16)
    part = functools.partial
    scratch = [
        pltpu.VMEM((width, hidden), BF16),
        pltpu.VMEM((width, hidden), BF16),
        pltpu.VMEM((hidden, width), BF16),
        pltpu.SemaphoreType.DMA((3, PACK)),
        pltpu.VMEM((n, PACKED, step), F32),
        pltpu.VMEM((rows, width), F32),
        pltpu.VMEM((PACK, rows, step), F32),
    ]
    tick1_scratch = list(scratch)
    tick1_scratch[5] = pltpu.VMEM((2, rows, width), F32)
    tick1_scratch += [pltpu.VMEM((rows, width), BF16)] * 2
    matmul = 0

    next_routes = shifted(routes[1:], "section", -1)
    prev_routes = shifted(routes[1:], "section", 1)
    prev2_routes = shifted(routes[:1], "section", 2)

    raw0, normed0, piece = call(
        first_rows_kernel,
        [one, one, ((FIRST, width), BF16)],
        [tokens, routes, cotangent],
        any_args=(2,),
        any_outs=(2,),
        scratch=[pltpu.SemaphoreType.DMA],
    )
    cot_a = shifted(piece, "section", -2)
    x0_blocks = from_group(normed0)
    t1, cot1 = call(
        other_rows_kernel, [one, one], [tokens, cotangent, next_routes, prev_routes]
    )
    cot1 = shifted(cot1, "section", -1)
    x0, pre_gate0, pre_up0, act0, *parts = call(
        part(forward_kernel, n),
        [((rows, width), BF16), ((rows, hidden), F32), ((rows, hidden), F32)]
        + [((rows, hidden), BF16)]
        + [one] * n,
        [*x0_blocks, gate, up, down, t1],
        any_args=(n, n + 1, n + 2, n + 3),
        scratch=scratch,
        vmem=VMEM_BIG,
        flops=3 * matmul,
    )
    parts = to_group(parts)
    upd0, h1, piece = call(
        part(update0_kernel, n),
        [one, one, ((SECOND, width), BF16)],
        [*parts, raw0, routes, gates, next_routes, t1, tokens, cot_a, cot1, prev2_routes],
        any_args=(n + 5, n + 6, n + 7, n + 8),
        any_outs=(2,),
        scratch=[pltpu.SemaphoreType.DMA],
    )
    h1 = shifted(h1, "section", 1)
    tok_a = shifted(piece, "section", 2)
    upd0 = shifted(upd0, "section", 2)

    enter1, piece = call(
        enter1_kernel,
        [((2 * PACKED, step), BF16), ((own - FIRST, width), BF16)],
        [h1, cot1, routes, gates, cotangent, tok_a],
        any_args=(4, 5),
        any_outs=(1,),
        scratch=[pltpu.SemaphoreType.DMA],
    )
    cot_b = shifted(piece, "section", -2)
    blocks = from_group(enter1)
    x0_all = copies_of(x0)
    xg1, small1, *parts = call(
        part(tick1_kernel, n),
        [((2 * rows, width), BF16), ((rows, 4 * hidden), BF16)] + [one] * n,
        [*blocks, act0, gate, up, down, upd0],
        any_args=(n + 1, n + 2, n + 3, n + 4),
        scratch=tick1_scratch,
        vmem=VMEM_BIG,
        flops=5 * matmul,
    )
    parts = to_group(parts)
    upd1, piece = call(
        part(grad1_kernel, n),
        [one, ((SECOND, width), BF16)],
        [*parts, h1, cot1, tokens, cot_b, x0_all[-1]],
        any_args=(n + 2, n + 3, n + 4),
        any_outs=(1,),
        scratch=[pltpu.SemaphoreType.DMA],
    )
    upd1 = shifted(upd1, "section", -1)
    tok_b = shifted(piece, "section", 2)
    xg1_all = copies_of(xg1)

    c0, enter0, piece = call(
        enter0_kernel,
        [one, one, ((own - 2 * SECOND, width), BF16)],
        [upd1, next_routes, routes, gates, cot_a, cot_b, tokens, tok_b],
        any_args=(6, 7),
        any_outs=(2,),
        scratch=[pltpu.SemaphoreType.DMA],
    )
    tok_c = shifted(piece, "section", 2)
    blocks = from_group(enter0)
    g0, small0, *parts = call(
        part(tick0_kernel, n),
        [((rows, width), BF16), ((rows, 2 * hidden), BF16)] + [one] * n,
        [*blocks, pre_gate0, pre_up0, gate, up, down, xg1_all[-1]],
        any_args=(n + 2, n + 3, n + 4, n + 5),
        scratch=scratch,
        vmem=VMEM_BIG,
        flops=3 * matmul,
    )
    parts = to_group(parts)
    outs = call(
        part(down_kernel, n),
        [one] * n,
        [small1, down, small0],
        any_args=(2,),
        scratch=[scratch[4], scratch[6]],
        vmem=VMEM_BIG,
        flops=matmul,
    )
    outs = to_group(outs)
    (last1,) = call(part(update1_kernel, n), [one], [*outs, h1, routes, gates])
    last1 = shifted(last1, "section", 1)
    small1_all = copies_of(small1)
    gate_out, up_out = input_grads(x0_all, xg1_all, small1_all, copies_of(small0))
    (down_out,) = down_grads(copies_of(g0), xg1_all, small1_all)
    (grad,) = call(
        part(finish_grad_kernel, n),
        [(tokens.shape, BF16)],
        [*parts, raw0, c0, routes, upd1, next_routes, cot_a, cot_b],
    )
    (state,) = call(
        finish_state_kernel,
        [(tokens.shape, BF16)],
        [tok_a, tok_b, tok_c, upd0, prev2_routes, last1, prev_routes],
    )
    return (grad, state, gate_out[None], up_out[None], down_out[None])


def solution(mesh):
    rows = P(("section", "expert", "dp"), None)
    slots = P(None, ("section", "expert", "dp"), None)
    cols = P("section", None, "expert")
    hidden = P("section", "expert", None)
    return jax.shard_map(
        shards,
        mesh=mesh,
        in_specs=(rows, rows, cols, cols, hidden, slots, slots),
        out_specs=(rows, rows, cols, cols, hidden),
        check_vma=False,
    )
```

time: 274 us -> 200 us (0.73)
  the two profiles are of different devices: /device:TPU:17 before, /device:TPU:0 now
where the time goes in v2:
time: 200 us; the launch traced here: 199 us
  waiting for transfers between devices  88.5 us (44%)
  starting transfers between devices  57.1 us (29%)
  Pallas kernels  48.2 us (24%)
  local copies, waits for them, and re-layouts  4.66 us (2%)
    ppermute x39, waiting for transfers between devices, shifted(): lax.ppermute(block, axis, [((i - distance) % size, i) for i in range(size)])  88.5 us
    ppermute x39, starting transfers between devices, shifted(): lax.ppermute(block, axis, [((i - distance) % size, i) for i in range(size)])  57.1 us
    pallas_call x13, Pallas kernels, call(): pl.pallas_call(kernel, out_shape=outs, in_specs=[anywhere if i in any_arg...  36.2 us
    pallas_call x1, Pallas kernels, input_grads(): pl.pallas_call(functools.partial(input_grad_kernel, m), grid=(PACK,), out...  6.41 us
    pallas_call x1, Pallas kernels, down_grads(): pl.pallas_call(functools.partial(down_grad_kernel, m), grid=(PACK,), out_...  5.57 us
    unnamed x20, local copies, waits for them, and re-layouts  4.66 us
  transfers between devices with their start and end apart: 39, of which 17 were waited for; matrix products, arithmetic and copies ran while one was open for 0% of the time, Pallas kernels for 22%

profile of v2, /device:TPU:0, one launch (start us, length us, event | category | flops | bytes accessed | tf_op | source)
XLA Modules:
  0.0 199.4 jit_solution(4939995656843603515)
XLA Ops:
  0.6 1.3 copy-done
  2.0 1.3 copy-done.2
  3.3 0.7 copy-done.5
  4.0 1.1 shard_map.110
  5.1 4.1 %collective-permute-start.8 = (bf16[64,5120]{1,0:T(8,128)(2,1)S(1)}, bf16[64,5120]{1,0:T(8,128)(2,1)S(1)}, u32[]{:S(2)}, u32[]{:S(2)}) collective-permute-start(bf16[64,5120]{1,0:T(8,128)(2,1)S(1)} %get-tuple-element.53), channel_id=1, source_target_pairs={{16,0},{24,8},{0,16},{8,24},{17,1},{25,9},{1,17},{9,25},{18,2},{26... | collective-permute-start | bytes 1966088 | tf_op jit(solution)/shard_map/ppermute | solution.py:25
  9.2 1.6 collective-permute-start.1
  10.7 1.4 collective-permute-start.2
  12.2 1.3 collective-permute-start.3
  13.5 9.7 %collective-permute-done.3.next_routes.refs_7_.refs_8_ = s32[1,4,128]{2,1,0:T(4,128)S(1)} collective-permute-done((s32[1,4,128]{2,1,0:T(4,128)S(1)}, s32[1,4,128]{2,1,0:T(4,128)S(1)}, u32[]{:S(2)}, u32[]{:S(2)}) %collective-permute-start.3) | collective-permute-done | bytes 2080 | tf_op jit(solution)/shard_map/ppermute | solution.py:25
  23.3 15.3 %collective-permute-start.4 = (s32[1,4,128]{2,1,0:T(4,128)S(1)}, s32[1,4,128]{2,1,0:T(4,128)S(1)}, u32[]{:S(2)}, u32[]{:S(2)}) collective-permute-start(s32[1,4,128]{2,1,0:T(4,128)S(1)} %get-tuple-element.88), channel_id=1, source_target_pairs={{24,0},{0,8},{8,16},{16,24},{25,1},{1,9},{9,17},{17,25},{26,2},{2,... | collective-permute-start | bytes 6152 | tf_op jit(solution)/shard_map/ppermute | solution.py:25
  38.6 1.3 collective-permute-done.4.prev_routes
  39.9 1.7 collective-permute-start.10
  41.6 1.3 copy-done.3
  43.0 0.8 shard_map.111
  43.8 3.0 %collective-permute-start.9 = (bf16[80,640]{1,0:T(8,128)(2,1)S(1)}, bf16[80,640]{1,0:T(8,128)(2,1)S(1)}, u32[]{:S(2)}, u32[]{:S(2)}) collective-permute-start(bf16[80,640]{1,0:T(8,128)(2,1)S(1)} %get-tuple-element.54), channel_id=1, source_target_pairs={{8,0},{16,8},{24,16},{0,24},{9,1},{17,9},{25,17},{1,25},{10,2},{18... | collective-permute-start | bytes 307208 | tf_op jit(solution)/shard_map/ppermute | solution.py:25
  46.8 6.6 %shard_map.112 = (bf16[48,5120]{1,0:T(8,128)(2,1)S(1)}, f32[48,512]{1,0:T(8,128)S(1)}, f32[48,512]{1,0:T(8,128)S(1)}, bf16[48,512]{1,0:T(8,128)(2,1)S(1)}, bf16[...) custom-call(bf16[80,640]{1,0:T(8,128)(2,1)S(1)} %get-tuple-element.4, ...), custom_call_target="tpu_custom_call" | custom-call | bytes 1024 | tf_op jit(solution)/shard_map/pallas_call | solution.py:38
  53.4 1.6 collective-permute-start.6
  55.2 0.4 collective-permute-done.5.refs_1_
  55.7 5.2 %collective-permute-done.6.refs_2_ = bf16[80,640]{1,0:T(8,128)(2,1)S(1)} collective-permute-done((bf16[80,640]{1,0:T(8,128)(2,1)S(1)}, bf16[80,640]{1,0:T(8,128)(2,1)S(1)}, u32[]{:S(2)}, u32[]{:S(2)}) %collective-permute-start.6) | collective-permute-done | bytes 102432 | tf_op jit(solution)/shard_map/ppermute | solution.py:25
  60.9 0.7 shard_map.113
  61.7 0.6 collective-permute-start.11
  62.3 6.0 %collective-permute-done.11.h.refs_4_ = bf16[80,640]{1,0:T(8,128)(2,1)S(1)} collective-permute-done((bf16[80,640]{1,0:T(8,128)(2,1)S(1)}, bf16[80,640]{1,0:T(8,128)(2,1)S(1)}, u32[]{:S(2)}, u32[]{:S(2)}) %collective-permute-start.11) | collective-permute-done | bytes 102432 | tf_op jit(solution)/shard_map/ppermute | solution.py:25
  68.3 2.7 %collective-permute-done.12._.bulk_a = bf16[16,5120]{1,0:T(8,128)(2,1)S(1)} collective-permute-done((bf16[16,5120]{1,0:T(8,128)(2,1)S(1)}, bf16[16,5120]{1,0:T(8,128)(2,1)S(1)}, u32[]{:S(2)}, u32[]{:S(2)}) %collective-permute-start.12) | collective-permute-done | bytes 163872 | tf_op jit(solution)/shard_map/ppermute | solution.py:25
  71.1 0.6 shard_map.114
  71.7 0.7 collective-permute-start.20
  72.4 2.3 %collective-permute-start.16 = (bf16[80,640]{1,0:T(8,128)(2,1)S(1)}, bf16[80,640]{1,0:T(8,128)(2,1)S(1)}, u32[]{:S(2)}, u32[]{:S(2)}) collective-permute-start(bf16[80,640]{1,0:T(8,128)(2,1)S(1)} %get-tuple-element.59), channel_id=1, source_target_pairs={{16,0},{24,8},{0,16},{8,24},{17,1},{25,9},{1,17},{9,25},{18,2},{26... | collective-permute-start | bytes 307208 | tf_op jit(solution)/shard_map/ppermute | solution.py:25
  74.7 1.5 collective-permute-start.21
  76.2 1.6 collective-permute-start.14
  77.8 26.8 %collective-permute-done.16.refs_8_.upd0 = bf16[80,640]{1,0:T(8,128)(2,1)S(1)} collective-permute-done((bf16[80,640]{1,0:T(8,128)(2,1)S(1)}, bf16[80,640]{1,0:T(8,128)(2,1)S(1)}, u32[]{:S(2)}, u32[]{:S(2)}) %collective-permute-start.16) | collective-permute-done | bytes 102432 | tf_op jit(solution)/shard_map/ppermute | solution.py:25
  104.6 1.2 collective-permute-start.15
  105.8 3.3 %collective-permute-done.15.refs_3_ = bf16[160,640]{1,0:T(8,128)(2,1)S(1)} collective-permute-done((bf16[160,640]{1,0:T(8,128)(2,1)S(1)}, bf16[160,640]{1,0:T(8,128)(2,1)S(1)}, u32[]{:S(2)}, u32[]{:S(2)}) %collective-permute-start.15) | collective-permute-done | bytes 204832 | tf_op jit(solution)/shard_map/ppermute | solution.py:25
  109.1 9.4 %shard_map.115 = (bf16[96,5120]{1,0:T(8,128)(2,1)S(1)}, bf16[48,2048]{1,0:T(8,128)(2,1)S(1)}, bf16[80,640]{1,0:T(8,128)(2,1)S(1)}, bf16[80,640]{1,0:T(8,128)(2,1...) custom-call(bf16[160,640]{1,0:T(8,128)(2,1)S(1)} %get-tuple-element.57.refs_0_, ...), custom_call_target="tpu_custom_call" | custom-call | bytes 1024 | tf_op jit(solution)/shard_map/pallas_call | solution.py:38
  118.5 1.6 collective-permute-start.27
  120.1 1.6 collective-permute-start.17
  122.1 2.4 %collective-permute-done.17.refs_1_ = bf16[80,640]{1,0:T(8,128)(2,1)S(1)} collective-permute-done((bf16[80,640]{1,0:T(8,128)(2,1)S(1)}, bf16[80,640]{1,0:T(8,128)(2,1)S(1)}, u32[]{:S(2)}, u32[]{:S(2)}) %collective-permute-start.17) | collective-permute-done | bytes 102432 | tf_op jit(solution)/shard_map/ppermute | solution.py:25
  124.6 3.0 %collective-permute-done.18.refs_2_ = bf16[80,640]{1,0:T(8,128)(2,1)S(1)} collective-permute-done((bf16[80,640]{1,0:T(8,128)(2,1)S(1)}, bf16[80,640]{1,0:T(8,128)(2,1)S(1)}, u32[]{:S(2)}, u32[]{:S(2)}) %collective-permute-start.18) | collective-permute-done | bytes 102432 | tf_op jit(solution)/shard_map/ppermute | solution.py:25
  127.6 0.7 shard_map.116
  128.3 0.8 collective-permute-start.22
  129.1 7.5 %collective-permute-done.22.upd1.refs_7_ = bf16[80,640]{1,0:T(8,128)(2,1)S(1)} collective-permute-done((bf16[80,640]{1,0:T(8,128)(2,1)S(1)}, bf16[80,640]{1,0:T(8,128)(2,1)S(1)}, u32[]{:S(2)}, u32[]{:S(2)}) %collective-permute-start.22) | collective-permute-done | bytes 102432 | tf_op jit(solution)/shard_map/ppermute | solution.py:25
  136.6 1.4 shard_map.117
  138.0 0.9 collective-permute-start.31
  138.9 0.6 collective-permute-start.25
  139.5 1.4 collective-permute-start.26
  140.9 2.6 %collective-permute-done.24.refs_1_ = bf16[80,640]{1,0:T(8,128)(2,1)S(1)} collective-permute-done((bf16[80,640]{1,0:T(8,128)(2,1)S(1)}, bf16[80,640]{1,0:T(8,128)(2,1)S(1)}, u32[]{:S(2)}, u32[]{:S(2)}) %collective-permute-start.24) | collective-permute-done | bytes 102432 | tf_op jit(solution)/shard_map/ppermute | solution.py:25
  143.6 1.1 collective-permute-done.25.refs_2_
  144.7 9.1 %shard_map.118 = (bf16[48,5120]{1,0:T(8,128)(2,1)S(1)}, bf16[48,1024]{1,0:T(8,128)(2,1)S(1)}, bf16[80,640]{1,0:T(8,128)(2,1)S(1)}, bf16[80,640]{1,0:T(8,128)(2,1...) custom-call(bf16[80,640]{1,0:T(8,128)(2,1)S(1)} %get-tuple-element.68.refs_0_, ...), custom_call_target="tpu_custom_call" | custom-call | bytes 1024 | tf_op jit(solution)/shard_map/pallas_call | solution.py:38
  153.8 0.5 collective-permute-start.38
  154.3 1.6 collective-permute-start.36
  155.9 1.1 shard_map.120
  157.0 1.1 collective-permute-start.32
  158.1 0.5 collective-permute-start.37
  158.5 13.2 %collective-permute-done.36.refs_5_ = bf16[48,2048]{1,0:T(8,128)(2,1)S(1)} collective-permute-done((bf16[48,2048]{1,0:T(8,128)(2,1)S(1)}, bf16[48,2048]{1,0:T(8,128)(2,1)S(1)}, u32[]{:S(2)}, u32[]{:S(2)}) %collective-permute-start.36) | collective-permute-done | bytes 196640 | tf_op jit(solution)/shard_map/ppermute | solution.py:25
  171.7 1.6 collective-permute-start.33
  173.3 0.5 collective-permute-done.37.refs_7_
  173.8 0.5 collective-permute-start.34
  174.4 1.2 collective-permute-start.28
  175.6 1.9 collective-permute-done.33.refs_2_
  177.5 0.5 collective-permute-start.29
  178.0 0.6 collective-permute-done.34.refs_3_
  178.8 3.9 %collective-permute-start.35 = (bf16[80,640]{1,0:T(8,128)(2,1)S(1)}, bf16[80,640]{1,0:T(8,128)(2,1)S(1)}, u32[]{:S(2)}, u32[]{:S(2)}) collective-permute-start(bf16[80,640]{1,0:T(8,128)(2,1)S(1)} %shard_map.121), channel_id=1, source_target_pairs={{24,0},{0,8},{8,16},{16,24},{25,1},{1,9},{9,17},{17,25},{26,2},{2,... | collective-permute-start | bytes 307208 | tf_op jit(solution)/shard_map/ppermute | solution.py:25
  182.8 6.4 %shard_map.123 = (bf16[5120,512]{1,0:T(8,128)(2,1)}, bf16[5120,512]{1,0:T(8,128)(2,1)}) custom-call(bf16[48,5120]{1,0:T(8,128)(2,1)S(1)} %get-tuple-element.65.refs_0_, bf16[48,5120]{1,0:T(8,128)(2,1)S(1)} %collective-permute-done.21.refs_8_.refs_1_, bf16[96,5120]{1,0:T(8,128)(2,1)S(1)} %get-tuple-element.71.refs_2_, ...), custom_call_target="tpu_custom_call" | custom-call | bytes 1024 | tf_op jit(solution)/shard_map/pallas_call | solution.py:429
  189.2 2.4 %shard_map.119 = bf16[128,5120]{1,0:T(8,128)(2,1)} custom-call(bf16[80,640]{1,0:T(8,128)(2,1)S(1)} %get-tuple-element.72.refs_0_, bf16[80,640]{1,0:T(8,128)(2,1)S(1)} %collective-permute-done.28.refs_1_, bf16[80,640]{1,0:T(8,128)(2,1)S(1)} %collective-permute-done.29.refs_2_, bf16[80,640]{1,0:T(8,128)(2,1)S(1)} %collective-permute-done.30.refs_3_, ...), custom_call_target="tpu_custom_call" | custom-call | bytes 1024 | tf_op jit(solution)/shard_map/pallas_call | solution.py:38
  191.6 5.6 %shard_map.124 = bf16[512,5120]{1,0:T(8,128)(2,1)} custom-call(bf16[48,5120]{1,0:T(8,128)(2,1)S(1)} %get-tuple-element.86.refs_0_, bf16[48,5120]{1,0:T(8,128)(2,1)S(1)} %collective-permute-done.38.refs_1_, bf16[96,5120]{1,0:T(8,128)(2,1)S(1)} %get-tuple-element.71.refs_2_, bf16[96,5120]{1,0:T(8,128)(2,1)S(1)} %collective-permute-done.27.refs_9_.refs_3_, ...), custom_call_target="tpu_custom_call" | custom-call | bytes 1024 | tf_op jit(solution)/shard_map/pallas_call | solution.py:448
  197.1 2.2 %shard_map.122 = bf16[128,5120]{1,0:T(8,128)(2,1)} custom-call(bf16[16,5120]{1,0:T(8,128)(2,1)S(1)} %collective-permute-done.12._.bulk_a, bf16[16,5120]{1,0:T(8,128)(2,1)S(1)} %collective-permute-done.23._.bulk_b, bf16[96,5120]{1,0:T(8,128)(2,1)S(1)} %collective-permute-done.31.bulk_c, bf16[80,640]{1,0:T(8,128)(2,1)S(1)} %collective-permute-done.16.refs_8_.upd0, ...), custom_call_target="tpu_custom_call" | custom-call | bytes 1024 | tf_op jit(solution)/shard_map/pallas_call | solution.py:38
  (51 shorter events, 1.2 us)
Async XLA Ops:
  0.6 1.3 copy-start
  1.9 1.3 copy-start.2
  3.3 0.7 copy-start.5
  5.1 55.8 %collective-permute-start.8 = (bf16[64,5120]{1,0:T(8,128)(2,1)S(1)}, bf16[64,5120]{1,0:T(8,128)(2,1)S(1)}, u32[]{:S(2)}, u32[]{:S(2)}) collective-permute-start(bf16[64,5120]{1,0:T(8,128)(2,1)S(1)} %get-tuple-element.53), channel_id=1, source_target_pairs={{16,0},{24,8},{0,16},{8,24},{17,1},{25,9},{1,17},{9,25},{18,2},{26... | collective-permute-start | bytes 1966088 | tf_op jit(solution)/shard_map/ppermute | solution.py:25
  9.2 34.6 %collective-permute-start = (bf16[80,640]{1,0:T(8,128)(2,1)S(1)}, bf16[80,640]{1,0:T(8,128)(2,1)S(1)}, u32[]{:S(2)}, u32[]{:S(2)}) collective-permute-start(bf16[80,640]{1,0:T(8,128)(2,1)S(1)} %get-tuple-element.46.refs_0_), channel_id=1, source_target_pairs={{6,0},{0,2},{2,4},{4,6},{7,1},{1,3},{3,5},{5,7},{14,8},{8,10},{10,... | collective-permute-start | bytes 307208 | tf_op jit(solution)/shard_map/ppermute | solution.py:25
  9.2 37.6 %collective-permute-start.1 = (bf16[80,640]{1,0:T(8,128)(2,1)S(1)}, bf16[80,640]{1,0:T(8,128)(2,1)S(1)}, u32[]{:S(2)}, u32[]{:S(2)}) collective-permute-start(bf16[80,640]{1,0:T(8,128)(2,1)S(1)} %get-tuple-element.46.refs_0_), channel_id=1, source_target_pairs={{4,0},{6,2},{0,4},{2,6},{5,1},{7,3},{1,5},{3,7},{12,8},{14,10},{8,... | collective-permute-start | bytes 307208 | tf_op jit(solution)/shard_map/ppermute | solution.py:25
  10.7 36.0 %collective-permute-start.2 = (bf16[80,640]{1,0:T(8,128)(2,1)S(1)}, bf16[80,640]{1,0:T(8,128)(2,1)S(1)}, u32[]{:S(2)}, u32[]{:S(2)}) collective-permute-start(bf16[80,640]{1,0:T(8,128)(2,1)S(1)} %get-tuple-element.46.refs_0_), channel_id=1, source_target_pairs={{2,0},{4,2},{6,4},{0,6},{3,1},{5,3},{7,5},{1,7},{10,8},{12,10},{14... | collective-permute-start | bytes 307208 | tf_op jit(solution)/shard_map/ppermute | solution.py:25
  12.2 11.1 %collective-permute-start.3 = (s32[1,4,128]{2,1,0:T(4,128)S(1)}, s32[1,4,128]{2,1,0:T(4,128)S(1)}, u32[]{:S(2)}, u32[]{:S(2)}) collective-permute-start(s32[1,4,128]{2,1,0:T(4,128)S(1)} %get-tuple-element.88), channel_id=1, source_target_pairs={{8,0},{16,8},{24,16},{0,24},{9,1},{17,9},{25,17},{1,25},{10,2},{18... | collective-permute-start | bytes 6152 | tf_op jit(solution)/shard_map/ppermute | solution.py:25
  23.3 16.7 %collective-permute-start.4 = (s32[1,4,128]{2,1,0:T(4,128)S(1)}, s32[1,4,128]{2,1,0:T(4,128)S(1)}, u32[]{:S(2)}, u32[]{:S(2)}) collective-permute-start(s32[1,4,128]{2,1,0:T(4,128)S(1)} %get-tuple-element.88), channel_id=1, source_target_pairs={{24,0},{0,8},{8,16},{16,24},{25,1},{1,9},{9,17},{17,25},{26,2},{2,... | collective-permute-start | bytes 6152 | tf_op jit(solution)/shard_map/ppermute | solution.py:25
  39.9 15.1 %collective-permute-start.10 = (s32[1,4,128]{2,1,0:T(4,128)S(1)}, s32[1,4,128]{2,1,0:T(4,128)S(1)}, u32[]{:S(2)}, u32[]{:S(2)}) collective-permute-start(s32[1,4,128]{2,1,0:T(4,128)S(1)} %get-tuple-element.87), channel_id=1, source_target_pairs={{16,0},{24,8},{0,16},{8,24},{17,1},{25,9},{1,17},{9,25},{18,2},{26... | collective-permute-start | bytes 6152 | tf_op jit(solution)/shard_map/ppermute | solution.py:25
  41.6 1.3 copy-start.3
  43.8 11.5 %collective-permute-start.9 = (bf16[80,640]{1,0:T(8,128)(2,1)S(1)}, bf16[80,640]{1,0:T(8,128)(2,1)S(1)}, u32[]{:S(2)}, u32[]{:S(2)}) collective-permute-start(bf16[80,640]{1,0:T(8,128)(2,1)S(1)} %get-tuple-element.54), channel_id=1, source_target_pairs={{8,0},{16,8},{24,16},{0,24},{9,1},{17,9},{25,17},{1,25},{10,2},{18... | collective-permute-start | bytes 307208 | tf_op jit(solution)/shard_map/ppermute | solution.py:25
  46.7 14.2 %copy-start.1 = (bf16[128,5120]{1,0:T(8,128)(2,1)S(1)}, bf16[128,5120]{1,0:T(8,128)(2,1)}, u32[]{:S(2)}) copy-start(bf16[128,5120]{1,0:T(8,128)(2,1)} %tokens.5) | copy-start | bytes 3932164
  46.8 14.2 %copy-start.6 = (s32[2,128,4]{1,2,0:T(4,128)S(1)}, s32[2,128,4]{1,2,0:T(4,128)}, u32[]{:S(2)}) copy-start(s32[2,128,4]{1,2,0:T(4,128)} %param.12) | copy-start | bytes 12292
  46.8 14.2 %copy-start.7 = (f32[2,128,4]{1,2,0:T(4,128)S(1)}, f32[2,128,4]{1,2,0:T(4,128)}, u32[]{:S(2)}) copy-start(f32[2,128,4]{1,2,0:T(4,128)} %param.13) | copy-start | bytes 12292
  46.8 24.3 %copy-start.4 = (bf16[128,5120]{1,0:T(8,128)(2,1)S(1)}, bf16[128,5120]{1,0:T(8,128)(2,1)}, u32[]{:S(2)}) copy-start(bf16[128,5120]{1,0:T(8,128)(2,1)} %cotangent.5) | copy-start | bytes 3932164
  53.4 2.3 %collective-permute-start.5 = (bf16[80,640]{1,0:T(8,128)(2,1)S(1)}, bf16[80,640]{1,0:T(8,128)(2,1)S(1)}, u32[]{:S(2)}, u32[]{:S(2)}) collective-permute-start(bf16[80,640]{1,0:T(8,128)(2,1)S(1)} %get-tuple-element.49), channel_id=1, source_target_pairs={{2,0},{4,2},{6,4},{0,6},{3,1},{5,3},{7,5},{1,7},{10,8},{12,10},{14... | collective-permute-start | bytes 307208 | tf_op jit(solution)/shard_map/ppermute | solution.py:25
  53.4 7.5 %collective-permute-start.6 = (bf16[80,640]{1,0:T(8,128)(2,1)S(1)}, bf16[80,640]{1,0:T(8,128)(2,1)S(1)}, u32[]{:S(2)}, u32[]{:S(2)}) collective-permute-start(bf16[80,640]{1,0:T(8,128)(2,1)S(1)} %get-tuple-element.50), channel_id=1, source_target_pairs={{4,0},{6,2},{0,4},{2,6},{5,1},{7,3},{1,5},{3,7},{12,8},{14,10},{8,... | collective-permute-start | bytes 307208 | tf_op jit(solution)/shard_map/ppermute | solution.py:25
  55.1 5.8 %collective-permute-start.7 = (bf16[80,640]{1,0:T(8,128)(2,1)S(1)}, bf16[80,640]{1,0:T(8,128)(2,1)S(1)}, u32[]{:S(2)}, u32[]{:S(2)}) collective-permute-start(bf16[80,640]{1,0:T(8,128)(2,1)S(1)} %get-tuple-element.51), channel_id=1, source_target_pairs={{6,0},{0,2},{2,4},{4,6},{7,1},{1,3},{3,5},{5,7},{14,8},{8,10},{10,... | collective-permute-start | bytes 307208 | tf_op jit(solution)/shard_map/ppermute | solution.py:25
  61.6 9.4 %collective-permute-start.12 = (bf16[16,5120]{1,0:T(8,128)(2,1)S(1)}, bf16[16,5120]{1,0:T(8,128)(2,1)S(1)}, u32[]{:S(2)}, u32[]{:S(2)}) collective-permute-start(bf16[16,5120]{1,0:T(8,128)(2,1)S(1)} %get-tuple-element.56), channel_id=1, source_target_pairs={{16,0},{24,8},{0,16},{8,24},{17,1},{25,9},{1,17},{9,25},{18,2},{26... | collective-permute-start | bytes 491528 | tf_op jit(solution)/shard_map/ppermute | solution.py:25
  61.7 6.6 %collective-permute-start.11 = (bf16[80,640]{1,0:T(8,128)(2,1)S(1)}, bf16[80,640]{1,0:T(8,128)(2,1)S(1)}, u32[]{:S(2)}, u32[]{:S(2)}) collective-permute-start(bf16[80,640]{1,0:T(8,128)(2,1)S(1)} %get-tuple-element.55), channel_id=1, source_target_pairs={{24,0},{0,8},{8,16},{16,24},{25,1},{1,9},{9,17},{17,25},{26,2},{2,... | collective-permute-start | bytes 307208 | tf_op jit(solution)/shard_map/ppermute | solution.py:25
  71.7 55.9 %collective-permute-start.20 = (bf16[64,5120]{1,0:T(8,128)(2,1)S(1)}, bf16[64,5120]{1,0:T(8,128)(2,1)S(1)}, u32[]{:S(2)}, u32[]{:S(2)}) collective-permute-start(bf16[64,5120]{1,0:T(8,128)(2,1)S(1)} %get-tuple-element.64), channel_id=1, source_target_pairs={{16,0},{24,8},{0,16},{8,24},{17,1},{25,9},{1,17},{9,25},{18,2},{26... | collective-permute-start | bytes 1966088 | tf_op jit(solution)/shard_map/ppermute | solution.py:25
  72.4 32.2 %collective-permute-start.16 = (bf16[80,640]{1,0:T(8,128)(2,1)S(1)}, bf16[80,640]{1,0:T(8,128)(2,1)S(1)}, u32[]{:S(2)}, u32[]{:S(2)}) collective-permute-start(bf16[80,640]{1,0:T(8,128)(2,1)S(1)} %get-tuple-element.59), channel_id=1, source_target_pairs={{16,0},{24,8},{0,16},{8,24},{17,1},{25,9},{1,17},{9,25},{18,2},{26... | collective-permute-start | bytes 307208 | tf_op jit(solution)/shard_map/ppermute | solution.py:25
  74.7 47.5 %collective-permute-start.21 = (bf16[48,5120]{1,0:T(8,128)(2,1)S(1)}, bf16[48,5120]{1,0:T(8,128)(2,1)S(1)}, u32[]{:S(2)}, u32[]{:S(2)}) collective-permute-start(bf16[48,5120]{1,0:T(8,128)(2,1)S(1)} %get-tuple-element.65.refs_0_), channel_id=1, source_target_pairs={{1,0},{0,1},{3,2},{2,3},{5,4},{4,5},{7,6},{6,7},{9,8},{8,9},{11,10... | collective-permute-start | bytes 1474568 | tf_op jit(solution)/shard_map/ppermute | solution.py:25
  76.2 29.6 %collective-permute-start.13 = (bf16[160,640]{1,0:T(8,128)(2,1)S(1)}, bf16[160,640]{1,0:T(8,128)(2,1)S(1)}, u32[]{:S(2)}, u32[]{:S(2)}) collective-permute-start(bf16[160,640]{1,0:T(8,128)(2,1)S(1)} %get-tuple-element.57.refs_0_), channel_id=1, source_target_pairs={{6,0},{0,2},{2,4},{4,6},{7,1},{1,3},{3,5},{5,7},{14,8},{8,10},{10,... | collective-permute-start | bytes 614408 | tf_op jit(solution)/shard_map/ppermute | solution.py:25
  76.2 29.6 %collective-permute-start.14 = (bf16[160,640]{1,0:T(8,128)(2,1)S(1)}, bf16[160,640]{1,0:T(8,128)(2,1)S(1)}, u32[]{:S(2)}, u32[]{:S(2)}) collective-permute-start(bf16[160,640]{1,0:T(8,128)(2,1)S(1)} %get-tuple-element.57.refs_0_), channel_id=1, source_target_pairs={{4,0},{6,2},{0,4},{2,6},{5,1},{7,3},{1,5},{3,7},{12,8},{14,10},{8,... | collective-permute-start | bytes 614408 | tf_op jit(solution)/shard_map/ppermute | solution.py:25
  104.6 4.5 %collective-permute-start.15 = (bf16[160,640]{1,0:T(8,128)(2,1)S(1)}, bf16[160,640]{1,0:T(8,128)(2,1)S(1)}, u32[]{:S(2)}, u32[]{:S(2)}) collective-permute-start(bf16[160,640]{1,0:T(8,128)(2,1)S(1)} %get-tuple-element.57.refs_0_), channel_id=1, source_target_pairs={{2,0},{4,2},{6,4},{0,6},{3,1},{5,3},{7,5},{1,7},{10,8},{12,10},{14... | collective-permute-start | bytes 614408 | tf_op jit(solution)/shard_map/ppermute | solution.py:25
  118.5 26.2 %collective-permute-start.27 = (bf16[96,5120]{1,0:T(8,128)(2,1)S(1)}, bf16[96,5120]{1,0:T(8,128)(2,1)S(1)}, u32[]{:S(2)}, u32[]{:S(2)}) collective-permute-start(bf16[96,5120]{1,0:T(8,128)(2,1)S(1)} %get-tuple-element.71.refs_2_), channel_id=1, source_target_pairs={{1,0},{0,1},{3,2},{2,3},{5,4},{4,5},{7,6},{6,7},{9,8},{8,9},{11,10... | collective-permute-start | bytes 2949128 | tf_op jit(solution)/shard_map/ppermute | solution.py:25
  120.1 4.5 %collective-permute-start.17 = (bf16[80,640]{1,0:T(8,128)(2,1)S(1)}, bf16[80,640]{1,0:T(8,128)(2,1)S(1)}, u32[]{:S(2)}, u32[]{:S(2)}) collective-permute-start(bf16[80,640]{1,0:T(8,128)(2,1)S(1)} %get-tuple-element.61), channel_id=1, source_target_pairs={{2,0},{4,2},{6,4},{0,6},{3,1},{5,3},{7,5},{1,7},{10,8},{12,10},{14... | collective-permute-start | bytes 307208 | tf_op jit(solution)/shard_map/ppermute | solution.py:25
  121.7 5.9 %collective-permute-start.18 = (bf16[80,640]{1,0:T(8,128)(2,1)S(1)}, bf16[80,640]{1,0:T(8,128)(2,1)S(1)}, u32[]{:S(2)}, u32[]{:S(2)}) collective-permute-start(bf16[80,640]{1,0:T(8,128)(2,1)S(1)} %get-tuple-element.62), channel_id=1, source_target_pairs={{4,0},{6,2},{0,4},{2,6},{5,1},{7,3},{1,5},{3,7},{12,8},{14,10},{8,... | collective-permute-start | bytes 307208 | tf_op jit(solution)/shard_map/ppermute | solution.py:25
  122.1 5.4 %collective-permute-start.19 = (bf16[80,640]{1,0:T(8,128)(2,1)S(1)}, bf16[80,640]{1,0:T(8,128)(2,1)S(1)}, u32[]{:S(2)}, u32[]{:S(2)}) collective-permute-start(bf16[80,640]{1,0:T(8,128)(2,1)S(1)} %get-tuple-element.63), channel_id=1, source_target_pairs={{6,0},{0,2},{2,4},{4,6},{7,1},{1,3},{3,5},{5,7},{14,8},{8,10},{10,... | collective-permute-start | bytes 307208 | tf_op jit(solution)/shard_map/ppermute | solution.py:25
  128.3 8.4 %collective-permute-start.23 = (bf16[16,5120]{1,0:T(8,128)(2,1)S(1)}, bf16[16,5120]{1,0:T(8,128)(2,1)S(1)}, u32[]{:S(2)}, u32[]{:S(2)}) collective-permute-start(bf16[16,5120]{1,0:T(8,128)(2,1)S(1)} %get-tuple-element.67), channel_id=1, source_target_pairs={{16,0},{24,8},{0,16},{8,24},{17,1},{25,9},{1,17},{9,25},{18,2},{26... | collective-permute-start | bytes 491528 | tf_op jit(solution)/shard_map/ppermute | solution.py:25
  128.3 8.3 %collective-permute-start.22 = (bf16[80,640]{1,0:T(8,128)(2,1)S(1)}, bf16[80,640]{1,0:T(8,128)(2,1)S(1)}, u32[]{:S(2)}, u32[]{:S(2)}) collective-permute-start(bf16[80,640]{1,0:T(8,128)(2,1)S(1)} %get-tuple-element.66), channel_id=1, source_target_pairs={{8,0},{16,8},{24,16},{0,24},{9,1},{17,9},{25,17},{1,25},{10,2},{18... | collective-permute-start | bytes 307208 | tf_op jit(solution)/shard_map/ppermute | solution.py:25
  136.6 19.2 %slice-start = ((s8[5242880]{0:T(1024)(128)(4,1)}), s8[4194304]{0:T(1024)(128)(4,1)S(1)}, s32[]{:S(2)}) async-start(s8[5242880]{0:T(1024)(128)(4,1)} %bitcast.11), calls=%async_computation | async-start | bytes 8388608
  138.0 59.1 %collective-permute-start.31 = (bf16[96,5120]{1,0:T(8,128)(2,1)S(1)}, bf16[96,5120]{1,0:T(8,128)(2,1)S(1)}, u32[]{:S(2)}, u32[]{:S(2)}) collective-permute-start(bf16[96,5120]{1,0:T(8,128)(2,1)S(1)} %get-tuple-element.77), channel_id=1, source_target_pairs={{16,0},{24,8},{0,16},{8,24},{17,1},{25,9},{1,17},{9,25},{18,2},{26... | collective-permute-start | bytes 2949128 | tf_op jit(solution)/shard_map/ppermute | solution.py:25
  138.9 4.6 %collective-permute-start.24 = (bf16[80,640]{1,0:T(8,128)(2,1)S(1)}, bf16[80,640]{1,0:T(8,128)(2,1)S(1)}, u32[]{:S(2)}, u32[]{:S(2)}) collective-permute-start(bf16[80,640]{1,0:T(8,128)(2,1)S(1)} %get-tuple-element.68.refs_0_), channel_id=1, source_target_pairs={{6,0},{0,2},{2,4},{4,6},{7,1},{1,3},{3,5},{5,7},{14,8},{8,10},{10,... | collective-permute-start | bytes 307208 | tf_op jit(solution)/shard_map/ppermute | solution.py:25
  138.9 5.7 %collective-permute-start.25 = (bf16[80,640]{1,0:T(8,128)(2,1)S(1)}, bf16[80,640]{1,0:T(8,128)(2,1)S(1)}, u32[]{:S(2)}, u32[]{:S(2)}) collective-permute-start(bf16[80,640]{1,0:T(8,128)(2,1)S(1)} %get-tuple-element.68.refs_0_), channel_id=1, source_target_pairs={{4,0},{6,2},{0,4},{2,6},{5,1},{7,3},{1,5},{3,7},{12,8},{14,10},{8,... | collective-permute-start | bytes 307208 | tf_op jit(solution)/shard_map/ppermute | solution.py:25
  139.5 5.2 %collective-permute-start.26 = (bf16[80,640]{1,0:T(8,128)(2,1)S(1)}, bf16[80,640]{1,0:T(8,128)(2,1)S(1)}, u32[]{:S(2)}, u32[]{:S(2)}) collective-permute-start(bf16[80,640]{1,0:T(8,128)(2,1)S(1)} %get-tuple-element.68.refs_0_), channel_id=1, source_target_pairs={{2,0},{4,2},{6,4},{0,6},{3,1},{5,3},{7,5},{1,7},{10,8},{12,10},{14... | collective-permute-start | bytes 307208 | tf_op jit(solution)/shard_map/ppermute | solution.py:25
  144.7 11.2 %slice-start.1 = ((s8[5242880]{0:T(1024)(128)(4,1)}), s8[1048576]{0:T(1024)(128)(4,1)S(1)}, s32[]{:S(2)}) async-start(s8[5242880]{0:T(1024)(128)(4,1)} %bitcast.11), calls=%async_computation.1 | async-start | bytes 2097152
  153.8 37.8 %collective-permute-start.38 = (bf16[48,5120]{1,0:T(8,128)(2,1)S(1)}, bf16[48,5120]{1,0:T(8,128)(2,1)S(1)}, u32[]{:S(2)}, u32[]{:S(2)}) collective-permute-start(bf16[48,5120]{1,0:T(8,128)(2,1)S(1)} %get-tuple-element.86.refs_0_), channel_id=1, source_target_pairs={{1,0},{0,1},{3,2},{2,3},{5,4},{4,5},{7,6},{6,7},{9,8},{8,9},{11,10... | collective-permute-start | bytes 1474568 | tf_op jit(solution)/shard_map/ppermute | solution.py:25
  154.3 17.4 %collective-permute-start.36 = (bf16[48,2048]{1,0:T(8,128)(2,1)S(1)}, bf16[48,2048]{1,0:T(8,128)(2,1)S(1)}, u32[]{:S(2)}, u32[]{:S(2)}) collective-permute-start(bf16[48,2048]{1,0:T(8,128)(2,1)S(1)} %get-tuple-element.78.act.refs_4_), channel_id=1, source_target_pairs={{1,0},{0,1},{3,2},{2,3},{5,4},{4,5},{7,6},{6,7},{9,8},{8,9},{11,10... | collective-permute-start | bytes 589832 | tf_op jit(solution)/shard_map/ppermute | solution.py:25
  157.0 17.4 %collective-permute-start.32 = (bf16[80,640]{1,0:T(8,128)(2,1)S(1)}, bf16[80,640]{1,0:T(8,128)(2,1)S(1)}, u32[]{:S(2)}, u32[]{:S(2)}) collective-permute-start(bf16[80,640]{1,0:T(8,128)(2,1)S(1)} %get-tuple-element.81), channel_id=1, source_target_pairs={{2,0},{4,2},{6,4},{0,6},{3,1},{5,3},{7,5},{1,7},{10,8},{12,10},{14... | collective-permute-start | bytes 307208 | tf_op jit(solution)/shard_map/ppermute | solution.py:25
  158.1 15.8 %collective-permute-start.37 = (bf16[48,1024]{1,0:T(8,128)(2,1)S(1)}, bf16[48,1024]{1,0:T(8,128)(2,1)S(1)}, u32[]{:S(2)}, u32[]{:S(2)}) collective-permute-start(bf16[48,1024]{1,0:T(8,128)(2,1)S(1)} %get-tuple-element.79._.refs_6_), channel_id=1, source_target_pairs={{1,0},{0,1},{3,2},{2,3},{5,4},{4,5},{7,6},{6,7},{9,8},{8,9},{11,10... | collective-permute-start | bytes 294920 | tf_op jit(solution)/shard_map/ppermute | solution.py:25
  171.7 5.8 %collective-permute-start.33 = (bf16[80,640]{1,0:T(8,128)(2,1)S(1)}, bf16[80,640]{1,0:T(8,128)(2,1)S(1)}, u32[]{:S(2)}, u32[]{:S(2)}) collective-permute-start(bf16[80,640]{1,0:T(8,128)(2,1)S(1)} %get-tuple-element.82), channel_id=1, source_target_pairs={{4,0},{6,2},{0,4},{2,6},{5,1},{7,3},{1,5},{3,7},{12,8},{14,10},{8,... | collective-permute-start | bytes 307208 | tf_op jit(solution)/shard_map/ppermute | solution.py:25
  173.8 4.7 %collective-permute-start.34 = (bf16[80,640]{1,0:T(8,128)(2,1)S(1)}, bf16[80,640]{1,0:T(8,128)(2,1)S(1)}, u32[]{:S(2)}, u32[]{:S(2)}) collective-permute-start(bf16[80,640]{1,0:T(8,128)(2,1)S(1)} %get-tuple-element.83), channel_id=1, source_target_pairs={{6,0},{0,2},{2,4},{4,6},{7,1},{1,3},{3,5},{5,7},{14,8},{8,10},{10,... | collective-permute-start | bytes 307208 | tf_op jit(solution)/shard_map/ppermute | solution.py:25
  174.4 4.4 %collective-permute-start.28 = (bf16[80,640]{1,0:T(8,128)(2,1)S(1)}, bf16[80,640]{1,0:T(8,128)(2,1)S(1)}, u32[]{:S(2)}, u32[]{:S(2)}) collective-permute-start(bf16[80,640]{1,0:T(8,128)(2,1)S(1)} %get-tuple-element.73), channel_id=1, source_target_pairs={{2,0},{4,2},{6,4},{0,6},{3,1},{5,3},{7,5},{1,7},{10,8},{12,10},{14... | collective-permute-start | bytes 307208 | tf_op jit(solution)/shard_map/ppermute | solution.py:25
  177.5 11.7 %collective-permute-start.29 = (bf16[80,640]{1,0:T(8,128)(2,1)S(1)}, bf16[80,640]{1,0:T(8,128)(2,1)S(1)}, u32[]{:S(2)}, u32[]{:S(2)}) collective-permute-start(bf16[80,640]{1,0:T(8,128)(2,1)S(1)} %get-tuple-element.74), channel_id=1, source_target_pairs={{4,0},{6,2},{0,4},{2,6},{5,1},{7,3},{1,5},{3,7},{12,8},{14,10},{8,... | collective-permute-start | bytes 307208 | tf_op jit(solution)/shard_map/ppermute | solution.py:25
  178.6 10.6 %collective-permute-start.30 = (bf16[80,640]{1,0:T(8,128)(2,1)S(1)}, bf16[80,640]{1,0:T(8,128)(2,1)S(1)}, u32[]{:S(2)}, u32[]{:S(2)}) collective-permute-start(bf16[80,640]{1,0:T(8,128)(2,1)S(1)} %get-tuple-element.75), channel_id=1, source_target_pairs={{6,0},{0,2},{2,4},{4,6},{7,1},{1,3},{3,5},{5,7},{14,8},{8,10},{10,... | collective-permute-start | bytes 307208 | tf_op jit(solution)/shard_map/ppermute | solution.py:25
  178.8 18.3 %collective-permute-start.35 = (bf16[80,640]{1,0:T(8,128)(2,1)S(1)}, bf16[80,640]{1,0:T(8,128)(2,1)S(1)}, u32[]{:S(2)}, u32[]{:S(2)}) collective-permute-start(bf16[80,640]{1,0:T(8,128)(2,1)S(1)} %shard_map.121), channel_id=1, source_target_pairs={{24,0},{0,8},{8,16},{16,24},{25,1},{1,9},{9,17},{17,25},{26,2},{2,... | collective-permute-start | bytes 307208 | tf_op jit(solution)/shard_map/ppermute | solution.py:25

commit v3 on v2

--- a/solution.py
+++ b/solution.py
@@ -10,8 +10,7 @@
 CAP = 10
 PACK = 8
 PACKED = CAP * PACK
-FIRST = 64
-SECOND = 16
+FIRST = 48
 EPSILON = 1e-06
 F32 = jnp.float32
 BF16 = jnp.bfloat16
@@ -30,7 +29,7 @@
 
 
 def call(
-    kernel, outs, args, *, any_args=(), any_outs=(), scratch=(), vmem=VMEM_SMALL, flops=0
+    kernel, outs, args, *, any_args=(), any_outs=(), scratch=(), vmem=VMEM_SMALL
 ):
     outs = [jax.ShapeDtypeStruct(s, d) for s, d in outs]
     anywhere = pl.BlockSpec(memory_space=pl.ANY)
@@ -42,7 +41,7 @@
         out_specs=[anywhere if i in any_outs else near for i in range(len(outs))],
         scratch_shapes=list(scratch),
         compiler_params=pltpu.CompilerParams(vmem_limit_bytes=vmem),
-        cost_estimate=pl.CostEstimate(flops=flops, bytes_accessed=COST_BYTES, transcendentals=0),
+        cost_estimate=pl.CostEstimate(flops=0, bytes_accessed=COST_BYTES, transcendentals=0),
     )(*args)
 
 
@@ -142,31 +141,32 @@
             out[r, k] = jnp.where(hit2[r], new2[r], value).astype(BF16)
 
 
-def first_rows_kernel(tokens, routes, cotangent, raw, normed, piece, sem):
-    copy = pltpu.make_async_copy(cotangent.at[pl.ds(0, FIRST)], piece, sem)
+def copy_rows(source, start, stop, piece, sem):
+    copy = pltpu.make_async_copy(source.at[pl.ds(start, stop - start)], piece, sem)
     copy.start()
+    return copy
+
+
+def first_rows_kernel(
+    tokens, cotangent, routes, next_routes, prev_routes, _, far, raw, normed, t1, cot, piece, sem
+):
+    copy = copy_rows(far, 0, FIRST, piece, sem)
     values = pick(select_of(routes[0]), [tokens])
     raw[...] = values.astype(BF16)
     normed[...] = (values * inv_rms_of(values)).astype(BF16)
+    cot[...] = pick(select_of(prev_routes[0]), [cotangent]).astype(BF16)
+    t1[...] = pick(select_of(next_routes[0]), [tokens]).astype(BF16)
     copy.wait()
 
 
-def other_rows_kernel(tokens, cotangent, next_routes, prev_routes, t1, cot):
-    t1[...] = pick(select_of(next_routes[0]), [tokens]).astype(BF16)
-    cot[...] = pick(select_of(prev_routes[0]), [cotangent]).astype(BF16)
-
-
 def update0_kernel(n, *refs):
-    parts, (raw, routes, gates, next_routes, t1, tokens) = refs[:n], refs[n : n + 6]
-    upd, onward, piece, sem = refs[n + 9 :]
-    copy = pltpu.make_async_copy(tokens.at[pl.ds(0, SECOND)], piece, sem)
-    copy.start()
+    parts, (raw, routes, gates, next_routes, t1) = refs[:n], refs[n : n + 5]
+    upd, onward = refs[n + 7 :]
     select = select_of(routes[0])
     weight = slot_gates(select, routes[0], gates[0])
     fresh = (raw[...].astype(F32) + weight * summed(parts)).astype(BF16)
     onward[...] = merged(select_of(next_routes[0]), select, fresh, t1[...].astype(F32))
     upd[...] = fresh
-    copy.wait()
 
 
 def update1_kernel(n, *refs):
@@ -176,10 +176,8 @@
     upd[...] = (h[...].astype(F32) + weight * summed(parts)).astype(BF16)
 
 
-def enter1_kernel(h, cot, routes, gates, cotangent, _, out, piece, sem):
-    rows = cotangent.shape[0]
-    copy = pltpu.make_async_copy(cotangent.at[pl.ds(FIRST, rows - FIRST)], piece, sem)
-    copy.start()
+def enter1_kernel(h, cot, routes, gates, cotangent, out, piece, sem):
+    copy = copy_rows(cotangent, FIRST, cotangent.shape[0], piece, sem)
     values = h[...].astype(F32)
     out[:PACKED] = (values * inv_rms_of(values)).astype(BF16)
     weight = slot_gates(select_of(routes[1]), routes[1], gates[1])
@@ -196,20 +194,14 @@
 
 
 def grad1_kernel(n, *refs):
-    parts, (h, cot, tokens) = refs[:n], refs[n : n + 3]
-    upd, piece, sem = refs[n + 5 :]
-    copy = pltpu.make_async_copy(tokens.at[pl.ds(SECOND, SECOND)], piece, sem)
-    copy.start()
+    parts, (h, cot, upd) = refs[:n], refs[n:]
     upd[...] = state_grad(parts, h[...], cot[...])
-    copy.wait()
 
 
 def enter0_kernel(
-    upd1, next_routes, routes, gates, bulk_a, bulk_b, tokens, _, c0, out, piece, sem
+    upd1, next_routes, routes, gates, bulk_a, bulk_b, tokens, _, __, c0, out, piece, sem
 ):
-    left = tokens.shape[0] - 2 * SECOND
-    copy = pltpu.make_async_copy(tokens.at[pl.ds(2 * SECOND, left)], piece, sem)
-    copy.start()
+    copy = copy_rows(tokens, 0, tokens.shape[0], piece, sem)
     select = select_of(routes[0])
     old = pick(select, [bulk_a, bulk_b])
     rows = merged(select, select_of(next_routes[0]), upd1[...], old)
@@ -226,11 +218,9 @@
     )
 
 
-def finish_state_kernel(
-    bulk_a, bulk_b, bulk_c, upd0, prev2_routes, upd1, prev_routes, out
-):
+def finish_state_kernel(bulk, upd0, prev2_routes, upd1, prev_routes, out):
     place_rows(
-        [bulk_a, bulk_b, bulk_c],
+        [bulk],
         select_of(prev2_routes[0]),
         upd0[...],
         select_of(prev_routes[0]),
@@ -315,9 +305,9 @@
 
 def down_kernel(n, act, down, _, *refs):
     parts, (unpacked, held) = refs[:n], refs[n:]
-    hidden = down.shape[0]
+    hidden, width = down.shape
     for c in range(PACK):
-        value = dot(act[:, hidden : 2 * hidden], down[:, columns(c, down.shape[1])])
+        value = dot(act[:, width + hidden :], down[:, columns(c, width)])
         spread_rows(value, c, n, held.at[c], unpacked)
     for i, p in enumerate(parts):
         p[...] = unpacked[i].astype(BF16)
@@ -335,7 +325,7 @@
 
 def tick1_kernel(n, *refs):
     blocks, (act0, gate, up, down, _) = refs[:n], refs[n : n + 5]
-    xg, small = refs[n + 5 : n + 7]
+    x_act, g_grad = refs[n + 5 : n + 7]
     parts = refs[n + 7 : 2 * n + 7]
     gate_v, up_v, down_v, sems, unpacked, whole32, held, x, g = refs[2 * n + 7 :]
     copies = weight_copies(gate, up, down, gate_v, up_v, down_v, sems)
@@ -344,10 +334,10 @@
             c.start()
     gather_rows(blocks, 0, unpacked, whole32.at[0], x)
     gather_rows(blocks, PACKED, unpacked, whole32.at[1], g)
-    rows, hidden = act0.shape
-    xg[:rows] = x[...]
-    xg[rows:] = g[...]
-    width = gate.shape[0]
+    width, hidden = gate.shape
+    x_act[:, :width] = x[...]
+    x_act[:, width : width + hidden] = act0[...]
+    g_grad[:, :width] = g[...]
     acc_g = jnp.zeros(act0.shape, F32)
     acc_u = jnp.zeros(act0.shape, F32)
     acc_a = jnp.zeros(act0.shape, F32)
@@ -360,18 +350,17 @@
         cd.wait()
         acc_a = acc_a + dot(g[:, k], down_v[:, k], 1, 1)
     gg, gu = silu_grads(acc_g, acc_u, acc_a)
-    small[:, :hidden] = act0[...]
-    small[:, hidden : 2 * hidden] = (acc_g * jax.nn.sigmoid(acc_g) * acc_u).astype(BF16)
-    small[:, 2 * hidden : 3 * hidden] = gg
-    small[:, 3 * hidden :] = gu
+    x_act[:, width + hidden :] = (acc_g * jax.nn.sigmoid(acc_g) * acc_u).astype(BF16)
+    g_grad[:, width : width + hidden] = gg
+    g_grad[:, width + hidden :] = gu
     back_rows(gg, gu, gate_v, up_v, held, unpacked, parts)
 
 
 def tick0_kernel(n, *refs):
-    blocks, (pre_gate, pre_up, gate, up, down, _) = refs[:n], refs[n : n + 6]
-    g, small = refs[n + 6 : n + 8]
-    parts = refs[n + 8 : 2 * n + 8]
-    gate_v, up_v, down_v, sems, unpacked, whole32, held = refs[2 * n + 8 :]
+    blocks, (pre_gate, pre_up, gate, up, down) = refs[:n], refs[n : n + 5]
+    (g_grad,) = refs[n + 5 : n + 6]
+    parts = refs[n + 6 : 2 * n + 6]
+    gate_v, up_v, down_v, sems, unpacked, whole32, held, g = refs[2 * n + 6 :]
     copies = weight_copies(gate, up, down, gate_v, up_v, down_v, sems)
     for _, _, cd in copies:
         cd.start()
@@ -379,15 +368,16 @@
         cg.start()
         cu.start()
     gather_rows(blocks, 0, unpacked, whole32, g)
-    hidden = pre_gate.shape[1]
+    width, hidden = gate.shape
+    g_grad[:, :width] = g[...]
     acc_a = jnp.zeros(pre_gate.shape, F32)
     for c, (_, _, cd) in enumerate(copies):
-        k = columns(c, gate.shape[0])
+        k = columns(c, width)
         cd.wait()
         acc_a = acc_a + dot(g[:, k], down_v[:, k], 1, 1)
     gg, gu = silu_grads(pre_gate[...], pre_up[...], acc_a)
-    small[:, :hidden] = gg
-    small[:, hidden:] = gu
+    g_grad[:, width : width + hidden] = gg
+    g_grad[:, width + hidden :] = gu
     for cg, cu, _ in copies:
         cg.wait()
         cu.wait()
@@ -399,61 +389,66 @@
 
 
 def input_grad_kernel(m, *refs):
-    x0, xg, small1, small0 = (refs[i * m : (i + 1) * m] for i in range(4))
-    gate_out, up_out = refs[4 * m :]
-    hidden = gate_out.shape[1]
-    x_t = whole_of([b[...] for b in x0] + [b[...] for b in xg]).T
-    gg = [b[:, :hidden] for b in small0] + [b[:, 2 * hidden : 3 * hidden] for b in small1]
-    gu = [b[:, hidden:] for b in small0] + [b[:, 3 * hidden :] for b in small1]
-    gate_out[...] = dot(x_t, whole_of(gg)).astype(BF16)
-    up_out[...] = dot(x_t, whole_of(gu)).astype(BF16)
+    x0, x1, gates0, ups0, gates1, ups1 = (refs[i * m : (i + 1) * m] for i in range(6))
+    gate_out, up_out = refs[6 * m :]
+    x_t = whole_of([b[...] for b in x0 + x1]).T
+    gate_out[...] = dot(x_t, whole_of([b[...] for b in gates0 + gates1])).astype(BF16)
+    up_out[...] = dot(x_t, whole_of([b[...] for b in ups0 + ups1])).astype(BF16)
 
 
 def down_grad_kernel(m, *refs):
-    g0, xg, small1 = (refs[i * m : (i + 1) * m] for i in range(3))
-    (down_out,) = refs[3 * m :]
-    hidden = down_out.shape[0]
-    act = [b[:, :hidden] for b in small1] + [b[:, hidden : 2 * hidden] for b in small1]
-    grads = [b[...] for b in g0] + [b[...] for b in xg]
-    down_out[...] = dot(whole_of(act), whole_of(grads), 0, 0).astype(BF16)
-
-
-def input_grads(x0, xg, small1, small0):
-    m = len(x0)
-    rows, width = x0[0].shape
-    hidden = small0[0].shape[1] // 2
+    g0, g1, act0, act1 = (refs[i * m : (i + 1) * m] for i in range(4))
+    (down_out,) = refs[4 * m :]
+    act = whole_of([b[...] for b in act0 + act1])
+    down_out[...] = dot(act, whole_of([b[...] for b in g0 + g1]), 0, 0).astype(BF16)
+
+
+def grads_call(kernel, wide, fixed, outs, out_block, out_index, hidden):
+    rows = wide[0].shape[0]
+    width = max(max(s) for s in outs)
     step = width // PACK
-    wide = pl.BlockSpec((rows, step), lambda c: (0, c))
-    whole = [pl.BlockSpec(a.shape, lambda c: (0, 0)) for a in small1 + small0]
-    out = pl.BlockSpec((step, hidden), lambda c: (c, 0))
     return pl.pallas_call(
-        functools.partial(input_grad_kernel, m),
+        kernel,
         grid=(PACK,),
-        out_shape=[jax.ShapeDtypeStruct((width, hidden), BF16)] * 2,
-        in_specs=[wide] * (2 * m) + whole,
-        out_specs=[out, out],
+        out_shape=[jax.ShapeDtypeStruct(s, BF16) for s in outs],
+        in_specs=[pl.BlockSpec((rows, step), lambda c: (0, c)) for _ in wide]
+        + [
+            pl.BlockSpec((rows, hidden), functools.partial(lambda i, c: (0, i), at))
+            for _, at in fixed
+        ],
+        out_specs=[pl.BlockSpec(out_block, out_index)] * len(outs),
         compiler_params=pltpu.CompilerParams(vmem_limit_bytes=VMEM_SMALL),
         cost_estimate=pl.CostEstimate(flops=0, bytes_accessed=COST_BYTES, transcendentals=0),
-    )(*x0, *xg, *small1, *small0)
-
-
-def down_grads(g0, xg, small1):
-    m = len(g0)
-    rows, width = g0[0].shape
-    hidden = small1[0].shape[1] // 4
-    step = width // PACK
-    wide = pl.BlockSpec((rows, step), lambda c: (0, c))
-    second = pl.BlockSpec((rows, step), lambda c: (1, c))
-    whole = [pl.BlockSpec(a.shape, lambda c: (0, 0)) for a in small1]
-    return pl.pallas_call(
-        functools.partial(down_grad_kernel, m),
-        grid=(PACK,),
-        out_shape=[jax.ShapeDtypeStruct((hidden, width), BF16)],
-        in_specs=[wide] * m + [second] * m + whole,
-        out_specs=[pl.BlockSpec((hidden, step), lambda c: (0, c))],
-        compiler_params=pltpu.CompilerParams(vmem_limit_bytes=VMEM_SMALL),
-        cost_estimate=pl.CostEstimate(flops=0, bytes_accessed=COST_BYTES, transcendentals=0),
-    )(*g0, *xg, *small1)
+    )(*wide, *(a for a, _ in fixed))
+
+
+def input_grads(x0, x_act1, g_grad0, g_grad1, width, hidden):
+    first = width // hidden
+    return grads_call(
+        functools.partial(input_grad_kernel, len(x0)),
+        x0 + x_act1,
+        [(a, first) for a in g_grad0]
+        + [(a, first + 1) for a in g_grad0]
+        + [(a, first) for a in g_grad1]
+        + [(a, first + 1) for a in g_grad1],
+        [(width, hidden)] * 2,
+        (width // PACK, hidden),
+        lambda c: (c, 0),
+        hidden,
+    )
+
+
+def down_grads(g_grad0, g_grad1, x_act1, width, hidden):
+    first = width // hidden
+    return grads_call(
+        functools.partial(down_grad_kernel, len(g_grad0)),
+        g_grad0 + g_grad1,
+        [(a, first) for a in x_act1] + [(a, first + 1) for a in x_act1],
+        [(hidden, width)],
+        (hidden, width // PACK),
+        lambda c: (0, c),
+        hidden,
+    )
 
 
 def from_group(block):
@@ -490,130 +485,111 @@
         pltpu.VMEM((rows, width), F32),
         pltpu.VMEM((PACK, rows, step), F32),
     ]
-    tick1_scratch = list(scratch)
-    tick1_scratch[5] = pltpu.VMEM((2, rows, width), F32)
-    tick1_scratch += [pltpu.VMEM((rows, width), BF16)] * 2
-    matmul = 0
+    both = pltpu.VMEM((rows, width), BF16)
+    tick1_scratch = [*scratch[:5], pltpu.VMEM((2, rows, width), F32), scratch[6], both, both]
+    wide = ((rows, width + 2 * hidden), BF16)
 
     next_routes = shifted(routes[1:], "section", -1)
     prev_routes = shifted(routes[1:], "section", 1)
     prev2_routes = shifted(routes[:1], "section", 2)
 
-    raw0, normed0, piece = call(
+    raw0, normed0, t1, cot1, piece = call(
         first_rows_kernel,
-        [one, one, ((FIRST, width), BF16)],
-        [tokens, routes, cotangent],
-        any_args=(2,),
-        any_outs=(2,),
+        [one, one, one, one, ((FIRST, width), BF16)],
+        [tokens, cotangent, routes, next_routes, prev_routes, prev2_routes, cotangent],
+        any_args=(5, 6),
+        any_outs=(4,),
         scratch=[pltpu.SemaphoreType.DMA],
     )
     cot_a = shifted(piece, "section", -2)
-    x0_blocks = from_group(normed0)
-    t1, cot1 = call(
-        other_rows_kernel, [one, one], [tokens, cotangent, next_routes, prev_routes]
-    )
     cot1 = shifted(cot1, "section", -1)
+    blocks = from_group(normed0)
     x0, pre_gate0, pre_up0, act0, *parts = call(
         part(forward_kernel, n),
         [((rows, width), BF16), ((rows, hidden), F32), ((rows, hidden), F32)]
         + [((rows, hidden), BF16)]
         + [one] * n,
-        [*x0_blocks, gate, up, down, t1],
+        [*blocks, gate, up, down, t1],
         any_args=(n, n + 1, n + 2, n + 3),
         scratch=scratch,
         vmem=VMEM_BIG,
-        flops=3 * matmul,
     )
     parts = to_group(parts)
-    upd0, h1, piece = call(
+    upd0, h1 = call(
         part(update0_kernel, n),
-        [one, one, ((SECOND, width), BF16)],
-        [*parts, raw0, routes, gates, next_routes, t1, tokens, cot_a, cot1, prev2_routes],
-        any_args=(n + 5, n + 6, n + 7, n + 8),
-        any_outs=(2,),
-        scratch=[pltpu.SemaphoreType.DMA],
+        [one, one],
+        [*parts, raw0, routes, gates, next_routes, t1, cot_a, cot1],
+        any_args=(n + 5, n + 6),
     )
     h1 = shifted(h1, "section", 1)
-    tok_a = shifted(piece, "section", 2)
     upd0 = shifted(upd0, "section", 2)
 
     enter1, piece = call(
         enter1_kernel,
         [((2 * PACKED, step), BF16), ((own - FIRST, width), BF16)],
-        [h1, cot1, routes, gates, cotangent, tok_a],
-        any_args=(4, 5),
+        [h1, cot1, routes, gates, cotangent],
+        any_args=(4,),
         any_outs=(1,),
         scratch=[pltpu.SemaphoreType.DMA],
     )
     cot_b = shifted(piece, "section", -2)
     blocks = from_group(enter1)
     x0_all = copies_of(x0)
-    xg1, small1, *parts = call(
+    x_act1, g_grad1, *parts = call(
         part(tick1_kernel, n),
-        [((2 * rows, width), BF16), ((rows, 4 * hidden), BF16)] + [one] * n,
-        [*blocks, act0, gate, up, down, upd0],
+        [wide, wide] + [one] * n,
+        [*blocks, act0, gate, up, down, x0_all[-1]],
         any_args=(n + 1, n + 2, n + 3, n + 4),
         scratch=tick1_scratch,
         vmem=VMEM_BIG,
-        flops=5 * matmul,
     )
     parts = to_group(parts)
-    upd1, piece = call(
-        part(grad1_kernel, n),
-        [one, ((SECOND, width), BF16)],
-        [*parts, h1, cot1, tokens, cot_b, x0_all[-1]],
-        any_args=(n + 2, n + 3, n + 4),
-        any_outs=(1,),
-        scratch=[pltpu.SemaphoreType.DMA],
-    )
-    upd1 = shifted(upd1, "section", -1)
-    tok_b = shifted(piece, "section", 2)
-    xg1_all = copies_of(xg1)
-
-    c0, enter0, piece = call(
-        enter0_kernel,
-        [one, one, ((own - 2 * SECOND, width), BF16)],
-        [upd1, next_routes, routes, gates, cot_a, cot_b, tokens, tok_b],
-        any_args=(6, 7),
-        any_outs=(2,),
-        scratch=[pltpu.SemaphoreType.DMA],
-    )
-    tok_c = shifted(piece, "section", 2)
-    blocks = from_group(enter0)
-    g0, small0, *parts = call(
-        part(tick0_kernel, n),
-        [((rows, width), BF16), ((rows, 2 * hidden), BF16)] + [one] * n,
-        [*blocks, pre_gate0, pre_up0, gate, up, down, xg1_all[-1]],
-        any_args=(n + 2, n + 3, n + 4, n + 5),
-        scratch=scratch,
-        vmem=VMEM_BIG,
-        flops=3 * matmul,
-    )
-    parts = to_group(parts)
+    (upd1,) = call(part(grad1_kernel, n), [one], [*parts, h1, cot1])
     outs = call(
         part(down_kernel, n),
         [one] * n,
-        [small1, down, small0],
+        [x_act1, down, upd1],
         any_args=(2,),
         scratch=[scratch[4], scratch[6]],
         vmem=VMEM_BIG,
-        flops=matmul,
-    )
-    outs = to_group(outs)
-    (last1,) = call(part(update1_kernel, n), [one], [*outs, h1, routes, gates])
-    last1 = shifted(last1, "section", 1)
-    small1_all = copies_of(small1)
-    gate_out, up_out = input_grads(x0_all, xg1_all, small1_all, copies_of(small0))
-    (down_out,) = down_grads(copies_of(g0), xg1_all, small1_all)
+    )
+    upd1 = shifted(upd1, "section", -1)
+    x_act1_all, g_grad1_all = copies_of(x_act1), copies_of(g_grad1)
+
+    c0, enter0, piece = call(
+        enter0_kernel,
+        [one, one, (tokens.shape, BF16)],
+        [upd1, next_routes, routes, gates, cot_a, cot_b, tokens, outs[0], x_act1_all[-1]],
+        any_args=(6, 7, 8),
+        any_outs=(2,),
+        scratch=[pltpu.SemaphoreType.DMA],
+    )
+    tok = shifted(piece, "section", 2)
+    blocks = from_group(enter0)
+    g_grad0, *parts = call(
+        part(tick0_kernel, n),
+        [wide] + [one] * n,
+        [*blocks, pre_gate0, pre_up0, gate, up, down],
+        any_args=(n + 2, n + 3, n + 4),
+        scratch=scratch + [both],
+        vmem=VMEM_BIG,
+    )
+    parts = to_group(parts)
+    g_grad0_all = copies_of(g_grad0)
     (grad,) = call(
         part(finish_grad_kernel, n),
         [(tokens.shape, BF16)],
         [*parts, raw0, c0, routes, upd1, next_routes, cot_a, cot_b],
     )
+    outs = to_group(outs)
+    (last1,) = call(part(update1_kernel, n), [one], [*outs, h1, routes, gates])
+    last1 = shifted(last1, "section", 1)
+    gate_out, up_out = input_grads(x0_all, x_act1_all, g_grad0_all, g_grad1_all, width, hidden)
+    (down_out,) = down_grads(g_grad0_all, g_grad1_all, x_act1_all, width, hidden)
     (state,) = call(
         finish_state_kernel,
         [(tokens.shape, BF16)],
-        [tok_a, tok_b, tok_c, upd0, prev2_routes, last1, prev_routes],
+        [tok, upd0, prev2_routes, last1, prev_routes],
     )
     return (grad, state, gate_out[None], up_out[None], down_out[None])
 

time: 200 us -> 159 us (0.80)
  waiting for transfers between devices: 88.5 us -> 52.4 us
  starting transfers between devices: 57.1 us -> 50.3 us
  Pallas kernels: 48.2 us -> 50.9 us
    ppermute x39 -> x36, waiting for transfers between devices: 88.5 us -> 52.4 us  [shifted(): lax.ppermute(block, axis, [((i - distance) % size, i) for i in range(size)])]
    ppermute x39 -> x36, starting transfers between devices: 57.1 us -> 50.3 us  [shifted(): lax.ppermute(block, axis, [((i - distance) % size, i) for i in range(size)])]
    pallas_call x13 -> x12, Pallas kernels: 36.2 us -> 37.7 us  [call(): pl.pallas_call(kernel, out_shape=outs, in_specs=[anywhere if i in any_arg...]
    unnamed x20 -> x14, local copies, waits for them, and re-layouts: 4.66 us -> 3.34 us
  transfers between devices with their start and end apart: 39 -> 36, of which waited for: 17 -> 21; matrix products, arithmetic and copies ran while one was open for 0% -> 0% of each run, Pallas kernels for 22% -> 29%
where the time goes in v3:
time: 159 us; the launch traced here: 158 us
  waiting for transfers between devices  52.4 us (33%)
  Pallas kernels  50.9 us (32%)
  starting transfers between devices  50.3 us (32%)
  local copies, waits for them, and re-layouts  4.04 us (3%)
    ppermute x36, waiting for transfers between devices, shifted(): lax.ppermute(block, axis, [((i - distance) % size, i) for i in range(size)])  52.4 us
    ppermute x36, starting transfers between devices, shifted(): lax.ppermute(block, axis, [((i - distance) % size, i) for i in range(size)])  50.3 us
    pallas_call x12, Pallas kernels, call(): pl.pallas_call(kernel, out_shape=outs, in_specs=[anywhere if i in any_arg...  37.7 us
    pallas_call x2, Pallas kernels, grads_call(): pl.pallas_call(kernel, grid=(PACK,), out_shape=[jax.ShapeDtypeStruct(s, B...  13.2 us
    unnamed x14, local copies, waits for them, and re-layouts  3.34 us
  transfers between devices with their start and end apart: 36, of which 21 were waited for; matrix products, arithmetic and copies ran while one was open for 0% of the time, Pallas kernels for 29%

profile of v3, /device:TPU:0, one launch (start us, length us, event | category | flops | bytes accessed | tf_op | source)
XLA Modules:
  0.0 158.4 jit_solution(17359695781233186836)
XLA Ops:
  0.6 0.7 fusion
  1.3 5.0 %collective-permute-start = (s32[1,4,128]{2,1,0:T(4,128)S(1)}, s32[1,4,128]{2,1,0:T(4,128)S(1)}, u32[]{:S(2)}, u32[]{:S(2)}) collective-permute-start(s32[1,4,128]{2,1,0:T(4,128)S(1)} %get-tuple-element.80), channel_id=1, source_target_pairs={{8,0},{16,8},{24,16},{0,24},{9,1},{17,9},{25,17},{1,25},{10,2},{18... | collective-permute-start | bytes 6152 | tf_op jit(solution)/shard_map/ppermute | solution.py:24
  6.4 1.0 collective-permute-start.2
  7.4 0.3 collective-permute-done.next_routes.refs_7_.refs_8_
  7.7 4.1 %collective-permute-done.1.prev_routes = s32[1,4,128]{2,1,0:T(4,128)S(1)} collective-permute-done((s32[1,4,128]{2,1,0:T(4,128)S(1)}, s32[1,4,128]{2,1,0:T(4,128)S(1)}, u32[]{:S(2)}, u32[]{:S(2)}) %collective-permute-start.1) | collective-permute-done | bytes 2080 | tf_op jit(solution)/shard_map/ppermute | solution.py:24
  11.8 1.3 copy-done
  13.1 1.3 copy-done.2
  14.4 0.7 copy-done.4
  15.1 1.8 %shard_map.110 = (bf16[80,640]{1,0:T(8,128)(2,1)S(1)}, bf16[80,640]{1,0:T(8,128)(2,1)S(1)}, bf16[80,640]{1,0:T(8,128)(2,1)S(1)}, bf16[80,640]{1,0:T(8,128)(2,1)S(1)}, bf16[48,5120]{1,0:T(8,128)(2,1)S(1)}) custom-call(bf16[128,5120]{1,0:T(8,128)(2,1)S(1)} %copy-done.2, bf16[128,5120]{1,0:T(8,128)(2,1)S(1)} %copy-done, s32[2,4,128]{2,1,0:T(4,128)S(1)} %bitcast.9, ...), custom_call_target="tpu_custom_call" | custom-call | bytes 1024 | tf_op jit(solution)/shard_map/pallas_call | solution.py:37
  17.1 1.6 collective-permute-start.4
  18.7 1.4 collective-permute-start.5
  20.1 2.9 %collective-permute-start.10 = (bf16[80,640]{1,0:T(8,128)(2,1)S(1)}, bf16[80,640]{1,0:T(8,128)(2,1)S(1)}, u32[]{:S(2)}, u32[]{:S(2)}) collective-permute-start(bf16[80,640]{1,0:T(8,128)(2,1)S(1)} %get-tuple-element.50), channel_id=1, source_target_pairs={{8,0},{16,8},{24,16},{0,24},{9,1},{17,9},{25,17},{1,25},{10,2},{18... | collective-permute-start | bytes 307208 | tf_op jit(solution)/shard_map/ppermute | solution.py:24
  23.0 0.5 collective-permute-done.5.refs_3_
  23.5 6.5 %shard_map.111 = (bf16[48,5120]{1,0:T(8,128)(2,1)S(1)}, f32[48,512]{1,0:T(8,128)S(1)}, f32[48,512]{1,0:T(8,128)S(1)}, bf16[48,512]{1,0:T(8,128)(2,1)S(1)}, bf16[...) custom-call(bf16[80,640]{1,0:T(8,128)(2,1)S(1)} %get-tuple-element.4, ...), custom_call_target="tpu_custom_call" | custom-call | bytes 1024 | tf_op jit(solution)/shard_map/pallas_call | solution.py:37
  30.1 1.6 collective-permute-start.15
  31.6 1.9 %collective-permute-start.6 = (bf16[80,640]{1,0:T(8,128)(2,1)S(1)}, bf16[80,640]{1,0:T(8,128)(2,1)S(1)}, u32[]{:S(2)}, u32[]{:S(2)}) collective-permute-start(bf16[80,640]{1,0:T(8,128)(2,1)S(1)} %get-tuple-element.45), channel_id=1, source_target_pairs={{2,0},{4,2},{6,4},{0,6},{3,1},{5,3},{7,5},{1,7},{10,8},{12,10},{14... | collective-permute-start | bytes 307208 | tf_op jit(solution)/shard_map/ppermute | solution.py:24
  33.8 2.6 %collective-permute-done.6.refs_1_ = bf16[80,640]{1,0:T(8,128)(2,1)S(1)} collective-permute-done((bf16[80,640]{1,0:T(8,128)(2,1)S(1)}, bf16[80,640]{1,0:T(8,128)(2,1)S(1)}, u32[]{:S(2)}, u32[]{:S(2)}) %collective-permute-start.6) | collective-permute-done | bytes 102432 | tf_op jit(solution)/shard_map/ppermute | solution.py:24
  36.4 2.8 %collective-permute-done.7.refs_2_ = bf16[80,640]{1,0:T(8,128)(2,1)S(1)} collective-permute-done((bf16[80,640]{1,0:T(8,128)(2,1)S(1)}, bf16[80,640]{1,0:T(8,128)(2,1)S(1)}, u32[]{:S(2)}, u32[]{:S(2)}) %collective-permute-start.7) | collective-permute-done | bytes 102432 | tf_op jit(solution)/shard_map/ppermute | solution.py:24
  39.2 0.9 collective-permute-done.9.refs_9_.bulk_a
  40.1 0.5 shard_map.112
  40.5 6.8 %collective-permute-start.11 = (bf16[80,640]{1,0:T(8,128)(2,1)S(1)}, bf16[80,640]{1,0:T(8,128)(2,1)S(1)}, u32[]{:S(2)}, u32[]{:S(2)}) collective-permute-start(bf16[80,640]{1,0:T(8,128)(2,1)S(1)} %get-tuple-element.51), channel_id=1, source_target_pairs={{24,0},{0,8},{8,16},{16,24},{25,1},{1,9},{9,17},{17,25},{26,2},{2,... | collective-permute-start | bytes 307208 | tf_op jit(solution)/shard_map/ppermute | solution.py:24
  47.3 2.3 %collective-permute-done.11.h.refs_4_ = bf16[80,640]{1,0:T(8,128)(2,1)S(1)} collective-permute-done((bf16[80,640]{1,0:T(8,128)(2,1)S(1)}, bf16[80,640]{1,0:T(8,128)(2,1)S(1)}, u32[]{:S(2)}, u32[]{:S(2)}) %collective-permute-start.11) | collective-permute-done | bytes 102432 | tf_op jit(solution)/shard_map/ppermute | solution.py:24
  49.6 0.5 shard_map.113
  50.1 1.9 %collective-permute-start.20 = (bf16[80,5120]{1,0:T(8,128)(2,1)S(1)}, bf16[80,5120]{1,0:T(8,128)(2,1)S(1)}, u32[]{:S(2)}, u32[]{:S(2)}) collective-permute-start(bf16[80,5120]{1,0:T(8,128)(2,1)S(1)} %get-tuple-element.59), channel_id=1, source_target_pairs={{16,0},{24,8},{0,16},{8,24},{17,1},{25,9},{1,17},{9,25},{18,2},{26... | collective-permute-start | bytes 2457608 | tf_op jit(solution)/shard_map/ppermute | solution.py:24
  52.0 1.5 collective-permute-start.13
  53.5 1.4 collective-permute-start.14
  55.0 3.8 %collective-permute-done.12.refs_1_ = bf16[160,640]{1,0:T(8,128)(2,1)S(1)} collective-permute-done((bf16[160,640]{1,0:T(8,128)(2,1)S(1)}, bf16[160,640]{1,0:T(8,128)(2,1)S(1)}, u32[]{:S(2)}, u32[]{:S(2)}) %collective-permute-start.12) | collective-permute-done | bytes 204832 | tf_op jit(solution)/shard_map/ppermute | solution.py:24
  58.8 1.1 collective-permute-done.13.refs_2_
  59.9 2.9 %collective-permute-done.14.refs_3_ = bf16[160,640]{1,0:T(8,128)(2,1)S(1)} collective-permute-done((bf16[160,640]{1,0:T(8,128)(2,1)S(1)}, bf16[160,640]{1,0:T(8,128)(2,1)S(1)}, u32[]{:S(2)}, u32[]{:S(2)}) %collective-permute-start.14) | collective-permute-done | bytes 204832 | tf_op jit(solution)/shard_map/ppermute | solution.py:24
  62.8 9.4 %shard_map.114 = (bf16[48,6144]{1,0:T(8,128)(2,1)S(1)}, bf16[48,6144]{1,0:T(8,128)(2,1)S(1)}, bf16[80,640]{1,0:T(8,128)(2,1)S(1)}, bf16[80,640]{1,0:T(8,128)(2,1...) custom-call(bf16[160,640]{1,0:T(8,128)(2,1)S(1)} %get-tuple-element.52.refs_0_, ...), custom_call_target="tpu_custom_call" | custom-call | bytes 1024 | tf_op jit(solution)/shard_map/pallas_call | solution.py:37
  72.2 1.6 collective-permute-start.21
  73.8 1.6 %collective-permute-start.16 = (bf16[80,640]{1,0:T(8,128)(2,1)S(1)}, bf16[80,640]{1,0:T(8,128)(2,1)S(1)}, u32[]{:S(2)}, u32[]{:S(2)}) collective-permute-start(bf16[80,640]{1,0:T(8,128)(2,1)S(1)} %get-tuple-element.56), channel_id=1, source_target_pairs={{2,0},{4,2},{6,4},{0,6},{3,1},{5,3},{7,5},{1,7},{10,8},{12,10},{14... | collective-permute-start | bytes 307208 | tf_op jit(solution)/shard_map/ppermute | solution.py:24
  75.4 0.5 collective-permute-start.17
  75.9 2.4 %collective-permute-done.16.refs_1_ = bf16[80,640]{1,0:T(8,128)(2,1)S(1)} collective-permute-done((bf16[80,640]{1,0:T(8,128)(2,1)S(1)}, bf16[80,640]{1,0:T(8,128)(2,1)S(1)}, u32[]{:S(2)}, u32[]{:S(2)}) %collective-permute-start.16) | collective-permute-done | bytes 102432 | tf_op jit(solution)/shard_map/ppermute | solution.py:24
  78.3 3.0 %collective-permute-done.17.refs_2_ = bf16[80,640]{1,0:T(8,128)(2,1)S(1)} collective-permute-done((bf16[80,640]{1,0:T(8,128)(2,1)S(1)}, bf16[80,640]{1,0:T(8,128)(2,1)S(1)}, u32[]{:S(2)}, u32[]{:S(2)}) %collective-permute-start.17) | collective-permute-done | bytes 102432 | tf_op jit(solution)/shard_map/ppermute | solution.py:24
  81.3 0.4 shard_map.115._
  81.7 3.2 %collective-permute-start.19 = (bf16[80,640]{1,0:T(8,128)(2,1)S(1)}, bf16[80,640]{1,0:T(8,128)(2,1)S(1)}, u32[]{:S(2)}, u32[]{:S(2)}) collective-permute-start(bf16[80,640]{1,0:T(8,128)(2,1)S(1)} %shard_map.115._), channel_id=1, source_target_pairs={{8,0},{16,8},{24,16},{0,24},{9,1},{17,9},{25,17},{1,25},{10,2},{18... | collective-permute-start | bytes 307208 | tf_op jit(solution)/shard_map/ppermute | solution.py:24
  84.9 3.6 %shard_map.116 = (bf16[80,640]{1,0:T(8,128)(2,1)S(1)}, bf16[80,640]{1,0:T(8,128)(2,1)S(1)}, bf16[80,640]{1,0:T(8,128)(2,1)S(1)}, bf16[80,640]{1,0:T(8,128)(2,1)S(1)}) custom-call(bf16[48,6144]{1,0:T(8,128)(2,1)S(1)} %get-tuple-element.60.act.refs_2_.refs_4_.refs_6_, bf16[512,5120]{1,0:T(8,128)(2,1)} %bitcast.21, bf16[80,640]{1,0:T(8,128)(2,1)S(1)} %shard_map.115._), custom_call_target="tpu_custom_call" | custom-call | bytes 1024 | tf_op jit(solution)/shard_map/pallas_call | solution.py:37
  88.5 0.8 collective-permute-done.19.upd1.refs_7_
  89.3 1.2 shard_map.117
  90.6 0.8 collective-permute-start.23
  91.4 1.4 collective-permute-start.24
  92.8 1.3 collective-permute-start.35
  94.1 1.2 collective-permute-done.22.refs_1_
  95.2 1.1 collective-permute-done.23.refs_2_
  96.4 9.0 %shard_map.118 = (bf16[48,6144]{1,0:T(8,128)(2,1)S(1)}, bf16[80,640]{1,0:T(8,128)(2,1)S(1)}, bf16[80,640]{1,0:T(8,128)(2,1)S(1)}, bf16[80,640]{1,0:T(8,128)(2,1)S(1)}, bf16[80,640]{1,0:T(8,128)(2,1)S(1)}) custom-call(bf16[80,640]{1,0:T(8,128)(2,1)S(1)} %get-tuple-element.62.refs_0_, bf16[80,640]{1,0:T(8,128)(2,1)S(1)} %collective-permute-done.22.refs_1_, ...), custom_call_target="tpu_custom_call" | custom-call | bytes 1024 | tf_op jit(solution)/shard_map/pallas_call | solution.py:37
  105.4 1.6 collective-permute-start.34
  107.0 1.5 collective-permute-start.30
  108.5 1.6 collective-permute-start.31
  110.1 1.2 collective-permute-done.30.refs_1_
  111.3 2.1 %collective-permute-start.32 = (bf16[80,640]{1,0:T(8,128)(2,1)S(1)}, bf16[80,640]{1,0:T(8,128)(2,1)S(1)}, u32[]{:S(2)}, u32[]{:S(2)}) collective-permute-start(bf16[80,640]{1,0:T(8,128)(2,1)S(1)} %get-tuple-element.74), channel_id=1, source_target_pairs={{6,0},{0,2},{2,4},{4,6},{7,1},{1,3},{3,5},{5,7},{14,8},{8,10},{10,... | collective-permute-start | bytes 307208 | tf_op jit(solution)/shard_map/ppermute | solution.py:24
  113.4 1.0 collective-permute-done.31.refs_2_
  114.4 1.4 collective-permute-done.32.refs_3_
  115.8 1.6 collective-permute-start.26
  117.5 0.3 collective-permute-start.27
  117.8 0.2 shard_map.120
  118.0 2.5 %collective-permute-done.26.refs_2_ = bf16[80,640]{1,0:T(8,128)(2,1)S(1)} collective-permute-done((bf16[80,640]{1,0:T(8,128)(2,1)S(1)}, bf16[80,640]{1,0:T(8,128)(2,1)S(1)}, u32[]{:S(2)}, u32[]{:S(2)}) %collective-permute-start.26) | collective-permute-done | bytes 102432 | tf_op jit(solution)/shard_map/ppermute | solution.py:24
  120.5 2.9 %collective-permute-start.29 = (bf16[80,640]{1,0:T(8,128)(2,1)S(1)}, bf16[80,640]{1,0:T(8,128)(2,1)S(1)}, u32[]{:S(2)}, u32[]{:S(2)}) collective-permute-start(bf16[80,640]{1,0:T(8,128)(2,1)S(1)} %get-tuple-element.71), channel_id=1, source_target_pairs={{16,0},{24,8},{0,16},{8,24},{17,1},{25,9},{1,17},{9,25},{18,2},{26... | collective-permute-start | bytes 307208 | tf_op jit(solution)/shard_map/ppermute | solution.py:24
  123.4 0.8 collective-permute-start.33
  124.2 2.4 %shard_map.119 = bf16[128,5120]{1,0:T(8,128)(2,1)} custom-call(bf16[80,640]{1,0:T(8,128)(2,1)S(1)} %get-tuple-element.65.refs_0_, bf16[80,640]{1,0:T(8,128)(2,1)S(1)} %collective-permute-done.25.refs_1_, bf16[80,640]{1,0:T(8,128)(2,1)S(1)} %collective-permute-done.26.refs_2_, bf16[80,640]{1,0:T(8,128)(2,1)S(1)} %collective-permute-done.27.refs_3_, ...), custom_call_target="tpu_custom_call" | custom-call | bytes 1024 | tf_op jit(solution)/shard_map/pallas_call | solution.py:37
  126.6 6.9 %shard_map.122 = (bf16[5120,512]{1,0:T(8,128)(2,1)}, bf16[5120,512]{1,0:T(8,128)(2,1)}) custom-call(bf16[48,5120]{1,0:T(8,128)(2,1)S(1)} %get-tuple-element.54.refs_0_, bf16[48,5120]{1,0:T(8,128)(2,1)S(1)} %collective-permute-done.15.refs_8_.refs_1_, bf16[48,6144]{1,0:T(8,128)(2,1)S(1)} %get-tuple-element.60.act.refs_2_.refs_4_.refs_6_, ...), custom_call_target="tpu_custom_call" | custom-call | bytes 1024 | tf_op jit(solution)/shard_map/pallas_call | solution.py:410
  133.5 6.3 %shard_map.123 = bf16[512,5120]{1,0:T(8,128)(2,1)} custom-call(bf16[48,6144]{1,0:T(8,128)(2,1)S(1)} %get-tuple-element.75.refs_4_.refs_6_.refs_0_, bf16[48,6144]{1,0:T(8,128)(2,1)S(1)} %collective-permute-done.34.refs_5_.refs_7_.refs_1_, bf16[48,6144]{1,0:T(8,128)(2,1)S(1)} %get-tuple-element.76.refs_8_.refs_10_.refs_2_, ...), custom_call_target="tpu_custom_call" | custom-call | bytes 1024 | tf_op jit(solution)/shard_map/pallas_call | solution.py:410
  139.8 16.4 %collective-permute-done.29.upd0 = bf16[80,640]{1,0:T(8,128)(2,1)S(1)} collective-permute-done((bf16[80,640]{1,0:T(8,128)(2,1)S(1)}, bf16[80,640]{1,0:T(8,128)(2,1)S(1)}, u32[]{:S(2)}, u32[]{:S(2)}) %collective-permute-start.29) | collective-permute-done | bytes 102432 | tf_op jit(solution)/shard_map/ppermute | solution.py:24
  156.2 2.2 %shard_map.121 = bf16[128,5120]{1,0:T(8,128)(2,1)} custom-call(bf16[128,5120]{1,0:T(8,128)(2,1)S(1)} %collective-permute-done.28.bulk, bf16[80,640]{1,0:T(8,128)(2,1)S(1)} %collective-permute-done.29.upd0, s32[1,4,128]{2,1,0:T(4,128)S(1)} %collective-permute-done.2._.prev2_routes, bf16[80,640]{1,0:T(8,128)(2,1)S(1)} %collective-permute-done.33.upd1, ...), custom_call_target="tpu_custom_call" | custom-call | bytes 1024 | tf_op jit(solution)/shard_map/pallas_call | solution.py:37
  (37 shorter events, 0.7 us)
Async XLA Ops:
  1.3 6.4 %collective-permute-start = (s32[1,4,128]{2,1,0:T(4,128)S(1)}, s32[1,4,128]{2,1,0:T(4,128)S(1)}, u32[]{:S(2)}, u32[]{:S(2)}) collective-permute-start(s32[1,4,128]{2,1,0:T(4,128)S(1)} %get-tuple-element.80), channel_id=1, source_target_pairs={{8,0},{16,8},{24,16},{0,24},{9,1},{17,9},{25,17},{1,25},{10,2},{18... | collective-permute-start | bytes 6152 | tf_op jit(solution)/shard_map/ppermute | solution.py:24
  6.4 5.4 %collective-permute-start.1 = (s32[1,4,128]{2,1,0:T(4,128)S(1)}, s32[1,4,128]{2,1,0:T(4,128)S(1)}, u32[]{:S(2)}, u32[]{:S(2)}) collective-permute-start(s32[1,4,128]{2,1,0:T(4,128)S(1)} %get-tuple-element.80), channel_id=1, source_target_pairs={{24,0},{0,8},{8,16},{16,24},{25,1},{1,9},{9,17},{17,25},{26,2},{2,... | collective-permute-start | bytes 6152 | tf_op jit(solution)/shard_map/ppermute | solution.py:24
  6.4 5.4 %collective-permute-start.2 = (s32[1,4,128]{2,1,0:T(4,128)S(1)}, s32[1,4,128]{2,1,0:T(4,128)S(1)}, u32[]{:S(2)}, u32[]{:S(2)}) collective-permute-start(s32[1,4,128]{2,1,0:T(4,128)S(1)} %get-tuple-element.79), channel_id=1, source_target_pairs={{16,0},{24,8},{0,16},{8,24},{17,1},{25,9},{1,17},{9,25},{18,2},{26... | collective-permute-start | bytes 6152 | tf_op jit(solution)/shard_map/ppermute | solution.py:24
  11.8 1.3 copy-start
  13.1 1.3 copy-start.2
  14.4 0.7 copy-start.4
  16.9 23.1 %collective-permute-start.9 = (bf16[48,5120]{1,0:T(8,128)(2,1)S(1)}, bf16[48,5120]{1,0:T(8,128)(2,1)S(1)}, u32[]{:S(2)}, u32[]{:S(2)}) collective-permute-start(bf16[48,5120]{1,0:T(8,128)(2,1)S(1)} %get-tuple-element.49), channel_id=1, source_target_pairs={{16,0},{24,8},{0,16},{8,24},{17,1},{25,9},{1,17},{9,25},{18,2},{26... | collective-permute-start | bytes 1474568 | tf_op jit(solution)/shard_map/ppermute | solution.py:24
  17.1 5.9 %collective-permute-start.3 = (bf16[80,640]{1,0:T(8,128)(2,1)S(1)}, bf16[80,640]{1,0:T(8,128)(2,1)S(1)}, u32[]{:S(2)}, u32[]{:S(2)}) collective-permute-start(bf16[80,640]{1,0:T(8,128)(2,1)S(1)} %get-tuple-element.42.refs_0_), channel_id=1, source_target_pairs={{6,0},{0,2},{2,4},{4,6},{7,1},{1,3},{3,5},{5,7},{14,8},{8,10},{10,... | collective-permute-start | bytes 307208 | tf_op jit(solution)/shard_map/ppermute | solution.py:24
  17.1 5.9 %collective-permute-start.4 = (bf16[80,640]{1,0:T(8,128)(2,1)S(1)}, bf16[80,640]{1,0:T(8,128)(2,1)S(1)}, u32[]{:S(2)}, u32[]{:S(2)}) collective-permute-start(bf16[80,640]{1,0:T(8,128)(2,1)S(1)} %get-tuple-element.42.refs_0_), channel_id=1, source_target_pairs={{4,0},{6,2},{0,4},{2,6},{5,1},{7,3},{1,5},{3,7},{12,8},{14,10},{8,... | collective-permute-start | bytes 307208 | tf_op jit(solution)/shard_map/ppermute | solution.py:24
  18.7 4.8 %collective-permute-start.5 = (bf16[80,640]{1,0:T(8,128)(2,1)S(1)}, bf16[80,640]{1,0:T(8,128)(2,1)S(1)}, u32[]{:S(2)}, u32[]{:S(2)}) collective-permute-start(bf16[80,640]{1,0:T(8,128)(2,1)S(1)} %get-tuple-element.42.refs_0_), channel_id=1, source_target_pairs={{2,0},{4,2},{6,4},{0,6},{3,1},{5,3},{7,5},{1,7},{10,8},{12,10},{14... | collective-permute-start | bytes 307208 | tf_op jit(solution)/shard_map/ppermute | solution.py:24
  20.1 13.7 %collective-permute-start.10 = (bf16[80,640]{1,0:T(8,128)(2,1)S(1)}, bf16[80,640]{1,0:T(8,128)(2,1)S(1)}, u32[]{:S(2)}, u32[]{:S(2)}) collective-permute-start(bf16[80,640]{1,0:T(8,128)(2,1)S(1)} %get-tuple-element.50), channel_id=1, source_target_pairs={{8,0},{16,8},{24,16},{0,24},{9,1},{17,9},{25,17},{1,25},{10,2},{18... | collective-permute-start | bytes 307208 | tf_op jit(solution)/shard_map/ppermute | solution.py:24
  23.5 16.6 %copy-start.5 = (s32[2,128,4]{1,2,0:T(4,128)S(1)}, s32[2,128,4]{1,2,0:T(4,128)}, u32[]{:S(2)}) copy-start(s32[2,128,4]{1,2,0:T(4,128)} %param.12) | copy-start | bytes 12292
  23.5 16.6 %copy-start.6 = (f32[2,128,4]{1,2,0:T(4,128)S(1)}, f32[2,128,4]{1,2,0:T(4,128)}, u32[]{:S(2)}) copy-start(f32[2,128,4]{1,2,0:T(4,128)} %param.13) | copy-start | bytes 12292
  23.5 26.1 %copy-start.1 = (bf16[128,5120]{1,0:T(8,128)(2,1)S(1)}, bf16[128,5120]{1,0:T(8,128)(2,1)}, u32[]{:S(2)}) copy-start(bf16[128,5120]{1,0:T(8,128)(2,1)} %cotangent.3) | copy-start | bytes 3932164
  30.1 24.9 %collective-permute-start.15 = (bf16[48,5120]{1,0:T(8,128)(2,1)S(1)}, bf16[48,5120]{1,0:T(8,128)(2,1)S(1)}, u32[]{:S(2)}, u32[]{:S(2)}) collective-permute-start(bf16[48,5120]{1,0:T(8,128)(2,1)S(1)} %get-tuple-element.54.refs_0_), channel_id=1, source_target_pairs={{1,0},{0,1},{3,2},{2,3},{5,4},{4,5},{7,6},{6,7},{9,8},{8,9},{11,10... | collective-permute-start | bytes 1474568 | tf_op jit(solution)/shard_map/ppermute | solution.py:24
  31.6 4.8 %collective-permute-start.6 = (bf16[80,640]{1,0:T(8,128)(2,1)S(1)}, bf16[80,640]{1,0:T(8,128)(2,1)S(1)}, u32[]{:S(2)}, u32[]{:S(2)}) collective-permute-start(bf16[80,640]{1,0:T(8,128)(2,1)S(1)} %get-tuple-element.45), channel_id=1, source_target_pairs={{2,0},{4,2},{6,4},{0,6},{3,1},{5,3},{7,5},{1,7},{10,8},{12,10},{14... | collective-permute-start | bytes 307208 | tf_op jit(solution)/shard_map/ppermute | solution.py:24
  33.5 5.6 %collective-permute-start.7 = (bf16[80,640]{1,0:T(8,128)(2,1)S(1)}, bf16[80,640]{1,0:T(8,128)(2,1)S(1)}, u32[]{:S(2)}, u32[]{:S(2)}) collective-permute-start(bf16[80,640]{1,0:T(8,128)(2,1)S(1)} %get-tuple-element.46), channel_id=1, source_target_pairs={{4,0},{6,2},{0,4},{2,6},{5,1},{7,3},{1,5},{3,7},{12,8},{14,10},{8,... | collective-permute-start | bytes 307208 | tf_op jit(solution)/shard_map/ppermute | solution.py:24
  33.8 5.4 %collective-permute-start.8 = (bf16[80,640]{1,0:T(8,128)(2,1)S(1)}, bf16[80,640]{1,0:T(8,128)(2,1)S(1)}, u32[]{:S(2)}, u32[]{:S(2)}) collective-permute-start(bf16[80,640]{1,0:T(8,128)(2,1)S(1)} %get-tuple-element.47), channel_id=1, source_target_pairs={{6,0},{0,2},{2,4},{4,6},{7,1},{1,3},{3,5},{5,7},{14,8},{8,10},{10,... | collective-permute-start | bytes 307208 | tf_op jit(solution)/shard_map/ppermute | solution.py:24
  40.5 9.0 %collective-permute-start.11 = (bf16[80,640]{1,0:T(8,128)(2,1)S(1)}, bf16[80,640]{1,0:T(8,128)(2,1)S(1)}, u32[]{:S(2)}, u32[]{:S(2)}) collective-permute-start(bf16[80,640]{1,0:T(8,128)(2,1)S(1)} %get-tuple-element.51), channel_id=1, source_target_pairs={{24,0},{0,8},{8,16},{16,24},{25,1},{1,9},{9,17},{17,25},{26,2},{2,... | collective-permute-start | bytes 307208 | tf_op jit(solution)/shard_map/ppermute | solution.py:24
  50.1 39.2 %collective-permute-start.20 = (bf16[80,5120]{1,0:T(8,128)(2,1)S(1)}, bf16[80,5120]{1,0:T(8,128)(2,1)S(1)}, u32[]{:S(2)}, u32[]{:S(2)}) collective-permute-start(bf16[80,5120]{1,0:T(8,128)(2,1)S(1)} %get-tuple-element.59), channel_id=1, source_target_pairs={{16,0},{24,8},{0,16},{8,24},{17,1},{25,9},{1,17},{9,25},{18,2},{26... | collective-permute-start | bytes 2457608 | tf_op jit(solution)/shard_map/ppermute | solution.py:24
  52.0 6.8 %collective-permute-start.12 = (bf16[160,640]{1,0:T(8,128)(2,1)S(1)}, bf16[160,640]{1,0:T(8,128)(2,1)S(1)}, u32[]{:S(2)}, u32[]{:S(2)}) collective-permute-start(bf16[160,640]{1,0:T(8,128)(2,1)S(1)} %get-tuple-element.52.refs_0_), channel_id=1, source_target_pairs={{6,0},{0,2},{2,4},{4,6},{7,1},{1,3},{3,5},{5,7},{14,8},{8,10},{10,... | collective-permute-start | bytes 614408 | tf_op jit(solution)/shard_map/ppermute | solution.py:24
  52.0 7.9 %collective-permute-start.13 = (bf16[160,640]{1,0:T(8,128)(2,1)S(1)}, bf16[160,640]{1,0:T(8,128)(2,1)S(1)}, u32[]{:S(2)}, u32[]{:S(2)}) collective-permute-start(bf16[160,640]{1,0:T(8,128)(2,1)S(1)} %get-tuple-element.52.refs_0_), channel_id=1, source_target_pairs={{4,0},{6,2},{0,4},{2,6},{5,1},{7,3},{1,5},{3,7},{12,8},{14,10},{8,... | collective-permute-start | bytes 614408 | tf_op jit(solution)/shard_map/ppermute | solution.py:24
  53.5 9.3 %collective-permute-start.14 = (bf16[160,640]{1,0:T(8,128)(2,1)S(1)}, bf16[160,640]{1,0:T(8,128)(2,1)S(1)}, u32[]{:S(2)}, u32[]{:S(2)}) collective-permute-start(bf16[160,640]{1,0:T(8,128)(2,1)S(1)} %get-tuple-element.52.refs_0_), channel_id=1, source_target_pairs={{2,0},{4,2},{6,4},{0,6},{3,1},{5,3},{7,5},{1,7},{10,8},{12,10},{14... | collective-permute-start | bytes 614408 | tf_op jit(solution)/shard_map/ppermute | solution.py:24
  72.2 17.1 %copy-start.3 = (bf16[128,5120]{1,0:T(8,128)(2,1)S(1)}, bf16[128,5120]{1,0:T(8,128)(2,1)}, u32[]{:S(2)}) copy-start(bf16[128,5120]{1,0:T(8,128)(2,1)} %tokens.3) | copy-start | bytes 3932164
  72.2 17.1 %collective-permute-start.21 = (bf16[48,6144]{1,0:T(8,128)(2,1)S(1)}, bf16[48,6144]{1,0:T(8,128)(2,1)S(1)}, u32[]{:S(2)}, u32[]{:S(2)}) collective-permute-start(bf16[48,6144]{1,0:T(8,128)(2,1)S(1)} %get-tuple-element.60.act.refs_2_.refs_4_.refs_6_), channel_id=1, source_target_pairs={{1,0},{0,1},{3,2},{2,3},{5,4},{4,5},{7,6},{6,7},{9,8},{8,9},{11,10... | collective-permute-start | bytes 1769480 | tf_op jit(solution)/shard_map/ppermute | solution.py:24
  73.8 4.5 %collective-permute-start.16 = (bf16[80,640]{1,0:T(8,128)(2,1)S(1)}, bf16[80,640]{1,0:T(8,128)(2,1)S(1)}, u32[]{:S(2)}, u32[]{:S(2)}) collective-permute-start(bf16[80,640]{1,0:T(8,128)(2,1)S(1)} %get-tuple-element.56), channel_id=1, source_target_pairs={{2,0},{4,2},{6,4},{0,6},{3,1},{5,3},{7,5},{1,7},{10,8},{12,10},{14... | collective-permute-start | bytes 307208 | tf_op jit(solution)/shard_map/ppermute | solution.py:24
  75.4 5.9 %collective-permute-start.17 = (bf16[80,640]{1,0:T(8,128)(2,1)S(1)}, bf16[80,640]{1,0:T(8,128)(2,1)S(1)}, u32[]{:S(2)}, u32[]{:S(2)}) collective-permute-start(bf16[80,640]{1,0:T(8,128)(2,1)S(1)} %get-tuple-element.57), channel_id=1, source_target_pairs={{4,0},{6,2},{0,4},{2,6},{5,1},{7,3},{1,5},{3,7},{12,8},{14,10},{8,... | collective-permute-start | bytes 307208 | tf_op jit(solution)/shard_map/ppermute | solution.py:24
  75.9 5.4 %collective-permute-start.18 = (bf16[80,640]{1,0:T(8,128)(2,1)S(1)}, bf16[80,640]{1,0:T(8,128)(2,1)S(1)}, u32[]{:S(2)}, u32[]{:S(2)}) collective-permute-start(bf16[80,640]{1,0:T(8,128)(2,1)S(1)} %get-tuple-element.58), channel_id=1, source_target_pairs={{6,0},{0,2},{2,4},{4,6},{7,1},{1,3},{3,5},{5,7},{14,8},{8,10},{10,... | collective-permute-start | bytes 307208 | tf_op jit(solution)/shard_map/ppermute | solution.py:24
  81.7 7.6 %collective-permute-start.19 = (bf16[80,640]{1,0:T(8,128)(2,1)S(1)}, bf16[80,640]{1,0:T(8,128)(2,1)S(1)}, u32[]{:S(2)}, u32[]{:S(2)}) collective-permute-start(bf16[80,640]{1,0:T(8,128)(2,1)S(1)} %shard_map.115._), channel_id=1, source_target_pairs={{8,0},{16,8},{24,16},{0,24},{9,1},{17,9},{25,17},{1,25},{10,2},{18... | collective-permute-start | bytes 307208 | tf_op jit(solution)/shard_map/ppermute | solution.py:24
  90.5 65.7 %collective-permute-start.28 = (bf16[128,5120]{1,0:T(8,128)(2,1)S(1)}, bf16[128,5120]{1,0:T(8,128)(2,1)S(1)}, u32[]{:S(2)}, u32[]{:S(2)}) collective-permute-start(bf16[128,5120]{1,0:T(8,128)(2,1)S(1)} %get-tuple-element.70), channel_id=1, source_target_pairs={{16,0},{24,8},{0,16},{8,24},{17,1},{25,9},{1,17},{9,25},{18,2},{26... | collective-permute-start | bytes 3932168 | tf_op jit(solution)/shard_map/ppermute | solution.py:24
  90.6 4.6 %collective-permute-start.22 = (bf16[80,640]{1,0:T(8,128)(2,1)S(1)}, bf16[80,640]{1,0:T(8,128)(2,1)S(1)}, u32[]{:S(2)}, u32[]{:S(2)}) collective-permute-start(bf16[80,640]{1,0:T(8,128)(2,1)S(1)} %get-tuple-element.62.refs_0_), channel_id=1, source_target_pairs={{6,0},{0,2},{2,4},{4,6},{7,1},{1,3},{3,5},{5,7},{14,8},{8,10},{10,... | collective-permute-start | bytes 307208 | tf_op jit(solution)/shard_map/ppermute | solution.py:24
  90.6 5.8 %collective-permute-start.23 = (bf16[80,640]{1,0:T(8,128)(2,1)S(1)}, bf16[80,640]{1,0:T(8,128)(2,1)S(1)}, u32[]{:S(2)}, u32[]{:S(2)}) collective-permute-start(bf16[80,640]{1,0:T(8,128)(2,1)S(1)} %get-tuple-element.62.refs_0_), channel_id=1, source_target_pairs={{4,0},{6,2},{0,4},{2,6},{5,1},{7,3},{1,5},{3,7},{12,8},{14,10},{8,... | collective-permute-start | bytes 307208 | tf_op jit(solution)/shard_map/ppermute | solution.py:24
  91.4 5.0 %collective-permute-start.24 = (bf16[80,640]{1,0:T(8,128)(2,1)S(1)}, bf16[80,640]{1,0:T(8,128)(2,1)S(1)}, u32[]{:S(2)}, u32[]{:S(2)}) collective-permute-start(bf16[80,640]{1,0:T(8,128)(2,1)S(1)} %get-tuple-element.62.refs_0_), channel_id=1, source_target_pairs={{2,0},{4,2},{6,4},{0,6},{3,1},{5,3},{7,5},{1,7},{10,8},{12,10},{14... | collective-permute-start | bytes 307208 | tf_op jit(solution)/shard_map/ppermute | solution.py:24
  92.8 33.7 %collective-permute-start.35 = (bf16[48,6144]{1,0:T(8,128)(2,1)S(1)}, bf16[48,6144]{1,0:T(8,128)(2,1)S(1)}, u32[]{:S(2)}, u32[]{:S(2)}) collective-permute-start(bf16[48,6144]{1,0:T(8,128)(2,1)S(1)} %get-tuple-element.76.refs_8_.refs_10_.refs_2_), channel_id=1, source_target_pairs={{1,0},{0,1},{3,2},{2,3},{5,4},{4,5},{7,6},{6,7},{9,8},{8,9},{11,10... | collective-permute-start | bytes 1769480 | tf_op jit(solution)/shard_map/ppermute | solution.py:24
  105.4 21.1 %collective-permute-start.34 = (bf16[48,6144]{1,0:T(8,128)(2,1)S(1)}, bf16[48,6144]{1,0:T(8,128)(2,1)S(1)}, u32[]{:S(2)}, u32[]{:S(2)}) collective-permute-start(bf16[48,6144]{1,0:T(8,128)(2,1)S(1)} %get-tuple-element.75.refs_4_.refs_6_.refs_0_), channel_id=1, source_target_pairs={{1,0},{0,1},{3,2},{2,3},{5,4},{4,5},{7,6},{6,7},{9,8},{8,9},{11,10... | collective-permute-start | bytes 1769480 | tf_op jit(solution)/shard_map/ppermute | solution.py:24
  107.0 4.3 %collective-permute-start.30 = (bf16[80,640]{1,0:T(8,128)(2,1)S(1)}, bf16[80,640]{1,0:T(8,128)(2,1)S(1)}, u32[]{:S(2)}, u32[]{:S(2)}) collective-permute-start(bf16[80,640]{1,0:T(8,128)(2,1)S(1)} %get-tuple-element.72), channel_id=1, source_target_pairs={{2,0},{4,2},{6,4},{0,6},{3,1},{5,3},{7,5},{1,7},{10,8},{12,10},{14... | collective-permute-start | bytes 307208 | tf_op jit(solution)/shard_map/ppermute | solution.py:24
  108.5 5.9 %collective-permute-start.31 = (bf16[80,640]{1,0:T(8,128)(2,1)S(1)}, bf16[80,640]{1,0:T(8,128)(2,1)S(1)}, u32[]{:S(2)}, u32[]{:S(2)}) collective-permute-start(bf16[80,640]{1,0:T(8,128)(2,1)S(1)} %get-tuple-element.73), channel_id=1, source_target_pairs={{4,0},{6,2},{0,4},{2,6},{5,1},{7,3},{1,5},{3,7},{12,8},{14,10},{8,... | collective-permute-start | bytes 307208 | tf_op jit(solution)/shard_map/ppermute | solution.py:24
  111.3 4.5 %collective-permute-start.32 = (bf16[80,640]{1,0:T(8,128)(2,1)S(1)}, bf16[80,640]{1,0:T(8,128)(2,1)S(1)}, u32[]{:S(2)}, u32[]{:S(2)}) collective-permute-start(bf16[80,640]{1,0:T(8,128)(2,1)S(1)} %get-tuple-element.74), channel_id=1, source_target_pairs={{6,0},{0,2},{2,4},{4,6},{7,1},{1,3},{3,5},{5,7},{14,8},{8,10},{10,... | collective-permute-start | bytes 307208 | tf_op jit(solution)/shard_map/ppermute | solution.py:24
  114.4 3.1 %collective-permute-start.25 = (bf16[80,640]{1,0:T(8,128)(2,1)S(1)}, bf16[80,640]{1,0:T(8,128)(2,1)S(1)}, u32[]{:S(2)}, u32[]{:S(2)}) collective-permute-start(bf16[80,640]{1,0:T(8,128)(2,1)S(1)} %get-tuple-element.66), channel_id=1, source_target_pairs={{2,0},{4,2},{6,4},{0,6},{3,1},{5,3},{7,5},{1,7},{10,8},{12,10},{14... | collective-permute-start | bytes 307208 | tf_op jit(solution)/shard_map/ppermute | solution.py:24
  115.8 4.7 %collective-permute-start.26 = (bf16[80,640]{1,0:T(8,128)(2,1)S(1)}, bf16[80,640]{1,0:T(8,128)(2,1)S(1)}, u32[]{:S(2)}, u32[]{:S(2)}) collective-permute-start(bf16[80,640]{1,0:T(8,128)(2,1)S(1)} %get-tuple-element.67), channel_id=1, source_target_pairs={{4,0},{6,2},{0,4},{2,6},{5,1},{7,3},{1,5},{3,7},{12,8},{14,10},{8,... | collective-permute-start | bytes 307208 | tf_op jit(solution)/shard_map/ppermute | solution.py:24
  117.5 5.9 %collective-permute-start.27 = (bf16[80,640]{1,0:T(8,128)(2,1)S(1)}, bf16[80,640]{1,0:T(8,128)(2,1)S(1)}, u32[]{:S(2)}, u32[]{:S(2)}) collective-permute-start(bf16[80,640]{1,0:T(8,128)(2,1)S(1)} %get-tuple-element.68), channel_id=1, source_target_pairs={{6,0},{0,2},{2,4},{4,6},{7,1},{1,3},{3,5},{5,7},{14,8},{8,10},{10,... | collective-permute-start | bytes 307208 | tf_op jit(solution)/shard_map/ppermute | solution.py:24
  120.5 35.6 %collective-permute-start.29 = (bf16[80,640]{1,0:T(8,128)(2,1)S(1)}, bf16[80,640]{1,0:T(8,128)(2,1)S(1)}, u32[]{:S(2)}, u32[]{:S(2)}) collective-permute-start(bf16[80,640]{1,0:T(8,128)(2,1)S(1)} %get-tuple-element.71), channel_id=1, source_target_pairs={{16,0},{24,8},{0,16},{8,24},{17,1},{25,9},{1,17},{9,25},{18,2},{26... | collective-permute-start | bytes 307208 | tf_op jit(solution)/shard_map/ppermute | solution.py:24
  123.4 32.7 %collective-permute-start.33 = (bf16[80,640]{1,0:T(8,128)(2,1)S(1)}, bf16[80,640]{1,0:T(8,128)(2,1)S(1)}, u32[]{:S(2)}, u32[]{:S(2)}) collective-permute-start(bf16[80,640]{1,0:T(8,128)(2,1)S(1)} %shard_map.120), channel_id=1, source_target_pairs={{24,0},{0,8},{8,16},{16,24},{25,1},{1,9},{9,17},{17,25},{26,2},{2,... | collective-permute-start | bytes 307208 | tf_op jit(solution)/shard_map/ppermute | solution.py:24

commit v4 on v3

--- a/solution.py
+++ b/solution.py
@@ -10,7 +10,8 @@
 CAP = 10
 PACK = 8
 PACKED = CAP * PACK
-FIRST = 48
+COT_PIECES = ((0, 32, 0, 8), (32, 64, 0, 8), (64, 128, 0, 3), (64, 128, 3, 8))
+TOK_PIECES = ((0, 96, 0, 8), (96, 128, 0, 8))
 EPSILON = 1e-06
 F32 = jnp.float32
 BF16 = jnp.bfloat16
@@ -78,16 +79,19 @@
     return slice(c * (width // PACK), (c + 1) * (width // PACK))
 
 
-def pick(select, rows):
+def pick(select, pieces):
     total = None
-    at = 0
-    for block in rows:
-        end = at + block.shape[0]
-        for c in range(PACK):
-            part = dot(chunk_of(select[:, at:end], c), block[:, columns(c, block.shape[1])])
+    for block, (r0, r1, c0, c1) in pieces:
+        width = block.shape[1] // (c1 - c0)
+        for c in range(c0, c1):
+            columns_here = slice((c - c0) * width, (c - c0 + 1) * width)
+            part = dot(chunk_of(select[:, r0:r1], c), block[:, columns_here])
             total = part if total is None else total + part
-        at = end
     return total
+
+
+def whole_block(block):
+    return [(block, (0, block.shape[0], 0, PACK))]
 
 
 def over_chunks(row_sums):
@@ -124,49 +128,58 @@
     return total
 
 
-def place_rows(bulk, first, rows1, second, rows2, out):
+def place_rows(pieces, first, rows1, second, rows2, out):
     ones = jnp.ones((PACKED, 128), BF16)
     hit1 = dot(chunk_of(first, 0), ones, 0, 0)[:, :1] > 0.5
     hit2 = dot(chunk_of(second, 0), ones, 0, 0)[:, :1] > 0.5
-    width = out.shape[1]
+    width = out.shape[1] // PACK
     for c in range(PACK):
-        k = columns(c, width)
         new1 = dot(chunk_of(first, c), rows1, 0, 0)
         new2 = dot(chunk_of(second, c), rows2, 0, 0)
-        at = 0
-        for block in bulk:
-            r = slice(at, at + block.shape[0])
-            at = r.stop
-            value = jnp.where(hit1[r], new1[r], block[:, k].astype(F32))
-            out[r, k] = jnp.where(hit2[r], new2[r], value).astype(BF16)
-
-
-def copy_rows(source, start, stop, piece, sem):
-    copy = pltpu.make_async_copy(source.at[pl.ds(start, stop - start)], piece, sem)
+        for block, (r0, r1, c0, c1) in pieces:
+            if c0 <= c < c1:
+                old = block[:, (c - c0) * width : (c - c0 + 1) * width].astype(F32)
+                value = jnp.where(hit1[r0:r1], new1[r0:r1], old)
+                value = jnp.where(hit2[r0:r1], new2[r0:r1], value)
+                out[r0:r1, columns(c, out.shape[1])] = value.astype(BF16)
+
+
+def piece_copy(source, place, piece, sem):
+    r0, r1, c0, c1 = place
+    width = source.shape[1] // PACK
+    block = source.at[pl.ds(r0, r1 - r0), pl.ds(c0 * width, (c1 - c0) * width)]
+    copy = pltpu.make_async_copy(block, piece, sem)
     copy.start()
     return copy
 
 
-def first_rows_kernel(
-    tokens, cotangent, routes, next_routes, prev_routes, _, far, raw, normed, t1, cot, piece, sem
-):
-    copy = copy_rows(far, 0, FIRST, piece, sem)
-    values = pick(select_of(routes[0]), [tokens])
+def first_rows_kernel(tokens, routes, far, raw, normed, piece, sem):
+    copy = piece_copy(far, COT_PIECES[0], piece, sem)
+    values = pick(select_of(routes[0]), whole_block(tokens))
     raw[...] = values.astype(BF16)
     normed[...] = (values * inv_rms_of(values)).astype(BF16)
-    cot[...] = pick(select_of(prev_routes[0]), [cotangent]).astype(BF16)
-    t1[...] = pick(select_of(next_routes[0]), [tokens]).astype(BF16)
     copy.wait()
 
 
+def other_rows_kernel(
+    tokens, cotangent, next_routes, prev_routes, _, __, ___, far, t1, cot, piece, sem
+):
+    copy = piece_copy(far, COT_PIECES[1], piece, sem)
+    cot[...] = pick(select_of(prev_routes[0]), whole_block(cotangent)).astype(BF16)
+    t1[...] = pick(select_of(next_routes[0]), whole_block(tokens)).astype(BF16)
+    copy.wait()
+
+
 def update0_kernel(n, *refs):
-    parts, (raw, routes, gates, next_routes, t1) = refs[:n], refs[n : n + 5]
-    upd, onward = refs[n + 7 :]
+    parts, (raw, routes, gates, next_routes, t1, cotangent) = refs[:n], refs[n : n + 6]
+    upd, onward, piece, sem = refs[n + 6 :]
+    copy = piece_copy(cotangent, COT_PIECES[2], piece, sem)
     select = select_of(routes[0])
     weight = slot_gates(select, routes[0], gates[0])
     fresh = (raw[...].astype(F32) + weight * summed(parts)).astype(BF16)
     onward[...] = merged(select_of(next_routes[0]), select, fresh, t1[...].astype(F32))
     upd[...] = fresh
+    copy.wait()
 
 
 def update1_kernel(n, *refs):
@@ -176,8 +189,8 @@
     upd[...] = (h[...].astype(F32) + weight * summed(parts)).astype(BF16)
 
 
-def enter1_kernel(h, cot, routes, gates, cotangent, out, piece, sem):
-    copy = copy_rows(cotangent, FIRST, cotangent.shape[0], piece, sem)
+def enter1_kernel(h, cot, routes, gates, cotangent, _, out, piece, sem):
+    copy = piece_copy(cotangent, COT_PIECES[3], piece, sem)
     values = h[...].astype(F32)
     out[:PACKED] = (values * inv_rms_of(values)).astype(BF16)
     weight = slot_gates(select_of(routes[1]), routes[1], gates[1])
@@ -194,16 +207,17 @@
 
 
 def grad1_kernel(n, *refs):
-    parts, (h, cot, upd) = refs[:n], refs[n:]
+    parts, (h, cot, tokens, upd, piece, sem) = refs[:n], refs[n:]
+    copy = piece_copy(tokens, TOK_PIECES[0], piece, sem)
     upd[...] = state_grad(parts, h[...], cot[...])
-
-
-def enter0_kernel(
-    upd1, next_routes, routes, gates, bulk_a, bulk_b, tokens, _, __, c0, out, piece, sem
-):
-    copy = copy_rows(tokens, 0, tokens.shape[0], piece, sem)
+    copy.wait()
+
+
+def enter0_kernel(m, upd1, next_routes, routes, gates, *refs):
+    bulk, (tokens, _, c0, out, piece, sem) = refs[:m], refs[m:]
+    copy = piece_copy(tokens, TOK_PIECES[1], piece, sem)
     select = select_of(routes[0])
-    old = pick(select, [bulk_a, bulk_b])
+    old = pick(select, list(zip(bulk, COT_PIECES)))
     rows = merged(select, select_of(next_routes[0]), upd1[...], old)
     c0[...] = rows
     out[...] = (slot_gates(select, routes[0], gates[0]) * rows.astype(F32)).astype(BF16)
@@ -211,16 +225,21 @@
 
 
 def finish_grad_kernel(n, *refs):
-    parts, (h, c, routes, upd1, next_routes, bulk_a, bulk_b, out) = refs[:n], refs[n:]
+    parts, (h, c, routes, upd1, next_routes, *bulk, out) = refs[:n], refs[n:]
     fresh = state_grad(parts, h[...], c[...])
     place_rows(
-        [bulk_a, bulk_b], select_of(next_routes[0]), upd1[...], select_of(routes[0]), fresh, out
-    )
-
-
-def finish_state_kernel(bulk, upd0, prev2_routes, upd1, prev_routes, out):
+        list(zip(bulk, COT_PIECES)),
+        select_of(next_routes[0]),
+        upd1[...],
+        select_of(routes[0]),
+        fresh,
+        out,
+    )
+
+
+def finish_state_kernel(first, rest, upd0, prev2_routes, upd1, prev_routes, out):
     place_rows(
-        [bulk],
+        list(zip([first, rest], TOK_PIECES)),
         select_of(prev2_routes[0]),
         upd0[...],
         select_of(prev_routes[0]),
@@ -272,10 +291,10 @@
 
 
 def forward_kernel(n, *refs):
-    blocks, (gate, up, down, _) = refs[:n], refs[n : n + 4]
-    x, pre_gate, pre_up, act = refs[n + 4 : n + 8]
-    parts = refs[n + 8 : 2 * n + 8]
-    gate_v, up_v, down_v, sems, unpacked, whole32, held = refs[2 * n + 8 :]
+    blocks, (gate, up, down) = refs[:n], refs[n : n + 3]
+    x, pre_gate, pre_up, act = refs[n + 3 : n + 7]
+    parts = refs[n + 7 : 2 * n + 7]
+    gate_v, up_v, down_v, sems, unpacked, whole32, held = refs[2 * n + 7 :]
     copies = weight_copies(gate, up, down, gate_v, up_v, down_v, sems)
     for cg, cu, _ in copies:
         cg.start()
@@ -307,7 +326,7 @@
     parts, (unpacked, held) = refs[:n], refs[n:]
     hidden, width = down.shape
     for c in range(PACK):
-        value = dot(act[:, width + hidden :], down[:, columns(c, width)])
+        value = dot(act[:, 2 * width + hidden :], down[:, columns(c, width)])
         spread_rows(value, c, n, held.at[c], unpacked)
     for i, p in enumerate(parts):
         p[...] = unpacked[i].astype(BF16)
@@ -324,10 +343,10 @@
 
 
 def tick1_kernel(n, *refs):
-    blocks, (act0, gate, up, down, _) = refs[:n], refs[n : n + 5]
-    x_act, g_grad = refs[n + 5 : n + 7]
-    parts = refs[n + 7 : 2 * n + 7]
-    gate_v, up_v, down_v, sems, unpacked, whole32, held, x, g = refs[2 * n + 7 :]
+    blocks, (x0, act0, gate, up, down, _) = refs[:n], refs[n : n + 6]
+    x_act, g_grad = refs[n + 6 : n + 8]
+    parts = refs[n + 8 : 2 * n + 8]
+    gate_v, up_v, down_v, sems, unpacked, whole32, held, x, g = refs[2 * n + 8 :]
     copies = weight_copies(gate, up, down, gate_v, up_v, down_v, sems)
     for three in copies:
         for c in three:
@@ -335,8 +354,9 @@
     gather_rows(blocks, 0, unpacked, whole32.at[0], x)
     gather_rows(blocks, PACKED, unpacked, whole32.at[1], g)
     width, hidden = gate.shape
-    x_act[:, :width] = x[...]
-    x_act[:, width : width + hidden] = act0[...]
+    x_act[:, :width] = x0[...]
+    x_act[:, width : 2 * width] = x[...]
+    x_act[:, 2 * width : 2 * width + hidden] = act0[...]
     g_grad[:, :width] = g[...]
     acc_g = jnp.zeros(act0.shape, F32)
     acc_u = jnp.zeros(act0.shape, F32)
@@ -350,7 +370,7 @@
         cd.wait()
         acc_a = acc_a + dot(g[:, k], down_v[:, k], 1, 1)
     gg, gu = silu_grads(acc_g, acc_u, acc_a)
-    x_act[:, width + hidden :] = (acc_g * jax.nn.sigmoid(acc_g) * acc_u).astype(BF16)
+    x_act[:, 2 * width + hidden :] = (acc_g * jax.nn.sigmoid(acc_g) * acc_u).astype(BF16)
     g_grad[:, width : width + hidden] = gg
     g_grad[:, width + hidden :] = gu
     back_rows(gg, gu, gate_v, up_v, held, unpacked, parts)
@@ -404,29 +424,31 @@
 
 
 def grads_call(kernel, wide, fixed, outs, out_block, out_index, hidden):
-    rows = wide[0].shape[0]
-    width = max(max(s) for s in outs)
-    step = width // PACK
+    rows = wide[0][0].shape[0]
+    step = max(max(s) for s in outs) // PACK
+
+    def chunked(at):
+        return pl.BlockSpec((rows, step), lambda c: (0, at + c))
+
+    def constant(at):
+        return pl.BlockSpec((rows, hidden), lambda c: (0, at))
+
     return pl.pallas_call(
         kernel,
         grid=(PACK,),
         out_shape=[jax.ShapeDtypeStruct(s, BF16) for s in outs],
-        in_specs=[pl.BlockSpec((rows, step), lambda c: (0, c)) for _ in wide]
-        + [
-            pl.BlockSpec((rows, hidden), functools.partial(lambda i, c: (0, i), at))
-            for _, at in fixed
-        ],
+        in_specs=[chunked(at) for _, at in wide] + [constant(at) for _, at in fixed],
         out_specs=[pl.BlockSpec(out_block, out_index)] * len(outs),
         compiler_params=pltpu.CompilerParams(vmem_limit_bytes=VMEM_SMALL),
         cost_estimate=pl.CostEstimate(flops=0, bytes_accessed=COST_BYTES, transcendentals=0),
-    )(*wide, *(a for a, _ in fixed))
-
-
-def input_grads(x0, x_act1, g_grad0, g_grad1, width, hidden):
+    )(*(a for a, _ in wide), *(a for a, _ in fixed))
+
+
+def input_grads(x_act, g_grad0, g_grad1, width, hidden):
     first = width // hidden
     return grads_call(
-        functools.partial(input_grad_kernel, len(x0)),
-        x0 + x_act1,
+        functools.partial(input_grad_kernel, len(x_act)),
+        [(a, 0) for a in x_act] + [(a, PACK) for a in x_act],
         [(a, first) for a in g_grad0]
         + [(a, first + 1) for a in g_grad0]
         + [(a, first) for a in g_grad1]
@@ -438,12 +460,12 @@
     )
 
 
-def down_grads(g_grad0, g_grad1, x_act1, width, hidden):
-    first = width // hidden
+def down_grads(g_grad0, g_grad1, x_act, width, hidden):
+    first = 2 * width // hidden
     return grads_call(
         functools.partial(down_grad_kernel, len(g_grad0)),
-        g_grad0 + g_grad1,
-        [(a, first) for a in x_act1] + [(a, first + 1) for a in x_act1],
+        [(a, 0) for a in g_grad0 + g_grad1],
+        [(a, first) for a in x_act] + [(a, first + 1) for a in x_act],
         [(hidden, width)],
         (hidden, width // PACK),
         lambda c: (0, c),
@@ -469,7 +491,6 @@
     gate, up, down = w_gate[0], w_up[0], w_down[0]
     width, hidden = gate.shape
     step = width // PACK
-    own = tokens.shape[0]
     n = lax.axis_size("expert")
     rows = -(-n * CAP // 16) * 16
     routes = jnp.transpose(routes, (0, 2, 1))
@@ -493,78 +514,107 @@
     prev_routes = shifted(routes[1:], "section", 1)
     prev2_routes = shifted(routes[:1], "section", 2)
 
-    raw0, normed0, t1, cot1, piece = call(
+    def shape_of(place):
+        r0, r1, c0, c1 = place
+        return ((r1 - r0, (c1 - c0) * step), BF16)
+
+    cot_shapes = [shape_of(place) for place in COT_PIECES]
+    tok_shapes = [shape_of(place) for place in TOK_PIECES]
+    dma = [pltpu.SemaphoreType.DMA]
+
+    raw0, normed0, piece = call(
         first_rows_kernel,
-        [one, one, one, one, ((FIRST, width), BF16)],
-        [tokens, cotangent, routes, next_routes, prev_routes, prev2_routes, cotangent],
-        any_args=(5, 6),
-        any_outs=(4,),
-        scratch=[pltpu.SemaphoreType.DMA],
-    )
-    cot_a = shifted(piece, "section", -2)
-    cot1 = shifted(cot1, "section", -1)
+        [one, one, cot_shapes[0]],
+        [tokens, routes, cotangent],
+        any_args=(2,),
+        any_outs=(2,),
+        scratch=dma,
+    )
+    cot_parts = [shifted(piece, "section", -2)]
     blocks = from_group(normed0)
     x0, pre_gate0, pre_up0, act0, *parts = call(
         part(forward_kernel, n),
         [((rows, width), BF16), ((rows, hidden), F32), ((rows, hidden), F32)]
         + [((rows, hidden), BF16)]
         + [one] * n,
-        [*blocks, gate, up, down, t1],
-        any_args=(n, n + 1, n + 2, n + 3),
+        [*blocks, gate, up, down],
+        any_args=(n, n + 1, n + 2),
         scratch=scratch,
         vmem=VMEM_BIG,
     )
+    t1, cot1, piece = call(
+        other_rows_kernel,
+        [one, one, cot_shapes[1]],
+        [tokens, cotangent, next_routes, prev_routes, prev2_routes, act0, cot_parts[0], cotangent],
+        any_args=(4, 5, 6, 7),
+        any_outs=(2,),
+        scratch=dma,
+    )
+    cot1 = shifted(cot1, "section", -1)
+    cot_parts.append(shifted(piece, "section", -2))
     parts = to_group(parts)
-    upd0, h1 = call(
+    upd0, h1, piece = call(
         part(update0_kernel, n),
-        [one, one],
-        [*parts, raw0, routes, gates, next_routes, t1, cot_a, cot1],
-        any_args=(n + 5, n + 6),
+        [one, one, cot_shapes[2]],
+        [*parts, raw0, routes, gates, next_routes, t1, cotangent],
+        any_args=(n + 5,),
+        any_outs=(2,),
+        scratch=dma,
     )
     h1 = shifted(h1, "section", 1)
+    cot_parts.append(shifted(piece, "section", -2))
     upd0 = shifted(upd0, "section", 2)
 
     enter1, piece = call(
         enter1_kernel,
-        [((2 * PACKED, step), BF16), ((own - FIRST, width), BF16)],
-        [h1, cot1, routes, gates, cotangent],
-        any_args=(4,),
+        [((2 * PACKED, step), BF16), cot_shapes[3]],
+        [h1, cot1, routes, gates, cotangent, cot_parts[1]],
+        any_args=(4, 5),
         any_outs=(1,),
-        scratch=[pltpu.SemaphoreType.DMA],
-    )
-    cot_b = shifted(piece, "section", -2)
+        scratch=dma,
+    )
+    cot_parts.append(shifted(piece, "section", -2))
     blocks = from_group(enter1)
-    x0_all = copies_of(x0)
-    x_act1, g_grad1, *parts = call(
+    x_act, g_grad1, *parts = call(
         part(tick1_kernel, n),
-        [wide, wide] + [one] * n,
-        [*blocks, act0, gate, up, down, x0_all[-1]],
-        any_args=(n + 1, n + 2, n + 3, n + 4),
+        [((rows, 2 * (width + hidden)), BF16), wide] + [one] * n,
+        [*blocks, x0, act0, gate, up, down, cot_parts[2]],
+        any_args=(n + 2, n + 3, n + 4, n + 5),
         scratch=tick1_scratch,
         vmem=VMEM_BIG,
     )
     parts = to_group(parts)
-    (upd1,) = call(part(grad1_kernel, n), [one], [*parts, h1, cot1])
+    upd1, piece = call(
+        part(grad1_kernel, n),
+        [one, tok_shapes[0]],
+        [*parts, h1, cot1, tokens],
+        any_args=(n + 2,),
+        any_outs=(1,),
+        scratch=dma,
+    )
+    upd1_here = upd1
+    upd1 = shifted(upd1, "section", -1)
+    tok_parts = [shifted(piece, "section", 2)]
     outs = call(
         part(down_kernel, n),
         [one] * n,
-        [x_act1, down, upd1],
+        [x_act, down, upd1_here],
         any_args=(2,),
         scratch=[scratch[4], scratch[6]],
         vmem=VMEM_BIG,
     )
-    upd1 = shifted(upd1, "section", -1)
-    x_act1_all, g_grad1_all = copies_of(x_act1), copies_of(g_grad1)
-
+    x_act_all, g_grad1_all = copies_of(x_act), copies_of(g_grad1)
+
+    m = len(cot_parts)
     c0, enter0, piece = call(
-        enter0_kernel,
-        [one, one, (tokens.shape, BF16)],
-        [upd1, next_routes, routes, gates, cot_a, cot_b, tokens, outs[0], x_act1_all[-1]],
-        any_args=(6, 7, 8),
+        part(enter0_kernel, m),
+        [one, one, tok_shapes[1]],
+        [upd1, next_routes, routes, gates, *cot_parts, tokens, outs[0]],
+        any_args=(m + 4, m + 5),
         any_outs=(2,),
-        scratch=[pltpu.SemaphoreType.DMA],
-    )
-    tok = shifted(piece, "section", 2)
+        scratch=dma,
+    )
+    tok_parts.append(shifted(piece, "section", 2))
     blocks = from_group(enter0)
     g_grad0, *parts = call(
         part(tick0_kernel, n),
@@ -579,17 +629,17 @@
     (grad,) = call(
         part(finish_grad_kernel, n),
         [(tokens.shape, BF16)],
-        [*parts, raw0, c0, routes, upd1, next_routes, cot_a, cot_b],
+        [*parts, raw0, c0, routes, upd1, next_routes, *cot_parts],
     )
     outs = to_group(outs)
     (last1,) = call(part(update1_kernel, n), [one], [*outs, h1, routes, gates])
     last1 = shifted(last1, "section", 1)
-    gate_out, up_out = input_grads(x0_all, x_act1_all, g_grad0_all, g_grad1_all, width, hidden)
-    (down_out,) = down_grads(g_grad0_all, g_grad1_all, x_act1_all, width, hidden)
+    gate_out, up_out = input_grads(x_act_all, g_grad0_all, g_grad1_all, width, hidden)
+    (down_out,) = down_grads(g_grad0_all, g_grad1_all, x_act_all, width, hidden)
     (state,) = call(
         finish_state_kernel,
         [(tokens.shape, BF16)],
-        [tok, upd0, prev2_routes, last1, prev_routes],
+        [*tok_parts, upd0, prev2_routes, last1, prev_routes],
     )
     return (grad, state, gate_out[None], up_out[None], down_out[None])
 

time: 159 us -> 175 us (1.10)
  starting transfers between devices: 50.3 us -> 77.8 us
  waiting for transfers between devices: 52.4 us -> 41.2 us
    ppermute x36 -> x38, starting transfers between devices: 50.3 us -> 77.8 us  [shifted(): lax.ppermute(block, axis, [((i - distance) % size, i) for i in range(size)])]
    ppermute x36 -> x38, waiting for transfers between devices: 52.4 us -> 41.2 us  [shifted(): lax.ppermute(block, axis, [((i - distance) % size, i) for i in range(size)])]
    pallas_call x12 -> x13, Pallas kernels: 37.7 us -> 38.4 us  [call(): pl.pallas_call(kernel, out_shape=outs, in_specs=[anywhere if i in any_arg...]
  transfers between devices with their start and end apart: 36 -> 38, of which waited for: 21 -> 17; matrix products, arithmetic and copies ran while one was open for 0% -> 0% of each run, Pallas kernels for 29% -> 27%
where the time goes in v4:
time: 175 us
  starting transfers between devices  77.8 us (44%)
  Pallas kernels  51.9 us (30%)
  waiting for transfers between devices  41.2 us (24%)
  local copies, waits for them, and re-layouts  3.33 us (2%)
    ppermute x38, starting transfers between devices, shifted(): lax.ppermute(block, axis, [((i - distance) % size, i) for i in range(size)])  77.8 us
    ppermute x38, waiting for transfers between devices, shifted(): lax.ppermute(block, axis, [((i - distance) % size, i) for i in range(size)])  41.2 us
    pallas_call x13, Pallas kernels, call(): pl.pallas_call(kernel, out_shape=outs, in_specs=[anywhere if i in any_arg...  38.4 us
    pallas_call x2, Pallas kernels, grads_call(): pl.pallas_call(kernel, grid=(PACK,), out_shape=[jax.ShapeDtypeStruct(s, B...  13.5 us
  transfers between devices with their start and end apart: 38, of which 17 were waited for; matrix products, arithmetic and copies ran while one was open for 0% of the time, Pallas kernels for 27%

profile of v4, /device:TPU:0, one launch (start us, length us, event | category | flops | bytes accessed | tf_op | source)
XLA Modules:
  0.0 175.1 jit_solution(16564902900112753883)
XLA Ops:
  0.6 1.3 copy-done
  2.0 1.3 copy-done.2
  3.3 0.7 copy-done.4
  4.0 1.0 shard_map.110
  5.0 4.1 %collective-permute-start.9 = (bf16[32,5120]{1,0:T(8,128)(2,1)S(1)}, bf16[32,5120]{1,0:T(8,128)(2,1)S(1)}, u32[]{:S(2)}, u32[]{:S(2)}) collective-permute-start(bf16[32,5120]{1,0:T(8,128)(2,1)S(1)} %get-tuple-element.53), channel_id=1, source_target_pairs={{16,0},{24,8},{0,16},{8,24},{17,1},{25,9},{1,17},{9,25},{18,2},{26... | collective-permute-start | bytes 983048 | tf_op jit(solution)/shard_map/ppermute | solution.py:25
  9.1 1.5 collective-permute-start.1
  10.6 1.4 collective-permute-start.2
  12.1 1.3 collective-permute-start.6
  13.4 0.3 collective-permute-done.refs_1_
  13.7 1.6 collective-permute-start.7
  15.3 0.3 collective-permute-start.8
  15.7 6.6 %shard_map.111 = (bf16[48,5120]{1,0:T(8,128)(2,1)S(1)}, f32[48,512]{1,0:T(8,128)S(1)}, f32[48,512]{1,0:T(8,128)S(1)}, bf16[48,512]{1,0:T(8,128)(2,1)S(1)}, bf16[...) custom-call(bf16[80,640]{1,0:T(8,128)(2,1)S(1)} %get-tuple-element.4, ...), custom_call_target="tpu_custom_call" | custom-call | bytes 1024 | tf_op jit(solution)/shard_map/pallas_call | solution.py:38
  22.3 1.7 collective-permute-done.8._.prev2_routes
  24.0 0.9 shard_map.112
  24.9 2.7 %collective-permute-start.12 = (bf16[32,5120]{1,0:T(8,128)(2,1)S(1)}, bf16[32,5120]{1,0:T(8,128)(2,1)S(1)}, u32[]{:S(2)}, u32[]{:S(2)}) collective-permute-start(bf16[32,5120]{1,0:T(8,128)(2,1)S(1)} %get-tuple-element.57), channel_id=1, source_target_pairs={{16,0},{24,8},{0,16},{8,24},{17,1},{25,9},{1,17},{9,25},{18,2},{26... | collective-permute-start | bytes 983048 | tf_op jit(solution)/shard_map/ppermute | solution.py:25
  27.6 0.5 collective-permute-start.3
  28.2 1.0 collective-permute-start.4
  29.4 1.6 collective-permute-done.3.refs_1_
  31.0 4.0 %collective-permute-done.4.refs_2_ = bf16[80,640]{1,0:T(8,128)(2,1)S(1)} collective-permute-done((bf16[80,640]{1,0:T(8,128)(2,1)S(1)}, bf16[80,640]{1,0:T(8,128)(2,1)S(1)}, u32[]{:S(2)}, u32[]{:S(2)}) %collective-permute-start.4) | collective-permute-done | bytes 102432 | tf_op jit(solution)/shard_map/ppermute | solution.py:25
  35.1 0.5 shard_map.113
  35.6 1.5 collective-permute-start.10
  37.1 2.4 %collective-permute-start.11 = (bf16[80,640]{1,0:T(8,128)(2,1)S(1)}, bf16[80,640]{1,0:T(8,128)(2,1)S(1)}, u32[]{:S(2)}, u32[]{:S(2)}) collective-permute-start(bf16[80,640]{1,0:T(8,128)(2,1)S(1)} %get-tuple-element.56), channel_id=1, source_target_pairs={{8,0},{16,8},{24,16},{0,24},{9,1},{17,9},{25,17},{1,25},{10,2},{18... | collective-permute-start | bytes 307208 | tf_op jit(solution)/shard_map/ppermute | solution.py:25
  39.5 3.9 %collective-permute-done.10.h.refs_4_ = bf16[80,640]{1,0:T(8,128)(2,1)S(1)} collective-permute-done((bf16[80,640]{1,0:T(8,128)(2,1)S(1)}, bf16[80,640]{1,0:T(8,128)(2,1)S(1)}, u32[]{:S(2)}, u32[]{:S(2)}) %collective-permute-start.10) | collective-permute-done | bytes 102432 | tf_op jit(solution)/shard_map/ppermute | solution.py:25
  43.4 1.8 %collective-permute-done.11.cot.refs_5_ = bf16[80,640]{1,0:T(8,128)(2,1)S(1)} collective-permute-done((bf16[80,640]{1,0:T(8,128)(2,1)S(1)}, bf16[80,640]{1,0:T(8,128)(2,1)S(1)}, u32[]{:S(2)}, u32[]{:S(2)}) %collective-permute-start.11) | collective-permute-done | bytes 102432 | tf_op jit(solution)/shard_map/ppermute | solution.py:25
  45.2 5.8 %collective-permute-done.12._.refs_1_.refs_10_ = bf16[32,5120]{1,0:T(8,128)(2,1)S(1)} collective-permute-done((bf16[32,5120]{1,0:T(8,128)(2,1)S(1)}, bf16[32,5120]{1,0:T(8,128)(2,1)S(1)}, u32[]{:S(2)}, u32[]{:S(2)}) %collective-permute-start.12) | collective-permute-done | bytes 327712 | tf_op jit(solution)/shard_map/ppermute | solution.py:25
  51.0 0.4 shard_map.114
  51.5 1.6 collective-permute-start.14
  53.2 1.4 collective-permute-start.15
  54.6 3.6 %collective-permute-start.21 = (bf16[64,3200]{1,0:T(8,128)(2,1)S(1)}, bf16[64,3200]{1,0:T(8,128)(2,1)S(1)}, u32[]{:S(2)}, u32[]{:S(2)}) collective-permute-start(bf16[64,3200]{1,0:T(8,128)(2,1)S(1)} %get-tuple-element.66), channel_id=1, source_target_pairs={{16,0},{24,8},{0,16},{8,24},{17,1},{25,9},{1,17},{9,25},{18,2},{26... | collective-permute-start | bytes 1228808 | tf_op jit(solution)/shard_map/ppermute | solution.py:25
  58.3 1.2 collective-permute-done.14.refs_2_
  59.5 2.9 %collective-permute-done.15.refs_3_ = bf16[160,640]{1,0:T(8,128)(2,1)S(1)} collective-permute-done((bf16[160,640]{1,0:T(8,128)(2,1)S(1)}, bf16[160,640]{1,0:T(8,128)(2,1)S(1)}, u32[]{:S(2)}, u32[]{:S(2)}) %collective-permute-start.15) | collective-permute-done | bytes 204832 | tf_op jit(solution)/shard_map/ppermute | solution.py:25
  62.4 9.4 %shard_map.115 = (bf16[48,11264]{1,0:T(8,128)(2,1)S(1)}, bf16[48,6144]{1,0:T(8,128)(2,1)S(1)}, bf16[80,640]{1,0:T(8,128)(2,1)S(1)}, bf16[80,640]{1,0:T(8,128)(2,...) custom-call(bf16[160,640]{1,0:T(8,128)(2,1)S(1)} %get-tuple-element.58.refs_0_, ...), custom_call_target="tpu_custom_call" | custom-call | bytes 1024 | tf_op jit(solution)/shard_map/pallas_call | solution.py:38
  71.8 2.3 %collective-permute-start.17 = (bf16[80,640]{1,0:T(8,128)(2,1)S(1)}, bf16[80,640]{1,0:T(8,128)(2,1)S(1)}, u32[]{:S(2)}, u32[]{:S(2)}) collective-permute-start(bf16[80,640]{1,0:T(8,128)(2,1)S(1)} %get-tuple-element.62), channel_id=1, source_target_pairs={{2,0},{4,2},{6,4},{0,6},{3,1},{5,3},{7,5},{1,7},{10,8},{12,10},{14... | collective-permute-start | bytes 307208 | tf_op jit(solution)/shard_map/ppermute | solution.py:25
  74.2 1.5 collective-permute-start.35
  75.7 1.3 collective-permute-done.17.refs_1_
  77.0 2.8 %collective-permute-done.18.refs_2_ = bf16[80,640]{1,0:T(8,128)(2,1)S(1)} collective-permute-done((bf16[80,640]{1,0:T(8,128)(2,1)S(1)}, bf16[80,640]{1,0:T(8,128)(2,1)S(1)}, u32[]{:S(2)}, u32[]{:S(2)}) %collective-permute-start.18) | collective-permute-done | bytes 102432 | tf_op jit(solution)/shard_map/ppermute | solution.py:25
  79.7 0.8 shard_map.116
  80.5 2.7 %collective-permute-start.20 = (bf16[80,640]{1,0:T(8,128)(2,1)S(1)}, bf16[80,640]{1,0:T(8,128)(2,1)S(1)}, u32[]{:S(2)}, u32[]{:S(2)}) collective-permute-start(bf16[80,640]{1,0:T(8,128)(2,1)S(1)} %get-tuple-element.65._), channel_id=1, source_target_pairs={{8,0},{16,8},{24,16},{0,24},{9,1},{17,9},{25,17},{1,25},{10,2},{18... | collective-permute-start | bytes 307208 | tf_op jit(solution)/shard_map/ppermute | solution.py:25
  83.2 1.9 %collective-permute-start.28 = (bf16[96,5120]{1,0:T(8,128)(2,1)S(1)}, bf16[96,5120]{1,0:T(8,128)(2,1)S(1)}, u32[]{:S(2)}, u32[]{:S(2)}) collective-permute-start(bf16[96,5120]{1,0:T(8,128)(2,1)S(1)} %get-tuple-element.77), channel_id=1, source_target_pairs={{16,0},{24,8},{0,16},{8,24},{17,1},{25,9},{1,17},{9,25},{18,2},{26... | collective-permute-start | bytes 2949128 | tf_op jit(solution)/shard_map/ppermute | solution.py:25
  85.1 3.6 %shard_map.117 = (bf16[80,640]{1,0:T(8,128)(2,1)S(1)}, bf16[80,640]{1,0:T(8,128)(2,1)S(1)}, bf16[80,640]{1,0:T(8,128)(2,1)S(1)}, bf16[80,640]{1,0:T(8,128)(2,1)S(1)}) custom-call(bf16[48,11264]{1,0:T(8,128)(2,1)S(1)} %get-tuple-element.67.act.refs_0_.refs_2_.refs_4_.refs_6_, bf16[512,5120]{1,0:T(8,128)(2,1)} %bitcast.21, bf16[80,640]{1,0:T(8,128)(2,1)S(1)} %get-tuple-element.65._), custom_call_target="tpu_custom_call" | custom-call | bytes 1024 | tf_op jit(solution)/shard_map/pallas_call | solution.py:38
  88.7 1.4 shard_map.118
  90.2 1.6 collective-permute-start.23
  91.8 1.4 collective-permute-start.24
  93.2 1.5 collective-permute-done.22.refs_1_
  94.8 1.2 collective-permute-done.23.refs_2_
  96.0 1.6 collective-permute-start.32
  97.6 0.8 collective-permute-start.33
  98.4 9.0 %shard_map.119 = (bf16[48,6144]{1,0:T(8,128)(2,1)S(1)}, bf16[80,640]{1,0:T(8,128)(2,1)S(1)}, bf16[80,640]{1,0:T(8,128)(2,1)S(1)}, bf16[80,640]{1,0:T(8,128)(2,1)S(1)}, bf16[80,640]{1,0:T(8,128)(2,1)S(1)}) custom-call(bf16[80,640]{1,0:T(8,128)(2,1)S(1)} %get-tuple-element.69.refs_0_, bf16[80,640]{1,0:T(8,128)(2,1)S(1)} %collective-permute-done.22.refs_1_, ...), custom_call_target="tpu_custom_call" | custom-call | bytes 1024 | tf_op jit(solution)/shard_map/pallas_call | solution.py:38
  107.4 1.6 collective-permute-start.37
  109.0 0.5 collective-permute-start.36
  109.5 0.4 collective-permute-start.25
  109.9 2.3 %collective-permute-done.25.refs_1_ = bf16[80,640]{1,0:T(8,128)(2,1)S(1)} collective-permute-done((bf16[80,640]{1,0:T(8,128)(2,1)S(1)}, bf16[80,640]{1,0:T(8,128)(2,1)S(1)}, u32[]{:S(2)}, u32[]{:S(2)}) %collective-permute-start.25) | collective-permute-done | bytes 102432 | tf_op jit(solution)/shard_map/ppermute | solution.py:25
  112.1 0.7 collective-permute-start.26
  112.8 4.8 %collective-permute-done.26.refs_2_ = bf16[80,640]{1,0:T(8,128)(2,1)S(1)} collective-permute-done((bf16[80,640]{1,0:T(8,128)(2,1)S(1)}, bf16[80,640]{1,0:T(8,128)(2,1)S(1)}, u32[]{:S(2)}, u32[]{:S(2)}) %collective-permute-start.26) | collective-permute-done | bytes 102432 | tf_op jit(solution)/shard_map/ppermute | solution.py:25
  117.7 0.3 collective-permute-start.27
  118.0 3.7 %collective-permute-done.27.refs_3_ = bf16[80,640]{1,0:T(8,128)(2,1)S(1)} collective-permute-done((bf16[80,640]{1,0:T(8,128)(2,1)S(1)}, bf16[80,640]{1,0:T(8,128)(2,1)S(1)}, u32[]{:S(2)}, u32[]{:S(2)}) %collective-permute-start.27) | collective-permute-done | bytes 102432 | tf_op jit(solution)/shard_map/ppermute | solution.py:25
  121.8 19.4 %collective-permute-start.29 = (bf16[32,5120]{1,0:T(8,128)(2,1)S(1)}, bf16[32,5120]{1,0:T(8,128)(2,1)S(1)}, u32[]{:S(2)}, u32[]{:S(2)}) collective-permute-start(bf16[32,5120]{1,0:T(8,128)(2,1)S(1)} %get-tuple-element.78), channel_id=1, source_target_pairs={{16,0},{24,8},{0,16},{8,24},{17,1},{25,9},{1,17},{9,25},{18,2},{26... | collective-permute-start | bytes 983048 | tf_op jit(solution)/shard_map/ppermute | solution.py:25
  141.2 0.2 shard_map.121
  141.5 2.0 %collective-permute-start.30 = (bf16[80,640]{1,0:T(8,128)(2,1)S(1)}, bf16[80,640]{1,0:T(8,128)(2,1)S(1)}, u32[]{:S(2)}, u32[]{:S(2)}) collective-permute-start(bf16[80,640]{1,0:T(8,128)(2,1)S(1)} %get-tuple-element.79), channel_id=1, source_target_pairs={{16,0},{24,8},{0,16},{8,24},{17,1},{25,9},{1,17},{9,25},{18,2},{26... | collective-permute-start | bytes 307208 | tf_op jit(solution)/shard_map/ppermute | solution.py:25
  143.5 13.4 %collective-permute-start.34 = (bf16[80,640]{1,0:T(8,128)(2,1)S(1)}, bf16[80,640]{1,0:T(8,128)(2,1)S(1)}, u32[]{:S(2)}, u32[]{:S(2)}) collective-permute-start(bf16[80,640]{1,0:T(8,128)(2,1)S(1)} %shard_map.121), channel_id=1, source_target_pairs={{24,0},{0,8},{8,16},{16,24},{25,1},{1,9},{9,17},{17,25},{26,2},{2,... | collective-permute-start | bytes 307208 | tf_op jit(solution)/shard_map/ppermute | solution.py:25
  156.9 2.4 %shard_map.120 = bf16[128,5120]{1,0:T(8,128)(2,1)} custom-call(bf16[80,640]{1,0:T(8,128)(2,1)S(1)} %get-tuple-element.72.refs_0_, bf16[80,640]{1,0:T(8,128)(2,1)S(1)} %collective-permute-done.25.refs_1_, bf16[80,640]{1,0:T(8,128)(2,1)S(1)} %collective-permute-done.26.refs_2_, bf16[80,640]{1,0:T(8,128)(2,1)S(1)} %collective-permute-done.27.refs_3_, ...), custom_call_target="tpu_custom_call" | custom-call | bytes 1024 | tf_op jit(solution)/shard_map/pallas_call | solution.py:38
  159.3 7.2 %shard_map.123 = (bf16[5120,512]{1,0:T(8,128)(2,1)}, bf16[5120,512]{1,0:T(8,128)(2,1)}) custom-call(bf16[48,11264]{1,0:T(8,128)(2,1)S(1)} %get-tuple-element.67.act.refs_0_.refs_2_.refs_4_.refs_6_, bf16[48,11264]{1,0:T(8,128)(2,1)S(1)} %collective-permute-done.35.refs_1_.refs_3_.refs_5_.refs_7_, ...), custom_call_target="tpu_custom_call" | custom-call | bytes 1024 | tf_op jit(solution)/shard_map/pallas_call | solution.py:436
  166.5 6.3 %shard_map.124 = bf16[512,5120]{1,0:T(8,128)(2,1)} custom-call(bf16[48,6144]{1,0:T(8,128)(2,1)S(1)} %get-tuple-element.83.refs_4_.refs_6_.refs_0_, bf16[48,6144]{1,0:T(8,128)(2,1)S(1)} %collective-permute-done.36.refs_5_.refs_7_.refs_1_, bf16[48,6144]{1,0:T(8,128)(2,1)S(1)} %get-tuple-element.84.refs_8_.refs_10_.refs_2_, ...), custom_call_target="tpu_custom_call" | custom-call | bytes 1024 | tf_op jit(solution)/shard_map/pallas_call | solution.py:436
  172.9 2.2 %shard_map.122 = bf16[128,5120]{1,0:T(8,128)(2,1)} custom-call(bf16[96,5120]{1,0:T(8,128)(2,1)S(1)} %collective-permute-done.28.first, bf16[32,5120]{1,0:T(8,128)(2,1)S(1)} %collective-permute-done.29.rest, bf16[80,640]{1,0:T(8,128)(2,1)S(1)} %collective-permute-done.30.upd0, s32[1,4,128]{2,1,0:T(4,128)S(1)} %collective-permute-done.8._.prev2_routes, ...), custom_call_target="tpu_custom_call" | custom-call | bytes 1024 | tf_op jit(solution)/shard_map/pallas_call | solution.py:38
  (42 shorter events, 0.8 us)
Async XLA Ops:
  0.6 1.3 copy-start
  1.9 1.3 copy-start.2
  3.3 0.7 copy-start.4
  5.0 19.0 %collective-permute-start.9 = (bf16[32,5120]{1,0:T(8,128)(2,1)S(1)}, bf16[32,5120]{1,0:T(8,128)(2,1)S(1)}, u32[]{:S(2)}, u32[]{:S(2)}) collective-permute-start(bf16[32,5120]{1,0:T(8,128)(2,1)S(1)} %get-tuple-element.53), channel_id=1, source_target_pairs={{16,0},{24,8},{0,16},{8,24},{17,1},{25,9},{1,17},{9,25},{18,2},{26... | collective-permute-start | bytes 983048 | tf_op jit(solution)/shard_map/ppermute | solution.py:25
  9.1 4.6 %collective-permute-start = (bf16[80,640]{1,0:T(8,128)(2,1)S(1)}, bf16[80,640]{1,0:T(8,128)(2,1)S(1)}, u32[]{:S(2)}, u32[]{:S(2)}) collective-permute-start(bf16[80,640]{1,0:T(8,128)(2,1)S(1)} %get-tuple-element.46.refs_0_), channel_id=1, source_target_pairs={{6,0},{0,2},{2,4},{4,6},{7,1},{1,3},{3,5},{5,7},{14,8},{8,10},{10,... | collective-permute-start | bytes 307208 | tf_op jit(solution)/shard_map/ppermute | solution.py:25
  9.1 6.2 %collective-permute-start.1 = (bf16[80,640]{1,0:T(8,128)(2,1)S(1)}, bf16[80,640]{1,0:T(8,128)(2,1)S(1)}, u32[]{:S(2)}, u32[]{:S(2)}) collective-permute-start(bf16[80,640]{1,0:T(8,128)(2,1)S(1)} %get-tuple-element.46.refs_0_), channel_id=1, source_target_pairs={{4,0},{6,2},{0,4},{2,6},{5,1},{7,3},{1,5},{3,7},{12,8},{14,10},{8,... | collective-permute-start | bytes 307208 | tf_op jit(solution)/shard_map/ppermute | solution.py:25
  10.6 5.0 %collective-permute-start.2 = (bf16[80,640]{1,0:T(8,128)(2,1)S(1)}, bf16[80,640]{1,0:T(8,128)(2,1)S(1)}, u32[]{:S(2)}, u32[]{:S(2)}) collective-permute-start(bf16[80,640]{1,0:T(8,128)(2,1)S(1)} %get-tuple-element.46.refs_0_), channel_id=1, source_target_pairs={{2,0},{4,2},{6,4},{0,6},{3,1},{5,3},{7,5},{1,7},{10,8},{12,10},{14... | collective-permute-start | bytes 307208 | tf_op jit(solution)/shard_map/ppermute | solution.py:25
  12.1 10.2 %collective-permute-start.6 = (s32[1,4,128]{2,1,0:T(4,128)S(1)}, s32[1,4,128]{2,1,0:T(4,128)S(1)}, u32[]{:S(2)}, u32[]{:S(2)}) collective-permute-start(s32[1,4,128]{2,1,0:T(4,128)S(1)} %get-tuple-element.88), channel_id=1, source_target_pairs={{8,0},{16,8},{24,16},{0,24},{9,1},{17,9},{25,17},{1,25},{10,2},{18... | collective-permute-start | bytes 6152 | tf_op jit(solution)/shard_map/ppermute | solution.py:25
  13.7 8.5 %collective-permute-start.7 = (s32[1,4,128]{2,1,0:T(4,128)S(1)}, s32[1,4,128]{2,1,0:T(4,128)S(1)}, u32[]{:S(2)}, u32[]{:S(2)}) collective-permute-start(s32[1,4,128]{2,1,0:T(4,128)S(1)} %get-tuple-element.88), channel_id=1, source_target_pairs={{24,0},{0,8},{8,16},{16,24},{25,1},{1,9},{9,17},{17,25},{26,2},{2,... | collective-permute-start | bytes 6152 | tf_op jit(solution)/shard_map/ppermute | solution.py:25
  15.3 8.7 %collective-permute-start.8 = (s32[1,4,128]{2,1,0:T(4,128)S(1)}, s32[1,4,128]{2,1,0:T(4,128)S(1)}, u32[]{:S(2)}, u32[]{:S(2)}) collective-permute-start(s32[1,4,128]{2,1,0:T(4,128)S(1)} %get-tuple-element.87), channel_id=1, source_target_pairs={{16,0},{24,8},{0,16},{8,24},{17,1},{25,9},{1,17},{9,25},{18,2},{26... | collective-permute-start | bytes 6152 | tf_op jit(solution)/shard_map/ppermute | solution.py:25
  15.6 8.4 %copy-start.1 = (bf16[128,5120]{1,0:T(8,128)(2,1)S(1)}, bf16[128,5120]{1,0:T(8,128)(2,1)}, u32[]{:S(2)}) copy-start(bf16[128,5120]{1,0:T(8,128)(2,1)} %cotangent.3) | copy-start | bytes 3932164
  15.6 8.4 %copy-start.3 = (bf16[128,5120]{1,0:T(8,128)(2,1)S(1)}, bf16[128,5120]{1,0:T(8,128)(2,1)}, u32[]{:S(2)}) copy-start(bf16[128,5120]{1,0:T(8,128)(2,1)} %refs_4_.1) | copy-start | bytes 3932164
  15.6 19.4 %copy-start.5 = (s32[2,128,4]{1,2,0:T(4,128)S(1)}, s32[2,128,4]{1,2,0:T(4,128)}, u32[]{:S(2)}) copy-start(s32[2,128,4]{1,2,0:T(4,128)} %param.12) | copy-start | bytes 12292
  15.6 19.4 %copy-start.6 = (f32[2,128,4]{1,2,0:T(4,128)S(1)}, f32[2,128,4]{1,2,0:T(4,128)}, u32[]{:S(2)}) copy-start(f32[2,128,4]{1,2,0:T(4,128)} %param.13) | copy-start | bytes 12292
  24.9 26.1 %collective-permute-start.12 = (bf16[32,5120]{1,0:T(8,128)(2,1)S(1)}, bf16[32,5120]{1,0:T(8,128)(2,1)S(1)}, u32[]{:S(2)}, u32[]{:S(2)}) collective-permute-start(bf16[32,5120]{1,0:T(8,128)(2,1)S(1)} %get-tuple-element.57), channel_id=1, source_target_pairs={{16,0},{24,8},{0,16},{8,24},{17,1},{25,9},{1,17},{9,25},{18,2},{26... | collective-permute-start | bytes 983048 | tf_op jit(solution)/shard_map/ppermute | solution.py:25
  27.6 3.4 %collective-permute-start.3 = (bf16[80,640]{1,0:T(8,128)(2,1)S(1)}, bf16[80,640]{1,0:T(8,128)(2,1)S(1)}, u32[]{:S(2)}, u32[]{:S(2)}) collective-permute-start(bf16[80,640]{1,0:T(8,128)(2,1)S(1)} %get-tuple-element.48), channel_id=1, source_target_pairs={{2,0},{4,2},{6,4},{0,6},{3,1},{5,3},{7,5},{1,7},{10,8},{12,10},{14... | collective-permute-start | bytes 307208 | tf_op jit(solution)/shard_map/ppermute | solution.py:25
  28.2 6.9 %collective-permute-start.4 = (bf16[80,640]{1,0:T(8,128)(2,1)S(1)}, bf16[80,640]{1,0:T(8,128)(2,1)S(1)}, u32[]{:S(2)}, u32[]{:S(2)}) collective-permute-start(bf16[80,640]{1,0:T(8,128)(2,1)S(1)} %get-tuple-element.49), channel_id=1, source_target_pairs={{4,0},{6,2},{0,4},{2,6},{5,1},{7,3},{1,5},{3,7},{12,8},{14,10},{8,... | collective-permute-start | bytes 307208 | tf_op jit(solution)/shard_map/ppermute | solution.py:25
  29.1 5.9 %collective-permute-start.5 = (bf16[80,640]{1,0:T(8,128)(2,1)S(1)}, bf16[80,640]{1,0:T(8,128)(2,1)S(1)}, u32[]{:S(2)}, u32[]{:S(2)}) collective-permute-start(bf16[80,640]{1,0:T(8,128)(2,1)S(1)} %get-tuple-element.50), channel_id=1, source_target_pairs={{6,0},{0,2},{2,4},{4,6},{7,1},{1,3},{3,5},{5,7},{14,8},{8,10},{10,... | collective-permute-start | bytes 307208 | tf_op jit(solution)/shard_map/ppermute | solution.py:25
  35.6 7.8 %collective-permute-start.10 = (bf16[80,640]{1,0:T(8,128)(2,1)S(1)}, bf16[80,640]{1,0:T(8,128)(2,1)S(1)}, u32[]{:S(2)}, u32[]{:S(2)}) collective-permute-start(bf16[80,640]{1,0:T(8,128)(2,1)S(1)} %get-tuple-element.55), channel_id=1, source_target_pairs={{24,0},{0,8},{8,16},{16,24},{25,1},{1,9},{9,17},{17,25},{26,2},{2,... | collective-permute-start | bytes 307208 | tf_op jit(solution)/shard_map/ppermute | solution.py:25
  37.1 8.1 %collective-permute-start.11 = (bf16[80,640]{1,0:T(8,128)(2,1)S(1)}, bf16[80,640]{1,0:T(8,128)(2,1)S(1)}, u32[]{:S(2)}, u32[]{:S(2)}) collective-permute-start(bf16[80,640]{1,0:T(8,128)(2,1)S(1)} %get-tuple-element.56), channel_id=1, source_target_pairs={{8,0},{16,8},{24,16},{0,24},{9,1},{17,9},{25,17},{1,25},{10,2},{18... | collective-permute-start | bytes 307208 | tf_op jit(solution)/shard_map/ppermute | solution.py:25
  39.5 18.7 %collective-permute-start.16 = (bf16[64,1920]{1,0:T(8,128)(2,1)S(1)}, bf16[64,1920]{1,0:T(8,128)(2,1)S(1)}, u32[]{:S(2)}, u32[]{:S(2)}) collective-permute-start(bf16[64,1920]{1,0:T(8,128)(2,1)S(1)} %get-tuple-element.60), channel_id=1, source_target_pairs={{16,0},{24,8},{0,16},{8,24},{17,1},{25,9},{1,17},{9,25},{18,2},{26... | collective-permute-start | bytes 737288 | tf_op jit(solution)/shard_map/ppermute | solution.py:25
  51.5 6.8 %collective-permute-start.13 = (bf16[160,640]{1,0:T(8,128)(2,1)S(1)}, bf16[160,640]{1,0:T(8,128)(2,1)S(1)}, u32[]{:S(2)}, u32[]{:S(2)}) collective-permute-start(bf16[160,640]{1,0:T(8,128)(2,1)S(1)} %get-tuple-element.58.refs_0_), channel_id=1, source_target_pairs={{6,0},{0,2},{2,4},{4,6},{7,1},{1,3},{3,5},{5,7},{14,8},{8,10},{10,... | collective-permute-start | bytes 614408 | tf_op jit(solution)/shard_map/ppermute | solution.py:25
  51.5 8.0 %collective-permute-start.14 = (bf16[160,640]{1,0:T(8,128)(2,1)S(1)}, bf16[160,640]{1,0:T(8,128)(2,1)S(1)}, u32[]{:S(2)}, u32[]{:S(2)}) collective-permute-start(bf16[160,640]{1,0:T(8,128)(2,1)S(1)} %get-tuple-element.58.refs_0_), channel_id=1, source_target_pairs={{4,0},{6,2},{0,4},{2,6},{5,1},{7,3},{1,5},{3,7},{12,8},{14,10},{8,... | collective-permute-start | bytes 614408 | tf_op jit(solution)/shard_map/ppermute | solution.py:25
  53.2 9.2 %collective-permute-start.15 = (bf16[160,640]{1,0:T(8,128)(2,1)S(1)}, bf16[160,640]{1,0:T(8,128)(2,1)S(1)}, u32[]{:S(2)}, u32[]{:S(2)}) collective-permute-start(bf16[160,640]{1,0:T(8,128)(2,1)S(1)} %get-tuple-element.58.refs_0_), channel_id=1, source_target_pairs={{2,0},{4,2},{6,4},{0,6},{3,1},{5,3},{7,5},{1,7},{10,8},{12,10},{14... | collective-permute-start | bytes 614408 | tf_op jit(solution)/shard_map/ppermute | solution.py:25
  54.6 34.2 %collective-permute-start.21 = (bf16[64,3200]{1,0:T(8,128)(2,1)S(1)}, bf16[64,3200]{1,0:T(8,128)(2,1)S(1)}, u32[]{:S(2)}, u32[]{:S(2)}) collective-permute-start(bf16[64,3200]{1,0:T(8,128)(2,1)S(1)} %get-tuple-element.66), channel_id=1, source_target_pairs={{16,0},{24,8},{0,16},{8,24},{17,1},{25,9},{1,17},{9,25},{18,2},{26... | collective-permute-start | bytes 1228808 | tf_op jit(solution)/shard_map/ppermute | solution.py:25
  71.8 5.2 %collective-permute-start.17 = (bf16[80,640]{1,0:T(8,128)(2,1)S(1)}, bf16[80,640]{1,0:T(8,128)(2,1)S(1)}, u32[]{:S(2)}, u32[]{:S(2)}) collective-permute-start(bf16[80,640]{1,0:T(8,128)(2,1)S(1)} %get-tuple-element.62), channel_id=1, source_target_pairs={{2,0},{4,2},{6,4},{0,6},{3,1},{5,3},{7,5},{1,7},{10,8},{12,10},{14... | collective-permute-start | bytes 307208 | tf_op jit(solution)/shard_map/ppermute | solution.py:25
  74.0 5.7 %collective-permute-start.18 = (bf16[80,640]{1,0:T(8,128)(2,1)S(1)}, bf16[80,640]{1,0:T(8,128)(2,1)S(1)}, u32[]{:S(2)}, u32[]{:S(2)}) collective-permute-start(bf16[80,640]{1,0:T(8,128)(2,1)S(1)} %get-tuple-element.63), channel_id=1, source_target_pairs={{4,0},{6,2},{0,4},{2,6},{5,1},{7,3},{1,5},{3,7},{12,8},{14,10},{8,... | collective-permute-start | bytes 307208 | tf_op jit(solution)/shard_map/ppermute | solution.py:25
  74.2 5.6 %collective-permute-start.19 = (bf16[80,640]{1,0:T(8,128)(2,1)S(1)}, bf16[80,640]{1,0:T(8,128)(2,1)S(1)}, u32[]{:S(2)}, u32[]{:S(2)}) collective-permute-start(bf16[80,640]{1,0:T(8,128)(2,1)S(1)} %get-tuple-element.64), channel_id=1, source_target_pairs={{6,0},{0,2},{2,4},{4,6},{7,1},{1,3},{3,5},{5,7},{14,8},{8,10},{10,... | collective-permute-start | bytes 307208 | tf_op jit(solution)/shard_map/ppermute | solution.py:25
  74.2 85.1 %collective-permute-start.35 = (bf16[48,11264]{1,0:T(8,128)(2,1)S(1)}, bf16[48,11264]{1,0:T(8,128)(2,1)S(1)}, u32[]{:S(2)}, u32[]{:S(2)}) collective-permute-start(bf16[48,11264]{1,0:T(8,128)(2,1)S(1)} %get-tuple-element.67.act.refs_0_.refs_2_.refs_4_.refs_6_), channel_id=1, source_target_pairs={{1,0},{0,1},{3,2},{2,3},{5,4},{4,5},{7,6},{6,7},{9,8},{8,9},{11,10... | collective-permute-start | bytes 3244040 | tf_op jit(solution)/shard_map/ppermute | solution.py:25
  80.5 8.2 %collective-permute-start.20 = (bf16[80,640]{1,0:T(8,128)(2,1)S(1)}, bf16[80,640]{1,0:T(8,128)(2,1)S(1)}, u32[]{:S(2)}, u32[]{:S(2)}) collective-permute-start(bf16[80,640]{1,0:T(8,128)(2,1)S(1)} %get-tuple-element.65._), channel_id=1, source_target_pairs={{8,0},{16,8},{24,16},{0,24},{9,1},{17,9},{25,17},{1,25},{10,2},{18... | collective-permute-start | bytes 307208 | tf_op jit(solution)/shard_map/ppermute | solution.py:25
  83.2 89.6 %collective-permute-start.28 = (bf16[96,5120]{1,0:T(8,128)(2,1)S(1)}, bf16[96,5120]{1,0:T(8,128)(2,1)S(1)}, u32[]{:S(2)}, u32[]{:S(2)}) collective-permute-start(bf16[96,5120]{1,0:T(8,128)(2,1)S(1)} %get-tuple-element.77), channel_id=1, source_target_pairs={{16,0},{24,8},{0,16},{8,24},{17,1},{25,9},{1,17},{9,25},{18,2},{26... | collective-permute-start | bytes 2949128 | tf_op jit(solution)/shard_map/ppermute | solution.py:25
  90.1 4.6 %collective-permute-start.22 = (bf16[80,640]{1,0:T(8,128)(2,1)S(1)}, bf16[80,640]{1,0:T(8,128)(2,1)S(1)}, u32[]{:S(2)}, u32[]{:S(2)}) collective-permute-start(bf16[80,640]{1,0:T(8,128)(2,1)S(1)} %get-tuple-element.69.refs_0_), channel_id=1, source_target_pairs={{6,0},{0,2},{2,4},{4,6},{7,1},{1,3},{3,5},{5,7},{14,8},{8,10},{10,... | collective-permute-start | bytes 307208 | tf_op jit(solution)/shard_map/ppermute | solution.py:25
  90.2 5.8 %collective-permute-start.23 = (bf16[80,640]{1,0:T(8,128)(2,1)S(1)}, bf16[80,640]{1,0:T(8,128)(2,1)S(1)}, u32[]{:S(2)}, u32[]{:S(2)}) collective-permute-start(bf16[80,640]{1,0:T(8,128)(2,1)S(1)} %get-tuple-element.69.refs_0_), channel_id=1, source_target_pairs={{4,0},{6,2},{0,4},{2,6},{5,1},{7,3},{1,5},{3,7},{12,8},{14,10},{8,... | collective-permute-start | bytes 307208 | tf_op jit(solution)/shard_map/ppermute | solution.py:25
  91.8 5.7 %collective-permute-start.24 = (bf16[80,640]{1,0:T(8,128)(2,1)S(1)}, bf16[80,640]{1,0:T(8,128)(2,1)S(1)}, u32[]{:S(2)}, u32[]{:S(2)}) collective-permute-start(bf16[80,640]{1,0:T(8,128)(2,1)S(1)} %get-tuple-element.69.refs_0_), channel_id=1, source_target_pairs={{2,0},{4,2},{6,4},{0,6},{3,1},{5,3},{7,5},{1,7},{10,8},{12,10},{14... | collective-permute-start | bytes 307208 | tf_op jit(solution)/shard_map/ppermute | solution.py:25
  94.8 12.6 %collective-permute-start.31 = (bf16[80,640]{1,0:T(8,128)(2,1)S(1)}, bf16[80,640]{1,0:T(8,128)(2,1)S(1)}, u32[]{:S(2)}, u32[]{:S(2)}) collective-permute-start(bf16[80,640]{1,0:T(8,128)(2,1)S(1)} %get-tuple-element.80), channel_id=1, source_target_pairs={{2,0},{4,2},{6,4},{0,6},{3,1},{5,3},{7,5},{1,7},{10,8},{12,10},{14... | collective-permute-start | bytes 307208 | tf_op jit(solution)/shard_map/ppermute | solution.py:25
  96.0 13.0 %collective-permute-start.32 = (bf16[80,640]{1,0:T(8,128)(2,1)S(1)}, bf16[80,640]{1,0:T(8,128)(2,1)S(1)}, u32[]{:S(2)}, u32[]{:S(2)}) collective-permute-start(bf16[80,640]{1,0:T(8,128)(2,1)S(1)} %get-tuple-element.81), channel_id=1, source_target_pairs={{4,0},{6,2},{0,4},{2,6},{5,1},{7,3},{1,5},{3,7},{12,8},{14,10},{8,... | collective-permute-start | bytes 307208 | tf_op jit(solution)/shard_map/ppermute | solution.py:25
  97.6 12.0 %collective-permute-start.33 = (bf16[80,640]{1,0:T(8,128)(2,1)S(1)}, bf16[80,640]{1,0:T(8,128)(2,1)S(1)}, u32[]{:S(2)}, u32[]{:S(2)}) collective-permute-start(bf16[80,640]{1,0:T(8,128)(2,1)S(1)} %get-tuple-element.82), channel_id=1, source_target_pairs={{6,0},{0,2},{2,4},{4,6},{7,1},{1,3},{3,5},{5,7},{14,8},{8,10},{10,... | collective-permute-start | bytes 307208 | tf_op jit(solution)/shard_map/ppermute | solution.py:25
  107.4 34.0 %collective-permute-start.37 = (bf16[48,6144]{1,0:T(8,128)(2,1)S(1)}, bf16[48,6144]{1,0:T(8,128)(2,1)S(1)}, u32[]{:S(2)}, u32[]{:S(2)}) collective-permute-start(bf16[48,6144]{1,0:T(8,128)(2,1)S(1)} %get-tuple-element.84.refs_8_.refs_10_.refs_2_), channel_id=1, source_target_pairs={{1,0},{0,1},{3,2},{2,3},{5,4},{4,5},{7,6},{6,7},{9,8},{8,9},{11,10... | collective-permute-start | bytes 1769480 | tf_op jit(solution)/shard_map/ppermute | solution.py:25
  109.0 34.5 %collective-permute-start.36 = (bf16[48,6144]{1,0:T(8,128)(2,1)S(1)}, bf16[48,6144]{1,0:T(8,128)(2,1)S(1)}, u32[]{:S(2)}, u32[]{:S(2)}) collective-permute-start(bf16[48,6144]{1,0:T(8,128)(2,1)S(1)} %get-tuple-element.83.refs_4_.refs_6_.refs_0_), channel_id=1, source_target_pairs={{1,0},{0,1},{3,2},{2,3},{5,4},{4,5},{7,6},{6,7},{9,8},{8,9},{11,10... | collective-permute-start | bytes 1769480 | tf_op jit(solution)/shard_map/ppermute | solution.py:25
  109.5 2.6 %collective-permute-start.25 = (bf16[80,640]{1,0:T(8,128)(2,1)S(1)}, bf16[80,640]{1,0:T(8,128)(2,1)S(1)}, u32[]{:S(2)}, u32[]{:S(2)}) collective-permute-start(bf16[80,640]{1,0:T(8,128)(2,1)S(1)} %get-tuple-element.73), channel_id=1, source_target_pairs={{2,0},{4,2},{6,4},{0,6},{3,1},{5,3},{7,5},{1,7},{10,8},{12,10},{14... | collective-permute-start | bytes 307208 | tf_op jit(solution)/shard_map/ppermute | solution.py:25
  112.1 5.5 %collective-permute-start.26 = (bf16[80,640]{1,0:T(8,128)(2,1)S(1)}, bf16[80,640]{1,0:T(8,128)(2,1)S(1)}, u32[]{:S(2)}, u32[]{:S(2)}) collective-permute-start(bf16[80,640]{1,0:T(8,128)(2,1)S(1)} %get-tuple-element.74), channel_id=1, source_target_pairs={{4,0},{6,2},{0,4},{2,6},{5,1},{7,3},{1,5},{3,7},{12,8},{14,10},{8,... | collective-permute-start | bytes 307208 | tf_op jit(solution)/shard_map/ppermute | solution.py:25
  117.7 4.1 %collective-permute-start.27 = (bf16[80,640]{1,0:T(8,128)(2,1)S(1)}, bf16[80,640]{1,0:T(8,128)(2,1)S(1)}, u32[]{:S(2)}, u32[]{:S(2)}) collective-permute-start(bf16[80,640]{1,0:T(8,128)(2,1)S(1)} %get-tuple-element.75), channel_id=1, source_target_pairs={{6,0},{0,2},{2,4},{4,6},{7,1},{1,3},{3,5},{5,7},{14,8},{8,10},{10,... | collective-permute-start | bytes 307208 | tf_op jit(solution)/shard_map/ppermute | solution.py:25
  121.8 51.1 %collective-permute-start.29 = (bf16[32,5120]{1,0:T(8,128)(2,1)S(1)}, bf16[32,5120]{1,0:T(8,128)(2,1)S(1)}, u32[]{:S(2)}, u32[]{:S(2)}) collective-permute-start(bf16[32,5120]{1,0:T(8,128)(2,1)S(1)} %get-tuple-element.78), channel_id=1, source_target_pairs={{16,0},{24,8},{0,16},{8,24},{17,1},{25,9},{1,17},{9,25},{18,2},{26... | collective-permute-start | bytes 983048 | tf_op jit(solution)/shard_map/ppermute | solution.py:25
  141.5 31.4 %collective-permute-start.30 = (bf16[80,640]{1,0:T(8,128)(2,1)S(1)}, bf16[80,640]{1,0:T(8,128)(2,1)S(1)}, u32[]{:S(2)}, u32[]{:S(2)}) collective-permute-start(bf16[80,640]{1,0:T(8,128)(2,1)S(1)} %get-tuple-element.79), channel_id=1, source_target_pairs={{16,0},{24,8},{0,16},{8,24},{17,1},{25,9},{1,17},{9,25},{18,2},{26... | collective-permute-start | bytes 307208 | tf_op jit(solution)/shard_map/ppermute | solution.py:25
  143.5 29.4 %collective-permute-start.34 = (bf16[80,640]{1,0:T(8,128)(2,1)S(1)}, bf16[80,640]{1,0:T(8,128)(2,1)S(1)}, u32[]{:S(2)}, u32[]{:S(2)}) collective-permute-start(bf16[80,640]{1,0:T(8,128)(2,1)S(1)} %shard_map.121), channel_id=1, source_target_pairs={{24,0},{0,8},{8,16},{16,24},{25,1},{1,9},{9,17},{17,25},{26,2},{2,... | collective-permute-start | bytes 307208 | tf_op jit(solution)/shard_map/ppermute | solution.py:25

commit v5 on v4

--- a/solution.py
+++ b/solution.py
@@ -11,12 +11,13 @@
 PACK = 8
 PACKED = CAP * PACK
 COT_PIECES = ((0, 32, 0, 8), (32, 64, 0, 8), (64, 128, 0, 3), (64, 128, 3, 8))
-TOK_PIECES = ((0, 96, 0, 8), (96, 128, 0, 8))
+TOK_PIECES = ((0, 16, 0, 8), (16, 128, 0, 8))
 EPSILON = 1e-06
 F32 = jnp.float32
 BF16 = jnp.bfloat16
-VMEM_BIG = 48 * 1024 * 1024
 VMEM_SMALL = 24 * 1024 * 1024
+VMEM_LOAD = 44 * 1024 * 1024
+VMEM_ALL = 60 * 1024 * 1024
 COST_BYTES = 1024
 
 
@@ -32,7 +33,7 @@
 def call(
     kernel, outs, args, *, any_args=(), any_outs=(), scratch=(), vmem=VMEM_SMALL
 ):
-    outs = [jax.ShapeDtypeStruct(s, d) for s, d in outs]
+    outs = [jax.ShapeDtypeStruct(*o) if isinstance(o, tuple) else o for o in outs]
     anywhere = pl.BlockSpec(memory_space=pl.ANY)
     near = pl.BlockSpec(memory_space=pltpu.VMEM)
     return pl.pallas_call(
@@ -153,16 +154,40 @@
     return copy
 
 
-def first_rows_kernel(tokens, routes, far, raw, normed, piece, sem):
-    copy = piece_copy(far, COT_PIECES[0], piece, sem)
-    values = pick(select_of(routes[0]), whole_block(tokens))
+def load_kernel(gate, up, down, gate_v, up_v, down_v, sems):
+    step = gate.shape[0] // PACK
+    copies = []
+    for c in range(PACK):
+        r = pl.ds(c * step, step)
+        copies += [
+            pltpu.make_async_copy(gate.at[r], gate_v.at[r], sems.at[0, c]),
+            pltpu.make_async_copy(up.at[r], up_v.at[r], sems.at[1, c]),
+            pltpu.make_async_copy(down.at[:, r], down_v.at[:, r], sems.at[2, c]),
+        ]
+    for copy in copies:
+        copy.start()
+    for copy in copies:
+        copy.wait()
+
+
+def first_rows_kernel(tokens, routes, cotangent, raw, normed, piece, sem, sems, held):
+    copy = piece_copy(cotangent, COT_PIECES[0], piece, sem)
+    fetches = []
+    for c in range(PACK):
+        k = columns(c, held.shape[1])
+        fetches.append(pltpu.make_async_copy(tokens.at[:, k], held.at[:, k], sems.at[c]))
+        fetches[-1].start()
+    select = select_of(routes[0])
+    for fetch in fetches:
+        fetch.wait()
+    values = pick(select, whole_block(held))
     raw[...] = values.astype(BF16)
     normed[...] = (values * inv_rms_of(values)).astype(BF16)
     copy.wait()
 
 
 def other_rows_kernel(
-    tokens, cotangent, next_routes, prev_routes, _, __, ___, far, t1, cot, piece, sem
+    tokens, cotangent, next_routes, prev_routes, _, __, far, t1, cot, piece, sem
 ):
     copy = piece_copy(far, COT_PIECES[1], piece, sem)
     cot[...] = pick(select_of(prev_routes[0]), whole_block(cotangent)).astype(BF16)
@@ -207,10 +232,8 @@
 
 
 def grad1_kernel(n, *refs):
-    parts, (h, cot, tokens, upd, piece, sem) = refs[:n], refs[n:]
-    copy = piece_copy(tokens, TOK_PIECES[0], piece, sem)
+    parts, (h, cot, upd) = refs[:n], refs[n:]
     upd[...] = state_grad(parts, h[...], cot[...])
-    copy.wait()
 
 
 def enter0_kernel(m, upd1, next_routes, routes, gates, *refs):
@@ -253,21 +276,6 @@
     grad_gate = (grad_act * pre_up * sig * (1.0 + pre_gate * (1.0 - sig))).astype(BF16)
     grad_up = (grad_act * (pre_gate * sig)).astype(BF16)
     return grad_gate, grad_up
-
-
-def weight_copies(gate, up, down, gate_v, up_v, down_v, sems):
-    out = []
-    step = gate.shape[0] // PACK
-    for c in range(PACK):
-        r = pl.ds(c * step, step)
-        out.append(
-            (
-                pltpu.make_async_copy(gate.at[r], gate_v.at[r], sems.at[0, c]),
-                pltpu.make_async_copy(up.at[r], up_v.at[r], sems.at[1, c]),
-                pltpu.make_async_copy(down.at[:, r], down_v.at[:, r], sems.at[2, c]),
-            )
-        )
-    return out
 
 
 def gather_rows(blocks, first, unpacked, whole32, whole):
@@ -294,30 +302,22 @@
     blocks, (gate, up, down) = refs[:n], refs[n : n + 3]
     x, pre_gate, pre_up, act = refs[n + 3 : n + 7]
     parts = refs[n + 7 : 2 * n + 7]
-    gate_v, up_v, down_v, sems, unpacked, whole32, held = refs[2 * n + 7 :]
-    copies = weight_copies(gate, up, down, gate_v, up_v, down_v, sems)
-    for cg, cu, _ in copies:
-        cg.start()
-        cu.start()
-    for _, _, cd in copies:
-        cd.start()
+    unpacked, whole32, held = refs[2 * n + 7 :]
     gather_rows(blocks, 0, unpacked, whole32, x)
-    acc_g = jnp.zeros(pre_gate.shape, F32)
-    acc_u = jnp.zeros(pre_up.shape, F32)
-    width = gate.shape[0]
-    for c, (cg, cu, _) in enumerate(copies):
-        k = columns(c, width)
-        cg.wait()
-        acc_g = acc_g + dot(x[:, k], gate_v[k])
-        cu.wait()
-        acc_u = acc_u + dot(x[:, k], up_v[k])
+    acc_g = dot(x[...], gate[...])
+    acc_u = dot(x[...], up[...])
     pre_gate[...] = acc_g
     pre_up[...] = acc_u
     activated = (acc_g * jax.nn.sigmoid(acc_g) * acc_u).astype(BF16)
     act[...] = activated
-    for c, (_, _, cd) in enumerate(copies):
-        cd.wait()
-        spread_rows(dot(activated, down_v[:, columns(c, width)]), c, n, held.at[c], unpacked)
+    out_rows(activated, down, held, unpacked, parts)
+
+
+def out_rows(act, down, held, unpacked, parts):
+    n = len(parts)
+    for c in range(PACK):
+        value = dot(act, down[:, columns(c, down.shape[1])])
+        spread_rows(value, c, n, held.at[c], unpacked)
     for i, p in enumerate(parts):
         p[...] = unpacked[i].astype(BF16)
 
@@ -325,152 +325,130 @@
 def down_kernel(n, act, down, _, *refs):
     parts, (unpacked, held) = refs[:n], refs[n:]
     hidden, width = down.shape
+    out_rows(act[:, width + hidden :], down, held, unpacked, parts)
+
+
+def back_rows(gg, gu, gate, up, held, unpacked, parts):
+    n = len(parts)
     for c in range(PACK):
-        value = dot(act[:, 2 * width + hidden :], down[:, columns(c, width)])
+        k = columns(c, gate.shape[0])
+        value = dot(gg, gate[k], 1, 1) + dot(gu, up[k], 1, 1)
         spread_rows(value, c, n, held.at[c], unpacked)
     for i, p in enumerate(parts):
         p[...] = unpacked[i].astype(BF16)
 
 
-def back_rows(gg, gu, gate_v, up_v, held, unpacked, parts):
-    n = len(parts)
-    for c in range(PACK):
-        k = columns(c, gate_v.shape[0])
-        value = dot(gg, gate_v[k], 1, 1) + dot(gu, up_v[k], 1, 1)
-        spread_rows(value, c, n, held.at[c], unpacked)
-    for i, p in enumerate(parts):
-        p[...] = unpacked[i].astype(BF16)
-
-
 def tick1_kernel(n, *refs):
-    blocks, (x0, act0, gate, up, down, _) = refs[:n], refs[n : n + 6]
-    x_act, g_grad = refs[n + 6 : n + 8]
-    parts = refs[n + 8 : 2 * n + 8]
-    gate_v, up_v, down_v, sems, unpacked, whole32, held, x, g = refs[2 * n + 8 :]
-    copies = weight_copies(gate, up, down, gate_v, up_v, down_v, sems)
-    for three in copies:
-        for c in three:
-            c.start()
+    blocks, (act0, gate, up, down, tokens, _) = refs[:n], refs[n : n + 6]
+    x_act, g_grad, piece = refs[n + 6 : n + 9]
+    parts = refs[n + 9 : 2 * n + 9]
+    sem, unpacked, whole32, held, x, g = refs[2 * n + 9 :]
+    copy = piece_copy(tokens, TOK_PIECES[0], piece, sem)
     gather_rows(blocks, 0, unpacked, whole32.at[0], x)
     gather_rows(blocks, PACKED, unpacked, whole32.at[1], g)
     width, hidden = gate.shape
-    x_act[:, :width] = x0[...]
-    x_act[:, width : 2 * width] = x[...]
-    x_act[:, 2 * width : 2 * width + hidden] = act0[...]
+    x_act[:, :width] = x[...]
+    x_act[:, width : width + hidden] = act0[...]
     g_grad[:, :width] = g[...]
-    acc_g = jnp.zeros(act0.shape, F32)
-    acc_u = jnp.zeros(act0.shape, F32)
-    acc_a = jnp.zeros(act0.shape, F32)
-    for c, (cg, cu, cd) in enumerate(copies):
-        k = columns(c, width)
-        cg.wait()
-        acc_g = acc_g + dot(x[:, k], gate_v[k])
-        cu.wait()
-        acc_u = acc_u + dot(x[:, k], up_v[k])
-        cd.wait()
-        acc_a = acc_a + dot(g[:, k], down_v[:, k], 1, 1)
+    acc_g = dot(x[...], gate[...])
+    acc_u = dot(x[...], up[...])
+    acc_a = dot(g[...], down[...], 1, 1)
     gg, gu = silu_grads(acc_g, acc_u, acc_a)
-    x_act[:, 2 * width + hidden :] = (acc_g * jax.nn.sigmoid(acc_g) * acc_u).astype(BF16)
+    x_act[:, width + hidden :] = (acc_g * jax.nn.sigmoid(acc_g) * acc_u).astype(BF16)
     g_grad[:, width : width + hidden] = gg
     g_grad[:, width + hidden :] = gu
-    back_rows(gg, gu, gate_v, up_v, held, unpacked, parts)
+    back_rows(gg, gu, gate, up, held, unpacked, parts)
+    copy.wait()
+
+
+def gather0_kernel(n, *refs):
+    blocks, (g, unpacked, whole32) = refs[:n], refs[n:]
+    gather_rows(blocks, 0, unpacked, whole32, g)
 
 
 def tick0_kernel(n, *refs):
-    blocks, (pre_gate, pre_up, gate, up, down) = refs[:n], refs[n : n + 5]
-    (g_grad,) = refs[n + 5 : n + 6]
-    parts = refs[n + 6 : 2 * n + 6]
-    gate_v, up_v, down_v, sems, unpacked, whole32, held, g = refs[2 * n + 6 :]
-    copies = weight_copies(gate, up, down, gate_v, up_v, down_v, sems)
-    for _, _, cd in copies:
-        cd.start()
-    for cg, cu, _ in copies:
-        cg.start()
-        cu.start()
-    gather_rows(blocks, 0, unpacked, whole32, g)
-    width, hidden = gate.shape
-    g_grad[:, :width] = g[...]
-    acc_a = jnp.zeros(pre_gate.shape, F32)
-    for c, (_, _, cd) in enumerate(copies):
-        k = columns(c, width)
-        cd.wait()
-        acc_a = acc_a + dot(g[:, k], down_v[:, k], 1, 1)
+    g, pre_gate, pre_up, gate, up, down, small = refs[:7]
+    parts = refs[7 : n + 7]
+    unpacked, held = refs[n + 7 :]
+    hidden = gate.shape[1]
+    acc_a = dot(g[...], down[...], 1, 1)
     gg, gu = silu_grads(pre_gate[...], pre_up[...], acc_a)
-    g_grad[:, width : width + hidden] = gg
-    g_grad[:, width + hidden :] = gu
-    for cg, cu, _ in copies:
-        cg.wait()
-        cu.wait()
-    back_rows(gg, gu, gate_v, up_v, held, unpacked, parts)
+    small[:, :hidden] = gg
+    small[:, hidden:] = gu
+    back_rows(gg, gu, gate, up, held, unpacked, parts)
 
 
 def whole_of(blocks):
     return jnp.concatenate(blocks, axis=0)
 
 
-def input_grad_kernel(m, *refs):
-    x0, x1, gates0, ups0, gates1, ups1 = (refs[i * m : (i + 1) * m] for i in range(6))
-    gate_out, up_out = refs[6 * m :]
-    x_t = whole_of([b[...] for b in x0 + x1]).T
-    gate_out[...] = dot(x_t, whole_of([b[...] for b in gates0 + gates1])).astype(BF16)
-    up_out[...] = dot(x_t, whole_of([b[...] for b in ups0 + ups1])).astype(BF16)
-
-
-def down_grad_kernel(m, *refs):
-    g0, g1, act0, act1 = (refs[i * m : (i + 1) * m] for i in range(4))
-    (down_out,) = refs[4 * m :]
-    act = whole_of([b[...] for b in act0 + act1])
-    down_out[...] = dot(act, whole_of([b[...] for b in g0 + g1]), 0, 0).astype(BF16)
-
-
-def grads_call(kernel, wide, fixed, outs, out_block, out_index, hidden):
-    rows = wide[0][0].shape[0]
-    step = max(max(s) for s in outs) // PACK
-
-    def chunked(at):
-        return pl.BlockSpec((rows, step), lambda c: (0, at + c))
-
-    def constant(at):
-        return pl.BlockSpec((rows, hidden), lambda c: (0, at))
-
+def turn_kernel(m, *refs):
+    x0, x1, act0, act1 = (refs[i * m : (i + 1) * m] for i in range(4))
+    x_t, act_t = refs[4 * m :]
+    x_t[...] = whole_of([b[...] for b in x0 + x1]).T
+
+    @pl.when(pl.program_id(0) == 0)
+    def _():
+        act_t[...] = whole_of([b[...] for b in act0 + act1]).T
+
+
+def weight_grad_kernel(m, x_t, act_t, *refs):
+    g0, g1, small0, gates1, ups1 = (refs[i * m : (i + 1) * m] for i in range(5))
+    gate_out, up_out, down_out = refs[5 * m :]
+    hidden = gate_out.shape[1]
+    gg = whole_of([b[:, :hidden] for b in small0] + [b[...] for b in gates1])
+    gu = whole_of([b[:, hidden:] for b in small0] + [b[...] for b in ups1])
+    gate_out[...] = dot(x_t[...], gg).astype(BF16)
+    up_out[...] = dot(x_t[...], gu).astype(BF16)
+    down_out[...] = dot(act_t[...], whole_of([b[...] for b in g0 + g1])).astype(BF16)
+
+
+def chunked_call(kernel, ins, outs):
     return pl.pallas_call(
         kernel,
         grid=(PACK,),
-        out_shape=[jax.ShapeDtypeStruct(s, BF16) for s in outs],
-        in_specs=[chunked(at) for _, at in wide] + [constant(at) for _, at in fixed],
-        out_specs=[pl.BlockSpec(out_block, out_index)] * len(outs),
+        out_shape=[jax.ShapeDtypeStruct(s, BF16) for s, _, _ in outs],
+        in_specs=[pl.BlockSpec(block, index) for _, block, index in ins],
+        out_specs=[pl.BlockSpec(block, index) for _, block, index in outs],
         compiler_params=pltpu.CompilerParams(vmem_limit_bytes=VMEM_SMALL),
         cost_estimate=pl.CostEstimate(flops=0, bytes_accessed=COST_BYTES, transcendentals=0),
-    )(*(a for a, _ in wide), *(a for a, _ in fixed))
-
-
-def input_grads(x_act, g_grad0, g_grad1, width, hidden):
+    )(*(a for a, _, _ in ins))
+
+
+def constant(at):
+    return lambda c: (0, at)
+
+
+def chunk_at(at):
+    return lambda c: (0, at + c)
+
+
+def turned(x0, x_act, width, hidden):
+    m = len(x_act)
+    rows = x_act[0].shape[0]
+    step = width // PACK
     first = width // hidden
-    return grads_call(
-        functools.partial(input_grad_kernel, len(x_act)),
-        [(a, 0) for a in x_act] + [(a, PACK) for a in x_act],
-        [(a, first) for a in g_grad0]
-        + [(a, first + 1) for a in g_grad0]
-        + [(a, first) for a in g_grad1]
-        + [(a, first + 1) for a in g_grad1],
-        [(width, hidden)] * 2,
-        (width // PACK, hidden),
-        lambda c: (c, 0),
-        hidden,
-    )
-
-
-def down_grads(g_grad0, g_grad1, x_act, width, hidden):
-    first = 2 * width // hidden
-    return grads_call(
-        functools.partial(down_grad_kernel, len(g_grad0)),
-        [(a, 0) for a in g_grad0 + g_grad1],
-        [(a, first) for a in x_act] + [(a, first + 1) for a in x_act],
-        [(hidden, width)],
-        (hidden, width // PACK),
-        lambda c: (0, c),
-        hidden,
-    )
+    ins = [(a, (rows, step), chunk_at(0)) for a in x0 + x_act]
+    ins += [(a, (rows, hidden), constant(at)) for at in (first, first + 1) for a in x_act]
+    outs = [
+        ((width, 2 * m * rows), (step, 2 * m * rows), lambda c: (c, 0)),
+        ((hidden, 2 * m * rows), (hidden, 2 * m * rows), lambda c: (0, 0)),
+    ]
+    return chunked_call(functools.partial(turn_kernel, m), ins, outs)
+
+
+def weight_grads(x_t, act_t, g0, g_grad1, small0, width, hidden):
+    m = len(g0)
+    rows = g0[0].shape[0]
+    step = width // PACK
+    first = width // hidden
+    ins = [(x_t, (step, x_t.shape[1]), lambda c: (c, 0)), (act_t, act_t.shape, constant(0))]
+    ins += [(a, (rows, step), chunk_at(0)) for a in g0 + g_grad1]
+    ins += [(a, a.shape, constant(0)) for a in small0]
+    ins += [(a, (rows, hidden), constant(at)) for at in (first, first + 1) for a in g_grad1]
+    tall = ((width, hidden), (step, hidden), lambda c: (c, 0))
+    outs = [tall, tall, ((hidden, width), (hidden, step), chunk_at(0))]
+    return chunked_call(functools.partial(weight_grad_kernel, m), ins, outs)
 
 
 def from_group(block):
@@ -497,18 +475,12 @@
     gates = jnp.transpose(gates, (0, 2, 1))
     one = ((PACKED, step), BF16)
     part = functools.partial
-    scratch = [
-        pltpu.VMEM((width, hidden), BF16),
-        pltpu.VMEM((width, hidden), BF16),
-        pltpu.VMEM((hidden, width), BF16),
-        pltpu.SemaphoreType.DMA((3, PACK)),
-        pltpu.VMEM((n, PACKED, step), F32),
-        pltpu.VMEM((rows, width), F32),
-        pltpu.VMEM((PACK, rows, step), F32),
-    ]
-    both = pltpu.VMEM((rows, width), BF16)
-    tick1_scratch = [*scratch[:5], pltpu.VMEM((2, rows, width), F32), scratch[6], both, both]
+    unpacked = pltpu.VMEM((n, PACKED, step), F32)
+    flat32 = pltpu.VMEM((rows, width), F32)
+    held = pltpu.VMEM((PACK, rows, step), F32)
+    flat = pltpu.VMEM((rows, width), BF16)
     wide = ((rows, width + 2 * hidden), BF16)
+    dma = [pltpu.SemaphoreType.DMA]
 
     next_routes = shifted(routes[1:], "section", -1)
     prev_routes = shifted(routes[1:], "section", 1)
@@ -520,15 +492,23 @@
 
     cot_shapes = [shape_of(place) for place in COT_PIECES]
     tok_shapes = [shape_of(place) for place in TOK_PIECES]
-    dma = [pltpu.SemaphoreType.DMA]
 
     raw0, normed0, piece = call(
         first_rows_kernel,
         [one, one, cot_shapes[0]],
         [tokens, routes, cotangent],
-        any_args=(2,),
+        any_args=(0, 2),
         any_outs=(2,),
-        scratch=dma,
+        scratch=[*dma, pltpu.SemaphoreType.DMA((PACK,)), pltpu.VMEM(tokens.shape, BF16)],
+        vmem=VMEM_ALL,
+    )
+    gate, up, down = call(
+        load_kernel,
+        [pltpu.VMEM(a.shape, BF16) for a in (gate, up, down)],
+        [gate, up, down],
+        any_args=(0, 1, 2),
+        scratch=[pltpu.SemaphoreType.DMA((3, PACK))],
+        vmem=VMEM_LOAD,
     )
     cot_parts = [shifted(piece, "section", -2)]
     blocks = from_group(normed0)
@@ -538,19 +518,18 @@
         + [((rows, hidden), BF16)]
         + [one] * n,
         [*blocks, gate, up, down],
-        any_args=(n, n + 1, n + 2),
-        scratch=scratch,
-        vmem=VMEM_BIG,
+        scratch=[unpacked, flat32, held],
     )
     t1, cot1, piece = call(
         other_rows_kernel,
         [one, one, cot_shapes[1]],
-        [tokens, cotangent, next_routes, prev_routes, prev2_routes, act0, cot_parts[0], cotangent],
-        any_args=(4, 5, 6, 7),
+        [tokens, cotangent, next_routes, prev_routes, act0, cot_parts[0], cotangent],
+        any_args=(4, 5, 6),
         any_outs=(2,),
         scratch=dma,
     )
     cot1 = shifted(cot1, "section", -1)
+    x0_all = copies_of(x0)
     cot_parts.append(shifted(piece, "section", -2))
     parts = to_group(parts)
     upd0, h1, piece = call(
@@ -575,67 +554,61 @@
     )
     cot_parts.append(shifted(piece, "section", -2))
     blocks = from_group(enter1)
-    x_act, g_grad1, *parts = call(
+    x_act, g_grad1, piece, *parts = call(
         part(tick1_kernel, n),
-        [((rows, 2 * (width + hidden)), BF16), wide] + [one] * n,
-        [*blocks, x0, act0, gate, up, down, cot_parts[2]],
-        any_args=(n + 2, n + 3, n + 4, n + 5),
-        scratch=tick1_scratch,
-        vmem=VMEM_BIG,
-    )
+        [wide, wide, tok_shapes[0]] + [one] * n,
+        [*blocks, act0, gate, up, down, tokens, cot_parts[2]],
+        any_args=(n + 4, n + 5),
+        any_outs=(2,),
+        scratch=[*dma, unpacked, pltpu.VMEM((2, rows, width), F32), held, flat, flat],
+    )
+    tok_parts = [shifted(piece, "section", 2)]
     parts = to_group(parts)
-    upd1, piece = call(
-        part(grad1_kernel, n),
-        [one, tok_shapes[0]],
-        [*parts, h1, cot1, tokens],
-        any_args=(n + 2,),
-        any_outs=(1,),
-        scratch=dma,
-    )
-    upd1_here = upd1
+    (upd1,) = call(part(grad1_kernel, n), [one], [*parts, h1, cot1])
     upd1 = shifted(upd1, "section", -1)
-    tok_parts = [shifted(piece, "section", 2)]
-    outs = call(
-        part(down_kernel, n),
-        [one] * n,
-        [x_act, down, upd1_here],
-        any_args=(2,),
-        scratch=[scratch[4], scratch[6]],
-        vmem=VMEM_BIG,
-    )
     x_act_all, g_grad1_all = copies_of(x_act), copies_of(g_grad1)
 
     m = len(cot_parts)
     c0, enter0, piece = call(
         part(enter0_kernel, m),
         [one, one, tok_shapes[1]],
-        [upd1, next_routes, routes, gates, *cot_parts, tokens, outs[0]],
+        [upd1, next_routes, routes, gates, *cot_parts, tokens, tok_parts[0]],
         any_args=(m + 4, m + 5),
         any_outs=(2,),
         scratch=dma,
     )
     tok_parts.append(shifted(piece, "section", 2))
     blocks = from_group(enter0)
-    g_grad0, *parts = call(
+    (g0,) = call(
+        part(gather0_kernel, n), [((rows, width), BF16)], blocks, scratch=[unpacked, flat32]
+    )
+    g0_all = copies_of(g0)
+    small0, *parts = call(
         part(tick0_kernel, n),
-        [wide] + [one] * n,
-        [*blocks, pre_gate0, pre_up0, gate, up, down],
-        any_args=(n + 2, n + 3, n + 4),
-        scratch=scratch + [both],
-        vmem=VMEM_BIG,
+        [((rows, 2 * hidden), BF16)] + [one] * n,
+        [g0, pre_gate0, pre_up0, gate, up, down],
+        scratch=[unpacked, held],
     )
     parts = to_group(parts)
-    g_grad0_all = copies_of(g_grad0)
     (grad,) = call(
         part(finish_grad_kernel, n),
         [(tokens.shape, BF16)],
         [*parts, raw0, c0, routes, upd1, next_routes, *cot_parts],
     )
+    outs = call(
+        part(down_kernel, n),
+        [one] * n,
+        [x_act, down, small0],
+        any_args=(2,),
+        scratch=[unpacked, held],
+    )
     outs = to_group(outs)
     (last1,) = call(part(update1_kernel, n), [one], [*outs, h1, routes, gates])
     last1 = shifted(last1, "section", 1)
-    gate_out, up_out = input_grads(x_act_all, g_grad0_all, g_grad1_all, width, hidden)
-    (down_out,) = down_grads(g_grad0_all, g_grad1_all, x_act_all, width, hidden)
+    x_t, act_t = turned(x0_all, x_act_all, width, hidden)
+    gate_out, up_out, down_out = weight_grads(
+        x_t, act_t, g0_all, g_grad1_all, copies_of(small0), width, hidden
+    )
     (state,) = call(
         finish_state_kernel,
         [(tokens.shape, BF16)],

time: 175 us -> 163 us (0.931)
  starting transfers between devices: 77.8 us -> 52.4 us
  waiting for transfers between devices: 41.2 us -> 54.6 us
  local copies, waits for them, and re-layouts: 3.33 us -> 0.73 us
  Pallas kernels: 51.9 us -> 54.1 us
    ppermute x38 -> x40, starting transfers between devices: 77.8 us -> 52.4 us  [shifted(): lax.ppermute(block, axis, [((i - distance) % size, i) for i in range(size)])]
    ppermute x38 -> x40, waiting for transfers between devices: 41.2 us -> 54.6 us  [shifted(): lax.ppermute(block, axis, [((i - distance) % size, i) for i in range(size)])]
    pallas_call x13 -> x15, Pallas kernels: 38.4 us -> 43.1 us  [call(): pl.pallas_call(kernel, out_shape=outs, in_specs=[anywhere if i in any_arg...]
    unnamed x14 -> x12, local copies, waits for them, and re-layouts: 3.33 us -> 0.04 us
    pallas_call x2, Pallas kernels: 13.5 us -> 11 us  [chunked_call(): pl.pallas_call(kernel, grid=(PACK,), out_shape=[jax.ShapeDtypeStruct(s, B...]
  transfers between devices with their start and end apart: 38 -> 40, of which waited for: 17 -> 19; matrix products, arithmetic and copies ran while one was open for 0% -> 0% of each run, Pallas kernels for 27% -> 23%
where the time goes in v5:
time: 163 us
  waiting for transfers between devices  54.6 us (33%)
  Pallas kernels  54.1 us (33%)
  starting transfers between devices  52.4 us (32%)
    ppermute x40, waiting for transfers between devices, shifted(): lax.ppermute(block, axis, [((i - distance) % size, i) for i in range(size)])  54.6 us
    ppermute x40, starting transfers between devices, shifted(): lax.ppermute(block, axis, [((i - distance) % size, i) for i in range(size)])  52.4 us
    pallas_call x15, Pallas kernels, call(): pl.pallas_call(kernel, out_shape=outs, in_specs=[anywhere if i in any_arg...  43.1 us
    pallas_call x2, Pallas kernels, chunked_call(): pl.pallas_call(kernel, grid=(PACK,), out_shape=[jax.ShapeDtypeStruct(s, B...  11 us
  transfers between devices with their start and end apart: 40, of which 19 were waited for; matrix products, arithmetic and copies ran while one was open for 0% of the time, Pallas kernels for 23%

profile of v5, /device:TPU:0, one launch (start us, length us, event | category | flops | bytes accessed | tf_op | source)
XLA Modules:
  0.0 162.8 jit_solution(16650955117964878564)
XLA Ops:
  0.6 12.5 %shard_map.110 = (bf16[80,640]{1,0:T(8,128)(2,1)}, bf16[80,640]{1,0:T(8,128)(2,1)}, bf16[32,5120]{1,0:T(8,128)(2,1)}) custom-call(bf16[128,5120]{1,0:T(8,128)(2,1)} %refs_4_.1, s32[2,4,128]{2,1,0:T(4,128)} %bitcast.8, bf16[128,5120]{1,0:T(8,128)(2,1)} %cotangent.5), custom_call_target="tpu_custom_call" | custom-call | bytes 1024 | tf_op jit(solution)/shard_map/pallas_call | solution.py:39
  13.1 4.1 %collective-permute-start.8 = (bf16[32,5120]{1,0:T(8,128)(2,1)}, bf16[32,5120]{1,0:T(8,128)(2,1)S(1)}, u32[]{:S(2)}, u32[]{:S(2)}) collective-permute-start(bf16[32,5120]{1,0:T(8,128)(2,1)} %get-tuple-element.61), channel_id=1, source_target_pairs={{16,0},{24,8},{0,16},{8,24},{17,1},{25,9},{1,17},{9,25},{18,2},{26... | collective-permute-start | bytes 983048 | tf_op jit(solution)/shard_map/ppermute | solution.py:26
  17.2 1.6 collective-permute-start.1
  18.8 1.4 collective-permute-start.2
  20.2 0.7 fusion
  20.9 1.3 collective-permute-start.6
  22.2 1.4 collective-permute-start.7
  23.6 5.7 %shard_map.111 = (bf16[5120,512]{1,0:T(8,128)(2,1)S(1)}, bf16[5120,512]{1,0:T(8,128)(2,1)S(1)}, bf16[512,5120]{1,0:T(8,128)(2,1)S(1)}) custom-call(bf16[5120,512]{1,0:T(8,128)(2,1)} %bitcast.19, bf16[5120,512]{1,0:T(8,128)(2,1)} %bitcast.20, bf16[512,5120]{1,0:T(8,128)(2,1)} %bitcast.21), custom_call_target="tpu_custom_call" | custom-call | bytes 1024 | tf_op jit(solution)/shard_map/pallas_call | solution.py:39
  29.5 3.1 %shard_map.112 = (bf16[48,5120]{1,0:T(8,128)(2,1)S(1)}, f32[48,512]{1,0:T(8,128)S(1)}, f32[48,512]{1,0:T(8,128)S(1)}, bf16[48,512]{1,0:T(8,128)(2,1)S(1)}, bf16[...) custom-call(bf16[80,640]{1,0:T(8,128)(2,1)S(1)} %copy-done.4, ...), custom_call_target="tpu_custom_call" | custom-call | bytes 1024 | tf_op jit(solution)/shard_map/pallas_call | solution.py:39
  32.6 0.9 shard_map.113
  33.5 2.4 %collective-permute-start.11 = (bf16[32,5120]{1,0:T(8,128)(2,1)S(1)}, bf16[32,5120]{1,0:T(8,128)(2,1)S(1)}, u32[]{:S(2)}, u32[]{:S(2)}) collective-permute-start(bf16[32,5120]{1,0:T(8,128)(2,1)S(1)} %get-tuple-element.65), channel_id=1, source_target_pairs={{16,0},{24,8},{0,16},{8,24},{17,1},{25,9},{1,17},{9,25},{18,2},{26... | collective-permute-start | bytes 983048 | tf_op jit(solution)/shard_map/ppermute | solution.py:26
  35.9 0.6 collective-permute-start.3
  36.5 1.0 collective-permute-start.4
  37.6 1.7 %collective-permute-done.3.refs_1_ = bf16[80,640]{1,0:T(8,128)(2,1)S(1)} collective-permute-done((bf16[80,640]{1,0:T(8,128)(2,1)S(1)}, bf16[80,640]{1,0:T(8,128)(2,1)S(1)}, u32[]{:S(2)}, u32[]{:S(2)}) %collective-permute-start.3) | collective-permute-done | bytes 102432 | tf_op jit(solution)/shard_map/ppermute | solution.py:26
  39.3 4.0 %collective-permute-done.4.refs_2_ = bf16[80,640]{1,0:T(8,128)(2,1)S(1)} collective-permute-done((bf16[80,640]{1,0:T(8,128)(2,1)S(1)}, bf16[80,640]{1,0:T(8,128)(2,1)S(1)}, u32[]{:S(2)}, u32[]{:S(2)}) %collective-permute-start.4) | collective-permute-done | bytes 102432 | tf_op jit(solution)/shard_map/ppermute | solution.py:26
  43.3 0.5 shard_map.114
  43.9 1.5 collective-permute-start.9
  45.3 2.4 %collective-permute-start.10 = (bf16[80,640]{1,0:T(8,128)(2,1)S(1)}, bf16[80,640]{1,0:T(8,128)(2,1)S(1)}, u32[]{:S(2)}, u32[]{:S(2)}) collective-permute-start(bf16[80,640]{1,0:T(8,128)(2,1)S(1)} %get-tuple-element.64), channel_id=1, source_target_pairs={{8,0},{16,8},{24,16},{0,24},{9,1},{17,9},{25,17},{1,25},{10,2},{18... | collective-permute-start | bytes 307208 | tf_op jit(solution)/shard_map/ppermute | solution.py:26
  47.7 3.9 %collective-permute-done.9.h.refs_4_ = bf16[80,640]{1,0:T(8,128)(2,1)S(1)} collective-permute-done((bf16[80,640]{1,0:T(8,128)(2,1)S(1)}, bf16[80,640]{1,0:T(8,128)(2,1)S(1)}, u32[]{:S(2)}, u32[]{:S(2)}) %collective-permute-start.9) | collective-permute-done | bytes 102432 | tf_op jit(solution)/shard_map/ppermute | solution.py:26
  51.6 1.8 %collective-permute-done.10.cot.refs_5_ = bf16[80,640]{1,0:T(8,128)(2,1)S(1)} collective-permute-done((bf16[80,640]{1,0:T(8,128)(2,1)S(1)}, bf16[80,640]{1,0:T(8,128)(2,1)S(1)}, u32[]{:S(2)}, u32[]{:S(2)}) %collective-permute-start.10) | collective-permute-done | bytes 102432 | tf_op jit(solution)/shard_map/ppermute | solution.py:26
  53.5 5.8 %collective-permute-done.11._.refs_1_.refs_10_ = bf16[32,5120]{1,0:T(8,128)(2,1)S(1)} collective-permute-done((bf16[32,5120]{1,0:T(8,128)(2,1)S(1)}, bf16[32,5120]{1,0:T(8,128)(2,1)S(1)}, u32[]{:S(2)}, u32[]{:S(2)}) %collective-permute-start.11) | collective-permute-done | bytes 327712 | tf_op jit(solution)/shard_map/ppermute | solution.py:26
  59.8 1.6 collective-permute-start.13
  61.4 1.4 collective-permute-start.14
  62.8 3.6 %collective-permute-start.20 = (bf16[64,3200]{1,0:T(8,128)(2,1)S(1)}, bf16[64,3200]{1,0:T(8,128)(2,1)S(1)}, u32[]{:S(2)}, u32[]{:S(2)}) collective-permute-start(bf16[64,3200]{1,0:T(8,128)(2,1)S(1)} %get-tuple-element.72), channel_id=1, source_target_pairs={{16,0},{24,8},{0,16},{8,24},{17,1},{25,9},{1,17},{9,25},{18,2},{26... | collective-permute-start | bytes 1228808 | tf_op jit(solution)/shard_map/ppermute | solution.py:26
  66.6 1.2 collective-permute-done.13.refs_2_
  67.8 2.8 %collective-permute-done.14.refs_3_ = bf16[160,640]{1,0:T(8,128)(2,1)S(1)} collective-permute-done((bf16[160,640]{1,0:T(8,128)(2,1)S(1)}, bf16[160,640]{1,0:T(8,128)(2,1)S(1)}, u32[]{:S(2)}, u32[]{:S(2)}) %collective-permute-start.14) | collective-permute-done | bytes 204832 | tf_op jit(solution)/shard_map/ppermute | solution.py:26
  70.6 7.0 %shard_map.116 = (bf16[48,6144]{1,0:T(8,128)(2,1)S(1)}, bf16[48,6144]{1,0:T(8,128)(2,1)S(1)}, bf16[16,5120]{1,0:T(8,128)(2,1)S(1)}, bf16[80,640]{1,0:T(8,128)(2,...) custom-call(bf16[160,640]{1,0:T(8,128)(2,1)S(1)} %get-tuple-element.66.refs_0_, ...), custom_call_target="tpu_custom_call" | custom-call | bytes 1024 | tf_op jit(solution)/shard_map/pallas_call | solution.py:39
  77.7 2.3 %collective-permute-start.16 = (bf16[80,640]{1,0:T(8,128)(2,1)S(1)}, bf16[80,640]{1,0:T(8,128)(2,1)S(1)}, u32[]{:S(2)}, u32[]{:S(2)}) collective-permute-start(bf16[80,640]{1,0:T(8,128)(2,1)S(1)} %get-tuple-element.69), channel_id=1, source_target_pairs={{2,0},{4,2},{6,4},{0,6},{3,1},{5,3},{7,5},{1,7},{10,8},{12,10},{14... | collective-permute-start | bytes 307208 | tf_op jit(solution)/shard_map/ppermute | solution.py:26
  80.1 3.9 %collective-permute-start.21 = (bf16[16,5120]{1,0:T(8,128)(2,1)S(1)}, bf16[16,5120]{1,0:T(8,128)(2,1)S(1)}, u32[]{:S(2)}, u32[]{:S(2)}) collective-permute-start(bf16[16,5120]{1,0:T(8,128)(2,1)S(1)} %get-tuple-element.73), channel_id=1, source_target_pairs={{16,0},{24,8},{0,16},{8,24},{17,1},{25,9},{1,17},{9,25},{18,2},{26... | collective-permute-start | bytes 491528 | tf_op jit(solution)/shard_map/ppermute | solution.py:26
  84.1 1.6 collective-permute-done.17.refs_2_
  85.6 0.4 shard_map.117
  86.1 2.6 %collective-permute-start.19 = (bf16[80,640]{1,0:T(8,128)(2,1)S(1)}, bf16[80,640]{1,0:T(8,128)(2,1)S(1)}, u32[]{:S(2)}, u32[]{:S(2)}) collective-permute-start(bf16[80,640]{1,0:T(8,128)(2,1)S(1)} %shard_map.117), channel_id=1, source_target_pairs={{8,0},{16,8},{24,16},{0,24},{9,1},{17,9},{25,17},{1,25},{10,2},{18... | collective-permute-start | bytes 307208 | tf_op jit(solution)/shard_map/ppermute | solution.py:26
  88.7 3.1 %collective-permute-done.21.refs_5_.first = bf16[16,5120]{1,0:T(8,128)(2,1)S(1)} collective-permute-done((bf16[16,5120]{1,0:T(8,128)(2,1)S(1)}, bf16[16,5120]{1,0:T(8,128)(2,1)S(1)}, u32[]{:S(2)}, u32[]{:S(2)}) %collective-permute-start.21) | collective-permute-done | bytes 163872 | tf_op jit(solution)/shard_map/ppermute | solution.py:26
  91.8 1.9 %collective-permute-done.19.upd1.refs_7_ = bf16[80,640]{1,0:T(8,128)(2,1)S(1)} collective-permute-done((bf16[80,640]{1,0:T(8,128)(2,1)S(1)}, bf16[80,640]{1,0:T(8,128)(2,1)S(1)}, u32[]{:S(2)}, u32[]{:S(2)}) %collective-permute-start.19) | collective-permute-done | bytes 102432 | tf_op jit(solution)/shard_map/ppermute | solution.py:26
  93.7 1.5 shard_map.118
  95.2 1.0 collective-permute-start.28
  96.2 1.5 collective-permute-start.35
  97.7 1.5 collective-permute-start.23
  99.3 1.4 collective-permute-start.24
  100.7 1.6 %collective-permute-done.22.refs_1_ = bf16[80,640]{1,0:T(8,128)(2,1)S(1)} collective-permute-done((bf16[80,640]{1,0:T(8,128)(2,1)S(1)}, bf16[80,640]{1,0:T(8,128)(2,1)S(1)}, u32[]{:S(2)}, u32[]{:S(2)}) %collective-permute-start.22) | collective-permute-done | bytes 102432 | tf_op jit(solution)/shard_map/ppermute | solution.py:26
  102.3 0.5 collective-permute-start.36
  102.9 0.6 collective-permute-done.23.refs_2_
  103.4 0.7 collective-permute-done.24.refs_3_
  104.3 4.9 %shard_map.120 = (bf16[48,1024]{1,0:T(8,128)(2,1)S(1)}, bf16[80,640]{1,0:T(8,128)(2,1)S(1)}, bf16[80,640]{1,0:T(8,128)(2,1)S(1)}, bf16[80,640]{1,0:T(8,128)(2,1)S(1)}, bf16[80,640]{1,0:T(8,128)(2,1)S(1)}) custom-call(bf16[48,5120]{1,0:T(8,128)(2,1)S(1)} %shard_map.119.refs_0_, f32[48,512]{1,0:T(8,128)S(1)} %get-tuple-element.75.refs_1_, ...), custom_call_target="tpu_custom_call" | custom-call | bytes 1024 | tf_op jit(solution)/shard_map/pallas_call | solution.py:39
  109.2 0.6 collective-permute-start.39
  109.8 1.9 %collective-permute-start.25 = (bf16[80,640]{1,0:T(8,128)(2,1)S(1)}, bf16[80,640]{1,0:T(8,128)(2,1)S(1)}, u32[]{:S(2)}, u32[]{:S(2)}) collective-permute-start(bf16[80,640]{1,0:T(8,128)(2,1)S(1)} %get-tuple-element.78), channel_id=1, source_target_pairs={{2,0},{4,2},{6,4},{0,6},{3,1},{5,3},{7,5},{1,7},{10,8},{12,10},{14... | collective-permute-start | bytes 307208 | tf_op jit(solution)/shard_map/ppermute | solution.py:26
  111.8 0.5 collective-permute-start.26
  112.3 11.4 %collective-permute-done.39.refs_5_ = bf16[48,1024]{1,0:T(8,128)(2,1)S(1)} collective-permute-done((bf16[48,1024]{1,0:T(8,128)(2,1)S(1)}, bf16[48,1024]{1,0:T(8,128)(2,1)S(1)}, u32[]{:S(2)}, u32[]{:S(2)}) %collective-permute-start.39) | collective-permute-done | bytes 98336 | tf_op jit(solution)/shard_map/ppermute | solution.py:26
  123.7 1.5 collective-permute-start.38
  125.2 1.1 shard_map.122
  126.3 0.6 collective-permute-start.37
  127.0 1.6 collective-permute-done.31.refs_1_
  128.6 1.4 collective-permute-start.32
  129.9 3.5 %collective-permute-done.32.refs_2_ = bf16[80,640]{1,0:T(8,128)(2,1)S(1)} collective-permute-done((bf16[80,640]{1,0:T(8,128)(2,1)S(1)}, bf16[80,640]{1,0:T(8,128)(2,1)S(1)}, u32[]{:S(2)}, u32[]{:S(2)}) %collective-permute-start.32) | collective-permute-done | bytes 102432 | tf_op jit(solution)/shard_map/ppermute | solution.py:26
  133.4 1.0 collective-permute-start.33
  134.4 3.3 %collective-permute-done.33.refs_3_ = bf16[80,640]{1,0:T(8,128)(2,1)S(1)} collective-permute-done((bf16[80,640]{1,0:T(8,128)(2,1)S(1)}, bf16[80,640]{1,0:T(8,128)(2,1)S(1)}, u32[]{:S(2)}, u32[]{:S(2)}) %collective-permute-start.33) | collective-permute-done | bytes 102432 | tf_op jit(solution)/shard_map/ppermute | solution.py:26
  138.0 3.8 %collective-permute-done.27.refs_3_ = bf16[80,640]{1,0:T(8,128)(2,1)S(1)} collective-permute-done((bf16[80,640]{1,0:T(8,128)(2,1)S(1)}, bf16[80,640]{1,0:T(8,128)(2,1)S(1)}, u32[]{:S(2)}, u32[]{:S(2)}) %collective-permute-start.27) | collective-permute-done | bytes 102432 | tf_op jit(solution)/shard_map/ppermute | solution.py:26
  141.9 1.4 collective-permute-start.29
  143.2 2.4 %collective-permute-start.34 = (bf16[80,640]{1,0:T(8,128)(2,1)S(1)}, bf16[80,640]{1,0:T(8,128)(2,1)S(1)}, u32[]{:S(2)}, u32[]{:S(2)}) collective-permute-start(bf16[80,640]{1,0:T(8,128)(2,1)S(1)} %shard_map.123), channel_id=1, source_target_pairs={{24,0},{0,8},{8,16},{16,24},{25,1},{1,9},{9,17},{17,25},{26,2},{2,... | collective-permute-start | bytes 307208 | tf_op jit(solution)/shard_map/ppermute | solution.py:26
  145.6 1.5 collective-permute-start.30
  147.1 2.4 %shard_map.121 = bf16[128,5120]{1,0:T(8,128)(2,1)} custom-call(bf16[80,640]{1,0:T(8,128)(2,1)S(1)} %get-tuple-element.77.refs_0_, bf16[80,640]{1,0:T(8,128)(2,1)S(1)} %collective-permute-done.25.refs_1_, bf16[80,640]{1,0:T(8,128)(2,1)S(1)} %collective-permute-done.26.refs_2_, bf16[80,640]{1,0:T(8,128)(2,1)S(1)} %collective-permute-done.27.refs_3_, ...), custom_call_target="tpu_custom_call" | custom-call | bytes 1024 | tf_op jit(solution)/shard_map/pallas_call | solution.py:39
  149.5 2.4 %shard_map.125 = (bf16[5120,192]{1,0:T(8,128)(2,1)S(1)}, bf16[512,192]{1,0:T(8,128)(2,1)S(1)}) custom-call(bf16[48,5120]{1,0:T(8,128)(2,1)S(1)} %get-tuple-element.90.refs_0_, bf16[48,5120]{1,0:T(8,128)(2,1)S(1)} %collective-permute-done.35.refs_1_, bf16[48,6144]{1,0:T(8,128)(2,1)S(1)} %get-tuple-element.84.act.refs_2_.refs_4_.refs_6_, ...), custom_call_target="tpu_custom_call" | custom-call | bytes 1024 | tf_op jit(solution)/shard_map/pallas_call | solution.py:407
  151.9 8.6 %shard_map.126 = (bf16[5120,512]{1,0:T(8,128)(2,1)}, bf16[5120,512]{1,0:T(8,128)(2,1)}, bf16[512,5120]{1,0:T(8,128)(2,1)}) custom-call(bf16[5120,192]{1,0:T(8,128)(2,1)S(1)} %get-tuple-element.91.x_t, bf16[512,192]{1,0:T(8,128)(2,1)S(1)} %get-tuple-element.92.act_t, bf16[48,5120]{1,0:T(8,128)(2,1)S(1)} %shard_map.119.refs_0_, ...), custom_call_target="tpu_custom_call" | custom-call | bytes 1024 | tf_op jit(solution)/shard_map/pallas_call | solution.py:407
  160.6 2.2 %shard_map.124 = bf16[128,5120]{1,0:T(8,128)(2,1)} custom-call(bf16[16,5120]{1,0:T(8,128)(2,1)S(1)} %collective-permute-done.21.refs_5_.first, bf16[112,5120]{1,0:T(8,128)(2,1)S(1)} %collective-permute-done.28.rest, bf16[80,640]{1,0:T(8,128)(2,1)S(1)} %collective-permute-done.29.upd0, s32[1,4,128]{2,1,0:T(4,128)S(1)} %collective-permute-done.30.prev2_routes, ...), custom_call_target="tpu_custom_call" | custom-call | bytes 1024 | tf_op jit(solution)/shard_map/pallas_call | solution.py:39
  (46 shorter events, 1.7 us)
Async XLA Ops:
  13.1 19.4 %collective-permute-start.8 = (bf16[32,5120]{1,0:T(8,128)(2,1)}, bf16[32,5120]{1,0:T(8,128)(2,1)S(1)}, u32[]{:S(2)}, u32[]{:S(2)}) collective-permute-start(bf16[32,5120]{1,0:T(8,128)(2,1)} %get-tuple-element.61), channel_id=1, source_target_pairs={{16,0},{24,8},{0,16},{8,24},{17,1},{25,9},{1,17},{9,25},{18,2},{26... | collective-permute-start | bytes 983048 | tf_op jit(solution)/shard_map/ppermute | solution.py:26
  17.2 5.0 %collective-permute-start = (bf16[80,640]{1,0:T(8,128)(2,1)}, bf16[80,640]{1,0:T(8,128)(2,1)S(1)}, u32[]{:S(2)}, u32[]{:S(2)}) collective-permute-start(bf16[80,640]{1,0:T(8,128)(2,1)} %get-tuple-element.51.refs_0_), channel_id=1, source_target_pairs={{6,0},{0,2},{2,4},{4,6},{7,1},{1,3},{3,5},{5,7},{14,8},{8,10},{10,... | collective-permute-start | bytes 307208 | tf_op jit(solution)/shard_map/ppermute | solution.py:26
  17.2 12.2 %collective-permute-start.1 = (bf16[80,640]{1,0:T(8,128)(2,1)}, bf16[80,640]{1,0:T(8,128)(2,1)S(1)}, u32[]{:S(2)}, u32[]{:S(2)}) collective-permute-start(bf16[80,640]{1,0:T(8,128)(2,1)} %get-tuple-element.51.refs_0_), channel_id=1, source_target_pairs={{4,0},{6,2},{0,4},{2,6},{5,1},{7,3},{1,5},{3,7},{12,8},{14,10},{8,... | collective-permute-start | bytes 307208 | tf_op jit(solution)/shard_map/ppermute | solution.py:26
  18.8 10.6 %collective-permute-start.2 = (bf16[80,640]{1,0:T(8,128)(2,1)}, bf16[80,640]{1,0:T(8,128)(2,1)S(1)}, u32[]{:S(2)}, u32[]{:S(2)}) collective-permute-start(bf16[80,640]{1,0:T(8,128)(2,1)} %get-tuple-element.51.refs_0_), channel_id=1, source_target_pairs={{2,0},{4,2},{6,4},{0,6},{3,1},{5,3},{7,5},{1,7},{10,8},{12,10},{14... | collective-permute-start | bytes 307208 | tf_op jit(solution)/shard_map/ppermute | solution.py:26
  20.9 11.6 %collective-permute-start.6 = (s32[1,4,128]{2,1,0:T(4,128)S(1)}, s32[1,4,128]{2,1,0:T(4,128)S(1)}, u32[]{:S(2)}, u32[]{:S(2)}) collective-permute-start(s32[1,4,128]{2,1,0:T(4,128)S(1)} %get-tuple-element.98), channel_id=1, source_target_pairs={{8,0},{16,8},{24,16},{0,24},{9,1},{17,9},{25,17},{1,25},{10,2},{18... | collective-permute-start | bytes 6152 | tf_op jit(solution)/shard_map/ppermute | solution.py:26
  22.2 10.3 %collective-permute-start.7 = (s32[1,4,128]{2,1,0:T(4,128)S(1)}, s32[1,4,128]{2,1,0:T(4,128)S(1)}, u32[]{:S(2)}, u32[]{:S(2)}) collective-permute-start(s32[1,4,128]{2,1,0:T(4,128)S(1)} %get-tuple-element.98), channel_id=1, source_target_pairs={{24,0},{0,8},{8,16},{16,24},{25,1},{1,9},{9,17},{17,25},{26,2},{2,... | collective-permute-start | bytes 6152 | tf_op jit(solution)/shard_map/ppermute | solution.py:26
  23.6 5.8 %copy-start.4 = (bf16[80,640]{1,0:T(8,128)(2,1)S(1)}, bf16[80,640]{1,0:T(8,128)(2,1)}, u32[]{:S(2)}) copy-start(bf16[80,640]{1,0:T(8,128)(2,1)} %get-tuple-element.51.refs_0_) | copy-start | bytes 307204
  29.4 3.2 %copy-start = (bf16[128,5120]{1,0:T(8,128)(2,1)S(1)}, bf16[128,5120]{1,0:T(8,128)(2,1)}, u32[]{:S(2)}) copy-start(bf16[128,5120]{1,0:T(8,128)(2,1)} %cotangent.5) | copy-start | bytes 3932164
  29.4 3.2 %copy-start.1 = (bf16[128,5120]{1,0:T(8,128)(2,1)S(1)}, bf16[128,5120]{1,0:T(8,128)(2,1)}, u32[]{:S(2)}) copy-start(bf16[128,5120]{1,0:T(8,128)(2,1)} %refs_4_.1) | copy-start | bytes 3932164
  29.4 13.9 %copy-start.2 = (bf16[80,640]{1,0:T(8,128)(2,1)S(1)}, bf16[80,640]{1,0:T(8,128)(2,1)}, u32[]{:S(2)}) copy-start(bf16[80,640]{1,0:T(8,128)(2,1)} %get-tuple-element.59.refs_4_) | copy-start | bytes 307204
  29.4 13.9 %copy-start.3 = (s32[2,128,4]{1,2,0:T(4,128)S(1)}, s32[2,128,4]{1,2,0:T(4,128)}, u32[]{:S(2)}) copy-start(s32[2,128,4]{1,2,0:T(4,128)} %param.12) | copy-start | bytes 12292
  29.5 13.9 %copy-start.5 = (f32[2,128,4]{1,2,0:T(4,128)S(1)}, f32[2,128,4]{1,2,0:T(4,128)}, u32[]{:S(2)}) copy-start(f32[2,128,4]{1,2,0:T(4,128)} %param.13) | copy-start | bytes 12292
  33.5 25.8 %collective-permute-start.11 = (bf16[32,5120]{1,0:T(8,128)(2,1)S(1)}, bf16[32,5120]{1,0:T(8,128)(2,1)S(1)}, u32[]{:S(2)}, u32[]{:S(2)}) collective-permute-start(bf16[32,5120]{1,0:T(8,128)(2,1)S(1)} %get-tuple-element.65), channel_id=1, source_target_pairs={{16,0},{24,8},{0,16},{8,24},{17,1},{25,9},{1,17},{9,25},{18,2},{26... | collective-permute-start | bytes 983048 | tf_op jit(solution)/shard_map/ppermute | solution.py:26
  35.9 3.4 %collective-permute-start.3 = (bf16[80,640]{1,0:T(8,128)(2,1)S(1)}, bf16[80,640]{1,0:T(8,128)(2,1)S(1)}, u32[]{:S(2)}, u32[]{:S(2)}) collective-permute-start(bf16[80,640]{1,0:T(8,128)(2,1)S(1)} %get-tuple-element.56), channel_id=1, source_target_pairs={{2,0},{4,2},{6,4},{0,6},{3,1},{5,3},{7,5},{1,7},{10,8},{12,10},{14... | collective-permute-start | bytes 307208 | tf_op jit(solution)/shard_map/ppermute | solution.py:26
  36.5 6.8 %collective-permute-start.4 = (bf16[80,640]{1,0:T(8,128)(2,1)S(1)}, bf16[80,640]{1,0:T(8,128)(2,1)S(1)}, u32[]{:S(2)}, u32[]{:S(2)}) collective-permute-start(bf16[80,640]{1,0:T(8,128)(2,1)S(1)} %get-tuple-element.57), channel_id=1, source_target_pairs={{4,0},{6,2},{0,4},{2,6},{5,1},{7,3},{1,5},{3,7},{12,8},{14,10},{8,... | collective-permute-start | bytes 307208 | tf_op jit(solution)/shard_map/ppermute | solution.py:26
  37.4 5.9 %collective-permute-start.5 = (bf16[80,640]{1,0:T(8,128)(2,1)S(1)}, bf16[80,640]{1,0:T(8,128)(2,1)S(1)}, u32[]{:S(2)}, u32[]{:S(2)}) collective-permute-start(bf16[80,640]{1,0:T(8,128)(2,1)S(1)} %get-tuple-element.58), channel_id=1, source_target_pairs={{6,0},{0,2},{2,4},{4,6},{7,1},{1,3},{3,5},{5,7},{14,8},{8,10},{10,... | collective-permute-start | bytes 307208 | tf_op jit(solution)/shard_map/ppermute | solution.py:26
  43.9 7.8 %collective-permute-start.9 = (bf16[80,640]{1,0:T(8,128)(2,1)S(1)}, bf16[80,640]{1,0:T(8,128)(2,1)S(1)}, u32[]{:S(2)}, u32[]{:S(2)}) collective-permute-start(bf16[80,640]{1,0:T(8,128)(2,1)S(1)} %get-tuple-element.63), channel_id=1, source_target_pairs={{24,0},{0,8},{8,16},{16,24},{25,1},{1,9},{9,17},{17,25},{26,2},{2,... | collective-permute-start | bytes 307208 | tf_op jit(solution)/shard_map/ppermute | solution.py:26
  45.3 8.1 %collective-permute-start.10 = (bf16[80,640]{1,0:T(8,128)(2,1)S(1)}, bf16[80,640]{1,0:T(8,128)(2,1)S(1)}, u32[]{:S(2)}, u32[]{:S(2)}) collective-permute-start(bf16[80,640]{1,0:T(8,128)(2,1)S(1)} %get-tuple-element.64), channel_id=1, source_target_pairs={{8,0},{16,8},{24,16},{0,24},{9,1},{17,9},{25,17},{1,25},{10,2},{18... | collective-permute-start | bytes 307208 | tf_op jit(solution)/shard_map/ppermute | solution.py:26
  47.7 18.7 %collective-permute-start.15 = (bf16[64,1920]{1,0:T(8,128)(2,1)S(1)}, bf16[64,1920]{1,0:T(8,128)(2,1)S(1)}, u32[]{:S(2)}, u32[]{:S(2)}) collective-permute-start(bf16[64,1920]{1,0:T(8,128)(2,1)S(1)} %get-tuple-element.67), channel_id=1, source_target_pairs={{16,0},{24,8},{0,16},{8,24},{17,1},{25,9},{1,17},{9,25},{18,2},{26... | collective-permute-start | bytes 737288 | tf_op jit(solution)/shard_map/ppermute | solution.py:26
  59.8 6.8 %collective-permute-start.12 = (bf16[160,640]{1,0:T(8,128)(2,1)S(1)}, bf16[160,640]{1,0:T(8,128)(2,1)S(1)}, u32[]{:S(2)}, u32[]{:S(2)}) collective-permute-start(bf16[160,640]{1,0:T(8,128)(2,1)S(1)} %get-tuple-element.66.refs_0_), channel_id=1, source_target_pairs={{6,0},{0,2},{2,4},{4,6},{7,1},{1,3},{3,5},{5,7},{14,8},{8,10},{10,... | collective-permute-start | bytes 614408 | tf_op jit(solution)/shard_map/ppermute | solution.py:26
  59.8 8.0 %collective-permute-start.13 = (bf16[160,640]{1,0:T(8,128)(2,1)S(1)}, bf16[160,640]{1,0:T(8,128)(2,1)S(1)}, u32[]{:S(2)}, u32[]{:S(2)}) collective-permute-start(bf16[160,640]{1,0:T(8,128)(2,1)S(1)} %get-tuple-element.66.refs_0_), channel_id=1, source_target_pairs={{4,0},{6,2},{0,4},{2,6},{5,1},{7,3},{1,5},{3,7},{12,8},{14,10},{8,... | collective-permute-start | bytes 614408 | tf_op jit(solution)/shard_map/ppermute | solution.py:26
  61.4 9.2 %collective-permute-start.14 = (bf16[160,640]{1,0:T(8,128)(2,1)S(1)}, bf16[160,640]{1,0:T(8,128)(2,1)S(1)}, u32[]{:S(2)}, u32[]{:S(2)}) collective-permute-start(bf16[160,640]{1,0:T(8,128)(2,1)S(1)} %get-tuple-element.66.refs_0_), channel_id=1, source_target_pairs={{2,0},{4,2},{6,4},{0,6},{3,1},{5,3},{7,5},{1,7},{10,8},{12,10},{14... | collective-permute-start | bytes 614408 | tf_op jit(solution)/shard_map/ppermute | solution.py:26
  62.8 30.9 %collective-permute-start.20 = (bf16[64,3200]{1,0:T(8,128)(2,1)S(1)}, bf16[64,3200]{1,0:T(8,128)(2,1)S(1)}, u32[]{:S(2)}, u32[]{:S(2)}) collective-permute-start(bf16[64,3200]{1,0:T(8,128)(2,1)S(1)} %get-tuple-element.72), channel_id=1, source_target_pairs={{16,0},{24,8},{0,16},{8,24},{17,1},{25,9},{1,17},{9,25},{18,2},{26... | collective-permute-start | bytes 1228808 | tf_op jit(solution)/shard_map/ppermute | solution.py:26
  77.7 6.4 %collective-permute-start.16 = (bf16[80,640]{1,0:T(8,128)(2,1)S(1)}, bf16[80,640]{1,0:T(8,128)(2,1)S(1)}, u32[]{:S(2)}, u32[]{:S(2)}) collective-permute-start(bf16[80,640]{1,0:T(8,128)(2,1)S(1)} %get-tuple-element.69), channel_id=1, source_target_pairs={{2,0},{4,2},{6,4},{0,6},{3,1},{5,3},{7,5},{1,7},{10,8},{12,10},{14... | collective-permute-start | bytes 307208 | tf_op jit(solution)/shard_map/ppermute | solution.py:26
  79.9 5.7 %collective-permute-start.17 = (bf16[80,640]{1,0:T(8,128)(2,1)S(1)}, bf16[80,640]{1,0:T(8,128)(2,1)S(1)}, u32[]{:S(2)}, u32[]{:S(2)}) collective-permute-start(bf16[80,640]{1,0:T(8,128)(2,1)S(1)} %get-tuple-element.70), channel_id=1, source_target_pairs={{4,0},{6,2},{0,4},{2,6},{5,1},{7,3},{1,5},{3,7},{12,8},{14,10},{8,... | collective-permute-start | bytes 307208 | tf_op jit(solution)/shard_map/ppermute | solution.py:26
  80.1 5.5 %collective-permute-start.18 = (bf16[80,640]{1,0:T(8,128)(2,1)S(1)}, bf16[80,640]{1,0:T(8,128)(2,1)S(1)}, u32[]{:S(2)}, u32[]{:S(2)}) collective-permute-start(bf16[80,640]{1,0:T(8,128)(2,1)S(1)} %get-tuple-element.71), channel_id=1, source_target_pairs={{6,0},{0,2},{2,4},{4,6},{7,1},{1,3},{3,5},{5,7},{14,8},{8,10},{10,... | collective-permute-start | bytes 307208 | tf_op jit(solution)/shard_map/ppermute | solution.py:26
  80.1 11.7 %collective-permute-start.21 = (bf16[16,5120]{1,0:T(8,128)(2,1)S(1)}, bf16[16,5120]{1,0:T(8,128)(2,1)S(1)}, u32[]{:S(2)}, u32[]{:S(2)}) collective-permute-start(bf16[16,5120]{1,0:T(8,128)(2,1)S(1)} %get-tuple-element.73), channel_id=1, source_target_pairs={{16,0},{24,8},{0,16},{8,24},{17,1},{25,9},{1,17},{9,25},{18,2},{26... | collective-permute-start | bytes 491528 | tf_op jit(solution)/shard_map/ppermute | solution.py:26
  86.1 7.6 %collective-permute-start.19 = (bf16[80,640]{1,0:T(8,128)(2,1)S(1)}, bf16[80,640]{1,0:T(8,128)(2,1)S(1)}, u32[]{:S(2)}, u32[]{:S(2)}) collective-permute-start(bf16[80,640]{1,0:T(8,128)(2,1)S(1)} %shard_map.117), channel_id=1, source_target_pairs={{8,0},{16,8},{24,16},{0,24},{9,1},{17,9},{25,17},{1,25},{10,2},{18... | collective-permute-start | bytes 307208 | tf_op jit(solution)/shard_map/ppermute | solution.py:26
  95.2 65.4 %collective-permute-start.28 = (bf16[112,5120]{1,0:T(8,128)(2,1)S(1)}, bf16[112,5120]{1,0:T(8,128)(2,1)S(1)}, u32[]{:S(2)}, u32[]{:S(2)}) collective-permute-start(bf16[112,5120]{1,0:T(8,128)(2,1)S(1)} %get-tuple-element.82), channel_id=1, source_target_pairs={{16,0},{24,8},{0,16},{8,24},{17,1},{25,9},{1,17},{9,25},{18,2},{26... | collective-permute-start | bytes 3440648 | tf_op jit(solution)/shard_map/ppermute | solution.py:26
  96.2 15.5 %collective-permute-start.35 = (bf16[48,5120]{1,0:T(8,128)(2,1)S(1)}, bf16[48,5120]{1,0:T(8,128)(2,1)S(1)}, u32[]{:S(2)}, u32[]{:S(2)}) collective-permute-start(bf16[48,5120]{1,0:T(8,128)(2,1)S(1)} %get-tuple-element.90.refs_0_), channel_id=1, source_target_pairs={{1,0},{0,1},{3,2},{2,3},{5,4},{4,5},{7,6},{6,7},{9,8},{8,9},{11,10... | collective-permute-start | bytes 1474568 | tf_op jit(solution)/shard_map/ppermute | solution.py:26
  97.7 4.6 %collective-permute-start.22 = (bf16[80,640]{1,0:T(8,128)(2,1)S(1)}, bf16[80,640]{1,0:T(8,128)(2,1)S(1)}, u32[]{:S(2)}, u32[]{:S(2)}) collective-permute-start(bf16[80,640]{1,0:T(8,128)(2,1)S(1)} %get-tuple-element.74.refs_0_), channel_id=1, source_target_pairs={{6,0},{0,2},{2,4},{4,6},{7,1},{1,3},{3,5},{5,7},{14,8},{8,10},{10,... | collective-permute-start | bytes 307208 | tf_op jit(solution)/shard_map/ppermute | solution.py:26
  97.7 5.7 %collective-permute-start.23 = (bf16[80,640]{1,0:T(8,128)(2,1)S(1)}, bf16[80,640]{1,0:T(8,128)(2,1)S(1)}, u32[]{:S(2)}, u32[]{:S(2)}) collective-permute-start(bf16[80,640]{1,0:T(8,128)(2,1)S(1)} %get-tuple-element.74.refs_0_), channel_id=1, source_target_pairs={{4,0},{6,2},{0,4},{2,6},{5,1},{7,3},{1,5},{3,7},{12,8},{14,10},{8,... | collective-permute-start | bytes 307208 | tf_op jit(solution)/shard_map/ppermute | solution.py:26
  99.3 4.9 %collective-permute-start.24 = (bf16[80,640]{1,0:T(8,128)(2,1)S(1)}, bf16[80,640]{1,0:T(8,128)(2,1)S(1)}, u32[]{:S(2)}, u32[]{:S(2)}) collective-permute-start(bf16[80,640]{1,0:T(8,128)(2,1)S(1)} %get-tuple-element.74.refs_0_), channel_id=1, source_target_pairs={{2,0},{4,2},{6,4},{0,6},{3,1},{5,3},{7,5},{1,7},{10,8},{12,10},{14... | collective-permute-start | bytes 307208 | tf_op jit(solution)/shard_map/ppermute | solution.py:26
  102.3 40.9 %collective-permute-start.36 = (bf16[48,6144]{1,0:T(8,128)(2,1)S(1)}, bf16[48,6144]{1,0:T(8,128)(2,1)S(1)}, u32[]{:S(2)}, u32[]{:S(2)}) collective-permute-start(bf16[48,6144]{1,0:T(8,128)(2,1)S(1)} %get-tuple-element.84.act.refs_2_.refs_4_.refs_6_), channel_id=1, source_target_pairs={{1,0},{0,1},{3,2},{2,3},{5,4},{4,5},{7,6},{6,7},{9,8},{8,9},{11,10... | collective-permute-start | bytes 1769480 | tf_op jit(solution)/shard_map/ppermute | solution.py:26
  109.2 14.5 %collective-permute-start.39 = (bf16[48,1024]{1,0:T(8,128)(2,1)S(1)}, bf16[48,1024]{1,0:T(8,128)(2,1)S(1)}, u32[]{:S(2)}, u32[]{:S(2)}) collective-permute-start(bf16[48,1024]{1,0:T(8,128)(2,1)S(1)} %get-tuple-element.85._.refs_4_), channel_id=1, source_target_pairs={{1,0},{0,1},{3,2},{2,3},{5,4},{4,5},{7,6},{6,7},{9,8},{8,9},{11,10... | collective-permute-start | bytes 294920 | tf_op jit(solution)/shard_map/ppermute | solution.py:26
  109.8 16.4 %collective-permute-start.25 = (bf16[80,640]{1,0:T(8,128)(2,1)S(1)}, bf16[80,640]{1,0:T(8,128)(2,1)S(1)}, u32[]{:S(2)}, u32[]{:S(2)}) collective-permute-start(bf16[80,640]{1,0:T(8,128)(2,1)S(1)} %get-tuple-element.78), channel_id=1, source_target_pairs={{2,0},{4,2},{6,4},{0,6},{3,1},{5,3},{7,5},{1,7},{10,8},{12,10},{14... | collective-permute-start | bytes 307208 | tf_op jit(solution)/shard_map/ppermute | solution.py:26
  111.8 14.6 %collective-permute-start.26 = (bf16[80,640]{1,0:T(8,128)(2,1)S(1)}, bf16[80,640]{1,0:T(8,128)(2,1)S(1)}, u32[]{:S(2)}, u32[]{:S(2)}) collective-permute-start(bf16[80,640]{1,0:T(8,128)(2,1)S(1)} %get-tuple-element.79), channel_id=1, source_target_pairs={{4,0},{6,2},{0,4},{2,6},{5,1},{7,3},{1,5},{3,7},{12,8},{14,10},{8,... | collective-permute-start | bytes 307208 | tf_op jit(solution)/shard_map/ppermute | solution.py:26
  123.7 21.9 %collective-permute-start.38 = (bf16[48,6144]{1,0:T(8,128)(2,1)S(1)}, bf16[48,6144]{1,0:T(8,128)(2,1)S(1)}, u32[]{:S(2)}, u32[]{:S(2)}) collective-permute-start(bf16[48,6144]{1,0:T(8,128)(2,1)S(1)} %get-tuple-element.93.refs_2_.refs_6_.refs_8_), channel_id=1, source_target_pairs={{1,0},{0,1},{3,2},{2,3},{5,4},{4,5},{7,6},{6,7},{9,8},{8,9},{11,10... | collective-permute-start | bytes 1769480 | tf_op jit(solution)/shard_map/ppermute | solution.py:26
  126.3 2.3 %collective-permute-start.31 = (bf16[80,640]{1,0:T(8,128)(2,1)S(1)}, bf16[80,640]{1,0:T(8,128)(2,1)S(1)}, u32[]{:S(2)}, u32[]{:S(2)}) collective-permute-start(bf16[80,640]{1,0:T(8,128)(2,1)S(1)} %get-tuple-element.87), channel_id=1, source_target_pairs={{2,0},{4,2},{6,4},{0,6},{3,1},{5,3},{7,5},{1,7},{10,8},{12,10},{14... | collective-permute-start | bytes 307208 | tf_op jit(solution)/shard_map/ppermute | solution.py:26
  126.3 25.6 %collective-permute-start.37 = (bf16[48,5120]{1,0:T(8,128)(2,1)S(1)}, bf16[48,5120]{1,0:T(8,128)(2,1)S(1)}, u32[]{:S(2)}, u32[]{:S(2)}) collective-permute-start(bf16[48,5120]{1,0:T(8,128)(2,1)S(1)} %shard_map.119.refs_0_), channel_id=1, source_target_pairs={{1,0},{0,1},{3,2},{2,3},{5,4},{4,5},{7,6},{6,7},{9,8},{8,9},{11,10... | collective-permute-start | bytes 1474568 | tf_op jit(solution)/shard_map/ppermute | solution.py:26
  128.6 4.9 %collective-permute-start.32 = (bf16[80,640]{1,0:T(8,128)(2,1)S(1)}, bf16[80,640]{1,0:T(8,128)(2,1)S(1)}, u32[]{:S(2)}, u32[]{:S(2)}) collective-permute-start(bf16[80,640]{1,0:T(8,128)(2,1)S(1)} %get-tuple-element.88), channel_id=1, source_target_pairs={{4,0},{6,2},{0,4},{2,6},{5,1},{7,3},{1,5},{3,7},{12,8},{14,10},{8,... | collective-permute-start | bytes 307208 | tf_op jit(solution)/shard_map/ppermute | solution.py:26
  133.4 4.3 %collective-permute-start.33 = (bf16[80,640]{1,0:T(8,128)(2,1)S(1)}, bf16[80,640]{1,0:T(8,128)(2,1)S(1)}, u32[]{:S(2)}, u32[]{:S(2)}) collective-permute-start(bf16[80,640]{1,0:T(8,128)(2,1)S(1)} %get-tuple-element.89), channel_id=1, source_target_pairs={{6,0},{0,2},{2,4},{4,6},{7,1},{1,3},{3,5},{5,7},{14,8},{8,10},{10,... | collective-permute-start | bytes 307208 | tf_op jit(solution)/shard_map/ppermute | solution.py:26
  137.8 4.1 %collective-permute-start.27 = (bf16[80,640]{1,0:T(8,128)(2,1)S(1)}, bf16[80,640]{1,0:T(8,128)(2,1)S(1)}, u32[]{:S(2)}, u32[]{:S(2)}) collective-permute-start(bf16[80,640]{1,0:T(8,128)(2,1)S(1)} %get-tuple-element.80), channel_id=1, source_target_pairs={{6,0},{0,2},{2,4},{4,6},{7,1},{1,3},{3,5},{5,7},{14,8},{8,10},{10,... | collective-permute-start | bytes 307208 | tf_op jit(solution)/shard_map/ppermute | solution.py:26
  141.9 18.7 %collective-permute-start.29 = (bf16[80,640]{1,0:T(8,128)(2,1)S(1)}, bf16[80,640]{1,0:T(8,128)(2,1)S(1)}, u32[]{:S(2)}, u32[]{:S(2)}) collective-permute-start(bf16[80,640]{1,0:T(8,128)(2,1)S(1)} %get-tuple-element.83), channel_id=1, source_target_pairs={{16,0},{24,8},{0,16},{8,24},{17,1},{25,9},{1,17},{9,25},{18,2},{26... | collective-permute-start | bytes 307208 | tf_op jit(solution)/shard_map/ppermute | solution.py:26
  143.2 17.4 %collective-permute-start.34 = (bf16[80,640]{1,0:T(8,128)(2,1)S(1)}, bf16[80,640]{1,0:T(8,128)(2,1)S(1)}, u32[]{:S(2)}, u32[]{:S(2)}) collective-permute-start(bf16[80,640]{1,0:T(8,128)(2,1)S(1)} %shard_map.123), channel_id=1, source_target_pairs={{24,0},{0,8},{8,16},{16,24},{25,1},{1,9},{9,17},{17,25},{26,2},{2,... | collective-permute-start | bytes 307208 | tf_op jit(solution)/shard_map/ppermute | solution.py:26
  145.6 15.0 %collective-permute-start.30 = (s32[1,4,128]{2,1,0:T(4,128)S(1)}, s32[1,4,128]{2,1,0:T(4,128)S(1)}, u32[]{:S(2)}, u32[]{:S(2)}) collective-permute-start(s32[1,4,128]{2,1,0:T(4,128)S(1)} %get-tuple-element.97), channel_id=1, source_target_pairs={{16,0},{24,8},{0,16},{8,24},{17,1},{25,9},{1,17},{9,25},{18,2},{26... | collective-permute-start | bytes 6152 | tf_op jit(solution)/shard_map/ppermute | solution.py:26

commit v6 on v5

--- a/solution.py
+++ b/solution.py
@@ -10,13 +10,13 @@
 CAP = 10
 PACK = 8
 PACKED = CAP * PACK
-COT_PIECES = ((0, 32, 0, 8), (32, 64, 0, 8), (64, 128, 0, 3), (64, 128, 3, 8))
-TOK_PIECES = ((0, 16, 0, 8), (16, 128, 0, 8))
+COT_PIECES = ((0, 48, 0, 8), (48, 64, 0, 8), (64, 128, 0, 8))
+TOK_PIECES = ((0, 128, 0, 8),)
 EPSILON = 1e-06
 F32 = jnp.float32
 BF16 = jnp.bfloat16
 VMEM_SMALL = 24 * 1024 * 1024
-VMEM_LOAD = 44 * 1024 * 1024
+VMEM_LOAD = 36 * 1024 * 1024
 VMEM_ALL = 60 * 1024 * 1024
 COST_BYTES = 1024
 
@@ -154,22 +154,6 @@
     return copy
 
 
-def load_kernel(gate, up, down, gate_v, up_v, down_v, sems):
-    step = gate.shape[0] // PACK
-    copies = []
-    for c in range(PACK):
-        r = pl.ds(c * step, step)
-        copies += [
-            pltpu.make_async_copy(gate.at[r], gate_v.at[r], sems.at[0, c]),
-            pltpu.make_async_copy(up.at[r], up_v.at[r], sems.at[1, c]),
-            pltpu.make_async_copy(down.at[:, r], down_v.at[:, r], sems.at[2, c]),
-        ]
-    for copy in copies:
-        copy.start()
-    for copy in copies:
-        copy.wait()
-
-
 def first_rows_kernel(tokens, routes, cotangent, raw, normed, piece, sem, sems, held):
     copy = piece_copy(cotangent, COT_PIECES[0], piece, sem)
     fetches = []
@@ -196,15 +180,12 @@
 
 
 def update0_kernel(n, *refs):
-    parts, (raw, routes, gates, next_routes, t1, cotangent) = refs[:n], refs[n : n + 6]
-    upd, onward, piece, sem = refs[n + 6 :]
-    copy = piece_copy(cotangent, COT_PIECES[2], piece, sem)
+    parts, (raw, routes, gates, next_routes, t1, upd, onward) = refs[:n], refs[n:]
     select = select_of(routes[0])
     weight = slot_gates(select, routes[0], gates[0])
     fresh = (raw[...].astype(F32) + weight * summed(parts)).astype(BF16)
     onward[...] = merged(select_of(next_routes[0]), select, fresh, t1[...].astype(F32))
     upd[...] = fresh
-    copy.wait()
 
 
 def update1_kernel(n, *refs):
@@ -215,7 +196,7 @@
 
 
 def enter1_kernel(h, cot, routes, gates, cotangent, _, out, piece, sem):
-    copy = piece_copy(cotangent, COT_PIECES[3], piece, sem)
+    copy = piece_copy(cotangent, COT_PIECES[2], piece, sem)
     values = h[...].astype(F32)
     out[:PACKED] = (values * inv_rms_of(values)).astype(BF16)
     weight = slot_gates(select_of(routes[1]), routes[1], gates[1])
@@ -232,13 +213,13 @@
 
 
 def grad1_kernel(n, *refs):
-    parts, (h, cot, upd) = refs[:n], refs[n:]
+    parts, (h, cot, _, __, upd) = refs[:n], refs[n:]
     upd[...] = state_grad(parts, h[...], cot[...])
 
 
 def enter0_kernel(m, upd1, next_routes, routes, gates, *refs):
     bulk, (tokens, _, c0, out, piece, sem) = refs[:m], refs[m:]
-    copy = piece_copy(tokens, TOK_PIECES[1], piece, sem)
+    copy = piece_copy(tokens, TOK_PIECES[0], piece, sem)
     select = select_of(routes[0])
     old = pick(select, list(zip(bulk, COT_PIECES)))
     rows = merged(select, select_of(next_routes[0]), upd1[...], old)
@@ -260,9 +241,9 @@
     )
 
 
-def finish_state_kernel(first, rest, upd0, prev2_routes, upd1, prev_routes, out):
+def finish_state_kernel(bulk, upd0, prev2_routes, upd1, prev_routes, out):
     place_rows(
-        list(zip([first, rest], TOK_PIECES)),
+        list(zip([bulk], TOK_PIECES)),
         select_of(prev2_routes[0]),
         upd0[...],
         select_of(prev_routes[0]),
@@ -300,17 +281,44 @@
 
 def forward_kernel(n, *refs):
     blocks, (gate, up, down) = refs[:n], refs[n : n + 3]
-    x, pre_gate, pre_up, act = refs[n + 3 : n + 7]
-    parts = refs[n + 7 : 2 * n + 7]
-    unpacked, whole32, held = refs[2 * n + 7 :]
+    x, pre_gate, pre_up, act, gate_v, up_v, down_v = refs[n + 3 : n + 10]
+    parts = refs[n + 10 : 2 * n + 10]
+    sems, unpacked, whole32, held = refs[2 * n + 10 :]
+    width = gate.shape[0]
+    fetches = []
+    for c in range(PACK):
+        k = columns(c, width)
+        fetches.append(
+            (
+                pltpu.make_async_copy(gate.at[k], gate_v.at[k], sems.at[0, c]),
+                pltpu.make_async_copy(up.at[k], up_v.at[k], sems.at[1, c]),
+                pltpu.make_async_copy(down.at[:, k], down_v.at[:, k], sems.at[2, c]),
+            )
+        )
+    for fetch_g, fetch_u, _ in fetches:
+        fetch_g.start()
+        fetch_u.start()
+    for _, _, fetch_d in fetches:
+        fetch_d.start()
     gather_rows(blocks, 0, unpacked, whole32, x)
-    acc_g = dot(x[...], gate[...])
-    acc_u = dot(x[...], up[...])
+    acc_g = jnp.zeros(pre_gate.shape, F32)
+    acc_u = jnp.zeros(pre_up.shape, F32)
+    for c, (fetch_g, fetch_u, _) in enumerate(fetches):
+        k = columns(c, width)
+        fetch_g.wait()
+        acc_g = acc_g + dot(x[:, k], gate_v[k])
+        fetch_u.wait()
+        acc_u = acc_u + dot(x[:, k], up_v[k])
     pre_gate[...] = acc_g
     pre_up[...] = acc_u
     activated = (acc_g * jax.nn.sigmoid(acc_g) * acc_u).astype(BF16)
     act[...] = activated
-    out_rows(activated, down, held, unpacked, parts)
+    for c, (_, _, fetch_d) in enumerate(fetches):
+        fetch_d.wait()
+        value = dot(activated, down_v[:, columns(c, width)])
+        spread_rows(value, c, n, held.at[c], unpacked)
+    for i, p in enumerate(parts):
+        p[...] = unpacked[i].astype(BF16)
 
 
 def out_rows(act, down, held, unpacked, parts):
@@ -339,11 +347,10 @@
 
 
 def tick1_kernel(n, *refs):
-    blocks, (act0, gate, up, down, tokens, _) = refs[:n], refs[n : n + 6]
-    x_act, g_grad, piece = refs[n + 6 : n + 9]
-    parts = refs[n + 9 : 2 * n + 9]
-    sem, unpacked, whole32, held, x, g = refs[2 * n + 9 :]
-    copy = piece_copy(tokens, TOK_PIECES[0], piece, sem)
+    blocks, (act0, gate, up, down) = refs[:n], refs[n : n + 4]
+    x_act, g_grad = refs[n + 4 : n + 6]
+    parts = refs[n + 6 : 2 * n + 6]
+    unpacked, whole32, held, x, g = refs[2 * n + 6 :]
     gather_rows(blocks, 0, unpacked, whole32.at[0], x)
     gather_rows(blocks, PACKED, unpacked, whole32.at[1], g)
     width, hidden = gate.shape
@@ -358,7 +365,6 @@
     g_grad[:, width : width + hidden] = gg
     g_grad[:, width + hidden :] = gu
     back_rows(gg, gu, gate, up, held, unpacked, parts)
-    copy.wait()
 
 
 def gather0_kernel(n, *refs):
@@ -498,27 +504,21 @@
         [one, one, cot_shapes[0]],
         [tokens, routes, cotangent],
         any_args=(0, 2),
-        any_outs=(2,),
         scratch=[*dma, pltpu.SemaphoreType.DMA((PACK,)), pltpu.VMEM(tokens.shape, BF16)],
         vmem=VMEM_ALL,
     )
-    gate, up, down = call(
-        load_kernel,
-        [pltpu.VMEM(a.shape, BF16) for a in (gate, up, down)],
-        [gate, up, down],
-        any_args=(0, 1, 2),
-        scratch=[pltpu.SemaphoreType.DMA((3, PACK))],
-        vmem=VMEM_LOAD,
-    )
     cot_parts = [shifted(piece, "section", -2)]
     blocks = from_group(normed0)
-    x0, pre_gate0, pre_up0, act0, *parts = call(
+    x0, pre_gate0, pre_up0, act0, gate, up, down, *parts = call(
         part(forward_kernel, n),
         [((rows, width), BF16), ((rows, hidden), F32), ((rows, hidden), F32)]
         + [((rows, hidden), BF16)]
+        + [pltpu.VMEM(a.shape, BF16) for a in (gate, up, down)]
         + [one] * n,
         [*blocks, gate, up, down],
-        scratch=[unpacked, flat32, held],
+        any_args=(n, n + 1, n + 2),
+        scratch=[pltpu.SemaphoreType.DMA((3, PACK)), unpacked, flat32, held],
+        vmem=VMEM_LOAD,
     )
     t1, cot1, piece = call(
         other_rows_kernel,
@@ -532,21 +532,15 @@
     x0_all = copies_of(x0)
     cot_parts.append(shifted(piece, "section", -2))
     parts = to_group(parts)
-    upd0, h1, piece = call(
-        part(update0_kernel, n),
-        [one, one, cot_shapes[2]],
-        [*parts, raw0, routes, gates, next_routes, t1, cotangent],
-        any_args=(n + 5,),
-        any_outs=(2,),
-        scratch=dma,
+    upd0, h1 = call(
+        part(update0_kernel, n), [one, one], [*parts, raw0, routes, gates, next_routes, t1]
     )
     h1 = shifted(h1, "section", 1)
-    cot_parts.append(shifted(piece, "section", -2))
     upd0 = shifted(upd0, "section", 2)
 
     enter1, piece = call(
         enter1_kernel,
-        [((2 * PACKED, step), BF16), cot_shapes[3]],
+        [((2 * PACKED, step), BF16), cot_shapes[2]],
         [h1, cot1, routes, gates, cotangent, cot_parts[1]],
         any_args=(4, 5),
         any_outs=(1,),
@@ -554,30 +548,32 @@
     )
     cot_parts.append(shifted(piece, "section", -2))
     blocks = from_group(enter1)
-    x_act, g_grad1, piece, *parts = call(
+    x_act, g_grad1, *parts = call(
         part(tick1_kernel, n),
-        [wide, wide, tok_shapes[0]] + [one] * n,
-        [*blocks, act0, gate, up, down, tokens, cot_parts[2]],
-        any_args=(n + 4, n + 5),
-        any_outs=(2,),
-        scratch=[*dma, unpacked, pltpu.VMEM((2, rows, width), F32), held, flat, flat],
-    )
-    tok_parts = [shifted(piece, "section", 2)]
+        [wide, wide] + [one] * n,
+        [*blocks, act0, gate, up, down],
+        scratch=[unpacked, pltpu.VMEM((2, rows, width), F32), held, flat, flat],
+    )
     parts = to_group(parts)
-    (upd1,) = call(part(grad1_kernel, n), [one], [*parts, h1, cot1])
+    (upd1,) = call(
+        part(grad1_kernel, n),
+        [one],
+        [*parts, h1, cot1, x0_all[-1], cot_parts[2]],
+        any_args=(n + 2, n + 3),
+    )
     upd1 = shifted(upd1, "section", -1)
     x_act_all, g_grad1_all = copies_of(x_act), copies_of(g_grad1)
 
     m = len(cot_parts)
     c0, enter0, piece = call(
         part(enter0_kernel, m),
-        [one, one, tok_shapes[1]],
-        [upd1, next_routes, routes, gates, *cot_parts, tokens, tok_parts[0]],
+        [one, one, tok_shapes[0]],
+        [upd1, next_routes, routes, gates, *cot_parts, tokens, x_act_all[-1]],
         any_args=(m + 4, m + 5),
         any_outs=(2,),
         scratch=dma,
     )
-    tok_parts.append(shifted(piece, "section", 2))
+    tok_parts = [shifted(piece, "section", 2)]
     blocks = from_group(enter0)
     (g0,) = call(
         part(gather0_kernel, n), [((rows, width), BF16)], blocks, scratch=[unpacked, flat32]

time: 163 us -> 156 us (0.957)
  waiting for transfers between devices: 54.6 us -> 69.9 us
  starting transfers between devices: 52.4 us -> 41.1 us
  Pallas kernels: 54.1 us -> 43.3 us
    ppermute x40 -> x38, waiting for transfers between devices: 54.6 us -> 69.9 us  [shifted(): lax.ppermute(block, axis, [((i - distance) % size, i) for i in range(size)])]
    ppermute x40 -> x38, starting transfers between devices: 52.4 us -> 41.1 us  [shifted(): lax.ppermute(block, axis, [((i - distance) % size, i) for i in range(size)])]
    pallas_call x15 -> x14, Pallas kernels: 43.1 us -> 32.3 us  [call(): pl.pallas_call(kernel, out_shape=outs, in_specs=[anywhere if i in any_arg...]
  transfers between devices with their start and end apart: 40 -> 38, of which waited for: 19 -> 22; matrix products, arithmetic and copies ran while one was open for 0% -> 0% of each run, Pallas kernels for 23% -> 23%
where the time goes in v6:
time: 156 us
  waiting for transfers between devices  69.9 us (45%)
  Pallas kernels  43.3 us (28%)
  starting transfers between devices  41.1 us (26%)
    ppermute x38, waiting for transfers between devices, shifted(): lax.ppermute(block, axis, [((i - distance) % size, i) for i in range(size)])  69.9 us
    ppermute x38, starting transfers between devices, shifted(): lax.ppermute(block, axis, [((i - distance) % size, i) for i in range(size)])  41.1 us
    pallas_call x14, Pallas kernels, call(): pl.pallas_call(kernel, out_shape=outs, in_specs=[anywhere if i in any_arg...  32.3 us
    pallas_call x2, Pallas kernels, chunked_call(): pl.pallas_call(kernel, grid=(PACK,), out_shape=[jax.ShapeDtypeStruct(s, B...  11 us
  transfers between devices with their start and end apart: 38, of which 22 were waited for; matrix products, arithmetic and copies ran while one was open for 0% of the time, Pallas kernels for 23%

profile of v6, /device:TPU:0, one launch (start us, length us, event | category | flops | bytes accessed | tf_op | source)
XLA Modules:
  0.0 156.0 jit_solution(15252736411976853721)
XLA Ops:
  0.6 3.9 %shard_map.110 = (bf16[80,640]{1,0:T(8,128)(2,1)}, bf16[80,640]{1,0:T(8,128)(2,1)}, bf16[48,5120]{1,0:T(8,128)(2,1)}) custom-call(bf16[128,5120]{1,0:T(8,128)(2,1)} %refs_3_.1, s32[2,4,128]{2,1,0:T(4,128)} %bitcast.8, bf16[128,5120]{1,0:T(8,128)(2,1)} %cotangent.5), custom_call_target="tpu_custom_call" | custom-call | bytes 1024 | tf_op jit(solution)/shard_map/pallas_call | solution.py:39
  4.6 4.1 %collective-permute-start.8 = (bf16[48,5120]{1,0:T(8,128)(2,1)}, bf16[48,5120]{1,0:T(8,128)(2,1)S(1)}, u32[]{:S(2)}, u32[]{:S(2)}) collective-permute-start(bf16[48,5120]{1,0:T(8,128)(2,1)} %get-tuple-element.56), channel_id=1, source_target_pairs={{16,0},{24,8},{0,16},{8,24},{17,1},{25,9},{1,17},{9,25},{18,2},{26... | collective-permute-start | bytes 1474568 | tf_op jit(solution)/shard_map/ppermute | solution.py:26
  8.7 0.7 collective-permute-start.2
  9.4 0.8 collective-permute-start.1
  10.2 0.2 collective-permute-start
  10.4 2.2 %collective-permute-done.2.refs_3_ = bf16[80,640]{1,0:T(8,128)(2,1)S(1)} collective-permute-done((bf16[80,640]{1,0:T(8,128)(2,1)}, bf16[80,640]{1,0:T(8,128)(2,1)S(1)}, u32[]{:S(2)}, u32[]{:S(2)}) %collective-permute-start.2) | collective-permute-done | bytes 102432 | tf_op jit(solution)/shard_map/ppermute | solution.py:26
  12.7 3.6 %collective-permute-done.1.refs_2_ = bf16[80,640]{1,0:T(8,128)(2,1)S(1)} collective-permute-done((bf16[80,640]{1,0:T(8,128)(2,1)}, bf16[80,640]{1,0:T(8,128)(2,1)S(1)}, u32[]{:S(2)}, u32[]{:S(2)}) %collective-permute-start.1) | collective-permute-done | bytes 102432 | tf_op jit(solution)/shard_map/ppermute | solution.py:26
  16.4 0.9 copy-done.4
  17.3 6.6 %shard_map.111 = (bf16[48,5120]{1,0:T(8,128)(2,1)S(1)}, f32[48,512]{1,0:T(8,128)S(1)}, f32[48,512]{1,0:T(8,128)S(1)}, bf16[48,512]{1,0:T(8,128)(2,1)S(1)}, bf16[...) custom-call(bf16[80,640]{1,0:T(8,128)(2,1)S(1)} %copy-done.4, ...), custom_call_target="tpu_custom_call" | custom-call | bytes 1024 | tf_op jit(solution)/shard_map/pallas_call | solution.py:39
  23.9 1.2 collective-permute-start.4
  25.3 1.6 %collective-permute-start.7 = (s32[1,4,128]{2,1,0:T(4,128)S(1)}, s32[1,4,128]{2,1,0:T(4,128)S(1)}, u32[]{:S(2)}, u32[]{:S(2)}) collective-permute-start(s32[1,4,128]{2,1,0:T(4,128)S(1)} %get-tuple-element.94), channel_id=1, source_target_pairs={{24,0},{0,8},{8,16},{16,24},{25,1},{1,9},{9,17},{17,25},{26,2},{2,... | collective-permute-start | bytes 6152 | tf_op jit(solution)/shard_map/ppermute | solution.py:26
  26.9 3.8 %collective-permute-done.7.prev_routes = s32[1,4,128]{2,1,0:T(4,128)S(1)} collective-permute-done((s32[1,4,128]{2,1,0:T(4,128)S(1)}, s32[1,4,128]{2,1,0:T(4,128)S(1)}, u32[]{:S(2)}, u32[]{:S(2)}) %collective-permute-start.7) | collective-permute-done | bytes 2080 | tf_op jit(solution)/shard_map/ppermute | solution.py:26
  30.7 3.6 %collective-permute-done.6.next_routes.refs_7_.refs_8_ = s32[1,4,128]{2,1,0:T(4,128)S(1)} collective-permute-done((s32[1,4,128]{2,1,0:T(4,128)S(1)}, s32[1,4,128]{2,1,0:T(4,128)S(1)}, u32[]{:S(2)}, u32[]{:S(2)}) %collective-permute-start.6) | collective-permute-done | bytes 2080 | tf_op jit(solution)/shard_map/ppermute | solution.py:26
  34.3 1.0 shard_map.112
  35.4 2.7 %collective-permute-start.11 = (bf16[16,5120]{1,0:T(8,128)(2,1)S(1)}, bf16[16,5120]{1,0:T(8,128)(2,1)S(1)}, u32[]{:S(2)}, u32[]{:S(2)}) collective-permute-start(bf16[16,5120]{1,0:T(8,128)(2,1)S(1)} %get-tuple-element.60), channel_id=1, source_target_pairs={{16,0},{24,8},{0,16},{8,24},{17,1},{25,9},{1,17},{9,25},{18,2},{26... | collective-permute-start | bytes 491528 | tf_op jit(solution)/shard_map/ppermute | solution.py:26
  38.1 0.5 shard_map.113
  38.6 3.8 %collective-permute-start.10 = (bf16[80,640]{1,0:T(8,128)(2,1)S(1)}, bf16[80,640]{1,0:T(8,128)(2,1)S(1)}, u32[]{:S(2)}, u32[]{:S(2)}) collective-permute-start(bf16[80,640]{1,0:T(8,128)(2,1)S(1)} %get-tuple-element.59), channel_id=1, source_target_pairs={{8,0},{16,8},{24,16},{0,24},{9,1},{17,9},{25,17},{1,25},{10,2},{18... | collective-permute-start | bytes 307208 | tf_op jit(solution)/shard_map/ppermute | solution.py:26
  42.4 3.2 %collective-permute-done.9.h.refs_4_ = bf16[80,640]{1,0:T(8,128)(2,1)S(1)} collective-permute-done((bf16[80,640]{1,0:T(8,128)(2,1)S(1)}, bf16[80,640]{1,0:T(8,128)(2,1)S(1)}, u32[]{:S(2)}, u32[]{:S(2)}) %collective-permute-start.9) | collective-permute-done | bytes 102432 | tf_op jit(solution)/shard_map/ppermute | solution.py:26
  45.6 1.3 collective-permute-done.10.cot.refs_5_
  46.8 0.9 collective-permute-done.11._.refs_1_.refs_10_
  47.8 0.6 shard_map.114
  48.4 1.6 %collective-permute-start.13 = (bf16[160,640]{1,0:T(8,128)(2,1)S(1)}, bf16[160,640]{1,0:T(8,128)(2,1)S(1)}, u32[]{:S(2)}, u32[]{:S(2)}) collective-permute-start(bf16[160,640]{1,0:T(8,128)(2,1)S(1)} %get-tuple-element.61.refs_0_), channel_id=1, source_target_pairs={{4,0},{6,2},{0,4},{2,6},{5,1},{7,3},{1,5},{3,7},{12,8},{14,10},{8,... | collective-permute-start | bytes 614408 | tf_op jit(solution)/shard_map/ppermute | solution.py:26
  50.2 2.3 %collective-permute-start.19 = (bf16[64,5120]{1,0:T(8,128)(2,1)S(1)}, bf16[64,5120]{1,0:T(8,128)(2,1)S(1)}, u32[]{:S(2)}, u32[]{:S(2)}) collective-permute-start(bf16[64,5120]{1,0:T(8,128)(2,1)S(1)} %get-tuple-element.70), channel_id=1, source_target_pairs={{16,0},{24,8},{0,16},{8,24},{17,1},{25,9},{1,17},{9,25},{18,2},{26... | collective-permute-start | bytes 1966088 | tf_op jit(solution)/shard_map/ppermute | solution.py:26
  52.5 1.5 collective-permute-start.18
  54.0 6.2 %collective-permute-done.13.refs_2_ = bf16[160,640]{1,0:T(8,128)(2,1)S(1)} collective-permute-done((bf16[160,640]{1,0:T(8,128)(2,1)S(1)}, bf16[160,640]{1,0:T(8,128)(2,1)S(1)}, u32[]{:S(2)}, u32[]{:S(2)}) %collective-permute-start.13) | collective-permute-done | bytes 204832 | tf_op jit(solution)/shard_map/ppermute | solution.py:26
  60.3 6.8 %shard_map.115 = (bf16[48,6144]{1,0:T(8,128)(2,1)S(1)}, bf16[48,6144]{1,0:T(8,128)(2,1)S(1)}, bf16[80,640]{1,0:T(8,128)(2,1)S(1)}, bf16[80,640]{1,0:T(8,128)(2,1...) custom-call(bf16[160,640]{1,0:T(8,128)(2,1)S(1)} %get-tuple-element.61.refs_0_, ...), custom_call_target="tpu_custom_call" | custom-call | bytes 1024 | tf_op jit(solution)/shard_map/pallas_call | solution.py:39
  67.1 1.5 collective-permute-start.21
  68.7 0.5 collective-permute-start.16
  69.2 0.2 collective-permute-start.17
  69.4 2.5 %collective-permute-done.15.refs_1_ = bf16[80,640]{1,0:T(8,128)(2,1)S(1)} collective-permute-done((bf16[80,640]{1,0:T(8,128)(2,1)S(1)}, bf16[80,640]{1,0:T(8,128)(2,1)S(1)}, u32[]{:S(2)}, u32[]{:S(2)}) %collective-permute-start.15) | collective-permute-done | bytes 102432 | tf_op jit(solution)/shard_map/ppermute | solution.py:26
  71.9 2.5 %collective-permute-done.16.refs_2_ = bf16[80,640]{1,0:T(8,128)(2,1)S(1)} collective-permute-done((bf16[80,640]{1,0:T(8,128)(2,1)S(1)}, bf16[80,640]{1,0:T(8,128)(2,1)S(1)}, u32[]{:S(2)}, u32[]{:S(2)}) %collective-permute-start.16) | collective-permute-done | bytes 102432 | tf_op jit(solution)/shard_map/ppermute | solution.py:26
  74.3 0.8 collective-permute-done.17.refs_3_
  75.1 7.1 %collective-permute-done.19.refs_7_.refs_2_.refs_11_ = bf16[64,5120]{1,0:T(8,128)(2,1)S(1)} collective-permute-done((bf16[64,5120]{1,0:T(8,128)(2,1)S(1)}, bf16[64,5120]{1,0:T(8,128)(2,1)S(1)}, u32[]{:S(2)}, u32[]{:S(2)}) %collective-permute-start.19) | collective-permute-done | bytes 655392 | tf_op jit(solution)/shard_map/ppermute | solution.py:26
  82.2 0.4 shard_map.116
  82.7 2.2 %collective-permute-start.20 = (bf16[80,640]{1,0:T(8,128)(2,1)S(1)}, bf16[80,640]{1,0:T(8,128)(2,1)S(1)}, u32[]{:S(2)}, u32[]{:S(2)}) collective-permute-start(bf16[80,640]{1,0:T(8,128)(2,1)S(1)} %shard_map.116), channel_id=1, source_target_pairs={{8,0},{16,8},{24,16},{0,24},{9,1},{17,9},{25,17},{1,25},{10,2},{18... | collective-permute-start | bytes 307208 | tf_op jit(solution)/shard_map/ppermute | solution.py:26
  84.9 2.5 %collective-permute-done.20.upd1.refs_7_ = bf16[80,640]{1,0:T(8,128)(2,1)S(1)} collective-permute-done((bf16[80,640]{1,0:T(8,128)(2,1)S(1)}, bf16[80,640]{1,0:T(8,128)(2,1)S(1)}, u32[]{:S(2)}, u32[]{:S(2)}) %collective-permute-start.20) | collective-permute-done | bytes 102432 | tf_op jit(solution)/shard_map/ppermute | solution.py:26
  87.4 1.4 shard_map.117
  88.8 0.8 collective-permute-start.28
  89.7 1.5 collective-permute-start.36
  91.2 1.2 collective-permute-start.23
  92.3 0.2 collective-permute-start.22
  92.5 1.2 collective-permute-done.24.refs_3_
  93.8 4.1 %collective-permute-done.23.refs_2_ = bf16[80,640]{1,0:T(8,128)(2,1)S(1)} collective-permute-done((bf16[80,640]{1,0:T(8,128)(2,1)S(1)}, bf16[80,640]{1,0:T(8,128)(2,1)S(1)}, u32[]{:S(2)}, u32[]{:S(2)}) %collective-permute-start.23) | collective-permute-done | bytes 102432 | tf_op jit(solution)/shard_map/ppermute | solution.py:26
  97.9 0.3 collective-permute-done.22.refs_1_
  98.4 0.6 collective-permute-start.35
  99.0 4.9 %shard_map.119 = (bf16[48,1024]{1,0:T(8,128)(2,1)S(1)}, bf16[80,640]{1,0:T(8,128)(2,1)S(1)}, bf16[80,640]{1,0:T(8,128)(2,1)S(1)}, bf16[80,640]{1,0:T(8,128)(2,1)S(1)}, bf16[80,640]{1,0:T(8,128)(2,1)S(1)}) custom-call(bf16[48,5120]{1,0:T(8,128)(2,1)S(1)} %shard_map.118.refs_0_, f32[48,512]{1,0:T(8,128)S(1)} %get-tuple-element.73.refs_1_, ...), custom_call_target="tpu_custom_call" | custom-call | bytes 1024 | tf_op jit(solution)/shard_map/pallas_call | solution.py:39
  103.9 1.1 shard_map.121
  105.1 1.0 collective-permute-start.32
  106.0 1.5 collective-permute-start.37
  107.5 8.8 %collective-permute-done.37.refs_5_ = bf16[48,1024]{1,0:T(8,128)(2,1)S(1)} collective-permute-done((bf16[48,1024]{1,0:T(8,128)(2,1)S(1)}, bf16[48,1024]{1,0:T(8,128)(2,1)S(1)}, u32[]{:S(2)}, u32[]{:S(2)}) %collective-permute-start.37) | collective-permute-done | bytes 98336 | tf_op jit(solution)/shard_map/ppermute | solution.py:26
  116.4 1.7 %collective-permute-start.25 = (bf16[80,640]{1,0:T(8,128)(2,1)S(1)}, bf16[80,640]{1,0:T(8,128)(2,1)S(1)}, u32[]{:S(2)}, u32[]{:S(2)}) collective-permute-start(bf16[80,640]{1,0:T(8,128)(2,1)S(1)} %get-tuple-element.76), channel_id=1, source_target_pairs={{2,0},{4,2},{6,4},{0,6},{3,1},{5,3},{7,5},{1,7},{10,8},{12,10},{14... | collective-permute-start | bytes 307208 | tf_op jit(solution)/shard_map/ppermute | solution.py:26
  118.1 1.8 %collective-permute-start.26 = (bf16[80,640]{1,0:T(8,128)(2,1)S(1)}, bf16[80,640]{1,0:T(8,128)(2,1)S(1)}, u32[]{:S(2)}, u32[]{:S(2)}) collective-permute-start(bf16[80,640]{1,0:T(8,128)(2,1)S(1)} %get-tuple-element.77), channel_id=1, source_target_pairs={{4,0},{6,2},{0,4},{2,6},{5,1},{7,3},{1,5},{3,7},{12,8},{14,10},{8,... | collective-permute-start | bytes 307208 | tf_op jit(solution)/shard_map/ppermute | solution.py:26
  119.9 0.5 collective-permute-done.33.refs_3_
  120.5 0.2 shard_map.122
  120.7 0.6 collective-permute-done.25.refs_1_
  121.3 1.6 %collective-permute-start.29 = (bf16[80,640]{1,0:T(8,128)(2,1)S(1)}, bf16[80,640]{1,0:T(8,128)(2,1)S(1)}, u32[]{:S(2)}, u32[]{:S(2)}) collective-permute-start(bf16[80,640]{1,0:T(8,128)(2,1)S(1)} %get-tuple-element.81), channel_id=1, source_target_pairs={{16,0},{24,8},{0,16},{8,24},{17,1},{25,9},{1,17},{9,25},{18,2},{26... | collective-permute-start | bytes 307208 | tf_op jit(solution)/shard_map/ppermute | solution.py:26
  122.9 2.0 %collective-permute-done.26.refs_2_ = bf16[80,640]{1,0:T(8,128)(2,1)S(1)} collective-permute-done((bf16[80,640]{1,0:T(8,128)(2,1)S(1)}, bf16[80,640]{1,0:T(8,128)(2,1)S(1)}, u32[]{:S(2)}, u32[]{:S(2)}) %collective-permute-start.26) | collective-permute-done | bytes 102432 | tf_op jit(solution)/shard_map/ppermute | solution.py:26
  125.0 3.2 %collective-permute-start.34 = (bf16[80,640]{1,0:T(8,128)(2,1)S(1)}, bf16[80,640]{1,0:T(8,128)(2,1)S(1)}, u32[]{:S(2)}, u32[]{:S(2)}) collective-permute-start(bf16[80,640]{1,0:T(8,128)(2,1)S(1)} %shard_map.122), channel_id=1, source_target_pairs={{24,0},{0,8},{8,16},{16,24},{25,1},{1,9},{9,17},{17,25},{26,2},{2,... | collective-permute-start | bytes 307208 | tf_op jit(solution)/shard_map/ppermute | solution.py:26
  128.2 0.4 collective-permute-start.30
  128.6 2.4 %shard_map.124 = (bf16[5120,192]{1,0:T(8,128)(2,1)S(1)}, bf16[512,192]{1,0:T(8,128)(2,1)S(1)}) custom-call(bf16[48,5120]{1,0:T(8,128)(2,1)S(1)} %get-tuple-element.69.refs_0_, bf16[48,5120]{1,0:T(8,128)(2,1)S(1)} %collective-permute-done.18.refs_6_.refs_1_, bf16[48,6144]{1,0:T(8,128)(2,1)S(1)} %get-tuple-element.71.act.refs_2_.refs_4_.refs_6_, ...), custom_call_target="tpu_custom_call" | custom-call | bytes 1024 | tf_op jit(solution)/shard_map/pallas_call | solution.py:413
  131.0 2.4 %shard_map.120 = bf16[128,5120]{1,0:T(8,128)(2,1)} custom-call(bf16[80,640]{1,0:T(8,128)(2,1)S(1)} %get-tuple-element.75.refs_0_, bf16[80,640]{1,0:T(8,128)(2,1)S(1)} %collective-permute-done.25.refs_1_, bf16[80,640]{1,0:T(8,128)(2,1)S(1)} %collective-permute-done.26.refs_2_, bf16[80,640]{1,0:T(8,128)(2,1)S(1)} %collective-permute-done.27.refs_3_, ...), custom_call_target="tpu_custom_call" | custom-call | bytes 1024 | tf_op jit(solution)/shard_map/pallas_call | solution.py:39
  133.4 8.6 %shard_map.125 = (bf16[5120,512]{1,0:T(8,128)(2,1)}, bf16[5120,512]{1,0:T(8,128)(2,1)}, bf16[512,5120]{1,0:T(8,128)(2,1)}) custom-call(bf16[5120,192]{1,0:T(8,128)(2,1)S(1)} %get-tuple-element.87.x_t, bf16[512,192]{1,0:T(8,128)(2,1)S(1)} %get-tuple-element.88.act_t, bf16[48,5120]{1,0:T(8,128)(2,1)S(1)} %shard_map.118.refs_0_, ...), custom_call_target="tpu_custom_call" | custom-call | bytes 1024 | tf_op jit(solution)/shard_map/pallas_call | solution.py:413
  142.0 11.8 %collective-permute-done.30.prev2_routes = s32[1,4,128]{2,1,0:T(4,128)S(1)} collective-permute-done((s32[1,4,128]{2,1,0:T(4,128)S(1)}, s32[1,4,128]{2,1,0:T(4,128)S(1)}, u32[]{:S(2)}, u32[]{:S(2)}) %collective-permute-start.30) | collective-permute-done | bytes 2080 | tf_op jit(solution)/shard_map/ppermute | solution.py:26
  153.8 2.2 %shard_map.123 = bf16[128,5120]{1,0:T(8,128)(2,1)} custom-call(bf16[128,5120]{1,0:T(8,128)(2,1)S(1)} %collective-permute-done.28.bulk, bf16[80,640]{1,0:T(8,128)(2,1)S(1)} %collective-permute-done.29.upd0, s32[1,4,128]{2,1,0:T(4,128)S(1)} %collective-permute-done.30.prev2_routes, bf16[80,640]{1,0:T(8,128)(2,1)S(1)} %collective-permute-done.34.upd1, ...), custom_call_target="tpu_custom_call" | custom-call | bytes 1024 | tf_op jit(solution)/shard_map/pallas_call | solution.py:39
  (41 shorter events, 1.0 us)
Async XLA Ops:
  4.6 29.7 %collective-permute-start.8 = (bf16[48,5120]{1,0:T(8,128)(2,1)}, bf16[48,5120]{1,0:T(8,128)(2,1)S(1)}, u32[]{:S(2)}, u32[]{:S(2)}) collective-permute-start(bf16[48,5120]{1,0:T(8,128)(2,1)} %get-tuple-element.56), channel_id=1, source_target_pairs={{16,0},{24,8},{0,16},{8,24},{17,1},{25,9},{1,17},{9,25},{18,2},{26... | collective-permute-start | bytes 1474568 | tf_op jit(solution)/shard_map/ppermute | solution.py:26
  8.7 4.0 %collective-permute-start.2 = (bf16[80,640]{1,0:T(8,128)(2,1)}, bf16[80,640]{1,0:T(8,128)(2,1)S(1)}, u32[]{:S(2)}, u32[]{:S(2)}) collective-permute-start(bf16[80,640]{1,0:T(8,128)(2,1)} %get-tuple-element.49.refs_0_), channel_id=1, source_target_pairs={{2,0},{4,2},{6,4},{0,6},{3,1},{5,3},{7,5},{1,7},{10,8},{12,10},{14... | collective-permute-start | bytes 307208 | tf_op jit(solution)/shard_map/ppermute | solution.py:26
  9.4 6.9 %collective-permute-start.1 = (bf16[80,640]{1,0:T(8,128)(2,1)}, bf16[80,640]{1,0:T(8,128)(2,1)S(1)}, u32[]{:S(2)}, u32[]{:S(2)}) collective-permute-start(bf16[80,640]{1,0:T(8,128)(2,1)} %get-tuple-element.49.refs_0_), channel_id=1, source_target_pairs={{4,0},{6,2},{0,4},{2,6},{5,1},{7,3},{1,5},{3,7},{12,8},{14,10},{8,... | collective-permute-start | bytes 307208 | tf_op jit(solution)/shard_map/ppermute | solution.py:26
  10.2 6.1 %collective-permute-start = (bf16[80,640]{1,0:T(8,128)(2,1)}, bf16[80,640]{1,0:T(8,128)(2,1)S(1)}, u32[]{:S(2)}, u32[]{:S(2)}) collective-permute-start(bf16[80,640]{1,0:T(8,128)(2,1)} %get-tuple-element.49.refs_0_), channel_id=1, source_target_pairs={{6,0},{0,2},{2,4},{4,6},{7,1},{1,3},{3,5},{5,7},{14,8},{8,10},{10,... | collective-permute-start | bytes 307208 | tf_op jit(solution)/shard_map/ppermute | solution.py:26
  16.3 0.9 copy-start.4
  17.2 8.1 %copy-start.3 = (s32[2,128,4]{1,2,0:T(4,128)S(1)}, s32[2,128,4]{1,2,0:T(4,128)}, u32[]{:S(2)}) copy-start(s32[2,128,4]{1,2,0:T(4,128)} %param.12) | copy-start | bytes 12292
  17.2 17.1 %copy-start = (bf16[128,5120]{1,0:T(8,128)(2,1)S(1)}, bf16[128,5120]{1,0:T(8,128)(2,1)}, u32[]{:S(2)}) copy-start(bf16[128,5120]{1,0:T(8,128)(2,1)} %cotangent.5) | copy-start | bytes 3932164
  17.2 17.1 %copy-start.1 = (bf16[128,5120]{1,0:T(8,128)(2,1)S(1)}, bf16[128,5120]{1,0:T(8,128)(2,1)}, u32[]{:S(2)}) copy-start(bf16[128,5120]{1,0:T(8,128)(2,1)} %refs_3_.1) | copy-start | bytes 3932164
  17.3 20.8 %copy-start.2 = (bf16[80,640]{1,0:T(8,128)(2,1)S(1)}, bf16[80,640]{1,0:T(8,128)(2,1)}, u32[]{:S(2)}) copy-start(bf16[80,640]{1,0:T(8,128)(2,1)} %get-tuple-element.54.refs_4_) | copy-start | bytes 307204
  17.3 20.8 %copy-start.5 = (f32[2,128,4]{1,2,0:T(4,128)S(1)}, f32[2,128,4]{1,2,0:T(4,128)}, u32[]{:S(2)}) copy-start(f32[2,128,4]{1,2,0:T(4,128)} %param.13) | copy-start | bytes 12292
  23.9 14.2 %collective-permute-start.3 = (bf16[80,640]{1,0:T(8,128)(2,1)S(1)}, bf16[80,640]{1,0:T(8,128)(2,1)S(1)}, u32[]{:S(2)}, u32[]{:S(2)}) collective-permute-start(bf16[80,640]{1,0:T(8,128)(2,1)S(1)} %get-tuple-element.51), channel_id=1, source_target_pairs={{2,0},{4,2},{6,4},{0,6},{3,1},{5,3},{7,5},{1,7},{10,8},{12,10},{14... | collective-permute-start | bytes 307208 | tf_op jit(solution)/shard_map/ppermute | solution.py:26
  23.9 14.1 %collective-permute-start.4 = (bf16[80,640]{1,0:T(8,128)(2,1)S(1)}, bf16[80,640]{1,0:T(8,128)(2,1)S(1)}, u32[]{:S(2)}, u32[]{:S(2)}) collective-permute-start(bf16[80,640]{1,0:T(8,128)(2,1)S(1)} %get-tuple-element.52), channel_id=1, source_target_pairs={{4,0},{6,2},{0,4},{2,6},{5,1},{7,3},{1,5},{3,7},{12,8},{14,10},{8,... | collective-permute-start | bytes 307208 | tf_op jit(solution)/shard_map/ppermute | solution.py:26
  25.2 12.9 %collective-permute-start.5 = (bf16[80,640]{1,0:T(8,128)(2,1)S(1)}, bf16[80,640]{1,0:T(8,128)(2,1)S(1)}, u32[]{:S(2)}, u32[]{:S(2)}) collective-permute-start(bf16[80,640]{1,0:T(8,128)(2,1)S(1)} %get-tuple-element.53), channel_id=1, source_target_pairs={{6,0},{0,2},{2,4},{4,6},{7,1},{1,3},{3,5},{5,7},{14,8},{8,10},{10,... | collective-permute-start | bytes 307208 | tf_op jit(solution)/shard_map/ppermute | solution.py:26
  25.3 5.4 %collective-permute-start.7 = (s32[1,4,128]{2,1,0:T(4,128)S(1)}, s32[1,4,128]{2,1,0:T(4,128)S(1)}, u32[]{:S(2)}, u32[]{:S(2)}) collective-permute-start(s32[1,4,128]{2,1,0:T(4,128)S(1)} %get-tuple-element.94), channel_id=1, source_target_pairs={{24,0},{0,8},{8,16},{16,24},{25,1},{1,9},{9,17},{17,25},{26,2},{2,... | collective-permute-start | bytes 6152 | tf_op jit(solution)/shard_map/ppermute | solution.py:26
  30.7 3.6 %collective-permute-start.6 = (s32[1,4,128]{2,1,0:T(4,128)S(1)}, s32[1,4,128]{2,1,0:T(4,128)S(1)}, u32[]{:S(2)}, u32[]{:S(2)}) collective-permute-start(s32[1,4,128]{2,1,0:T(4,128)S(1)} %get-tuple-element.94), channel_id=1, source_target_pairs={{8,0},{16,8},{24,16},{0,24},{9,1},{17,9},{25,17},{1,25},{10,2},{18... | collective-permute-start | bytes 6152 | tf_op jit(solution)/shard_map/ppermute | solution.py:26
  35.4 12.4 %collective-permute-start.11 = (bf16[16,5120]{1,0:T(8,128)(2,1)S(1)}, bf16[16,5120]{1,0:T(8,128)(2,1)S(1)}, u32[]{:S(2)}, u32[]{:S(2)}) collective-permute-start(bf16[16,5120]{1,0:T(8,128)(2,1)S(1)} %get-tuple-element.60), channel_id=1, source_target_pairs={{16,0},{24,8},{0,16},{8,24},{17,1},{25,9},{1,17},{9,25},{18,2},{26... | collective-permute-start | bytes 491528 | tf_op jit(solution)/shard_map/ppermute | solution.py:26
  38.5 7.1 %collective-permute-start.9 = (bf16[80,640]{1,0:T(8,128)(2,1)S(1)}, bf16[80,640]{1,0:T(8,128)(2,1)S(1)}, u32[]{:S(2)}, u32[]{:S(2)}) collective-permute-start(bf16[80,640]{1,0:T(8,128)(2,1)S(1)} %get-tuple-element.58), channel_id=1, source_target_pairs={{24,0},{0,8},{8,16},{16,24},{25,1},{1,9},{9,17},{17,25},{26,2},{2,... | collective-permute-start | bytes 307208 | tf_op jit(solution)/shard_map/ppermute | solution.py:26
  38.6 8.2 %collective-permute-start.10 = (bf16[80,640]{1,0:T(8,128)(2,1)S(1)}, bf16[80,640]{1,0:T(8,128)(2,1)S(1)}, u32[]{:S(2)}, u32[]{:S(2)}) collective-permute-start(bf16[80,640]{1,0:T(8,128)(2,1)S(1)} %get-tuple-element.59), channel_id=1, source_target_pairs={{8,0},{16,8},{24,16},{0,24},{9,1},{17,9},{25,17},{1,25},{10,2},{18... | collective-permute-start | bytes 307208 | tf_op jit(solution)/shard_map/ppermute | solution.py:26
  48.4 5.6 %collective-permute-start.14 = (bf16[160,640]{1,0:T(8,128)(2,1)S(1)}, bf16[160,640]{1,0:T(8,128)(2,1)S(1)}, u32[]{:S(2)}, u32[]{:S(2)}) collective-permute-start(bf16[160,640]{1,0:T(8,128)(2,1)S(1)} %get-tuple-element.61.refs_0_), channel_id=1, source_target_pairs={{2,0},{4,2},{6,4},{0,6},{3,1},{5,3},{7,5},{1,7},{10,8},{12,10},{14... | collective-permute-start | bytes 614408 | tf_op jit(solution)/shard_map/ppermute | solution.py:26
  48.4 11.8 %collective-permute-start.13 = (bf16[160,640]{1,0:T(8,128)(2,1)S(1)}, bf16[160,640]{1,0:T(8,128)(2,1)S(1)}, u32[]{:S(2)}, u32[]{:S(2)}) collective-permute-start(bf16[160,640]{1,0:T(8,128)(2,1)S(1)} %get-tuple-element.61.refs_0_), channel_id=1, source_target_pairs={{4,0},{6,2},{0,4},{2,6},{5,1},{7,3},{1,5},{3,7},{12,8},{14,10},{8,... | collective-permute-start | bytes 614408 | tf_op jit(solution)/shard_map/ppermute | solution.py:26
  50.0 10.2 %collective-permute-start.12 = (bf16[160,640]{1,0:T(8,128)(2,1)S(1)}, bf16[160,640]{1,0:T(8,128)(2,1)S(1)}, u32[]{:S(2)}, u32[]{:S(2)}) collective-permute-start(bf16[160,640]{1,0:T(8,128)(2,1)S(1)} %get-tuple-element.61.refs_0_), channel_id=1, source_target_pairs={{6,0},{0,2},{2,4},{4,6},{7,1},{1,3},{3,5},{5,7},{14,8},{8,10},{10,... | collective-permute-start | bytes 614408 | tf_op jit(solution)/shard_map/ppermute | solution.py:26
  50.2 32.0 %collective-permute-start.19 = (bf16[64,5120]{1,0:T(8,128)(2,1)S(1)}, bf16[64,5120]{1,0:T(8,128)(2,1)S(1)}, u32[]{:S(2)}, u32[]{:S(2)}) collective-permute-start(bf16[64,5120]{1,0:T(8,128)(2,1)S(1)} %get-tuple-element.70), channel_id=1, source_target_pairs={{16,0},{24,8},{0,16},{8,24},{17,1},{25,9},{1,17},{9,25},{18,2},{26... | collective-permute-start | bytes 1966088 | tf_op jit(solution)/shard_map/ppermute | solution.py:26
  52.5 16.7 %collective-permute-start.18 = (bf16[48,5120]{1,0:T(8,128)(2,1)S(1)}, bf16[48,5120]{1,0:T(8,128)(2,1)S(1)}, u32[]{:S(2)}, u32[]{:S(2)}) collective-permute-start(bf16[48,5120]{1,0:T(8,128)(2,1)S(1)} %get-tuple-element.69.refs_0_), channel_id=1, source_target_pairs={{1,0},{0,1},{3,2},{2,3},{5,4},{4,5},{7,6},{6,7},{9,8},{8,9},{11,10... | collective-permute-start | bytes 1474568 | tf_op jit(solution)/shard_map/ppermute | solution.py:26
  67.1 20.3 %collective-permute-start.21 = (bf16[48,6144]{1,0:T(8,128)(2,1)S(1)}, bf16[48,6144]{1,0:T(8,128)(2,1)S(1)}, u32[]{:S(2)}, u32[]{:S(2)}) collective-permute-start(bf16[48,6144]{1,0:T(8,128)(2,1)S(1)} %get-tuple-element.71.act.refs_2_.refs_4_.refs_6_), channel_id=1, source_target_pairs={{1,0},{0,1},{3,2},{2,3},{5,4},{4,5},{7,6},{6,7},{9,8},{8,9},{11,10... | collective-permute-start | bytes 1769480 | tf_op jit(solution)/shard_map/ppermute | solution.py:26
  68.7 3.2 %collective-permute-start.15 = (bf16[80,640]{1,0:T(8,128)(2,1)S(1)}, bf16[80,640]{1,0:T(8,128)(2,1)S(1)}, u32[]{:S(2)}, u32[]{:S(2)}) collective-permute-start(bf16[80,640]{1,0:T(8,128)(2,1)S(1)} %get-tuple-element.66), channel_id=1, source_target_pairs={{2,0},{4,2},{6,4},{0,6},{3,1},{5,3},{7,5},{1,7},{10,8},{12,10},{14... | collective-permute-start | bytes 307208 | tf_op jit(solution)/shard_map/ppermute | solution.py:26
  68.7 5.7 %collective-permute-start.16 = (bf16[80,640]{1,0:T(8,128)(2,1)S(1)}, bf16[80,640]{1,0:T(8,128)(2,1)S(1)}, u32[]{:S(2)}, u32[]{:S(2)}) collective-permute-start(bf16[80,640]{1,0:T(8,128)(2,1)S(1)} %get-tuple-element.67), channel_id=1, source_target_pairs={{4,0},{6,2},{0,4},{2,6},{5,1},{7,3},{1,5},{3,7},{12,8},{14,10},{8,... | collective-permute-start | bytes 307208 | tf_op jit(solution)/shard_map/ppermute | solution.py:26
  69.2 5.9 %collective-permute-start.17 = (bf16[80,640]{1,0:T(8,128)(2,1)S(1)}, bf16[80,640]{1,0:T(8,128)(2,1)S(1)}, u32[]{:S(2)}, u32[]{:S(2)}) collective-permute-start(bf16[80,640]{1,0:T(8,128)(2,1)S(1)} %get-tuple-element.68), channel_id=1, source_target_pairs={{6,0},{0,2},{2,4},{4,6},{7,1},{1,3},{3,5},{5,7},{14,8},{8,10},{10,... | collective-permute-start | bytes 307208 | tf_op jit(solution)/shard_map/ppermute | solution.py:26
  82.7 4.7 %collective-permute-start.20 = (bf16[80,640]{1,0:T(8,128)(2,1)S(1)}, bf16[80,640]{1,0:T(8,128)(2,1)S(1)}, u32[]{:S(2)}, u32[]{:S(2)}) collective-permute-start(bf16[80,640]{1,0:T(8,128)(2,1)S(1)} %shard_map.116), channel_id=1, source_target_pairs={{8,0},{16,8},{24,16},{0,24},{9,1},{17,9},{25,17},{1,25},{10,2},{18... | collective-permute-start | bytes 307208 | tf_op jit(solution)/shard_map/ppermute | solution.py:26
  88.8 65.0 %collective-permute-start.28 = (bf16[128,5120]{1,0:T(8,128)(2,1)S(1)}, bf16[128,5120]{1,0:T(8,128)(2,1)S(1)}, u32[]{:S(2)}, u32[]{:S(2)}) collective-permute-start(bf16[128,5120]{1,0:T(8,128)(2,1)S(1)} %get-tuple-element.80), channel_id=1, source_target_pairs={{16,0},{24,8},{0,16},{8,24},{17,1},{25,9},{1,17},{9,25},{18,2},{26... | collective-permute-start | bytes 3932168 | tf_op jit(solution)/shard_map/ppermute | solution.py:26
  89.7 16.4 %collective-permute-start.36 = (bf16[48,6144]{1,0:T(8,128)(2,1)S(1)}, bf16[48,6144]{1,0:T(8,128)(2,1)S(1)}, u32[]{:S(2)}, u32[]{:S(2)}) collective-permute-start(bf16[48,6144]{1,0:T(8,128)(2,1)S(1)} %get-tuple-element.89.refs_2_.refs_6_.refs_8_), channel_id=1, source_target_pairs={{1,0},{0,1},{3,2},{2,3},{5,4},{4,5},{7,6},{6,7},{9,8},{8,9},{11,10... | collective-permute-start | bytes 1769480 | tf_op jit(solution)/shard_map/ppermute | solution.py:26
  91.1 2.6 %collective-permute-start.24 = (bf16[80,640]{1,0:T(8,128)(2,1)S(1)}, bf16[80,640]{1,0:T(8,128)(2,1)S(1)}, u32[]{:S(2)}, u32[]{:S(2)}) collective-permute-start(bf16[80,640]{1,0:T(8,128)(2,1)S(1)} %get-tuple-element.72.refs_0_), channel_id=1, source_target_pairs={{2,0},{4,2},{6,4},{0,6},{3,1},{5,3},{7,5},{1,7},{10,8},{12,10},{14... | collective-permute-start | bytes 307208 | tf_op jit(solution)/shard_map/ppermute | solution.py:26
  91.2 6.8 %collective-permute-start.23 = (bf16[80,640]{1,0:T(8,128)(2,1)S(1)}, bf16[80,640]{1,0:T(8,128)(2,1)S(1)}, u32[]{:S(2)}, u32[]{:S(2)}) collective-permute-start(bf16[80,640]{1,0:T(8,128)(2,1)S(1)} %get-tuple-element.72.refs_0_), channel_id=1, source_target_pairs={{4,0},{6,2},{0,4},{2,6},{5,1},{7,3},{1,5},{3,7},{12,8},{14,10},{8,... | collective-permute-start | bytes 307208 | tf_op jit(solution)/shard_map/ppermute | solution.py:26
  92.3 5.9 %collective-permute-start.22 = (bf16[80,640]{1,0:T(8,128)(2,1)S(1)}, bf16[80,640]{1,0:T(8,128)(2,1)S(1)}, u32[]{:S(2)}, u32[]{:S(2)}) collective-permute-start(bf16[80,640]{1,0:T(8,128)(2,1)S(1)} %get-tuple-element.72.refs_0_), channel_id=1, source_target_pairs={{6,0},{0,2},{2,4},{4,6},{7,1},{1,3},{3,5},{5,7},{14,8},{8,10},{10,... | collective-permute-start | bytes 307208 | tf_op jit(solution)/shard_map/ppermute | solution.py:26
  98.4 35.0 %collective-permute-start.35 = (bf16[48,5120]{1,0:T(8,128)(2,1)S(1)}, bf16[48,5120]{1,0:T(8,128)(2,1)S(1)}, u32[]{:S(2)}, u32[]{:S(2)}) collective-permute-start(bf16[48,5120]{1,0:T(8,128)(2,1)S(1)} %shard_map.118.refs_0_), channel_id=1, source_target_pairs={{1,0},{0,1},{3,2},{2,3},{5,4},{4,5},{7,6},{6,7},{9,8},{8,9},{11,10... | collective-permute-start | bytes 1474568 | tf_op jit(solution)/shard_map/ppermute | solution.py:26
  105.0 11.4 %collective-permute-start.31 = (bf16[80,640]{1,0:T(8,128)(2,1)S(1)}, bf16[80,640]{1,0:T(8,128)(2,1)S(1)}, u32[]{:S(2)}, u32[]{:S(2)}) collective-permute-start(bf16[80,640]{1,0:T(8,128)(2,1)S(1)} %get-tuple-element.84), channel_id=1, source_target_pairs={{2,0},{4,2},{6,4},{0,6},{3,1},{5,3},{7,5},{1,7},{10,8},{12,10},{14... | collective-permute-start | bytes 307208 | tf_op jit(solution)/shard_map/ppermute | solution.py:26
  105.1 13.0 %collective-permute-start.32 = (bf16[80,640]{1,0:T(8,128)(2,1)S(1)}, bf16[80,640]{1,0:T(8,128)(2,1)S(1)}, u32[]{:S(2)}, u32[]{:S(2)}) collective-permute-start(bf16[80,640]{1,0:T(8,128)(2,1)S(1)} %get-tuple-element.85), channel_id=1, source_target_pairs={{4,0},{6,2},{0,4},{2,6},{5,1},{7,3},{1,5},{3,7},{12,8},{14,10},{8,... | collective-permute-start | bytes 307208 | tf_op jit(solution)/shard_map/ppermute | solution.py:26
  106.0 10.3 %collective-permute-start.37 = (bf16[48,1024]{1,0:T(8,128)(2,1)S(1)}, bf16[48,1024]{1,0:T(8,128)(2,1)S(1)}, u32[]{:S(2)}, u32[]{:S(2)}) collective-permute-start(bf16[48,1024]{1,0:T(8,128)(2,1)S(1)} %get-tuple-element.82._.refs_4_), channel_id=1, source_target_pairs={{1,0},{0,1},{3,2},{2,3},{5,4},{4,5},{7,6},{6,7},{9,8},{8,9},{11,10... | collective-permute-start | bytes 294920 | tf_op jit(solution)/shard_map/ppermute | solution.py:26
  116.4 4.1 %collective-permute-start.33 = (bf16[80,640]{1,0:T(8,128)(2,1)S(1)}, bf16[80,640]{1,0:T(8,128)(2,1)S(1)}, u32[]{:S(2)}, u32[]{:S(2)}) collective-permute-start(bf16[80,640]{1,0:T(8,128)(2,1)S(1)} %get-tuple-element.86), channel_id=1, source_target_pairs={{6,0},{0,2},{2,4},{4,6},{7,1},{1,3},{3,5},{5,7},{14,8},{8,10},{10,... | collective-permute-start | bytes 307208 | tf_op jit(solution)/shard_map/ppermute | solution.py:26
  116.4 5.0 %collective-permute-start.25 = (bf16[80,640]{1,0:T(8,128)(2,1)S(1)}, bf16[80,640]{1,0:T(8,128)(2,1)S(1)}, u32[]{:S(2)}, u32[]{:S(2)}) collective-permute-start(bf16[80,640]{1,0:T(8,128)(2,1)S(1)} %get-tuple-element.76), channel_id=1, source_target_pairs={{2,0},{4,2},{6,4},{0,6},{3,1},{5,3},{7,5},{1,7},{10,8},{12,10},{14... | collective-permute-start | bytes 307208 | tf_op jit(solution)/shard_map/ppermute | solution.py:26
  118.1 6.8 %collective-permute-start.26 = (bf16[80,640]{1,0:T(8,128)(2,1)S(1)}, bf16[80,640]{1,0:T(8,128)(2,1)S(1)}, u32[]{:S(2)}, u32[]{:S(2)}) collective-permute-start(bf16[80,640]{1,0:T(8,128)(2,1)S(1)} %get-tuple-element.77), channel_id=1, source_target_pairs={{4,0},{6,2},{0,4},{2,6},{5,1},{7,3},{1,5},{3,7},{12,8},{14,10},{8,... | collective-permute-start | bytes 307208 | tf_op jit(solution)/shard_map/ppermute | solution.py:26
  120.5 7.7 %collective-permute-start.27 = (bf16[80,640]{1,0:T(8,128)(2,1)S(1)}, bf16[80,640]{1,0:T(8,128)(2,1)S(1)}, u32[]{:S(2)}, u32[]{:S(2)}) collective-permute-start(bf16[80,640]{1,0:T(8,128)(2,1)S(1)} %get-tuple-element.78), channel_id=1, source_target_pairs={{6,0},{0,2},{2,4},{4,6},{7,1},{1,3},{3,5},{5,7},{14,8},{8,10},{10,... | collective-permute-start | bytes 307208 | tf_op jit(solution)/shard_map/ppermute | solution.py:26
  121.3 32.5 %collective-permute-start.29 = (bf16[80,640]{1,0:T(8,128)(2,1)S(1)}, bf16[80,640]{1,0:T(8,128)(2,1)S(1)}, u32[]{:S(2)}, u32[]{:S(2)}) collective-permute-start(bf16[80,640]{1,0:T(8,128)(2,1)S(1)} %get-tuple-element.81), channel_id=1, source_target_pairs={{16,0},{24,8},{0,16},{8,24},{17,1},{25,9},{1,17},{9,25},{18,2},{26... | collective-permute-start | bytes 307208 | tf_op jit(solution)/shard_map/ppermute | solution.py:26
  125.0 28.8 %collective-permute-start.34 = (bf16[80,640]{1,0:T(8,128)(2,1)S(1)}, bf16[80,640]{1,0:T(8,128)(2,1)S(1)}, u32[]{:S(2)}, u32[]{:S(2)}) collective-permute-start(bf16[80,640]{1,0:T(8,128)(2,1)S(1)} %shard_map.122), channel_id=1, source_target_pairs={{24,0},{0,8},{8,16},{16,24},{25,1},{1,9},{9,17},{17,25},{26,2},{2,... | collective-permute-start | bytes 307208 | tf_op jit(solution)/shard_map/ppermute | solution.py:26
  128.2 25.6 %collective-permute-start.30 = (s32[1,4,128]{2,1,0:T(4,128)S(1)}, s32[1,4,128]{2,1,0:T(4,128)S(1)}, u32[]{:S(2)}, u32[]{:S(2)}) collective-permute-start(s32[1,4,128]{2,1,0:T(4,128)S(1)} %get-tuple-element.93), channel_id=1, source_target_pairs={{16,0},{24,8},{0,16},{8,24},{17,1},{25,9},{1,17},{9,25},{18,2},{26... | collective-permute-start | bytes 6152 | tf_op jit(solution)/shard_map/ppermute | solution.py:26

commit v7 on v6

--- a/solution.py
+++ b/solution.py
@@ -10,7 +10,6 @@
 CAP = 10
 PACK = 8
 PACKED = CAP * PACK
-COT_PIECES = ((0, 48, 0, 8), (48, 64, 0, 8), (64, 128, 0, 8))
 TOK_PIECES = ((0, 128, 0, 8),)
 EPSILON = 1e-06
 F32 = jnp.float32
@@ -31,7 +30,7 @@
 
 
 def call(
-    kernel, outs, args, *, any_args=(), any_outs=(), scratch=(), vmem=VMEM_SMALL
+    kernel, outs, args, *, any_args=(), any_outs=(), scratch=(), vmem=VMEM_SMALL, aliases=None
 ):
     outs = [jax.ShapeDtypeStruct(*o) if isinstance(o, tuple) else o for o in outs]
     anywhere = pl.BlockSpec(memory_space=pl.ANY)
@@ -44,6 +43,7 @@
         scratch_shapes=list(scratch),
         compiler_params=pltpu.CompilerParams(vmem_limit_bytes=vmem),
         cost_estimate=pl.CostEstimate(flops=0, bytes_accessed=COST_BYTES, transcendentals=0),
+        input_output_aliases=aliases or {},
     )(*args)
 
 
@@ -154,38 +154,39 @@
     return copy
 
 
-def first_rows_kernel(tokens, routes, cotangent, raw, normed, piece, sem, sems, held):
-    copy = piece_copy(cotangent, COT_PIECES[0], piece, sem)
+def first_rows_kernel(tokens, routes_far, raw, normed, sems, held, routes):
+    fetch_routes = pltpu.make_async_copy(routes_far, routes, sems.at[PACK])
+    fetch_routes.start()
     fetches = []
     for c in range(PACK):
         k = columns(c, held.shape[1])
         fetches.append(pltpu.make_async_copy(tokens.at[:, k], held.at[:, k], sems.at[c]))
         fetches[-1].start()
+    fetch_routes.wait()
     select = select_of(routes[0])
     for fetch in fetches:
         fetch.wait()
     values = pick(select, whole_block(held))
     raw[...] = values.astype(BF16)
     normed[...] = (values * inv_rms_of(values)).astype(BF16)
-    copy.wait()
-
-
-def other_rows_kernel(
-    tokens, cotangent, next_routes, prev_routes, _, __, far, t1, cot, piece, sem
-):
-    copy = piece_copy(far, COT_PIECES[1], piece, sem)
-    cot[...] = pick(select_of(prev_routes[0]), whole_block(cotangent)).astype(BF16)
-    t1[...] = pick(select_of(next_routes[0]), whole_block(tokens)).astype(BF16)
-    copy.wait()
 
 
 def update0_kernel(n, *refs):
-    parts, (raw, routes, gates, next_routes, t1, upd, onward) = refs[:n], refs[n:]
+    parts, (raw, routes, gates, tokens, next_routes, upd, onward) = refs[:n], refs[n:]
     select = select_of(routes[0])
+    select_next = select_of(next_routes[0])
     weight = slot_gates(select, routes[0], gates[0])
     fresh = (raw[...].astype(F32) + weight * summed(parts)).astype(BF16)
-    onward[...] = merged(select_of(next_routes[0]), select, fresh, t1[...].astype(F32))
+    old = pick(select_next, whole_block(tokens))
+    onward[...] = merged(select_next, select, fresh, old)
     upd[...] = fresh
+
+
+def grad_rows_kernel(bulk, routes, gates, cot, scaled):
+    select = select_of(routes[1])
+    values = pick(select, whole_block(bulk))
+    cot[...] = values.astype(BF16)
+    scaled[...] = (slot_gates(select, routes[1], gates[1]) * values).astype(BF16)
 
 
 def update1_kernel(n, *refs):
@@ -195,13 +196,10 @@
     upd[...] = (h[...].astype(F32) + weight * summed(parts)).astype(BF16)
 
 
-def enter1_kernel(h, cot, routes, gates, cotangent, _, out, piece, sem):
-    copy = piece_copy(cotangent, COT_PIECES[2], piece, sem)
+def enter1_kernel(h, scaled, _, out, __):
     values = h[...].astype(F32)
     out[:PACKED] = (values * inv_rms_of(values)).astype(BF16)
-    weight = slot_gates(select_of(routes[1]), routes[1], gates[1])
-    out[PACKED:] = (weight * cot[...].astype(F32)).astype(BF16)
-    copy.wait()
+    out[PACKED:] = scaled[...]
 
 
 def state_grad(parts, h, c):
@@ -213,26 +211,30 @@
 
 
 def grad1_kernel(n, *refs):
-    parts, (h, cot, _, __, upd) = refs[:n], refs[n:]
+    parts, (h, cot, _, upd) = refs[:n], refs[n:]
     upd[...] = state_grad(parts, h[...], cot[...])
 
 
-def enter0_kernel(m, upd1, next_routes, routes, gates, *refs):
-    bulk, (tokens, _, c0, out, piece, sem) = refs[:m], refs[m:]
-    copy = piece_copy(tokens, TOK_PIECES[0], piece, sem)
+def enter0_kernel(upd1, next_routes, routes, gates, bulk, tokens, _, c0, out, *refs):
+    pieces, sems = refs[:-1], refs[-1]
+    copies = [
+        piece_copy(tokens, place, piece, sems.at[i])
+        for i, (place, piece) in enumerate(zip(TOK_PIECES, pieces))
+    ]
     select = select_of(routes[0])
-    old = pick(select, list(zip(bulk, COT_PIECES)))
+    old = pick(select, whole_block(bulk))
     rows = merged(select, select_of(next_routes[0]), upd1[...], old)
     c0[...] = rows
     out[...] = (slot_gates(select, routes[0], gates[0]) * rows.astype(F32)).astype(BF16)
-    copy.wait()
+    for copy in copies:
+        copy.wait()
 
 
 def finish_grad_kernel(n, *refs):
-    parts, (h, c, routes, upd1, next_routes, *bulk, out) = refs[:n], refs[n:]
+    parts, (h, c, routes, upd1, next_routes, bulk, out) = refs[:n], refs[n:]
     fresh = state_grad(parts, h[...], c[...])
     place_rows(
-        list(zip(bulk, COT_PIECES)),
+        whole_block(bulk),
         select_of(next_routes[0]),
         upd1[...],
         select_of(routes[0]),
@@ -241,9 +243,10 @@
     )
 
 
-def finish_state_kernel(bulk, upd0, prev2_routes, upd1, prev_routes, out):
+def finish_state_kernel(m, *refs):
+    bulk, (upd0, prev2_routes, upd1, prev_routes, out) = refs[:m], refs[m:]
     place_rows(
-        list(zip([bulk], TOK_PIECES)),
+        list(zip(bulk, TOK_PIECES)),
         select_of(prev2_routes[0]),
         upd0[...],
         select_of(prev_routes[0]),
@@ -488,6 +491,7 @@
     wide = ((rows, width + 2 * hidden), BF16)
     dma = [pltpu.SemaphoreType.DMA]
 
+    cot1_all = shifted(cotangent, "section", -1)
     next_routes = shifted(routes[1:], "section", -1)
     prev_routes = shifted(routes[1:], "section", 1)
     prev2_routes = shifted(routes[:1], "section", 2)
@@ -496,18 +500,20 @@
         r0, r1, c0, c1 = place
         return ((r1 - r0, (c1 - c0) * step), BF16)
 
-    cot_shapes = [shape_of(place) for place in COT_PIECES]
     tok_shapes = [shape_of(place) for place in TOK_PIECES]
 
-    raw0, normed0, piece = call(
+    raw0, normed0 = call(
         first_rows_kernel,
-        [one, one, cot_shapes[0]],
-        [tokens, routes, cotangent],
-        any_args=(0, 2),
-        scratch=[*dma, pltpu.SemaphoreType.DMA((PACK,)), pltpu.VMEM(tokens.shape, BF16)],
+        [one, one],
+        [tokens, routes],
+        any_args=(0, 1),
+        scratch=[
+            pltpu.SemaphoreType.DMA((PACK + 1,)),
+            pltpu.VMEM(tokens.shape, BF16),
+            pltpu.VMEM(routes.shape, jnp.int32),
+        ],
         vmem=VMEM_ALL,
     )
-    cot_parts = [shifted(piece, "section", -2)]
     blocks = from_group(normed0)
     x0, pre_gate0, pre_up0, act0, gate, up, down, *parts = call(
         part(forward_kernel, n),
@@ -520,33 +526,24 @@
         scratch=[pltpu.SemaphoreType.DMA((3, PACK)), unpacked, flat32, held],
         vmem=VMEM_LOAD,
     )
-    t1, cot1, piece = call(
-        other_rows_kernel,
-        [one, one, cot_shapes[1]],
-        [tokens, cotangent, next_routes, prev_routes, act0, cot_parts[0], cotangent],
-        any_args=(4, 5, 6),
-        any_outs=(2,),
-        scratch=dma,
-    )
-    cot1 = shifted(cot1, "section", -1)
     x0_all = copies_of(x0)
-    cot_parts.append(shifted(piece, "section", -2))
     parts = to_group(parts)
     upd0, h1 = call(
-        part(update0_kernel, n), [one, one], [*parts, raw0, routes, gates, next_routes, t1]
+        part(update0_kernel, n), [one, one], [*parts, raw0, routes, gates, tokens, next_routes]
     )
     h1 = shifted(h1, "section", 1)
+    cot1, scaled1 = call(grad_rows_kernel, [one, one], [cot1_all, routes, gates])
     upd0 = shifted(upd0, "section", 2)
 
-    enter1, piece = call(
+    enter1, cot1_all = call(
         enter1_kernel,
-        [((2 * PACKED, step), BF16), cot_shapes[2]],
-        [h1, cot1, routes, gates, cotangent, cot_parts[1]],
-        any_args=(4, 5),
+        [((2 * PACKED, step), BF16), (tokens.shape, BF16)],
+        [h1, scaled1, cot1_all],
+        any_args=(2,),
         any_outs=(1,),
-        scratch=dma,
-    )
-    cot_parts.append(shifted(piece, "section", -2))
+        aliases={2: 1},
+    )
+    cot0_all = shifted(cot1_all, "section", -1)
     blocks = from_group(enter1)
     x_act, g_grad1, *parts = call(
         part(tick1_kernel, n),
@@ -558,22 +555,21 @@
     (upd1,) = call(
         part(grad1_kernel, n),
         [one],
-        [*parts, h1, cot1, x0_all[-1], cot_parts[2]],
-        any_args=(n + 2, n + 3),
+        [*parts, h1, cot1, x0_all[-1]],
+        any_args=(n + 2,),
     )
     upd1 = shifted(upd1, "section", -1)
     x_act_all, g_grad1_all = copies_of(x_act), copies_of(g_grad1)
 
-    m = len(cot_parts)
-    c0, enter0, piece = call(
-        part(enter0_kernel, m),
-        [one, one, tok_shapes[0]],
-        [upd1, next_routes, routes, gates, *cot_parts, tokens, x_act_all[-1]],
-        any_args=(m + 4, m + 5),
-        any_outs=(2,),
-        scratch=dma,
-    )
-    tok_parts = [shifted(piece, "section", 2)]
+    c0, enter0, *pieces = call(
+        enter0_kernel,
+        [one, one, *tok_shapes],
+        [upd1, next_routes, routes, gates, cot0_all, tokens, x_act_all[-1]],
+        any_args=(5, 6),
+        any_outs=tuple(range(2, 2 + len(tok_shapes))),
+        scratch=[pltpu.SemaphoreType.DMA((len(tok_shapes),))],
+    )
+    tok_parts = [shifted(piece, "section", 2) for piece in pieces]
     blocks = from_group(enter0)
     (g0,) = call(
         part(gather0_kernel, n), [((rows, width), BF16)], blocks, scratch=[unpacked, flat32]
@@ -589,7 +585,7 @@
     (grad,) = call(
         part(finish_grad_kernel, n),
         [(tokens.shape, BF16)],
-        [*parts, raw0, c0, routes, upd1, next_routes, *cot_parts],
+        [*parts, raw0, c0, routes, upd1, next_routes, cot0_all],
     )
     outs = call(
         part(down_kernel, n),
@@ -606,7 +602,7 @@
         x_t, act_t, g0_all, g_grad1_all, copies_of(small0), width, hidden
     )
     (state,) = call(
-        finish_state_kernel,
+        part(finish_state_kernel, len(tok_parts)),
         [(tokens.shape, BF16)],
         [*tok_parts, upd0, prev2_routes, last1, prev_routes],
     )

time: 156 us -> 144 us (0.923)
  starting transfers between devices: 41.1 us -> 33.6 us
  waiting for transfers between devices: 69.9 us -> 66.9 us
  Pallas kernels: 43.3 us -> 41.2 us
    ppermute x38 -> x36, starting transfers between devices: 41.1 us -> 33.6 us  [shifted(): lax.ppermute(block, axis, [((i - distance) % size, i) for i in range(size)])]
    ppermute x38 -> x36, waiting for transfers between devices: 69.9 us -> 66.9 us  [shifted(): lax.ppermute(block, axis, [((i - distance) % size, i) for i in range(size)])]
    pallas_call x14, Pallas kernels: 32.3 us -> 30.2 us  [call(): pl.pallas_call(kernel, out_shape=outs, in_specs=[anywhere if i in any_arg...]
  transfers between devices with their start and end apart: 38 -> 36, of which waited for: 22 -> 18; matrix products, arithmetic and copies ran while one was open for 0% -> 0% of each run, Pallas kernels for 23% -> 26%
where the time goes in v7:
time: 144 us; the launch traced here: 143 us
  waiting for transfers between devices  66.9 us (46%)
  Pallas kernels  41.2 us (29%)
  starting transfers between devices  33.6 us (23%)
    ppermute x36, waiting for transfers between devices, shifted(): lax.ppermute(block, axis, [((i - distance) % size, i) for i in range(size)])  66.9 us
    ppermute x36, starting transfers between devices, shifted(): lax.ppermute(block, axis, [((i - distance) % size, i) for i in range(size)])  33.6 us
    pallas_call x14, Pallas kernels, call(): pl.pallas_call(kernel, out_shape=outs, in_specs=[anywhere if i in any_arg...  30.2 us
    pallas_call x2, Pallas kernels, chunked_call(): pl.pallas_call(kernel, grid=(PACK,), out_shape=[jax.ShapeDtypeStruct(s, B...  11 us
  transfers between devices with their start and end apart: 36, of which 18 were waited for; matrix products, arithmetic and copies ran while one was open for 0% of the time, Pallas kernels for 26%

profile of v7, /device:TPU:0, one launch (start us, length us, event | category | flops | bytes accessed | tf_op | source)
XLA Modules:
  0.0 143.4 jit_solution(9454275112169849244)
XLA Ops:
  0.6 5.1 %collective-permute-start.8 = (bf16[128,5120]{1,0:T(8,128)(2,1)}, bf16[128,5120]{1,0:T(8,128)(2,1)S(1)}, u32[]{:S(2)}, u32[]{:S(2)}) collective-permute-start(bf16[128,5120]{1,0:T(8,128)(2,1)} %param.8), channel_id=1, source_target_pairs={{8,0},{16,8},{24,16},{0,24},{9,1},{17,9},{25,17},{1,25},{10,2},{18... | collective-permute-start | bytes 3932168 | tf_op jit(solution)/shard_map/ppermute | solution.py:25
  5.7 2.9 %shard_map.110 = (bf16[80,640]{1,0:T(8,128)(2,1)}, bf16[80,640]{1,0:T(8,128)(2,1)}) custom-call(bf16[128,5120]{1,0:T(8,128)(2,1)} %tokens.3, s32[2,4,128]{2,1,0:T(4,128)} %bitcast.8), custom_call_target="tpu_custom_call" | custom-call | bytes 1024 | tf_op jit(solution)/shard_map/pallas_call | solution.py:38
  8.7 0.7 collective-permute-start.2
  9.4 0.9 collective-permute-start.1
  10.3 0.2 collective-permute-start
  10.5 2.2 %collective-permute-done.2.refs_3_ = bf16[80,640]{1,0:T(8,128)(2,1)S(1)} collective-permute-done((bf16[80,640]{1,0:T(8,128)(2,1)}, bf16[80,640]{1,0:T(8,128)(2,1)S(1)}, u32[]{:S(2)}, u32[]{:S(2)}) %collective-permute-start.2) | collective-permute-done | bytes 102432 | tf_op jit(solution)/shard_map/ppermute | solution.py:25
  12.7 3.7 %collective-permute-done.1.refs_2_ = bf16[80,640]{1,0:T(8,128)(2,1)S(1)} collective-permute-done((bf16[80,640]{1,0:T(8,128)(2,1)}, bf16[80,640]{1,0:T(8,128)(2,1)S(1)}, u32[]{:S(2)}, u32[]{:S(2)}) %collective-permute-start.1) | collective-permute-done | bytes 102432 | tf_op jit(solution)/shard_map/ppermute | solution.py:25
  16.4 0.9 copy-done.3
  17.3 6.5 %shard_map.111 = (bf16[48,5120]{1,0:T(8,128)(2,1)S(1)}, f32[48,512]{1,0:T(8,128)S(1)}, f32[48,512]{1,0:T(8,128)S(1)}, bf16[48,512]{1,0:T(8,128)(2,1)S(1)}, bf16[...) custom-call(bf16[80,640]{1,0:T(8,128)(2,1)S(1)} %copy-done.3, ...), custom_call_target="tpu_custom_call" | custom-call | bytes 1024 | tf_op jit(solution)/shard_map/pallas_call | solution.py:38
  23.9 1.2 collective-permute-start.4
  25.1 0.2 collective-permute-start.5
  25.3 0.5 collective-permute-start.6
  25.8 8.3 %collective-permute-done.6.refs_8_.next_routes = s32[1,4,128]{2,1,0:T(4,128)S(1)} collective-permute-done((s32[1,4,128]{2,1,0:T(4,128)S(1)}, s32[1,4,128]{2,1,0:T(4,128)S(1)}, u32[]{:S(2)}, u32[]{:S(2)}) %collective-permute-start.6) | collective-permute-done | bytes 2080 | tf_op jit(solution)/shard_map/ppermute | solution.py:25
  34.1 0.7 shard_map.112
  34.9 0.4 collective-permute-start.7
  35.3 0.5 shard_map.113
  35.8 6.0 %collective-permute-done.7.h.refs_4_ = bf16[80,640]{1,0:T(8,128)(2,1)S(1)} collective-permute-done((bf16[80,640]{1,0:T(8,128)(2,1)S(1)}, bf16[80,640]{1,0:T(8,128)(2,1)S(1)}, u32[]{:S(2)}, u32[]{:S(2)}) %collective-permute-start.7) | collective-permute-done | bytes 102432 | tf_op jit(solution)/shard_map/ppermute | solution.py:25
  41.8 0.3 shard_map.114
  42.1 2.0 %collective-permute-start.17 = (bf16[128,5120]{1,0:T(8,128)(2,1)S(1)}, bf16[128,5120]{1,0:T(8,128)(2,1)S(1)}, u32[]{:S(2)}, u32[]{:S(2)}) collective-permute-start(bf16[128,5120]{1,0:T(8,128)(2,1)S(1)} %get-tuple-element.66), channel_id=1, source_target_pairs={{8,0},{16,8},{24,16},{0,24},{9,1},{17,9},{25,17},{1,25},{10,2},{18... | collective-permute-start | bytes 3932168 | tf_op jit(solution)/shard_map/ppermute | solution.py:25
  44.2 1.5 %collective-permute-start.10 = (bf16[160,640]{1,0:T(8,128)(2,1)S(1)}, bf16[160,640]{1,0:T(8,128)(2,1)S(1)}, u32[]{:S(2)}, u32[]{:S(2)}) collective-permute-start(bf16[160,640]{1,0:T(8,128)(2,1)S(1)} %get-tuple-element.55.refs_0_), channel_id=1, source_target_pairs={{4,0},{6,2},{0,4},{2,6},{5,1},{7,3},{1,5},{3,7},{12,8},{14,10},{8,... | collective-permute-start | bytes 614408 | tf_op jit(solution)/shard_map/ppermute | solution.py:25
  45.7 0.2 collective-permute-start.9
  45.9 1.5 %collective-permute-start.15 = (bf16[48,5120]{1,0:T(8,128)(2,1)S(1)}, bf16[48,5120]{1,0:T(8,128)(2,1)S(1)}, u32[]{:S(2)}, u32[]{:S(2)}) collective-permute-start(bf16[48,5120]{1,0:T(8,128)(2,1)S(1)} %get-tuple-element.65.refs_0_), channel_id=1, source_target_pairs={{1,0},{0,1},{3,2},{2,3},{5,4},{4,5},{7,6},{6,7},{9,8},{8,9},{11,10... | collective-permute-start | bytes 1474568 | tf_op jit(solution)/shard_map/ppermute | solution.py:25
  47.4 1.1 collective-permute-done.11.refs_3_
  48.6 7.4 %collective-permute-done.10.refs_2_ = bf16[160,640]{1,0:T(8,128)(2,1)S(1)} collective-permute-done((bf16[160,640]{1,0:T(8,128)(2,1)S(1)}, bf16[160,640]{1,0:T(8,128)(2,1)S(1)}, u32[]{:S(2)}, u32[]{:S(2)}) %collective-permute-start.10) | collective-permute-done | bytes 204832 | tf_op jit(solution)/shard_map/ppermute | solution.py:25
  56.0 6.8 %shard_map.115 = (bf16[48,6144]{1,0:T(8,128)(2,1)S(1)}, bf16[48,6144]{1,0:T(8,128)(2,1)S(1)}, bf16[80,640]{1,0:T(8,128)(2,1)S(1)}, bf16[80,640]{1,0:T(8,128)(2,1...) custom-call(bf16[160,640]{1,0:T(8,128)(2,1)S(1)} %get-tuple-element.55.refs_0_, ...), custom_call_target="tpu_custom_call" | custom-call | bytes 1024 | tf_op jit(solution)/shard_map/pallas_call | solution.py:38
  62.8 1.6 %collective-permute-start.18 = (bf16[48,6144]{1,0:T(8,128)(2,1)S(1)}, bf16[48,6144]{1,0:T(8,128)(2,1)S(1)}, u32[]{:S(2)}, u32[]{:S(2)}) collective-permute-start(bf16[48,6144]{1,0:T(8,128)(2,1)S(1)} %get-tuple-element.67.act.refs_2_.refs_4_.refs_6_), channel_id=1, source_target_pairs={{1,0},{0,1},{3,2},{2,3},{5,4},{4,5},{7,6},{6,7},{9,8},{8,9},{11,10... | collective-permute-start | bytes 1769480 | tf_op jit(solution)/shard_map/ppermute | solution.py:25
  64.4 0.5 collective-permute-start.13
  64.9 0.2 collective-permute-start.14
  65.1 2.5 %collective-permute-done.12.refs_1_ = bf16[80,640]{1,0:T(8,128)(2,1)S(1)} collective-permute-done((bf16[80,640]{1,0:T(8,128)(2,1)S(1)}, bf16[80,640]{1,0:T(8,128)(2,1)S(1)}, u32[]{:S(2)}, u32[]{:S(2)}) %collective-permute-start.12) | collective-permute-done | bytes 102432 | tf_op jit(solution)/shard_map/ppermute | solution.py:25
  67.6 2.4 %collective-permute-done.13.refs_2_ = bf16[80,640]{1,0:T(8,128)(2,1)S(1)} collective-permute-done((bf16[80,640]{1,0:T(8,128)(2,1)S(1)}, bf16[80,640]{1,0:T(8,128)(2,1)S(1)}, u32[]{:S(2)}, u32[]{:S(2)}) %collective-permute-start.13) | collective-permute-done | bytes 102432 | tf_op jit(solution)/shard_map/ppermute | solution.py:25
  70.1 0.8 collective-permute-done.14.refs_3_
  70.8 0.4 shard_map.116
  71.3 0.1 collective-permute-start.16
  71.4 4.6 %collective-permute-done.16.upd1.refs_7_ = bf16[80,640]{1,0:T(8,128)(2,1)S(1)} collective-permute-done((bf16[80,640]{1,0:T(8,128)(2,1)S(1)}, bf16[80,640]{1,0:T(8,128)(2,1)S(1)}, u32[]{:S(2)}, u32[]{:S(2)}) %collective-permute-start.16) | collective-permute-done | bytes 102432 | tf_op jit(solution)/shard_map/ppermute | solution.py:25
  76.0 0.3 collective-permute-done.18._.refs_3_.refs_5_.refs_7_
  76.3 0.9 shard_map.117
  77.2 0.1 collective-permute-start.25
  77.2 1.6 %collective-permute-start.34 = (bf16[48,6144]{1,0:T(8,128)(2,1)S(1)}, bf16[48,6144]{1,0:T(8,128)(2,1)S(1)}, u32[]{:S(2)}, u32[]{:S(2)}) collective-permute-start(bf16[48,6144]{1,0:T(8,128)(2,1)S(1)} %get-tuple-element.85.refs_2_.refs_6_.refs_8_), channel_id=1, source_target_pairs={{1,0},{0,1},{3,2},{2,3},{5,4},{4,5},{7,6},{6,7},{9,8},{8,9},{11,10... | collective-permute-start | bytes 1769480 | tf_op jit(solution)/shard_map/ppermute | solution.py:25
  78.8 1.6 %collective-permute-start.20 = (bf16[80,640]{1,0:T(8,128)(2,1)S(1)}, bf16[80,640]{1,0:T(8,128)(2,1)S(1)}, u32[]{:S(2)}, u32[]{:S(2)}) collective-permute-start(bf16[80,640]{1,0:T(8,128)(2,1)S(1)} %get-tuple-element.68.refs_0_), channel_id=1, source_target_pairs={{4,0},{6,2},{0,4},{2,6},{5,1},{7,3},{1,5},{3,7},{12,8},{14,10},{8,... | collective-permute-start | bytes 307208 | tf_op jit(solution)/shard_map/ppermute | solution.py:25
  80.4 0.2 collective-permute-start.19
  80.6 0.5 collective-permute-done.21.refs_3_
  81.1 5.2 %collective-permute-done.20.refs_2_ = bf16[80,640]{1,0:T(8,128)(2,1)S(1)} collective-permute-done((bf16[80,640]{1,0:T(8,128)(2,1)S(1)}, bf16[80,640]{1,0:T(8,128)(2,1)S(1)}, u32[]{:S(2)}, u32[]{:S(2)}) %collective-permute-start.20) | collective-permute-done | bytes 102432 | tf_op jit(solution)/shard_map/ppermute | solution.py:25
  86.3 0.2 shard_map.118.refs_0_
  86.5 0.6 collective-permute-start.33
  87.1 4.9 %shard_map.119 = (bf16[48,1024]{1,0:T(8,128)(2,1)S(1)}, bf16[80,640]{1,0:T(8,128)(2,1)S(1)}, bf16[80,640]{1,0:T(8,128)(2,1)S(1)}, bf16[80,640]{1,0:T(8,128)(2,1)S(1)}, bf16[80,640]{1,0:T(8,128)(2,1)S(1)}) custom-call(bf16[48,5120]{1,0:T(8,128)(2,1)S(1)} %shard_map.118.refs_0_, f32[48,512]{1,0:T(8,128)S(1)} %get-tuple-element.69.refs_1_, ...), custom_call_target="tpu_custom_call" | custom-call | bytes 1024 | tf_op jit(solution)/shard_map/pallas_call | solution.py:38
  92.0 1.1 shard_map.121
  93.1 0.5 collective-permute-start.29
  93.7 1.5 %collective-permute-start.35 = (bf16[48,1024]{1,0:T(8,128)(2,1)S(1)}, bf16[48,1024]{1,0:T(8,128)(2,1)S(1)}, u32[]{:S(2)}, u32[]{:S(2)}) collective-permute-start(bf16[48,1024]{1,0:T(8,128)(2,1)S(1)} %get-tuple-element.78._.refs_4_), channel_id=1, source_target_pairs={{1,0},{0,1},{3,2},{2,3},{5,4},{4,5},{7,6},{6,7},{9,8},{8,9},{11,10... | collective-permute-start | bytes 294920 | tf_op jit(solution)/shard_map/ppermute | solution.py:25
  95.2 8.1 %collective-permute-done.35.refs_5_ = bf16[48,1024]{1,0:T(8,128)(2,1)S(1)} collective-permute-done((bf16[48,1024]{1,0:T(8,128)(2,1)S(1)}, bf16[48,1024]{1,0:T(8,128)(2,1)S(1)}, u32[]{:S(2)}, u32[]{:S(2)}) %collective-permute-start.35) | collective-permute-done | bytes 98336 | tf_op jit(solution)/shard_map/ppermute | solution.py:25
  103.3 1.7 %collective-permute-start.22 = (bf16[80,640]{1,0:T(8,128)(2,1)S(1)}, bf16[80,640]{1,0:T(8,128)(2,1)S(1)}, u32[]{:S(2)}, u32[]{:S(2)}) collective-permute-start(bf16[80,640]{1,0:T(8,128)(2,1)S(1)} %get-tuple-element.72), channel_id=1, source_target_pairs={{2,0},{4,2},{6,4},{0,6},{3,1},{5,3},{7,5},{1,7},{10,8},{12,10},{14... | collective-permute-start | bytes 307208 | tf_op jit(solution)/shard_map/ppermute | solution.py:25
  105.0 1.8 %collective-permute-start.23 = (bf16[80,640]{1,0:T(8,128)(2,1)S(1)}, bf16[80,640]{1,0:T(8,128)(2,1)S(1)}, u32[]{:S(2)}, u32[]{:S(2)}) collective-permute-start(bf16[80,640]{1,0:T(8,128)(2,1)S(1)} %get-tuple-element.73), channel_id=1, source_target_pairs={{4,0},{6,2},{0,4},{2,6},{5,1},{7,3},{1,5},{3,7},{12,8},{14,10},{8,... | collective-permute-start | bytes 307208 | tf_op jit(solution)/shard_map/ppermute | solution.py:25
  106.8 0.5 collective-permute-done.30.refs_3_
  107.4 0.2 shard_map.122
  107.6 0.6 collective-permute-done.22.refs_1_
  108.2 2.6 %collective-permute-start.26 = (bf16[80,640]{1,0:T(8,128)(2,1)S(1)}, bf16[80,640]{1,0:T(8,128)(2,1)S(1)}, u32[]{:S(2)}, u32[]{:S(2)}) collective-permute-start(bf16[80,640]{1,0:T(8,128)(2,1)S(1)} %get-tuple-element.77), channel_id=1, source_target_pairs={{16,0},{24,8},{0,16},{8,24},{17,1},{25,9},{1,17},{9,25},{18,2},{26... | collective-permute-start | bytes 307208 | tf_op jit(solution)/shard_map/ppermute | solution.py:25
  110.8 1.1 collective-permute-done.23.refs_2_
  111.8 1.0 collective-permute-start.31
  112.8 1.9 %collective-permute-start.27 = (s32[1,4,128]{2,1,0:T(4,128)S(1)}, s32[1,4,128]{2,1,0:T(4,128)S(1)}, u32[]{:S(2)}, u32[]{:S(2)}) collective-permute-start(s32[1,4,128]{2,1,0:T(4,128)S(1)} %get-tuple-element.89), channel_id=1, source_target_pairs={{16,0},{24,8},{0,16},{8,24},{17,1},{25,9},{1,17},{9,25},{18,2},{26... | collective-permute-start | bytes 6152 | tf_op jit(solution)/shard_map/ppermute | solution.py:25
  114.8 1.4 %collective-permute-start.32 = (s32[1,4,128]{2,1,0:T(4,128)S(1)}, s32[1,4,128]{2,1,0:T(4,128)S(1)}, u32[]{:S(2)}, u32[]{:S(2)}) collective-permute-start(s32[1,4,128]{2,1,0:T(4,128)S(1)} %get-tuple-element.90), channel_id=1, source_target_pairs={{24,0},{0,8},{8,16},{16,24},{25,1},{1,9},{9,17},{17,25},{26,2},{2,... | collective-permute-start | bytes 6152 | tf_op jit(solution)/shard_map/ppermute | solution.py:25
  116.2 2.4 %shard_map.124 = (bf16[5120,192]{1,0:T(8,128)(2,1)S(1)}, bf16[512,192]{1,0:T(8,128)(2,1)S(1)}) custom-call(bf16[48,5120]{1,0:T(8,128)(2,1)S(1)} %get-tuple-element.65.refs_0_, bf16[48,5120]{1,0:T(8,128)(2,1)S(1)} %collective-permute-done.15.refs_6_.refs_1_, bf16[48,6144]{1,0:T(8,128)(2,1)S(1)} %get-tuple-element.67.act.refs_2_.refs_4_.refs_6_, ...), custom_call_target="tpu_custom_call" | custom-call | bytes 1024 | tf_op jit(solution)/shard_map/pallas_call | solution.py:416
  118.7 2.4 %shard_map.120 = bf16[128,5120]{1,0:T(8,128)(2,1)} custom-call(bf16[80,640]{1,0:T(8,128)(2,1)S(1)} %get-tuple-element.71.refs_0_, bf16[80,640]{1,0:T(8,128)(2,1)S(1)} %collective-permute-done.22.refs_1_, bf16[80,640]{1,0:T(8,128)(2,1)S(1)} %collective-permute-done.23.refs_2_, bf16[80,640]{1,0:T(8,128)(2,1)S(1)} %collective-permute-done.24.refs_3_, ...), custom_call_target="tpu_custom_call" | custom-call | bytes 1024 | tf_op jit(solution)/shard_map/pallas_call | solution.py:38
  121.0 8.6 %shard_map.125 = (bf16[5120,512]{1,0:T(8,128)(2,1)}, bf16[5120,512]{1,0:T(8,128)(2,1)}, bf16[512,5120]{1,0:T(8,128)(2,1)}) custom-call(bf16[5120,192]{1,0:T(8,128)(2,1)S(1)} %get-tuple-element.83.x_t, bf16[512,192]{1,0:T(8,128)(2,1)S(1)} %get-tuple-element.84.act_t, bf16[48,5120]{1,0:T(8,128)(2,1)S(1)} %shard_map.118.refs_0_, ...), custom_call_target="tpu_custom_call" | custom-call | bytes 1024 | tf_op jit(solution)/shard_map/pallas_call | solution.py:416
  129.6 11.5 %collective-permute-done.27.refs_2_ = s32[1,4,128]{2,1,0:T(4,128)S(1)} collective-permute-done((s32[1,4,128]{2,1,0:T(4,128)S(1)}, s32[1,4,128]{2,1,0:T(4,128)S(1)}, u32[]{:S(2)}, u32[]{:S(2)}) %collective-permute-start.27) | collective-permute-done | bytes 2080 | tf_op jit(solution)/shard_map/ppermute | solution.py:25
  141.2 2.2 %shard_map.123 = bf16[128,5120]{1,0:T(8,128)(2,1)} custom-call(bf16[128,5120]{1,0:T(8,128)(2,1)S(1)} %collective-permute-done.25.refs_0_, bf16[80,640]{1,0:T(8,128)(2,1)S(1)} %collective-permute-done.26.refs_1_, s32[1,4,128]{2,1,0:T(4,128)S(1)} %collective-permute-done.27.refs_2_, bf16[80,640]{1,0:T(8,128)(2,1)S(1)} %collective-permute-done.31.refs_3_, ...), custom_call_target="tpu_custom_call" | custom-call | bytes 1024 | tf_op jit(solution)/shard_map/pallas_call | solution.py:38
  (35 shorter events, 0.3 us)
Async XLA Ops:
  0.6 34.7 %collective-permute-start.8 = (bf16[128,5120]{1,0:T(8,128)(2,1)}, bf16[128,5120]{1,0:T(8,128)(2,1)S(1)}, u32[]{:S(2)}, u32[]{:S(2)}) collective-permute-start(bf16[128,5120]{1,0:T(8,128)(2,1)} %param.8), channel_id=1, source_target_pairs={{8,0},{16,8},{24,16},{0,24},{9,1},{17,9},{25,17},{1,25},{10,2},{18... | collective-permute-start | bytes 3932168 | tf_op jit(solution)/shard_map/ppermute | solution.py:25
  8.7 4.0 %collective-permute-start.2 = (bf16[80,640]{1,0:T(8,128)(2,1)}, bf16[80,640]{1,0:T(8,128)(2,1)S(1)}, u32[]{:S(2)}, u32[]{:S(2)}) collective-permute-start(bf16[80,640]{1,0:T(8,128)(2,1)} %get-tuple-element.47.refs_0_), channel_id=1, source_target_pairs={{2,0},{4,2},{6,4},{0,6},{3,1},{5,3},{7,5},{1,7},{10,8},{12,10},{14... | collective-permute-start | bytes 307208 | tf_op jit(solution)/shard_map/ppermute | solution.py:25
  9.4 6.9 %collective-permute-start.1 = (bf16[80,640]{1,0:T(8,128)(2,1)}, bf16[80,640]{1,0:T(8,128)(2,1)S(1)}, u32[]{:S(2)}, u32[]{:S(2)}) collective-permute-start(bf16[80,640]{1,0:T(8,128)(2,1)} %get-tuple-element.47.refs_0_), channel_id=1, source_target_pairs={{4,0},{6,2},{0,4},{2,6},{5,1},{7,3},{1,5},{3,7},{12,8},{14,10},{8,... | collective-permute-start | bytes 307208 | tf_op jit(solution)/shard_map/ppermute | solution.py:25
  10.3 6.1 %collective-permute-start = (bf16[80,640]{1,0:T(8,128)(2,1)}, bf16[80,640]{1,0:T(8,128)(2,1)S(1)}, u32[]{:S(2)}, u32[]{:S(2)}) collective-permute-start(bf16[80,640]{1,0:T(8,128)(2,1)} %get-tuple-element.47.refs_0_), channel_id=1, source_target_pairs={{6,0},{0,2},{2,4},{4,6},{7,1},{1,3},{3,5},{5,7},{14,8},{8,10},{10,... | collective-permute-start | bytes 307208 | tf_op jit(solution)/shard_map/ppermute | solution.py:25
  16.4 0.9 copy-start.3
  17.3 8.0 %copy-start.2 = (s32[2,128,4]{1,2,0:T(4,128)S(1)}, s32[2,128,4]{1,2,0:T(4,128)}, u32[]{:S(2)}) copy-start(s32[2,128,4]{1,2,0:T(4,128)} %param.12) | copy-start | bytes 12292
  17.3 16.9 %copy-start = (bf16[128,5120]{1,0:T(8,128)(2,1)S(1)}, bf16[128,5120]{1,0:T(8,128)(2,1)}, u32[]{:S(2)}) copy-start(bf16[128,5120]{1,0:T(8,128)(2,1)} %tokens.3) | copy-start | bytes 3932164
  17.3 16.9 %copy-start.1 = (bf16[80,640]{1,0:T(8,128)(2,1)S(1)}, bf16[80,640]{1,0:T(8,128)(2,1)}, u32[]{:S(2)}) copy-start(bf16[80,640]{1,0:T(8,128)(2,1)} %get-tuple-element.52.refs_4_) | copy-start | bytes 307204
  17.3 16.9 %copy-start.4 = (f32[2,128,4]{1,2,0:T(4,128)S(1)}, f32[2,128,4]{1,2,0:T(4,128)}, u32[]{:S(2)}) copy-start(f32[2,128,4]{1,2,0:T(4,128)} %param.13) | copy-start | bytes 12292
  23.8 10.3 %collective-permute-start.3 = (bf16[80,640]{1,0:T(8,128)(2,1)S(1)}, bf16[80,640]{1,0:T(8,128)(2,1)S(1)}, u32[]{:S(2)}, u32[]{:S(2)}) collective-permute-start(bf16[80,640]{1,0:T(8,128)(2,1)S(1)} %get-tuple-element.49), channel_id=1, source_target_pairs={{2,0},{4,2},{6,4},{0,6},{3,1},{5,3},{7,5},{1,7},{10,8},{12,10},{14... | collective-permute-start | bytes 307208 | tf_op jit(solution)/shard_map/ppermute | solution.py:25
  23.9 10.2 %collective-permute-start.4 = (bf16[80,640]{1,0:T(8,128)(2,1)S(1)}, bf16[80,640]{1,0:T(8,128)(2,1)S(1)}, u32[]{:S(2)}, u32[]{:S(2)}) collective-permute-start(bf16[80,640]{1,0:T(8,128)(2,1)S(1)} %get-tuple-element.50), channel_id=1, source_target_pairs={{4,0},{6,2},{0,4},{2,6},{5,1},{7,3},{1,5},{3,7},{12,8},{14,10},{8,... | collective-permute-start | bytes 307208 | tf_op jit(solution)/shard_map/ppermute | solution.py:25
  25.1 9.0 %collective-permute-start.5 = (bf16[80,640]{1,0:T(8,128)(2,1)S(1)}, bf16[80,640]{1,0:T(8,128)(2,1)S(1)}, u32[]{:S(2)}, u32[]{:S(2)}) collective-permute-start(bf16[80,640]{1,0:T(8,128)(2,1)S(1)} %get-tuple-element.51), channel_id=1, source_target_pairs={{6,0},{0,2},{2,4},{4,6},{7,1},{1,3},{3,5},{5,7},{14,8},{8,10},{10,... | collective-permute-start | bytes 307208 | tf_op jit(solution)/shard_map/ppermute | solution.py:25
  25.3 8.8 %collective-permute-start.6 = (s32[1,4,128]{2,1,0:T(4,128)S(1)}, s32[1,4,128]{2,1,0:T(4,128)S(1)}, u32[]{:S(2)}, u32[]{:S(2)}) collective-permute-start(s32[1,4,128]{2,1,0:T(4,128)S(1)} %get-tuple-element.90), channel_id=1, source_target_pairs={{8,0},{16,8},{24,16},{0,24},{9,1},{17,9},{25,17},{1,25},{10,2},{18... | collective-permute-start | bytes 6152 | tf_op jit(solution)/shard_map/ppermute | solution.py:25
  34.9 6.9 %collective-permute-start.7 = (bf16[80,640]{1,0:T(8,128)(2,1)S(1)}, bf16[80,640]{1,0:T(8,128)(2,1)S(1)}, u32[]{:S(2)}, u32[]{:S(2)}) collective-permute-start(bf16[80,640]{1,0:T(8,128)(2,1)S(1)} %get-tuple-element.53), channel_id=1, source_target_pairs={{24,0},{0,8},{8,16},{16,24},{25,1},{1,9},{9,17},{17,25},{26,2},{2,... | collective-permute-start | bytes 307208 | tf_op jit(solution)/shard_map/ppermute | solution.py:25
  42.1 34.1 %collective-permute-start.17 = (bf16[128,5120]{1,0:T(8,128)(2,1)S(1)}, bf16[128,5120]{1,0:T(8,128)(2,1)S(1)}, u32[]{:S(2)}, u32[]{:S(2)}) collective-permute-start(bf16[128,5120]{1,0:T(8,128)(2,1)S(1)} %get-tuple-element.66), channel_id=1, source_target_pairs={{8,0},{16,8},{24,16},{0,24},{9,1},{17,9},{25,17},{1,25},{10,2},{18... | collective-permute-start | bytes 3932168 | tf_op jit(solution)/shard_map/ppermute | solution.py:25
  44.2 4.4 %collective-permute-start.11 = (bf16[160,640]{1,0:T(8,128)(2,1)S(1)}, bf16[160,640]{1,0:T(8,128)(2,1)S(1)}, u32[]{:S(2)}, u32[]{:S(2)}) collective-permute-start(bf16[160,640]{1,0:T(8,128)(2,1)S(1)} %get-tuple-element.55.refs_0_), channel_id=1, source_target_pairs={{2,0},{4,2},{6,4},{0,6},{3,1},{5,3},{7,5},{1,7},{10,8},{12,10},{14... | collective-permute-start | bytes 614408 | tf_op jit(solution)/shard_map/ppermute | solution.py:25
  44.2 11.8 %collective-permute-start.10 = (bf16[160,640]{1,0:T(8,128)(2,1)S(1)}, bf16[160,640]{1,0:T(8,128)(2,1)S(1)}, u32[]{:S(2)}, u32[]{:S(2)}) collective-permute-start(bf16[160,640]{1,0:T(8,128)(2,1)S(1)} %get-tuple-element.55.refs_0_), channel_id=1, source_target_pairs={{4,0},{6,2},{0,4},{2,6},{5,1},{7,3},{1,5},{3,7},{12,8},{14,10},{8,... | collective-permute-start | bytes 614408 | tf_op jit(solution)/shard_map/ppermute | solution.py:25
  45.7 10.3 %collective-permute-start.9 = (bf16[160,640]{1,0:T(8,128)(2,1)S(1)}, bf16[160,640]{1,0:T(8,128)(2,1)S(1)}, u32[]{:S(2)}, u32[]{:S(2)}) collective-permute-start(bf16[160,640]{1,0:T(8,128)(2,1)S(1)} %get-tuple-element.55.refs_0_), channel_id=1, source_target_pairs={{6,0},{0,2},{2,4},{4,6},{7,1},{1,3},{3,5},{5,7},{14,8},{8,10},{10,... | collective-permute-start | bytes 614408 | tf_op jit(solution)/shard_map/ppermute | solution.py:25
  45.9 19.0 %collective-permute-start.15 = (bf16[48,5120]{1,0:T(8,128)(2,1)S(1)}, bf16[48,5120]{1,0:T(8,128)(2,1)S(1)}, u32[]{:S(2)}, u32[]{:S(2)}) collective-permute-start(bf16[48,5120]{1,0:T(8,128)(2,1)S(1)} %get-tuple-element.65.refs_0_), channel_id=1, source_target_pairs={{1,0},{0,1},{3,2},{2,3},{5,4},{4,5},{7,6},{6,7},{9,8},{8,9},{11,10... | collective-permute-start | bytes 1474568 | tf_op jit(solution)/shard_map/ppermute | solution.py:25
  62.8 13.4 %collective-permute-start.18 = (bf16[48,6144]{1,0:T(8,128)(2,1)S(1)}, bf16[48,6144]{1,0:T(8,128)(2,1)S(1)}, u32[]{:S(2)}, u32[]{:S(2)}) collective-permute-start(bf16[48,6144]{1,0:T(8,128)(2,1)S(1)} %get-tuple-element.67.act.refs_2_.refs_4_.refs_6_), channel_id=1, source_target_pairs={{1,0},{0,1},{3,2},{2,3},{5,4},{4,5},{7,6},{6,7},{9,8},{8,9},{11,10... | collective-permute-start | bytes 1769480 | tf_op jit(solution)/shard_map/ppermute | solution.py:25
  64.4 3.2 %collective-permute-start.12 = (bf16[80,640]{1,0:T(8,128)(2,1)S(1)}, bf16[80,640]{1,0:T(8,128)(2,1)S(1)}, u32[]{:S(2)}, u32[]{:S(2)}) collective-permute-start(bf16[80,640]{1,0:T(8,128)(2,1)S(1)} %get-tuple-element.61), channel_id=1, source_target_pairs={{2,0},{4,2},{6,4},{0,6},{3,1},{5,3},{7,5},{1,7},{10,8},{12,10},{14... | collective-permute-start | bytes 307208 | tf_op jit(solution)/shard_map/ppermute | solution.py:25
  64.4 5.7 %collective-permute-start.13 = (bf16[80,640]{1,0:T(8,128)(2,1)S(1)}, bf16[80,640]{1,0:T(8,128)(2,1)S(1)}, u32[]{:S(2)}, u32[]{:S(2)}) collective-permute-start(bf16[80,640]{1,0:T(8,128)(2,1)S(1)} %get-tuple-element.62), channel_id=1, source_target_pairs={{4,0},{6,2},{0,4},{2,6},{5,1},{7,3},{1,5},{3,7},{12,8},{14,10},{8,... | collective-permute-start | bytes 307208 | tf_op jit(solution)/shard_map/ppermute | solution.py:25
  64.9 5.9 %collective-permute-start.14 = (bf16[80,640]{1,0:T(8,128)(2,1)S(1)}, bf16[80,640]{1,0:T(8,128)(2,1)S(1)}, u32[]{:S(2)}, u32[]{:S(2)}) collective-permute-start(bf16[80,640]{1,0:T(8,128)(2,1)S(1)} %get-tuple-element.63), channel_id=1, source_target_pairs={{6,0},{0,2},{2,4},{4,6},{7,1},{1,3},{3,5},{5,7},{14,8},{8,10},{10,... | collective-permute-start | bytes 307208 | tf_op jit(solution)/shard_map/ppermute | solution.py:25
  71.3 4.7 %collective-permute-start.16 = (bf16[80,640]{1,0:T(8,128)(2,1)S(1)}, bf16[80,640]{1,0:T(8,128)(2,1)S(1)}, u32[]{:S(2)}, u32[]{:S(2)}) collective-permute-start(bf16[80,640]{1,0:T(8,128)(2,1)S(1)} %shard_map.116), channel_id=1, source_target_pairs={{8,0},{16,8},{24,16},{0,24},{9,1},{17,9},{25,17},{1,25},{10,2},{18... | collective-permute-start | bytes 307208 | tf_op jit(solution)/shard_map/ppermute | solution.py:25
  77.2 64.0 %collective-permute-start.25 = (bf16[128,5120]{1,0:T(8,128)(2,1)S(1)}, bf16[128,5120]{1,0:T(8,128)(2,1)S(1)}, u32[]{:S(2)}, u32[]{:S(2)}) collective-permute-start(bf16[128,5120]{1,0:T(8,128)(2,1)S(1)} %get-tuple-element.76), channel_id=1, source_target_pairs={{16,0},{24,8},{0,16},{8,24},{17,1},{25,9},{1,17},{9,25},{18,2},{26... | collective-permute-start | bytes 3932168 | tf_op jit(solution)/shard_map/ppermute | solution.py:25
  77.2 16.4 %collective-permute-start.34 = (bf16[48,6144]{1,0:T(8,128)(2,1)S(1)}, bf16[48,6144]{1,0:T(8,128)(2,1)S(1)}, u32[]{:S(2)}, u32[]{:S(2)}) collective-permute-start(bf16[48,6144]{1,0:T(8,128)(2,1)S(1)} %get-tuple-element.85.refs_2_.refs_6_.refs_8_), channel_id=1, source_target_pairs={{1,0},{0,1},{3,2},{2,3},{5,4},{4,5},{7,6},{6,7},{9,8},{8,9},{11,10... | collective-permute-start | bytes 1769480 | tf_op jit(solution)/shard_map/ppermute | solution.py:25
  78.8 2.3 %collective-permute-start.21 = (bf16[80,640]{1,0:T(8,128)(2,1)S(1)}, bf16[80,640]{1,0:T(8,128)(2,1)S(1)}, u32[]{:S(2)}, u32[]{:S(2)}) collective-permute-start(bf16[80,640]{1,0:T(8,128)(2,1)S(1)} %get-tuple-element.68.refs_0_), channel_id=1, source_target_pairs={{2,0},{4,2},{6,4},{0,6},{3,1},{5,3},{7,5},{1,7},{10,8},{12,10},{14... | collective-permute-start | bytes 307208 | tf_op jit(solution)/shard_map/ppermute | solution.py:25
  78.8 7.5 %collective-permute-start.20 = (bf16[80,640]{1,0:T(8,128)(2,1)S(1)}, bf16[80,640]{1,0:T(8,128)(2,1)S(1)}, u32[]{:S(2)}, u32[]{:S(2)}) collective-permute-start(bf16[80,640]{1,0:T(8,128)(2,1)S(1)} %get-tuple-element.68.refs_0_), channel_id=1, source_target_pairs={{4,0},{6,2},{0,4},{2,6},{5,1},{7,3},{1,5},{3,7},{12,8},{14,10},{8,... | collective-permute-start | bytes 307208 | tf_op jit(solution)/shard_map/ppermute | solution.py:25
  80.4 5.9 %collective-permute-start.19 = (bf16[80,640]{1,0:T(8,128)(2,1)S(1)}, bf16[80,640]{1,0:T(8,128)(2,1)S(1)}, u32[]{:S(2)}, u32[]{:S(2)}) collective-permute-start(bf16[80,640]{1,0:T(8,128)(2,1)S(1)} %get-tuple-element.68.refs_0_), channel_id=1, source_target_pairs={{6,0},{0,2},{2,4},{4,6},{7,1},{1,3},{3,5},{5,7},{14,8},{8,10},{10,... | collective-permute-start | bytes 307208 | tf_op jit(solution)/shard_map/ppermute | solution.py:25
  86.5 28.3 %collective-permute-start.33 = (bf16[48,5120]{1,0:T(8,128)(2,1)S(1)}, bf16[48,5120]{1,0:T(8,128)(2,1)S(1)}, u32[]{:S(2)}, u32[]{:S(2)}) collective-permute-start(bf16[48,5120]{1,0:T(8,128)(2,1)S(1)} %shard_map.118.refs_0_), channel_id=1, source_target_pairs={{1,0},{0,1},{3,2},{2,3},{5,4},{4,5},{7,6},{6,7},{9,8},{8,9},{11,10... | collective-permute-start | bytes 1474568 | tf_op jit(solution)/shard_map/ppermute | solution.py:25
  93.1 10.2 %collective-permute-start.28 = (bf16[80,640]{1,0:T(8,128)(2,1)S(1)}, bf16[80,640]{1,0:T(8,128)(2,1)S(1)}, u32[]{:S(2)}, u32[]{:S(2)}) collective-permute-start(bf16[80,640]{1,0:T(8,128)(2,1)S(1)} %get-tuple-element.80), channel_id=1, source_target_pairs={{2,0},{4,2},{6,4},{0,6},{3,1},{5,3},{7,5},{1,7},{10,8},{12,10},{14... | collective-permute-start | bytes 307208 | tf_op jit(solution)/shard_map/ppermute | solution.py:25
  93.1 11.9 %collective-permute-start.29 = (bf16[80,640]{1,0:T(8,128)(2,1)S(1)}, bf16[80,640]{1,0:T(8,128)(2,1)S(1)}, u32[]{:S(2)}, u32[]{:S(2)}) collective-permute-start(bf16[80,640]{1,0:T(8,128)(2,1)S(1)} %get-tuple-element.81), channel_id=1, source_target_pairs={{4,0},{6,2},{0,4},{2,6},{5,1},{7,3},{1,5},{3,7},{12,8},{14,10},{8,... | collective-permute-start | bytes 307208 | tf_op jit(solution)/shard_map/ppermute | solution.py:25
  93.7 9.6 %collective-permute-start.35 = (bf16[48,1024]{1,0:T(8,128)(2,1)S(1)}, bf16[48,1024]{1,0:T(8,128)(2,1)S(1)}, u32[]{:S(2)}, u32[]{:S(2)}) collective-permute-start(bf16[48,1024]{1,0:T(8,128)(2,1)S(1)} %get-tuple-element.78._.refs_4_), channel_id=1, source_target_pairs={{1,0},{0,1},{3,2},{2,3},{5,4},{4,5},{7,6},{6,7},{9,8},{8,9},{11,10... | collective-permute-start | bytes 294920 | tf_op jit(solution)/shard_map/ppermute | solution.py:25
  103.3 4.1 %collective-permute-start.30 = (bf16[80,640]{1,0:T(8,128)(2,1)S(1)}, bf16[80,640]{1,0:T(8,128)(2,1)S(1)}, u32[]{:S(2)}, u32[]{:S(2)}) collective-permute-start(bf16[80,640]{1,0:T(8,128)(2,1)S(1)} %get-tuple-element.82), channel_id=1, source_target_pairs={{6,0},{0,2},{2,4},{4,6},{7,1},{1,3},{3,5},{5,7},{14,8},{8,10},{10,... | collective-permute-start | bytes 307208 | tf_op jit(solution)/shard_map/ppermute | solution.py:25
  103.3 5.0 %collective-permute-start.22 = (bf16[80,640]{1,0:T(8,128)(2,1)S(1)}, bf16[80,640]{1,0:T(8,128)(2,1)S(1)}, u32[]{:S(2)}, u32[]{:S(2)}) collective-permute-start(bf16[80,640]{1,0:T(8,128)(2,1)S(1)} %get-tuple-element.72), channel_id=1, source_target_pairs={{2,0},{4,2},{6,4},{0,6},{3,1},{5,3},{7,5},{1,7},{10,8},{12,10},{14... | collective-permute-start | bytes 307208 | tf_op jit(solution)/shard_map/ppermute | solution.py:25
  105.0 6.8 %collective-permute-start.23 = (bf16[80,640]{1,0:T(8,128)(2,1)S(1)}, bf16[80,640]{1,0:T(8,128)(2,1)S(1)}, u32[]{:S(2)}, u32[]{:S(2)}) collective-permute-start(bf16[80,640]{1,0:T(8,128)(2,1)S(1)} %get-tuple-element.73), channel_id=1, source_target_pairs={{4,0},{6,2},{0,4},{2,6},{5,1},{7,3},{1,5},{3,7},{12,8},{14,10},{8,... | collective-permute-start | bytes 307208 | tf_op jit(solution)/shard_map/ppermute | solution.py:25
  107.3 5.5 %collective-permute-start.24 = (bf16[80,640]{1,0:T(8,128)(2,1)S(1)}, bf16[80,640]{1,0:T(8,128)(2,1)S(1)}, u32[]{:S(2)}, u32[]{:S(2)}) collective-permute-start(bf16[80,640]{1,0:T(8,128)(2,1)S(1)} %get-tuple-element.74), channel_id=1, source_target_pairs={{6,0},{0,2},{2,4},{4,6},{7,1},{1,3},{3,5},{5,7},{14,8},{8,10},{10,... | collective-permute-start | bytes 307208 | tf_op jit(solution)/shard_map/ppermute | solution.py:25
  108.2 33.0 %collective-permute-start.26 = (bf16[80,640]{1,0:T(8,128)(2,1)S(1)}, bf16[80,640]{1,0:T(8,128)(2,1)S(1)}, u32[]{:S(2)}, u32[]{:S(2)}) collective-permute-start(bf16[80,640]{1,0:T(8,128)(2,1)S(1)} %get-tuple-element.77), channel_id=1, source_target_pairs={{16,0},{24,8},{0,16},{8,24},{17,1},{25,9},{1,17},{9,25},{18,2},{26... | collective-permute-start | bytes 307208 | tf_op jit(solution)/shard_map/ppermute | solution.py:25
  111.8 29.3 %collective-permute-start.31 = (bf16[80,640]{1,0:T(8,128)(2,1)S(1)}, bf16[80,640]{1,0:T(8,128)(2,1)S(1)}, u32[]{:S(2)}, u32[]{:S(2)}) collective-permute-start(bf16[80,640]{1,0:T(8,128)(2,1)S(1)} %shard_map.122), channel_id=1, source_target_pairs={{24,0},{0,8},{8,16},{16,24},{25,1},{1,9},{9,17},{17,25},{26,2},{2,... | collective-permute-start | bytes 307208 | tf_op jit(solution)/shard_map/ppermute | solution.py:25
  112.8 28.3 %collective-permute-start.27 = (s32[1,4,128]{2,1,0:T(4,128)S(1)}, s32[1,4,128]{2,1,0:T(4,128)S(1)}, u32[]{:S(2)}, u32[]{:S(2)}) collective-permute-start(s32[1,4,128]{2,1,0:T(4,128)S(1)} %get-tuple-element.89), channel_id=1, source_target_pairs={{16,0},{24,8},{0,16},{8,24},{17,1},{25,9},{1,17},{9,25},{18,2},{26... | collective-permute-start | bytes 6152 | tf_op jit(solution)/shard_map/ppermute | solution.py:25
  114.8 26.4 %collective-permute-start.32 = (s32[1,4,128]{2,1,0:T(4,128)S(1)}, s32[1,4,128]{2,1,0:T(4,128)S(1)}, u32[]{:S(2)}, u32[]{:S(2)}) collective-permute-start(s32[1,4,128]{2,1,0:T(4,128)S(1)} %get-tuple-element.90), channel_id=1, source_target_pairs={{24,0},{0,8},{8,16},{16,24},{25,1},{1,9},{9,17},{17,25},{26,2},{2,... | collective-permute-start | bytes 6152 | tf_op jit(solution)/shard_map/ppermute | solution.py:25

commit v8 on v7

--- a/solution.py
+++ b/solution.py
@@ -10,7 +10,6 @@
 CAP = 10
 PACK = 8
 PACKED = CAP * PACK
-TOK_PIECES = ((0, 128, 0, 8),)
 EPSILON = 1e-06
 F32 = jnp.float32
 BF16 = jnp.bfloat16
@@ -18,6 +17,7 @@
 VMEM_LOAD = 36 * 1024 * 1024
 VMEM_ALL = 60 * 1024 * 1024
 COST_BYTES = 1024
+EARLY = 1
 
 
 def shifted(block, axis, distance):
@@ -129,32 +129,17 @@
     return total
 
 
-def place_rows(pieces, first, rows1, second, rows2, out):
+def hit_rows(select):
     ones = jnp.ones((PACKED, 128), BF16)
-    hit1 = dot(chunk_of(first, 0), ones, 0, 0)[:, :1] > 0.5
-    hit2 = dot(chunk_of(second, 0), ones, 0, 0)[:, :1] > 0.5
-    width = out.shape[1] // PACK
-    for c in range(PACK):
-        new1 = dot(chunk_of(first, c), rows1, 0, 0)
-        new2 = dot(chunk_of(second, c), rows2, 0, 0)
-        for block, (r0, r1, c0, c1) in pieces:
-            if c0 <= c < c1:
-                old = block[:, (c - c0) * width : (c - c0 + 1) * width].astype(F32)
-                value = jnp.where(hit1[r0:r1], new1[r0:r1], old)
-                value = jnp.where(hit2[r0:r1], new2[r0:r1], value)
-                out[r0:r1, columns(c, out.shape[1])] = value.astype(BF16)
-
-
-def piece_copy(source, place, piece, sem):
-    r0, r1, c0, c1 = place
-    width = source.shape[1] // PACK
-    block = source.at[pl.ds(r0, r1 - r0), pl.ds(c0 * width, (c1 - c0) * width)]
-    copy = pltpu.make_async_copy(block, piece, sem)
-    copy.start()
-    return copy
-
-
-def first_rows_kernel(tokens, routes_far, raw, normed, sems, held, routes):
+    return dot(chunk_of(select, 0), ones, 0, 0)[:, :1] > 0.5
+
+
+def placed(c, old, first, hit1, rows1, second, hit2, rows2):
+    value = jnp.where(hit1, dot(chunk_of(first, c), rows1, 0, 0), old.astype(F32))
+    return jnp.where(hit2, dot(chunk_of(second, c), rows2, 0, 0), value).astype(BF16)
+
+
+def first_rows_kernel(tokens, routes_far, raw, normed, early, sems, held, routes):
     fetch_routes = pltpu.make_async_copy(routes_far, routes, sems.at[PACK])
     fetch_routes.start()
     fetches = []
@@ -169,6 +154,9 @@
     values = pick(select, whole_block(held))
     raw[...] = values.astype(BF16)
     normed[...] = (values * inv_rms_of(values)).astype(BF16)
+    height, width = held.shape
+    for c in range(EARLY):
+        early[c * height : (c + 1) * height] = held[:, columns(c, width)]
 
 
 def update0_kernel(n, *refs):
@@ -196,7 +184,7 @@
     upd[...] = (h[...].astype(F32) + weight * summed(parts)).astype(BF16)
 
 
-def enter1_kernel(h, scaled, _, out, __):
+def enter1_kernel(h, scaled, _, __, out, ___):
     values = h[...].astype(F32)
     out[:PACKED] = (values * inv_rms_of(values)).astype(BF16)
     out[PACKED:] = scaled[...]
@@ -211,48 +199,57 @@
 
 
 def grad1_kernel(n, *refs):
-    parts, (h, cot, _, upd) = refs[:n], refs[n:]
+    parts, (h, cot, upd) = refs[:n], refs[n:]
     upd[...] = state_grad(parts, h[...], cot[...])
 
 
-def enter0_kernel(upd1, next_routes, routes, gates, bulk, tokens, _, c0, out, *refs):
-    pieces, sems = refs[:-1], refs[-1]
-    copies = [
-        piece_copy(tokens, place, piece, sems.at[i])
-        for i, (place, piece) in enumerate(zip(TOK_PIECES, pieces))
-    ]
+def enter0_kernel(upd1, next_routes, routes, gates, bulk, tokens, c0, out, rest, sem):
+    step = tokens.shape[1] // PACK
+    copy = pltpu.make_async_copy(tokens.at[:, pl.ds(EARLY * step, (PACK - EARLY) * step)], rest, sem)
+    copy.start()
     select = select_of(routes[0])
     old = pick(select, whole_block(bulk))
     rows = merged(select, select_of(next_routes[0]), upd1[...], old)
     c0[...] = rows
     out[...] = (slot_gates(select, routes[0], gates[0]) * rows.astype(F32)).astype(BF16)
-    for copy in copies:
-        copy.wait()
+    copy.wait()
 
 
 def finish_grad_kernel(n, *refs):
     parts, (h, c, routes, upd1, next_routes, bulk, out) = refs[:n], refs[n:]
     fresh = state_grad(parts, h[...], c[...])
-    place_rows(
-        whole_block(bulk),
-        select_of(next_routes[0]),
-        upd1[...],
-        select_of(routes[0]),
-        fresh,
-        out,
-    )
-
-
-def finish_state_kernel(m, *refs):
-    bulk, (upd0, prev2_routes, upd1, prev_routes, out) = refs[:m], refs[m:]
-    place_rows(
-        list(zip(bulk, TOK_PIECES)),
-        select_of(prev2_routes[0]),
-        upd0[...],
-        select_of(prev_routes[0]),
-        upd1[...],
-        out,
-    )
+    first, second = select_of(next_routes[0]), select_of(routes[0])
+    hit1, hit2 = hit_rows(first), hit_rows(second)
+    for chunk in range(PACK):
+        k = columns(chunk, out.shape[1])
+        out[:, k] = placed(chunk, bulk[:, k], first, hit1, upd1[...], second, hit2, fresh)
+
+
+def finish_state_kernel(
+    early, rest, upd0, prev2_routes, upd1, prev_routes, out, ins, outs, in_sems, out_sems
+):
+    height, width = out.shape
+    fetches = []
+    for chunk in range(PACK - EARLY):
+        k = columns(chunk, width)
+        fetches.append(pltpu.make_async_copy(rest.at[:, k], ins.at[chunk], in_sems.at[chunk]))
+        fetches[-1].start()
+    first, second = select_of(prev2_routes[0]), select_of(prev_routes[0])
+    hit1, hit2 = hit_rows(first), hit_rows(second)
+    rows1, rows2 = upd0[...], upd1[...]
+    stores = []
+    for chunk in range(PACK):
+        if chunk < EARLY:
+            old = early[chunk * height : (chunk + 1) * height]
+        else:
+            fetches[chunk - EARLY].wait()
+            old = ins[chunk - EARLY]
+        outs[chunk] = placed(chunk, old, first, hit1, rows1, second, hit2, rows2)
+        k = columns(chunk, width)
+        stores.append(pltpu.make_async_copy(outs.at[chunk], out.at[:, k], out_sems.at[chunk]))
+        stores[-1].start()
+    for store in stores:
+        store.wait()
 
 
 def silu_grads(pre_gate, pre_up, grad_act):
@@ -336,7 +333,7 @@
 def down_kernel(n, act, down, _, *refs):
     parts, (unpacked, held) = refs[:n], refs[n:]
     hidden, width = down.shape
-    out_rows(act[:, width + hidden :], down, held, unpacked, parts)
+    out_rows(act[:, 3 * width + hidden : 3 * width + 2 * hidden], down, held, unpacked, parts)
 
 
 def back_rows(gg, gu, gate, up, held, unpacked, parts):
@@ -350,45 +347,45 @@
 
 
 def tick1_kernel(n, *refs):
-    blocks, (act0, gate, up, down) = refs[:n], refs[n : n + 4]
-    x_act, g_grad = refs[n + 4 : n + 6]
+    blocks, (x0, act0, gate, up, down) = refs[:n], refs[n : n + 5]
+    (kept,) = refs[n + 5 : n + 6]
     parts = refs[n + 6 : 2 * n + 6]
     unpacked, whole32, held, x, g = refs[2 * n + 6 :]
     gather_rows(blocks, 0, unpacked, whole32.at[0], x)
     gather_rows(blocks, PACKED, unpacked, whole32.at[1], g)
     width, hidden = gate.shape
-    x_act[:, :width] = x[...]
-    x_act[:, width : width + hidden] = act0[...]
-    g_grad[:, :width] = g[...]
+    kept[:, :width] = x0[...]
+    kept[:, width : 2 * width] = x[...]
+    kept[:, 2 * width : 3 * width] = g[...]
+    narrow = [slice(3 * width + i * hidden, 3 * width + (i + 1) * hidden) for i in range(4)]
+    kept[:, narrow[0]] = act0[...]
     acc_g = dot(x[...], gate[...])
     acc_u = dot(x[...], up[...])
     acc_a = dot(g[...], down[...], 1, 1)
     gg, gu = silu_grads(acc_g, acc_u, acc_a)
-    x_act[:, width + hidden :] = (acc_g * jax.nn.sigmoid(acc_g) * acc_u).astype(BF16)
+    kept[:, narrow[1]] = (acc_g * jax.nn.sigmoid(acc_g) * acc_u).astype(BF16)
+    kept[:, narrow[2]] = gg
+    kept[:, narrow[3]] = gu
+    back_rows(gg, gu, gate, up, held, unpacked, parts)
+
+
+def tick0_kernel(n, *refs):
+    blocks, (pre_gate, pre_up, gate, up, down) = refs[:n], refs[n : n + 5]
+    (g_grad,) = refs[n + 5 : n + 6]
+    parts = refs[n + 6 : 2 * n + 6]
+    unpacked, whole32, held, g = refs[2 * n + 6 :]
+    gather_rows(blocks, 0, unpacked, whole32, g)
+    width, hidden = gate.shape
+    g_grad[:, :width] = g[...]
+    acc_a = dot(g[...], down[...], 1, 1)
+    gg, gu = silu_grads(pre_gate[...], pre_up[...], acc_a)
     g_grad[:, width : width + hidden] = gg
     g_grad[:, width + hidden :] = gu
     back_rows(gg, gu, gate, up, held, unpacked, parts)
 
 
-def gather0_kernel(n, *refs):
-    blocks, (g, unpacked, whole32) = refs[:n], refs[n:]
-    gather_rows(blocks, 0, unpacked, whole32, g)
-
-
-def tick0_kernel(n, *refs):
-    g, pre_gate, pre_up, gate, up, down, small = refs[:7]
-    parts = refs[7 : n + 7]
-    unpacked, held = refs[n + 7 :]
-    hidden = gate.shape[1]
-    acc_a = dot(g[...], down[...], 1, 1)
-    gg, gu = silu_grads(pre_gate[...], pre_up[...], acc_a)
-    small[:, :hidden] = gg
-    small[:, hidden:] = gu
-    back_rows(gg, gu, gate, up, held, unpacked, parts)
-
-
 def whole_of(blocks):
-    return jnp.concatenate(blocks, axis=0)
+    return jnp.concatenate([b.astype(F32) for b in blocks], axis=0).astype(BF16)
 
 
 def turn_kernel(m, *refs):
@@ -401,24 +398,33 @@
         act_t[...] = whole_of([b[...] for b in act0 + act1]).T
 
 
-def weight_grad_kernel(m, x_t, act_t, *refs):
-    g0, g1, small0, gates1, ups1 = (refs[i * m : (i + 1) * m] for i in range(5))
-    gate_out, up_out, down_out = refs[5 * m :]
+def down_grad_kernel(m, act_t, *refs):
+    g0, g1, (down_out,) = refs[:m], refs[m : 2 * m], refs[2 * m :]
+    down_out[...] = dot(act_t[...], whole_of([b[...] for b in g0 + g1])).astype(BF16)
+
+
+def input_grad_kernel(m, x_t, *refs):
+    gates0, ups0, gates1, ups1 = (refs[i * m : (i + 1) * m] for i in range(4))
+    gate_out, up_out, both = refs[4 * m :]
     hidden = gate_out.shape[1]
-    gg = whole_of([b[:, :hidden] for b in small0] + [b[...] for b in gates1])
-    gu = whole_of([b[:, hidden:] for b in small0] + [b[...] for b in ups1])
-    gate_out[...] = dot(x_t[...], gg).astype(BF16)
-    up_out[...] = dot(x_t[...], gu).astype(BF16)
-    down_out[...] = dot(act_t[...], whole_of([b[...] for b in g0 + g1])).astype(BF16)
-
-
-def chunked_call(kernel, ins, outs):
+
+    @pl.when(pl.program_id(0) == 0)
+    def _():
+        both[:, :hidden] = whole_of([b[...] for b in gates0 + gates1])
+        both[:, hidden:] = whole_of([b[...] for b in ups0 + ups1])
+
+    gate_out[...] = dot(x_t[...], both[:, :hidden]).astype(BF16)
+    up_out[...] = dot(x_t[...], both[:, hidden:]).astype(BF16)
+
+
+def chunked_call(kernel, ins, outs, scratch=()):
     return pl.pallas_call(
         kernel,
         grid=(PACK,),
         out_shape=[jax.ShapeDtypeStruct(s, BF16) for s, _, _ in outs],
         in_specs=[pl.BlockSpec(block, index) for _, block, index in ins],
         out_specs=[pl.BlockSpec(block, index) for _, block, index in outs],
+        scratch_shapes=list(scratch),
         compiler_params=pltpu.CompilerParams(vmem_limit_bytes=VMEM_SMALL),
         cost_estimate=pl.CostEstimate(flops=0, bytes_accessed=COST_BYTES, transcendentals=0),
     )(*(a for a, _, _ in ins))
@@ -432,13 +438,13 @@
     return lambda c: (0, at + c)
 
 
-def turned(x0, x_act, width, hidden):
-    m = len(x_act)
-    rows = x_act[0].shape[0]
+def turned(kept, width, hidden):
+    m = len(kept)
+    rows = kept[0].shape[0]
     step = width // PACK
-    first = width // hidden
-    ins = [(a, (rows, step), chunk_at(0)) for a in x0 + x_act]
-    ins += [(a, (rows, hidden), constant(at)) for at in (first, first + 1) for a in x_act]
+    first = 3 * width // hidden
+    ins = [(a, (rows, step), chunk_at(at)) for at in (0, PACK) for a in kept]
+    ins += [(a, (rows, hidden), constant(at)) for at in (first, first + 1) for a in kept]
     outs = [
         ((width, 2 * m * rows), (step, 2 * m * rows), lambda c: (c, 0)),
         ((hidden, 2 * m * rows), (hidden, 2 * m * rows), lambda c: (0, 0)),
@@ -446,18 +452,27 @@
     return chunked_call(functools.partial(turn_kernel, m), ins, outs)
 
 
-def weight_grads(x_t, act_t, g0, g_grad1, small0, width, hidden):
-    m = len(g0)
-    rows = g0[0].shape[0]
+def down_grads(act_t, g_grad0, kept, width, hidden):
+    rows = kept[0].shape[0]
     step = width // PACK
-    first = width // hidden
-    ins = [(x_t, (step, x_t.shape[1]), lambda c: (c, 0)), (act_t, act_t.shape, constant(0))]
-    ins += [(a, (rows, step), chunk_at(0)) for a in g0 + g_grad1]
-    ins += [(a, a.shape, constant(0)) for a in small0]
-    ins += [(a, (rows, hidden), constant(at)) for at in (first, first + 1) for a in g_grad1]
+    ins = [(act_t, act_t.shape, constant(0))]
+    ins += [(a, (rows, step), chunk_at(0)) for a in g_grad0]
+    ins += [(a, (rows, step), chunk_at(2 * PACK)) for a in kept]
+    outs = [((hidden, width), (hidden, step), chunk_at(0))]
+    return chunked_call(functools.partial(down_grad_kernel, len(kept)), ins, outs)
+
+
+def input_grads(x_t, g_grad0, kept, width, hidden):
+    m = len(kept)
+    rows = kept[0].shape[0]
+    step = width // PACK
+    first, second = width // hidden, 3 * width // hidden + 2
+    ins = [(x_t, (step, x_t.shape[1]), lambda c: (c, 0))]
+    ins += [(a, (rows, hidden), constant(at)) for at in (first, first + 1) for a in g_grad0]
+    ins += [(a, (rows, hidden), constant(at)) for at in (second, second + 1) for a in kept]
     tall = ((width, hidden), (step, hidden), lambda c: (c, 0))
-    outs = [tall, tall, ((hidden, width), (hidden, step), chunk_at(0))]
-    return chunked_call(functools.partial(weight_grad_kernel, m), ins, outs)
+    scratch = [pltpu.VMEM((2 * m * rows, 2 * hidden), BF16)]
+    return chunked_call(functools.partial(input_grad_kernel, m), ins, [tall, tall], scratch)
 
 
 def from_group(block):
@@ -479,7 +494,7 @@
     width, hidden = gate.shape
     step = width // PACK
     n = lax.axis_size("expert")
-    rows = -(-n * CAP // 16) * 16
+    rows = -(-n * CAP // 8) * 8
     routes = jnp.transpose(routes, (0, 2, 1))
     gates = jnp.transpose(gates, (0, 2, 1))
     one = ((PACKED, step), BF16)
@@ -496,15 +511,9 @@
     prev_routes = shifted(routes[1:], "section", 1)
     prev2_routes = shifted(routes[:1], "section", 2)
 
-    def shape_of(place):
-        r0, r1, c0, c1 = place
-        return ((r1 - r0, (c1 - c0) * step), BF16)
-
-    tok_shapes = [shape_of(place) for place in TOK_PIECES]
-
-    raw0, normed0 = call(
+    raw0, normed0, early = call(
         first_rows_kernel,
-        [one, one],
+        [pltpu.VMEM(*one), pltpu.VMEM(*one), pltpu.VMEM((EARLY * tokens.shape[0], step), BF16)],
         [tokens, routes],
         any_args=(0, 1),
         scratch=[
@@ -514,6 +523,7 @@
         ],
         vmem=VMEM_ALL,
     )
+    early = shifted(early, "section", 2)
     blocks = from_group(normed0)
     x0, pre_gate0, pre_up0, act0, gate, up, down, *parts = call(
         part(forward_kernel, n),
@@ -526,7 +536,6 @@
         scratch=[pltpu.SemaphoreType.DMA((3, PACK)), unpacked, flat32, held],
         vmem=VMEM_LOAD,
     )
-    x0_all = copies_of(x0)
     parts = to_group(parts)
     upd0, h1 = call(
         part(update0_kernel, n), [one, one], [*parts, raw0, routes, gates, tokens, next_routes]
@@ -538,50 +547,46 @@
     enter1, cot1_all = call(
         enter1_kernel,
         [((2 * PACKED, step), BF16), (tokens.shape, BF16)],
-        [h1, scaled1, cot1_all],
-        any_args=(2,),
+        [h1, scaled1, cot1_all, early],
+        any_args=(2, 3),
         any_outs=(1,),
         aliases={2: 1},
     )
     cot0_all = shifted(cot1_all, "section", -1)
     blocks = from_group(enter1)
-    x_act, g_grad1, *parts = call(
+    kept, *parts = call(
         part(tick1_kernel, n),
-        [wide, wide] + [one] * n,
-        [*blocks, act0, gate, up, down],
+        [((rows, 3 * width + 4 * hidden), BF16)] + [one] * n,
+        [*blocks, x0, act0, gate, up, down],
         scratch=[unpacked, pltpu.VMEM((2, rows, width), F32), held, flat, flat],
     )
     parts = to_group(parts)
     (upd1,) = call(
         part(grad1_kernel, n),
         [one],
-        [*parts, h1, cot1, x0_all[-1]],
-        any_args=(n + 2,),
+        [*parts, h1, cot1],
     )
     upd1 = shifted(upd1, "section", -1)
-    x_act_all, g_grad1_all = copies_of(x_act), copies_of(g_grad1)
-
-    c0, enter0, *pieces = call(
+    kept_all = copies_of(kept)
+
+    c0, enter0, rest = call(
         enter0_kernel,
-        [one, one, *tok_shapes],
-        [upd1, next_routes, routes, gates, cot0_all, tokens, x_act_all[-1]],
-        any_args=(5, 6),
-        any_outs=tuple(range(2, 2 + len(tok_shapes))),
-        scratch=[pltpu.SemaphoreType.DMA((len(tok_shapes),))],
-    )
-    tok_parts = [shifted(piece, "section", 2) for piece in pieces]
+        [one, one, ((tokens.shape[0], width - EARLY * step), BF16)],
+        [upd1, next_routes, routes, gates, cot0_all, tokens],
+        any_args=(5,),
+        any_outs=(2,),
+        scratch=[pltpu.SemaphoreType.DMA],
+    )
+    rest = shifted(rest, "section", 2)
     blocks = from_group(enter0)
-    (g0,) = call(
-        part(gather0_kernel, n), [((rows, width), BF16)], blocks, scratch=[unpacked, flat32]
-    )
-    g0_all = copies_of(g0)
-    small0, *parts = call(
+    g_grad0, *parts = call(
         part(tick0_kernel, n),
-        [((rows, 2 * hidden), BF16)] + [one] * n,
-        [g0, pre_gate0, pre_up0, gate, up, down],
-        scratch=[unpacked, held],
+        [wide] + [one] * n,
+        [*blocks, pre_gate0, pre_up0, gate, up, down],
+        scratch=[unpacked, flat32, held, flat],
     )
     parts = to_group(parts)
+    g_grad0_all = copies_of(g_grad0)
     (grad,) = call(
         part(finish_grad_kernel, n),
         [(tokens.shape, BF16)],
@@ -590,21 +595,29 @@
     outs = call(
         part(down_kernel, n),
         [one] * n,
-        [x_act, down, small0],
+        [kept, down, g_grad0],
         any_args=(2,),
         scratch=[unpacked, held],
     )
     outs = to_group(outs)
     (last1,) = call(part(update1_kernel, n), [one], [*outs, h1, routes, gates])
     last1 = shifted(last1, "section", 1)
-    x_t, act_t = turned(x0_all, x_act_all, width, hidden)
-    gate_out, up_out, down_out = weight_grads(
-        x_t, act_t, g0_all, g_grad1_all, copies_of(small0), width, hidden
-    )
+    x_t, act_t = turned(kept_all, width, hidden)
+    (down_out,) = down_grads(act_t, g_grad0_all, kept_all, width, hidden)
+    gate_out, up_out = input_grads(x_t, g_grad0_all, kept_all, width, hidden)
+    chunks = pltpu.VMEM((PACK, tokens.shape[0], step), BF16)
     (state,) = call(
-        part(finish_state_kernel, len(tok_parts)),
+        finish_state_kernel,
         [(tokens.shape, BF16)],
-        [*tok_parts, upd0, prev2_routes, last1, prev_routes],
+        [early, rest, upd0, prev2_routes, last1, prev_routes],
+        any_args=(1,),
+        any_outs=(0,),
+        scratch=[
+            chunks,
+            chunks,
+            pltpu.SemaphoreType.DMA((PACK,)),
+            pltpu.SemaphoreType.DMA((PACK,)),
+        ],
     )
     return (grad, state, gate_out[None], up_out[None], down_out[None])
 

time: 144 us -> 142 us (0.986)
  waiting for transfers between devices: 66.9 us -> 53.5 us
  starting transfers between devices: 33.6 us -> 40.8 us
  Pallas kernels: 41.2 us -> 45.7 us
    ppermute x36 -> x34, waiting for transfers between devices: 66.9 us -> 53.5 us  [shifted(): lax.ppermute(block, axis, [((i - distance) % size, i) for i in range(size)])]
    ppermute x36 -> x34, starting transfers between devices: 33.6 us -> 40.8 us  [shifted(): lax.ppermute(block, axis, [((i - distance) % size, i) for i in range(size)])]
    pallas_call x2 -> x3, Pallas kernels: 11 us -> 15 us  [chunked_call(): pl.pallas_call(kernel, grid=(PACK,), out_shape=[jax.ShapeDtypeStruct(s, B...]
    pallas_call x14 -> x13, Pallas kernels: 30.2 us -> 30.7 us  [call(): pl.pallas_call(kernel, out_shape=outs, in_specs=[anywhere if i in any_arg...]
  transfers between devices with their start and end apart: 36 -> 34, of which waited for: 18 -> 20; matrix products, arithmetic and copies ran while one was open for 0% -> 0% of each run, Pallas kernels for 26% -> 30%
where the time goes in v8:
time: 142 us
  waiting for transfers between devices  53.5 us (38%)
  Pallas kernels  45.7 us (32%)
  starting transfers between devices  40.8 us (29%)
    ppermute x34, waiting for transfers between devices, shifted(): lax.ppermute(block, axis, [((i - distance) % size, i) for i in range(size)])  53.5 us
    ppermute x34, starting transfers between devices, shifted(): lax.ppermute(block, axis, [((i - distance) % size, i) for i in range(size)])  40.8 us
    pallas_call x13, Pallas kernels, call(): pl.pallas_call(kernel, out_shape=outs, in_specs=[anywhere if i in any_arg...  30.7 us
    pallas_call x3, Pallas kernels, chunked_call(): pl.pallas_call(kernel, grid=(PACK,), out_shape=[jax.ShapeDtypeStruct(s, B...  15 us
  transfers between devices with their start and end apart: 34, of which 20 were waited for; matrix products, arithmetic and copies ran while one was open for 0% of the time, Pallas kernels for 30%

profile of v8, /device:TPU:0, one launch (start us, length us, event | category | flops | bytes accessed | tf_op | source)
XLA Modules:
  0.0 141.7 jit_solution(17752204685869161826)
XLA Ops:
  0.6 5.1 %collective-permute-start.8 = (bf16[128,5120]{1,0:T(8,128)(2,1)}, bf16[128,5120]{1,0:T(8,128)(2,1)S(1)}, u32[]{:S(2)}, u32[]{:S(2)}) collective-permute-start(bf16[128,5120]{1,0:T(8,128)(2,1)} %param.8), channel_id=1, source_target_pairs={{8,0},{16,8},{24,16},{0,24},{9,1},{17,9},{25,17},{1,25},{10,2},{18... | collective-permute-start | bytes 3932168 | tf_op jit(solution)/shard_map/ppermute | solution.py:25
  5.7 2.3 %shard_map.110 = (bf16[80,640]{1,0:T(8,128)(2,1)S(1)}, bf16[80,640]{1,0:T(8,128)(2,1)S(1)}, bf16[128,640]{1,0:T(8,128)(2,1)S(1)}) custom-call(bf16[128,5120]{1,0:T(8,128)(2,1)} %tokens.3, s32[2,4,128]{2,1,0:T(4,128)} %bitcast.8), custom_call_target="tpu_custom_call" | custom-call | bytes 1024 | tf_op jit(solution)/shard_map/pallas_call | solution.py:38
  8.0 0.7 copy-done.3
  8.7 1.5 %collective-permute-start.1 = (bf16[80,640]{1,0:T(8,128)(2,1)S(1)}, bf16[80,640]{1,0:T(8,128)(2,1)S(1)}, u32[]{:S(2)}, u32[]{:S(2)}) collective-permute-start(bf16[80,640]{1,0:T(8,128)(2,1)S(1)} %get-tuple-element.46.refs_0_), channel_id=1, source_target_pairs={{4,0},{6,2},{0,4},{2,6},{5,1},{7,3},{1,5},{3,7},{12,8},{14,10},{8,... | collective-permute-start | bytes 307208 | tf_op jit(solution)/shard_map/ppermute | solution.py:25
  10.2 1.4 %collective-permute-start.2 = (bf16[80,640]{1,0:T(8,128)(2,1)S(1)}, bf16[80,640]{1,0:T(8,128)(2,1)S(1)}, u32[]{:S(2)}, u32[]{:S(2)}) collective-permute-start(bf16[80,640]{1,0:T(8,128)(2,1)S(1)} %get-tuple-element.46.refs_0_), channel_id=1, source_target_pairs={{2,0},{4,2},{6,4},{0,6},{3,1},{5,3},{7,5},{1,7},{10,8},{12,10},{14... | collective-permute-start | bytes 307208 | tf_op jit(solution)/shard_map/ppermute | solution.py:25
  11.7 1.6 %collective-permute-done.refs_1_ = bf16[80,640]{1,0:T(8,128)(2,1)S(1)} collective-permute-done((bf16[80,640]{1,0:T(8,128)(2,1)S(1)}, bf16[80,640]{1,0:T(8,128)(2,1)S(1)}, u32[]{:S(2)}, u32[]{:S(2)}) %collective-permute-start) | collective-permute-done | bytes 102432 | tf_op jit(solution)/shard_map/ppermute | solution.py:25
  13.3 1.1 collective-permute-done.1.refs_2_
  14.4 0.7 collective-permute-done.2.refs_3_
  15.1 6.5 %shard_map.111 = (bf16[40,5120]{1,0:T(8,128)(2,1)S(1)}, f32[40,512]{1,0:T(8,128)S(1)}, f32[40,512]{1,0:T(8,128)S(1)}, bf16[40,512]{1,0:T(8,128)(2,1)S(1)}, bf16[...) custom-call(bf16[80,640]{1,0:T(8,128)(2,1)S(1)} %get-tuple-element.4, ...), custom_call_target="tpu_custom_call" | custom-call | bytes 1024 | tf_op jit(solution)/shard_map/pallas_call | solution.py:38
  21.7 2.3 %collective-permute-start.3 = (bf16[80,640]{1,0:T(8,128)(2,1)S(1)}, bf16[80,640]{1,0:T(8,128)(2,1)S(1)}, u32[]{:S(2)}, u32[]{:S(2)}) collective-permute-start(bf16[80,640]{1,0:T(8,128)(2,1)S(1)} %get-tuple-element.48), channel_id=1, source_target_pairs={{2,0},{4,2},{6,4},{0,6},{3,1},{5,3},{7,5},{1,7},{10,8},{12,10},{14... | collective-permute-start | bytes 307208 | tf_op jit(solution)/shard_map/ppermute | solution.py:25
  23.9 0.5 collective-permute-start.4
  24.4 0.5 collective-permute-start.6
  24.9 9.2 %collective-permute-done.6.refs_8_.next_routes = s32[1,4,128]{2,1,0:T(4,128)S(1)} collective-permute-done((s32[1,4,128]{2,1,0:T(4,128)S(1)}, s32[1,4,128]{2,1,0:T(4,128)S(1)}, u32[]{:S(2)}, u32[]{:S(2)}) %collective-permute-start.6) | collective-permute-done | bytes 2080 | tf_op jit(solution)/shard_map/ppermute | solution.py:25
  34.1 1.4 collective-permute-start.9
  35.5 0.7 shard_map.112
  36.2 3.4 %collective-permute-start.7 = (bf16[80,640]{1,0:T(8,128)(2,1)S(1)}, bf16[80,640]{1,0:T(8,128)(2,1)S(1)}, u32[]{:S(2)}, u32[]{:S(2)}) collective-permute-start(bf16[80,640]{1,0:T(8,128)(2,1)S(1)} %get-tuple-element.52), channel_id=1, source_target_pairs={{24,0},{0,8},{8,16},{16,24},{25,1},{1,9},{9,17},{17,25},{26,2},{2,... | collective-permute-start | bytes 307208 | tf_op jit(solution)/shard_map/ppermute | solution.py:25
  39.7 0.5 shard_map.113
  40.2 5.5 %collective-permute-done.9.__.early = bf16[128,640]{1,0:T(8,128)(2,1)S(1)} collective-permute-done((bf16[128,640]{1,0:T(8,128)(2,1)S(1)}, bf16[128,640]{1,0:T(8,128)(2,1)S(1)}, u32[]{:S(2)}, u32[]{:S(2)}) %collective-permute-start.9) | collective-permute-done | bytes 163872 | tf_op jit(solution)/shard_map/ppermute | solution.py:25
  45.8 0.3 shard_map.114
  46.1 1.4 collective-permute-start.17
  47.5 1.6 %collective-permute-start.11 = (bf16[160,640]{1,0:T(8,128)(2,1)S(1)}, bf16[160,640]{1,0:T(8,128)(2,1)S(1)}, u32[]{:S(2)}, u32[]{:S(2)}) collective-permute-start(bf16[160,640]{1,0:T(8,128)(2,1)S(1)} %get-tuple-element.55.refs_0_), channel_id=1, source_target_pairs={{4,0},{6,2},{0,4},{2,6},{5,1},{7,3},{1,5},{3,7},{12,8},{14,10},{8,... | collective-permute-start | bytes 614408 | tf_op jit(solution)/shard_map/ppermute | solution.py:25
  49.0 1.4 %collective-permute-start.12 = (bf16[160,640]{1,0:T(8,128)(2,1)S(1)}, bf16[160,640]{1,0:T(8,128)(2,1)S(1)}, u32[]{:S(2)}, u32[]{:S(2)}) collective-permute-start(bf16[160,640]{1,0:T(8,128)(2,1)S(1)} %get-tuple-element.55.refs_0_), channel_id=1, source_target_pairs={{2,0},{4,2},{6,4},{0,6},{3,1},{5,3},{7,5},{1,7},{10,8},{12,10},{14... | collective-permute-start | bytes 614408 | tf_op jit(solution)/shard_map/ppermute | solution.py:25
  50.5 3.8 %collective-permute-done.10.refs_1_ = bf16[160,640]{1,0:T(8,128)(2,1)S(1)} collective-permute-done((bf16[160,640]{1,0:T(8,128)(2,1)S(1)}, bf16[160,640]{1,0:T(8,128)(2,1)S(1)}, u32[]{:S(2)}, u32[]{:S(2)}) %collective-permute-start.10) | collective-permute-done | bytes 204832 | tf_op jit(solution)/shard_map/ppermute | solution.py:25
  54.3 1.1 collective-permute-done.11.refs_2_
  55.4 2.9 %collective-permute-done.12.refs_3_ = bf16[160,640]{1,0:T(8,128)(2,1)S(1)} collective-permute-done((bf16[160,640]{1,0:T(8,128)(2,1)S(1)}, bf16[160,640]{1,0:T(8,128)(2,1)S(1)}, u32[]{:S(2)}, u32[]{:S(2)}) %collective-permute-start.12) | collective-permute-done | bytes 204832 | tf_op jit(solution)/shard_map/ppermute | solution.py:25
  58.3 6.8 %shard_map.115 = (bf16[40,17408]{1,0:T(8,128)(2,1)S(1)}, bf16[80,640]{1,0:T(8,128)(2,1)S(1)}, bf16[80,640]{1,0:T(8,128)(2,1)S(1)}, bf16[80,640]{1,0:T(8,128)(2,1)S(1)}, bf16[80,640]{1,0:T(8,128)(2,1)S(1)}) custom-call(bf16[160,640]{1,0:T(8,128)(2,1)S(1)} %get-tuple-element.55.refs_0_, bf16[160,640]{1,0:T(8,128)(2,1)S(1)} %collective-permute-done.10.refs_1_, ...), custom_call_target="tpu_custom_call" | custom-call | bytes 1024 | tf_op jit(solution)/shard_map/pallas_call | solution.py:38
  65.2 1.6 %collective-permute-start.32 = (bf16[40,17408]{1,0:T(8,128)(2,1)S(1)}, bf16[40,17408]{1,0:T(8,128)(2,1)S(1)}, u32[]{:S(2)}, u32[]{:S(2)}) collective-permute-start(bf16[40,17408]{1,0:T(8,128)(2,1)S(1)} %get-tuple-element.77.act.refs_0_.refs_2_.refs_4_.refs_6_), channel_id=1, source_target_pairs={{1,0},{0,1},{3,2},{2,3},{5,4},{4,5},{7,6},{6,7},{9,8},{8,9},{11,10... | collective-permute-start | bytes 4177928 | tf_op jit(solution)/shard_map/ppermute | solution.py:25
  66.7 1.9 %collective-permute-start.13 = (bf16[80,640]{1,0:T(8,128)(2,1)S(1)}, bf16[80,640]{1,0:T(8,128)(2,1)S(1)}, u32[]{:S(2)}, u32[]{:S(2)}) collective-permute-start(bf16[80,640]{1,0:T(8,128)(2,1)S(1)} %get-tuple-element.62), channel_id=1, source_target_pairs={{2,0},{4,2},{6,4},{0,6},{3,1},{5,3},{7,5},{1,7},{10,8},{12,10},{14... | collective-permute-start | bytes 307208 | tf_op jit(solution)/shard_map/ppermute | solution.py:25
  68.6 0.5 collective-permute-start.14
  69.1 2.4 %collective-permute-done.13.refs_1_ = bf16[80,640]{1,0:T(8,128)(2,1)S(1)} collective-permute-done((bf16[80,640]{1,0:T(8,128)(2,1)S(1)}, bf16[80,640]{1,0:T(8,128)(2,1)S(1)}, u32[]{:S(2)}, u32[]{:S(2)}) %collective-permute-start.13) | collective-permute-done | bytes 102432 | tf_op jit(solution)/shard_map/ppermute | solution.py:25
  71.5 3.0 %collective-permute-done.14.refs_2_ = bf16[80,640]{1,0:T(8,128)(2,1)S(1)} collective-permute-done((bf16[80,640]{1,0:T(8,128)(2,1)S(1)}, bf16[80,640]{1,0:T(8,128)(2,1)S(1)}, u32[]{:S(2)}, u32[]{:S(2)}) %collective-permute-start.14) | collective-permute-done | bytes 102432 | tf_op jit(solution)/shard_map/ppermute | solution.py:25
  74.5 0.4 shard_map.116
  75.0 1.8 %collective-permute-start.16 = (bf16[80,640]{1,0:T(8,128)(2,1)S(1)}, bf16[80,640]{1,0:T(8,128)(2,1)S(1)}, u32[]{:S(2)}, u32[]{:S(2)}) collective-permute-start(bf16[80,640]{1,0:T(8,128)(2,1)S(1)} %shard_map.116), channel_id=1, source_target_pairs={{8,0},{16,8},{24,16},{0,24},{9,1},{17,9},{25,17},{1,25},{10,2},{18... | collective-permute-start | bytes 307208 | tf_op jit(solution)/shard_map/ppermute | solution.py:25
  76.8 2.9 %collective-permute-done.16.upd1.refs_7_ = bf16[80,640]{1,0:T(8,128)(2,1)S(1)} collective-permute-done((bf16[80,640]{1,0:T(8,128)(2,1)S(1)}, bf16[80,640]{1,0:T(8,128)(2,1)S(1)}, u32[]{:S(2)}, u32[]{:S(2)}) %collective-permute-start.16) | collective-permute-done | bytes 102432 | tf_op jit(solution)/shard_map/ppermute | solution.py:25
  79.7 0.9 shard_map.117
  80.6 0.9 collective-permute-start.24
  81.5 1.5 %collective-permute-start.19 = (bf16[80,640]{1,0:T(8,128)(2,1)S(1)}, bf16[80,640]{1,0:T(8,128)(2,1)S(1)}, u32[]{:S(2)}, u32[]{:S(2)}) collective-permute-start(bf16[80,640]{1,0:T(8,128)(2,1)S(1)} %get-tuple-element.67.refs_0_), channel_id=1, source_target_pairs={{4,0},{6,2},{0,4},{2,6},{5,1},{7,3},{1,5},{3,7},{12,8},{14,10},{8,... | collective-permute-start | bytes 307208 | tf_op jit(solution)/shard_map/ppermute | solution.py:25
  83.0 1.4 %collective-permute-start.20 = (bf16[80,640]{1,0:T(8,128)(2,1)S(1)}, bf16[80,640]{1,0:T(8,128)(2,1)S(1)}, u32[]{:S(2)}, u32[]{:S(2)}) collective-permute-start(bf16[80,640]{1,0:T(8,128)(2,1)S(1)} %get-tuple-element.67.refs_0_), channel_id=1, source_target_pairs={{2,0},{4,2},{6,4},{0,6},{3,1},{5,3},{7,5},{1,7},{10,8},{12,10},{14... | collective-permute-start | bytes 307208 | tf_op jit(solution)/shard_map/ppermute | solution.py:25
  84.5 1.6 %collective-permute-done.18.refs_1_ = bf16[80,640]{1,0:T(8,128)(2,1)S(1)} collective-permute-done((bf16[80,640]{1,0:T(8,128)(2,1)S(1)}, bf16[80,640]{1,0:T(8,128)(2,1)S(1)}, u32[]{:S(2)}, u32[]{:S(2)}) %collective-permute-start.18) | collective-permute-done | bytes 102432 | tf_op jit(solution)/shard_map/ppermute | solution.py:25
  86.1 1.1 collective-permute-done.19.refs_2_
  87.2 0.7 collective-permute-done.20.refs_3_
  87.9 5.1 %shard_map.118 = (bf16[40,6144]{1,0:T(8,128)(2,1)S(1)}, bf16[80,640]{1,0:T(8,128)(2,1)S(1)}, bf16[80,640]{1,0:T(8,128)(2,1)S(1)}, bf16[80,640]{1,0:T(8,128)(2,1)S(1)}, bf16[80,640]{1,0:T(8,128)(2,1)S(1)}) custom-call(bf16[80,640]{1,0:T(8,128)(2,1)S(1)} %get-tuple-element.67.refs_0_, bf16[80,640]{1,0:T(8,128)(2,1)S(1)} %collective-permute-done.18.refs_1_, ...), custom_call_target="tpu_custom_call" | custom-call | bytes 1024 | tf_op jit(solution)/shard_map/pallas_call | solution.py:38
  92.9 1.6 %collective-permute-start.33 = (bf16[40,6144]{1,0:T(8,128)(2,1)S(1)}, bf16[40,6144]{1,0:T(8,128)(2,1)S(1)}, u32[]{:S(2)}, u32[]{:S(2)}) collective-permute-start(bf16[40,6144]{1,0:T(8,128)(2,1)S(1)} %get-tuple-element.78._.refs_0_.refs_2_), channel_id=1, source_target_pairs={{1,0},{0,1},{3,2},{2,3},{5,4},{4,5},{7,6},{6,7},{9,8},{8,9},{11,10... | collective-permute-start | bytes 1474568 | tf_op jit(solution)/shard_map/ppermute | solution.py:25
  94.5 1.9 %collective-permute-start.21 = (bf16[80,640]{1,0:T(8,128)(2,1)S(1)}, bf16[80,640]{1,0:T(8,128)(2,1)S(1)}, u32[]{:S(2)}, u32[]{:S(2)}) collective-permute-start(bf16[80,640]{1,0:T(8,128)(2,1)S(1)} %get-tuple-element.71), channel_id=1, source_target_pairs={{2,0},{4,2},{6,4},{0,6},{3,1},{5,3},{7,5},{1,7},{10,8},{12,10},{14... | collective-permute-start | bytes 307208 | tf_op jit(solution)/shard_map/ppermute | solution.py:25
  96.4 1.1 shard_map.120
  97.5 0.1 collective-permute-start.27
  97.6 1.1 collective-permute-done.21.refs_1_
  98.7 0.5 collective-permute-start.28
  99.2 0.6 collective-permute-done.27.refs_1_
  99.8 1.1 collective-permute-start.29
  100.9 3.5 %collective-permute-done.28.refs_2_ = bf16[80,640]{1,0:T(8,128)(2,1)S(1)} collective-permute-done((bf16[80,640]{1,0:T(8,128)(2,1)S(1)}, bf16[80,640]{1,0:T(8,128)(2,1)S(1)}, u32[]{:S(2)}, u32[]{:S(2)}) %collective-permute-start.28) | collective-permute-done | bytes 102432 | tf_op jit(solution)/shard_map/ppermute | solution.py:25
  104.4 1.1 collective-permute-done.29.refs_3_
  105.5 0.2 shard_map.121
  105.8 4.3 %collective-permute-done.22.refs_2_ = bf16[80,640]{1,0:T(8,128)(2,1)S(1)} collective-permute-done((bf16[80,640]{1,0:T(8,128)(2,1)S(1)}, bf16[80,640]{1,0:T(8,128)(2,1)S(1)}, u32[]{:S(2)}, u32[]{:S(2)}) %collective-permute-start.22) | collective-permute-done | bytes 102432 | tf_op jit(solution)/shard_map/ppermute | solution.py:25
  110.1 1.2 collective-permute-start.25
  111.3 1.5 %collective-permute-start.30 = (bf16[80,640]{1,0:T(8,128)(2,1)S(1)}, bf16[80,640]{1,0:T(8,128)(2,1)S(1)}, u32[]{:S(2)}, u32[]{:S(2)}) collective-permute-start(bf16[80,640]{1,0:T(8,128)(2,1)S(1)} %shard_map.121), channel_id=1, source_target_pairs={{24,0},{0,8},{8,16},{16,24},{25,1},{1,9},{9,17},{17,25},{26,2},{2,... | collective-permute-start | bytes 307208 | tf_op jit(solution)/shard_map/ppermute | solution.py:25
  112.8 2.6 %collective-permute-start.26 = (s32[1,4,128]{2,1,0:T(4,128)S(1)}, s32[1,4,128]{2,1,0:T(4,128)S(1)}, u32[]{:S(2)}, u32[]{:S(2)}) collective-permute-start(s32[1,4,128]{2,1,0:T(4,128)S(1)} %get-tuple-element.87), channel_id=1, source_target_pairs={{16,0},{24,8},{0,16},{8,24},{17,1},{25,9},{1,17},{9,25},{18,2},{26... | collective-permute-start | bytes 6152 | tf_op jit(solution)/shard_map/ppermute | solution.py:25
  115.4 0.3 collective-permute-start.31
  115.7 2.4 %shard_map.119 = bf16[128,5120]{1,0:T(8,128)(2,1)} custom-call(bf16[80,640]{1,0:T(8,128)(2,1)S(1)} %get-tuple-element.70.refs_0_, bf16[80,640]{1,0:T(8,128)(2,1)S(1)} %collective-permute-done.21.refs_1_, bf16[80,640]{1,0:T(8,128)(2,1)S(1)} %collective-permute-done.22.refs_2_, bf16[80,640]{1,0:T(8,128)(2,1)S(1)} %collective-permute-done.23.refs_3_, ...), custom_call_target="tpu_custom_call" | custom-call | bytes 1024 | tf_op jit(solution)/shard_map/pallas_call | solution.py:38
  118.1 2.9 %shard_map.123 = (bf16[5120,160]{1,0:T(8,128)(2,1)S(1)}, bf16[512,160]{1,0:T(8,128)(2,1)S(1)}) custom-call(bf16[40,17408]{1,0:T(8,128)(2,1)S(1)} %get-tuple-element.77.act.refs_0_.refs_2_.refs_4_.refs_6_, bf16[40,17408]{1,0:T(8,128)(2,1)S(1)} %collective-permute-done.32.refs_1_.refs_3_.refs_5_.refs_7_, ...), custom_call_target="tpu_custom_call" | custom-call | bytes 1024 | tf_op jit(solution)/shard_map/pallas_call | solution.py:421
  121.0 6.2 %shard_map.124 = (bf16[5120,512]{1,0:T(8,128)(2,1)}, bf16[5120,512]{1,0:T(8,128)(2,1)}) custom-call(bf16[5120,160]{1,0:T(8,128)(2,1)S(1)} %get-tuple-element.83.x_t, bf16[40,6144]{1,0:T(8,128)(2,1)S(1)} %get-tuple-element.78._.refs_0_.refs_2_, bf16[40,6144]{1,0:T(8,128)(2,1)S(1)} %collective-permute-done.33.refs_1_.refs_3_, ...), custom_call_target="tpu_custom_call" | custom-call | bytes 1024 | tf_op jit(solution)/shard_map/pallas_call | solution.py:421
  127.2 5.9 %shard_map.125 = bf16[512,5120]{1,0:T(8,128)(2,1)} custom-call(bf16[512,160]{1,0:T(8,128)(2,1)S(1)} %get-tuple-element.86.act_t, bf16[40,6144]{1,0:T(8,128)(2,1)S(1)} %get-tuple-element.78._.refs_0_.refs_2_, bf16[40,6144]{1,0:T(8,128)(2,1)S(1)} %collective-permute-done.33.refs_1_.refs_3_, ...), custom_call_target="tpu_custom_call" | custom-call | bytes 1024 | tf_op jit(solution)/shard_map/pallas_call | solution.py:421
  133.1 5.1 %collective-permute-done.26.prev2_routes = s32[1,4,128]{2,1,0:T(4,128)S(1)} collective-permute-done((s32[1,4,128]{2,1,0:T(4,128)S(1)}, s32[1,4,128]{2,1,0:T(4,128)S(1)}, u32[]{:S(2)}, u32[]{:S(2)}) %collective-permute-start.26) | collective-permute-done | bytes 2080 | tf_op jit(solution)/shard_map/ppermute | solution.py:25
  138.2 3.3 %shard_map.122 = bf16[128,5120]{1,0:T(8,128)(2,1)} custom-call(bf16[128,640]{1,0:T(8,128)(2,1)S(1)} %collective-permute-done.9.__.early, bf16[128,4480]{1,0:T(8,128)(2,1)S(1)} %collective-permute-done.24.rest, bf16[80,640]{1,0:T(8,128)(2,1)S(1)} %collective-permute-done.25.upd0, s32[1,4,128]{2,1,0:T(4,128)S(1)} %collective-permute-done.26.prev2_routes, ...), custom_call_target="tpu_custom_call" | custom-call | bytes 1024 | tf_op jit(solution)/shard_map/pallas_call | solution.py:38
  (31 shorter events, 0.1 us)
Async XLA Ops:
  0.6 39.0 %collective-permute-start.8 = (bf16[128,5120]{1,0:T(8,128)(2,1)}, bf16[128,5120]{1,0:T(8,128)(2,1)S(1)}, u32[]{:S(2)}, u32[]{:S(2)}) collective-permute-start(bf16[128,5120]{1,0:T(8,128)(2,1)} %param.8), channel_id=1, source_target_pairs={{8,0},{16,8},{24,16},{0,24},{9,1},{17,9},{25,17},{1,25},{10,2},{18... | collective-permute-start | bytes 3932168 | tf_op jit(solution)/shard_map/ppermute | solution.py:25
  8.0 0.7 copy-start.3
  8.7 4.6 %collective-permute-start = (bf16[80,640]{1,0:T(8,128)(2,1)S(1)}, bf16[80,640]{1,0:T(8,128)(2,1)S(1)}, u32[]{:S(2)}, u32[]{:S(2)}) collective-permute-start(bf16[80,640]{1,0:T(8,128)(2,1)S(1)} %get-tuple-element.46.refs_0_), channel_id=1, source_target_pairs={{6,0},{0,2},{2,4},{4,6},{7,1},{1,3},{3,5},{5,7},{14,8},{8,10},{10,... | collective-permute-start | bytes 307208 | tf_op jit(solution)/shard_map/ppermute | solution.py:25
  8.7 5.7 %collective-permute-start.1 = (bf16[80,640]{1,0:T(8,128)(2,1)S(1)}, bf16[80,640]{1,0:T(8,128)(2,1)S(1)}, u32[]{:S(2)}, u32[]{:S(2)}) collective-permute-start(bf16[80,640]{1,0:T(8,128)(2,1)S(1)} %get-tuple-element.46.refs_0_), channel_id=1, source_target_pairs={{4,0},{6,2},{0,4},{2,6},{5,1},{7,3},{1,5},{3,7},{12,8},{14,10},{8,... | collective-permute-start | bytes 307208 | tf_op jit(solution)/shard_map/ppermute | solution.py:25
  10.2 4.9 %collective-permute-start.2 = (bf16[80,640]{1,0:T(8,128)(2,1)S(1)}, bf16[80,640]{1,0:T(8,128)(2,1)S(1)}, u32[]{:S(2)}, u32[]{:S(2)}) collective-permute-start(bf16[80,640]{1,0:T(8,128)(2,1)S(1)} %get-tuple-element.46.refs_0_), channel_id=1, source_target_pairs={{2,0},{4,2},{6,4},{0,6},{3,1},{5,3},{7,5},{1,7},{10,8},{12,10},{14... | collective-permute-start | bytes 307208 | tf_op jit(solution)/shard_map/ppermute | solution.py:25
  15.1 9.3 %copy-start.1 = (s32[2,128,4]{1,2,0:T(4,128)S(1)}, s32[2,128,4]{1,2,0:T(4,128)}, u32[]{:S(2)}) copy-start(s32[2,128,4]{1,2,0:T(4,128)} %param.12) | copy-start | bytes 12292
  15.1 19.0 %copy-start.4 = (bf16[128,640]{1,0:T(8,128)(2,1)S(1)}, bf16[128,640]{1,0:T(8,128)(2,1)}, u32[]{:S(2)}) copy-start(bf16[128,640]{1,0:T(8,128)(2,1)} %copy-done.3) | copy-start | bytes 491524
  15.1 20.4 %copy-start = (bf16[128,5120]{1,0:T(8,128)(2,1)S(1)}, bf16[128,5120]{1,0:T(8,128)(2,1)}, u32[]{:S(2)}) copy-start(bf16[128,5120]{1,0:T(8,128)(2,1)} %tokens.3) | copy-start | bytes 3932164
  15.1 20.4 %copy-start.2 = (f32[2,128,4]{1,2,0:T(4,128)S(1)}, f32[2,128,4]{1,2,0:T(4,128)}, u32[]{:S(2)}) copy-start(f32[2,128,4]{1,2,0:T(4,128)} %param.13) | copy-start | bytes 12292
  21.7 13.8 %collective-permute-start.3 = (bf16[80,640]{1,0:T(8,128)(2,1)S(1)}, bf16[80,640]{1,0:T(8,128)(2,1)S(1)}, u32[]{:S(2)}, u32[]{:S(2)}) collective-permute-start(bf16[80,640]{1,0:T(8,128)(2,1)S(1)} %get-tuple-element.48), channel_id=1, source_target_pairs={{2,0},{4,2},{6,4},{0,6},{3,1},{5,3},{7,5},{1,7},{10,8},{12,10},{14... | collective-permute-start | bytes 307208 | tf_op jit(solution)/shard_map/ppermute | solution.py:25
  23.9 11.6 %collective-permute-start.4 = (bf16[80,640]{1,0:T(8,128)(2,1)S(1)}, bf16[80,640]{1,0:T(8,128)(2,1)S(1)}, u32[]{:S(2)}, u32[]{:S(2)}) collective-permute-start(bf16[80,640]{1,0:T(8,128)(2,1)S(1)} %get-tuple-element.49), channel_id=1, source_target_pairs={{4,0},{6,2},{0,4},{2,6},{5,1},{7,3},{1,5},{3,7},{12,8},{14,10},{8,... | collective-permute-start | bytes 307208 | tf_op jit(solution)/shard_map/ppermute | solution.py:25
  24.4 11.1 %collective-permute-start.5 = (bf16[80,640]{1,0:T(8,128)(2,1)S(1)}, bf16[80,640]{1,0:T(8,128)(2,1)S(1)}, u32[]{:S(2)}, u32[]{:S(2)}) collective-permute-start(bf16[80,640]{1,0:T(8,128)(2,1)S(1)} %get-tuple-element.50), channel_id=1, source_target_pairs={{6,0},{0,2},{2,4},{4,6},{7,1},{1,3},{3,5},{5,7},{14,8},{8,10},{10,... | collective-permute-start | bytes 307208 | tf_op jit(solution)/shard_map/ppermute | solution.py:25
  24.4 9.7 %collective-permute-start.6 = (s32[1,4,128]{2,1,0:T(4,128)S(1)}, s32[1,4,128]{2,1,0:T(4,128)S(1)}, u32[]{:S(2)}, u32[]{:S(2)}) collective-permute-start(s32[1,4,128]{2,1,0:T(4,128)S(1)} %get-tuple-element.88), channel_id=1, source_target_pairs={{8,0},{16,8},{24,16},{0,24},{9,1},{17,9},{25,17},{1,25},{10,2},{18... | collective-permute-start | bytes 6152 | tf_op jit(solution)/shard_map/ppermute | solution.py:25
  34.1 11.7 %collective-permute-start.9 = (bf16[128,640]{1,0:T(8,128)(2,1)S(1)}, bf16[128,640]{1,0:T(8,128)(2,1)S(1)}, u32[]{:S(2)}, u32[]{:S(2)}) collective-permute-start(bf16[128,640]{1,0:T(8,128)(2,1)S(1)} %copy-done.4), channel_id=1, source_target_pairs={{16,0},{24,8},{0,16},{8,24},{17,1},{25,9},{1,17},{9,25},{18,2},{26... | collective-permute-start | bytes 491528 | tf_op jit(solution)/shard_map/ppermute | solution.py:25
  36.2 9.5 %collective-permute-start.7 = (bf16[80,640]{1,0:T(8,128)(2,1)S(1)}, bf16[80,640]{1,0:T(8,128)(2,1)S(1)}, u32[]{:S(2)}, u32[]{:S(2)}) collective-permute-start(bf16[80,640]{1,0:T(8,128)(2,1)S(1)} %get-tuple-element.52), channel_id=1, source_target_pairs={{24,0},{0,8},{8,16},{16,24},{25,1},{1,9},{9,17},{17,25},{26,2},{2,... | collective-permute-start | bytes 307208 | tf_op jit(solution)/shard_map/ppermute | solution.py:25
  46.1 33.6 %collective-permute-start.17 = (bf16[128,5120]{1,0:T(8,128)(2,1)S(1)}, bf16[128,5120]{1,0:T(8,128)(2,1)S(1)}, u32[]{:S(2)}, u32[]{:S(2)}) collective-permute-start(bf16[128,5120]{1,0:T(8,128)(2,1)S(1)} %get-tuple-element.66), channel_id=1, source_target_pairs={{8,0},{16,8},{24,16},{0,24},{9,1},{17,9},{25,17},{1,25},{10,2},{18... | collective-permute-start | bytes 3932168 | tf_op jit(solution)/shard_map/ppermute | solution.py:25
  47.5 6.8 %collective-permute-start.10 = (bf16[160,640]{1,0:T(8,128)(2,1)S(1)}, bf16[160,640]{1,0:T(8,128)(2,1)S(1)}, u32[]{:S(2)}, u32[]{:S(2)}) collective-permute-start(bf16[160,640]{1,0:T(8,128)(2,1)S(1)} %get-tuple-element.55.refs_0_), channel_id=1, source_target_pairs={{6,0},{0,2},{2,4},{4,6},{7,1},{1,3},{3,5},{5,7},{14,8},{8,10},{10,... | collective-permute-start | bytes 614408 | tf_op jit(solution)/shard_map/ppermute | solution.py:25
  47.5 7.9 %collective-permute-start.11 = (bf16[160,640]{1,0:T(8,128)(2,1)S(1)}, bf16[160,640]{1,0:T(8,128)(2,1)S(1)}, u32[]{:S(2)}, u32[]{:S(2)}) collective-permute-start(bf16[160,640]{1,0:T(8,128)(2,1)S(1)} %get-tuple-element.55.refs_0_), channel_id=1, source_target_pairs={{4,0},{6,2},{0,4},{2,6},{5,1},{7,3},{1,5},{3,7},{12,8},{14,10},{8,... | collective-permute-start | bytes 614408 | tf_op jit(solution)/shard_map/ppermute | solution.py:25
  49.0 9.3 %collective-permute-start.12 = (bf16[160,640]{1,0:T(8,128)(2,1)S(1)}, bf16[160,640]{1,0:T(8,128)(2,1)S(1)}, u32[]{:S(2)}, u32[]{:S(2)}) collective-permute-start(bf16[160,640]{1,0:T(8,128)(2,1)S(1)} %get-tuple-element.55.refs_0_), channel_id=1, source_target_pairs={{2,0},{4,2},{6,4},{0,6},{3,1},{5,3},{7,5},{1,7},{10,8},{12,10},{14... | collective-permute-start | bytes 614408 | tf_op jit(solution)/shard_map/ppermute | solution.py:25
  65.2 47.6 %collective-permute-start.32 = (bf16[40,17408]{1,0:T(8,128)(2,1)S(1)}, bf16[40,17408]{1,0:T(8,128)(2,1)S(1)}, u32[]{:S(2)}, u32[]{:S(2)}) collective-permute-start(bf16[40,17408]{1,0:T(8,128)(2,1)S(1)} %get-tuple-element.77.act.refs_0_.refs_2_.refs_4_.refs_6_), channel_id=1, source_target_pairs={{1,0},{0,1},{3,2},{2,3},{5,4},{4,5},{7,6},{6,7},{9,8},{8,9},{11,10... | collective-permute-start | bytes 4177928 | tf_op jit(solution)/shard_map/ppermute | solution.py:25
  66.7 4.8 %collective-permute-start.13 = (bf16[80,640]{1,0:T(8,128)(2,1)S(1)}, bf16[80,640]{1,0:T(8,128)(2,1)S(1)}, u32[]{:S(2)}, u32[]{:S(2)}) collective-permute-start(bf16[80,640]{1,0:T(8,128)(2,1)S(1)} %get-tuple-element.62), channel_id=1, source_target_pairs={{2,0},{4,2},{6,4},{0,6},{3,1},{5,3},{7,5},{1,7},{10,8},{12,10},{14... | collective-permute-start | bytes 307208 | tf_op jit(solution)/shard_map/ppermute | solution.py:25
  68.6 5.9 %collective-permute-start.14 = (bf16[80,640]{1,0:T(8,128)(2,1)S(1)}, bf16[80,640]{1,0:T(8,128)(2,1)S(1)}, u32[]{:S(2)}, u32[]{:S(2)}) collective-permute-start(bf16[80,640]{1,0:T(8,128)(2,1)S(1)} %get-tuple-element.63), channel_id=1, source_target_pairs={{4,0},{6,2},{0,4},{2,6},{5,1},{7,3},{1,5},{3,7},{12,8},{14,10},{8,... | collective-permute-start | bytes 307208 | tf_op jit(solution)/shard_map/ppermute | solution.py:25
  69.1 5.4 %collective-permute-start.15 = (bf16[80,640]{1,0:T(8,128)(2,1)S(1)}, bf16[80,640]{1,0:T(8,128)(2,1)S(1)}, u32[]{:S(2)}, u32[]{:S(2)}) collective-permute-start(bf16[80,640]{1,0:T(8,128)(2,1)S(1)} %get-tuple-element.64), channel_id=1, source_target_pairs={{6,0},{0,2},{2,4},{4,6},{7,1},{1,3},{3,5},{5,7},{14,8},{8,10},{10,... | collective-permute-start | bytes 307208 | tf_op jit(solution)/shard_map/ppermute | solution.py:25
  75.0 4.7 %collective-permute-start.16 = (bf16[80,640]{1,0:T(8,128)(2,1)S(1)}, bf16[80,640]{1,0:T(8,128)(2,1)S(1)}, u32[]{:S(2)}, u32[]{:S(2)}) collective-permute-start(bf16[80,640]{1,0:T(8,128)(2,1)S(1)} %shard_map.116), channel_id=1, source_target_pairs={{8,0},{16,8},{24,16},{0,24},{9,1},{17,9},{25,17},{1,25},{10,2},{18... | collective-permute-start | bytes 307208 | tf_op jit(solution)/shard_map/ppermute | solution.py:25
  80.6 57.6 %collective-permute-start.24 = (bf16[128,4480]{1,0:T(8,128)(2,1)S(1)}, bf16[128,4480]{1,0:T(8,128)(2,1)S(1)}, u32[]{:S(2)}, u32[]{:S(2)}) collective-permute-start(bf16[128,4480]{1,0:T(8,128)(2,1)S(1)} %get-tuple-element.75), channel_id=1, source_target_pairs={{16,0},{24,8},{0,16},{8,24},{17,1},{25,9},{1,17},{9,25},{18,2},{26... | collective-permute-start | bytes 3440648 | tf_op jit(solution)/shard_map/ppermute | solution.py:25
  81.5 4.6 %collective-permute-start.18 = (bf16[80,640]{1,0:T(8,128)(2,1)S(1)}, bf16[80,640]{1,0:T(8,128)(2,1)S(1)}, u32[]{:S(2)}, u32[]{:S(2)}) collective-permute-start(bf16[80,640]{1,0:T(8,128)(2,1)S(1)} %get-tuple-element.67.refs_0_), channel_id=1, source_target_pairs={{6,0},{0,2},{2,4},{4,6},{7,1},{1,3},{3,5},{5,7},{14,8},{8,10},{10,... | collective-permute-start | bytes 307208 | tf_op jit(solution)/shard_map/ppermute | solution.py:25
  81.5 5.7 %collective-permute-start.19 = (bf16[80,640]{1,0:T(8,128)(2,1)S(1)}, bf16[80,640]{1,0:T(8,128)(2,1)S(1)}, u32[]{:S(2)}, u32[]{:S(2)}) collective-permute-start(bf16[80,640]{1,0:T(8,128)(2,1)S(1)} %get-tuple-element.67.refs_0_), channel_id=1, source_target_pairs={{4,0},{6,2},{0,4},{2,6},{5,1},{7,3},{1,5},{3,7},{12,8},{14,10},{8,... | collective-permute-start | bytes 307208 | tf_op jit(solution)/shard_map/ppermute | solution.py:25
  83.0 4.9 %collective-permute-start.20 = (bf16[80,640]{1,0:T(8,128)(2,1)S(1)}, bf16[80,640]{1,0:T(8,128)(2,1)S(1)}, u32[]{:S(2)}, u32[]{:S(2)}) collective-permute-start(bf16[80,640]{1,0:T(8,128)(2,1)S(1)} %get-tuple-element.67.refs_0_), channel_id=1, source_target_pairs={{2,0},{4,2},{6,4},{0,6},{3,1},{5,3},{7,5},{1,7},{10,8},{12,10},{14... | collective-permute-start | bytes 307208 | tf_op jit(solution)/shard_map/ppermute | solution.py:25
  92.9 22.4 %collective-permute-start.33 = (bf16[40,6144]{1,0:T(8,128)(2,1)S(1)}, bf16[40,6144]{1,0:T(8,128)(2,1)S(1)}, u32[]{:S(2)}, u32[]{:S(2)}) collective-permute-start(bf16[40,6144]{1,0:T(8,128)(2,1)S(1)} %get-tuple-element.78._.refs_0_.refs_2_), channel_id=1, source_target_pairs={{1,0},{0,1},{3,2},{2,3},{5,4},{4,5},{7,6},{6,7},{9,8},{8,9},{11,10... | collective-permute-start | bytes 1474568 | tf_op jit(solution)/shard_map/ppermute | solution.py:25
  94.5 4.2 %collective-permute-start.21 = (bf16[80,640]{1,0:T(8,128)(2,1)S(1)}, bf16[80,640]{1,0:T(8,128)(2,1)S(1)}, u32[]{:S(2)}, u32[]{:S(2)}) collective-permute-start(bf16[80,640]{1,0:T(8,128)(2,1)S(1)} %get-tuple-element.71), channel_id=1, source_target_pairs={{2,0},{4,2},{6,4},{0,6},{3,1},{5,3},{7,5},{1,7},{10,8},{12,10},{14... | collective-permute-start | bytes 307208 | tf_op jit(solution)/shard_map/ppermute | solution.py:25
  97.5 2.3 %collective-permute-start.27 = (bf16[80,640]{1,0:T(8,128)(2,1)S(1)}, bf16[80,640]{1,0:T(8,128)(2,1)S(1)}, u32[]{:S(2)}, u32[]{:S(2)}) collective-permute-start(bf16[80,640]{1,0:T(8,128)(2,1)S(1)} %get-tuple-element.80), channel_id=1, source_target_pairs={{2,0},{4,2},{6,4},{0,6},{3,1},{5,3},{7,5},{1,7},{10,8},{12,10},{14... | collective-permute-start | bytes 307208 | tf_op jit(solution)/shard_map/ppermute | solution.py:25
  98.7 5.7 %collective-permute-start.28 = (bf16[80,640]{1,0:T(8,128)(2,1)S(1)}, bf16[80,640]{1,0:T(8,128)(2,1)S(1)}, u32[]{:S(2)}, u32[]{:S(2)}) collective-permute-start(bf16[80,640]{1,0:T(8,128)(2,1)S(1)} %get-tuple-element.81), channel_id=1, source_target_pairs={{4,0},{6,2},{0,4},{2,6},{5,1},{7,3},{1,5},{3,7},{12,8},{14,10},{8,... | collective-permute-start | bytes 307208 | tf_op jit(solution)/shard_map/ppermute | solution.py:25
  99.8 5.7 %collective-permute-start.29 = (bf16[80,640]{1,0:T(8,128)(2,1)S(1)}, bf16[80,640]{1,0:T(8,128)(2,1)S(1)}, u32[]{:S(2)}, u32[]{:S(2)}) collective-permute-start(bf16[80,640]{1,0:T(8,128)(2,1)S(1)} %get-tuple-element.82), channel_id=1, source_target_pairs={{6,0},{0,2},{2,4},{4,6},{7,1},{1,3},{3,5},{5,7},{14,8},{8,10},{10,... | collective-permute-start | bytes 307208 | tf_op jit(solution)/shard_map/ppermute | solution.py:25
  104.4 5.7 %collective-permute-start.22 = (bf16[80,640]{1,0:T(8,128)(2,1)S(1)}, bf16[80,640]{1,0:T(8,128)(2,1)S(1)}, u32[]{:S(2)}, u32[]{:S(2)}) collective-permute-start(bf16[80,640]{1,0:T(8,128)(2,1)S(1)} %get-tuple-element.72), channel_id=1, source_target_pairs={{4,0},{6,2},{0,4},{2,6},{5,1},{7,3},{1,5},{3,7},{12,8},{14,10},{8,... | collective-permute-start | bytes 307208 | tf_op jit(solution)/shard_map/ppermute | solution.py:25
  105.5 5.7 %collective-permute-start.23 = (bf16[80,640]{1,0:T(8,128)(2,1)S(1)}, bf16[80,640]{1,0:T(8,128)(2,1)S(1)}, u32[]{:S(2)}, u32[]{:S(2)}) collective-permute-start(bf16[80,640]{1,0:T(8,128)(2,1)S(1)} %get-tuple-element.73), channel_id=1, source_target_pairs={{6,0},{0,2},{2,4},{4,6},{7,1},{1,3},{3,5},{5,7},{14,8},{8,10},{10,... | collective-permute-start | bytes 307208 | tf_op jit(solution)/shard_map/ppermute | solution.py:25
  110.1 28.1 %collective-permute-start.25 = (bf16[80,640]{1,0:T(8,128)(2,1)S(1)}, bf16[80,640]{1,0:T(8,128)(2,1)S(1)}, u32[]{:S(2)}, u32[]{:S(2)}) collective-permute-start(bf16[80,640]{1,0:T(8,128)(2,1)S(1)} %get-tuple-element.76), channel_id=1, source_target_pairs={{16,0},{24,8},{0,16},{8,24},{17,1},{25,9},{1,17},{9,25},{18,2},{26... | collective-permute-start | bytes 307208 | tf_op jit(solution)/shard_map/ppermute | solution.py:25
  111.3 26.9 %collective-permute-start.30 = (bf16[80,640]{1,0:T(8,128)(2,1)S(1)}, bf16[80,640]{1,0:T(8,128)(2,1)S(1)}, u32[]{:S(2)}, u32[]{:S(2)}) collective-permute-start(bf16[80,640]{1,0:T(8,128)(2,1)S(1)} %shard_map.121), channel_id=1, source_target_pairs={{24,0},{0,8},{8,16},{16,24},{25,1},{1,9},{9,17},{17,25},{26,2},{2,... | collective-permute-start | bytes 307208 | tf_op jit(solution)/shard_map/ppermute | solution.py:25
  112.8 25.4 %collective-permute-start.26 = (s32[1,4,128]{2,1,0:T(4,128)S(1)}, s32[1,4,128]{2,1,0:T(4,128)S(1)}, u32[]{:S(2)}, u32[]{:S(2)}) collective-permute-start(s32[1,4,128]{2,1,0:T(4,128)S(1)} %get-tuple-element.87), channel_id=1, source_target_pairs={{16,0},{24,8},{0,16},{8,24},{17,1},{25,9},{1,17},{9,25},{18,2},{26... | collective-permute-start | bytes 6152 | tf_op jit(solution)/shard_map/ppermute | solution.py:25
  115.4 22.8 %collective-permute-start.31 = (s32[1,4,128]{2,1,0:T(4,128)S(1)}, s32[1,4,128]{2,1,0:T(4,128)S(1)}, u32[]{:S(2)}, u32[]{:S(2)}) collective-permute-start(s32[1,4,128]{2,1,0:T(4,128)S(1)} %get-tuple-element.88), channel_id=1, source_target_pairs={{24,0},{0,8},{8,16},{16,24},{25,1},{1,9},{9,17},{17,25},{26,2},{2,... | collective-permute-start | bytes 6152 | tf_op jit(solution)/shard_map/ppermute | solution.py:25

commit v9 on v8

--- a/solution.py
+++ b/solution.py
@@ -134,19 +134,23 @@
     return dot(chunk_of(select, 0), ones, 0, 0)[:, :1] > 0.5
 
 
-def placed(c, old, first, hit1, rows1, second, hit2, rows2):
-    value = jnp.where(hit1, dot(chunk_of(first, c), rows1, 0, 0), old.astype(F32))
-    return jnp.where(hit2, dot(chunk_of(second, c), rows2, 0, 0), value).astype(BF16)
+def placed(c, old, select, hit, rows):
+    return jnp.where(hit, dot(chunk_of(select, c), rows, 0, 0), old.astype(F32)).astype(BF16)
+
+
+def start_rows(source, target, sems):
+    copies = []
+    for i in range(source.shape[0] // 16):
+        r = pl.ds(16 * i, 16)
+        copies.append(pltpu.make_async_copy(source.at[r], target.at[r], sems.at[i]))
+        copies[-1].start()
+    return copies
 
 
 def first_rows_kernel(tokens, routes_far, raw, normed, early, sems, held, routes):
-    fetch_routes = pltpu.make_async_copy(routes_far, routes, sems.at[PACK])
+    fetch_routes = pltpu.make_async_copy(routes_far, routes, sems.at[sems.shape[0] - 1])
     fetch_routes.start()
-    fetches = []
-    for c in range(PACK):
-        k = columns(c, held.shape[1])
-        fetches.append(pltpu.make_async_copy(tokens.at[:, k], held.at[:, k], sems.at[c]))
-        fetches[-1].start()
+    fetches = start_rows(tokens, held, sems)
     fetch_routes.wait()
     select = select_of(routes[0])
     for fetch in fetches:
@@ -160,7 +164,7 @@
 
 
 def update0_kernel(n, *refs):
-    parts, (raw, routes, gates, tokens, next_routes, upd, onward) = refs[:n], refs[n:]
+    parts, (raw, routes, gates, tokens, next_routes, upd, onward, part) = refs[:n], refs[n:]
     select = select_of(routes[0])
     select_next = select_of(next_routes[0])
     weight = slot_gates(select, routes[0], gates[0])
@@ -168,6 +172,21 @@
     old = pick(select_next, whole_block(tokens))
     onward[...] = merged(select_next, select, fresh, old)
     upd[...] = fresh
+    part[...] = jnp.zeros(part.shape, BF16)
+    part[: EARLY * CAP] = fresh[: EARLY * CAP]
+
+
+def merge_kernel(tokens, upd, routes, out):
+    select = select_of(routes[0])
+    hit = hit_rows(select)
+    width = tokens.shape[1]
+    for c in range(EARLY, PACK):
+        value = placed(c, tokens[:, columns(c, width)], select, hit, upd[...])
+        out[:, columns(c - EARLY, width)] = value
+
+
+def release_kernel(_, __, ___, ____):
+    pass
 
 
 def grad_rows_kernel(bulk, routes, gates, cot, scaled):
@@ -184,7 +203,7 @@
     upd[...] = (h[...].astype(F32) + weight * summed(parts)).astype(BF16)
 
 
-def enter1_kernel(h, scaled, _, __, out, ___):
+def enter1_kernel(h, scaled, _, __, ___, ____, out, _____):
     values = h[...].astype(F32)
     out[:PACKED] = (values * inv_rms_of(values)).astype(BF16)
     out[PACKED:] = scaled[...]
@@ -203,16 +222,12 @@
     upd[...] = state_grad(parts, h[...], cot[...])
 
 
-def enter0_kernel(upd1, next_routes, routes, gates, bulk, tokens, c0, out, rest, sem):
-    step = tokens.shape[1] // PACK
-    copy = pltpu.make_async_copy(tokens.at[:, pl.ds(EARLY * step, (PACK - EARLY) * step)], rest, sem)
-    copy.start()
+def enter0_kernel(upd1, next_routes, routes, gates, bulk, _, c0, out):
     select = select_of(routes[0])
     old = pick(select, whole_block(bulk))
     rows = merged(select, select_of(next_routes[0]), upd1[...], old)
     c0[...] = rows
     out[...] = (slot_gates(select, routes[0], gates[0]) * rows.astype(F32)).astype(BF16)
-    copy.wait()
 
 
 def finish_grad_kernel(n, *refs):
@@ -222,33 +237,30 @@
     hit1, hit2 = hit_rows(first), hit_rows(second)
     for chunk in range(PACK):
         k = columns(chunk, out.shape[1])
-        out[:, k] = placed(chunk, bulk[:, k], first, hit1, upd1[...], second, hit2, fresh)
+        value = placed(chunk, bulk[:, k], first, hit1, upd1[...])
+        out[:, k] = placed(chunk, value, second, hit2, fresh)
 
 
 def finish_state_kernel(
-    early, rest, upd0, prev2_routes, upd1, prev_routes, out, ins, outs, in_sems, out_sems
+    early, rest, part, prev2_routes, upd1, prev_routes, out, ins, outs, in_sems, out_sems
 ):
+    fetches = start_rows(rest, ins, in_sems)
     height, width = out.shape
-    fetches = []
-    for chunk in range(PACK - EARLY):
-        k = columns(chunk, width)
-        fetches.append(pltpu.make_async_copy(rest.at[:, k], ins.at[chunk], in_sems.at[chunk]))
-        fetches[-1].start()
     first, second = select_of(prev2_routes[0]), select_of(prev_routes[0])
     hit1, hit2 = hit_rows(first), hit_rows(second)
-    rows1, rows2 = upd0[...], upd1[...]
-    stores = []
-    for chunk in range(PACK):
-        if chunk < EARLY:
-            old = early[chunk * height : (chunk + 1) * height]
-        else:
-            fetches[chunk - EARLY].wait()
-            old = ins[chunk - EARLY]
-        outs[chunk] = placed(chunk, old, first, hit1, rows1, second, hit2, rows2)
-        k = columns(chunk, width)
-        stores.append(pltpu.make_async_copy(outs.at[chunk], out.at[:, k], out_sems.at[chunk]))
-        stores[-1].start()
-    for store in stores:
+    for c in range(EARLY):
+        old = early[c * height : (c + 1) * height]
+        rows = jnp.concatenate(
+            [part[...].astype(F32), jnp.zeros((PACKED - part.shape[0], part.shape[1]), F32)], axis=0
+        )
+        value = placed(c, old, first, hit1, rows.astype(BF16))
+        outs[:, columns(c, width)] = placed(c, value, second, hit2, upd1[...])
+    for fetch in fetches:
+        fetch.wait()
+    for c in range(EARLY, PACK):
+        value = ins[:, columns(c - EARLY, width)]
+        outs[:, columns(c, width)] = placed(c, value, second, hit2, upd1[...])
+    for store in start_rows(outs, out, out_sems):
         store.wait()
 
 
@@ -513,11 +525,11 @@
 
     raw0, normed0, early = call(
         first_rows_kernel,
-        [pltpu.VMEM(*one), pltpu.VMEM(*one), pltpu.VMEM((EARLY * tokens.shape[0], step), BF16)],
+        [pltpu.VMEM(*one), pltpu.VMEM(*one), ((EARLY * tokens.shape[0], step), BF16)],
         [tokens, routes],
         any_args=(0, 1),
         scratch=[
-            pltpu.SemaphoreType.DMA((PACK + 1,)),
+            pltpu.SemaphoreType.DMA((tokens.shape[0] // 16 + 1,)),
             pltpu.VMEM(tokens.shape, BF16),
             pltpu.VMEM(routes.shape, jnp.int32),
         ],
@@ -537,18 +549,26 @@
         vmem=VMEM_LOAD,
     )
     parts = to_group(parts)
-    upd0, h1 = call(
-        part(update0_kernel, n), [one, one], [*parts, raw0, routes, gates, tokens, next_routes]
+    few = -(-EARLY * CAP // 16) * 16
+    upd0, h1, part0 = call(
+        part(update0_kernel, n),
+        [one, one, ((few, step), BF16)],
+        [*parts, raw0, routes, gates, tokens, next_routes],
     )
     h1 = shifted(h1, "section", 1)
     cot1, scaled1 = call(grad_rows_kernel, [one, one], [cot1_all, routes, gates])
-    upd0 = shifted(upd0, "section", 2)
+    part0 = shifted(part0, "section", 2)
+    (rest,) = call(
+        merge_kernel,
+        [((tokens.shape[0], width - EARLY * step), BF16)],
+        [tokens, upd0, routes],
+    )
 
     enter1, cot1_all = call(
         enter1_kernel,
         [((2 * PACKED, step), BF16), (tokens.shape, BF16)],
-        [h1, scaled1, cot1_all, early],
-        any_args=(2, 3),
+        [h1, scaled1, cot1_all, early, prev_routes, prev2_routes],
+        any_args=(2, 3, 4, 5),
         any_outs=(1,),
         aliases={2: 1},
     )
@@ -569,13 +589,19 @@
     upd1 = shifted(upd1, "section", -1)
     kept_all = copies_of(kept)
 
-    c0, enter0, rest = call(
+    (rest,) = call(
+        release_kernel,
+        [((tokens.shape[0], width - EARLY * step), BF16)],
+        [rest, cot0_all, upd1],
+        any_args=(0, 1, 2),
+        any_outs=(0,),
+        aliases={0: 0},
+    )
+    c0, enter0 = call(
         enter0_kernel,
-        [one, one, ((tokens.shape[0], width - EARLY * step), BF16)],
-        [upd1, next_routes, routes, gates, cot0_all, tokens],
+        [one, one],
+        [upd1, next_routes, routes, gates, cot0_all, rest],
         any_args=(5,),
-        any_outs=(2,),
-        scratch=[pltpu.SemaphoreType.DMA],
     )
     rest = shifted(rest, "section", 2)
     blocks = from_group(enter0)
@@ -605,18 +631,18 @@
     x_t, act_t = turned(kept_all, width, hidden)
     (down_out,) = down_grads(act_t, g_grad0_all, kept_all, width, hidden)
     gate_out, up_out = input_grads(x_t, g_grad0_all, kept_all, width, hidden)
-    chunks = pltpu.VMEM((PACK, tokens.shape[0], step), BF16)
+    blocks16 = pltpu.SemaphoreType.DMA((tokens.shape[0] // 16,))
     (state,) = call(
         finish_state_kernel,
         [(tokens.shape, BF16)],
-        [early, rest, upd0, prev2_routes, last1, prev_routes],
+        [early, rest, part0, prev2_routes, last1, prev_routes],
         any_args=(1,),
         any_outs=(0,),
         scratch=[
-            chunks,
-            chunks,
-            pltpu.SemaphoreType.DMA((PACK,)),
-            pltpu.SemaphoreType.DMA((PACK,)),
+            pltpu.VMEM(rest.shape, BF16),
+            pltpu.VMEM(tokens.shape, BF16),
+            blocks16,
+            blocks16,
         ],
     )
     return (grad, state, gate_out[None], up_out[None], down_out[None])

time: 142 us -> 139 us (0.979)
  starting transfers between devices: 40.8 us -> 38.1 us
  Pallas kernels: 45.7 us -> 47.2 us
    ppermute x34, starting transfers between devices: 40.8 us -> 38.1 us  [shifted(): lax.ppermute(block, axis, [((i - distance) % size, i) for i in range(size)])]
    pallas_call x13 -> x15, Pallas kernels: 30.7 us -> 32.2 us  [call(): pl.pallas_call(kernel, out_shape=outs, in_specs=[anywhere if i in any_arg...]
  transfers between devices with their start and end apart: 34 -> 34, of which waited for: 20 -> 21; matrix products, arithmetic and copies ran while one was open for 0% -> 0% of each run, Pallas kernels for 30% -> 31%
where the time goes in v9:
time: 139 us
  waiting for transfers between devices  52.3 us (38%)
  Pallas kernels  47.2 us (34%)
  starting transfers between devices  38.1 us (27%)
    ppermute x34, waiting for transfers between devices, shifted(): lax.ppermute(block, axis, [((i - distance) % size, i) for i in range(size)])  52.3 us
    ppermute x34, starting transfers between devices, shifted(): lax.ppermute(block, axis, [((i - distance) % size, i) for i in range(size)])  38.1 us
    pallas_call x15, Pallas kernels, call(): pl.pallas_call(kernel, out_shape=outs, in_specs=[anywhere if i in any_arg...  32.2 us
    pallas_call x3, Pallas kernels, chunked_call(): pl.pallas_call(kernel, grid=(PACK,), out_shape=[jax.ShapeDtypeStruct(s, B...  15 us
  transfers between devices with their start and end apart: 34, of which 21 were waited for; matrix products, arithmetic and copies ran while one was open for 0% of the time, Pallas kernels for 31%

profile of v9, /device:TPU:0, one launch (start us, length us, event | category | flops | bytes accessed | tf_op | source)
XLA Modules:
  0.0 138.7 jit_solution(3483753582729805285)
XLA Ops:
  0.6 5.1 %collective-permute-start.8 = (bf16[128,5120]{1,0:T(8,128)(2,1)}, bf16[128,5120]{1,0:T(8,128)(2,1)S(1)}, u32[]{:S(2)}, u32[]{:S(2)}) collective-permute-start(bf16[128,5120]{1,0:T(8,128)(2,1)} %param.8), channel_id=1, source_target_pairs={{8,0},{16,8},{24,16},{0,24},{9,1},{17,9},{25,17},{1,25},{10,2},{18... | collective-permute-start | bytes 3932168 | tf_op jit(solution)/shard_map/ppermute | solution.py:25
  5.7 2.9 %shard_map.110 = (bf16[80,640]{1,0:T(8,128)(2,1)S(1)}, bf16[80,640]{1,0:T(8,128)(2,1)S(1)}, bf16[128,640]{1,0:T(8,128)(2,1)}) custom-call(bf16[128,5120]{1,0:T(8,128)(2,1)} %tokens.3, s32[2,4,128]{2,1,0:T(4,128)} %bitcast.8), custom_call_target="tpu_custom_call" | custom-call | bytes 1024 | tf_op jit(solution)/shard_map/pallas_call | solution.py:38
  8.6 0.1 collective-permute-start
  8.7 1.6 %collective-permute-start.1 = (bf16[80,640]{1,0:T(8,128)(2,1)S(1)}, bf16[80,640]{1,0:T(8,128)(2,1)S(1)}, u32[]{:S(2)}, u32[]{:S(2)}) collective-permute-start(bf16[80,640]{1,0:T(8,128)(2,1)S(1)} %get-tuple-element.46.refs_0_), channel_id=1, source_target_pairs={{4,0},{6,2},{0,4},{2,6},{5,1},{7,3},{1,5},{3,7},{12,8},{14,10},{8,... | collective-permute-start | bytes 307208 | tf_op jit(solution)/shard_map/ppermute | solution.py:25
  10.2 1.4 %collective-permute-start.2 = (bf16[80,640]{1,0:T(8,128)(2,1)S(1)}, bf16[80,640]{1,0:T(8,128)(2,1)S(1)}, u32[]{:S(2)}, u32[]{:S(2)}) collective-permute-start(bf16[80,640]{1,0:T(8,128)(2,1)S(1)} %get-tuple-element.46.refs_0_), channel_id=1, source_target_pairs={{2,0},{4,2},{6,4},{0,6},{3,1},{5,3},{7,5},{1,7},{10,8},{12,10},{14... | collective-permute-start | bytes 307208 | tf_op jit(solution)/shard_map/ppermute | solution.py:25
  11.6 1.6 %collective-permute-done.refs_1_ = bf16[80,640]{1,0:T(8,128)(2,1)S(1)} collective-permute-done((bf16[80,640]{1,0:T(8,128)(2,1)S(1)}, bf16[80,640]{1,0:T(8,128)(2,1)S(1)}, u32[]{:S(2)}, u32[]{:S(2)}) %collective-permute-start) | collective-permute-done | bytes 102432 | tf_op jit(solution)/shard_map/ppermute | solution.py:25
  13.2 1.2 collective-permute-done.1.refs_2_
  14.4 0.6 collective-permute-done.2.refs_3_
  15.1 6.5 %shard_map.111 = (bf16[40,5120]{1,0:T(8,128)(2,1)S(1)}, f32[40,512]{1,0:T(8,128)S(1)}, f32[40,512]{1,0:T(8,128)S(1)}, bf16[40,512]{1,0:T(8,128)(2,1)S(1)}, bf16[...) custom-call(bf16[80,640]{1,0:T(8,128)(2,1)S(1)} %get-tuple-element.4, ...), custom_call_target="tpu_custom_call" | custom-call | bytes 1024 | tf_op jit(solution)/shard_map/pallas_call | solution.py:38
  21.6 2.3 %collective-permute-start.3 = (bf16[80,640]{1,0:T(8,128)(2,1)S(1)}, bf16[80,640]{1,0:T(8,128)(2,1)S(1)}, u32[]{:S(2)}, u32[]{:S(2)}) collective-permute-start(bf16[80,640]{1,0:T(8,128)(2,1)S(1)} %get-tuple-element.48), channel_id=1, source_target_pairs={{2,0},{4,2},{6,4},{0,6},{3,1},{5,3},{7,5},{1,7},{10,8},{12,10},{14... | collective-permute-start | bytes 307208 | tf_op jit(solution)/shard_map/ppermute | solution.py:25
  23.9 0.5 collective-permute-start.4
  24.4 0.5 collective-permute-start.6
  24.9 9.2 %collective-permute-done.6.refs_8_.next_routes = s32[1,4,128]{2,1,0:T(4,128)S(1)} collective-permute-done((s32[1,4,128]{2,1,0:T(4,128)S(1)}, s32[1,4,128]{2,1,0:T(4,128)S(1)}, u32[]{:S(2)}, u32[]{:S(2)}) %collective-permute-start.6) | collective-permute-done | bytes 2080 | tf_op jit(solution)/shard_map/ppermute | solution.py:25
  34.1 1.4 collective-permute-start.9
  35.5 0.7 shard_map.112
  36.2 3.4 %collective-permute-start.7 = (bf16[80,640]{1,0:T(8,128)(2,1)S(1)}, bf16[80,640]{1,0:T(8,128)(2,1)S(1)}, u32[]{:S(2)}, u32[]{:S(2)}) collective-permute-start(bf16[80,640]{1,0:T(8,128)(2,1)S(1)} %get-tuple-element.52), channel_id=1, source_target_pairs={{24,0},{0,8},{8,16},{16,24},{25,1},{1,9},{9,17},{17,25},{26,2},{2,... | collective-permute-start | bytes 307208 | tf_op jit(solution)/shard_map/ppermute | solution.py:25
  39.7 0.1 collective-permute-start.10
  39.7 0.9 collective-permute-start.11
  40.7 0.5 shard_map.113
  41.2 3.9 %collective-permute-done.10.___.prev_routes = s32[1,4,128]{2,1,0:T(4,128)S(1)} collective-permute-done((s32[1,4,128]{2,1,0:T(4,128)S(1)}, s32[1,4,128]{2,1,0:T(4,128)S(1)}, u32[]{:S(2)}, u32[]{:S(2)}) %collective-permute-start.10) | collective-permute-done | bytes 2080 | tf_op jit(solution)/shard_map/ppermute | solution.py:25
  45.2 0.7 collective-permute-done.11.____.prev2_routes
  45.9 0.3 shard_map.114
  46.2 2.6 %collective-permute-start.19 = (bf16[128,5120]{1,0:T(8,128)(2,1)S(1)}, bf16[128,5120]{1,0:T(8,128)(2,1)S(1)}, u32[]{:S(2)}, u32[]{:S(2)}) collective-permute-start(bf16[128,5120]{1,0:T(8,128)(2,1)S(1)} %get-tuple-element.66), channel_id=1, source_target_pairs={{8,0},{16,8},{24,16},{0,24},{9,1},{17,9},{25,17},{1,25},{10,2},{18... | collective-permute-start | bytes 3932168 | tf_op jit(solution)/shard_map/ppermute | solution.py:25
  48.8 1.5 %collective-permute-start.13 = (bf16[160,640]{1,0:T(8,128)(2,1)S(1)}, bf16[160,640]{1,0:T(8,128)(2,1)S(1)}, u32[]{:S(2)}, u32[]{:S(2)}) collective-permute-start(bf16[160,640]{1,0:T(8,128)(2,1)S(1)} %get-tuple-element.55.refs_0_), channel_id=1, source_target_pairs={{4,0},{6,2},{0,4},{2,6},{5,1},{7,3},{1,5},{3,7},{12,8},{14,10},{8,... | collective-permute-start | bytes 614408 | tf_op jit(solution)/shard_map/ppermute | solution.py:25
  50.4 1.4 %collective-permute-start.14 = (bf16[160,640]{1,0:T(8,128)(2,1)S(1)}, bf16[160,640]{1,0:T(8,128)(2,1)S(1)}, u32[]{:S(2)}, u32[]{:S(2)}) collective-permute-start(bf16[160,640]{1,0:T(8,128)(2,1)S(1)} %get-tuple-element.55.refs_0_), channel_id=1, source_target_pairs={{2,0},{4,2},{6,4},{0,6},{3,1},{5,3},{7,5},{1,7},{10,8},{12,10},{14... | collective-permute-start | bytes 614408 | tf_op jit(solution)/shard_map/ppermute | solution.py:25
  51.8 3.8 %collective-permute-done.12.refs_1_ = bf16[160,640]{1,0:T(8,128)(2,1)S(1)} collective-permute-done((bf16[160,640]{1,0:T(8,128)(2,1)S(1)}, bf16[160,640]{1,0:T(8,128)(2,1)S(1)}, u32[]{:S(2)}, u32[]{:S(2)}) %collective-permute-start.12) | collective-permute-done | bytes 204832 | tf_op jit(solution)/shard_map/ppermute | solution.py:25
  55.6 1.1 collective-permute-done.13.refs_2_
  56.7 2.9 %collective-permute-done.14.refs_3_ = bf16[160,640]{1,0:T(8,128)(2,1)S(1)} collective-permute-done((bf16[160,640]{1,0:T(8,128)(2,1)S(1)}, bf16[160,640]{1,0:T(8,128)(2,1)S(1)}, u32[]{:S(2)}, u32[]{:S(2)}) %collective-permute-start.14) | collective-permute-done | bytes 204832 | tf_op jit(solution)/shard_map/ppermute | solution.py:25
  59.6 6.8 %shard_map.115 = (bf16[40,17408]{1,0:T(8,128)(2,1)S(1)}, bf16[80,640]{1,0:T(8,128)(2,1)S(1)}, bf16[80,640]{1,0:T(8,128)(2,1)S(1)}, bf16[80,640]{1,0:T(8,128)(2,1)S(1)}, bf16[80,640]{1,0:T(8,128)(2,1)S(1)}) custom-call(bf16[160,640]{1,0:T(8,128)(2,1)S(1)} %get-tuple-element.55.refs_0_, bf16[160,640]{1,0:T(8,128)(2,1)S(1)} %collective-permute-done.12.refs_1_, ...), custom_call_target="tpu_custom_call" | custom-call | bytes 1024 | tf_op jit(solution)/shard_map/pallas_call | solution.py:38
  66.5 1.6 %collective-permute-start.32 = (bf16[40,17408]{1,0:T(8,128)(2,1)S(1)}, bf16[40,17408]{1,0:T(8,128)(2,1)S(1)}, u32[]{:S(2)}, u32[]{:S(2)}) collective-permute-start(bf16[40,17408]{1,0:T(8,128)(2,1)S(1)} %get-tuple-element.77.act.refs_0_.refs_2_.refs_4_.refs_6_), channel_id=1, source_target_pairs={{1,0},{0,1},{3,2},{2,3},{5,4},{4,5},{7,6},{6,7},{9,8},{8,9},{11,10... | collective-permute-start | bytes 4177928 | tf_op jit(solution)/shard_map/ppermute | solution.py:25
  68.0 1.9 %collective-permute-start.15 = (bf16[80,640]{1,0:T(8,128)(2,1)S(1)}, bf16[80,640]{1,0:T(8,128)(2,1)S(1)}, u32[]{:S(2)}, u32[]{:S(2)}) collective-permute-start(bf16[80,640]{1,0:T(8,128)(2,1)S(1)} %get-tuple-element.62), channel_id=1, source_target_pairs={{2,0},{4,2},{6,4},{0,6},{3,1},{5,3},{7,5},{1,7},{10,8},{12,10},{14... | collective-permute-start | bytes 307208 | tf_op jit(solution)/shard_map/ppermute | solution.py:25
  70.0 0.5 collective-permute-start.16
  70.5 2.4 %collective-permute-done.15.refs_1_ = bf16[80,640]{1,0:T(8,128)(2,1)S(1)} collective-permute-done((bf16[80,640]{1,0:T(8,128)(2,1)S(1)}, bf16[80,640]{1,0:T(8,128)(2,1)S(1)}, u32[]{:S(2)}, u32[]{:S(2)}) %collective-permute-start.15) | collective-permute-done | bytes 102432 | tf_op jit(solution)/shard_map/ppermute | solution.py:25
  72.8 3.0 %collective-permute-done.16.refs_2_ = bf16[80,640]{1,0:T(8,128)(2,1)S(1)} collective-permute-done((bf16[80,640]{1,0:T(8,128)(2,1)S(1)}, bf16[80,640]{1,0:T(8,128)(2,1)S(1)}, u32[]{:S(2)}, u32[]{:S(2)}) %collective-permute-start.16) | collective-permute-done | bytes 102432 | tf_op jit(solution)/shard_map/ppermute | solution.py:25
  75.8 0.5 shard_map.116
  76.3 0.6 collective-permute-start.18
  76.9 0.7 shard_map.117._
  77.6 3.4 %collective-permute-done.18.___.upd1.refs_7_ = bf16[80,640]{1,0:T(8,128)(2,1)S(1)} collective-permute-done((bf16[80,640]{1,0:T(8,128)(2,1)S(1)}, bf16[80,640]{1,0:T(8,128)(2,1)S(1)}, u32[]{:S(2)}, u32[]{:S(2)}) %collective-permute-start.18) | collective-permute-done | bytes 102432 | tf_op jit(solution)/shard_map/ppermute | solution.py:25
  81.0 0.8 shard_map.119
  81.8 0.1 collective-permute-start.20
  81.9 1.6 %collective-permute-start.21 = (bf16[80,640]{1,0:T(8,128)(2,1)S(1)}, bf16[80,640]{1,0:T(8,128)(2,1)S(1)}, u32[]{:S(2)}, u32[]{:S(2)}) collective-permute-start(bf16[80,640]{1,0:T(8,128)(2,1)S(1)} %get-tuple-element.68.refs_0_), channel_id=1, source_target_pairs={{4,0},{6,2},{0,4},{2,6},{5,1},{7,3},{1,5},{3,7},{12,8},{14,10},{8,... | collective-permute-start | bytes 307208 | tf_op jit(solution)/shard_map/ppermute | solution.py:25
  83.5 1.4 %collective-permute-start.22 = (bf16[80,640]{1,0:T(8,128)(2,1)S(1)}, bf16[80,640]{1,0:T(8,128)(2,1)S(1)}, u32[]{:S(2)}, u32[]{:S(2)}) collective-permute-start(bf16[80,640]{1,0:T(8,128)(2,1)S(1)} %get-tuple-element.68.refs_0_), channel_id=1, source_target_pairs={{2,0},{4,2},{6,4},{0,6},{3,1},{5,3},{7,5},{1,7},{10,8},{12,10},{14... | collective-permute-start | bytes 307208 | tf_op jit(solution)/shard_map/ppermute | solution.py:25
  84.9 1.6 %collective-permute-done.20.refs_1_ = bf16[80,640]{1,0:T(8,128)(2,1)S(1)} collective-permute-done((bf16[80,640]{1,0:T(8,128)(2,1)S(1)}, bf16[80,640]{1,0:T(8,128)(2,1)S(1)}, u32[]{:S(2)}, u32[]{:S(2)}) %collective-permute-start.20) | collective-permute-done | bytes 102432 | tf_op jit(solution)/shard_map/ppermute | solution.py:25
  86.4 1.2 collective-permute-done.21.refs_2_
  87.7 0.6 collective-permute-done.22.refs_3_
  88.3 5.1 %shard_map.120 = (bf16[40,6144]{1,0:T(8,128)(2,1)S(1)}, bf16[80,640]{1,0:T(8,128)(2,1)S(1)}, bf16[80,640]{1,0:T(8,128)(2,1)S(1)}, bf16[80,640]{1,0:T(8,128)(2,1)S(1)}, bf16[80,640]{1,0:T(8,128)(2,1)S(1)}) custom-call(bf16[80,640]{1,0:T(8,128)(2,1)S(1)} %get-tuple-element.68.refs_0_, bf16[80,640]{1,0:T(8,128)(2,1)S(1)} %collective-permute-done.20.refs_1_, ...), custom_call_target="tpu_custom_call" | custom-call | bytes 1024 | tf_op jit(solution)/shard_map/pallas_call | solution.py:38
  93.4 1.1 collective-permute-start.33
  94.5 1.9 %collective-permute-start.23 = (bf16[80,640]{1,0:T(8,128)(2,1)S(1)}, bf16[80,640]{1,0:T(8,128)(2,1)S(1)}, u32[]{:S(2)}, u32[]{:S(2)}) collective-permute-start(bf16[80,640]{1,0:T(8,128)(2,1)S(1)} %get-tuple-element.72), channel_id=1, source_target_pairs={{2,0},{4,2},{6,4},{0,6},{3,1},{5,3},{7,5},{1,7},{10,8},{12,10},{14... | collective-permute-start | bytes 307208 | tf_op jit(solution)/shard_map/ppermute | solution.py:25
  96.4 1.1 shard_map.122
  97.6 1.1 collective-permute-done.23.refs_1_
  98.7 0.5 collective-permute-start.29
  99.2 0.7 collective-permute-done.28.refs_1_
  99.8 1.1 collective-permute-start.30
  100.9 3.5 %collective-permute-done.29.refs_2_ = bf16[80,640]{1,0:T(8,128)(2,1)S(1)} collective-permute-done((bf16[80,640]{1,0:T(8,128)(2,1)S(1)}, bf16[80,640]{1,0:T(8,128)(2,1)S(1)}, u32[]{:S(2)}, u32[]{:S(2)}) %collective-permute-start.29) | collective-permute-done | bytes 102432 | tf_op jit(solution)/shard_map/ppermute | solution.py:25
  104.4 1.1 collective-permute-done.30.refs_3_
  105.5 0.2 shard_map.123
  105.8 4.4 %collective-permute-done.24.refs_2_ = bf16[80,640]{1,0:T(8,128)(2,1)S(1)} collective-permute-done((bf16[80,640]{1,0:T(8,128)(2,1)S(1)}, bf16[80,640]{1,0:T(8,128)(2,1)S(1)}, u32[]{:S(2)}, u32[]{:S(2)}) %collective-permute-start.24) | collective-permute-done | bytes 102432 | tf_op jit(solution)/shard_map/ppermute | solution.py:25
  110.1 3.0 %collective-permute-start.31 = (bf16[80,640]{1,0:T(8,128)(2,1)S(1)}, bf16[80,640]{1,0:T(8,128)(2,1)S(1)}, u32[]{:S(2)}, u32[]{:S(2)}) collective-permute-start(bf16[80,640]{1,0:T(8,128)(2,1)S(1)} %shard_map.123), channel_id=1, source_target_pairs={{24,0},{0,8},{8,16},{16,24},{25,1},{1,9},{9,17},{17,25},{26,2},{2,... | collective-permute-start | bytes 307208 | tf_op jit(solution)/shard_map/ppermute | solution.py:25
  113.1 2.4 %shard_map.121 = bf16[128,5120]{1,0:T(8,128)(2,1)} custom-call(bf16[80,640]{1,0:T(8,128)(2,1)S(1)} %get-tuple-element.71.refs_0_, bf16[80,640]{1,0:T(8,128)(2,1)S(1)} %collective-permute-done.23.refs_1_, bf16[80,640]{1,0:T(8,128)(2,1)S(1)} %collective-permute-done.24.refs_2_, bf16[80,640]{1,0:T(8,128)(2,1)S(1)} %collective-permute-done.25.refs_3_, ...), custom_call_target="tpu_custom_call" | custom-call | bytes 1024 | tf_op jit(solution)/shard_map/pallas_call | solution.py:38
  115.6 2.9 %shard_map.125 = (bf16[5120,160]{1,0:T(8,128)(2,1)S(1)}, bf16[512,160]{1,0:T(8,128)(2,1)S(1)}) custom-call(bf16[40,17408]{1,0:T(8,128)(2,1)S(1)} %get-tuple-element.77.act.refs_0_.refs_2_.refs_4_.refs_6_, bf16[40,17408]{1,0:T(8,128)(2,1)S(1)} %collective-permute-done.32.refs_1_.refs_3_.refs_5_.refs_7_, ...), custom_call_target="tpu_custom_call" | custom-call | bytes 1024 | tf_op jit(solution)/shard_map/pallas_call | solution.py:433
  118.4 6.2 %shard_map.126 = (bf16[5120,512]{1,0:T(8,128)(2,1)}, bf16[5120,512]{1,0:T(8,128)(2,1)}) custom-call(bf16[5120,160]{1,0:T(8,128)(2,1)S(1)} %get-tuple-element.83.x_t, bf16[40,6144]{1,0:T(8,128)(2,1)S(1)} %get-tuple-element.78._.refs_0_.refs_2_, bf16[40,6144]{1,0:T(8,128)(2,1)S(1)} %collective-permute-done.33.refs_1_.refs_3_, ...), custom_call_target="tpu_custom_call" | custom-call | bytes 1024 | tf_op jit(solution)/shard_map/pallas_call | solution.py:433
  124.7 5.9 %shard_map.127 = bf16[512,5120]{1,0:T(8,128)(2,1)} custom-call(bf16[512,160]{1,0:T(8,128)(2,1)S(1)} %get-tuple-element.86.act_t, bf16[40,6144]{1,0:T(8,128)(2,1)S(1)} %get-tuple-element.78._.refs_0_.refs_2_, bf16[40,6144]{1,0:T(8,128)(2,1)S(1)} %collective-permute-done.33.refs_1_.refs_3_, ...), custom_call_target="tpu_custom_call" | custom-call | bytes 1024 | tf_op jit(solution)/shard_map/pallas_call | solution.py:433
  130.6 4.3 %collective-permute-done.27.part = bf16[16,640]{1,0:T(8,128)(2,1)S(1)} collective-permute-done((bf16[16,640]{1,0:T(8,128)(2,1)S(1)}, bf16[16,640]{1,0:T(8,128)(2,1)S(1)}, u32[]{:S(2)}, u32[]{:S(2)}) %collective-permute-start.27) | collective-permute-done | bytes 20512 | tf_op jit(solution)/shard_map/ppermute | solution.py:25
  134.9 3.6 %shard_map.124 = bf16[128,5120]{1,0:T(8,128)(2,1)} custom-call(bf16[128,640]{1,0:T(8,128)(2,1)S(1)} %collective-permute-done.9.__.early, bf16[128,4480]{1,0:T(8,128)(2,1)S(1)} %collective-permute-done.26.rest, bf16[16,640]{1,0:T(8,128)(2,1)S(1)} %collective-permute-done.27.part, s32[1,4,128]{2,1,0:T(4,128)S(1)} %collective-permute-done.11.____.prev2_routes, ...), custom_call_target="tpu_custom_call" | custom-call | bytes 1024 | tf_op jit(solution)/shard_map/pallas_call | solution.py:38
  (31 shorter events, 0.1 us)
Async XLA Ops:
  0.6 40.1 %collective-permute-start.8 = (bf16[128,5120]{1,0:T(8,128)(2,1)}, bf16[128,5120]{1,0:T(8,128)(2,1)S(1)}, u32[]{:S(2)}, u32[]{:S(2)}) collective-permute-start(bf16[128,5120]{1,0:T(8,128)(2,1)} %param.8), channel_id=1, source_target_pairs={{8,0},{16,8},{24,16},{0,24},{9,1},{17,9},{25,17},{1,25},{10,2},{18... | collective-permute-start | bytes 3932168 | tf_op jit(solution)/shard_map/ppermute | solution.py:25
  8.6 4.6 %collective-permute-start = (bf16[80,640]{1,0:T(8,128)(2,1)S(1)}, bf16[80,640]{1,0:T(8,128)(2,1)S(1)}, u32[]{:S(2)}, u32[]{:S(2)}) collective-permute-start(bf16[80,640]{1,0:T(8,128)(2,1)S(1)} %get-tuple-element.46.refs_0_), channel_id=1, source_target_pairs={{6,0},{0,2},{2,4},{4,6},{7,1},{1,3},{3,5},{5,7},{14,8},{8,10},{10,... | collective-permute-start | bytes 307208 | tf_op jit(solution)/shard_map/ppermute | solution.py:25
  8.7 5.8 %collective-permute-start.1 = (bf16[80,640]{1,0:T(8,128)(2,1)S(1)}, bf16[80,640]{1,0:T(8,128)(2,1)S(1)}, u32[]{:S(2)}, u32[]{:S(2)}) collective-permute-start(bf16[80,640]{1,0:T(8,128)(2,1)S(1)} %get-tuple-element.46.refs_0_), channel_id=1, source_target_pairs={{4,0},{6,2},{0,4},{2,6},{5,1},{7,3},{1,5},{3,7},{12,8},{14,10},{8,... | collective-permute-start | bytes 307208 | tf_op jit(solution)/shard_map/ppermute | solution.py:25
  10.2 4.8 %collective-permute-start.2 = (bf16[80,640]{1,0:T(8,128)(2,1)S(1)}, bf16[80,640]{1,0:T(8,128)(2,1)S(1)}, u32[]{:S(2)}, u32[]{:S(2)}) collective-permute-start(bf16[80,640]{1,0:T(8,128)(2,1)S(1)} %get-tuple-element.46.refs_0_), channel_id=1, source_target_pairs={{2,0},{4,2},{6,4},{0,6},{3,1},{5,3},{7,5},{1,7},{10,8},{12,10},{14... | collective-permute-start | bytes 307208 | tf_op jit(solution)/shard_map/ppermute | solution.py:25
  15.1 9.3 %copy-start.1 = (s32[2,128,4]{1,2,0:T(4,128)S(1)}, s32[2,128,4]{1,2,0:T(4,128)}, u32[]{:S(2)}) copy-start(s32[2,128,4]{1,2,0:T(4,128)} %param.12) | copy-start | bytes 12292
  15.1 19.0 %copy-start.3 = (bf16[128,640]{1,0:T(8,128)(2,1)S(1)}, bf16[128,640]{1,0:T(8,128)(2,1)}, u32[]{:S(2)}) copy-start(bf16[128,640]{1,0:T(8,128)(2,1)} %get-tuple-element.54) | copy-start | bytes 491524
  15.1 20.4 %copy-start = (bf16[128,5120]{1,0:T(8,128)(2,1)S(1)}, bf16[128,5120]{1,0:T(8,128)(2,1)}, u32[]{:S(2)}) copy-start(bf16[128,5120]{1,0:T(8,128)(2,1)} %tokens.3) | copy-start | bytes 3932164
  15.1 20.5 %copy-start.2 = (f32[2,128,4]{1,2,0:T(4,128)S(1)}, f32[2,128,4]{1,2,0:T(4,128)}, u32[]{:S(2)}) copy-start(f32[2,128,4]{1,2,0:T(4,128)} %param.13) | copy-start | bytes 12292
  21.6 13.9 %collective-permute-start.3 = (bf16[80,640]{1,0:T(8,128)(2,1)S(1)}, bf16[80,640]{1,0:T(8,128)(2,1)S(1)}, u32[]{:S(2)}, u32[]{:S(2)}) collective-permute-start(bf16[80,640]{1,0:T(8,128)(2,1)S(1)} %get-tuple-element.48), channel_id=1, source_target_pairs={{2,0},{4,2},{6,4},{0,6},{3,1},{5,3},{7,5},{1,7},{10,8},{12,10},{14... | collective-permute-start | bytes 307208 | tf_op jit(solution)/shard_map/ppermute | solution.py:25
  23.9 11.6 %collective-permute-start.4 = (bf16[80,640]{1,0:T(8,128)(2,1)S(1)}, bf16[80,640]{1,0:T(8,128)(2,1)S(1)}, u32[]{:S(2)}, u32[]{:S(2)}) collective-permute-start(bf16[80,640]{1,0:T(8,128)(2,1)S(1)} %get-tuple-element.49), channel_id=1, source_target_pairs={{4,0},{6,2},{0,4},{2,6},{5,1},{7,3},{1,5},{3,7},{12,8},{14,10},{8,... | collective-permute-start | bytes 307208 | tf_op jit(solution)/shard_map/ppermute | solution.py:25
  24.4 11.1 %collective-permute-start.5 = (bf16[80,640]{1,0:T(8,128)(2,1)S(1)}, bf16[80,640]{1,0:T(8,128)(2,1)S(1)}, u32[]{:S(2)}, u32[]{:S(2)}) collective-permute-start(bf16[80,640]{1,0:T(8,128)(2,1)S(1)} %get-tuple-element.50), channel_id=1, source_target_pairs={{6,0},{0,2},{2,4},{4,6},{7,1},{1,3},{3,5},{5,7},{14,8},{8,10},{10,... | collective-permute-start | bytes 307208 | tf_op jit(solution)/shard_map/ppermute | solution.py:25
  24.4 9.7 %collective-permute-start.6 = (s32[1,4,128]{2,1,0:T(4,128)S(1)}, s32[1,4,128]{2,1,0:T(4,128)S(1)}, u32[]{:S(2)}, u32[]{:S(2)}) collective-permute-start(s32[1,4,128]{2,1,0:T(4,128)S(1)} %get-tuple-element.88), channel_id=1, source_target_pairs={{8,0},{16,8},{24,16},{0,24},{9,1},{17,9},{25,17},{1,25},{10,2},{18... | collective-permute-start | bytes 6152 | tf_op jit(solution)/shard_map/ppermute | solution.py:25
  34.1 11.8 %collective-permute-start.9 = (bf16[128,640]{1,0:T(8,128)(2,1)S(1)}, bf16[128,640]{1,0:T(8,128)(2,1)S(1)}, u32[]{:S(2)}, u32[]{:S(2)}) collective-permute-start(bf16[128,640]{1,0:T(8,128)(2,1)S(1)} %copy-done.3), channel_id=1, source_target_pairs={{16,0},{24,8},{0,16},{8,24},{17,1},{25,9},{1,17},{9,25},{18,2},{26... | collective-permute-start | bytes 491528 | tf_op jit(solution)/shard_map/ppermute | solution.py:25
  36.2 9.6 %collective-permute-start.7 = (bf16[80,640]{1,0:T(8,128)(2,1)S(1)}, bf16[80,640]{1,0:T(8,128)(2,1)S(1)}, u32[]{:S(2)}, u32[]{:S(2)}) collective-permute-start(bf16[80,640]{1,0:T(8,128)(2,1)S(1)} %get-tuple-element.52), channel_id=1, source_target_pairs={{24,0},{0,8},{8,16},{16,24},{25,1},{1,9},{9,17},{17,25},{26,2},{2,... | collective-permute-start | bytes 307208 | tf_op jit(solution)/shard_map/ppermute | solution.py:25
  39.7 5.5 %collective-permute-start.10 = (s32[1,4,128]{2,1,0:T(4,128)S(1)}, s32[1,4,128]{2,1,0:T(4,128)S(1)}, u32[]{:S(2)}, u32[]{:S(2)}) collective-permute-start(s32[1,4,128]{2,1,0:T(4,128)S(1)} %get-tuple-element.88), channel_id=1, source_target_pairs={{24,0},{0,8},{8,16},{16,24},{25,1},{1,9},{9,17},{17,25},{26,2},{2,... | collective-permute-start | bytes 6152 | tf_op jit(solution)/shard_map/ppermute | solution.py:25
  39.7 6.1 %collective-permute-start.11 = (s32[1,4,128]{2,1,0:T(4,128)S(1)}, s32[1,4,128]{2,1,0:T(4,128)S(1)}, u32[]{:S(2)}, u32[]{:S(2)}) collective-permute-start(s32[1,4,128]{2,1,0:T(4,128)S(1)} %get-tuple-element.87), channel_id=1, source_target_pairs={{16,0},{24,8},{0,16},{8,24},{17,1},{25,9},{1,17},{9,25},{18,2},{26... | collective-permute-start | bytes 6152 | tf_op jit(solution)/shard_map/ppermute | solution.py:25
  46.2 34.8 %collective-permute-start.19 = (bf16[128,5120]{1,0:T(8,128)(2,1)S(1)}, bf16[128,5120]{1,0:T(8,128)(2,1)S(1)}, u32[]{:S(2)}, u32[]{:S(2)}) collective-permute-start(bf16[128,5120]{1,0:T(8,128)(2,1)S(1)} %get-tuple-element.66), channel_id=1, source_target_pairs={{8,0},{16,8},{24,16},{0,24},{9,1},{17,9},{25,17},{1,25},{10,2},{18... | collective-permute-start | bytes 3932168 | tf_op jit(solution)/shard_map/ppermute | solution.py:25
  48.8 6.8 %collective-permute-start.12 = (bf16[160,640]{1,0:T(8,128)(2,1)S(1)}, bf16[160,640]{1,0:T(8,128)(2,1)S(1)}, u32[]{:S(2)}, u32[]{:S(2)}) collective-permute-start(bf16[160,640]{1,0:T(8,128)(2,1)S(1)} %get-tuple-element.55.refs_0_), channel_id=1, source_target_pairs={{6,0},{0,2},{2,4},{4,6},{7,1},{1,3},{3,5},{5,7},{14,8},{8,10},{10,... | collective-permute-start | bytes 614408 | tf_op jit(solution)/shard_map/ppermute | solution.py:25
  48.8 7.9 %collective-permute-start.13 = (bf16[160,640]{1,0:T(8,128)(2,1)S(1)}, bf16[160,640]{1,0:T(8,128)(2,1)S(1)}, u32[]{:S(2)}, u32[]{:S(2)}) collective-permute-start(bf16[160,640]{1,0:T(8,128)(2,1)S(1)} %get-tuple-element.55.refs_0_), channel_id=1, source_target_pairs={{4,0},{6,2},{0,4},{2,6},{5,1},{7,3},{1,5},{3,7},{12,8},{14,10},{8,... | collective-permute-start | bytes 614408 | tf_op jit(solution)/shard_map/ppermute | solution.py:25
  50.4 9.3 %collective-permute-start.14 = (bf16[160,640]{1,0:T(8,128)(2,1)S(1)}, bf16[160,640]{1,0:T(8,128)(2,1)S(1)}, u32[]{:S(2)}, u32[]{:S(2)}) collective-permute-start(bf16[160,640]{1,0:T(8,128)(2,1)S(1)} %get-tuple-element.55.refs_0_), channel_id=1, source_target_pairs={{2,0},{4,2},{6,4},{0,6},{3,1},{5,3},{7,5},{1,7},{10,8},{12,10},{14... | collective-permute-start | bytes 614408 | tf_op jit(solution)/shard_map/ppermute | solution.py:25
  66.5 49.1 %collective-permute-start.32 = (bf16[40,17408]{1,0:T(8,128)(2,1)S(1)}, bf16[40,17408]{1,0:T(8,128)(2,1)S(1)}, u32[]{:S(2)}, u32[]{:S(2)}) collective-permute-start(bf16[40,17408]{1,0:T(8,128)(2,1)S(1)} %get-tuple-element.77.act.refs_0_.refs_2_.refs_4_.refs_6_), channel_id=1, source_target_pairs={{1,0},{0,1},{3,2},{2,3},{5,4},{4,5},{7,6},{6,7},{9,8},{8,9},{11,10... | collective-permute-start | bytes 4177928 | tf_op jit(solution)/shard_map/ppermute | solution.py:25
  68.0 4.8 %collective-permute-start.15 = (bf16[80,640]{1,0:T(8,128)(2,1)S(1)}, bf16[80,640]{1,0:T(8,128)(2,1)S(1)}, u32[]{:S(2)}, u32[]{:S(2)}) collective-permute-start(bf16[80,640]{1,0:T(8,128)(2,1)S(1)} %get-tuple-element.62), channel_id=1, source_target_pairs={{2,0},{4,2},{6,4},{0,6},{3,1},{5,3},{7,5},{1,7},{10,8},{12,10},{14... | collective-permute-start | bytes 307208 | tf_op jit(solution)/shard_map/ppermute | solution.py:25
  70.0 5.9 %collective-permute-start.16 = (bf16[80,640]{1,0:T(8,128)(2,1)S(1)}, bf16[80,640]{1,0:T(8,128)(2,1)S(1)}, u32[]{:S(2)}, u32[]{:S(2)}) collective-permute-start(bf16[80,640]{1,0:T(8,128)(2,1)S(1)} %get-tuple-element.63), channel_id=1, source_target_pairs={{4,0},{6,2},{0,4},{2,6},{5,1},{7,3},{1,5},{3,7},{12,8},{14,10},{8,... | collective-permute-start | bytes 307208 | tf_op jit(solution)/shard_map/ppermute | solution.py:25
  70.5 5.4 %collective-permute-start.17 = (bf16[80,640]{1,0:T(8,128)(2,1)S(1)}, bf16[80,640]{1,0:T(8,128)(2,1)S(1)}, u32[]{:S(2)}, u32[]{:S(2)}) collective-permute-start(bf16[80,640]{1,0:T(8,128)(2,1)S(1)} %get-tuple-element.64), channel_id=1, source_target_pairs={{6,0},{0,2},{2,4},{4,6},{7,1},{1,3},{3,5},{5,7},{14,8},{8,10},{10,... | collective-permute-start | bytes 307208 | tf_op jit(solution)/shard_map/ppermute | solution.py:25
  76.3 4.7 %collective-permute-start.18 = (bf16[80,640]{1,0:T(8,128)(2,1)S(1)}, bf16[80,640]{1,0:T(8,128)(2,1)S(1)}, u32[]{:S(2)}, u32[]{:S(2)}) collective-permute-start(bf16[80,640]{1,0:T(8,128)(2,1)S(1)} %shard_map.116), channel_id=1, source_target_pairs={{8,0},{16,8},{24,16},{0,24},{9,1},{17,9},{25,17},{1,25},{10,2},{18... | collective-permute-start | bytes 307208 | tf_op jit(solution)/shard_map/ppermute | solution.py:25
  81.0 53.8 %collective-permute-start.26 = (bf16[128,4480]{1,0:T(8,128)(2,1)S(1)}, bf16[128,4480]{1,0:T(8,128)(2,1)S(1)}, u32[]{:S(2)}, u32[]{:S(2)}) collective-permute-start(bf16[128,4480]{1,0:T(8,128)(2,1)S(1)} %shard_map.118._), channel_id=1, source_target_pairs={{16,0},{24,8},{0,16},{8,24},{17,1},{25,9},{1,17},{9,25},{18,2},{26... | collective-permute-start | bytes 3440648 | tf_op jit(solution)/shard_map/ppermute | solution.py:25
  81.8 4.6 %collective-permute-start.20 = (bf16[80,640]{1,0:T(8,128)(2,1)S(1)}, bf16[80,640]{1,0:T(8,128)(2,1)S(1)}, u32[]{:S(2)}, u32[]{:S(2)}) collective-permute-start(bf16[80,640]{1,0:T(8,128)(2,1)S(1)} %get-tuple-element.68.refs_0_), channel_id=1, source_target_pairs={{6,0},{0,2},{2,4},{4,6},{7,1},{1,3},{3,5},{5,7},{14,8},{8,10},{10,... | collective-permute-start | bytes 307208 | tf_op jit(solution)/shard_map/ppermute | solution.py:25
  81.9 5.8 %collective-permute-start.21 = (bf16[80,640]{1,0:T(8,128)(2,1)S(1)}, bf16[80,640]{1,0:T(8,128)(2,1)S(1)}, u32[]{:S(2)}, u32[]{:S(2)}) collective-permute-start(bf16[80,640]{1,0:T(8,128)(2,1)S(1)} %get-tuple-element.68.refs_0_), channel_id=1, source_target_pairs={{4,0},{6,2},{0,4},{2,6},{5,1},{7,3},{1,5},{3,7},{12,8},{14,10},{8,... | collective-permute-start | bytes 307208 | tf_op jit(solution)/shard_map/ppermute | solution.py:25
  83.5 4.8 %collective-permute-start.22 = (bf16[80,640]{1,0:T(8,128)(2,1)S(1)}, bf16[80,640]{1,0:T(8,128)(2,1)S(1)}, u32[]{:S(2)}, u32[]{:S(2)}) collective-permute-start(bf16[80,640]{1,0:T(8,128)(2,1)S(1)} %get-tuple-element.68.refs_0_), channel_id=1, source_target_pairs={{2,0},{4,2},{6,4},{0,6},{3,1},{5,3},{7,5},{1,7},{10,8},{12,10},{14... | collective-permute-start | bytes 307208 | tf_op jit(solution)/shard_map/ppermute | solution.py:25
  93.4 25.1 %collective-permute-start.33 = (bf16[40,6144]{1,0:T(8,128)(2,1)S(1)}, bf16[40,6144]{1,0:T(8,128)(2,1)S(1)}, u32[]{:S(2)}, u32[]{:S(2)}) collective-permute-start(bf16[40,6144]{1,0:T(8,128)(2,1)S(1)} %get-tuple-element.78._.refs_0_.refs_2_), channel_id=1, source_target_pairs={{1,0},{0,1},{3,2},{2,3},{5,4},{4,5},{7,6},{6,7},{9,8},{8,9},{11,10... | collective-permute-start | bytes 1474568 | tf_op jit(solution)/shard_map/ppermute | solution.py:25
  94.5 4.2 %collective-permute-start.23 = (bf16[80,640]{1,0:T(8,128)(2,1)S(1)}, bf16[80,640]{1,0:T(8,128)(2,1)S(1)}, u32[]{:S(2)}, u32[]{:S(2)}) collective-permute-start(bf16[80,640]{1,0:T(8,128)(2,1)S(1)} %get-tuple-element.72), channel_id=1, source_target_pairs={{2,0},{4,2},{6,4},{0,6},{3,1},{5,3},{7,5},{1,7},{10,8},{12,10},{14... | collective-permute-start | bytes 307208 | tf_op jit(solution)/shard_map/ppermute | solution.py:25
  97.5 2.3 %collective-permute-start.28 = (bf16[80,640]{1,0:T(8,128)(2,1)S(1)}, bf16[80,640]{1,0:T(8,128)(2,1)S(1)}, u32[]{:S(2)}, u32[]{:S(2)}) collective-permute-start(bf16[80,640]{1,0:T(8,128)(2,1)S(1)} %get-tuple-element.80), channel_id=1, source_target_pairs={{2,0},{4,2},{6,4},{0,6},{3,1},{5,3},{7,5},{1,7},{10,8},{12,10},{14... | collective-permute-start | bytes 307208 | tf_op jit(solution)/shard_map/ppermute | solution.py:25
  98.7 5.7 %collective-permute-start.29 = (bf16[80,640]{1,0:T(8,128)(2,1)S(1)}, bf16[80,640]{1,0:T(8,128)(2,1)S(1)}, u32[]{:S(2)}, u32[]{:S(2)}) collective-permute-start(bf16[80,640]{1,0:T(8,128)(2,1)S(1)} %get-tuple-element.81), channel_id=1, source_target_pairs={{4,0},{6,2},{0,4},{2,6},{5,1},{7,3},{1,5},{3,7},{12,8},{14,10},{8,... | collective-permute-start | bytes 307208 | tf_op jit(solution)/shard_map/ppermute | solution.py:25
  99.8 5.7 %collective-permute-start.30 = (bf16[80,640]{1,0:T(8,128)(2,1)S(1)}, bf16[80,640]{1,0:T(8,128)(2,1)S(1)}, u32[]{:S(2)}, u32[]{:S(2)}) collective-permute-start(bf16[80,640]{1,0:T(8,128)(2,1)S(1)} %get-tuple-element.82), channel_id=1, source_target_pairs={{6,0},{0,2},{2,4},{4,6},{7,1},{1,3},{3,5},{5,7},{14,8},{8,10},{10,... | collective-permute-start | bytes 307208 | tf_op jit(solution)/shard_map/ppermute | solution.py:25
  104.4 5.7 %collective-permute-start.24 = (bf16[80,640]{1,0:T(8,128)(2,1)S(1)}, bf16[80,640]{1,0:T(8,128)(2,1)S(1)}, u32[]{:S(2)}, u32[]{:S(2)}) collective-permute-start(bf16[80,640]{1,0:T(8,128)(2,1)S(1)} %get-tuple-element.73), channel_id=1, source_target_pairs={{4,0},{6,2},{0,4},{2,6},{5,1},{7,3},{1,5},{3,7},{12,8},{14,10},{8,... | collective-permute-start | bytes 307208 | tf_op jit(solution)/shard_map/ppermute | solution.py:25
  105.5 7.6 %collective-permute-start.25 = (bf16[80,640]{1,0:T(8,128)(2,1)S(1)}, bf16[80,640]{1,0:T(8,128)(2,1)S(1)}, u32[]{:S(2)}, u32[]{:S(2)}) collective-permute-start(bf16[80,640]{1,0:T(8,128)(2,1)S(1)} %get-tuple-element.74), channel_id=1, source_target_pairs={{6,0},{0,2},{2,4},{4,6},{7,1},{1,3},{3,5},{5,7},{14,8},{8,10},{10,... | collective-permute-start | bytes 307208 | tf_op jit(solution)/shard_map/ppermute | solution.py:25
  110.1 24.7 %collective-permute-start.31 = (bf16[80,640]{1,0:T(8,128)(2,1)S(1)}, bf16[80,640]{1,0:T(8,128)(2,1)S(1)}, u32[]{:S(2)}, u32[]{:S(2)}) collective-permute-start(bf16[80,640]{1,0:T(8,128)(2,1)S(1)} %shard_map.123), channel_id=1, source_target_pairs={{24,0},{0,8},{8,16},{16,24},{25,1},{1,9},{9,17},{17,25},{26,2},{2,... | collective-permute-start | bytes 307208 | tf_op jit(solution)/shard_map/ppermute | solution.py:25
  113.1 21.7 %collective-permute-start.27 = (bf16[16,640]{1,0:T(8,128)(2,1)S(1)}, bf16[16,640]{1,0:T(8,128)(2,1)S(1)}, u32[]{:S(2)}, u32[]{:S(2)}) collective-permute-start(bf16[16,640]{1,0:T(8,128)(2,1)S(1)} %get-tuple-element.76), channel_id=1, source_target_pairs={{16,0},{24,8},{0,16},{8,24},{17,1},{25,9},{1,17},{9,25},{18,2},{26... | collective-permute-start | bytes 61448 | tf_op jit(solution)/shard_map/ppermute | solution.py:25

commit v10 on v9

--- a/solution.py
+++ b/solution.py
@@ -203,7 +203,8 @@
     upd[...] = (h[...].astype(F32) + weight * summed(parts)).astype(BF16)
 
 
-def enter1_kernel(h, scaled, _, __, ___, ____, out, _____):
+def enter1_kernel(h, scaled, *refs):
+    out = refs[-2]
     values = h[...].astype(F32)
     out[:PACKED] = (values * inv_rms_of(values)).astype(BF16)
     out[PACKED:] = scaled[...]
@@ -241,26 +242,21 @@
         out[:, k] = placed(chunk, value, second, hit2, fresh)
 
 
-def finish_state_kernel(
-    early, rest, part, prev2_routes, upd1, prev_routes, out, ins, outs, in_sems, out_sems
-):
-    fetches = start_rows(rest, ins, in_sems)
+def finish_state_kernel(early, rest, part, prev2_routes, upd1, prev_routes, out, outs, sems):
     height, width = out.shape
     first, second = select_of(prev2_routes[0]), select_of(prev_routes[0])
     hit1, hit2 = hit_rows(first), hit_rows(second)
-    for c in range(EARLY):
-        old = early[c * height : (c + 1) * height]
-        rows = jnp.concatenate(
-            [part[...].astype(F32), jnp.zeros((PACKED - part.shape[0], part.shape[1]), F32)], axis=0
-        )
-        value = placed(c, old, first, hit1, rows.astype(BF16))
+    rows = jnp.concatenate(
+        [part[...].astype(F32), jnp.zeros((PACKED - part.shape[0], part.shape[1]), F32)], axis=0
+    )
+    for c in range(PACK):
+        if c < EARLY:
+            old = early[c * height : (c + 1) * height]
+            value = placed(c, old, first, hit1, rows.astype(BF16))
+        else:
+            value = rest[:, columns(c - EARLY, width)]
         outs[:, columns(c, width)] = placed(c, value, second, hit2, upd1[...])
-    for fetch in fetches:
-        fetch.wait()
-    for c in range(EARLY, PACK):
-        value = ins[:, columns(c - EARLY, width)]
-        outs[:, columns(c, width)] = placed(c, value, second, hit2, upd1[...])
-    for store in start_rows(outs, out, out_sems):
+    for store in start_rows(outs, out, sems):
         store.wait()
 
 
@@ -411,8 +407,15 @@
 
 
 def down_grad_kernel(m, act_t, *refs):
-    g0, g1, (down_out,) = refs[:m], refs[m : 2 * m], refs[2 * m :]
-    down_out[...] = dot(act_t[...], whole_of([b[...] for b in g0 + g1])).astype(BF16)
+    g0, g1, (down_out, both) = refs[:m], refs[m : 2 * m], refs[2 * m :]
+
+    @pl.when(pl.program_id(0) == 0)
+    def _():
+        both[...] = whole_of([b[...] for b in g0 + g1])
+
+    for c in range(PACK):
+        k = columns(c, both.shape[1])
+        down_out[:, k] = dot(act_t[...], both[:, k]).astype(BF16)
 
 
 def input_grad_kernel(m, x_t, *refs):
@@ -429,10 +432,10 @@
     up_out[...] = dot(x_t[...], both[:, hidden:]).astype(BF16)
 
 
-def chunked_call(kernel, ins, outs, scratch=()):
+def chunked_call(kernel, ins, outs, scratch=(), steps=PACK):
     return pl.pallas_call(
         kernel,
-        grid=(PACK,),
+        grid=(steps,),
         out_shape=[jax.ShapeDtypeStruct(s, BF16) for s, _, _ in outs],
         in_specs=[pl.BlockSpec(block, index) for _, block, index in ins],
         out_specs=[pl.BlockSpec(block, index) for _, block, index in outs],
@@ -465,13 +468,16 @@
 
 
 def down_grads(act_t, g_grad0, kept, width, hidden):
+    m = len(kept)
     rows = kept[0].shape[0]
-    step = width // PACK
-    ins = [(act_t, act_t.shape, constant(0))]
-    ins += [(a, (rows, step), chunk_at(0)) for a in g_grad0]
-    ins += [(a, (rows, step), chunk_at(2 * PACK)) for a in kept]
-    outs = [((hidden, width), (hidden, step), chunk_at(0))]
-    return chunked_call(functools.partial(down_grad_kernel, len(kept)), ins, outs)
+    block = max(hidden // 4, 16)
+    ins = [(act_t, (block, act_t.shape[1]), lambda c: (c, 0))]
+    ins += [(a, (rows, width), constant(0)) for a in g_grad0]
+    ins += [(a, (rows, width), constant(2)) for a in kept]
+    outs = [((hidden, width), (block, width), lambda c: (c, 0))]
+    scratch = [pltpu.VMEM((2 * m * rows, width), BF16)]
+    kernel = functools.partial(down_grad_kernel, m)
+    return chunked_call(kernel, ins, outs, scratch, hidden // block)
 
 
 def input_grads(x_t, g_grad0, kept, width, hidden):
@@ -567,8 +573,8 @@
     enter1, cot1_all = call(
         enter1_kernel,
         [((2 * PACKED, step), BF16), (tokens.shape, BF16)],
-        [h1, scaled1, cot1_all, early, prev_routes, prev2_routes],
-        any_args=(2, 3, 4, 5),
+        [h1, scaled1, cot1_all, early, prev_routes, prev2_routes, part0],
+        any_args=(2, 3, 4, 5, 6),
         any_outs=(1,),
         aliases={2: 1},
     )
@@ -631,18 +637,14 @@
     x_t, act_t = turned(kept_all, width, hidden)
     (down_out,) = down_grads(act_t, g_grad0_all, kept_all, width, hidden)
     gate_out, up_out = input_grads(x_t, g_grad0_all, kept_all, width, hidden)
-    blocks16 = pltpu.SemaphoreType.DMA((tokens.shape[0] // 16,))
     (state,) = call(
         finish_state_kernel,
         [(tokens.shape, BF16)],
         [early, rest, part0, prev2_routes, last1, prev_routes],
-        any_args=(1,),
         any_outs=(0,),
         scratch=[
-            pltpu.VMEM(rest.shape, BF16),
             pltpu.VMEM(tokens.shape, BF16),
-            blocks16,
-            blocks16,
+            pltpu.SemaphoreType.DMA((tokens.shape[0] // 16,)),
         ],
     )
     return (grad, state, gate_out[None], up_out[None], down_out[None])

time: 139 us -> 137 us (0.986)
  Pallas kernels: 47.2 us -> 43.6 us
  starting transfers between devices: 38.1 us -> 40.4 us
    ppermute x34, starting transfers between devices: 38.1 us -> 40.4 us  [shifted(): lax.ppermute(block, axis, [((i - distance) % size, i) for i in range(size)])]
    pallas_call x3, Pallas kernels: 15 us -> 13.1 us  [chunked_call(): pl.pallas_call(kernel, grid=(steps,), out_shape=[jax.ShapeDtypeStruct(s,...]
    pallas_call x15, Pallas kernels: 32.2 us -> 30.5 us  [call(): pl.pallas_call(kernel, out_shape=outs, in_specs=[anywhere if i in any_arg...]
  transfers between devices with their start and end apart: 34 -> 34, of which waited for: 21 -> 21; matrix products, arithmetic and copies ran while one was open for 0% -> 0% of each run, Pallas kernels for 31% -> 30%
where the time goes in v10:
time: 137 us
  waiting for transfers between devices  51.9 us (38%)
  Pallas kernels  43.6 us (32%)
  starting transfers between devices  40.4 us (29%)
    ppermute x34, waiting for transfers between devices, shifted(): lax.ppermute(block, axis, [((i - distance) % size, i) for i in range(size)])  51.9 us
    ppermute x34, starting transfers between devices, shifted(): lax.ppermute(block, axis, [((i - distance) % size, i) for i in range(size)])  40.4 us
    pallas_call x15, Pallas kernels, call(): pl.pallas_call(kernel, out_shape=outs, in_specs=[anywhere if i in any_arg...  30.5 us
    pallas_call x3, Pallas kernels, chunked_call(): pl.pallas_call(kernel, grid=(steps,), out_shape=[jax.ShapeDtypeStruct(s,...  13.1 us
  transfers between devices with their start and end apart: 34, of which 21 were waited for; matrix products, arithmetic and copies ran while one was open for 0% of the time, Pallas kernels for 30%

profile of v10, /device:TPU:0, one launch (start us, length us, event | category | flops | bytes accessed | tf_op | source)
XLA Modules:
  0.0 137.0 jit_solution(5752087658362689440)
XLA Ops:
  0.6 5.1 %collective-permute-start.8 = (bf16[128,5120]{1,0:T(8,128)(2,1)}, bf16[128,5120]{1,0:T(8,128)(2,1)S(1)}, u32[]{:S(2)}, u32[]{:S(2)}) collective-permute-start(bf16[128,5120]{1,0:T(8,128)(2,1)} %param.8), channel_id=1, source_target_pairs={{8,0},{16,8},{24,16},{0,24},{9,1},{17,9},{25,17},{1,25},{10,2},{18... | collective-permute-start | bytes 3932168 | tf_op jit(solution)/shard_map/ppermute | solution.py:25
  5.7 2.9 %shard_map.110 = (bf16[80,640]{1,0:T(8,128)(2,1)S(1)}, bf16[80,640]{1,0:T(8,128)(2,1)S(1)}, bf16[128,640]{1,0:T(8,128)(2,1)}) custom-call(bf16[128,5120]{1,0:T(8,128)(2,1)} %tokens.3, s32[2,4,128]{2,1,0:T(4,128)} %bitcast.8), custom_call_target="tpu_custom_call" | custom-call | bytes 1024 | tf_op jit(solution)/shard_map/pallas_call | solution.py:38
  8.6 0.1 collective-permute-start
  8.7 1.6 %collective-permute-start.1 = (bf16[80,640]{1,0:T(8,128)(2,1)S(1)}, bf16[80,640]{1,0:T(8,128)(2,1)S(1)}, u32[]{:S(2)}, u32[]{:S(2)}) collective-permute-start(bf16[80,640]{1,0:T(8,128)(2,1)S(1)} %get-tuple-element.46.refs_0_), channel_id=1, source_target_pairs={{4,0},{6,2},{0,4},{2,6},{5,1},{7,3},{1,5},{3,7},{12,8},{14,10},{8,... | collective-permute-start | bytes 307208 | tf_op jit(solution)/shard_map/ppermute | solution.py:25
  10.2 1.4 %collective-permute-start.2 = (bf16[80,640]{1,0:T(8,128)(2,1)S(1)}, bf16[80,640]{1,0:T(8,128)(2,1)S(1)}, u32[]{:S(2)}, u32[]{:S(2)}) collective-permute-start(bf16[80,640]{1,0:T(8,128)(2,1)S(1)} %get-tuple-element.46.refs_0_), channel_id=1, source_target_pairs={{2,0},{4,2},{6,4},{0,6},{3,1},{5,3},{7,5},{1,7},{10,8},{12,10},{14... | collective-permute-start | bytes 307208 | tf_op jit(solution)/shard_map/ppermute | solution.py:25
  11.6 1.6 %collective-permute-done.refs_1_ = bf16[80,640]{1,0:T(8,128)(2,1)S(1)} collective-permute-done((bf16[80,640]{1,0:T(8,128)(2,1)S(1)}, bf16[80,640]{1,0:T(8,128)(2,1)S(1)}, u32[]{:S(2)}, u32[]{:S(2)}) %collective-permute-start) | collective-permute-done | bytes 102432 | tf_op jit(solution)/shard_map/ppermute | solution.py:25
  13.2 1.2 collective-permute-done.1.refs_2_
  14.4 0.6 collective-permute-done.2.refs_3_
  15.1 6.5 %shard_map.111 = (bf16[40,5120]{1,0:T(8,128)(2,1)S(1)}, f32[40,512]{1,0:T(8,128)S(1)}, f32[40,512]{1,0:T(8,128)S(1)}, bf16[40,512]{1,0:T(8,128)(2,1)S(1)}, bf16[...) custom-call(bf16[80,640]{1,0:T(8,128)(2,1)S(1)} %get-tuple-element.4, ...), custom_call_target="tpu_custom_call" | custom-call | bytes 1024 | tf_op jit(solution)/shard_map/pallas_call | solution.py:38
  21.6 2.3 %collective-permute-start.3 = (bf16[80,640]{1,0:T(8,128)(2,1)S(1)}, bf16[80,640]{1,0:T(8,128)(2,1)S(1)}, u32[]{:S(2)}, u32[]{:S(2)}) collective-permute-start(bf16[80,640]{1,0:T(8,128)(2,1)S(1)} %get-tuple-element.48), channel_id=1, source_target_pairs={{2,0},{4,2},{6,4},{0,6},{3,1},{5,3},{7,5},{1,7},{10,8},{12,10},{14... | collective-permute-start | bytes 307208 | tf_op jit(solution)/shard_map/ppermute | solution.py:25
  23.9 0.5 collective-permute-start.4
  24.4 0.5 collective-permute-start.6
  24.9 9.2 %collective-permute-done.6.refs_8_.next_routes = s32[1,4,128]{2,1,0:T(4,128)S(1)} collective-permute-done((s32[1,4,128]{2,1,0:T(4,128)S(1)}, s32[1,4,128]{2,1,0:T(4,128)S(1)}, u32[]{:S(2)}, u32[]{:S(2)}) %collective-permute-start.6) | collective-permute-done | bytes 2080 | tf_op jit(solution)/shard_map/ppermute | solution.py:25
  34.1 1.4 %collective-permute-start.9 = (bf16[128,640]{1,0:T(8,128)(2,1)S(1)}, bf16[128,640]{1,0:T(8,128)(2,1)S(1)}, u32[]{:S(2)}, u32[]{:S(2)}) collective-permute-start(bf16[128,640]{1,0:T(8,128)(2,1)S(1)} %copy-done.3), channel_id=1, source_target_pairs={{16,0},{24,8},{0,16},{8,24},{17,1},{25,9},{1,17},{9,25},{18,2},{26... | collective-permute-start | bytes 491528 | tf_op jit(solution)/shard_map/ppermute | solution.py:25
  35.5 0.7 shard_map.112
  36.2 3.4 %collective-permute-start.7 = (bf16[80,640]{1,0:T(8,128)(2,1)S(1)}, bf16[80,640]{1,0:T(8,128)(2,1)S(1)}, u32[]{:S(2)}, u32[]{:S(2)}) collective-permute-start(bf16[80,640]{1,0:T(8,128)(2,1)S(1)} %get-tuple-element.52), channel_id=1, source_target_pairs={{24,0},{0,8},{8,16},{16,24},{25,1},{1,9},{9,17},{17,25},{26,2},{2,... | collective-permute-start | bytes 307208 | tf_op jit(solution)/shard_map/ppermute | solution.py:25
  39.7 1.0 collective-permute-start.10
  40.7 2.0 %collective-permute-start.11 = (s32[1,4,128]{2,1,0:T(4,128)S(1)}, s32[1,4,128]{2,1,0:T(4,128)S(1)}, u32[]{:S(2)}, u32[]{:S(2)}) collective-permute-start(s32[1,4,128]{2,1,0:T(4,128)S(1)} %get-tuple-element.87), channel_id=1, source_target_pairs={{16,0},{24,8},{0,16},{8,24},{17,1},{25,9},{1,17},{9,25},{18,2},{26... | collective-permute-start | bytes 6152 | tf_op jit(solution)/shard_map/ppermute | solution.py:25
  42.7 0.5 shard_map.113
  43.2 1.9 %collective-permute-done.10.refs_2_.prev_routes = s32[1,4,128]{2,1,0:T(4,128)S(1)} collective-permute-done((s32[1,4,128]{2,1,0:T(4,128)S(1)}, s32[1,4,128]{2,1,0:T(4,128)S(1)}, u32[]{:S(2)}, u32[]{:S(2)}) %collective-permute-start.10) | collective-permute-done | bytes 2080 | tf_op jit(solution)/shard_map/ppermute | solution.py:25
  45.2 1.6 %collective-permute-done.11.refs_3_.prev2_routes = s32[1,4,128]{2,1,0:T(4,128)S(1)} collective-permute-done((s32[1,4,128]{2,1,0:T(4,128)S(1)}, s32[1,4,128]{2,1,0:T(4,128)S(1)}, u32[]{:S(2)}, u32[]{:S(2)}) %collective-permute-start.11) | collective-permute-done | bytes 2080 | tf_op jit(solution)/shard_map/ppermute | solution.py:25
  46.8 0.3 shard_map.114
  47.1 2.6 %collective-permute-start.20 = (bf16[128,5120]{1,0:T(8,128)(2,1)S(1)}, bf16[128,5120]{1,0:T(8,128)(2,1)S(1)}, u32[]{:S(2)}, u32[]{:S(2)}) collective-permute-start(bf16[128,5120]{1,0:T(8,128)(2,1)S(1)} %get-tuple-element.67), channel_id=1, source_target_pairs={{8,0},{16,8},{24,16},{0,24},{9,1},{17,9},{25,17},{1,25},{10,2},{18... | collective-permute-start | bytes 3932168 | tf_op jit(solution)/shard_map/ppermute | solution.py:25
  49.7 1.5 %collective-permute-start.14 = (bf16[160,640]{1,0:T(8,128)(2,1)S(1)}, bf16[160,640]{1,0:T(8,128)(2,1)S(1)}, u32[]{:S(2)}, u32[]{:S(2)}) collective-permute-start(bf16[160,640]{1,0:T(8,128)(2,1)S(1)} %get-tuple-element.56.refs_0_), channel_id=1, source_target_pairs={{4,0},{6,2},{0,4},{2,6},{5,1},{7,3},{1,5},{3,7},{12,8},{14,10},{8,... | collective-permute-start | bytes 614408 | tf_op jit(solution)/shard_map/ppermute | solution.py:25
  51.2 1.4 %collective-permute-start.15 = (bf16[160,640]{1,0:T(8,128)(2,1)S(1)}, bf16[160,640]{1,0:T(8,128)(2,1)S(1)}, u32[]{:S(2)}, u32[]{:S(2)}) collective-permute-start(bf16[160,640]{1,0:T(8,128)(2,1)S(1)} %get-tuple-element.56.refs_0_), channel_id=1, source_target_pairs={{2,0},{4,2},{6,4},{0,6},{3,1},{5,3},{7,5},{1,7},{10,8},{12,10},{14... | collective-permute-start | bytes 614408 | tf_op jit(solution)/shard_map/ppermute | solution.py:25
  52.7 3.8 %collective-permute-done.13.refs_1_ = bf16[160,640]{1,0:T(8,128)(2,1)S(1)} collective-permute-done((bf16[160,640]{1,0:T(8,128)(2,1)S(1)}, bf16[160,640]{1,0:T(8,128)(2,1)S(1)}, u32[]{:S(2)}, u32[]{:S(2)}) %collective-permute-start.13) | collective-permute-done | bytes 204832 | tf_op jit(solution)/shard_map/ppermute | solution.py:25
  56.5 1.1 collective-permute-done.14.refs_2_
  57.6 2.9 %collective-permute-done.15.refs_3_ = bf16[160,640]{1,0:T(8,128)(2,1)S(1)} collective-permute-done((bf16[160,640]{1,0:T(8,128)(2,1)S(1)}, bf16[160,640]{1,0:T(8,128)(2,1)S(1)}, u32[]{:S(2)}, u32[]{:S(2)}) %collective-permute-start.15) | collective-permute-done | bytes 204832 | tf_op jit(solution)/shard_map/ppermute | solution.py:25
  60.5 6.8 %shard_map.115 = (bf16[40,17408]{1,0:T(8,128)(2,1)S(1)}, bf16[80,640]{1,0:T(8,128)(2,1)S(1)}, bf16[80,640]{1,0:T(8,128)(2,1)S(1)}, bf16[80,640]{1,0:T(8,128)(2,1)S(1)}, bf16[80,640]{1,0:T(8,128)(2,1)S(1)}) custom-call(bf16[160,640]{1,0:T(8,128)(2,1)S(1)} %get-tuple-element.56.refs_0_, bf16[160,640]{1,0:T(8,128)(2,1)S(1)} %collective-permute-done.13.refs_1_, ...), custom_call_target="tpu_custom_call" | custom-call | bytes 1024 | tf_op jit(solution)/shard_map/pallas_call | solution.py:38
  67.3 1.6 %collective-permute-start.32 = (bf16[40,17408]{1,0:T(8,128)(2,1)S(1)}, bf16[40,17408]{1,0:T(8,128)(2,1)S(1)}, u32[]{:S(2)}, u32[]{:S(2)}) collective-permute-start(bf16[40,17408]{1,0:T(8,128)(2,1)S(1)} %get-tuple-element.77.act.refs_0_.refs_2_.refs_4_.refs_6_), channel_id=1, source_target_pairs={{1,0},{0,1},{3,2},{2,3},{5,4},{4,5},{7,6},{6,7},{9,8},{8,9},{11,10... | collective-permute-start | bytes 4177928 | tf_op jit(solution)/shard_map/ppermute | solution.py:25
  68.9 1.9 %collective-permute-start.16 = (bf16[80,640]{1,0:T(8,128)(2,1)S(1)}, bf16[80,640]{1,0:T(8,128)(2,1)S(1)}, u32[]{:S(2)}, u32[]{:S(2)}) collective-permute-start(bf16[80,640]{1,0:T(8,128)(2,1)S(1)} %get-tuple-element.63), channel_id=1, source_target_pairs={{2,0},{4,2},{6,4},{0,6},{3,1},{5,3},{7,5},{1,7},{10,8},{12,10},{14... | collective-permute-start | bytes 307208 | tf_op jit(solution)/shard_map/ppermute | solution.py:25
  70.8 0.5 collective-permute-start.17
  71.3 2.4 %collective-permute-done.16.refs_1_ = bf16[80,640]{1,0:T(8,128)(2,1)S(1)} collective-permute-done((bf16[80,640]{1,0:T(8,128)(2,1)S(1)}, bf16[80,640]{1,0:T(8,128)(2,1)S(1)}, u32[]{:S(2)}, u32[]{:S(2)}) %collective-permute-start.16) | collective-permute-done | bytes 102432 | tf_op jit(solution)/shard_map/ppermute | solution.py:25
  73.7 3.0 %collective-permute-done.17.refs_2_ = bf16[80,640]{1,0:T(8,128)(2,1)S(1)} collective-permute-done((bf16[80,640]{1,0:T(8,128)(2,1)S(1)}, bf16[80,640]{1,0:T(8,128)(2,1)S(1)}, u32[]{:S(2)}, u32[]{:S(2)}) %collective-permute-start.17) | collective-permute-done | bytes 102432 | tf_op jit(solution)/shard_map/ppermute | solution.py:25
  76.7 0.5 shard_map.116
  77.2 0.6 collective-permute-start.19
  77.8 0.7 shard_map.117._
  78.5 3.4 %collective-permute-done.19.___.upd1.refs_7_ = bf16[80,640]{1,0:T(8,128)(2,1)S(1)} collective-permute-done((bf16[80,640]{1,0:T(8,128)(2,1)S(1)}, bf16[80,640]{1,0:T(8,128)(2,1)S(1)}, u32[]{:S(2)}, u32[]{:S(2)}) %collective-permute-start.19) | collective-permute-done | bytes 102432 | tf_op jit(solution)/shard_map/ppermute | solution.py:25
  81.9 0.8 shard_map.119
  82.7 0.1 collective-permute-start.21
  82.8 1.6 %collective-permute-start.22 = (bf16[80,640]{1,0:T(8,128)(2,1)S(1)}, bf16[80,640]{1,0:T(8,128)(2,1)S(1)}, u32[]{:S(2)}, u32[]{:S(2)}) collective-permute-start(bf16[80,640]{1,0:T(8,128)(2,1)S(1)} %get-tuple-element.69.refs_0_), channel_id=1, source_target_pairs={{4,0},{6,2},{0,4},{2,6},{5,1},{7,3},{1,5},{3,7},{12,8},{14,10},{8,... | collective-permute-start | bytes 307208 | tf_op jit(solution)/shard_map/ppermute | solution.py:25
  84.4 1.4 %collective-permute-start.23 = (bf16[80,640]{1,0:T(8,128)(2,1)S(1)}, bf16[80,640]{1,0:T(8,128)(2,1)S(1)}, u32[]{:S(2)}, u32[]{:S(2)}) collective-permute-start(bf16[80,640]{1,0:T(8,128)(2,1)S(1)} %get-tuple-element.69.refs_0_), channel_id=1, source_target_pairs={{2,0},{4,2},{6,4},{0,6},{3,1},{5,3},{7,5},{1,7},{10,8},{12,10},{14... | collective-permute-start | bytes 307208 | tf_op jit(solution)/shard_map/ppermute | solution.py:25
  85.7 1.6 %collective-permute-done.21.refs_1_ = bf16[80,640]{1,0:T(8,128)(2,1)S(1)} collective-permute-done((bf16[80,640]{1,0:T(8,128)(2,1)S(1)}, bf16[80,640]{1,0:T(8,128)(2,1)S(1)}, u32[]{:S(2)}, u32[]{:S(2)}) %collective-permute-start.21) | collective-permute-done | bytes 102432 | tf_op jit(solution)/shard_map/ppermute | solution.py:25
  87.3 1.2 collective-permute-done.22.refs_2_
  88.5 0.6 collective-permute-done.23.refs_3_
  89.2 5.1 %shard_map.120 = (bf16[40,6144]{1,0:T(8,128)(2,1)S(1)}, bf16[80,640]{1,0:T(8,128)(2,1)S(1)}, bf16[80,640]{1,0:T(8,128)(2,1)S(1)}, bf16[80,640]{1,0:T(8,128)(2,1)S(1)}, bf16[80,640]{1,0:T(8,128)(2,1)S(1)}) custom-call(bf16[80,640]{1,0:T(8,128)(2,1)S(1)} %get-tuple-element.69.refs_0_, bf16[80,640]{1,0:T(8,128)(2,1)S(1)} %collective-permute-done.21.refs_1_, ...), custom_call_target="tpu_custom_call" | custom-call | bytes 1024 | tf_op jit(solution)/shard_map/pallas_call | solution.py:38
  94.2 1.1 collective-permute-start.33
  95.4 1.9 %collective-permute-start.24 = (bf16[80,640]{1,0:T(8,128)(2,1)S(1)}, bf16[80,640]{1,0:T(8,128)(2,1)S(1)}, u32[]{:S(2)}, u32[]{:S(2)}) collective-permute-start(bf16[80,640]{1,0:T(8,128)(2,1)S(1)} %get-tuple-element.73), channel_id=1, source_target_pairs={{2,0},{4,2},{6,4},{0,6},{3,1},{5,3},{7,5},{1,7},{10,8},{12,10},{14... | collective-permute-start | bytes 307208 | tf_op jit(solution)/shard_map/ppermute | solution.py:25
  97.3 1.1 shard_map.122
  98.5 1.1 collective-permute-done.24.refs_1_
  99.6 0.5 collective-permute-start.29
  100.1 0.6 collective-permute-done.28.refs_1_
  100.7 1.1 collective-permute-start.30
  101.8 3.5 %collective-permute-done.29.refs_2_ = bf16[80,640]{1,0:T(8,128)(2,1)S(1)} collective-permute-done((bf16[80,640]{1,0:T(8,128)(2,1)S(1)}, bf16[80,640]{1,0:T(8,128)(2,1)S(1)}, u32[]{:S(2)}, u32[]{:S(2)}) %collective-permute-start.29) | collective-permute-done | bytes 102432 | tf_op jit(solution)/shard_map/ppermute | solution.py:25
  105.3 1.1 collective-permute-done.30.refs_3_
  106.4 0.2 shard_map.123
  106.7 4.3 %collective-permute-done.25.refs_2_ = bf16[80,640]{1,0:T(8,128)(2,1)S(1)} collective-permute-done((bf16[80,640]{1,0:T(8,128)(2,1)S(1)}, bf16[80,640]{1,0:T(8,128)(2,1)S(1)}, u32[]{:S(2)}, u32[]{:S(2)}) %collective-permute-start.25) | collective-permute-done | bytes 102432 | tf_op jit(solution)/shard_map/ppermute | solution.py:25
  111.0 3.3 %collective-permute-start.31 = (bf16[80,640]{1,0:T(8,128)(2,1)S(1)}, bf16[80,640]{1,0:T(8,128)(2,1)S(1)}, u32[]{:S(2)}, u32[]{:S(2)}) collective-permute-start(bf16[80,640]{1,0:T(8,128)(2,1)S(1)} %shard_map.123), channel_id=1, source_target_pairs={{24,0},{0,8},{8,16},{16,24},{25,1},{1,9},{9,17},{17,25},{26,2},{2,... | collective-permute-start | bytes 307208 | tf_op jit(solution)/shard_map/ppermute | solution.py:25
  114.3 2.4 %shard_map.121 = bf16[128,5120]{1,0:T(8,128)(2,1)} custom-call(bf16[80,640]{1,0:T(8,128)(2,1)S(1)} %get-tuple-element.72.refs_0_, bf16[80,640]{1,0:T(8,128)(2,1)S(1)} %collective-permute-done.24.refs_1_, bf16[80,640]{1,0:T(8,128)(2,1)S(1)} %collective-permute-done.25.refs_2_, bf16[80,640]{1,0:T(8,128)(2,1)S(1)} %collective-permute-done.26.refs_3_, ...), custom_call_target="tpu_custom_call" | custom-call | bytes 1024 | tf_op jit(solution)/shard_map/pallas_call | solution.py:38
  116.7 2.9 %shard_map.125 = (bf16[5120,160]{1,0:T(8,128)(2,1)S(1)}, bf16[512,160]{1,0:T(8,128)(2,1)S(1)}) custom-call(bf16[40,17408]{1,0:T(8,128)(2,1)S(1)} %get-tuple-element.77.act.refs_0_.refs_2_.refs_4_.refs_6_, bf16[40,17408]{1,0:T(8,128)(2,1)S(1)} %collective-permute-done.32.refs_1_.refs_3_.refs_5_.refs_7_, ...), custom_call_target="tpu_custom_call" | custom-call | bytes 1024 | tf_op jit(solution)/shard_map/pallas_call | solution.py:436
  119.6 6.2 %shard_map.126 = (bf16[5120,512]{1,0:T(8,128)(2,1)}, bf16[5120,512]{1,0:T(8,128)(2,1)}) custom-call(bf16[5120,160]{1,0:T(8,128)(2,1)S(1)} %get-tuple-element.83.x_t, bf16[40,6144]{1,0:T(8,128)(2,1)S(1)} %get-tuple-element.78._.refs_0_.refs_2_, bf16[40,6144]{1,0:T(8,128)(2,1)S(1)} %collective-permute-done.33.refs_1_.refs_3_, ...), custom_call_target="tpu_custom_call" | custom-call | bytes 1024 | tf_op jit(solution)/shard_map/pallas_call | solution.py:436
  125.8 4.1 %shard_map.127 = bf16[512,5120]{1,0:T(8,128)(2,1)} custom-call(bf16[512,160]{1,0:T(8,128)(2,1)S(1)} %get-tuple-element.86.act_t, bf16[40,6144]{1,0:T(8,128)(2,1)S(1)} %get-tuple-element.78._.refs_0_.refs_2_, bf16[40,6144]{1,0:T(8,128)(2,1)S(1)} %collective-permute-done.33.refs_1_.refs_3_, ...), custom_call_target="tpu_custom_call" | custom-call | bytes 1024 | tf_op jit(solution)/shard_map/pallas_call | solution.py:436
  129.9 5.0 %collective-permute-done.27.rest = bf16[128,4480]{1,0:T(8,128)(2,1)S(1)} collective-permute-done((bf16[128,4480]{1,0:T(8,128)(2,1)S(1)}, bf16[128,4480]{1,0:T(8,128)(2,1)S(1)}, u32[]{:S(2)}, u32[]{:S(2)}) %collective-permute-start.27) | collective-permute-done | bytes 1146912 | tf_op jit(solution)/shard_map/ppermute | solution.py:25
  134.9 1.9 %shard_map.124 = bf16[128,5120]{1,0:T(8,128)(2,1)} custom-call(bf16[128,640]{1,0:T(8,128)(2,1)S(1)} %collective-permute-done.9.refs_1_.early, bf16[128,4480]{1,0:T(8,128)(2,1)S(1)} %collective-permute-done.27.rest, bf16[16,640]{1,0:T(8,128)(2,1)S(1)} %collective-permute-done.12.refs_4_.part, s32[1,4,128]{2,1,0:T(4,128)S(1)} %collective-permute-done.11.refs_3_.prev2_routes, ...), custom_call_target="tpu_custom_call" | custom-call | bytes 1024 | tf_op jit(solution)/shard_map/pallas_call | solution.py:38
  (31 shorter events, 0.1 us)
Async XLA Ops:
  0.6 40.1 %collective-permute-start.8 = (bf16[128,5120]{1,0:T(8,128)(2,1)}, bf16[128,5120]{1,0:T(8,128)(2,1)S(1)}, u32[]{:S(2)}, u32[]{:S(2)}) collective-permute-start(bf16[128,5120]{1,0:T(8,128)(2,1)} %param.8), channel_id=1, source_target_pairs={{8,0},{16,8},{24,16},{0,24},{9,1},{17,9},{25,17},{1,25},{10,2},{18... | collective-permute-start | bytes 3932168 | tf_op jit(solution)/shard_map/ppermute | solution.py:25
  8.6 4.6 %collective-permute-start = (bf16[80,640]{1,0:T(8,128)(2,1)S(1)}, bf16[80,640]{1,0:T(8,128)(2,1)S(1)}, u32[]{:S(2)}, u32[]{:S(2)}) collective-permute-start(bf16[80,640]{1,0:T(8,128)(2,1)S(1)} %get-tuple-element.46.refs_0_), channel_id=1, source_target_pairs={{6,0},{0,2},{2,4},{4,6},{7,1},{1,3},{3,5},{5,7},{14,8},{8,10},{10,... | collective-permute-start | bytes 307208 | tf_op jit(solution)/shard_map/ppermute | solution.py:25
  8.7 5.8 %collective-permute-start.1 = (bf16[80,640]{1,0:T(8,128)(2,1)S(1)}, bf16[80,640]{1,0:T(8,128)(2,1)S(1)}, u32[]{:S(2)}, u32[]{:S(2)}) collective-permute-start(bf16[80,640]{1,0:T(8,128)(2,1)S(1)} %get-tuple-element.46.refs_0_), channel_id=1, source_target_pairs={{4,0},{6,2},{0,4},{2,6},{5,1},{7,3},{1,5},{3,7},{12,8},{14,10},{8,... | collective-permute-start | bytes 307208 | tf_op jit(solution)/shard_map/ppermute | solution.py:25
  10.2 4.8 %collective-permute-start.2 = (bf16[80,640]{1,0:T(8,128)(2,1)S(1)}, bf16[80,640]{1,0:T(8,128)(2,1)S(1)}, u32[]{:S(2)}, u32[]{:S(2)}) collective-permute-start(bf16[80,640]{1,0:T(8,128)(2,1)S(1)} %get-tuple-element.46.refs_0_), channel_id=1, source_target_pairs={{2,0},{4,2},{6,4},{0,6},{3,1},{5,3},{7,5},{1,7},{10,8},{12,10},{14... | collective-permute-start | bytes 307208 | tf_op jit(solution)/shard_map/ppermute | solution.py:25
  15.1 9.3 %copy-start.1 = (s32[2,128,4]{1,2,0:T(4,128)S(1)}, s32[2,128,4]{1,2,0:T(4,128)}, u32[]{:S(2)}) copy-start(s32[2,128,4]{1,2,0:T(4,128)} %param.12) | copy-start | bytes 12292
  15.1 19.0 %copy-start.3 = (bf16[128,640]{1,0:T(8,128)(2,1)S(1)}, bf16[128,640]{1,0:T(8,128)(2,1)}, u32[]{:S(2)}) copy-start(bf16[128,640]{1,0:T(8,128)(2,1)} %get-tuple-element.54) | copy-start | bytes 491524
  15.1 20.4 %copy-start = (bf16[128,5120]{1,0:T(8,128)(2,1)S(1)}, bf16[128,5120]{1,0:T(8,128)(2,1)}, u32[]{:S(2)}) copy-start(bf16[128,5120]{1,0:T(8,128)(2,1)} %tokens.3) | copy-start | bytes 3932164
  15.1 20.5 %copy-start.2 = (f32[2,128,4]{1,2,0:T(4,128)S(1)}, f32[2,128,4]{1,2,0:T(4,128)}, u32[]{:S(2)}) copy-start(f32[2,128,4]{1,2,0:T(4,128)} %param.13) | copy-start | bytes 12292
  21.6 13.9 %collective-permute-start.3 = (bf16[80,640]{1,0:T(8,128)(2,1)S(1)}, bf16[80,640]{1,0:T(8,128)(2,1)S(1)}, u32[]{:S(2)}, u32[]{:S(2)}) collective-permute-start(bf16[80,640]{1,0:T(8,128)(2,1)S(1)} %get-tuple-element.48), channel_id=1, source_target_pairs={{2,0},{4,2},{6,4},{0,6},{3,1},{5,3},{7,5},{1,7},{10,8},{12,10},{14... | collective-permute-start | bytes 307208 | tf_op jit(solution)/shard_map/ppermute | solution.py:25
  23.9 11.6 %collective-permute-start.4 = (bf16[80,640]{1,0:T(8,128)(2,1)S(1)}, bf16[80,640]{1,0:T(8,128)(2,1)S(1)}, u32[]{:S(2)}, u32[]{:S(2)}) collective-permute-start(bf16[80,640]{1,0:T(8,128)(2,1)S(1)} %get-tuple-element.49), channel_id=1, source_target_pairs={{4,0},{6,2},{0,4},{2,6},{5,1},{7,3},{1,5},{3,7},{12,8},{14,10},{8,... | collective-permute-start | bytes 307208 | tf_op jit(solution)/shard_map/ppermute | solution.py:25
  24.4 11.1 %collective-permute-start.5 = (bf16[80,640]{1,0:T(8,128)(2,1)S(1)}, bf16[80,640]{1,0:T(8,128)(2,1)S(1)}, u32[]{:S(2)}, u32[]{:S(2)}) collective-permute-start(bf16[80,640]{1,0:T(8,128)(2,1)S(1)} %get-tuple-element.50), channel_id=1, source_target_pairs={{6,0},{0,2},{2,4},{4,6},{7,1},{1,3},{3,5},{5,7},{14,8},{8,10},{10,... | collective-permute-start | bytes 307208 | tf_op jit(solution)/shard_map/ppermute | solution.py:25
  24.4 9.7 %collective-permute-start.6 = (s32[1,4,128]{2,1,0:T(4,128)S(1)}, s32[1,4,128]{2,1,0:T(4,128)S(1)}, u32[]{:S(2)}, u32[]{:S(2)}) collective-permute-start(s32[1,4,128]{2,1,0:T(4,128)S(1)} %get-tuple-element.88), channel_id=1, source_target_pairs={{8,0},{16,8},{24,16},{0,24},{9,1},{17,9},{25,17},{1,25},{10,2},{18... | collective-permute-start | bytes 6152 | tf_op jit(solution)/shard_map/ppermute | solution.py:25
  34.1 12.6 %collective-permute-start.9 = (bf16[128,640]{1,0:T(8,128)(2,1)S(1)}, bf16[128,640]{1,0:T(8,128)(2,1)S(1)}, u32[]{:S(2)}, u32[]{:S(2)}) collective-permute-start(bf16[128,640]{1,0:T(8,128)(2,1)S(1)} %copy-done.3), channel_id=1, source_target_pairs={{16,0},{24,8},{0,16},{8,24},{17,1},{25,9},{1,17},{9,25},{18,2},{26... | collective-permute-start | bytes 491528 | tf_op jit(solution)/shard_map/ppermute | solution.py:25
  36.2 10.5 %collective-permute-start.7 = (bf16[80,640]{1,0:T(8,128)(2,1)S(1)}, bf16[80,640]{1,0:T(8,128)(2,1)S(1)}, u32[]{:S(2)}, u32[]{:S(2)}) collective-permute-start(bf16[80,640]{1,0:T(8,128)(2,1)S(1)} %get-tuple-element.52), channel_id=1, source_target_pairs={{24,0},{0,8},{8,16},{16,24},{25,1},{1,9},{9,17},{17,25},{26,2},{2,... | collective-permute-start | bytes 307208 | tf_op jit(solution)/shard_map/ppermute | solution.py:25
  39.7 7.1 %collective-permute-start.12 = (bf16[16,640]{1,0:T(8,128)(2,1)S(1)}, bf16[16,640]{1,0:T(8,128)(2,1)S(1)}, u32[]{:S(2)}, u32[]{:S(2)}) collective-permute-start(bf16[16,640]{1,0:T(8,128)(2,1)S(1)} %get-tuple-element.55), channel_id=1, source_target_pairs={{16,0},{24,8},{0,16},{8,24},{17,1},{25,9},{1,17},{9,25},{18,2},{26... | collective-permute-start | bytes 61448 | tf_op jit(solution)/shard_map/ppermute | solution.py:25
  39.7 5.5 %collective-permute-start.10 = (s32[1,4,128]{2,1,0:T(4,128)S(1)}, s32[1,4,128]{2,1,0:T(4,128)S(1)}, u32[]{:S(2)}, u32[]{:S(2)}) collective-permute-start(s32[1,4,128]{2,1,0:T(4,128)S(1)} %get-tuple-element.88), channel_id=1, source_target_pairs={{24,0},{0,8},{8,16},{16,24},{25,1},{1,9},{9,17},{17,25},{26,2},{2,... | collective-permute-start | bytes 6152 | tf_op jit(solution)/shard_map/ppermute | solution.py:25
  40.7 6.1 %collective-permute-start.11 = (s32[1,4,128]{2,1,0:T(4,128)S(1)}, s32[1,4,128]{2,1,0:T(4,128)S(1)}, u32[]{:S(2)}, u32[]{:S(2)}) collective-permute-start(s32[1,4,128]{2,1,0:T(4,128)S(1)} %get-tuple-element.87), channel_id=1, source_target_pairs={{16,0},{24,8},{0,16},{8,24},{17,1},{25,9},{1,17},{9,25},{18,2},{26... | collective-permute-start | bytes 6152 | tf_op jit(solution)/shard_map/ppermute | solution.py:25
  47.1 34.8 %collective-permute-start.20 = (bf16[128,5120]{1,0:T(8,128)(2,1)S(1)}, bf16[128,5120]{1,0:T(8,128)(2,1)S(1)}, u32[]{:S(2)}, u32[]{:S(2)}) collective-permute-start(bf16[128,5120]{1,0:T(8,128)(2,1)S(1)} %get-tuple-element.67), channel_id=1, source_target_pairs={{8,0},{16,8},{24,16},{0,24},{9,1},{17,9},{25,17},{1,25},{10,2},{18... | collective-permute-start | bytes 3932168 | tf_op jit(solution)/shard_map/ppermute | solution.py:25
  49.7 6.8 %collective-permute-start.13 = (bf16[160,640]{1,0:T(8,128)(2,1)S(1)}, bf16[160,640]{1,0:T(8,128)(2,1)S(1)}, u32[]{:S(2)}, u32[]{:S(2)}) collective-permute-start(bf16[160,640]{1,0:T(8,128)(2,1)S(1)} %get-tuple-element.56.refs_0_), channel_id=1, source_target_pairs={{6,0},{0,2},{2,4},{4,6},{7,1},{1,3},{3,5},{5,7},{14,8},{8,10},{10,... | collective-permute-start | bytes 614408 | tf_op jit(solution)/shard_map/ppermute | solution.py:25
  49.7 7.9 %collective-permute-start.14 = (bf16[160,640]{1,0:T(8,128)(2,1)S(1)}, bf16[160,640]{1,0:T(8,128)(2,1)S(1)}, u32[]{:S(2)}, u32[]{:S(2)}) collective-permute-start(bf16[160,640]{1,0:T(8,128)(2,1)S(1)} %get-tuple-element.56.refs_0_), channel_id=1, source_target_pairs={{4,0},{6,2},{0,4},{2,6},{5,1},{7,3},{1,5},{3,7},{12,8},{14,10},{8,... | collective-permute-start | bytes 614408 | tf_op jit(solution)/shard_map/ppermute | solution.py:25
  51.2 9.3 %collective-permute-start.15 = (bf16[160,640]{1,0:T(8,128)(2,1)S(1)}, bf16[160,640]{1,0:T(8,128)(2,1)S(1)}, u32[]{:S(2)}, u32[]{:S(2)}) collective-permute-start(bf16[160,640]{1,0:T(8,128)(2,1)S(1)} %get-tuple-element.56.refs_0_), channel_id=1, source_target_pairs={{2,0},{4,2},{6,4},{0,6},{3,1},{5,3},{7,5},{1,7},{10,8},{12,10},{14... | collective-permute-start | bytes 614408 | tf_op jit(solution)/shard_map/ppermute | solution.py:25
  67.3 49.4 %collective-permute-start.32 = (bf16[40,17408]{1,0:T(8,128)(2,1)S(1)}, bf16[40,17408]{1,0:T(8,128)(2,1)S(1)}, u32[]{:S(2)}, u32[]{:S(2)}) collective-permute-start(bf16[40,17408]{1,0:T(8,128)(2,1)S(1)} %get-tuple-element.77.act.refs_0_.refs_2_.refs_4_.refs_6_), channel_id=1, source_target_pairs={{1,0},{0,1},{3,2},{2,3},{5,4},{4,5},{7,6},{6,7},{9,8},{8,9},{11,10... | collective-permute-start | bytes 4177928 | tf_op jit(solution)/shard_map/ppermute | solution.py:25
  68.9 4.8 %collective-permute-start.16 = (bf16[80,640]{1,0:T(8,128)(2,1)S(1)}, bf16[80,640]{1,0:T(8,128)(2,1)S(1)}, u32[]{:S(2)}, u32[]{:S(2)}) collective-permute-start(bf16[80,640]{1,0:T(8,128)(2,1)S(1)} %get-tuple-element.63), channel_id=1, source_target_pairs={{2,0},{4,2},{6,4},{0,6},{3,1},{5,3},{7,5},{1,7},{10,8},{12,10},{14... | collective-permute-start | bytes 307208 | tf_op jit(solution)/shard_map/ppermute | solution.py:25
  70.8 5.9 %collective-permute-start.17 = (bf16[80,640]{1,0:T(8,128)(2,1)S(1)}, bf16[80,640]{1,0:T(8,128)(2,1)S(1)}, u32[]{:S(2)}, u32[]{:S(2)}) collective-permute-start(bf16[80,640]{1,0:T(8,128)(2,1)S(1)} %get-tuple-element.64), channel_id=1, source_target_pairs={{4,0},{6,2},{0,4},{2,6},{5,1},{7,3},{1,5},{3,7},{12,8},{14,10},{8,... | collective-permute-start | bytes 307208 | tf_op jit(solution)/shard_map/ppermute | solution.py:25
  71.3 5.4 %collective-permute-start.18 = (bf16[80,640]{1,0:T(8,128)(2,1)S(1)}, bf16[80,640]{1,0:T(8,128)(2,1)S(1)}, u32[]{:S(2)}, u32[]{:S(2)}) collective-permute-start(bf16[80,640]{1,0:T(8,128)(2,1)S(1)} %get-tuple-element.65), channel_id=1, source_target_pairs={{6,0},{0,2},{2,4},{4,6},{7,1},{1,3},{3,5},{5,7},{14,8},{8,10},{10,... | collective-permute-start | bytes 307208 | tf_op jit(solution)/shard_map/ppermute | solution.py:25
  77.2 4.7 %collective-permute-start.19 = (bf16[80,640]{1,0:T(8,128)(2,1)S(1)}, bf16[80,640]{1,0:T(8,128)(2,1)S(1)}, u32[]{:S(2)}, u32[]{:S(2)}) collective-permute-start(bf16[80,640]{1,0:T(8,128)(2,1)S(1)} %shard_map.116), channel_id=1, source_target_pairs={{8,0},{16,8},{24,16},{0,24},{9,1},{17,9},{25,17},{1,25},{10,2},{18... | collective-permute-start | bytes 307208 | tf_op jit(solution)/shard_map/ppermute | solution.py:25
  81.9 53.0 %collective-permute-start.27 = (bf16[128,4480]{1,0:T(8,128)(2,1)S(1)}, bf16[128,4480]{1,0:T(8,128)(2,1)S(1)}, u32[]{:S(2)}, u32[]{:S(2)}) collective-permute-start(bf16[128,4480]{1,0:T(8,128)(2,1)S(1)} %shard_map.118._), channel_id=1, source_target_pairs={{16,0},{24,8},{0,16},{8,24},{17,1},{25,9},{1,17},{9,25},{18,2},{26... | collective-permute-start | bytes 3440648 | tf_op jit(solution)/shard_map/ppermute | solution.py:25
  82.7 4.6 %collective-permute-start.21 = (bf16[80,640]{1,0:T(8,128)(2,1)S(1)}, bf16[80,640]{1,0:T(8,128)(2,1)S(1)}, u32[]{:S(2)}, u32[]{:S(2)}) collective-permute-start(bf16[80,640]{1,0:T(8,128)(2,1)S(1)} %get-tuple-element.69.refs_0_), channel_id=1, source_target_pairs={{6,0},{0,2},{2,4},{4,6},{7,1},{1,3},{3,5},{5,7},{14,8},{8,10},{10,... | collective-permute-start | bytes 307208 | tf_op jit(solution)/shard_map/ppermute | solution.py:25
  82.8 5.8 %collective-permute-start.22 = (bf16[80,640]{1,0:T(8,128)(2,1)S(1)}, bf16[80,640]{1,0:T(8,128)(2,1)S(1)}, u32[]{:S(2)}, u32[]{:S(2)}) collective-permute-start(bf16[80,640]{1,0:T(8,128)(2,1)S(1)} %get-tuple-element.69.refs_0_), channel_id=1, source_target_pairs={{4,0},{6,2},{0,4},{2,6},{5,1},{7,3},{1,5},{3,7},{12,8},{14,10},{8,... | collective-permute-start | bytes 307208 | tf_op jit(solution)/shard_map/ppermute | solution.py:25
  84.4 4.8 %collective-permute-start.23 = (bf16[80,640]{1,0:T(8,128)(2,1)S(1)}, bf16[80,640]{1,0:T(8,128)(2,1)S(1)}, u32[]{:S(2)}, u32[]{:S(2)}) collective-permute-start(bf16[80,640]{1,0:T(8,128)(2,1)S(1)} %get-tuple-element.69.refs_0_), channel_id=1, source_target_pairs={{2,0},{4,2},{6,4},{0,6},{3,1},{5,3},{7,5},{1,7},{10,8},{12,10},{14... | collective-permute-start | bytes 307208 | tf_op jit(solution)/shard_map/ppermute | solution.py:25
  94.2 25.4 %collective-permute-start.33 = (bf16[40,6144]{1,0:T(8,128)(2,1)S(1)}, bf16[40,6144]{1,0:T(8,128)(2,1)S(1)}, u32[]{:S(2)}, u32[]{:S(2)}) collective-permute-start(bf16[40,6144]{1,0:T(8,128)(2,1)S(1)} %get-tuple-element.78._.refs_0_.refs_2_), channel_id=1, source_target_pairs={{1,0},{0,1},{3,2},{2,3},{5,4},{4,5},{7,6},{6,7},{9,8},{8,9},{11,10... | collective-permute-start | bytes 1474568 | tf_op jit(solution)/shard_map/ppermute | solution.py:25
  95.4 4.2 %collective-permute-start.24 = (bf16[80,640]{1,0:T(8,128)(2,1)S(1)}, bf16[80,640]{1,0:T(8,128)(2,1)S(1)}, u32[]{:S(2)}, u32[]{:S(2)}) collective-permute-start(bf16[80,640]{1,0:T(8,128)(2,1)S(1)} %get-tuple-element.73), channel_id=1, source_target_pairs={{2,0},{4,2},{6,4},{0,6},{3,1},{5,3},{7,5},{1,7},{10,8},{12,10},{14... | collective-permute-start | bytes 307208 | tf_op jit(solution)/shard_map/ppermute | solution.py:25
  98.4 2.3 %collective-permute-start.28 = (bf16[80,640]{1,0:T(8,128)(2,1)S(1)}, bf16[80,640]{1,0:T(8,128)(2,1)S(1)}, u32[]{:S(2)}, u32[]{:S(2)}) collective-permute-start(bf16[80,640]{1,0:T(8,128)(2,1)S(1)} %get-tuple-element.80), channel_id=1, source_target_pairs={{2,0},{4,2},{6,4},{0,6},{3,1},{5,3},{7,5},{1,7},{10,8},{12,10},{14... | collective-permute-start | bytes 307208 | tf_op jit(solution)/shard_map/ppermute | solution.py:25
  99.6 5.7 %collective-permute-start.29 = (bf16[80,640]{1,0:T(8,128)(2,1)S(1)}, bf16[80,640]{1,0:T(8,128)(2,1)S(1)}, u32[]{:S(2)}, u32[]{:S(2)}) collective-permute-start(bf16[80,640]{1,0:T(8,128)(2,1)S(1)} %get-tuple-element.81), channel_id=1, source_target_pairs={{4,0},{6,2},{0,4},{2,6},{5,1},{7,3},{1,5},{3,7},{12,8},{14,10},{8,... | collective-permute-start | bytes 307208 | tf_op jit(solution)/shard_map/ppermute | solution.py:25
  100.7 5.7 %collective-permute-start.30 = (bf16[80,640]{1,0:T(8,128)(2,1)S(1)}, bf16[80,640]{1,0:T(8,128)(2,1)S(1)}, u32[]{:S(2)}, u32[]{:S(2)}) collective-permute-start(bf16[80,640]{1,0:T(8,128)(2,1)S(1)} %get-tuple-element.82), channel_id=1, source_target_pairs={{6,0},{0,2},{2,4},{4,6},{7,1},{1,3},{3,5},{5,7},{14,8},{8,10},{10,... | collective-permute-start | bytes 307208 | tf_op jit(solution)/shard_map/ppermute | solution.py:25
  105.3 5.7 %collective-permute-start.25 = (bf16[80,640]{1,0:T(8,128)(2,1)S(1)}, bf16[80,640]{1,0:T(8,128)(2,1)S(1)}, u32[]{:S(2)}, u32[]{:S(2)}) collective-permute-start(bf16[80,640]{1,0:T(8,128)(2,1)S(1)} %get-tuple-element.74), channel_id=1, source_target_pairs={{4,0},{6,2},{0,4},{2,6},{5,1},{7,3},{1,5},{3,7},{12,8},{14,10},{8,... | collective-permute-start | bytes 307208 | tf_op jit(solution)/shard_map/ppermute | solution.py:25
  106.4 7.9 %collective-permute-start.26 = (bf16[80,640]{1,0:T(8,128)(2,1)S(1)}, bf16[80,640]{1,0:T(8,128)(2,1)S(1)}, u32[]{:S(2)}, u32[]{:S(2)}) collective-permute-start(bf16[80,640]{1,0:T(8,128)(2,1)S(1)} %get-tuple-element.75), channel_id=1, source_target_pairs={{6,0},{0,2},{2,4},{4,6},{7,1},{1,3},{3,5},{5,7},{14,8},{8,10},{10,... | collective-permute-start | bytes 307208 | tf_op jit(solution)/shard_map/ppermute | solution.py:25
  111.0 18.9 %collective-permute-start.31 = (bf16[80,640]{1,0:T(8,128)(2,1)S(1)}, bf16[80,640]{1,0:T(8,128)(2,1)S(1)}, u32[]{:S(2)}, u32[]{:S(2)}) collective-permute-start(bf16[80,640]{1,0:T(8,128)(2,1)S(1)} %shard_map.123), channel_id=1, source_target_pairs={{24,0},{0,8},{8,16},{16,24},{25,1},{1,9},{9,17},{17,25},{26,2},{2,... | collective-permute-start | bytes 307208 | tf_op jit(solution)/shard_map/ppermute | solution.py:25

commit v11 on v10

--- a/solution.py
+++ b/solution.py
@@ -17,6 +17,8 @@
 VMEM_LOAD = 36 * 1024 * 1024
 VMEM_ALL = 60 * 1024 * 1024
 COST_BYTES = 1024
+TOP = 4
+TAIL = 16
 EARLY = 1
 
 
@@ -164,28 +166,34 @@
 
 
 def update0_kernel(n, *refs):
-    parts, (raw, routes, gates, tokens, next_routes, upd, onward, part) = refs[:n], refs[n:]
+    parts, (raw, routes, gates, tokens, next_routes, upd, onward) = refs[:n], refs[n:]
     select = select_of(routes[0])
     select_next = select_of(next_routes[0])
     weight = slot_gates(select, routes[0], gates[0])
     fresh = (raw[...].astype(F32) + weight * summed(parts)).astype(BF16)
     old = pick(select_next, whole_block(tokens))
-    onward[...] = merged(select_next, select, fresh, old)
+    onward[:PACKED] = merged(select_next, select, fresh, old)
+    names = routes[1].astype(F32)
+    names = jnp.concatenate([names, jnp.full((TAIL - names.shape[0], names.shape[1]), 1.0)], 0)
+    onward[PACKED:] = jnp.zeros((TAIL, onward.shape[1]), BF16)
+    onward[PACKED:, : names.shape[1]] = names.astype(BF16)
     upd[...] = fresh
-    part[...] = jnp.zeros(part.shape, BF16)
-    part[: EARLY * CAP] = fresh[: EARLY * CAP]
-
-
-def merge_kernel(tokens, upd, routes, out):
+
+
+def merge_kernel(tokens, upd, routes, out, last):
     select = select_of(routes[0])
     hit = hit_rows(select)
-    width = tokens.shape[1]
+    height, width = tokens.shape
     for c in range(EARLY, PACK):
         value = placed(c, tokens[:, columns(c, width)], select, hit, upd[...])
-        out[:, columns(c - EARLY, width)] = value
-
-
-def release_kernel(_, __, ___, ____):
+        out[(c - EARLY) * height : (c - EARLY + 1) * height] = value
+    last[...] = jnp.zeros(last.shape, F32)
+    last[:CAP] = upd[...].astype(F32)[:CAP]
+    last[CAP : CAP + routes.shape[1], :height] = routes[0].astype(F32)
+    out[(PACK - EARLY) * height :] = last[...].astype(BF16)
+
+
+def release_kernel(*_):
     pass
 
 
@@ -200,12 +208,11 @@
     parts, (h, routes, gates, upd) = refs[:n], refs[n:]
     select = select_of(routes[1])
     weight = slot_gates(select, routes[1], gates[1])
-    upd[...] = (h[...].astype(F32) + weight * summed(parts)).astype(BF16)
-
-
-def enter1_kernel(h, scaled, *refs):
-    out = refs[-2]
-    values = h[...].astype(F32)
+    upd[...] = (h[:PACKED].astype(F32) + weight * summed(parts)).astype(BF16)
+
+
+def enter1_kernel(h, scaled, _, __, out, ___):
+    values = h[:PACKED].astype(F32)
     out[:PACKED] = (values * inv_rms_of(values)).astype(BF16)
     out[PACKED:] = scaled[...]
 
@@ -220,7 +227,7 @@
 
 def grad1_kernel(n, *refs):
     parts, (h, cot, upd) = refs[:n], refs[n:]
-    upd[...] = state_grad(parts, h[...], cot[...])
+    upd[...] = state_grad(parts, h[:PACKED], cot[...])
 
 
 def enter0_kernel(upd1, next_routes, routes, gates, bulk, _, c0, out):
@@ -242,19 +249,19 @@
         out[:, k] = placed(chunk, value, second, hit2, fresh)
 
 
-def finish_state_kernel(early, rest, part, prev2_routes, upd1, prev_routes, out, outs, sems):
+def finish_state_kernel(early, rest, upd1, h, out, outs, last, sems):
     height, width = out.shape
-    first, second = select_of(prev2_routes[0]), select_of(prev_routes[0])
+    at = (PACK - EARLY) * height
+    last[...] = rest[at:].astype(F32)
+    first = select_of(last[CAP : CAP + TOP, :height])
+    second = select_of(h[PACKED:].astype(F32)[:TOP, :height])
     hit1, hit2 = hit_rows(first), hit_rows(second)
-    rows = jnp.concatenate(
-        [part[...].astype(F32), jnp.zeros((PACKED - part.shape[0], part.shape[1]), F32)], axis=0
-    )
+    rows = jnp.concatenate([last[...], jnp.zeros((PACKED - TAIL, last.shape[1]), F32)], axis=0)
     for c in range(PACK):
         if c < EARLY:
-            old = early[c * height : (c + 1) * height]
-            value = placed(c, old, first, hit1, rows.astype(BF16))
+            value = placed(c, early[...], first, hit1, rows.astype(BF16))
         else:
-            value = rest[:, columns(c - EARLY, width)]
+            value = rest[(c - EARLY) * height : (c - EARLY + 1) * height]
         outs[:, columns(c, width)] = placed(c, value, second, hit2, upd1[...])
     for store in start_rows(outs, out, sems):
         store.wait()
@@ -267,13 +274,13 @@
     return grad_gate, grad_up
 
 
-def gather_rows(blocks, first, unpacked, whole32, whole):
+def gather_rows(blocks, unpacked, whole32, whole):
     width = whole.shape[1]
     used = len(blocks) * CAP
     if used < whole.shape[0]:
         whole32[used:] = jnp.zeros((whole.shape[0] - used, width), F32)
     for i, b in enumerate(blocks):
-        unpacked[i] = b[first : first + PACKED].astype(F32)
+        unpacked[i] = b[...].astype(F32)
         for c in range(PACK):
             whole32[i * CAP : (i + 1) * CAP, columns(c, width)] = unpacked[
                 i, c * CAP : (c + 1) * CAP
@@ -308,7 +315,7 @@
         fetch_u.start()
     for _, _, fetch_d in fetches:
         fetch_d.start()
-    gather_rows(blocks, 0, unpacked, whole32, x)
+    gather_rows(blocks, unpacked, whole32, x)
     acc_g = jnp.zeros(pre_gate.shape, F32)
     acc_u = jnp.zeros(pre_up.shape, F32)
     for c, (fetch_g, fetch_u, _) in enumerate(fetches):
@@ -359,8 +366,8 @@
     (kept,) = refs[n + 5 : n + 6]
     parts = refs[n + 6 : 2 * n + 6]
     unpacked, whole32, held, x, g = refs[2 * n + 6 :]
-    gather_rows(blocks, 0, unpacked, whole32.at[0], x)
-    gather_rows(blocks, PACKED, unpacked, whole32.at[1], g)
+    gather_rows([b.at[:PACKED] for b in blocks], unpacked, whole32.at[0], x)
+    gather_rows([b.at[PACKED:] for b in blocks], unpacked, whole32.at[1], g)
     width, hidden = gate.shape
     kept[:, :width] = x0[...]
     kept[:, width : 2 * width] = x[...]
@@ -382,7 +389,7 @@
     (g_grad,) = refs[n + 5 : n + 6]
     parts = refs[n + 6 : 2 * n + 6]
     unpacked, whole32, held, g = refs[2 * n + 6 :]
-    gather_rows(blocks, 0, unpacked, whole32, g)
+    gather_rows(blocks, unpacked, whole32, g)
     width, hidden = gate.shape
     g_grad[:, :width] = g[...]
     acc_a = dot(g[...], down[...], 1, 1)
@@ -526,8 +533,6 @@
 
     cot1_all = shifted(cotangent, "section", -1)
     next_routes = shifted(routes[1:], "section", -1)
-    prev_routes = shifted(routes[1:], "section", 1)
-    prev2_routes = shifted(routes[:1], "section", 2)
 
     raw0, normed0, early = call(
         first_rows_kernel,
@@ -555,26 +560,25 @@
         vmem=VMEM_LOAD,
     )
     parts = to_group(parts)
-    few = -(-EARLY * CAP // 16) * 16
-    upd0, h1, part0 = call(
+    upd0, h1 = call(
         part(update0_kernel, n),
-        [one, one, ((few, step), BF16)],
+        [one, ((PACKED + TAIL, step), BF16)],
         [*parts, raw0, routes, gates, tokens, next_routes],
     )
     h1 = shifted(h1, "section", 1)
-    cot1, scaled1 = call(grad_rows_kernel, [one, one], [cot1_all, routes, gates])
-    part0 = shifted(part0, "section", 2)
     (rest,) = call(
         merge_kernel,
-        [((tokens.shape[0], width - EARLY * step), BF16)],
+        [(((PACK - EARLY) * tokens.shape[0] + TAIL, step), BF16)],
         [tokens, upd0, routes],
-    )
+        scratch=[pltpu.VMEM((TAIL, step), F32)],
+    )
+    cot1, scaled1 = call(grad_rows_kernel, [one, one], [cot1_all, routes, gates])
 
     enter1, cot1_all = call(
         enter1_kernel,
         [((2 * PACKED, step), BF16), (tokens.shape, BF16)],
-        [h1, scaled1, cot1_all, early, prev_routes, prev2_routes, part0],
-        any_args=(2, 3, 4, 5, 6),
+        [h1, scaled1, cot1_all, early],
+        any_args=(2, 3),
         any_outs=(1,),
         aliases={2: 1},
     )
@@ -597,7 +601,7 @@
 
     (rest,) = call(
         release_kernel,
-        [((tokens.shape[0], width - EARLY * step), BF16)],
+        [(rest.shape, BF16)],
         [rest, cot0_all, upd1],
         any_args=(0, 1, 2),
         any_outs=(0,),
@@ -640,10 +644,11 @@
     (state,) = call(
         finish_state_kernel,
         [(tokens.shape, BF16)],
-        [early, rest, part0, prev2_routes, last1, prev_routes],
+        [early, rest, last1, h1],
         any_outs=(0,),
         scratch=[
             pltpu.VMEM(tokens.shape, BF16),
+            pltpu.VMEM((TAIL, step), F32),
             pltpu.SemaphoreType.DMA((tokens.shape[0] // 16,)),
         ],
     )

time: 137 us -> 136 us (level)
  starting transfers between devices: 40.4 us -> 37.9 us
  waiting for transfers between devices: 51.9 us -> 53.4 us
    ppermute x34 -> x31, starting transfers between devices: 40.4 us -> 37.9 us  [shifted(): lax.ppermute(block, axis, [((i - distance) % size, i) for i in range(size)])]
    ppermute x34 -> x31, waiting for transfers between devices: 51.9 us -> 53.4 us  [shifted(): lax.ppermute(block, axis, [((i - distance) % size, i) for i in range(size)])]
  transfers between devices with their start and end apart: 34 -> 31, of which waited for: 21 -> 20; matrix products, arithmetic and copies ran while one was open for 0% -> 0% of each run, Pallas kernels for 30% -> 30%
where the time goes in v11:
time: 136 us
  waiting for transfers between devices  53.4 us (39%)
  Pallas kernels  43.6 us (32%)
  starting transfers between devices  37.9 us (28%)
    ppermute x31, waiting for transfers between devices, shifted(): lax.ppermute(block, axis, [((i - distance) % size, i) for i in range(size)])  53.4 us
    ppermute x31, starting transfers between devices, shifted(): lax.ppermute(block, axis, [((i - distance) % size, i) for i in range(size)])  37.9 us
    pallas_call x15, Pallas kernels, call(): pl.pallas_call(kernel, out_shape=outs, in_specs=[anywhere if i in any_arg...  30.5 us
    pallas_call x3, Pallas kernels, chunked_call(): pl.pallas_call(kernel, grid=(steps,), out_shape=[jax.ShapeDtypeStruct(s,...  13.1 us
  transfers between devices with their start and end apart: 31, of which 20 were waited for; matrix products, arithmetic and copies ran while one was open for 0% of the time, Pallas kernels for 30%

profile of v11, /device:TPU:0, one launch (start us, length us, event | category | flops | bytes accessed | tf_op | source)
XLA Modules:
  0.0 135.9 jit_solution(15399919636130382569)
XLA Ops:
  0.6 5.1 %collective-permute-start.8 = (bf16[128,5120]{1,0:T(8,128)(2,1)}, bf16[128,5120]{1,0:T(8,128)(2,1)S(1)}, u32[]{:S(2)}, u32[]{:S(2)}) collective-permute-start(bf16[128,5120]{1,0:T(8,128)(2,1)} %param.8), channel_id=1, source_target_pairs={{8,0},{16,8},{24,16},{0,24},{9,1},{17,9},{25,17},{1,25},{10,2},{18... | collective-permute-start | bytes 3932168 | tf_op jit(solution)/shard_map/ppermute | solution.py:27
  5.7 2.9 %shard_map.110 = (bf16[80,640]{1,0:T(8,128)(2,1)S(1)}, bf16[80,640]{1,0:T(8,128)(2,1)S(1)}, bf16[128,640]{1,0:T(8,128)(2,1)}) custom-call(bf16[128,5120]{1,0:T(8,128)(2,1)} %tokens.3, s32[2,4,128]{2,1,0:T(4,128)} %bitcast.8), custom_call_target="tpu_custom_call" | custom-call | bytes 1024 | tf_op jit(solution)/shard_map/pallas_call | solution.py:40
  8.6 0.1 collective-permute-start
  8.7 1.6 %collective-permute-start.1 = (bf16[80,640]{1,0:T(8,128)(2,1)S(1)}, bf16[80,640]{1,0:T(8,128)(2,1)S(1)}, u32[]{:S(2)}, u32[]{:S(2)}) collective-permute-start(bf16[80,640]{1,0:T(8,128)(2,1)S(1)} %get-tuple-element.45.refs_0_), channel_id=1, source_target_pairs={{4,0},{6,2},{0,4},{2,6},{5,1},{7,3},{1,5},{3,7},{12,8},{14,10},{8,... | collective-permute-start | bytes 307208 | tf_op jit(solution)/shard_map/ppermute | solution.py:27
  10.2 1.4 %collective-permute-start.2 = (bf16[80,640]{1,0:T(8,128)(2,1)S(1)}, bf16[80,640]{1,0:T(8,128)(2,1)S(1)}, u32[]{:S(2)}, u32[]{:S(2)}) collective-permute-start(bf16[80,640]{1,0:T(8,128)(2,1)S(1)} %get-tuple-element.45.refs_0_), channel_id=1, source_target_pairs={{2,0},{4,2},{6,4},{0,6},{3,1},{5,3},{7,5},{1,7},{10,8},{12,10},{14... | collective-permute-start | bytes 307208 | tf_op jit(solution)/shard_map/ppermute | solution.py:27
  11.6 1.6 %collective-permute-done.refs_1_ = bf16[80,640]{1,0:T(8,128)(2,1)S(1)} collective-permute-done((bf16[80,640]{1,0:T(8,128)(2,1)S(1)}, bf16[80,640]{1,0:T(8,128)(2,1)S(1)}, u32[]{:S(2)}, u32[]{:S(2)}) %collective-permute-start) | collective-permute-done | bytes 102432 | tf_op jit(solution)/shard_map/ppermute | solution.py:27
  13.2 1.2 collective-permute-done.1.refs_2_
  14.4 0.6 collective-permute-done.2.refs_3_
  15.1 6.5 %shard_map.111 = (bf16[40,5120]{1,0:T(8,128)(2,1)S(1)}, f32[40,512]{1,0:T(8,128)S(1)}, f32[40,512]{1,0:T(8,128)S(1)}, bf16[40,512]{1,0:T(8,128)(2,1)S(1)}, bf16[...) custom-call(bf16[80,640]{1,0:T(8,128)(2,1)S(1)} %get-tuple-element.4, ...), custom_call_target="tpu_custom_call" | custom-call | bytes 1024 | tf_op jit(solution)/shard_map/pallas_call | solution.py:40
  21.6 2.3 %collective-permute-start.3 = (bf16[80,640]{1,0:T(8,128)(2,1)S(1)}, bf16[80,640]{1,0:T(8,128)(2,1)S(1)}, u32[]{:S(2)}, u32[]{:S(2)}) collective-permute-start(bf16[80,640]{1,0:T(8,128)(2,1)S(1)} %get-tuple-element.47), channel_id=1, source_target_pairs={{2,0},{4,2},{6,4},{0,6},{3,1},{5,3},{7,5},{1,7},{10,8},{12,10},{14... | collective-permute-start | bytes 307208 | tf_op jit(solution)/shard_map/ppermute | solution.py:27
  23.9 0.5 collective-permute-start.4
  24.4 0.0 collective-permute-start.5
  24.4 0.5 collective-permute-start.6
  24.9 9.2 %collective-permute-done.6.refs_8_.next_routes = s32[1,4,128]{2,1,0:T(4,128)S(1)} collective-permute-done((s32[1,4,128]{2,1,0:T(4,128)S(1)}, s32[1,4,128]{2,1,0:T(4,128)S(1)}, u32[]{:S(2)}, u32[]{:S(2)}) %collective-permute-start.6) | collective-permute-done | bytes 2080 | tf_op jit(solution)/shard_map/ppermute | solution.py:27
  34.1 1.4 %collective-permute-start.9 = (bf16[128,640]{1,0:T(8,128)(2,1)S(1)}, bf16[128,640]{1,0:T(8,128)(2,1)S(1)}, u32[]{:S(2)}, u32[]{:S(2)}) collective-permute-start(bf16[128,640]{1,0:T(8,128)(2,1)S(1)} %copy-done.3), channel_id=1, source_target_pairs={{16,0},{24,8},{0,16},{8,24},{17,1},{25,9},{1,17},{9,25},{18,2},{26... | collective-permute-start | bytes 491528 | tf_op jit(solution)/shard_map/ppermute | solution.py:27
  35.5 0.7 shard_map.112
  36.2 3.4 %collective-permute-start.7 = (bf16[96,640]{1,0:T(8,128)(2,1)S(1)}, bf16[96,640]{1,0:T(8,128)(2,1)S(1)}, u32[]{:S(2)}, u32[]{:S(2)}) collective-permute-start(bf16[96,640]{1,0:T(8,128)(2,1)S(1)} %get-tuple-element.51), channel_id=1, source_target_pairs={{24,0},{0,8},{8,16},{16,24},{25,1},{1,9},{9,17},{17,25},{26,2},{2,... | collective-permute-start | bytes 368648 | tf_op jit(solution)/shard_map/ppermute | solution.py:27
  39.7 0.5 shard_map.113
  40.2 6.0 %collective-permute-done.9.__.early = bf16[128,640]{1,0:T(8,128)(2,1)S(1)} collective-permute-done((bf16[128,640]{1,0:T(8,128)(2,1)S(1)}, bf16[128,640]{1,0:T(8,128)(2,1)S(1)}, u32[]{:S(2)}, u32[]{:S(2)}) %collective-permute-start.9) | collective-permute-done | bytes 163872 | tf_op jit(solution)/shard_map/ppermute | solution.py:27
  46.2 0.3 shard_map.114
  46.5 1.2 collective-permute-start.17
  47.7 1.6 %collective-permute-start.11 = (bf16[160,640]{1,0:T(8,128)(2,1)S(1)}, bf16[160,640]{1,0:T(8,128)(2,1)S(1)}, u32[]{:S(2)}, u32[]{:S(2)}) collective-permute-start(bf16[160,640]{1,0:T(8,128)(2,1)S(1)} %get-tuple-element.54.refs_0_), channel_id=1, source_target_pairs={{4,0},{6,2},{0,4},{2,6},{5,1},{7,3},{1,5},{3,7},{12,8},{14,10},{8,... | collective-permute-start | bytes 614408 | tf_op jit(solution)/shard_map/ppermute | solution.py:27
  49.3 1.4 %collective-permute-start.12 = (bf16[160,640]{1,0:T(8,128)(2,1)S(1)}, bf16[160,640]{1,0:T(8,128)(2,1)S(1)}, u32[]{:S(2)}, u32[]{:S(2)}) collective-permute-start(bf16[160,640]{1,0:T(8,128)(2,1)S(1)} %get-tuple-element.54.refs_0_), channel_id=1, source_target_pairs={{2,0},{4,2},{6,4},{0,6},{3,1},{5,3},{7,5},{1,7},{10,8},{12,10},{14... | collective-permute-start | bytes 614408 | tf_op jit(solution)/shard_map/ppermute | solution.py:27
  50.7 3.8 %collective-permute-done.10.refs_1_ = bf16[160,640]{1,0:T(8,128)(2,1)S(1)} collective-permute-done((bf16[160,640]{1,0:T(8,128)(2,1)S(1)}, bf16[160,640]{1,0:T(8,128)(2,1)S(1)}, u32[]{:S(2)}, u32[]{:S(2)}) %collective-permute-start.10) | collective-permute-done | bytes 204832 | tf_op jit(solution)/shard_map/ppermute | solution.py:27
  54.5 1.1 collective-permute-done.11.refs_2_
  55.6 2.9 %collective-permute-done.12.refs_3_ = bf16[160,640]{1,0:T(8,128)(2,1)S(1)} collective-permute-done((bf16[160,640]{1,0:T(8,128)(2,1)S(1)}, bf16[160,640]{1,0:T(8,128)(2,1)S(1)}, u32[]{:S(2)}, u32[]{:S(2)}) %collective-permute-start.12) | collective-permute-done | bytes 204832 | tf_op jit(solution)/shard_map/ppermute | solution.py:27
  58.5 6.8 %shard_map.115 = (bf16[40,17408]{1,0:T(8,128)(2,1)S(1)}, bf16[80,640]{1,0:T(8,128)(2,1)S(1)}, bf16[80,640]{1,0:T(8,128)(2,1)S(1)}, bf16[80,640]{1,0:T(8,128)(2,1)S(1)}, bf16[80,640]{1,0:T(8,128)(2,1)S(1)}) custom-call(bf16[160,640]{1,0:T(8,128)(2,1)S(1)} %get-tuple-element.54.refs_0_, bf16[160,640]{1,0:T(8,128)(2,1)S(1)} %collective-permute-done.10.refs_1_, ...), custom_call_target="tpu_custom_call" | custom-call | bytes 1024 | tf_op jit(solution)/shard_map/pallas_call | solution.py:40
  65.4 1.6 %collective-permute-start.29 = (bf16[40,17408]{1,0:T(8,128)(2,1)S(1)}, bf16[40,17408]{1,0:T(8,128)(2,1)S(1)}, u32[]{:S(2)}, u32[]{:S(2)}) collective-permute-start(bf16[40,17408]{1,0:T(8,128)(2,1)S(1)} %get-tuple-element.75.act.refs_0_.refs_2_.refs_4_.refs_6_), channel_id=1, source_target_pairs={{1,0},{0,1},{3,2},{2,3},{5,4},{4,5},{7,6},{6,7},{9,8},{8,9},{11,10... | collective-permute-start | bytes 4177928 | tf_op jit(solution)/shard_map/ppermute | solution.py:27
  66.9 1.9 %collective-permute-start.13 = (bf16[80,640]{1,0:T(8,128)(2,1)S(1)}, bf16[80,640]{1,0:T(8,128)(2,1)S(1)}, u32[]{:S(2)}, u32[]{:S(2)}) collective-permute-start(bf16[80,640]{1,0:T(8,128)(2,1)S(1)} %get-tuple-element.61), channel_id=1, source_target_pairs={{2,0},{4,2},{6,4},{0,6},{3,1},{5,3},{7,5},{1,7},{10,8},{12,10},{14... | collective-permute-start | bytes 307208 | tf_op jit(solution)/shard_map/ppermute | solution.py:27
  68.9 0.5 collective-permute-start.14
  69.4 2.4 %collective-permute-done.13.refs_1_ = bf16[80,640]{1,0:T(8,128)(2,1)S(1)} collective-permute-done((bf16[80,640]{1,0:T(8,128)(2,1)S(1)}, bf16[80,640]{1,0:T(8,128)(2,1)S(1)}, u32[]{:S(2)}, u32[]{:S(2)}) %collective-permute-start.13) | collective-permute-done | bytes 102432 | tf_op jit(solution)/shard_map/ppermute | solution.py:27
  71.7 3.0 %collective-permute-done.14.refs_2_ = bf16[80,640]{1,0:T(8,128)(2,1)S(1)} collective-permute-done((bf16[80,640]{1,0:T(8,128)(2,1)S(1)}, bf16[80,640]{1,0:T(8,128)(2,1)S(1)}, u32[]{:S(2)}, u32[]{:S(2)}) %collective-permute-start.14) | collective-permute-done | bytes 102432 | tf_op jit(solution)/shard_map/ppermute | solution.py:27
  74.7 0.4 shard_map.116
  75.2 2.0 %collective-permute-start.16 = (bf16[80,640]{1,0:T(8,128)(2,1)S(1)}, bf16[80,640]{1,0:T(8,128)(2,1)S(1)}, u32[]{:S(2)}, u32[]{:S(2)}) collective-permute-start(bf16[80,640]{1,0:T(8,128)(2,1)S(1)} %shard_map.116), channel_id=1, source_target_pairs={{8,0},{16,8},{24,16},{0,24},{9,1},{17,9},{25,17},{1,25},{10,2},{18... | collective-permute-start | bytes 307208 | tf_op jit(solution)/shard_map/ppermute | solution.py:27
  77.2 0.7 shard_map.117.__0_
  77.9 2.0 %collective-permute-done.16.__2_.upd1.refs_7_ = bf16[80,640]{1,0:T(8,128)(2,1)S(1)} collective-permute-done((bf16[80,640]{1,0:T(8,128)(2,1)S(1)}, bf16[80,640]{1,0:T(8,128)(2,1)S(1)}, u32[]{:S(2)}, u32[]{:S(2)}) %collective-permute-start.16) | collective-permute-done | bytes 102432 | tf_op jit(solution)/shard_map/ppermute | solution.py:27
  79.9 1.0 collective-permute-start.24
  80.9 0.8 shard_map.119
  81.7 0.1 collective-permute-start.18
  81.8 1.6 %collective-permute-start.19 = (bf16[80,640]{1,0:T(8,128)(2,1)S(1)}, bf16[80,640]{1,0:T(8,128)(2,1)S(1)}, u32[]{:S(2)}, u32[]{:S(2)}) collective-permute-start(bf16[80,640]{1,0:T(8,128)(2,1)S(1)} %get-tuple-element.67.refs_0_), channel_id=1, source_target_pairs={{4,0},{6,2},{0,4},{2,6},{5,1},{7,3},{1,5},{3,7},{12,8},{14,10},{8,... | collective-permute-start | bytes 307208 | tf_op jit(solution)/shard_map/ppermute | solution.py:27
  83.4 1.4 %collective-permute-start.20 = (bf16[80,640]{1,0:T(8,128)(2,1)S(1)}, bf16[80,640]{1,0:T(8,128)(2,1)S(1)}, u32[]{:S(2)}, u32[]{:S(2)}) collective-permute-start(bf16[80,640]{1,0:T(8,128)(2,1)S(1)} %get-tuple-element.67.refs_0_), channel_id=1, source_target_pairs={{2,0},{4,2},{6,4},{0,6},{3,1},{5,3},{7,5},{1,7},{10,8},{12,10},{14... | collective-permute-start | bytes 307208 | tf_op jit(solution)/shard_map/ppermute | solution.py:27
  84.8 1.6 %collective-permute-done.18.refs_1_ = bf16[80,640]{1,0:T(8,128)(2,1)S(1)} collective-permute-done((bf16[80,640]{1,0:T(8,128)(2,1)S(1)}, bf16[80,640]{1,0:T(8,128)(2,1)S(1)}, u32[]{:S(2)}, u32[]{:S(2)}) %collective-permute-start.18) | collective-permute-done | bytes 102432 | tf_op jit(solution)/shard_map/ppermute | solution.py:27
  86.4 1.2 collective-permute-done.19.refs_2_
  87.6 0.6 collective-permute-done.20.refs_3_
  88.2 5.1 %shard_map.120 = (bf16[40,6144]{1,0:T(8,128)(2,1)S(1)}, bf16[80,640]{1,0:T(8,128)(2,1)S(1)}, bf16[80,640]{1,0:T(8,128)(2,1)S(1)}, bf16[80,640]{1,0:T(8,128)(2,1)S(1)}, bf16[80,640]{1,0:T(8,128)(2,1)S(1)}) custom-call(bf16[80,640]{1,0:T(8,128)(2,1)S(1)} %get-tuple-element.67.refs_0_, bf16[80,640]{1,0:T(8,128)(2,1)S(1)} %collective-permute-done.18.refs_1_, ...), custom_call_target="tpu_custom_call" | custom-call | bytes 1024 | tf_op jit(solution)/shard_map/pallas_call | solution.py:40
  93.3 1.6 %collective-permute-start.30 = (bf16[40,6144]{1,0:T(8,128)(2,1)S(1)}, bf16[40,6144]{1,0:T(8,128)(2,1)S(1)}, u32[]{:S(2)}, u32[]{:S(2)}) collective-permute-start(bf16[40,6144]{1,0:T(8,128)(2,1)S(1)} %get-tuple-element.76._.refs_0_.refs_2_), channel_id=1, source_target_pairs={{1,0},{0,1},{3,2},{2,3},{5,4},{4,5},{7,6},{6,7},{9,8},{8,9},{11,10... | collective-permute-start | bytes 1474568 | tf_op jit(solution)/shard_map/ppermute | solution.py:27
  94.8 1.9 %collective-permute-start.21 = (bf16[80,640]{1,0:T(8,128)(2,1)S(1)}, bf16[80,640]{1,0:T(8,128)(2,1)S(1)}, u32[]{:S(2)}, u32[]{:S(2)}) collective-permute-start(bf16[80,640]{1,0:T(8,128)(2,1)S(1)} %get-tuple-element.71), channel_id=1, source_target_pairs={{2,0},{4,2},{6,4},{0,6},{3,1},{5,3},{7,5},{1,7},{10,8},{12,10},{14... | collective-permute-start | bytes 307208 | tf_op jit(solution)/shard_map/ppermute | solution.py:27
  96.7 1.1 shard_map.122
  97.8 0.1 collective-permute-start.25
  97.9 1.1 collective-permute-done.21.refs_1_
  99.0 0.5 collective-permute-start.26
  99.5 0.6 collective-permute-done.25.refs_1_
  100.2 1.1 collective-permute-start.27
  101.2 3.5 %collective-permute-done.26.refs_2_ = bf16[80,640]{1,0:T(8,128)(2,1)S(1)} collective-permute-done((bf16[80,640]{1,0:T(8,128)(2,1)S(1)}, bf16[80,640]{1,0:T(8,128)(2,1)S(1)}, u32[]{:S(2)}, u32[]{:S(2)}) %collective-permute-start.26) | collective-permute-done | bytes 102432 | tf_op jit(solution)/shard_map/ppermute | solution.py:27
  104.7 1.1 collective-permute-done.27.refs_3_
  105.9 0.2 shard_map.123
  106.1 4.3 %collective-permute-done.22.refs_2_ = bf16[80,640]{1,0:T(8,128)(2,1)S(1)} collective-permute-done((bf16[80,640]{1,0:T(8,128)(2,1)S(1)}, bf16[80,640]{1,0:T(8,128)(2,1)S(1)}, u32[]{:S(2)}, u32[]{:S(2)}) %collective-permute-start.22) | collective-permute-done | bytes 102432 | tf_op jit(solution)/shard_map/ppermute | solution.py:27
  110.4 2.3 %collective-permute-start.28 = (bf16[80,640]{1,0:T(8,128)(2,1)S(1)}, bf16[80,640]{1,0:T(8,128)(2,1)S(1)}, u32[]{:S(2)}, u32[]{:S(2)}) collective-permute-start(bf16[80,640]{1,0:T(8,128)(2,1)S(1)} %shard_map.123), channel_id=1, source_target_pairs={{24,0},{0,8},{8,16},{16,24},{25,1},{1,9},{9,17},{17,25},{26,2},{2,... | collective-permute-start | bytes 307208 | tf_op jit(solution)/shard_map/ppermute | solution.py:27
  112.8 2.4 %shard_map.121 = bf16[128,5120]{1,0:T(8,128)(2,1)} custom-call(bf16[80,640]{1,0:T(8,128)(2,1)S(1)} %get-tuple-element.70.refs_0_, bf16[80,640]{1,0:T(8,128)(2,1)S(1)} %collective-permute-done.21.refs_1_, bf16[80,640]{1,0:T(8,128)(2,1)S(1)} %collective-permute-done.22.refs_2_, bf16[80,640]{1,0:T(8,128)(2,1)S(1)} %collective-permute-done.23.refs_3_, ...), custom_call_target="tpu_custom_call" | custom-call | bytes 1024 | tf_op jit(solution)/shard_map/pallas_call | solution.py:40
  115.2 2.9 %shard_map.125 = (bf16[5120,160]{1,0:T(8,128)(2,1)S(1)}, bf16[512,160]{1,0:T(8,128)(2,1)S(1)}) custom-call(bf16[40,17408]{1,0:T(8,128)(2,1)S(1)} %get-tuple-element.75.act.refs_0_.refs_2_.refs_4_.refs_6_, bf16[40,17408]{1,0:T(8,128)(2,1)S(1)} %collective-permute-done.29.refs_1_.refs_3_.refs_5_.refs_7_, ...), custom_call_target="tpu_custom_call" | custom-call | bytes 1024 | tf_op jit(solution)/shard_map/pallas_call | solution.py:443
  118.1 6.2 %shard_map.126 = (bf16[5120,512]{1,0:T(8,128)(2,1)}, bf16[5120,512]{1,0:T(8,128)(2,1)}) custom-call(bf16[5120,160]{1,0:T(8,128)(2,1)S(1)} %get-tuple-element.81.x_t, bf16[40,6144]{1,0:T(8,128)(2,1)S(1)} %get-tuple-element.76._.refs_0_.refs_2_, bf16[40,6144]{1,0:T(8,128)(2,1)S(1)} %collective-permute-done.30.refs_1_.refs_3_, ...), custom_call_target="tpu_custom_call" | custom-call | bytes 1024 | tf_op jit(solution)/shard_map/pallas_call | solution.py:443
  124.3 4.1 %shard_map.127 = bf16[512,5120]{1,0:T(8,128)(2,1)} custom-call(bf16[512,160]{1,0:T(8,128)(2,1)S(1)} %get-tuple-element.84.act_t, bf16[40,6144]{1,0:T(8,128)(2,1)S(1)} %get-tuple-element.76._.refs_0_.refs_2_, bf16[40,6144]{1,0:T(8,128)(2,1)S(1)} %collective-permute-done.30.refs_1_.refs_3_, ...), custom_call_target="tpu_custom_call" | custom-call | bytes 1024 | tf_op jit(solution)/shard_map/pallas_call | solution.py:443
  128.3 5.5 %collective-permute-done.24.rest = bf16[912,640]{1,0:T(8,128)(2,1)S(1)} collective-permute-done((bf16[912,640]{1,0:T(8,128)(2,1)S(1)}, bf16[912,640]{1,0:T(8,128)(2,1)S(1)}, u32[]{:S(2)}, u32[]{:S(2)}) %collective-permute-start.24) | collective-permute-done | bytes 1167392 | tf_op jit(solution)/shard_map/ppermute | solution.py:27
  133.8 1.9 %shard_map.124 = bf16[128,5120]{1,0:T(8,128)(2,1)} custom-call(bf16[128,640]{1,0:T(8,128)(2,1)S(1)} %collective-permute-done.9.__.early, bf16[912,640]{1,0:T(8,128)(2,1)S(1)} %collective-permute-done.24.rest, bf16[80,640]{1,0:T(8,128)(2,1)S(1)} %collective-permute-done.28.upd1, bf16[96,640]{1,0:T(8,128)(2,1)S(1)} %collective-permute-done.7.h.refs_4_), custom_call_target="tpu_custom_call" | custom-call | bytes 1024 | tf_op jit(solution)/shard_map/pallas_call | solution.py:40
  (25 shorter events, 0.1 us)
Async XLA Ops:
  0.6 39.1 %collective-permute-start.8 = (bf16[128,5120]{1,0:T(8,128)(2,1)}, bf16[128,5120]{1,0:T(8,128)(2,1)S(1)}, u32[]{:S(2)}, u32[]{:S(2)}) collective-permute-start(bf16[128,5120]{1,0:T(8,128)(2,1)} %param.8), channel_id=1, source_target_pairs={{8,0},{16,8},{24,16},{0,24},{9,1},{17,9},{25,17},{1,25},{10,2},{18... | collective-permute-start | bytes 3932168 | tf_op jit(solution)/shard_map/ppermute | solution.py:27
  8.6 4.6 %collective-permute-start = (bf16[80,640]{1,0:T(8,128)(2,1)S(1)}, bf16[80,640]{1,0:T(8,128)(2,1)S(1)}, u32[]{:S(2)}, u32[]{:S(2)}) collective-permute-start(bf16[80,640]{1,0:T(8,128)(2,1)S(1)} %get-tuple-element.45.refs_0_), channel_id=1, source_target_pairs={{6,0},{0,2},{2,4},{4,6},{7,1},{1,3},{3,5},{5,7},{14,8},{8,10},{10,... | collective-permute-start | bytes 307208 | tf_op jit(solution)/shard_map/ppermute | solution.py:27
  8.7 5.8 %collective-permute-start.1 = (bf16[80,640]{1,0:T(8,128)(2,1)S(1)}, bf16[80,640]{1,0:T(8,128)(2,1)S(1)}, u32[]{:S(2)}, u32[]{:S(2)}) collective-permute-start(bf16[80,640]{1,0:T(8,128)(2,1)S(1)} %get-tuple-element.45.refs_0_), channel_id=1, source_target_pairs={{4,0},{6,2},{0,4},{2,6},{5,1},{7,3},{1,5},{3,7},{12,8},{14,10},{8,... | collective-permute-start | bytes 307208 | tf_op jit(solution)/shard_map/ppermute | solution.py:27
  10.2 4.8 %collective-permute-start.2 = (bf16[80,640]{1,0:T(8,128)(2,1)S(1)}, bf16[80,640]{1,0:T(8,128)(2,1)S(1)}, u32[]{:S(2)}, u32[]{:S(2)}) collective-permute-start(bf16[80,640]{1,0:T(8,128)(2,1)S(1)} %get-tuple-element.45.refs_0_), channel_id=1, source_target_pairs={{2,0},{4,2},{6,4},{0,6},{3,1},{5,3},{7,5},{1,7},{10,8},{12,10},{14... | collective-permute-start | bytes 307208 | tf_op jit(solution)/shard_map/ppermute | solution.py:27
  15.1 9.3 %copy-start.1 = (s32[2,128,4]{1,2,0:T(4,128)S(1)}, s32[2,128,4]{1,2,0:T(4,128)}, u32[]{:S(2)}) copy-start(s32[2,128,4]{1,2,0:T(4,128)} %param.12) | copy-start | bytes 12292
  15.1 19.0 %copy-start.3 = (bf16[128,640]{1,0:T(8,128)(2,1)S(1)}, bf16[128,640]{1,0:T(8,128)(2,1)}, u32[]{:S(2)}) copy-start(bf16[128,640]{1,0:T(8,128)(2,1)} %get-tuple-element.53) | copy-start | bytes 491524
  15.1 20.4 %copy-start = (bf16[128,5120]{1,0:T(8,128)(2,1)S(1)}, bf16[128,5120]{1,0:T(8,128)(2,1)}, u32[]{:S(2)}) copy-start(bf16[128,5120]{1,0:T(8,128)(2,1)} %tokens.3) | copy-start | bytes 3932164
  15.1 20.5 %copy-start.2 = (f32[2,128,4]{1,2,0:T(4,128)S(1)}, f32[2,128,4]{1,2,0:T(4,128)}, u32[]{:S(2)}) copy-start(f32[2,128,4]{1,2,0:T(4,128)} %param.13) | copy-start | bytes 12292
  21.6 13.9 %collective-permute-start.3 = (bf16[80,640]{1,0:T(8,128)(2,1)S(1)}, bf16[80,640]{1,0:T(8,128)(2,1)S(1)}, u32[]{:S(2)}, u32[]{:S(2)}) collective-permute-start(bf16[80,640]{1,0:T(8,128)(2,1)S(1)} %get-tuple-element.47), channel_id=1, source_target_pairs={{2,0},{4,2},{6,4},{0,6},{3,1},{5,3},{7,5},{1,7},{10,8},{12,10},{14... | collective-permute-start | bytes 307208 | tf_op jit(solution)/shard_map/ppermute | solution.py:27
  23.9 11.6 %collective-permute-start.4 = (bf16[80,640]{1,0:T(8,128)(2,1)S(1)}, bf16[80,640]{1,0:T(8,128)(2,1)S(1)}, u32[]{:S(2)}, u32[]{:S(2)}) collective-permute-start(bf16[80,640]{1,0:T(8,128)(2,1)S(1)} %get-tuple-element.48), channel_id=1, source_target_pairs={{4,0},{6,2},{0,4},{2,6},{5,1},{7,3},{1,5},{3,7},{12,8},{14,10},{8,... | collective-permute-start | bytes 307208 | tf_op jit(solution)/shard_map/ppermute | solution.py:27
  24.4 11.1 %collective-permute-start.5 = (bf16[80,640]{1,0:T(8,128)(2,1)S(1)}, bf16[80,640]{1,0:T(8,128)(2,1)S(1)}, u32[]{:S(2)}, u32[]{:S(2)}) collective-permute-start(bf16[80,640]{1,0:T(8,128)(2,1)S(1)} %get-tuple-element.49), channel_id=1, source_target_pairs={{6,0},{0,2},{2,4},{4,6},{7,1},{1,3},{3,5},{5,7},{14,8},{8,10},{10,... | collective-permute-start | bytes 307208 | tf_op jit(solution)/shard_map/ppermute | solution.py:27
  24.4 9.7 %collective-permute-start.6 = (s32[1,4,128]{2,1,0:T(4,128)S(1)}, s32[1,4,128]{2,1,0:T(4,128)S(1)}, u32[]{:S(2)}, u32[]{:S(2)}) collective-permute-start(s32[1,4,128]{2,1,0:T(4,128)S(1)} %slice.4), channel_id=1, source_target_pairs={{8,0},{16,8},{24,16},{0,24},{9,1},{17,9},{25,17},{1,25},{10,2},{18... | collective-permute-start | bytes 6152 | tf_op jit(solution)/shard_map/ppermute | solution.py:27
  34.1 12.1 %collective-permute-start.9 = (bf16[128,640]{1,0:T(8,128)(2,1)S(1)}, bf16[128,640]{1,0:T(8,128)(2,1)S(1)}, u32[]{:S(2)}, u32[]{:S(2)}) collective-permute-start(bf16[128,640]{1,0:T(8,128)(2,1)S(1)} %copy-done.3), channel_id=1, source_target_pairs={{16,0},{24,8},{0,16},{8,24},{17,1},{25,9},{1,17},{9,25},{18,2},{26... | collective-permute-start | bytes 491528 | tf_op jit(solution)/shard_map/ppermute | solution.py:27
  36.2 10.0 %collective-permute-start.7 = (bf16[96,640]{1,0:T(8,128)(2,1)S(1)}, bf16[96,640]{1,0:T(8,128)(2,1)S(1)}, u32[]{:S(2)}, u32[]{:S(2)}) collective-permute-start(bf16[96,640]{1,0:T(8,128)(2,1)S(1)} %get-tuple-element.51), channel_id=1, source_target_pairs={{24,0},{0,8},{8,16},{16,24},{25,1},{1,9},{9,17},{17,25},{26,2},{2,... | collective-permute-start | bytes 368648 | tf_op jit(solution)/shard_map/ppermute | solution.py:27
  46.5 33.4 %collective-permute-start.17 = (bf16[128,5120]{1,0:T(8,128)(2,1)S(1)}, bf16[128,5120]{1,0:T(8,128)(2,1)S(1)}, u32[]{:S(2)}, u32[]{:S(2)}) collective-permute-start(bf16[128,5120]{1,0:T(8,128)(2,1)S(1)} %get-tuple-element.65), channel_id=1, source_target_pairs={{8,0},{16,8},{24,16},{0,24},{9,1},{17,9},{25,17},{1,25},{10,2},{18... | collective-permute-start | bytes 3932168 | tf_op jit(solution)/shard_map/ppermute | solution.py:27
  47.7 6.8 %collective-permute-start.10 = (bf16[160,640]{1,0:T(8,128)(2,1)S(1)}, bf16[160,640]{1,0:T(8,128)(2,1)S(1)}, u32[]{:S(2)}, u32[]{:S(2)}) collective-permute-start(bf16[160,640]{1,0:T(8,128)(2,1)S(1)} %get-tuple-element.54.refs_0_), channel_id=1, source_target_pairs={{6,0},{0,2},{2,4},{4,6},{7,1},{1,3},{3,5},{5,7},{14,8},{8,10},{10,... | collective-permute-start | bytes 614408 | tf_op jit(solution)/shard_map/ppermute | solution.py:27
  47.7 7.9 %collective-permute-start.11 = (bf16[160,640]{1,0:T(8,128)(2,1)S(1)}, bf16[160,640]{1,0:T(8,128)(2,1)S(1)}, u32[]{:S(2)}, u32[]{:S(2)}) collective-permute-start(bf16[160,640]{1,0:T(8,128)(2,1)S(1)} %get-tuple-element.54.refs_0_), channel_id=1, source_target_pairs={{4,0},{6,2},{0,4},{2,6},{5,1},{7,3},{1,5},{3,7},{12,8},{14,10},{8,... | collective-permute-start | bytes 614408 | tf_op jit(solution)/shard_map/ppermute | solution.py:27
  49.3 9.3 %collective-permute-start.12 = (bf16[160,640]{1,0:T(8,128)(2,1)S(1)}, bf16[160,640]{1,0:T(8,128)(2,1)S(1)}, u32[]{:S(2)}, u32[]{:S(2)}) collective-permute-start(bf16[160,640]{1,0:T(8,128)(2,1)S(1)} %get-tuple-element.54.refs_0_), channel_id=1, source_target_pairs={{2,0},{4,2},{6,4},{0,6},{3,1},{5,3},{7,5},{1,7},{10,8},{12,10},{14... | collective-permute-start | bytes 614408 | tf_op jit(solution)/shard_map/ppermute | solution.py:27
  65.4 49.8 %collective-permute-start.29 = (bf16[40,17408]{1,0:T(8,128)(2,1)S(1)}, bf16[40,17408]{1,0:T(8,128)(2,1)S(1)}, u32[]{:S(2)}, u32[]{:S(2)}) collective-permute-start(bf16[40,17408]{1,0:T(8,128)(2,1)S(1)} %get-tuple-element.75.act.refs_0_.refs_2_.refs_4_.refs_6_), channel_id=1, source_target_pairs={{1,0},{0,1},{3,2},{2,3},{5,4},{4,5},{7,6},{6,7},{9,8},{8,9},{11,10... | collective-permute-start | bytes 4177928 | tf_op jit(solution)/shard_map/ppermute | solution.py:27
  66.9 4.8 %collective-permute-start.13 = (bf16[80,640]{1,0:T(8,128)(2,1)S(1)}, bf16[80,640]{1,0:T(8,128)(2,1)S(1)}, u32[]{:S(2)}, u32[]{:S(2)}) collective-permute-start(bf16[80,640]{1,0:T(8,128)(2,1)S(1)} %get-tuple-element.61), channel_id=1, source_target_pairs={{2,0},{4,2},{6,4},{0,6},{3,1},{5,3},{7,5},{1,7},{10,8},{12,10},{14... | collective-permute-start | bytes 307208 | tf_op jit(solution)/shard_map/ppermute | solution.py:27
  68.9 5.9 %collective-permute-start.14 = (bf16[80,640]{1,0:T(8,128)(2,1)S(1)}, bf16[80,640]{1,0:T(8,128)(2,1)S(1)}, u32[]{:S(2)}, u32[]{:S(2)}) collective-permute-start(bf16[80,640]{1,0:T(8,128)(2,1)S(1)} %get-tuple-element.62), channel_id=1, source_target_pairs={{4,0},{6,2},{0,4},{2,6},{5,1},{7,3},{1,5},{3,7},{12,8},{14,10},{8,... | collective-permute-start | bytes 307208 | tf_op jit(solution)/shard_map/ppermute | solution.py:27
  69.4 5.4 %collective-permute-start.15 = (bf16[80,640]{1,0:T(8,128)(2,1)S(1)}, bf16[80,640]{1,0:T(8,128)(2,1)S(1)}, u32[]{:S(2)}, u32[]{:S(2)}) collective-permute-start(bf16[80,640]{1,0:T(8,128)(2,1)S(1)} %get-tuple-element.63), channel_id=1, source_target_pairs={{6,0},{0,2},{2,4},{4,6},{7,1},{1,3},{3,5},{5,7},{14,8},{8,10},{10,... | collective-permute-start | bytes 307208 | tf_op jit(solution)/shard_map/ppermute | solution.py:27
  75.2 4.7 %collective-permute-start.16 = (bf16[80,640]{1,0:T(8,128)(2,1)S(1)}, bf16[80,640]{1,0:T(8,128)(2,1)S(1)}, u32[]{:S(2)}, u32[]{:S(2)}) collective-permute-start(bf16[80,640]{1,0:T(8,128)(2,1)S(1)} %shard_map.116), channel_id=1, source_target_pairs={{8,0},{16,8},{24,16},{0,24},{9,1},{17,9},{25,17},{1,25},{10,2},{18... | collective-permute-start | bytes 307208 | tf_op jit(solution)/shard_map/ppermute | solution.py:27
  79.9 53.9 %collective-permute-start.24 = (bf16[912,640]{1,0:T(8,128)(2,1)S(1)}, bf16[912,640]{1,0:T(8,128)(2,1)S(1)}, u32[]{:S(2)}, u32[]{:S(2)}) collective-permute-start(bf16[912,640]{1,0:T(8,128)(2,1)S(1)} %shard_map.118._), channel_id=1, source_target_pairs={{16,0},{24,8},{0,16},{8,24},{17,1},{25,9},{1,17},{9,25},{18,2},{26... | collective-permute-start | bytes 3502088 | tf_op jit(solution)/shard_map/ppermute | solution.py:27
  81.7 4.6 %collective-permute-start.18 = (bf16[80,640]{1,0:T(8,128)(2,1)S(1)}, bf16[80,640]{1,0:T(8,128)(2,1)S(1)}, u32[]{:S(2)}, u32[]{:S(2)}) collective-permute-start(bf16[80,640]{1,0:T(8,128)(2,1)S(1)} %get-tuple-element.67.refs_0_), channel_id=1, source_target_pairs={{6,0},{0,2},{2,4},{4,6},{7,1},{1,3},{3,5},{5,7},{14,8},{8,10},{10,... | collective-permute-start | bytes 307208 | tf_op jit(solution)/shard_map/ppermute | solution.py:27
  81.8 5.8 %collective-permute-start.19 = (bf16[80,640]{1,0:T(8,128)(2,1)S(1)}, bf16[80,640]{1,0:T(8,128)(2,1)S(1)}, u32[]{:S(2)}, u32[]{:S(2)}) collective-permute-start(bf16[80,640]{1,0:T(8,128)(2,1)S(1)} %get-tuple-element.67.refs_0_), channel_id=1, source_target_pairs={{4,0},{6,2},{0,4},{2,6},{5,1},{7,3},{1,5},{3,7},{12,8},{14,10},{8,... | collective-permute-start | bytes 307208 | tf_op jit(solution)/shard_map/ppermute | solution.py:27
  83.4 4.8 %collective-permute-start.20 = (bf16[80,640]{1,0:T(8,128)(2,1)S(1)}, bf16[80,640]{1,0:T(8,128)(2,1)S(1)}, u32[]{:S(2)}, u32[]{:S(2)}) collective-permute-start(bf16[80,640]{1,0:T(8,128)(2,1)S(1)} %get-tuple-element.67.refs_0_), channel_id=1, source_target_pairs={{2,0},{4,2},{6,4},{0,6},{3,1},{5,3},{7,5},{1,7},{10,8},{12,10},{14... | collective-permute-start | bytes 307208 | tf_op jit(solution)/shard_map/ppermute | solution.py:27
  93.3 24.8 %collective-permute-start.30 = (bf16[40,6144]{1,0:T(8,128)(2,1)S(1)}, bf16[40,6144]{1,0:T(8,128)(2,1)S(1)}, u32[]{:S(2)}, u32[]{:S(2)}) collective-permute-start(bf16[40,6144]{1,0:T(8,128)(2,1)S(1)} %get-tuple-element.76._.refs_0_.refs_2_), channel_id=1, source_target_pairs={{1,0},{0,1},{3,2},{2,3},{5,4},{4,5},{7,6},{6,7},{9,8},{8,9},{11,10... | collective-permute-start | bytes 1474568 | tf_op jit(solution)/shard_map/ppermute | solution.py:27
  94.8 4.2 %collective-permute-start.21 = (bf16[80,640]{1,0:T(8,128)(2,1)S(1)}, bf16[80,640]{1,0:T(8,128)(2,1)S(1)}, u32[]{:S(2)}, u32[]{:S(2)}) collective-permute-start(bf16[80,640]{1,0:T(8,128)(2,1)S(1)} %get-tuple-element.71), channel_id=1, source_target_pairs={{2,0},{4,2},{6,4},{0,6},{3,1},{5,3},{7,5},{1,7},{10,8},{12,10},{14... | collective-permute-start | bytes 307208 | tf_op jit(solution)/shard_map/ppermute | solution.py:27
  97.8 2.3 %collective-permute-start.25 = (bf16[80,640]{1,0:T(8,128)(2,1)S(1)}, bf16[80,640]{1,0:T(8,128)(2,1)S(1)}, u32[]{:S(2)}, u32[]{:S(2)}) collective-permute-start(bf16[80,640]{1,0:T(8,128)(2,1)S(1)} %get-tuple-element.78), channel_id=1, source_target_pairs={{2,0},{4,2},{6,4},{0,6},{3,1},{5,3},{7,5},{1,7},{10,8},{12,10},{14... | collective-permute-start | bytes 307208 | tf_op jit(solution)/shard_map/ppermute | solution.py:27
  99.0 5.7 %collective-permute-start.26 = (bf16[80,640]{1,0:T(8,128)(2,1)S(1)}, bf16[80,640]{1,0:T(8,128)(2,1)S(1)}, u32[]{:S(2)}, u32[]{:S(2)}) collective-permute-start(bf16[80,640]{1,0:T(8,128)(2,1)S(1)} %get-tuple-element.79), channel_id=1, source_target_pairs={{4,0},{6,2},{0,4},{2,6},{5,1},{7,3},{1,5},{3,7},{12,8},{14,10},{8,... | collective-permute-start | bytes 307208 | tf_op jit(solution)/shard_map/ppermute | solution.py:27
  100.2 5.7 %collective-permute-start.27 = (bf16[80,640]{1,0:T(8,128)(2,1)S(1)}, bf16[80,640]{1,0:T(8,128)(2,1)S(1)}, u32[]{:S(2)}, u32[]{:S(2)}) collective-permute-start(bf16[80,640]{1,0:T(8,128)(2,1)S(1)} %get-tuple-element.80), channel_id=1, source_target_pairs={{6,0},{0,2},{2,4},{4,6},{7,1},{1,3},{3,5},{5,7},{14,8},{8,10},{10,... | collective-permute-start | bytes 307208 | tf_op jit(solution)/shard_map/ppermute | solution.py:27
  104.7 5.7 %collective-permute-start.22 = (bf16[80,640]{1,0:T(8,128)(2,1)S(1)}, bf16[80,640]{1,0:T(8,128)(2,1)S(1)}, u32[]{:S(2)}, u32[]{:S(2)}) collective-permute-start(bf16[80,640]{1,0:T(8,128)(2,1)S(1)} %get-tuple-element.72), channel_id=1, source_target_pairs={{4,0},{6,2},{0,4},{2,6},{5,1},{7,3},{1,5},{3,7},{12,8},{14,10},{8,... | collective-permute-start | bytes 307208 | tf_op jit(solution)/shard_map/ppermute | solution.py:27
  105.9 6.9 %collective-permute-start.23 = (bf16[80,640]{1,0:T(8,128)(2,1)S(1)}, bf16[80,640]{1,0:T(8,128)(2,1)S(1)}, u32[]{:S(2)}, u32[]{:S(2)}) collective-permute-start(bf16[80,640]{1,0:T(8,128)(2,1)S(1)} %get-tuple-element.73), channel_id=1, source_target_pairs={{6,0},{0,2},{2,4},{4,6},{7,1},{1,3},{3,5},{5,7},{14,8},{8,10},{10,... | collective-permute-start | bytes 307208 | tf_op jit(solution)/shard_map/ppermute | solution.py:27
  110.4 17.9 %collective-permute-start.28 = (bf16[80,640]{1,0:T(8,128)(2,1)S(1)}, bf16[80,640]{1,0:T(8,128)(2,1)S(1)}, u32[]{:S(2)}, u32[]{:S(2)}) collective-permute-start(bf16[80,640]{1,0:T(8,128)(2,1)S(1)} %shard_map.123), channel_id=1, source_target_pairs={{24,0},{0,8},{8,16},{16,24},{25,1},{1,9},{9,17},{17,25},{26,2},{2,... | collective-permute-start | bytes 307208 | tf_op jit(solution)/shard_map/ppermute | solution.py:27

commit v12 on v11

--- a/solution.py
+++ b/solution.py
@@ -172,15 +172,11 @@
     weight = slot_gates(select, routes[0], gates[0])
     fresh = (raw[...].astype(F32) + weight * summed(parts)).astype(BF16)
     old = pick(select_next, whole_block(tokens))
-    onward[:PACKED] = merged(select_next, select, fresh, old)
-    names = routes[1].astype(F32)
-    names = jnp.concatenate([names, jnp.full((TAIL - names.shape[0], names.shape[1]), 1.0)], 0)
-    onward[PACKED:] = jnp.zeros((TAIL, onward.shape[1]), BF16)
-    onward[PACKED:, : names.shape[1]] = names.astype(BF16)
+    onward[...] = merged(select_next, select, fresh, old)
     upd[...] = fresh
 
 
-def merge_kernel(tokens, upd, routes, out, last):
+def merge_kernel(tokens, upd, routes, next_routes, out, last):
     select = select_of(routes[0])
     hit = hit_rows(select)
     height, width = tokens.shape
@@ -189,7 +185,8 @@
         out[(c - EARLY) * height : (c - EARLY + 1) * height] = value
     last[...] = jnp.zeros(last.shape, F32)
     last[:CAP] = upd[...].astype(F32)[:CAP]
-    last[CAP : CAP + routes.shape[1], :height] = routes[0].astype(F32)
+    last[CAP : CAP + TOP, :height] = routes[0].astype(F32)
+    last[CAP : CAP + TOP, height : 2 * height] = next_routes[0].astype(F32)
     out[(PACK - EARLY) * height :] = last[...].astype(BF16)
 
 
@@ -208,11 +205,11 @@
     parts, (h, routes, gates, upd) = refs[:n], refs[n:]
     select = select_of(routes[1])
     weight = slot_gates(select, routes[1], gates[1])
-    upd[...] = (h[:PACKED].astype(F32) + weight * summed(parts)).astype(BF16)
+    upd[...] = (h[...].astype(F32) + weight * summed(parts)).astype(BF16)
 
 
 def enter1_kernel(h, scaled, _, __, out, ___):
-    values = h[:PACKED].astype(F32)
+    values = h[...].astype(F32)
     out[:PACKED] = (values * inv_rms_of(values)).astype(BF16)
     out[PACKED:] = scaled[...]
 
@@ -227,7 +224,7 @@
 
 def grad1_kernel(n, *refs):
     parts, (h, cot, upd) = refs[:n], refs[n:]
-    upd[...] = state_grad(parts, h[:PACKED], cot[...])
+    upd[...] = state_grad(parts, h[...], cot[...])
 
 
 def enter0_kernel(upd1, next_routes, routes, gates, bulk, _, c0, out):
@@ -249,22 +246,31 @@
         out[:, k] = placed(chunk, value, second, hit2, fresh)
 
 
-def finish_state_kernel(early, rest, upd1, h, out, outs, last, sems):
+def finish_state_kernel(early, rest, upd1, out, outs, last, sems):
     height, width = out.shape
     at = (PACK - EARLY) * height
     last[...] = rest[at:].astype(F32)
     first = select_of(last[CAP : CAP + TOP, :height])
-    second = select_of(h[PACKED:].astype(F32)[:TOP, :height])
+    second = select_of(last[CAP : CAP + TOP, height : 2 * height])
     hit1, hit2 = hit_rows(first), hit_rows(second)
     rows = jnp.concatenate([last[...], jnp.zeros((PACKED - TAIL, last.shape[1]), F32)], axis=0)
-    for c in range(PACK):
-        if c < EARLY:
-            value = placed(c, early[...], first, hit1, rows.astype(BF16))
-        else:
-            value = rest[(c - EARLY) * height : (c - EARLY + 1) * height]
-        outs[:, columns(c, width)] = placed(c, value, second, hit2, upd1[...])
-    for store in start_rows(outs, out, sems):
-        store.wait()
+    rows1, rows2 = rows.astype(BF16), upd1[...]
+    copies = []
+    for r0 in range(0, height, height // 2):
+        r = slice(r0, r0 + height // 2)
+        for c in range(PACK):
+            if c < EARLY:
+                value = placed(c, early[r], first[:, r], hit1[r], rows1)
+            else:
+                start = (c - EARLY) * height + r0
+                value = rest[start : start + height // 2]
+            outs[r, columns(c, width)] = placed(c, value, second[:, r], hit2[r], rows2)
+        for i in range(r0 // 16, r.stop // 16):
+            b = pl.ds(16 * i, 16)
+            copies.append(pltpu.make_async_copy(outs.at[b], out.at[b], sems.at[i]))
+            copies[-1].start()
+    for copy in copies:
+        copy.wait()
 
 
 def silu_grads(pre_gate, pre_up, grad_act):
@@ -562,14 +568,14 @@
     parts = to_group(parts)
     upd0, h1 = call(
         part(update0_kernel, n),
-        [one, ((PACKED + TAIL, step), BF16)],
+        [one, one],
         [*parts, raw0, routes, gates, tokens, next_routes],
     )
     h1 = shifted(h1, "section", 1)
     (rest,) = call(
         merge_kernel,
         [(((PACK - EARLY) * tokens.shape[0] + TAIL, step), BF16)],
-        [tokens, upd0, routes],
+        [tokens, upd0, routes, next_routes],
         scratch=[pltpu.VMEM((TAIL, step), F32)],
     )
     cot1, scaled1 = call(grad_rows_kernel, [one, one], [cot1_all, routes, gates])
@@ -644,7 +650,7 @@
     (state,) = call(
         finish_state_kernel,
         [(tokens.shape, BF16)],
-        [early, rest, last1, h1],
+        [early, rest, last1],
         any_outs=(0,),
         scratch=[
             pltpu.VMEM(tokens.shape, BF16),

time: 136 us -> 136 us (level)
  no operation moved by 1% of the time
where the time goes in v12:
time: 136 us
  waiting for transfers between devices  53.4 us (39%)
  Pallas kernels  43.6 us (32%)
  starting transfers between devices  37.7 us (28%)
    ppermute x31, waiting for transfers between devices, shifted(): lax.ppermute(block, axis, [((i - distance) % size, i) for i in range(size)])  53.4 us
    ppermute x31, starting transfers between devices, shifted(): lax.ppermute(block, axis, [((i - distance) % size, i) for i in range(size)])  37.7 us
    pallas_call x15, Pallas kernels, call(): pl.pallas_call(kernel, out_shape=outs, in_specs=[anywhere if i in any_arg...  30.5 us
    pallas_call x3, Pallas kernels, chunked_call(): pl.pallas_call(kernel, grid=(steps,), out_shape=[jax.ShapeDtypeStruct(s,...  13.1 us
  transfers between devices with their start and end apart: 31, of which 20 were waited for; matrix products, arithmetic and copies ran while one was open for 0% of the time, Pallas kernels for 30%

profile of v12, /device:TPU:0, one launch (start us, length us, event | category | flops | bytes accessed | tf_op | source)
XLA Modules:
  0.0 135.7 jit_solution(12481590538035597701)
XLA Ops:
  0.6 5.1 %collective-permute-start.8 = (bf16[128,5120]{1,0:T(8,128)(2,1)}, bf16[128,5120]{1,0:T(8,128)(2,1)S(1)}, u32[]{:S(2)}, u32[]{:S(2)}) collective-permute-start(bf16[128,5120]{1,0:T(8,128)(2,1)} %param.8), channel_id=1, source_target_pairs={{8,0},{16,8},{24,16},{0,24},{9,1},{17,9},{25,17},{1,25},{10,2},{18... | collective-permute-start | bytes 3932168 | tf_op jit(solution)/shard_map/ppermute | solution.py:27
  5.7 2.9 %shard_map.110 = (bf16[80,640]{1,0:T(8,128)(2,1)S(1)}, bf16[80,640]{1,0:T(8,128)(2,1)S(1)}, bf16[128,640]{1,0:T(8,128)(2,1)}) custom-call(bf16[128,5120]{1,0:T(8,128)(2,1)} %tokens.3, s32[2,4,128]{2,1,0:T(4,128)} %bitcast.8), custom_call_target="tpu_custom_call" | custom-call | bytes 1024 | tf_op jit(solution)/shard_map/pallas_call | solution.py:40
  8.6 0.1 collective-permute-start
  8.7 1.6 %collective-permute-start.1 = (bf16[80,640]{1,0:T(8,128)(2,1)S(1)}, bf16[80,640]{1,0:T(8,128)(2,1)S(1)}, u32[]{:S(2)}, u32[]{:S(2)}) collective-permute-start(bf16[80,640]{1,0:T(8,128)(2,1)S(1)} %get-tuple-element.45.refs_0_), channel_id=1, source_target_pairs={{4,0},{6,2},{0,4},{2,6},{5,1},{7,3},{1,5},{3,7},{12,8},{14,10},{8,... | collective-permute-start | bytes 307208 | tf_op jit(solution)/shard_map/ppermute | solution.py:27
  10.2 1.4 %collective-permute-start.2 = (bf16[80,640]{1,0:T(8,128)(2,1)S(1)}, bf16[80,640]{1,0:T(8,128)(2,1)S(1)}, u32[]{:S(2)}, u32[]{:S(2)}) collective-permute-start(bf16[80,640]{1,0:T(8,128)(2,1)S(1)} %get-tuple-element.45.refs_0_), channel_id=1, source_target_pairs={{2,0},{4,2},{6,4},{0,6},{3,1},{5,3},{7,5},{1,7},{10,8},{12,10},{14... | collective-permute-start | bytes 307208 | tf_op jit(solution)/shard_map/ppermute | solution.py:27
  11.6 1.6 %collective-permute-done.refs_1_ = bf16[80,640]{1,0:T(8,128)(2,1)S(1)} collective-permute-done((bf16[80,640]{1,0:T(8,128)(2,1)S(1)}, bf16[80,640]{1,0:T(8,128)(2,1)S(1)}, u32[]{:S(2)}, u32[]{:S(2)}) %collective-permute-start) | collective-permute-done | bytes 102432 | tf_op jit(solution)/shard_map/ppermute | solution.py:27
  13.2 1.2 collective-permute-done.1.refs_2_
  14.4 0.6 collective-permute-done.2.refs_3_
  15.1 6.5 %shard_map.111 = (bf16[40,5120]{1,0:T(8,128)(2,1)S(1)}, f32[40,512]{1,0:T(8,128)S(1)}, f32[40,512]{1,0:T(8,128)S(1)}, bf16[40,512]{1,0:T(8,128)(2,1)S(1)}, bf16[...) custom-call(bf16[80,640]{1,0:T(8,128)(2,1)S(1)} %get-tuple-element.4, ...), custom_call_target="tpu_custom_call" | custom-call | bytes 1024 | tf_op jit(solution)/shard_map/pallas_call | solution.py:40
  21.6 2.3 %collective-permute-start.3 = (bf16[80,640]{1,0:T(8,128)(2,1)S(1)}, bf16[80,640]{1,0:T(8,128)(2,1)S(1)}, u32[]{:S(2)}, u32[]{:S(2)}) collective-permute-start(bf16[80,640]{1,0:T(8,128)(2,1)S(1)} %get-tuple-element.47), channel_id=1, source_target_pairs={{2,0},{4,2},{6,4},{0,6},{3,1},{5,3},{7,5},{1,7},{10,8},{12,10},{14... | collective-permute-start | bytes 307208 | tf_op jit(solution)/shard_map/ppermute | solution.py:27
  23.9 0.5 collective-permute-start.4
  24.4 0.5 collective-permute-start.6
  24.9 9.2 %collective-permute-done.6.refs_8_.next_routes = s32[1,4,128]{2,1,0:T(4,128)S(1)} collective-permute-done((s32[1,4,128]{2,1,0:T(4,128)S(1)}, s32[1,4,128]{2,1,0:T(4,128)S(1)}, u32[]{:S(2)}, u32[]{:S(2)}) %collective-permute-start.6) | collective-permute-done | bytes 2080 | tf_op jit(solution)/shard_map/ppermute | solution.py:27
  34.1 1.4 %collective-permute-start.9 = (bf16[128,640]{1,0:T(8,128)(2,1)S(1)}, bf16[128,640]{1,0:T(8,128)(2,1)S(1)}, u32[]{:S(2)}, u32[]{:S(2)}) collective-permute-start(bf16[128,640]{1,0:T(8,128)(2,1)S(1)} %copy-done.3), channel_id=1, source_target_pairs={{16,0},{24,8},{0,16},{8,24},{17,1},{25,9},{1,17},{9,25},{18,2},{26... | collective-permute-start | bytes 491528 | tf_op jit(solution)/shard_map/ppermute | solution.py:27
  35.5 0.0 collective-permute-done.3.refs_1_
  35.5 0.7 shard_map.112
  36.2 3.4 %collective-permute-start.7 = (bf16[80,640]{1,0:T(8,128)(2,1)S(1)}, bf16[80,640]{1,0:T(8,128)(2,1)S(1)}, u32[]{:S(2)}, u32[]{:S(2)}) collective-permute-start(bf16[80,640]{1,0:T(8,128)(2,1)S(1)} %get-tuple-element.51), channel_id=1, source_target_pairs={{24,0},{0,8},{8,16},{16,24},{25,1},{1,9},{9,17},{17,25},{26,2},{2,... | collective-permute-start | bytes 307208 | tf_op jit(solution)/shard_map/ppermute | solution.py:27
  39.7 0.5 shard_map.113
  40.2 5.5 %collective-permute-done.9.__.early = bf16[128,640]{1,0:T(8,128)(2,1)S(1)} collective-permute-done((bf16[128,640]{1,0:T(8,128)(2,1)S(1)}, bf16[128,640]{1,0:T(8,128)(2,1)S(1)}, u32[]{:S(2)}, u32[]{:S(2)}) %collective-permute-start.9) | collective-permute-done | bytes 163872 | tf_op jit(solution)/shard_map/ppermute | solution.py:27
  45.8 0.3 shard_map.114
  46.1 1.4 %collective-permute-start.17 = (bf16[128,5120]{1,0:T(8,128)(2,1)S(1)}, bf16[128,5120]{1,0:T(8,128)(2,1)S(1)}, u32[]{:S(2)}, u32[]{:S(2)}) collective-permute-start(bf16[128,5120]{1,0:T(8,128)(2,1)S(1)} %get-tuple-element.65), channel_id=1, source_target_pairs={{8,0},{16,8},{24,16},{0,24},{9,1},{17,9},{25,17},{1,25},{10,2},{18... | collective-permute-start | bytes 3932168 | tf_op jit(solution)/shard_map/ppermute | solution.py:27
  47.5 1.6 %collective-permute-start.11 = (bf16[160,640]{1,0:T(8,128)(2,1)S(1)}, bf16[160,640]{1,0:T(8,128)(2,1)S(1)}, u32[]{:S(2)}, u32[]{:S(2)}) collective-permute-start(bf16[160,640]{1,0:T(8,128)(2,1)S(1)} %get-tuple-element.54.refs_0_), channel_id=1, source_target_pairs={{4,0},{6,2},{0,4},{2,6},{5,1},{7,3},{1,5},{3,7},{12,8},{14,10},{8,... | collective-permute-start | bytes 614408 | tf_op jit(solution)/shard_map/ppermute | solution.py:27
  49.0 1.4 %collective-permute-start.12 = (bf16[160,640]{1,0:T(8,128)(2,1)S(1)}, bf16[160,640]{1,0:T(8,128)(2,1)S(1)}, u32[]{:S(2)}, u32[]{:S(2)}) collective-permute-start(bf16[160,640]{1,0:T(8,128)(2,1)S(1)} %get-tuple-element.54.refs_0_), channel_id=1, source_target_pairs={{2,0},{4,2},{6,4},{0,6},{3,1},{5,3},{7,5},{1,7},{10,8},{12,10},{14... | collective-permute-start | bytes 614408 | tf_op jit(solution)/shard_map/ppermute | solution.py:27
  50.5 3.8 %collective-permute-done.10.refs_1_ = bf16[160,640]{1,0:T(8,128)(2,1)S(1)} collective-permute-done((bf16[160,640]{1,0:T(8,128)(2,1)S(1)}, bf16[160,640]{1,0:T(8,128)(2,1)S(1)}, u32[]{:S(2)}, u32[]{:S(2)}) %collective-permute-start.10) | collective-permute-done | bytes 204832 | tf_op jit(solution)/shard_map/ppermute | solution.py:27
  54.3 1.1 collective-permute-done.11.refs_2_
  55.4 2.9 %collective-permute-done.12.refs_3_ = bf16[160,640]{1,0:T(8,128)(2,1)S(1)} collective-permute-done((bf16[160,640]{1,0:T(8,128)(2,1)S(1)}, bf16[160,640]{1,0:T(8,128)(2,1)S(1)}, u32[]{:S(2)}, u32[]{:S(2)}) %collective-permute-start.12) | collective-permute-done | bytes 204832 | tf_op jit(solution)/shard_map/ppermute | solution.py:27
  58.3 6.8 %shard_map.115 = (bf16[40,17408]{1,0:T(8,128)(2,1)S(1)}, bf16[80,640]{1,0:T(8,128)(2,1)S(1)}, bf16[80,640]{1,0:T(8,128)(2,1)S(1)}, bf16[80,640]{1,0:T(8,128)(2,1)S(1)}, bf16[80,640]{1,0:T(8,128)(2,1)S(1)}) custom-call(bf16[160,640]{1,0:T(8,128)(2,1)S(1)} %get-tuple-element.54.refs_0_, bf16[160,640]{1,0:T(8,128)(2,1)S(1)} %collective-permute-done.10.refs_1_, ...), custom_call_target="tpu_custom_call" | custom-call | bytes 1024 | tf_op jit(solution)/shard_map/pallas_call | solution.py:40
  65.2 1.6 %collective-permute-start.29 = (bf16[40,17408]{1,0:T(8,128)(2,1)S(1)}, bf16[40,17408]{1,0:T(8,128)(2,1)S(1)}, u32[]{:S(2)}, u32[]{:S(2)}) collective-permute-start(bf16[40,17408]{1,0:T(8,128)(2,1)S(1)} %get-tuple-element.75.act.refs_0_.refs_2_.refs_4_.refs_6_), channel_id=1, source_target_pairs={{1,0},{0,1},{3,2},{2,3},{5,4},{4,5},{7,6},{6,7},{9,8},{8,9},{11,10... | collective-permute-start | bytes 4177928 | tf_op jit(solution)/shard_map/ppermute | solution.py:27
  66.7 1.9 %collective-permute-start.13 = (bf16[80,640]{1,0:T(8,128)(2,1)S(1)}, bf16[80,640]{1,0:T(8,128)(2,1)S(1)}, u32[]{:S(2)}, u32[]{:S(2)}) collective-permute-start(bf16[80,640]{1,0:T(8,128)(2,1)S(1)} %get-tuple-element.61), channel_id=1, source_target_pairs={{2,0},{4,2},{6,4},{0,6},{3,1},{5,3},{7,5},{1,7},{10,8},{12,10},{14... | collective-permute-start | bytes 307208 | tf_op jit(solution)/shard_map/ppermute | solution.py:27
  68.6 0.5 collective-permute-start.14
  69.1 2.4 %collective-permute-done.13.refs_1_ = bf16[80,640]{1,0:T(8,128)(2,1)S(1)} collective-permute-done((bf16[80,640]{1,0:T(8,128)(2,1)S(1)}, bf16[80,640]{1,0:T(8,128)(2,1)S(1)}, u32[]{:S(2)}, u32[]{:S(2)}) %collective-permute-start.13) | collective-permute-done | bytes 102432 | tf_op jit(solution)/shard_map/ppermute | solution.py:27
  71.5 3.0 %collective-permute-done.14.refs_2_ = bf16[80,640]{1,0:T(8,128)(2,1)S(1)} collective-permute-done((bf16[80,640]{1,0:T(8,128)(2,1)S(1)}, bf16[80,640]{1,0:T(8,128)(2,1)S(1)}, u32[]{:S(2)}, u32[]{:S(2)}) %collective-permute-start.14) | collective-permute-done | bytes 102432 | tf_op jit(solution)/shard_map/ppermute | solution.py:27
  74.5 0.4 shard_map.116
  75.0 1.8 %collective-permute-start.16 = (bf16[80,640]{1,0:T(8,128)(2,1)S(1)}, bf16[80,640]{1,0:T(8,128)(2,1)S(1)}, u32[]{:S(2)}, u32[]{:S(2)}) collective-permute-start(bf16[80,640]{1,0:T(8,128)(2,1)S(1)} %shard_map.116), channel_id=1, source_target_pairs={{8,0},{16,8},{24,16},{0,24},{9,1},{17,9},{25,17},{1,25},{10,2},{18... | collective-permute-start | bytes 307208 | tf_op jit(solution)/shard_map/ppermute | solution.py:27
  76.8 0.7 shard_map.117.__0_
  77.5 2.2 %collective-permute-done.16.__2_.upd1.refs_7_ = bf16[80,640]{1,0:T(8,128)(2,1)S(1)} collective-permute-done((bf16[80,640]{1,0:T(8,128)(2,1)S(1)}, bf16[80,640]{1,0:T(8,128)(2,1)S(1)}, u32[]{:S(2)}, u32[]{:S(2)}) %collective-permute-start.16) | collective-permute-done | bytes 102432 | tf_op jit(solution)/shard_map/ppermute | solution.py:27
  79.7 0.8 collective-permute-start.24
  80.5 0.8 shard_map.119
  81.3 0.1 collective-permute-start.18
  81.4 1.6 %collective-permute-start.19 = (bf16[80,640]{1,0:T(8,128)(2,1)S(1)}, bf16[80,640]{1,0:T(8,128)(2,1)S(1)}, u32[]{:S(2)}, u32[]{:S(2)}) collective-permute-start(bf16[80,640]{1,0:T(8,128)(2,1)S(1)} %get-tuple-element.67.refs_0_), channel_id=1, source_target_pairs={{4,0},{6,2},{0,4},{2,6},{5,1},{7,3},{1,5},{3,7},{12,8},{14,10},{8,... | collective-permute-start | bytes 307208 | tf_op jit(solution)/shard_map/ppermute | solution.py:27
  83.0 1.4 %collective-permute-start.20 = (bf16[80,640]{1,0:T(8,128)(2,1)S(1)}, bf16[80,640]{1,0:T(8,128)(2,1)S(1)}, u32[]{:S(2)}, u32[]{:S(2)}) collective-permute-start(bf16[80,640]{1,0:T(8,128)(2,1)S(1)} %get-tuple-element.67.refs_0_), channel_id=1, source_target_pairs={{2,0},{4,2},{6,4},{0,6},{3,1},{5,3},{7,5},{1,7},{10,8},{12,10},{14... | collective-permute-start | bytes 307208 | tf_op jit(solution)/shard_map/ppermute | solution.py:27
  84.3 1.6 %collective-permute-done.18.refs_1_ = bf16[80,640]{1,0:T(8,128)(2,1)S(1)} collective-permute-done((bf16[80,640]{1,0:T(8,128)(2,1)S(1)}, bf16[80,640]{1,0:T(8,128)(2,1)S(1)}, u32[]{:S(2)}, u32[]{:S(2)}) %collective-permute-start.18) | collective-permute-done | bytes 102432 | tf_op jit(solution)/shard_map/ppermute | solution.py:27
  85.9 1.2 collective-permute-done.19.refs_2_
  87.1 0.6 collective-permute-done.20.refs_3_
  87.8 5.1 %shard_map.120 = (bf16[40,6144]{1,0:T(8,128)(2,1)S(1)}, bf16[80,640]{1,0:T(8,128)(2,1)S(1)}, bf16[80,640]{1,0:T(8,128)(2,1)S(1)}, bf16[80,640]{1,0:T(8,128)(2,1)S(1)}, bf16[80,640]{1,0:T(8,128)(2,1)S(1)}) custom-call(bf16[80,640]{1,0:T(8,128)(2,1)S(1)} %get-tuple-element.67.refs_0_, bf16[80,640]{1,0:T(8,128)(2,1)S(1)} %collective-permute-done.18.refs_1_, ...), custom_call_target="tpu_custom_call" | custom-call | bytes 1024 | tf_op jit(solution)/shard_map/pallas_call | solution.py:40
  92.8 1.6 %collective-permute-start.30 = (bf16[40,6144]{1,0:T(8,128)(2,1)S(1)}, bf16[40,6144]{1,0:T(8,128)(2,1)S(1)}, u32[]{:S(2)}, u32[]{:S(2)}) collective-permute-start(bf16[40,6144]{1,0:T(8,128)(2,1)S(1)} %get-tuple-element.76._.refs_0_.refs_2_), channel_id=1, source_target_pairs={{1,0},{0,1},{3,2},{2,3},{5,4},{4,5},{7,6},{6,7},{9,8},{8,9},{11,10... | collective-permute-start | bytes 1474568 | tf_op jit(solution)/shard_map/ppermute | solution.py:27
  94.4 1.9 %collective-permute-start.21 = (bf16[80,640]{1,0:T(8,128)(2,1)S(1)}, bf16[80,640]{1,0:T(8,128)(2,1)S(1)}, u32[]{:S(2)}, u32[]{:S(2)}) collective-permute-start(bf16[80,640]{1,0:T(8,128)(2,1)S(1)} %get-tuple-element.71), channel_id=1, source_target_pairs={{2,0},{4,2},{6,4},{0,6},{3,1},{5,3},{7,5},{1,7},{10,8},{12,10},{14... | collective-permute-start | bytes 307208 | tf_op jit(solution)/shard_map/ppermute | solution.py:27
  96.3 1.1 shard_map.122
  97.4 0.1 collective-permute-start.25
  97.5 1.1 collective-permute-done.21.refs_1_
  98.6 0.5 collective-permute-start.26
  99.1 0.6 collective-permute-done.25.refs_1_
  99.7 1.1 collective-permute-start.27
  100.8 3.5 %collective-permute-done.26.refs_2_ = bf16[80,640]{1,0:T(8,128)(2,1)S(1)} collective-permute-done((bf16[80,640]{1,0:T(8,128)(2,1)S(1)}, bf16[80,640]{1,0:T(8,128)(2,1)S(1)}, u32[]{:S(2)}, u32[]{:S(2)}) %collective-permute-start.26) | collective-permute-done | bytes 102432 | tf_op jit(solution)/shard_map/ppermute | solution.py:27
  104.3 1.1 collective-permute-done.27.refs_3_
  105.4 0.2 shard_map.123
  105.7 4.3 %collective-permute-done.22.refs_2_ = bf16[80,640]{1,0:T(8,128)(2,1)S(1)} collective-permute-done((bf16[80,640]{1,0:T(8,128)(2,1)S(1)}, bf16[80,640]{1,0:T(8,128)(2,1)S(1)}, u32[]{:S(2)}, u32[]{:S(2)}) %collective-permute-start.22) | collective-permute-done | bytes 102432 | tf_op jit(solution)/shard_map/ppermute | solution.py:27
  110.0 2.3 %collective-permute-start.28 = (bf16[80,640]{1,0:T(8,128)(2,1)S(1)}, bf16[80,640]{1,0:T(8,128)(2,1)S(1)}, u32[]{:S(2)}, u32[]{:S(2)}) collective-permute-start(bf16[80,640]{1,0:T(8,128)(2,1)S(1)} %shard_map.123), channel_id=1, source_target_pairs={{24,0},{0,8},{8,16},{16,24},{25,1},{1,9},{9,17},{17,25},{26,2},{2,... | collective-permute-start | bytes 307208 | tf_op jit(solution)/shard_map/ppermute | solution.py:27
  112.3 2.4 %shard_map.121 = bf16[128,5120]{1,0:T(8,128)(2,1)} custom-call(bf16[80,640]{1,0:T(8,128)(2,1)S(1)} %get-tuple-element.70.refs_0_, bf16[80,640]{1,0:T(8,128)(2,1)S(1)} %collective-permute-done.21.refs_1_, bf16[80,640]{1,0:T(8,128)(2,1)S(1)} %collective-permute-done.22.refs_2_, bf16[80,640]{1,0:T(8,128)(2,1)S(1)} %collective-permute-done.23.refs_3_, ...), custom_call_target="tpu_custom_call" | custom-call | bytes 1024 | tf_op jit(solution)/shard_map/pallas_call | solution.py:40
  114.8 2.9 %shard_map.125 = (bf16[5120,160]{1,0:T(8,128)(2,1)S(1)}, bf16[512,160]{1,0:T(8,128)(2,1)S(1)}) custom-call(bf16[40,17408]{1,0:T(8,128)(2,1)S(1)} %get-tuple-element.75.act.refs_0_.refs_2_.refs_4_.refs_6_, bf16[40,17408]{1,0:T(8,128)(2,1)S(1)} %collective-permute-done.29.refs_1_.refs_3_.refs_5_.refs_7_, ...), custom_call_target="tpu_custom_call" | custom-call | bytes 1024 | tf_op jit(solution)/shard_map/pallas_call | solution.py:449
  117.6 6.2 %shard_map.126 = (bf16[5120,512]{1,0:T(8,128)(2,1)}, bf16[5120,512]{1,0:T(8,128)(2,1)}) custom-call(bf16[5120,160]{1,0:T(8,128)(2,1)S(1)} %get-tuple-element.81.x_t, bf16[40,6144]{1,0:T(8,128)(2,1)S(1)} %get-tuple-element.76._.refs_0_.refs_2_, bf16[40,6144]{1,0:T(8,128)(2,1)S(1)} %collective-permute-done.30.refs_1_.refs_3_, ...), custom_call_target="tpu_custom_call" | custom-call | bytes 1024 | tf_op jit(solution)/shard_map/pallas_call | solution.py:449
  123.8 4.1 %shard_map.127 = bf16[512,5120]{1,0:T(8,128)(2,1)} custom-call(bf16[512,160]{1,0:T(8,128)(2,1)S(1)} %get-tuple-element.84.act_t, bf16[40,6144]{1,0:T(8,128)(2,1)S(1)} %get-tuple-element.76._.refs_0_.refs_2_, bf16[40,6144]{1,0:T(8,128)(2,1)S(1)} %collective-permute-done.30.refs_1_.refs_3_, ...), custom_call_target="tpu_custom_call" | custom-call | bytes 1024 | tf_op jit(solution)/shard_map/pallas_call | solution.py:449
  127.9 5.7 %collective-permute-done.24.rest = bf16[912,640]{1,0:T(8,128)(2,1)S(1)} collective-permute-done((bf16[912,640]{1,0:T(8,128)(2,1)S(1)}, bf16[912,640]{1,0:T(8,128)(2,1)S(1)}, u32[]{:S(2)}, u32[]{:S(2)}) %collective-permute-start.24) | collective-permute-done | bytes 1167392 | tf_op jit(solution)/shard_map/ppermute | solution.py:27
  133.6 1.9 %shard_map.124 = bf16[128,5120]{1,0:T(8,128)(2,1)} custom-call(bf16[128,640]{1,0:T(8,128)(2,1)S(1)} %collective-permute-done.9.__.early, bf16[912,640]{1,0:T(8,128)(2,1)S(1)} %collective-permute-done.24.rest, bf16[80,640]{1,0:T(8,128)(2,1)S(1)} %collective-permute-done.28.upd1), custom_call_target="tpu_custom_call" | custom-call | bytes 1024 | tf_op jit(solution)/shard_map/pallas_call | solution.py:40
  (25 shorter events, 0.1 us)
Async XLA Ops:
  0.6 39.0 %collective-permute-start.8 = (bf16[128,5120]{1,0:T(8,128)(2,1)}, bf16[128,5120]{1,0:T(8,128)(2,1)S(1)}, u32[]{:S(2)}, u32[]{:S(2)}) collective-permute-start(bf16[128,5120]{1,0:T(8,128)(2,1)} %param.8), channel_id=1, source_target_pairs={{8,0},{16,8},{24,16},{0,24},{9,1},{17,9},{25,17},{1,25},{10,2},{18... | collective-permute-start | bytes 3932168 | tf_op jit(solution)/shard_map/ppermute | solution.py:27
  8.6 4.6 %collective-permute-start = (bf16[80,640]{1,0:T(8,128)(2,1)S(1)}, bf16[80,640]{1,0:T(8,128)(2,1)S(1)}, u32[]{:S(2)}, u32[]{:S(2)}) collective-permute-start(bf16[80,640]{1,0:T(8,128)(2,1)S(1)} %get-tuple-element.45.refs_0_), channel_id=1, source_target_pairs={{6,0},{0,2},{2,4},{4,6},{7,1},{1,3},{3,5},{5,7},{14,8},{8,10},{10,... | collective-permute-start | bytes 307208 | tf_op jit(solution)/shard_map/ppermute | solution.py:27
  8.7 5.8 %collective-permute-start.1 = (bf16[80,640]{1,0:T(8,128)(2,1)S(1)}, bf16[80,640]{1,0:T(8,128)(2,1)S(1)}, u32[]{:S(2)}, u32[]{:S(2)}) collective-permute-start(bf16[80,640]{1,0:T(8,128)(2,1)S(1)} %get-tuple-element.45.refs_0_), channel_id=1, source_target_pairs={{4,0},{6,2},{0,4},{2,6},{5,1},{7,3},{1,5},{3,7},{12,8},{14,10},{8,... | collective-permute-start | bytes 307208 | tf_op jit(solution)/shard_map/ppermute | solution.py:27
  10.2 4.8 %collective-permute-start.2 = (bf16[80,640]{1,0:T(8,128)(2,1)S(1)}, bf16[80,640]{1,0:T(8,128)(2,1)S(1)}, u32[]{:S(2)}, u32[]{:S(2)}) collective-permute-start(bf16[80,640]{1,0:T(8,128)(2,1)S(1)} %get-tuple-element.45.refs_0_), channel_id=1, source_target_pairs={{2,0},{4,2},{6,4},{0,6},{3,1},{5,3},{7,5},{1,7},{10,8},{12,10},{14... | collective-permute-start | bytes 307208 | tf_op jit(solution)/shard_map/ppermute | solution.py:27
  15.1 9.3 %copy-start.1 = (s32[2,128,4]{1,2,0:T(4,128)S(1)}, s32[2,128,4]{1,2,0:T(4,128)}, u32[]{:S(2)}) copy-start(s32[2,128,4]{1,2,0:T(4,128)} %param.12) | copy-start | bytes 12292
  15.1 19.0 %copy-start.3 = (bf16[128,640]{1,0:T(8,128)(2,1)S(1)}, bf16[128,640]{1,0:T(8,128)(2,1)}, u32[]{:S(2)}) copy-start(bf16[128,640]{1,0:T(8,128)(2,1)} %get-tuple-element.53) | copy-start | bytes 491524
  15.1 20.4 %copy-start = (bf16[128,5120]{1,0:T(8,128)(2,1)S(1)}, bf16[128,5120]{1,0:T(8,128)(2,1)}, u32[]{:S(2)}) copy-start(bf16[128,5120]{1,0:T(8,128)(2,1)} %tokens.3) | copy-start | bytes 3932164
  15.1 20.5 %copy-start.2 = (f32[2,128,4]{1,2,0:T(4,128)S(1)}, f32[2,128,4]{1,2,0:T(4,128)}, u32[]{:S(2)}) copy-start(f32[2,128,4]{1,2,0:T(4,128)} %param.13) | copy-start | bytes 12292
  21.6 13.9 %collective-permute-start.3 = (bf16[80,640]{1,0:T(8,128)(2,1)S(1)}, bf16[80,640]{1,0:T(8,128)(2,1)S(1)}, u32[]{:S(2)}, u32[]{:S(2)}) collective-permute-start(bf16[80,640]{1,0:T(8,128)(2,1)S(1)} %get-tuple-element.47), channel_id=1, source_target_pairs={{2,0},{4,2},{6,4},{0,6},{3,1},{5,3},{7,5},{1,7},{10,8},{12,10},{14... | collective-permute-start | bytes 307208 | tf_op jit(solution)/shard_map/ppermute | solution.py:27
  23.9 11.6 %collective-permute-start.4 = (bf16[80,640]{1,0:T(8,128)(2,1)S(1)}, bf16[80,640]{1,0:T(8,128)(2,1)S(1)}, u32[]{:S(2)}, u32[]{:S(2)}) collective-permute-start(bf16[80,640]{1,0:T(8,128)(2,1)S(1)} %get-tuple-element.48), channel_id=1, source_target_pairs={{4,0},{6,2},{0,4},{2,6},{5,1},{7,3},{1,5},{3,7},{12,8},{14,10},{8,... | collective-permute-start | bytes 307208 | tf_op jit(solution)/shard_map/ppermute | solution.py:27
  24.4 11.1 %collective-permute-start.5 = (bf16[80,640]{1,0:T(8,128)(2,1)S(1)}, bf16[80,640]{1,0:T(8,128)(2,1)S(1)}, u32[]{:S(2)}, u32[]{:S(2)}) collective-permute-start(bf16[80,640]{1,0:T(8,128)(2,1)S(1)} %get-tuple-element.49), channel_id=1, source_target_pairs={{6,0},{0,2},{2,4},{4,6},{7,1},{1,3},{3,5},{5,7},{14,8},{8,10},{10,... | collective-permute-start | bytes 307208 | tf_op jit(solution)/shard_map/ppermute | solution.py:27
  24.4 9.7 %collective-permute-start.6 = (s32[1,4,128]{2,1,0:T(4,128)S(1)}, s32[1,4,128]{2,1,0:T(4,128)S(1)}, u32[]{:S(2)}, u32[]{:S(2)}) collective-permute-start(s32[1,4,128]{2,1,0:T(4,128)S(1)} %slice.4), channel_id=1, source_target_pairs={{8,0},{16,8},{24,16},{0,24},{9,1},{17,9},{25,17},{1,25},{10,2},{18... | collective-permute-start | bytes 6152 | tf_op jit(solution)/shard_map/ppermute | solution.py:27
  34.1 11.7 %collective-permute-start.9 = (bf16[128,640]{1,0:T(8,128)(2,1)S(1)}, bf16[128,640]{1,0:T(8,128)(2,1)S(1)}, u32[]{:S(2)}, u32[]{:S(2)}) collective-permute-start(bf16[128,640]{1,0:T(8,128)(2,1)S(1)} %copy-done.3), channel_id=1, source_target_pairs={{16,0},{24,8},{0,16},{8,24},{17,1},{25,9},{1,17},{9,25},{18,2},{26... | collective-permute-start | bytes 491528 | tf_op jit(solution)/shard_map/ppermute | solution.py:27
  36.2 9.5 %collective-permute-start.7 = (bf16[80,640]{1,0:T(8,128)(2,1)S(1)}, bf16[80,640]{1,0:T(8,128)(2,1)S(1)}, u32[]{:S(2)}, u32[]{:S(2)}) collective-permute-start(bf16[80,640]{1,0:T(8,128)(2,1)S(1)} %get-tuple-element.51), channel_id=1, source_target_pairs={{24,0},{0,8},{8,16},{16,24},{25,1},{1,9},{9,17},{17,25},{26,2},{2,... | collective-permute-start | bytes 307208 | tf_op jit(solution)/shard_map/ppermute | solution.py:27
  46.1 33.6 %collective-permute-start.17 = (bf16[128,5120]{1,0:T(8,128)(2,1)S(1)}, bf16[128,5120]{1,0:T(8,128)(2,1)S(1)}, u32[]{:S(2)}, u32[]{:S(2)}) collective-permute-start(bf16[128,5120]{1,0:T(8,128)(2,1)S(1)} %get-tuple-element.65), channel_id=1, source_target_pairs={{8,0},{16,8},{24,16},{0,24},{9,1},{17,9},{25,17},{1,25},{10,2},{18... | collective-permute-start | bytes 3932168 | tf_op jit(solution)/shard_map/ppermute | solution.py:27
  47.5 6.8 %collective-permute-start.10 = (bf16[160,640]{1,0:T(8,128)(2,1)S(1)}, bf16[160,640]{1,0:T(8,128)(2,1)S(1)}, u32[]{:S(2)}, u32[]{:S(2)}) collective-permute-start(bf16[160,640]{1,0:T(8,128)(2,1)S(1)} %get-tuple-element.54.refs_0_), channel_id=1, source_target_pairs={{6,0},{0,2},{2,4},{4,6},{7,1},{1,3},{3,5},{5,7},{14,8},{8,10},{10,... | collective-permute-start | bytes 614408 | tf_op jit(solution)/shard_map/ppermute | solution.py:27
  47.5 7.9 %collective-permute-start.11 = (bf16[160,640]{1,0:T(8,128)(2,1)S(1)}, bf16[160,640]{1,0:T(8,128)(2,1)S(1)}, u32[]{:S(2)}, u32[]{:S(2)}) collective-permute-start(bf16[160,640]{1,0:T(8,128)(2,1)S(1)} %get-tuple-element.54.refs_0_), channel_id=1, source_target_pairs={{4,0},{6,2},{0,4},{2,6},{5,1},{7,3},{1,5},{3,7},{12,8},{14,10},{8,... | collective-permute-start | bytes 614408 | tf_op jit(solution)/shard_map/ppermute | solution.py:27
  49.0 9.3 %collective-permute-start.12 = (bf16[160,640]{1,0:T(8,128)(2,1)S(1)}, bf16[160,640]{1,0:T(8,128)(2,1)S(1)}, u32[]{:S(2)}, u32[]{:S(2)}) collective-permute-start(bf16[160,640]{1,0:T(8,128)(2,1)S(1)} %get-tuple-element.54.refs_0_), channel_id=1, source_target_pairs={{2,0},{4,2},{6,4},{0,6},{3,1},{5,3},{7,5},{1,7},{10,8},{12,10},{14... | collective-permute-start | bytes 614408 | tf_op jit(solution)/shard_map/ppermute | solution.py:27
  65.2 49.6 %collective-permute-start.29 = (bf16[40,17408]{1,0:T(8,128)(2,1)S(1)}, bf16[40,17408]{1,0:T(8,128)(2,1)S(1)}, u32[]{:S(2)}, u32[]{:S(2)}) collective-permute-start(bf16[40,17408]{1,0:T(8,128)(2,1)S(1)} %get-tuple-element.75.act.refs_0_.refs_2_.refs_4_.refs_6_), channel_id=1, source_target_pairs={{1,0},{0,1},{3,2},{2,3},{5,4},{4,5},{7,6},{6,7},{9,8},{8,9},{11,10... | collective-permute-start | bytes 4177928 | tf_op jit(solution)/shard_map/ppermute | solution.py:27
  66.7 4.8 %collective-permute-start.13 = (bf16[80,640]{1,0:T(8,128)(2,1)S(1)}, bf16[80,640]{1,0:T(8,128)(2,1)S(1)}, u32[]{:S(2)}, u32[]{:S(2)}) collective-permute-start(bf16[80,640]{1,0:T(8,128)(2,1)S(1)} %get-tuple-element.61), channel_id=1, source_target_pairs={{2,0},{4,2},{6,4},{0,6},{3,1},{5,3},{7,5},{1,7},{10,8},{12,10},{14... | collective-permute-start | bytes 307208 | tf_op jit(solution)/shard_map/ppermute | solution.py:27
  68.6 5.9 %collective-permute-start.14 = (bf16[80,640]{1,0:T(8,128)(2,1)S(1)}, bf16[80,640]{1,0:T(8,128)(2,1)S(1)}, u32[]{:S(2)}, u32[]{:S(2)}) collective-permute-start(bf16[80,640]{1,0:T(8,128)(2,1)S(1)} %get-tuple-element.62), channel_id=1, source_target_pairs={{4,0},{6,2},{0,4},{2,6},{5,1},{7,3},{1,5},{3,7},{12,8},{14,10},{8,... | collective-permute-start | bytes 307208 | tf_op jit(solution)/shard_map/ppermute | solution.py:27
  69.1 5.4 %collective-permute-start.15 = (bf16[80,640]{1,0:T(8,128)(2,1)S(1)}, bf16[80,640]{1,0:T(8,128)(2,1)S(1)}, u32[]{:S(2)}, u32[]{:S(2)}) collective-permute-start(bf16[80,640]{1,0:T(8,128)(2,1)S(1)} %get-tuple-element.63), channel_id=1, source_target_pairs={{6,0},{0,2},{2,4},{4,6},{7,1},{1,3},{3,5},{5,7},{14,8},{8,10},{10,... | collective-permute-start | bytes 307208 | tf_op jit(solution)/shard_map/ppermute | solution.py:27
  75.0 4.7 %collective-permute-start.16 = (bf16[80,640]{1,0:T(8,128)(2,1)S(1)}, bf16[80,640]{1,0:T(8,128)(2,1)S(1)}, u32[]{:S(2)}, u32[]{:S(2)}) collective-permute-start(bf16[80,640]{1,0:T(8,128)(2,1)S(1)} %shard_map.116), channel_id=1, source_target_pairs={{8,0},{16,8},{24,16},{0,24},{9,1},{17,9},{25,17},{1,25},{10,2},{18... | collective-permute-start | bytes 307208 | tf_op jit(solution)/shard_map/ppermute | solution.py:27
  79.7 53.9 %collective-permute-start.24 = (bf16[912,640]{1,0:T(8,128)(2,1)S(1)}, bf16[912,640]{1,0:T(8,128)(2,1)S(1)}, u32[]{:S(2)}, u32[]{:S(2)}) collective-permute-start(bf16[912,640]{1,0:T(8,128)(2,1)S(1)} %shard_map.118._), channel_id=1, source_target_pairs={{16,0},{24,8},{0,16},{8,24},{17,1},{25,9},{1,17},{9,25},{18,2},{26... | collective-permute-start | bytes 3502088 | tf_op jit(solution)/shard_map/ppermute | solution.py:27
  81.3 4.6 %collective-permute-start.18 = (bf16[80,640]{1,0:T(8,128)(2,1)S(1)}, bf16[80,640]{1,0:T(8,128)(2,1)S(1)}, u32[]{:S(2)}, u32[]{:S(2)}) collective-permute-start(bf16[80,640]{1,0:T(8,128)(2,1)S(1)} %get-tuple-element.67.refs_0_), channel_id=1, source_target_pairs={{6,0},{0,2},{2,4},{4,6},{7,1},{1,3},{3,5},{5,7},{14,8},{8,10},{10,... | collective-permute-start | bytes 307208 | tf_op jit(solution)/shard_map/ppermute | solution.py:27
  81.4 5.8 %collective-permute-start.19 = (bf16[80,640]{1,0:T(8,128)(2,1)S(1)}, bf16[80,640]{1,0:T(8,128)(2,1)S(1)}, u32[]{:S(2)}, u32[]{:S(2)}) collective-permute-start(bf16[80,640]{1,0:T(8,128)(2,1)S(1)} %get-tuple-element.67.refs_0_), channel_id=1, source_target_pairs={{4,0},{6,2},{0,4},{2,6},{5,1},{7,3},{1,5},{3,7},{12,8},{14,10},{8,... | collective-permute-start | bytes 307208 | tf_op jit(solution)/shard_map/ppermute | solution.py:27
  83.0 4.8 %collective-permute-start.20 = (bf16[80,640]{1,0:T(8,128)(2,1)S(1)}, bf16[80,640]{1,0:T(8,128)(2,1)S(1)}, u32[]{:S(2)}, u32[]{:S(2)}) collective-permute-start(bf16[80,640]{1,0:T(8,128)(2,1)S(1)} %get-tuple-element.67.refs_0_), channel_id=1, source_target_pairs={{2,0},{4,2},{6,4},{0,6},{3,1},{5,3},{7,5},{1,7},{10,8},{12,10},{14... | collective-permute-start | bytes 307208 | tf_op jit(solution)/shard_map/ppermute | solution.py:27
  92.8 24.8 %collective-permute-start.30 = (bf16[40,6144]{1,0:T(8,128)(2,1)S(1)}, bf16[40,6144]{1,0:T(8,128)(2,1)S(1)}, u32[]{:S(2)}, u32[]{:S(2)}) collective-permute-start(bf16[40,6144]{1,0:T(8,128)(2,1)S(1)} %get-tuple-element.76._.refs_0_.refs_2_), channel_id=1, source_target_pairs={{1,0},{0,1},{3,2},{2,3},{5,4},{4,5},{7,6},{6,7},{9,8},{8,9},{11,10... | collective-permute-start | bytes 1474568 | tf_op jit(solution)/shard_map/ppermute | solution.py:27
  94.4 4.2 %collective-permute-start.21 = (bf16[80,640]{1,0:T(8,128)(2,1)S(1)}, bf16[80,640]{1,0:T(8,128)(2,1)S(1)}, u32[]{:S(2)}, u32[]{:S(2)}) collective-permute-start(bf16[80,640]{1,0:T(8,128)(2,1)S(1)} %get-tuple-element.71), channel_id=1, source_target_pairs={{2,0},{4,2},{6,4},{0,6},{3,1},{5,3},{7,5},{1,7},{10,8},{12,10},{14... | collective-permute-start | bytes 307208 | tf_op jit(solution)/shard_map/ppermute | solution.py:27
  97.4 2.3 %collective-permute-start.25 = (bf16[80,640]{1,0:T(8,128)(2,1)S(1)}, bf16[80,640]{1,0:T(8,128)(2,1)S(1)}, u32[]{:S(2)}, u32[]{:S(2)}) collective-permute-start(bf16[80,640]{1,0:T(8,128)(2,1)S(1)} %get-tuple-element.78), channel_id=1, source_target_pairs={{2,0},{4,2},{6,4},{0,6},{3,1},{5,3},{7,5},{1,7},{10,8},{12,10},{14... | collective-permute-start | bytes 307208 | tf_op jit(solution)/shard_map/ppermute | solution.py:27
  98.6 5.7 %collective-permute-start.26 = (bf16[80,640]{1,0:T(8,128)(2,1)S(1)}, bf16[80,640]{1,0:T(8,128)(2,1)S(1)}, u32[]{:S(2)}, u32[]{:S(2)}) collective-permute-start(bf16[80,640]{1,0:T(8,128)(2,1)S(1)} %get-tuple-element.79), channel_id=1, source_target_pairs={{4,0},{6,2},{0,4},{2,6},{5,1},{7,3},{1,5},{3,7},{12,8},{14,10},{8,... | collective-permute-start | bytes 307208 | tf_op jit(solution)/shard_map/ppermute | solution.py:27
  99.7 5.7 %collective-permute-start.27 = (bf16[80,640]{1,0:T(8,128)(2,1)S(1)}, bf16[80,640]{1,0:T(8,128)(2,1)S(1)}, u32[]{:S(2)}, u32[]{:S(2)}) collective-permute-start(bf16[80,640]{1,0:T(8,128)(2,1)S(1)} %get-tuple-element.80), channel_id=1, source_target_pairs={{6,0},{0,2},{2,4},{4,6},{7,1},{1,3},{3,5},{5,7},{14,8},{8,10},{10,... | collective-permute-start | bytes 307208 | tf_op jit(solution)/shard_map/ppermute | solution.py:27
  104.3 5.7 %collective-permute-start.22 = (bf16[80,640]{1,0:T(8,128)(2,1)S(1)}, bf16[80,640]{1,0:T(8,128)(2,1)S(1)}, u32[]{:S(2)}, u32[]{:S(2)}) collective-permute-start(bf16[80,640]{1,0:T(8,128)(2,1)S(1)} %get-tuple-element.72), channel_id=1, source_target_pairs={{4,0},{6,2},{0,4},{2,6},{5,1},{7,3},{1,5},{3,7},{12,8},{14,10},{8,... | collective-permute-start | bytes 307208 | tf_op jit(solution)/shard_map/ppermute | solution.py:27
  105.4 6.9 %collective-permute-start.23 = (bf16[80,640]{1,0:T(8,128)(2,1)S(1)}, bf16[80,640]{1,0:T(8,128)(2,1)S(1)}, u32[]{:S(2)}, u32[]{:S(2)}) collective-permute-start(bf16[80,640]{1,0:T(8,128)(2,1)S(1)} %get-tuple-element.73), channel_id=1, source_target_pairs={{6,0},{0,2},{2,4},{4,6},{7,1},{1,3},{3,5},{5,7},{14,8},{8,10},{10,... | collective-permute-start | bytes 307208 | tf_op jit(solution)/shard_map/ppermute | solution.py:27
  110.0 17.9 %collective-permute-start.28 = (bf16[80,640]{1,0:T(8,128)(2,1)S(1)}, bf16[80,640]{1,0:T(8,128)(2,1)S(1)}, u32[]{:S(2)}, u32[]{:S(2)}) collective-permute-start(bf16[80,640]{1,0:T(8,128)(2,1)S(1)} %shard_map.123), channel_id=1, source_target_pairs={{24,0},{0,8},{8,16},{16,24},{25,1},{1,9},{9,17},{17,25},{26,2},{2,... | collective-permute-start | bytes 307208 | tf_op jit(solution)/shard_map/ppermute | solution.py:27

commit v13 on v12

--- a/solution.py
+++ b/solution.py
@@ -208,7 +208,7 @@
     upd[...] = (h[...].astype(F32) + weight * summed(parts)).astype(BF16)
 
 
-def enter1_kernel(h, scaled, _, __, out, ___):
+def enter1_kernel(h, scaled, out):
     values = h[...].astype(F32)
     out[:PACKED] = (values * inv_rms_of(values)).astype(BF16)
     out[PACKED:] = scaled[...]
@@ -246,25 +246,33 @@
         out[:, k] = placed(chunk, value, second, hit2, fresh)
 
 
-def finish_state_kernel(early, rest, upd1, out, outs, last, sems):
+def prepare_state_kernel(early, rest, out, turned_select, hit, last):
     height, width = out.shape
     at = (PACK - EARLY) * height
     last[...] = rest[at:].astype(F32)
     first = select_of(last[CAP : CAP + TOP, :height])
     second = select_of(last[CAP : CAP + TOP, height : 2 * height])
-    hit1, hit2 = hit_rows(first), hit_rows(second)
     rows = jnp.concatenate([last[...], jnp.zeros((PACKED - TAIL, last.shape[1]), F32)], axis=0)
-    rows1, rows2 = rows.astype(BF16), upd1[...]
+    out[:, columns(0, width)] = placed(0, early[...], first, hit_rows(first), rows.astype(BF16))
+    for c in range(EARLY, PACK):
+        out[:, columns(c, width)] = rest[(c - EARLY) * height : (c - EARLY + 1) * height]
+    turned_select[...] = second.T
+    ones = jnp.ones((PACKED, 128), BF16)
+    hit[...] = dot(chunk_of(second, 0), ones, 0, 0)
+
+
+def finish_state_kernel(base, turned_select, hit, upd1, out, outs, sems):
+    height, width = out.shape
+    _, chunk = packed_index(turned_select.shape, 1)
     copies = []
     for r0 in range(0, height, height // 2):
         r = slice(r0, r0 + height // 2)
+        taken = hit[r, :1] > 0.5
         for c in range(PACK):
-            if c < EARLY:
-                value = placed(c, early[r], first[:, r], hit1[r], rows1)
-            else:
-                start = (c - EARLY) * height + r0
-                value = rest[start : start + height // 2]
-            outs[r, columns(c, width)] = placed(c, value, second[:, r], hit2[r], rows2)
+            k = columns(c, width)
+            select = jnp.where(chunk[r] == c, turned_select[r], 0.0).astype(BF16)
+            value = jnp.where(taken, dot(select, upd1[...]), base[r, k].astype(F32))
+            outs[r, k] = value.astype(BF16)
         for i in range(r0 // 16, r.stop // 16):
             b = pl.ds(16 * i, 16)
             copies.append(pltpu.make_async_copy(outs.at[b], out.at[b], sems.at[i]))
@@ -580,13 +588,18 @@
     )
     cot1, scaled1 = call(grad_rows_kernel, [one, one], [cot1_all, routes, gates])
 
-    enter1, cot1_all = call(
+    (enter1,) = call(
         enter1_kernel,
-        [((2 * PACKED, step), BF16), (tokens.shape, BF16)],
-        [h1, scaled1, cot1_all, early],
-        any_args=(2, 3),
-        any_outs=(1,),
-        aliases={2: 1},
+        [((2 * PACKED, step), BF16)],
+        [h1, scaled1],
+    )
+    (cot1_all,) = call(
+        release_kernel,
+        [(tokens.shape, BF16)],
+        [cot1_all, h1, scaled1, early],
+        any_args=(0, 1, 2, 3),
+        any_outs=(0,),
+        aliases={0: 0},
     )
     cot0_all = shifted(cot1_all, "section", -1)
     blocks = from_group(enter1)
@@ -647,16 +660,23 @@
     x_t, act_t = turned(kept_all, width, hidden)
     (down_out,) = down_grads(act_t, g_grad0_all, kept_all, width, hidden)
     gate_out, up_out = input_grads(x_t, g_grad0_all, kept_all, width, hidden)
+    height = tokens.shape[0]
+    base, turned_select, hit = call(
+        prepare_state_kernel,
+        [
+            pltpu.VMEM(tokens.shape, BF16),
+            pltpu.VMEM((height, PACKED), F32),
+            pltpu.VMEM((height, 128), F32),
+        ],
+        [early, rest],
+        scratch=[pltpu.VMEM((TAIL, step), F32)],
+    )
     (state,) = call(
         finish_state_kernel,
         [(tokens.shape, BF16)],
-        [early, rest, last1],
+        [base, turned_select, hit, last1],
         any_outs=(0,),
-        scratch=[
-            pltpu.VMEM(tokens.shape, BF16),
-            pltpu.VMEM((TAIL, step), F32),
-            pltpu.SemaphoreType.DMA((tokens.shape[0] // 16,)),
-        ],
+        scratch=[pltpu.VMEM(tokens.shape, BF16), pltpu.SemaphoreType.DMA((height // 16,))],
     )
     return (grad, state, gate_out[None], up_out[None], down_out[None])
 

time: 136 us -> 136 us (level)
    pallas_call x15 -> x17, Pallas kernels: 30.5 us -> 30.5 us  [call(): pl.pallas_call(kernel, out_shape=outs, in_specs=[anywhere if i in any_arg...]
  transfers between devices with their start and end apart: 31 -> 31, of which waited for: 20 -> 20; matrix products, arithmetic and copies ran while one was open for 0% -> 0% of each run, Pallas kernels for 30% -> 31%
where the time goes in v13:
time: 136 us
  waiting for transfers between devices  53.4 us (39%)
  Pallas kernels  43.7 us (32%)
  starting transfers between devices  37.7 us (28%)
    ppermute x31, waiting for transfers between devices, shifted(): lax.ppermute(block, axis, [((i - distance) % size, i) for i in range(size)])  53.4 us
    ppermute x31, starting transfers between devices, shifted(): lax.ppermute(block, axis, [((i - distance) % size, i) for i in range(size)])  37.7 us
    pallas_call x17, Pallas kernels, call(): pl.pallas_call(kernel, out_shape=outs, in_specs=[anywhere if i in any_arg...  30.5 us
    pallas_call x3, Pallas kernels, chunked_call(): pl.pallas_call(kernel, grid=(steps,), out_shape=[jax.ShapeDtypeStruct(s,...  13.1 us
  transfers between devices with their start and end apart: 31, of which 20 were waited for; matrix products, arithmetic and copies ran while one was open for 0% of the time, Pallas kernels for 31%

profile of v13, /device:TPU:0, one launch (start us, length us, event | category | flops | bytes accessed | tf_op | source)
XLA Modules:
  0.0 135.7 jit_solution(1708776528332942207)
XLA Ops:
  0.6 5.1 %collective-permute-start.8 = (bf16[128,5120]{1,0:T(8,128)(2,1)}, bf16[128,5120]{1,0:T(8,128)(2,1)S(1)}, u32[]{:S(2)}, u32[]{:S(2)}) collective-permute-start(bf16[128,5120]{1,0:T(8,128)(2,1)} %param.8), channel_id=1, source_target_pairs={{8,0},{16,8},{24,16},{0,24},{9,1},{17,9},{25,17},{1,25},{10,2},{18... | collective-permute-start | bytes 3932168 | tf_op jit(solution)/shard_map/ppermute | solution.py:27
  5.7 2.9 %shard_map.110 = (bf16[80,640]{1,0:T(8,128)(2,1)S(1)}, bf16[80,640]{1,0:T(8,128)(2,1)S(1)}, bf16[128,640]{1,0:T(8,128)(2,1)}) custom-call(bf16[128,5120]{1,0:T(8,128)(2,1)} %tokens.3, s32[2,4,128]{2,1,0:T(4,128)} %bitcast.8), custom_call_target="tpu_custom_call" | custom-call | bytes 1024 | tf_op jit(solution)/shard_map/pallas_call | solution.py:40
  8.7 1.6 %collective-permute-start.1 = (bf16[80,640]{1,0:T(8,128)(2,1)S(1)}, bf16[80,640]{1,0:T(8,128)(2,1)S(1)}, u32[]{:S(2)}, u32[]{:S(2)}) collective-permute-start(bf16[80,640]{1,0:T(8,128)(2,1)S(1)} %get-tuple-element.46.refs_0_), channel_id=1, source_target_pairs={{4,0},{6,2},{0,4},{2,6},{5,1},{7,3},{1,5},{3,7},{12,8},{14,10},{8,... | collective-permute-start | bytes 307208 | tf_op jit(solution)/shard_map/ppermute | solution.py:27
  10.2 1.4 %collective-permute-start.2 = (bf16[80,640]{1,0:T(8,128)(2,1)S(1)}, bf16[80,640]{1,0:T(8,128)(2,1)S(1)}, u32[]{:S(2)}, u32[]{:S(2)}) collective-permute-start(bf16[80,640]{1,0:T(8,128)(2,1)S(1)} %get-tuple-element.46.refs_0_), channel_id=1, source_target_pairs={{2,0},{4,2},{6,4},{0,6},{3,1},{5,3},{7,5},{1,7},{10,8},{12,10},{14... | collective-permute-start | bytes 307208 | tf_op jit(solution)/shard_map/ppermute | solution.py:27
  11.6 1.6 %collective-permute-done.refs_1_ = bf16[80,640]{1,0:T(8,128)(2,1)S(1)} collective-permute-done((bf16[80,640]{1,0:T(8,128)(2,1)S(1)}, bf16[80,640]{1,0:T(8,128)(2,1)S(1)}, u32[]{:S(2)}, u32[]{:S(2)}) %collective-permute-start) | collective-permute-done | bytes 102432 | tf_op jit(solution)/shard_map/ppermute | solution.py:27
  13.2 1.2 collective-permute-done.1.refs_2_
  14.4 0.6 collective-permute-done.2.refs_3_
  15.1 6.5 %shard_map.111 = (bf16[40,5120]{1,0:T(8,128)(2,1)S(1)}, f32[40,512]{1,0:T(8,128)S(1)}, f32[40,512]{1,0:T(8,128)S(1)}, bf16[40,512]{1,0:T(8,128)(2,1)S(1)}, bf16[...) custom-call(bf16[80,640]{1,0:T(8,128)(2,1)S(1)} %get-tuple-element.4, ...), custom_call_target="tpu_custom_call" | custom-call | bytes 1024 | tf_op jit(solution)/shard_map/pallas_call | solution.py:40
  21.6 2.3 %collective-permute-start.3 = (bf16[80,640]{1,0:T(8,128)(2,1)S(1)}, bf16[80,640]{1,0:T(8,128)(2,1)S(1)}, u32[]{:S(2)}, u32[]{:S(2)}) collective-permute-start(bf16[80,640]{1,0:T(8,128)(2,1)S(1)} %get-tuple-element.48), channel_id=1, source_target_pairs={{2,0},{4,2},{6,4},{0,6},{3,1},{5,3},{7,5},{1,7},{10,8},{12,10},{14... | collective-permute-start | bytes 307208 | tf_op jit(solution)/shard_map/ppermute | solution.py:27
  23.9 0.5 collective-permute-start.4
  24.4 0.5 collective-permute-start.6
  24.9 9.2 %collective-permute-done.6.refs_8_.next_routes = s32[1,4,128]{2,1,0:T(4,128)S(1)} collective-permute-done((s32[1,4,128]{2,1,0:T(4,128)S(1)}, s32[1,4,128]{2,1,0:T(4,128)S(1)}, u32[]{:S(2)}, u32[]{:S(2)}) %collective-permute-start.6) | collective-permute-done | bytes 2080 | tf_op jit(solution)/shard_map/ppermute | solution.py:27
  34.1 1.4 %collective-permute-start.16 = (bf16[128,640]{1,0:T(8,128)(2,1)S(1)}, bf16[128,640]{1,0:T(8,128)(2,1)S(1)}, u32[]{:S(2)}, u32[]{:S(2)}) collective-permute-start(bf16[128,640]{1,0:T(8,128)(2,1)S(1)} %copy-done.3), channel_id=1, source_target_pairs={{16,0},{24,8},{0,16},{8,24},{17,1},{25,9},{1,17},{9,25},{18,2},{26... | collective-permute-start | bytes 491528 | tf_op jit(solution)/shard_map/ppermute | solution.py:27
  35.5 0.7 shard_map.112
  36.2 3.4 %collective-permute-start.7 = (bf16[80,640]{1,0:T(8,128)(2,1)S(1)}, bf16[80,640]{1,0:T(8,128)(2,1)S(1)}, u32[]{:S(2)}, u32[]{:S(2)}) collective-permute-start(bf16[80,640]{1,0:T(8,128)(2,1)S(1)} %get-tuple-element.52), channel_id=1, source_target_pairs={{24,0},{0,8},{8,16},{16,24},{25,1},{1,9},{9,17},{17,25},{26,2},{2,... | collective-permute-start | bytes 307208 | tf_op jit(solution)/shard_map/ppermute | solution.py:27
  39.7 0.5 shard_map.113
  40.2 5.5 %collective-permute-done.16.__3_.early = bf16[128,640]{1,0:T(8,128)(2,1)S(1)} collective-permute-done((bf16[128,640]{1,0:T(8,128)(2,1)S(1)}, bf16[128,640]{1,0:T(8,128)(2,1)S(1)}, u32[]{:S(2)}, u32[]{:S(2)}) %collective-permute-start.16) | collective-permute-done | bytes 163872 | tf_op jit(solution)/shard_map/ppermute | solution.py:27
  45.8 1.3 collective-permute-start.17
  47.1 0.3 shard_map.114.refs_0_
  47.4 0.1 collective-permute-start.9
  47.5 1.6 %collective-permute-start.10 = (bf16[160,640]{1,0:T(8,128)(2,1)S(1)}, bf16[160,640]{1,0:T(8,128)(2,1)S(1)}, u32[]{:S(2)}, u32[]{:S(2)}) collective-permute-start(bf16[160,640]{1,0:T(8,128)(2,1)S(1)} %shard_map.114.refs_0_), channel_id=1, source_target_pairs={{4,0},{6,2},{0,4},{2,6},{5,1},{7,3},{1,5},{3,7},{12,8},{14,10},{8,... | collective-permute-start | bytes 614408 | tf_op jit(solution)/shard_map/ppermute | solution.py:27
  49.1 1.4 %collective-permute-start.11 = (bf16[160,640]{1,0:T(8,128)(2,1)S(1)}, bf16[160,640]{1,0:T(8,128)(2,1)S(1)}, u32[]{:S(2)}, u32[]{:S(2)}) collective-permute-start(bf16[160,640]{1,0:T(8,128)(2,1)S(1)} %shard_map.114.refs_0_), channel_id=1, source_target_pairs={{2,0},{4,2},{6,4},{0,6},{3,1},{5,3},{7,5},{1,7},{10,8},{12,10},{14... | collective-permute-start | bytes 614408 | tf_op jit(solution)/shard_map/ppermute | solution.py:27
  50.5 3.8 %collective-permute-done.9.refs_1_ = bf16[160,640]{1,0:T(8,128)(2,1)S(1)} collective-permute-done((bf16[160,640]{1,0:T(8,128)(2,1)S(1)}, bf16[160,640]{1,0:T(8,128)(2,1)S(1)}, u32[]{:S(2)}, u32[]{:S(2)}) %collective-permute-start.9) | collective-permute-done | bytes 204832 | tf_op jit(solution)/shard_map/ppermute | solution.py:27
  54.3 1.2 collective-permute-done.10.refs_2_
  55.5 2.8 %collective-permute-done.11.refs_3_ = bf16[160,640]{1,0:T(8,128)(2,1)S(1)} collective-permute-done((bf16[160,640]{1,0:T(8,128)(2,1)S(1)}, bf16[160,640]{1,0:T(8,128)(2,1)S(1)}, u32[]{:S(2)}, u32[]{:S(2)}) %collective-permute-start.11) | collective-permute-done | bytes 204832 | tf_op jit(solution)/shard_map/ppermute | solution.py:27
  58.3 6.9 %shard_map.115 = (bf16[40,17408]{1,0:T(8,128)(2,1)S(1)}, bf16[80,640]{1,0:T(8,128)(2,1)S(1)}, bf16[80,640]{1,0:T(8,128)(2,1)S(1)}, bf16[80,640]{1,0:T(8,128)(2,1)S(1)}, bf16[80,640]{1,0:T(8,128)(2,1)S(1)}) custom-call(bf16[160,640]{1,0:T(8,128)(2,1)S(1)} %shard_map.114.refs_0_, bf16[160,640]{1,0:T(8,128)(2,1)S(1)} %collective-permute-done.9.refs_1_, ...), custom_call_target="tpu_custom_call" | custom-call | bytes 1024 | tf_op jit(solution)/shard_map/pallas_call | solution.py:40
  65.2 1.6 %collective-permute-start.29 = (bf16[40,17408]{1,0:T(8,128)(2,1)S(1)}, bf16[40,17408]{1,0:T(8,128)(2,1)S(1)}, u32[]{:S(2)}, u32[]{:S(2)}) collective-permute-start(bf16[40,17408]{1,0:T(8,128)(2,1)S(1)} %get-tuple-element.77.act.refs_0_.refs_2_.refs_4_.refs_6_), channel_id=1, source_target_pairs={{1,0},{0,1},{3,2},{2,3},{5,4},{4,5},{7,6},{6,7},{9,8},{8,9},{11,10... | collective-permute-start | bytes 4177928 | tf_op jit(solution)/shard_map/ppermute | solution.py:27
  66.7 1.9 %collective-permute-start.12 = (bf16[80,640]{1,0:T(8,128)(2,1)S(1)}, bf16[80,640]{1,0:T(8,128)(2,1)S(1)}, u32[]{:S(2)}, u32[]{:S(2)}) collective-permute-start(bf16[80,640]{1,0:T(8,128)(2,1)S(1)} %get-tuple-element.60), channel_id=1, source_target_pairs={{2,0},{4,2},{6,4},{0,6},{3,1},{5,3},{7,5},{1,7},{10,8},{12,10},{14... | collective-permute-start | bytes 307208 | tf_op jit(solution)/shard_map/ppermute | solution.py:27
  68.6 0.5 collective-permute-start.13
  69.2 2.4 %collective-permute-done.12.refs_1_ = bf16[80,640]{1,0:T(8,128)(2,1)S(1)} collective-permute-done((bf16[80,640]{1,0:T(8,128)(2,1)S(1)}, bf16[80,640]{1,0:T(8,128)(2,1)S(1)}, u32[]{:S(2)}, u32[]{:S(2)}) %collective-permute-start.12) | collective-permute-done | bytes 102432 | tf_op jit(solution)/shard_map/ppermute | solution.py:27
  71.5 3.0 %collective-permute-done.13.refs_2_ = bf16[80,640]{1,0:T(8,128)(2,1)S(1)} collective-permute-done((bf16[80,640]{1,0:T(8,128)(2,1)S(1)}, bf16[80,640]{1,0:T(8,128)(2,1)S(1)}, u32[]{:S(2)}, u32[]{:S(2)}) %collective-permute-start.13) | collective-permute-done | bytes 102432 | tf_op jit(solution)/shard_map/ppermute | solution.py:27
  74.5 0.4 shard_map.116
  75.0 1.8 %collective-permute-start.15 = (bf16[80,640]{1,0:T(8,128)(2,1)S(1)}, bf16[80,640]{1,0:T(8,128)(2,1)S(1)}, u32[]{:S(2)}, u32[]{:S(2)}) collective-permute-start(bf16[80,640]{1,0:T(8,128)(2,1)S(1)} %shard_map.116), channel_id=1, source_target_pairs={{8,0},{16,8},{24,16},{0,24},{9,1},{17,9},{25,17},{1,25},{10,2},{18... | collective-permute-start | bytes 307208 | tf_op jit(solution)/shard_map/ppermute | solution.py:27
  76.8 0.7 shard_map.118.__0_
  77.5 2.2 %collective-permute-done.15.__2_.upd1.refs_7_ = bf16[80,640]{1,0:T(8,128)(2,1)S(1)} collective-permute-done((bf16[80,640]{1,0:T(8,128)(2,1)S(1)}, bf16[80,640]{1,0:T(8,128)(2,1)S(1)}, u32[]{:S(2)}, u32[]{:S(2)}) %collective-permute-start.15) | collective-permute-done | bytes 102432 | tf_op jit(solution)/shard_map/ppermute | solution.py:27
  79.7 0.4 collective-permute-start.24
  80.1 0.8 shard_map.120
  80.9 0.1 collective-permute-start.18
  81.0 1.6 %collective-permute-start.19 = (bf16[80,640]{1,0:T(8,128)(2,1)S(1)}, bf16[80,640]{1,0:T(8,128)(2,1)S(1)}, u32[]{:S(2)}, u32[]{:S(2)}) collective-permute-start(bf16[80,640]{1,0:T(8,128)(2,1)S(1)} %get-tuple-element.66.refs_0_), channel_id=1, source_target_pairs={{4,0},{6,2},{0,4},{2,6},{5,1},{7,3},{1,5},{3,7},{12,8},{14,10},{8,... | collective-permute-start | bytes 307208 | tf_op jit(solution)/shard_map/ppermute | solution.py:27
  82.6 1.4 %collective-permute-start.20 = (bf16[80,640]{1,0:T(8,128)(2,1)S(1)}, bf16[80,640]{1,0:T(8,128)(2,1)S(1)}, u32[]{:S(2)}, u32[]{:S(2)}) collective-permute-start(bf16[80,640]{1,0:T(8,128)(2,1)S(1)} %get-tuple-element.66.refs_0_), channel_id=1, source_target_pairs={{2,0},{4,2},{6,4},{0,6},{3,1},{5,3},{7,5},{1,7},{10,8},{12,10},{14... | collective-permute-start | bytes 307208 | tf_op jit(solution)/shard_map/ppermute | solution.py:27
  83.9 1.6 %collective-permute-done.18.refs_1_ = bf16[80,640]{1,0:T(8,128)(2,1)S(1)} collective-permute-done((bf16[80,640]{1,0:T(8,128)(2,1)S(1)}, bf16[80,640]{1,0:T(8,128)(2,1)S(1)}, u32[]{:S(2)}, u32[]{:S(2)}) %collective-permute-start.18) | collective-permute-done | bytes 102432 | tf_op jit(solution)/shard_map/ppermute | solution.py:27
  85.5 1.2 collective-permute-done.19.refs_2_
  86.7 0.6 collective-permute-done.20.refs_3_
  87.4 5.1 %shard_map.121 = (bf16[40,6144]{1,0:T(8,128)(2,1)S(1)}, bf16[80,640]{1,0:T(8,128)(2,1)S(1)}, bf16[80,640]{1,0:T(8,128)(2,1)S(1)}, bf16[80,640]{1,0:T(8,128)(2,1)S(1)}, bf16[80,640]{1,0:T(8,128)(2,1)S(1)}) custom-call(bf16[80,640]{1,0:T(8,128)(2,1)S(1)} %get-tuple-element.66.refs_0_, bf16[80,640]{1,0:T(8,128)(2,1)S(1)} %collective-permute-done.18.refs_1_, ...), custom_call_target="tpu_custom_call" | custom-call | bytes 1024 | tf_op jit(solution)/shard_map/pallas_call | solution.py:40
  92.4 1.6 %collective-permute-start.30 = (bf16[40,6144]{1,0:T(8,128)(2,1)S(1)}, bf16[40,6144]{1,0:T(8,128)(2,1)S(1)}, u32[]{:S(2)}, u32[]{:S(2)}) collective-permute-start(bf16[40,6144]{1,0:T(8,128)(2,1)S(1)} %get-tuple-element.78._.refs_0_.refs_2_), channel_id=1, source_target_pairs={{1,0},{0,1},{3,2},{2,3},{5,4},{4,5},{7,6},{6,7},{9,8},{8,9},{11,10... | collective-permute-start | bytes 1474568 | tf_op jit(solution)/shard_map/ppermute | solution.py:27
  94.0 1.9 %collective-permute-start.21 = (bf16[80,640]{1,0:T(8,128)(2,1)S(1)}, bf16[80,640]{1,0:T(8,128)(2,1)S(1)}, u32[]{:S(2)}, u32[]{:S(2)}) collective-permute-start(bf16[80,640]{1,0:T(8,128)(2,1)S(1)} %get-tuple-element.70), channel_id=1, source_target_pairs={{2,0},{4,2},{6,4},{0,6},{3,1},{5,3},{7,5},{1,7},{10,8},{12,10},{14... | collective-permute-start | bytes 307208 | tf_op jit(solution)/shard_map/ppermute | solution.py:27
  95.9 1.1 shard_map.124
  97.0 0.1 collective-permute-start.25
  97.1 1.1 collective-permute-done.21.refs_1_
  98.2 0.5 collective-permute-start.26
  98.7 0.6 collective-permute-done.25.refs_1_
  99.3 1.1 collective-permute-start.27
  100.4 3.5 %collective-permute-done.26.refs_2_ = bf16[80,640]{1,0:T(8,128)(2,1)S(1)} collective-permute-done((bf16[80,640]{1,0:T(8,128)(2,1)S(1)}, bf16[80,640]{1,0:T(8,128)(2,1)S(1)}, u32[]{:S(2)}, u32[]{:S(2)}) %collective-permute-start.26) | collective-permute-done | bytes 102432 | tf_op jit(solution)/shard_map/ppermute | solution.py:27
  103.9 1.1 collective-permute-done.27.refs_3_
  105.0 0.2 shard_map.125
  105.3 4.3 %collective-permute-done.22.refs_2_ = bf16[80,640]{1,0:T(8,128)(2,1)S(1)} collective-permute-done((bf16[80,640]{1,0:T(8,128)(2,1)S(1)}, bf16[80,640]{1,0:T(8,128)(2,1)S(1)}, u32[]{:S(2)}, u32[]{:S(2)}) %collective-permute-start.22) | collective-permute-done | bytes 102432 | tf_op jit(solution)/shard_map/ppermute | solution.py:27
  109.6 2.7 %collective-permute-start.28 = (bf16[80,640]{1,0:T(8,128)(2,1)S(1)}, bf16[80,640]{1,0:T(8,128)(2,1)S(1)}, u32[]{:S(2)}, u32[]{:S(2)}) collective-permute-start(bf16[80,640]{1,0:T(8,128)(2,1)S(1)} %shard_map.125), channel_id=1, source_target_pairs={{24,0},{0,8},{8,16},{16,24},{25,1},{1,9},{9,17},{17,25},{26,2},{2,... | collective-permute-start | bytes 307208 | tf_op jit(solution)/shard_map/ppermute | solution.py:27
  112.3 2.4 %shard_map.122 = bf16[128,5120]{1,0:T(8,128)(2,1)} custom-call(bf16[80,640]{1,0:T(8,128)(2,1)S(1)} %get-tuple-element.69.refs_0_, bf16[80,640]{1,0:T(8,128)(2,1)S(1)} %collective-permute-done.21.refs_1_, bf16[80,640]{1,0:T(8,128)(2,1)S(1)} %collective-permute-done.22.refs_2_, bf16[80,640]{1,0:T(8,128)(2,1)S(1)} %collective-permute-done.23.refs_3_, ...), custom_call_target="tpu_custom_call" | custom-call | bytes 1024 | tf_op jit(solution)/shard_map/pallas_call | solution.py:40
  114.8 2.9 %shard_map.127 = (bf16[5120,160]{1,0:T(8,128)(2,1)S(1)}, bf16[512,160]{1,0:T(8,128)(2,1)S(1)}) custom-call(bf16[40,17408]{1,0:T(8,128)(2,1)S(1)} %get-tuple-element.77.act.refs_0_.refs_2_.refs_4_.refs_6_, bf16[40,17408]{1,0:T(8,128)(2,1)S(1)} %collective-permute-done.29.refs_1_.refs_3_.refs_5_.refs_7_, ...), custom_call_target="tpu_custom_call" | custom-call | bytes 1024 | tf_op jit(solution)/shard_map/pallas_call | solution.py:457
  117.6 6.2 %shard_map.128 = (bf16[5120,512]{1,0:T(8,128)(2,1)}, bf16[5120,512]{1,0:T(8,128)(2,1)}) custom-call(bf16[5120,160]{1,0:T(8,128)(2,1)S(1)} %get-tuple-element.83.x_t, bf16[40,6144]{1,0:T(8,128)(2,1)S(1)} %get-tuple-element.78._.refs_0_.refs_2_, bf16[40,6144]{1,0:T(8,128)(2,1)S(1)} %collective-permute-done.30.refs_1_.refs_3_, ...), custom_call_target="tpu_custom_call" | custom-call | bytes 1024 | tf_op jit(solution)/shard_map/pallas_call | solution.py:457
  123.9 4.1 %shard_map.129 = bf16[512,5120]{1,0:T(8,128)(2,1)} custom-call(bf16[512,160]{1,0:T(8,128)(2,1)S(1)} %get-tuple-element.86.act_t, bf16[40,6144]{1,0:T(8,128)(2,1)S(1)} %get-tuple-element.78._.refs_0_.refs_2_, bf16[40,6144]{1,0:T(8,128)(2,1)S(1)} %collective-permute-done.30.refs_1_.refs_3_, ...), custom_call_target="tpu_custom_call" | custom-call | bytes 1024 | tf_op jit(solution)/shard_map/pallas_call | solution.py:457
  127.9 5.7 %collective-permute-done.24.rest = bf16[912,640]{1,0:T(8,128)(2,1)S(1)} collective-permute-done((bf16[912,640]{1,0:T(8,128)(2,1)S(1)}, bf16[912,640]{1,0:T(8,128)(2,1)S(1)}, u32[]{:S(2)}, u32[]{:S(2)}) %collective-permute-start.24) | collective-permute-done | bytes 1167392 | tf_op jit(solution)/shard_map/ppermute | solution.py:27
  133.6 0.5 shard_map.123
  134.1 1.4 %shard_map.126 = bf16[128,5120]{1,0:T(8,128)(2,1)} custom-call(bf16[128,5120]{1,0:T(8,128)(2,1)S(1)} %get-tuple-element.74.base, f32[128,80]{1,0:T(8,128)S(1)} %get-tuple-element.75.turned_select, f32[128,128]{1,0:T(8,128)S(1)} %get-tuple-element.76.hit, bf16[80,640]{1,0:T(8,128)(2,1)S(1)} %collective-permute-done.28.upd1), custom_call_target="tpu_custom_call" | custom-call | bytes 1024 | tf_op jit(solution)/shard_map/pallas_call | solution.py:40
  (27 shorter events, 0.1 us)
Async XLA Ops:
  0.6 39.0 %collective-permute-start.8 = (bf16[128,5120]{1,0:T(8,128)(2,1)}, bf16[128,5120]{1,0:T(8,128)(2,1)S(1)}, u32[]{:S(2)}, u32[]{:S(2)}) collective-permute-start(bf16[128,5120]{1,0:T(8,128)(2,1)} %param.8), channel_id=1, source_target_pairs={{8,0},{16,8},{24,16},{0,24},{9,1},{17,9},{25,17},{1,25},{10,2},{18... | collective-permute-start | bytes 3932168 | tf_op jit(solution)/shard_map/ppermute | solution.py:27
  8.6 4.6 %collective-permute-start = (bf16[80,640]{1,0:T(8,128)(2,1)S(1)}, bf16[80,640]{1,0:T(8,128)(2,1)S(1)}, u32[]{:S(2)}, u32[]{:S(2)}) collective-permute-start(bf16[80,640]{1,0:T(8,128)(2,1)S(1)} %get-tuple-element.46.refs_0_), channel_id=1, source_target_pairs={{6,0},{0,2},{2,4},{4,6},{7,1},{1,3},{3,5},{5,7},{14,8},{8,10},{10,... | collective-permute-start | bytes 307208 | tf_op jit(solution)/shard_map/ppermute | solution.py:27
  8.7 5.8 %collective-permute-start.1 = (bf16[80,640]{1,0:T(8,128)(2,1)S(1)}, bf16[80,640]{1,0:T(8,128)(2,1)S(1)}, u32[]{:S(2)}, u32[]{:S(2)}) collective-permute-start(bf16[80,640]{1,0:T(8,128)(2,1)S(1)} %get-tuple-element.46.refs_0_), channel_id=1, source_target_pairs={{4,0},{6,2},{0,4},{2,6},{5,1},{7,3},{1,5},{3,7},{12,8},{14,10},{8,... | collective-permute-start | bytes 307208 | tf_op jit(solution)/shard_map/ppermute | solution.py:27
  10.2 4.8 %collective-permute-start.2 = (bf16[80,640]{1,0:T(8,128)(2,1)S(1)}, bf16[80,640]{1,0:T(8,128)(2,1)S(1)}, u32[]{:S(2)}, u32[]{:S(2)}) collective-permute-start(bf16[80,640]{1,0:T(8,128)(2,1)S(1)} %get-tuple-element.46.refs_0_), channel_id=1, source_target_pairs={{2,0},{4,2},{6,4},{0,6},{3,1},{5,3},{7,5},{1,7},{10,8},{12,10},{14... | collective-permute-start | bytes 307208 | tf_op jit(solution)/shard_map/ppermute | solution.py:27
  15.1 9.3 %copy-start.1 = (s32[2,128,4]{1,2,0:T(4,128)S(1)}, s32[2,128,4]{1,2,0:T(4,128)}, u32[]{:S(2)}) copy-start(s32[2,128,4]{1,2,0:T(4,128)} %param.12) | copy-start | bytes 12292
  15.1 19.0 %copy-start.3 = (bf16[128,640]{1,0:T(8,128)(2,1)S(1)}, bf16[128,640]{1,0:T(8,128)(2,1)}, u32[]{:S(2)}) copy-start(bf16[128,640]{1,0:T(8,128)(2,1)} %get-tuple-element.64) | copy-start | bytes 491524
  15.1 20.4 %copy-start = (bf16[128,5120]{1,0:T(8,128)(2,1)S(1)}, bf16[128,5120]{1,0:T(8,128)(2,1)}, u32[]{:S(2)}) copy-start(bf16[128,5120]{1,0:T(8,128)(2,1)} %tokens.3) | copy-start | bytes 3932164
  15.1 20.5 %copy-start.2 = (f32[2,128,4]{1,2,0:T(4,128)S(1)}, f32[2,128,4]{1,2,0:T(4,128)}, u32[]{:S(2)}) copy-start(f32[2,128,4]{1,2,0:T(4,128)} %param.13) | copy-start | bytes 12292
  21.6 13.9 %collective-permute-start.3 = (bf16[80,640]{1,0:T(8,128)(2,1)S(1)}, bf16[80,640]{1,0:T(8,128)(2,1)S(1)}, u32[]{:S(2)}, u32[]{:S(2)}) collective-permute-start(bf16[80,640]{1,0:T(8,128)(2,1)S(1)} %get-tuple-element.48), channel_id=1, source_target_pairs={{2,0},{4,2},{6,4},{0,6},{3,1},{5,3},{7,5},{1,7},{10,8},{12,10},{14... | collective-permute-start | bytes 307208 | tf_op jit(solution)/shard_map/ppermute | solution.py:27
  23.9 11.6 %collective-permute-start.4 = (bf16[80,640]{1,0:T(8,128)(2,1)S(1)}, bf16[80,640]{1,0:T(8,128)(2,1)S(1)}, u32[]{:S(2)}, u32[]{:S(2)}) collective-permute-start(bf16[80,640]{1,0:T(8,128)(2,1)S(1)} %get-tuple-element.49), channel_id=1, source_target_pairs={{4,0},{6,2},{0,4},{2,6},{5,1},{7,3},{1,5},{3,7},{12,8},{14,10},{8,... | collective-permute-start | bytes 307208 | tf_op jit(solution)/shard_map/ppermute | solution.py:27
  24.4 11.1 %collective-permute-start.5 = (bf16[80,640]{1,0:T(8,128)(2,1)S(1)}, bf16[80,640]{1,0:T(8,128)(2,1)S(1)}, u32[]{:S(2)}, u32[]{:S(2)}) collective-permute-start(bf16[80,640]{1,0:T(8,128)(2,1)S(1)} %get-tuple-element.50), channel_id=1, source_target_pairs={{6,0},{0,2},{2,4},{4,6},{7,1},{1,3},{3,5},{5,7},{14,8},{8,10},{10,... | collective-permute-start | bytes 307208 | tf_op jit(solution)/shard_map/ppermute | solution.py:27
  24.4 9.7 %collective-permute-start.6 = (s32[1,4,128]{2,1,0:T(4,128)S(1)}, s32[1,4,128]{2,1,0:T(4,128)S(1)}, u32[]{:S(2)}, u32[]{:S(2)}) collective-permute-start(s32[1,4,128]{2,1,0:T(4,128)S(1)} %slice.4), channel_id=1, source_target_pairs={{8,0},{16,8},{24,16},{0,24},{9,1},{17,9},{25,17},{1,25},{10,2},{18... | collective-permute-start | bytes 6152 | tf_op jit(solution)/shard_map/ppermute | solution.py:27
  34.1 11.7 %collective-permute-start.16 = (bf16[128,640]{1,0:T(8,128)(2,1)S(1)}, bf16[128,640]{1,0:T(8,128)(2,1)S(1)}, u32[]{:S(2)}, u32[]{:S(2)}) collective-permute-start(bf16[128,640]{1,0:T(8,128)(2,1)S(1)} %copy-done.3), channel_id=1, source_target_pairs={{16,0},{24,8},{0,16},{8,24},{17,1},{25,9},{1,17},{9,25},{18,2},{26... | collective-permute-start | bytes 491528 | tf_op jit(solution)/shard_map/ppermute | solution.py:27
  36.2 9.5 %collective-permute-start.7 = (bf16[80,640]{1,0:T(8,128)(2,1)S(1)}, bf16[80,640]{1,0:T(8,128)(2,1)S(1)}, u32[]{:S(2)}, u32[]{:S(2)}) collective-permute-start(bf16[80,640]{1,0:T(8,128)(2,1)S(1)} %get-tuple-element.52), channel_id=1, source_target_pairs={{24,0},{0,8},{8,16},{16,24},{25,1},{1,9},{9,17},{17,25},{26,2},{2,... | collective-permute-start | bytes 307208 | tf_op jit(solution)/shard_map/ppermute | solution.py:27
  45.8 33.9 %collective-permute-start.17 = (bf16[128,5120]{1,0:T(8,128)(2,1)S(1)}, bf16[128,5120]{1,0:T(8,128)(2,1)S(1)}, u32[]{:S(2)}, u32[]{:S(2)}) collective-permute-start(bf16[128,5120]{1,0:T(8,128)(2,1)S(1)} %shard_map.117), channel_id=1, source_target_pairs={{8,0},{16,8},{24,16},{0,24},{9,1},{17,9},{25,17},{1,25},{10,2},{18... | collective-permute-start | bytes 3932168 | tf_op jit(solution)/shard_map/ppermute | solution.py:27
  47.4 6.8 %collective-permute-start.9 = (bf16[160,640]{1,0:T(8,128)(2,1)S(1)}, bf16[160,640]{1,0:T(8,128)(2,1)S(1)}, u32[]{:S(2)}, u32[]{:S(2)}) collective-permute-start(bf16[160,640]{1,0:T(8,128)(2,1)S(1)} %shard_map.114.refs_0_), channel_id=1, source_target_pairs={{6,0},{0,2},{2,4},{4,6},{7,1},{1,3},{3,5},{5,7},{14,8},{8,10},{10,... | collective-permute-start | bytes 614408 | tf_op jit(solution)/shard_map/ppermute | solution.py:27
  47.5 8.0 %collective-permute-start.10 = (bf16[160,640]{1,0:T(8,128)(2,1)S(1)}, bf16[160,640]{1,0:T(8,128)(2,1)S(1)}, u32[]{:S(2)}, u32[]{:S(2)}) collective-permute-start(bf16[160,640]{1,0:T(8,128)(2,1)S(1)} %shard_map.114.refs_0_), channel_id=1, source_target_pairs={{4,0},{6,2},{0,4},{2,6},{5,1},{7,3},{1,5},{3,7},{12,8},{14,10},{8,... | collective-permute-start | bytes 614408 | tf_op jit(solution)/shard_map/ppermute | solution.py:27
  49.1 9.2 %collective-permute-start.11 = (bf16[160,640]{1,0:T(8,128)(2,1)S(1)}, bf16[160,640]{1,0:T(8,128)(2,1)S(1)}, u32[]{:S(2)}, u32[]{:S(2)}) collective-permute-start(bf16[160,640]{1,0:T(8,128)(2,1)S(1)} %shard_map.114.refs_0_), channel_id=1, source_target_pairs={{2,0},{4,2},{6,4},{0,6},{3,1},{5,3},{7,5},{1,7},{10,8},{12,10},{14... | collective-permute-start | bytes 614408 | tf_op jit(solution)/shard_map/ppermute | solution.py:27
  65.2 49.6 %collective-permute-start.29 = (bf16[40,17408]{1,0:T(8,128)(2,1)S(1)}, bf16[40,17408]{1,0:T(8,128)(2,1)S(1)}, u32[]{:S(2)}, u32[]{:S(2)}) collective-permute-start(bf16[40,17408]{1,0:T(8,128)(2,1)S(1)} %get-tuple-element.77.act.refs_0_.refs_2_.refs_4_.refs_6_), channel_id=1, source_target_pairs={{1,0},{0,1},{3,2},{2,3},{5,4},{4,5},{7,6},{6,7},{9,8},{8,9},{11,10... | collective-permute-start | bytes 4177928 | tf_op jit(solution)/shard_map/ppermute | solution.py:27
  66.7 4.8 %collective-permute-start.12 = (bf16[80,640]{1,0:T(8,128)(2,1)S(1)}, bf16[80,640]{1,0:T(8,128)(2,1)S(1)}, u32[]{:S(2)}, u32[]{:S(2)}) collective-permute-start(bf16[80,640]{1,0:T(8,128)(2,1)S(1)} %get-tuple-element.60), channel_id=1, source_target_pairs={{2,0},{4,2},{6,4},{0,6},{3,1},{5,3},{7,5},{1,7},{10,8},{12,10},{14... | collective-permute-start | bytes 307208 | tf_op jit(solution)/shard_map/ppermute | solution.py:27
  68.6 5.9 %collective-permute-start.13 = (bf16[80,640]{1,0:T(8,128)(2,1)S(1)}, bf16[80,640]{1,0:T(8,128)(2,1)S(1)}, u32[]{:S(2)}, u32[]{:S(2)}) collective-permute-start(bf16[80,640]{1,0:T(8,128)(2,1)S(1)} %get-tuple-element.61), channel_id=1, source_target_pairs={{4,0},{6,2},{0,4},{2,6},{5,1},{7,3},{1,5},{3,7},{12,8},{14,10},{8,... | collective-permute-start | bytes 307208 | tf_op jit(solution)/shard_map/ppermute | solution.py:27
  69.1 5.4 %collective-permute-start.14 = (bf16[80,640]{1,0:T(8,128)(2,1)S(1)}, bf16[80,640]{1,0:T(8,128)(2,1)S(1)}, u32[]{:S(2)}, u32[]{:S(2)}) collective-permute-start(bf16[80,640]{1,0:T(8,128)(2,1)S(1)} %get-tuple-element.62), channel_id=1, source_target_pairs={{6,0},{0,2},{2,4},{4,6},{7,1},{1,3},{3,5},{5,7},{14,8},{8,10},{10,... | collective-permute-start | bytes 307208 | tf_op jit(solution)/shard_map/ppermute | solution.py:27
  75.0 4.7 %collective-permute-start.15 = (bf16[80,640]{1,0:T(8,128)(2,1)S(1)}, bf16[80,640]{1,0:T(8,128)(2,1)S(1)}, u32[]{:S(2)}, u32[]{:S(2)}) collective-permute-start(bf16[80,640]{1,0:T(8,128)(2,1)S(1)} %shard_map.116), channel_id=1, source_target_pairs={{8,0},{16,8},{24,16},{0,24},{9,1},{17,9},{25,17},{1,25},{10,2},{18... | collective-permute-start | bytes 307208 | tf_op jit(solution)/shard_map/ppermute | solution.py:27
  79.7 53.9 %collective-permute-start.24 = (bf16[912,640]{1,0:T(8,128)(2,1)S(1)}, bf16[912,640]{1,0:T(8,128)(2,1)S(1)}, u32[]{:S(2)}, u32[]{:S(2)}) collective-permute-start(bf16[912,640]{1,0:T(8,128)(2,1)S(1)} %shard_map.119._), channel_id=1, source_target_pairs={{16,0},{24,8},{0,16},{8,24},{17,1},{25,9},{1,17},{9,25},{18,2},{26... | collective-permute-start | bytes 3502088 | tf_op jit(solution)/shard_map/ppermute | solution.py:27
  80.9 4.6 %collective-permute-start.18 = (bf16[80,640]{1,0:T(8,128)(2,1)S(1)}, bf16[80,640]{1,0:T(8,128)(2,1)S(1)}, u32[]{:S(2)}, u32[]{:S(2)}) collective-permute-start(bf16[80,640]{1,0:T(8,128)(2,1)S(1)} %get-tuple-element.66.refs_0_), channel_id=1, source_target_pairs={{6,0},{0,2},{2,4},{4,6},{7,1},{1,3},{3,5},{5,7},{14,8},{8,10},{10,... | collective-permute-start | bytes 307208 | tf_op jit(solution)/shard_map/ppermute | solution.py:27
  81.0 5.8 %collective-permute-start.19 = (bf16[80,640]{1,0:T(8,128)(2,1)S(1)}, bf16[80,640]{1,0:T(8,128)(2,1)S(1)}, u32[]{:S(2)}, u32[]{:S(2)}) collective-permute-start(bf16[80,640]{1,0:T(8,128)(2,1)S(1)} %get-tuple-element.66.refs_0_), channel_id=1, source_target_pairs={{4,0},{6,2},{0,4},{2,6},{5,1},{7,3},{1,5},{3,7},{12,8},{14,10},{8,... | collective-permute-start | bytes 307208 | tf_op jit(solution)/shard_map/ppermute | solution.py:27
  82.6 4.8 %collective-permute-start.20 = (bf16[80,640]{1,0:T(8,128)(2,1)S(1)}, bf16[80,640]{1,0:T(8,128)(2,1)S(1)}, u32[]{:S(2)}, u32[]{:S(2)}) collective-permute-start(bf16[80,640]{1,0:T(8,128)(2,1)S(1)} %get-tuple-element.66.refs_0_), channel_id=1, source_target_pairs={{2,0},{4,2},{6,4},{0,6},{3,1},{5,3},{7,5},{1,7},{10,8},{12,10},{14... | collective-permute-start | bytes 307208 | tf_op jit(solution)/shard_map/ppermute | solution.py:27
  92.4 25.2 %collective-permute-start.30 = (bf16[40,6144]{1,0:T(8,128)(2,1)S(1)}, bf16[40,6144]{1,0:T(8,128)(2,1)S(1)}, u32[]{:S(2)}, u32[]{:S(2)}) collective-permute-start(bf16[40,6144]{1,0:T(8,128)(2,1)S(1)} %get-tuple-element.78._.refs_0_.refs_2_), channel_id=1, source_target_pairs={{1,0},{0,1},{3,2},{2,3},{5,4},{4,5},{7,6},{6,7},{9,8},{8,9},{11,10... | collective-permute-start | bytes 1474568 | tf_op jit(solution)/shard_map/ppermute | solution.py:27
  94.0 4.2 %collective-permute-start.21 = (bf16[80,640]{1,0:T(8,128)(2,1)S(1)}, bf16[80,640]{1,0:T(8,128)(2,1)S(1)}, u32[]{:S(2)}, u32[]{:S(2)}) collective-permute-start(bf16[80,640]{1,0:T(8,128)(2,1)S(1)} %get-tuple-element.70), channel_id=1, source_target_pairs={{2,0},{4,2},{6,4},{0,6},{3,1},{5,3},{7,5},{1,7},{10,8},{12,10},{14... | collective-permute-start | bytes 307208 | tf_op jit(solution)/shard_map/ppermute | solution.py:27
  97.0 2.3 %collective-permute-start.25 = (bf16[80,640]{1,0:T(8,128)(2,1)S(1)}, bf16[80,640]{1,0:T(8,128)(2,1)S(1)}, u32[]{:S(2)}, u32[]{:S(2)}) collective-permute-start(bf16[80,640]{1,0:T(8,128)(2,1)S(1)} %get-tuple-element.80), channel_id=1, source_target_pairs={{2,0},{4,2},{6,4},{0,6},{3,1},{5,3},{7,5},{1,7},{10,8},{12,10},{14... | collective-permute-start | bytes 307208 | tf_op jit(solution)/shard_map/ppermute | solution.py:27
  98.2 5.7 %collective-permute-start.26 = (bf16[80,640]{1,0:T(8,128)(2,1)S(1)}, bf16[80,640]{1,0:T(8,128)(2,1)S(1)}, u32[]{:S(2)}, u32[]{:S(2)}) collective-permute-start(bf16[80,640]{1,0:T(8,128)(2,1)S(1)} %get-tuple-element.81), channel_id=1, source_target_pairs={{4,0},{6,2},{0,4},{2,6},{5,1},{7,3},{1,5},{3,7},{12,8},{14,10},{8,... | collective-permute-start | bytes 307208 | tf_op jit(solution)/shard_map/ppermute | solution.py:27
  99.3 5.7 %collective-permute-start.27 = (bf16[80,640]{1,0:T(8,128)(2,1)S(1)}, bf16[80,640]{1,0:T(8,128)(2,1)S(1)}, u32[]{:S(2)}, u32[]{:S(2)}) collective-permute-start(bf16[80,640]{1,0:T(8,128)(2,1)S(1)} %get-tuple-element.82), channel_id=1, source_target_pairs={{6,0},{0,2},{2,4},{4,6},{7,1},{1,3},{3,5},{5,7},{14,8},{8,10},{10,... | collective-permute-start | bytes 307208 | tf_op jit(solution)/shard_map/ppermute | solution.py:27
  103.9 5.7 %collective-permute-start.22 = (bf16[80,640]{1,0:T(8,128)(2,1)S(1)}, bf16[80,640]{1,0:T(8,128)(2,1)S(1)}, u32[]{:S(2)}, u32[]{:S(2)}) collective-permute-start(bf16[80,640]{1,0:T(8,128)(2,1)S(1)} %get-tuple-element.71), channel_id=1, source_target_pairs={{4,0},{6,2},{0,4},{2,6},{5,1},{7,3},{1,5},{3,7},{12,8},{14,10},{8,... | collective-permute-start | bytes 307208 | tf_op jit(solution)/shard_map/ppermute | solution.py:27
  105.0 7.3 %collective-permute-start.23 = (bf16[80,640]{1,0:T(8,128)(2,1)S(1)}, bf16[80,640]{1,0:T(8,128)(2,1)S(1)}, u32[]{:S(2)}, u32[]{:S(2)}) collective-permute-start(bf16[80,640]{1,0:T(8,128)(2,1)S(1)} %get-tuple-element.72), channel_id=1, source_target_pairs={{6,0},{0,2},{2,4},{4,6},{7,1},{1,3},{3,5},{5,7},{14,8},{8,10},{10,... | collective-permute-start | bytes 307208 | tf_op jit(solution)/shard_map/ppermute | solution.py:27
  109.6 24.5 %collective-permute-start.28 = (bf16[80,640]{1,0:T(8,128)(2,1)S(1)}, bf16[80,640]{1,0:T(8,128)(2,1)S(1)}, u32[]{:S(2)}, u32[]{:S(2)}) collective-permute-start(bf16[80,640]{1,0:T(8,128)(2,1)S(1)} %shard_map.125), channel_id=1, source_target_pairs={{24,0},{0,8},{8,16},{16,24},{25,1},{1,9},{9,17},{17,25},{26,2},{2,... | collective-permute-start | bytes 307208 | tf_op jit(solution)/shard_map/ppermute | solution.py:27

commit v14 on v13

--- a/solution.py
+++ b/solution.py
@@ -533,7 +533,7 @@
     width, hidden = gate.shape
     step = width // PACK
     n = lax.axis_size("expert")
-    rows = -(-n * CAP // 8) * 8
+    rows = -(-n * CAP // 16) * 16
     routes = jnp.transpose(routes, (0, 2, 1))
     gates = jnp.transpose(gates, (0, 2, 1))
     one = ((PACKED, step), BF16)

time: 136 us -> 136 us (level)
  no operation moved by 1% of the time
where the time goes in v14:
time: 136 us
  waiting for transfers between devices  53.1 us (39%)
  Pallas kernels  43.9 us (32%)
  starting transfers between devices  37.7 us (28%)
    ppermute x31, waiting for transfers between devices, shifted(): lax.ppermute(block, axis, [((i - distance) % size, i) for i in range(size)])  53.1 us
    ppermute x31, starting transfers between devices, shifted(): lax.ppermute(block, axis, [((i - distance) % size, i) for i in range(size)])  37.7 us
    pallas_call x17, Pallas kernels, call(): pl.pallas_call(kernel, out_shape=outs, in_specs=[anywhere if i in any_arg...  30.5 us
    pallas_call x3, Pallas kernels, chunked_call(): pl.pallas_call(kernel, grid=(steps,), out_shape=[jax.ShapeDtypeStruct(s,...  13.4 us
  transfers between devices with their start and end apart: 31, of which 20 were waited for; matrix products, arithmetic and copies ran while one was open for 0% of the time, Pallas kernels for 31%

profile of v14, /device:TPU:0, one launch (start us, length us, event | category | flops | bytes accessed | tf_op | source)
XLA Modules:
  0.0 135.7 jit_solution(6822467087134782018)
XLA Ops:
  0.6 5.1 %collective-permute-start.8 = (bf16[128,5120]{1,0:T(8,128)(2,1)}, bf16[128,5120]{1,0:T(8,128)(2,1)S(1)}, u32[]{:S(2)}, u32[]{:S(2)}) collective-permute-start(bf16[128,5120]{1,0:T(8,128)(2,1)} %param.8), channel_id=1, source_target_pairs={{8,0},{16,8},{24,16},{0,24},{9,1},{17,9},{25,17},{1,25},{10,2},{18... | collective-permute-start | bytes 3932168 | tf_op jit(solution)/shard_map/ppermute | solution.py:27
  5.7 2.9 %shard_map.110 = (bf16[80,640]{1,0:T(8,128)(2,1)S(1)}, bf16[80,640]{1,0:T(8,128)(2,1)S(1)}, bf16[128,640]{1,0:T(8,128)(2,1)}) custom-call(bf16[128,5120]{1,0:T(8,128)(2,1)} %tokens.3, s32[2,4,128]{2,1,0:T(4,128)} %bitcast.8), custom_call_target="tpu_custom_call" | custom-call | bytes 1024 | tf_op jit(solution)/shard_map/pallas_call | solution.py:40
  8.6 0.1 collective-permute-start
  8.7 1.6 %collective-permute-start.1 = (bf16[80,640]{1,0:T(8,128)(2,1)S(1)}, bf16[80,640]{1,0:T(8,128)(2,1)S(1)}, u32[]{:S(2)}, u32[]{:S(2)}) collective-permute-start(bf16[80,640]{1,0:T(8,128)(2,1)S(1)} %get-tuple-element.46.refs_0_), channel_id=1, source_target_pairs={{4,0},{6,2},{0,4},{2,6},{5,1},{7,3},{1,5},{3,7},{12,8},{14,10},{8,... | collective-permute-start | bytes 307208 | tf_op jit(solution)/shard_map/ppermute | solution.py:27
  10.2 1.4 %collective-permute-start.2 = (bf16[80,640]{1,0:T(8,128)(2,1)S(1)}, bf16[80,640]{1,0:T(8,128)(2,1)S(1)}, u32[]{:S(2)}, u32[]{:S(2)}) collective-permute-start(bf16[80,640]{1,0:T(8,128)(2,1)S(1)} %get-tuple-element.46.refs_0_), channel_id=1, source_target_pairs={{2,0},{4,2},{6,4},{0,6},{3,1},{5,3},{7,5},{1,7},{10,8},{12,10},{14... | collective-permute-start | bytes 307208 | tf_op jit(solution)/shard_map/ppermute | solution.py:27
  11.6 1.6 %collective-permute-done.refs_1_ = bf16[80,640]{1,0:T(8,128)(2,1)S(1)} collective-permute-done((bf16[80,640]{1,0:T(8,128)(2,1)S(1)}, bf16[80,640]{1,0:T(8,128)(2,1)S(1)}, u32[]{:S(2)}, u32[]{:S(2)}) %collective-permute-start) | collective-permute-done | bytes 102432 | tf_op jit(solution)/shard_map/ppermute | solution.py:27
  13.2 1.2 collective-permute-done.1.refs_2_
  14.4 0.6 collective-permute-done.2.refs_3_
  15.1 6.5 %shard_map.111 = (bf16[48,5120]{1,0:T(8,128)(2,1)S(1)}, f32[48,512]{1,0:T(8,128)S(1)}, f32[48,512]{1,0:T(8,128)S(1)}, bf16[48,512]{1,0:T(8,128)(2,1)S(1)}, bf16[...) custom-call(bf16[80,640]{1,0:T(8,128)(2,1)S(1)} %get-tuple-element.4, ...), custom_call_target="tpu_custom_call" | custom-call | bytes 1024 | tf_op jit(solution)/shard_map/pallas_call | solution.py:40
  21.6 2.3 %collective-permute-start.3 = (bf16[80,640]{1,0:T(8,128)(2,1)S(1)}, bf16[80,640]{1,0:T(8,128)(2,1)S(1)}, u32[]{:S(2)}, u32[]{:S(2)}) collective-permute-start(bf16[80,640]{1,0:T(8,128)(2,1)S(1)} %get-tuple-element.48), channel_id=1, source_target_pairs={{2,0},{4,2},{6,4},{0,6},{3,1},{5,3},{7,5},{1,7},{10,8},{12,10},{14... | collective-permute-start | bytes 307208 | tf_op jit(solution)/shard_map/ppermute | solution.py:27
  23.9 0.5 collective-permute-start.4
  24.4 0.5 collective-permute-start.6
  24.9 9.2 %collective-permute-done.6.refs_8_.next_routes = s32[1,4,128]{2,1,0:T(4,128)S(1)} collective-permute-done((s32[1,4,128]{2,1,0:T(4,128)S(1)}, s32[1,4,128]{2,1,0:T(4,128)S(1)}, u32[]{:S(2)}, u32[]{:S(2)}) %collective-permute-start.6) | collective-permute-done | bytes 2080 | tf_op jit(solution)/shard_map/ppermute | solution.py:27
  34.1 1.4 %collective-permute-start.16 = (bf16[128,640]{1,0:T(8,128)(2,1)S(1)}, bf16[128,640]{1,0:T(8,128)(2,1)S(1)}, u32[]{:S(2)}, u32[]{:S(2)}) collective-permute-start(bf16[128,640]{1,0:T(8,128)(2,1)S(1)} %copy-done.3), channel_id=1, source_target_pairs={{16,0},{24,8},{0,16},{8,24},{17,1},{25,9},{1,17},{9,25},{18,2},{26... | collective-permute-start | bytes 491528 | tf_op jit(solution)/shard_map/ppermute | solution.py:27
  35.5 0.7 shard_map.112
  36.2 3.4 %collective-permute-start.7 = (bf16[80,640]{1,0:T(8,128)(2,1)S(1)}, bf16[80,640]{1,0:T(8,128)(2,1)S(1)}, u32[]{:S(2)}, u32[]{:S(2)}) collective-permute-start(bf16[80,640]{1,0:T(8,128)(2,1)S(1)} %get-tuple-element.52), channel_id=1, source_target_pairs={{24,0},{0,8},{8,16},{16,24},{25,1},{1,9},{9,17},{17,25},{26,2},{2,... | collective-permute-start | bytes 307208 | tf_op jit(solution)/shard_map/ppermute | solution.py:27
  39.7 0.5 shard_map.113
  40.2 5.6 %collective-permute-done.16.__3_.early = bf16[128,640]{1,0:T(8,128)(2,1)S(1)} collective-permute-done((bf16[128,640]{1,0:T(8,128)(2,1)S(1)}, bf16[128,640]{1,0:T(8,128)(2,1)S(1)}, u32[]{:S(2)}, u32[]{:S(2)}) %collective-permute-start.16) | collective-permute-done | bytes 163872 | tf_op jit(solution)/shard_map/ppermute | solution.py:27
  45.8 1.3 collective-permute-start.17
  47.1 0.3 shard_map.114.refs_0_
  47.5 1.6 %collective-permute-start.10 = (bf16[160,640]{1,0:T(8,128)(2,1)S(1)}, bf16[160,640]{1,0:T(8,128)(2,1)S(1)}, u32[]{:S(2)}, u32[]{:S(2)}) collective-permute-start(bf16[160,640]{1,0:T(8,128)(2,1)S(1)} %shard_map.114.refs_0_), channel_id=1, source_target_pairs={{4,0},{6,2},{0,4},{2,6},{5,1},{7,3},{1,5},{3,7},{12,8},{14,10},{8,... | collective-permute-start | bytes 614408 | tf_op jit(solution)/shard_map/ppermute | solution.py:27
  49.1 1.4 %collective-permute-start.11 = (bf16[160,640]{1,0:T(8,128)(2,1)S(1)}, bf16[160,640]{1,0:T(8,128)(2,1)S(1)}, u32[]{:S(2)}, u32[]{:S(2)}) collective-permute-start(bf16[160,640]{1,0:T(8,128)(2,1)S(1)} %shard_map.114.refs_0_), channel_id=1, source_target_pairs={{2,0},{4,2},{6,4},{0,6},{3,1},{5,3},{7,5},{1,7},{10,8},{12,10},{14... | collective-permute-start | bytes 614408 | tf_op jit(solution)/shard_map/ppermute | solution.py:27
  50.5 3.8 %collective-permute-done.9.refs_1_ = bf16[160,640]{1,0:T(8,128)(2,1)S(1)} collective-permute-done((bf16[160,640]{1,0:T(8,128)(2,1)S(1)}, bf16[160,640]{1,0:T(8,128)(2,1)S(1)}, u32[]{:S(2)}, u32[]{:S(2)}) %collective-permute-start.9) | collective-permute-done | bytes 204832 | tf_op jit(solution)/shard_map/ppermute | solution.py:27
  54.3 1.2 collective-permute-done.10.refs_2_
  55.5 2.8 %collective-permute-done.11.refs_3_ = bf16[160,640]{1,0:T(8,128)(2,1)S(1)} collective-permute-done((bf16[160,640]{1,0:T(8,128)(2,1)S(1)}, bf16[160,640]{1,0:T(8,128)(2,1)S(1)}, u32[]{:S(2)}, u32[]{:S(2)}) %collective-permute-start.11) | collective-permute-done | bytes 204832 | tf_op jit(solution)/shard_map/ppermute | solution.py:27
  58.3 6.9 %shard_map.115 = (bf16[48,17408]{1,0:T(8,128)(2,1)S(1)}, bf16[80,640]{1,0:T(8,128)(2,1)S(1)}, bf16[80,640]{1,0:T(8,128)(2,1)S(1)}, bf16[80,640]{1,0:T(8,128)(2,1)S(1)}, bf16[80,640]{1,0:T(8,128)(2,1)S(1)}) custom-call(bf16[160,640]{1,0:T(8,128)(2,1)S(1)} %shard_map.114.refs_0_, bf16[160,640]{1,0:T(8,128)(2,1)S(1)} %collective-permute-done.9.refs_1_, ...), custom_call_target="tpu_custom_call" | custom-call | bytes 1024 | tf_op jit(solution)/shard_map/pallas_call | solution.py:40
  65.2 1.6 %collective-permute-start.29 = (bf16[48,17408]{1,0:T(8,128)(2,1)S(1)}, bf16[48,17408]{1,0:T(8,128)(2,1)S(1)}, u32[]{:S(2)}, u32[]{:S(2)}) collective-permute-start(bf16[48,17408]{1,0:T(8,128)(2,1)S(1)} %get-tuple-element.77.act.refs_0_.refs_2_.refs_4_.refs_6_), channel_id=1, source_target_pairs={{1,0},{0,1},{3,2},{2,3},{5,4},{4,5},{7,6},{6,7},{9,8},{8,9},{11,10... | collective-permute-start | bytes 5013512 | tf_op jit(solution)/shard_map/ppermute | solution.py:27
  66.7 1.9 %collective-permute-start.12 = (bf16[80,640]{1,0:T(8,128)(2,1)S(1)}, bf16[80,640]{1,0:T(8,128)(2,1)S(1)}, u32[]{:S(2)}, u32[]{:S(2)}) collective-permute-start(bf16[80,640]{1,0:T(8,128)(2,1)S(1)} %get-tuple-element.60), channel_id=1, source_target_pairs={{2,0},{4,2},{6,4},{0,6},{3,1},{5,3},{7,5},{1,7},{10,8},{12,10},{14... | collective-permute-start | bytes 307208 | tf_op jit(solution)/shard_map/ppermute | solution.py:27
  68.6 0.5 collective-permute-start.13
  69.2 2.4 %collective-permute-done.12.refs_1_ = bf16[80,640]{1,0:T(8,128)(2,1)S(1)} collective-permute-done((bf16[80,640]{1,0:T(8,128)(2,1)S(1)}, bf16[80,640]{1,0:T(8,128)(2,1)S(1)}, u32[]{:S(2)}, u32[]{:S(2)}) %collective-permute-start.12) | collective-permute-done | bytes 102432 | tf_op jit(solution)/shard_map/ppermute | solution.py:27
  71.5 3.0 %collective-permute-done.13.refs_2_ = bf16[80,640]{1,0:T(8,128)(2,1)S(1)} collective-permute-done((bf16[80,640]{1,0:T(8,128)(2,1)S(1)}, bf16[80,640]{1,0:T(8,128)(2,1)S(1)}, u32[]{:S(2)}, u32[]{:S(2)}) %collective-permute-start.13) | collective-permute-done | bytes 102432 | tf_op jit(solution)/shard_map/ppermute | solution.py:27
  74.5 0.4 shard_map.116
  75.0 1.8 %collective-permute-start.15 = (bf16[80,640]{1,0:T(8,128)(2,1)S(1)}, bf16[80,640]{1,0:T(8,128)(2,1)S(1)}, u32[]{:S(2)}, u32[]{:S(2)}) collective-permute-start(bf16[80,640]{1,0:T(8,128)(2,1)S(1)} %shard_map.116), channel_id=1, source_target_pairs={{8,0},{16,8},{24,16},{0,24},{9,1},{17,9},{25,17},{1,25},{10,2},{18... | collective-permute-start | bytes 307208 | tf_op jit(solution)/shard_map/ppermute | solution.py:27
  76.8 0.7 shard_map.118.__0_
  77.5 2.2 %collective-permute-done.15.__2_.upd1.refs_7_ = bf16[80,640]{1,0:T(8,128)(2,1)S(1)} collective-permute-done((bf16[80,640]{1,0:T(8,128)(2,1)S(1)}, bf16[80,640]{1,0:T(8,128)(2,1)S(1)}, u32[]{:S(2)}, u32[]{:S(2)}) %collective-permute-start.15) | collective-permute-done | bytes 102432 | tf_op jit(solution)/shard_map/ppermute | solution.py:27
  79.7 0.4 collective-permute-start.24
  80.1 0.8 shard_map.120
  80.9 0.1 collective-permute-start.18
  81.0 1.6 %collective-permute-start.19 = (bf16[80,640]{1,0:T(8,128)(2,1)S(1)}, bf16[80,640]{1,0:T(8,128)(2,1)S(1)}, u32[]{:S(2)}, u32[]{:S(2)}) collective-permute-start(bf16[80,640]{1,0:T(8,128)(2,1)S(1)} %get-tuple-element.66.refs_0_), channel_id=1, source_target_pairs={{4,0},{6,2},{0,4},{2,6},{5,1},{7,3},{1,5},{3,7},{12,8},{14,10},{8,... | collective-permute-start | bytes 307208 | tf_op jit(solution)/shard_map/ppermute | solution.py:27
  82.6 1.4 %collective-permute-start.20 = (bf16[80,640]{1,0:T(8,128)(2,1)S(1)}, bf16[80,640]{1,0:T(8,128)(2,1)S(1)}, u32[]{:S(2)}, u32[]{:S(2)}) collective-permute-start(bf16[80,640]{1,0:T(8,128)(2,1)S(1)} %get-tuple-element.66.refs_0_), channel_id=1, source_target_pairs={{2,0},{4,2},{6,4},{0,6},{3,1},{5,3},{7,5},{1,7},{10,8},{12,10},{14... | collective-permute-start | bytes 307208 | tf_op jit(solution)/shard_map/ppermute | solution.py:27
  83.9 1.6 %collective-permute-done.18.refs_1_ = bf16[80,640]{1,0:T(8,128)(2,1)S(1)} collective-permute-done((bf16[80,640]{1,0:T(8,128)(2,1)S(1)}, bf16[80,640]{1,0:T(8,128)(2,1)S(1)}, u32[]{:S(2)}, u32[]{:S(2)}) %collective-permute-start.18) | collective-permute-done | bytes 102432 | tf_op jit(solution)/shard_map/ppermute | solution.py:27
  85.5 1.2 collective-permute-done.19.refs_2_
  86.7 0.6 collective-permute-done.20.refs_3_
  87.4 5.0 %shard_map.121 = (bf16[48,6144]{1,0:T(8,128)(2,1)S(1)}, bf16[80,640]{1,0:T(8,128)(2,1)S(1)}, bf16[80,640]{1,0:T(8,128)(2,1)S(1)}, bf16[80,640]{1,0:T(8,128)(2,1)S(1)}, bf16[80,640]{1,0:T(8,128)(2,1)S(1)}) custom-call(bf16[80,640]{1,0:T(8,128)(2,1)S(1)} %get-tuple-element.66.refs_0_, bf16[80,640]{1,0:T(8,128)(2,1)S(1)} %collective-permute-done.18.refs_1_, ...), custom_call_target="tpu_custom_call" | custom-call | bytes 1024 | tf_op jit(solution)/shard_map/pallas_call | solution.py:40
  92.4 1.6 %collective-permute-start.30 = (bf16[48,6144]{1,0:T(8,128)(2,1)S(1)}, bf16[48,6144]{1,0:T(8,128)(2,1)S(1)}, u32[]{:S(2)}, u32[]{:S(2)}) collective-permute-start(bf16[48,6144]{1,0:T(8,128)(2,1)S(1)} %get-tuple-element.78._.refs_0_.refs_2_), channel_id=1, source_target_pairs={{1,0},{0,1},{3,2},{2,3},{5,4},{4,5},{7,6},{6,7},{9,8},{8,9},{11,10... | collective-permute-start | bytes 1769480 | tf_op jit(solution)/shard_map/ppermute | solution.py:27
  94.0 1.9 %collective-permute-start.21 = (bf16[80,640]{1,0:T(8,128)(2,1)S(1)}, bf16[80,640]{1,0:T(8,128)(2,1)S(1)}, u32[]{:S(2)}, u32[]{:S(2)}) collective-permute-start(bf16[80,640]{1,0:T(8,128)(2,1)S(1)} %get-tuple-element.70), channel_id=1, source_target_pairs={{2,0},{4,2},{6,4},{0,6},{3,1},{5,3},{7,5},{1,7},{10,8},{12,10},{14... | collective-permute-start | bytes 307208 | tf_op jit(solution)/shard_map/ppermute | solution.py:27
  95.9 1.1 shard_map.124
  97.0 0.1 collective-permute-start.25
  97.1 1.1 collective-permute-done.21.refs_1_
  98.2 0.5 collective-permute-start.26
  98.7 0.6 collective-permute-done.25.refs_1_
  99.3 1.1 collective-permute-start.27
  100.4 3.5 %collective-permute-done.26.refs_2_ = bf16[80,640]{1,0:T(8,128)(2,1)S(1)} collective-permute-done((bf16[80,640]{1,0:T(8,128)(2,1)S(1)}, bf16[80,640]{1,0:T(8,128)(2,1)S(1)}, u32[]{:S(2)}, u32[]{:S(2)}) %collective-permute-start.26) | collective-permute-done | bytes 102432 | tf_op jit(solution)/shard_map/ppermute | solution.py:27
  103.9 1.1 collective-permute-done.27.refs_3_
  105.0 0.2 shard_map.125
  105.3 4.3 %collective-permute-done.22.refs_2_ = bf16[80,640]{1,0:T(8,128)(2,1)S(1)} collective-permute-done((bf16[80,640]{1,0:T(8,128)(2,1)S(1)}, bf16[80,640]{1,0:T(8,128)(2,1)S(1)}, u32[]{:S(2)}, u32[]{:S(2)}) %collective-permute-start.22) | collective-permute-done | bytes 102432 | tf_op jit(solution)/shard_map/ppermute | solution.py:27
  109.6 2.7 %collective-permute-start.28 = (bf16[80,640]{1,0:T(8,128)(2,1)S(1)}, bf16[80,640]{1,0:T(8,128)(2,1)S(1)}, u32[]{:S(2)}, u32[]{:S(2)}) collective-permute-start(bf16[80,640]{1,0:T(8,128)(2,1)S(1)} %shard_map.125), channel_id=1, source_target_pairs={{24,0},{0,8},{8,16},{16,24},{25,1},{1,9},{9,17},{17,25},{26,2},{2,... | collective-permute-start | bytes 307208 | tf_op jit(solution)/shard_map/ppermute | solution.py:27
  112.3 2.4 %shard_map.122 = bf16[128,5120]{1,0:T(8,128)(2,1)} custom-call(bf16[80,640]{1,0:T(8,128)(2,1)S(1)} %get-tuple-element.69.refs_0_, bf16[80,640]{1,0:T(8,128)(2,1)S(1)} %collective-permute-done.21.refs_1_, bf16[80,640]{1,0:T(8,128)(2,1)S(1)} %collective-permute-done.22.refs_2_, bf16[80,640]{1,0:T(8,128)(2,1)S(1)} %collective-permute-done.23.refs_3_, ...), custom_call_target="tpu_custom_call" | custom-call | bytes 1024 | tf_op jit(solution)/shard_map/pallas_call | solution.py:40
  114.7 3.1 %shard_map.127 = (bf16[5120,192]{1,0:T(8,128)(2,1)S(1)}, bf16[512,192]{1,0:T(8,128)(2,1)S(1)}) custom-call(bf16[48,17408]{1,0:T(8,128)(2,1)S(1)} %get-tuple-element.77.act.refs_0_.refs_2_.refs_4_.refs_6_, bf16[48,17408]{1,0:T(8,128)(2,1)S(1)} %collective-permute-done.29.refs_1_.refs_3_.refs_5_.refs_7_, ...), custom_call_target="tpu_custom_call" | custom-call | bytes 1024 | tf_op jit(solution)/shard_map/pallas_call | solution.py:457
  117.8 6.2 %shard_map.128 = (bf16[5120,512]{1,0:T(8,128)(2,1)}, bf16[5120,512]{1,0:T(8,128)(2,1)}) custom-call(bf16[5120,192]{1,0:T(8,128)(2,1)S(1)} %get-tuple-element.83.x_t, bf16[48,6144]{1,0:T(8,128)(2,1)S(1)} %get-tuple-element.78._.refs_0_.refs_2_, bf16[48,6144]{1,0:T(8,128)(2,1)S(1)} %collective-permute-done.30.refs_1_.refs_3_, ...), custom_call_target="tpu_custom_call" | custom-call | bytes 1024 | tf_op jit(solution)/shard_map/pallas_call | solution.py:457
  124.1 4.1 %shard_map.129 = bf16[512,5120]{1,0:T(8,128)(2,1)} custom-call(bf16[512,192]{1,0:T(8,128)(2,1)S(1)} %get-tuple-element.86.act_t, bf16[48,6144]{1,0:T(8,128)(2,1)S(1)} %get-tuple-element.78._.refs_0_.refs_2_, bf16[48,6144]{1,0:T(8,128)(2,1)S(1)} %collective-permute-done.30.refs_1_.refs_3_, ...), custom_call_target="tpu_custom_call" | custom-call | bytes 1024 | tf_op jit(solution)/shard_map/pallas_call | solution.py:457
  128.2 5.4 %collective-permute-done.24.rest = bf16[912,640]{1,0:T(8,128)(2,1)S(1)} collective-permute-done((bf16[912,640]{1,0:T(8,128)(2,1)S(1)}, bf16[912,640]{1,0:T(8,128)(2,1)S(1)}, u32[]{:S(2)}, u32[]{:S(2)}) %collective-permute-start.24) | collective-permute-done | bytes 1167392 | tf_op jit(solution)/shard_map/ppermute | solution.py:27
  133.6 0.5 shard_map.123
  134.1 1.4 %shard_map.126 = bf16[128,5120]{1,0:T(8,128)(2,1)} custom-call(bf16[128,5120]{1,0:T(8,128)(2,1)S(1)} %get-tuple-element.74.base, f32[128,80]{1,0:T(8,128)S(1)} %get-tuple-element.75.turned_select, f32[128,128]{1,0:T(8,128)S(1)} %get-tuple-element.76.hit, bf16[80,640]{1,0:T(8,128)(2,1)S(1)} %collective-permute-done.28.upd1), custom_call_target="tpu_custom_call" | custom-call | bytes 1024 | tf_op jit(solution)/shard_map/pallas_call | solution.py:40
  (27 shorter events, 0.1 us)
Async XLA Ops:
  0.6 39.0 %collective-permute-start.8 = (bf16[128,5120]{1,0:T(8,128)(2,1)}, bf16[128,5120]{1,0:T(8,128)(2,1)S(1)}, u32[]{:S(2)}, u32[]{:S(2)}) collective-permute-start(bf16[128,5120]{1,0:T(8,128)(2,1)} %param.8), channel_id=1, source_target_pairs={{8,0},{16,8},{24,16},{0,24},{9,1},{17,9},{25,17},{1,25},{10,2},{18... | collective-permute-start | bytes 3932168 | tf_op jit(solution)/shard_map/ppermute | solution.py:27
  8.6 4.6 %collective-permute-start = (bf16[80,640]{1,0:T(8,128)(2,1)S(1)}, bf16[80,640]{1,0:T(8,128)(2,1)S(1)}, u32[]{:S(2)}, u32[]{:S(2)}) collective-permute-start(bf16[80,640]{1,0:T(8,128)(2,1)S(1)} %get-tuple-element.46.refs_0_), channel_id=1, source_target_pairs={{6,0},{0,2},{2,4},{4,6},{7,1},{1,3},{3,5},{5,7},{14,8},{8,10},{10,... | collective-permute-start | bytes 307208 | tf_op jit(solution)/shard_map/ppermute | solution.py:27
  8.7 5.8 %collective-permute-start.1 = (bf16[80,640]{1,0:T(8,128)(2,1)S(1)}, bf16[80,640]{1,0:T(8,128)(2,1)S(1)}, u32[]{:S(2)}, u32[]{:S(2)}) collective-permute-start(bf16[80,640]{1,0:T(8,128)(2,1)S(1)} %get-tuple-element.46.refs_0_), channel_id=1, source_target_pairs={{4,0},{6,2},{0,4},{2,6},{5,1},{7,3},{1,5},{3,7},{12,8},{14,10},{8,... | collective-permute-start | bytes 307208 | tf_op jit(solution)/shard_map/ppermute | solution.py:27
  10.2 4.8 %collective-permute-start.2 = (bf16[80,640]{1,0:T(8,128)(2,1)S(1)}, bf16[80,640]{1,0:T(8,128)(2,1)S(1)}, u32[]{:S(2)}, u32[]{:S(2)}) collective-permute-start(bf16[80,640]{1,0:T(8,128)(2,1)S(1)} %get-tuple-element.46.refs_0_), channel_id=1, source_target_pairs={{2,0},{4,2},{6,4},{0,6},{3,1},{5,3},{7,5},{1,7},{10,8},{12,10},{14... | collective-permute-start | bytes 307208 | tf_op jit(solution)/shard_map/ppermute | solution.py:27
  15.1 9.3 %copy-start.1 = (s32[2,128,4]{1,2,0:T(4,128)S(1)}, s32[2,128,4]{1,2,0:T(4,128)}, u32[]{:S(2)}) copy-start(s32[2,128,4]{1,2,0:T(4,128)} %param.12) | copy-start | bytes 12292
  15.1 19.0 %copy-start.3 = (bf16[128,640]{1,0:T(8,128)(2,1)S(1)}, bf16[128,640]{1,0:T(8,128)(2,1)}, u32[]{:S(2)}) copy-start(bf16[128,640]{1,0:T(8,128)(2,1)} %get-tuple-element.64) | copy-start | bytes 491524
  15.1 20.4 %copy-start = (bf16[128,5120]{1,0:T(8,128)(2,1)S(1)}, bf16[128,5120]{1,0:T(8,128)(2,1)}, u32[]{:S(2)}) copy-start(bf16[128,5120]{1,0:T(8,128)(2,1)} %tokens.3) | copy-start | bytes 3932164
  15.1 20.5 %copy-start.2 = (f32[2,128,4]{1,2,0:T(4,128)S(1)}, f32[2,128,4]{1,2,0:T(4,128)}, u32[]{:S(2)}) copy-start(f32[2,128,4]{1,2,0:T(4,128)} %param.13) | copy-start | bytes 12292
  21.6 13.9 %collective-permute-start.3 = (bf16[80,640]{1,0:T(8,128)(2,1)S(1)}, bf16[80,640]{1,0:T(8,128)(2,1)S(1)}, u32[]{:S(2)}, u32[]{:S(2)}) collective-permute-start(bf16[80,640]{1,0:T(8,128)(2,1)S(1)} %get-tuple-element.48), channel_id=1, source_target_pairs={{2,0},{4,2},{6,4},{0,6},{3,1},{5,3},{7,5},{1,7},{10,8},{12,10},{14... | collective-permute-start | bytes 307208 | tf_op jit(solution)/shard_map/ppermute | solution.py:27
  23.9 11.6 %collective-permute-start.4 = (bf16[80,640]{1,0:T(8,128)(2,1)S(1)}, bf16[80,640]{1,0:T(8,128)(2,1)S(1)}, u32[]{:S(2)}, u32[]{:S(2)}) collective-permute-start(bf16[80,640]{1,0:T(8,128)(2,1)S(1)} %get-tuple-element.49), channel_id=1, source_target_pairs={{4,0},{6,2},{0,4},{2,6},{5,1},{7,3},{1,5},{3,7},{12,8},{14,10},{8,... | collective-permute-start | bytes 307208 | tf_op jit(solution)/shard_map/ppermute | solution.py:27
  24.4 11.1 %collective-permute-start.5 = (bf16[80,640]{1,0:T(8,128)(2,1)S(1)}, bf16[80,640]{1,0:T(8,128)(2,1)S(1)}, u32[]{:S(2)}, u32[]{:S(2)}) collective-permute-start(bf16[80,640]{1,0:T(8,128)(2,1)S(1)} %get-tuple-element.50), channel_id=1, source_target_pairs={{6,0},{0,2},{2,4},{4,6},{7,1},{1,3},{3,5},{5,7},{14,8},{8,10},{10,... | collective-permute-start | bytes 307208 | tf_op jit(solution)/shard_map/ppermute | solution.py:27
  24.4 9.7 %collective-permute-start.6 = (s32[1,4,128]{2,1,0:T(4,128)S(1)}, s32[1,4,128]{2,1,0:T(4,128)S(1)}, u32[]{:S(2)}, u32[]{:S(2)}) collective-permute-start(s32[1,4,128]{2,1,0:T(4,128)S(1)} %slice.4), channel_id=1, source_target_pairs={{8,0},{16,8},{24,16},{0,24},{9,1},{17,9},{25,17},{1,25},{10,2},{18... | collective-permute-start | bytes 6152 | tf_op jit(solution)/shard_map/ppermute | solution.py:27
  34.1 11.7 %collective-permute-start.16 = (bf16[128,640]{1,0:T(8,128)(2,1)S(1)}, bf16[128,640]{1,0:T(8,128)(2,1)S(1)}, u32[]{:S(2)}, u32[]{:S(2)}) collective-permute-start(bf16[128,640]{1,0:T(8,128)(2,1)S(1)} %copy-done.3), channel_id=1, source_target_pairs={{16,0},{24,8},{0,16},{8,24},{17,1},{25,9},{1,17},{9,25},{18,2},{26... | collective-permute-start | bytes 491528 | tf_op jit(solution)/shard_map/ppermute | solution.py:27
  36.2 9.5 %collective-permute-start.7 = (bf16[80,640]{1,0:T(8,128)(2,1)S(1)}, bf16[80,640]{1,0:T(8,128)(2,1)S(1)}, u32[]{:S(2)}, u32[]{:S(2)}) collective-permute-start(bf16[80,640]{1,0:T(8,128)(2,1)S(1)} %get-tuple-element.52), channel_id=1, source_target_pairs={{24,0},{0,8},{8,16},{16,24},{25,1},{1,9},{9,17},{17,25},{26,2},{2,... | collective-permute-start | bytes 307208 | tf_op jit(solution)/shard_map/ppermute | solution.py:27
  45.8 33.9 %collective-permute-start.17 = (bf16[128,5120]{1,0:T(8,128)(2,1)S(1)}, bf16[128,5120]{1,0:T(8,128)(2,1)S(1)}, u32[]{:S(2)}, u32[]{:S(2)}) collective-permute-start(bf16[128,5120]{1,0:T(8,128)(2,1)S(1)} %shard_map.117), channel_id=1, source_target_pairs={{8,0},{16,8},{24,16},{0,24},{9,1},{17,9},{25,17},{1,25},{10,2},{18... | collective-permute-start | bytes 3932168 | tf_op jit(solution)/shard_map/ppermute | solution.py:27
  47.4 6.8 %collective-permute-start.9 = (bf16[160,640]{1,0:T(8,128)(2,1)S(1)}, bf16[160,640]{1,0:T(8,128)(2,1)S(1)}, u32[]{:S(2)}, u32[]{:S(2)}) collective-permute-start(bf16[160,640]{1,0:T(8,128)(2,1)S(1)} %shard_map.114.refs_0_), channel_id=1, source_target_pairs={{6,0},{0,2},{2,4},{4,6},{7,1},{1,3},{3,5},{5,7},{14,8},{8,10},{10,... | collective-permute-start | bytes 614408 | tf_op jit(solution)/shard_map/ppermute | solution.py:27
  47.5 8.0 %collective-permute-start.10 = (bf16[160,640]{1,0:T(8,128)(2,1)S(1)}, bf16[160,640]{1,0:T(8,128)(2,1)S(1)}, u32[]{:S(2)}, u32[]{:S(2)}) collective-permute-start(bf16[160,640]{1,0:T(8,128)(2,1)S(1)} %shard_map.114.refs_0_), channel_id=1, source_target_pairs={{4,0},{6,2},{0,4},{2,6},{5,1},{7,3},{1,5},{3,7},{12,8},{14,10},{8,... | collective-permute-start | bytes 614408 | tf_op jit(solution)/shard_map/ppermute | solution.py:27
  49.1 9.2 %collective-permute-start.11 = (bf16[160,640]{1,0:T(8,128)(2,1)S(1)}, bf16[160,640]{1,0:T(8,128)(2,1)S(1)}, u32[]{:S(2)}, u32[]{:S(2)}) collective-permute-start(bf16[160,640]{1,0:T(8,128)(2,1)S(1)} %shard_map.114.refs_0_), channel_id=1, source_target_pairs={{2,0},{4,2},{6,4},{0,6},{3,1},{5,3},{7,5},{1,7},{10,8},{12,10},{14... | collective-permute-start | bytes 614408 | tf_op jit(solution)/shard_map/ppermute | solution.py:27
  65.2 49.6 %collective-permute-start.29 = (bf16[48,17408]{1,0:T(8,128)(2,1)S(1)}, bf16[48,17408]{1,0:T(8,128)(2,1)S(1)}, u32[]{:S(2)}, u32[]{:S(2)}) collective-permute-start(bf16[48,17408]{1,0:T(8,128)(2,1)S(1)} %get-tuple-element.77.act.refs_0_.refs_2_.refs_4_.refs_6_), channel_id=1, source_target_pairs={{1,0},{0,1},{3,2},{2,3},{5,4},{4,5},{7,6},{6,7},{9,8},{8,9},{11,10... | collective-permute-start | bytes 5013512 | tf_op jit(solution)/shard_map/ppermute | solution.py:27
  66.7 4.8 %collective-permute-start.12 = (bf16[80,640]{1,0:T(8,128)(2,1)S(1)}, bf16[80,640]{1,0:T(8,128)(2,1)S(1)}, u32[]{:S(2)}, u32[]{:S(2)}) collective-permute-start(bf16[80,640]{1,0:T(8,128)(2,1)S(1)} %get-tuple-element.60), channel_id=1, source_target_pairs={{2,0},{4,2},{6,4},{0,6},{3,1},{5,3},{7,5},{1,7},{10,8},{12,10},{14... | collective-permute-start | bytes 307208 | tf_op jit(solution)/shard_map/ppermute | solution.py:27
  68.6 5.9 %collective-permute-start.13 = (bf16[80,640]{1,0:T(8,128)(2,1)S(1)}, bf16[80,640]{1,0:T(8,128)(2,1)S(1)}, u32[]{:S(2)}, u32[]{:S(2)}) collective-permute-start(bf16[80,640]{1,0:T(8,128)(2,1)S(1)} %get-tuple-element.61), channel_id=1, source_target_pairs={{4,0},{6,2},{0,4},{2,6},{5,1},{7,3},{1,5},{3,7},{12,8},{14,10},{8,... | collective-permute-start | bytes 307208 | tf_op jit(solution)/shard_map/ppermute | solution.py:27
  69.1 5.4 %collective-permute-start.14 = (bf16[80,640]{1,0:T(8,128)(2,1)S(1)}, bf16[80,640]{1,0:T(8,128)(2,1)S(1)}, u32[]{:S(2)}, u32[]{:S(2)}) collective-permute-start(bf16[80,640]{1,0:T(8,128)(2,1)S(1)} %get-tuple-element.62), channel_id=1, source_target_pairs={{6,0},{0,2},{2,4},{4,6},{7,1},{1,3},{3,5},{5,7},{14,8},{8,10},{10,... | collective-permute-start | bytes 307208 | tf_op jit(solution)/shard_map/ppermute | solution.py:27
  75.0 4.7 %collective-permute-start.15 = (bf16[80,640]{1,0:T(8,128)(2,1)S(1)}, bf16[80,640]{1,0:T(8,128)(2,1)S(1)}, u32[]{:S(2)}, u32[]{:S(2)}) collective-permute-start(bf16[80,640]{1,0:T(8,128)(2,1)S(1)} %shard_map.116), channel_id=1, source_target_pairs={{8,0},{16,8},{24,16},{0,24},{9,1},{17,9},{25,17},{1,25},{10,2},{18... | collective-permute-start | bytes 307208 | tf_op jit(solution)/shard_map/ppermute | solution.py:27
  79.7 53.9 %collective-permute-start.24 = (bf16[912,640]{1,0:T(8,128)(2,1)S(1)}, bf16[912,640]{1,0:T(8,128)(2,1)S(1)}, u32[]{:S(2)}, u32[]{:S(2)}) collective-permute-start(bf16[912,640]{1,0:T(8,128)(2,1)S(1)} %shard_map.119._), channel_id=1, source_target_pairs={{16,0},{24,8},{0,16},{8,24},{17,1},{25,9},{1,17},{9,25},{18,2},{26... | collective-permute-start | bytes 3502088 | tf_op jit(solution)/shard_map/ppermute | solution.py:27
  80.9 4.6 %collective-permute-start.18 = (bf16[80,640]{1,0:T(8,128)(2,1)S(1)}, bf16[80,640]{1,0:T(8,128)(2,1)S(1)}, u32[]{:S(2)}, u32[]{:S(2)}) collective-permute-start(bf16[80,640]{1,0:T(8,128)(2,1)S(1)} %get-tuple-element.66.refs_0_), channel_id=1, source_target_pairs={{6,0},{0,2},{2,4},{4,6},{7,1},{1,3},{3,5},{5,7},{14,8},{8,10},{10,... | collective-permute-start | bytes 307208 | tf_op jit(solution)/shard_map/ppermute | solution.py:27
  81.0 5.8 %collective-permute-start.19 = (bf16[80,640]{1,0:T(8,128)(2,1)S(1)}, bf16[80,640]{1,0:T(8,128)(2,1)S(1)}, u32[]{:S(2)}, u32[]{:S(2)}) collective-permute-start(bf16[80,640]{1,0:T(8,128)(2,1)S(1)} %get-tuple-element.66.refs_0_), channel_id=1, source_target_pairs={{4,0},{6,2},{0,4},{2,6},{5,1},{7,3},{1,5},{3,7},{12,8},{14,10},{8,... | collective-permute-start | bytes 307208 | tf_op jit(solution)/shard_map/ppermute | solution.py:27
  82.6 4.8 %collective-permute-start.20 = (bf16[80,640]{1,0:T(8,128)(2,1)S(1)}, bf16[80,640]{1,0:T(8,128)(2,1)S(1)}, u32[]{:S(2)}, u32[]{:S(2)}) collective-permute-start(bf16[80,640]{1,0:T(8,128)(2,1)S(1)} %get-tuple-element.66.refs_0_), channel_id=1, source_target_pairs={{2,0},{4,2},{6,4},{0,6},{3,1},{5,3},{7,5},{1,7},{10,8},{12,10},{14... | collective-permute-start | bytes 307208 | tf_op jit(solution)/shard_map/ppermute | solution.py:27
  92.4 25.4 %collective-permute-start.30 = (bf16[48,6144]{1,0:T(8,128)(2,1)S(1)}, bf16[48,6144]{1,0:T(8,128)(2,1)S(1)}, u32[]{:S(2)}, u32[]{:S(2)}) collective-permute-start(bf16[48,6144]{1,0:T(8,128)(2,1)S(1)} %get-tuple-element.78._.refs_0_.refs_2_), channel_id=1, source_target_pairs={{1,0},{0,1},{3,2},{2,3},{5,4},{4,5},{7,6},{6,7},{9,8},{8,9},{11,10... | collective-permute-start | bytes 1769480 | tf_op jit(solution)/shard_map/ppermute | solution.py:27
  94.0 4.2 %collective-permute-start.21 = (bf16[80,640]{1,0:T(8,128)(2,1)S(1)}, bf16[80,640]{1,0:T(8,128)(2,1)S(1)}, u32[]{:S(2)}, u32[]{:S(2)}) collective-permute-start(bf16[80,640]{1,0:T(8,128)(2,1)S(1)} %get-tuple-element.70), channel_id=1, source_target_pairs={{2,0},{4,2},{6,4},{0,6},{3,1},{5,3},{7,5},{1,7},{10,8},{12,10},{14... | collective-permute-start | bytes 307208 | tf_op jit(solution)/shard_map/ppermute | solution.py:27
  97.0 2.3 %collective-permute-start.25 = (bf16[80,640]{1,0:T(8,128)(2,1)S(1)}, bf16[80,640]{1,0:T(8,128)(2,1)S(1)}, u32[]{:S(2)}, u32[]{:S(2)}) collective-permute-start(bf16[80,640]{1,0:T(8,128)(2,1)S(1)} %get-tuple-element.80), channel_id=1, source_target_pairs={{2,0},{4,2},{6,4},{0,6},{3,1},{5,3},{7,5},{1,7},{10,8},{12,10},{14... | collective-permute-start | bytes 307208 | tf_op jit(solution)/shard_map/ppermute | solution.py:27
  98.2 5.7 %collective-permute-start.26 = (bf16[80,640]{1,0:T(8,128)(2,1)S(1)}, bf16[80,640]{1,0:T(8,128)(2,1)S(1)}, u32[]{:S(2)}, u32[]{:S(2)}) collective-permute-start(bf16[80,640]{1,0:T(8,128)(2,1)S(1)} %get-tuple-element.81), channel_id=1, source_target_pairs={{4,0},{6,2},{0,4},{2,6},{5,1},{7,3},{1,5},{3,7},{12,8},{14,10},{8,... | collective-permute-start | bytes 307208 | tf_op jit(solution)/shard_map/ppermute | solution.py:27
  99.3 5.7 %collective-permute-start.27 = (bf16[80,640]{1,0:T(8,128)(2,1)S(1)}, bf16[80,640]{1,0:T(8,128)(2,1)S(1)}, u32[]{:S(2)}, u32[]{:S(2)}) collective-permute-start(bf16[80,640]{1,0:T(8,128)(2,1)S(1)} %get-tuple-element.82), channel_id=1, source_target_pairs={{6,0},{0,2},{2,4},{4,6},{7,1},{1,3},{3,5},{5,7},{14,8},{8,10},{10,... | collective-permute-start | bytes 307208 | tf_op jit(solution)/shard_map/ppermute | solution.py:27
  103.9 5.7 %collective-permute-start.22 = (bf16[80,640]{1,0:T(8,128)(2,1)S(1)}, bf16[80,640]{1,0:T(8,128)(2,1)S(1)}, u32[]{:S(2)}, u32[]{:S(2)}) collective-permute-start(bf16[80,640]{1,0:T(8,128)(2,1)S(1)} %get-tuple-element.71), channel_id=1, source_target_pairs={{4,0},{6,2},{0,4},{2,6},{5,1},{7,3},{1,5},{3,7},{12,8},{14,10},{8,... | collective-permute-start | bytes 307208 | tf_op jit(solution)/shard_map/ppermute | solution.py:27
  105.0 7.3 %collective-permute-start.23 = (bf16[80,640]{1,0:T(8,128)(2,1)S(1)}, bf16[80,640]{1,0:T(8,128)(2,1)S(1)}, u32[]{:S(2)}, u32[]{:S(2)}) collective-permute-start(bf16[80,640]{1,0:T(8,128)(2,1)S(1)} %get-tuple-element.72), channel_id=1, source_target_pairs={{6,0},{0,2},{2,4},{4,6},{7,1},{1,3},{3,5},{5,7},{14,8},{8,10},{10,... | collective-permute-start | bytes 307208 | tf_op jit(solution)/shard_map/ppermute | solution.py:27
  109.6 24.5 %collective-permute-start.28 = (bf16[80,640]{1,0:T(8,128)(2,1)S(1)}, bf16[80,640]{1,0:T(8,128)(2,1)S(1)}, u32[]{:S(2)}, u32[]{:S(2)}) collective-permute-start(bf16[80,640]{1,0:T(8,128)(2,1)S(1)} %shard_map.125), channel_id=1, source_target_pairs={{24,0},{0,8},{8,16},{16,24},{25,1},{1,9},{9,17},{17,25},{26,2},{2,... | collective-permute-start | bytes 307208 | tf_op jit(solution)/shard_map/ppermute | solution.py:27

commit v15 on v14

--- a/solution.py
+++ b/solution.py
@@ -149,7 +149,9 @@
     return copies
 
 
-def first_rows_kernel(tokens, routes_far, raw, normed, early, sems, held, routes):
+def first_rows_kernel(
+    tokens, routes_far, gates, raw, normed, early, mask, weight, sems, held, routes
+):
     fetch_routes = pltpu.make_async_copy(routes_far, routes, sems.at[sems.shape[0] - 1])
     fetch_routes.start()
     fetches = start_rows(tokens, held, sems)
@@ -157,6 +159,9 @@
     select = select_of(routes[0])
     for fetch in fetches:
         fetch.wait()
+    mask[...] = select.astype(BF16)
+    gate = slot_gates(select, routes[0], gates[0])
+    weight[...] = jnp.broadcast_to(gate, weight.shape)
     values = pick(select, whole_block(held))
     raw[...] = values.astype(BF16)
     normed[...] = (values * inv_rms_of(values)).astype(BF16)
@@ -166,11 +171,10 @@
 
 
 def update0_kernel(n, *refs):
-    parts, (raw, routes, gates, tokens, next_routes, upd, onward) = refs[:n], refs[n:]
-    select = select_of(routes[0])
+    parts, (raw, mask, weight, tokens, next_routes, upd, onward) = refs[:n], refs[n:]
+    select = mask[...]
     select_next = select_of(next_routes[0])
-    weight = slot_gates(select, routes[0], gates[0])
-    fresh = (raw[...].astype(F32) + weight * summed(parts)).astype(BF16)
+    fresh = (raw[...].astype(F32) + weight[:, :1] * summed(parts)).astype(BF16)
     old = pick(select_next, whole_block(tokens))
     onward[...] = merged(select_next, select, fresh, old)
     upd[...] = fresh
@@ -548,10 +552,16 @@
     cot1_all = shifted(cotangent, "section", -1)
     next_routes = shifted(routes[1:], "section", -1)
 
-    raw0, normed0, early = call(
+    raw0, normed0, early, mask0, weight0 = call(
         first_rows_kernel,
-        [pltpu.VMEM(*one), pltpu.VMEM(*one), ((EARLY * tokens.shape[0], step), BF16)],
-        [tokens, routes],
+        [
+            pltpu.VMEM(*one),
+            pltpu.VMEM(*one),
+            ((EARLY * tokens.shape[0], step), BF16),
+            pltpu.VMEM((PACKED, tokens.shape[0]), BF16),
+            pltpu.VMEM((PACKED, 128), F32),
+        ],
+        [tokens, routes, gates],
         any_args=(0, 1),
         scratch=[
             pltpu.SemaphoreType.DMA((tokens.shape[0] // 16 + 1,)),
@@ -577,7 +587,7 @@
     upd0, h1 = call(
         part(update0_kernel, n),
         [one, one],
-        [*parts, raw0, routes, gates, tokens, next_routes],
+        [*parts, raw0, mask0, weight0, tokens, next_routes],
     )
     h1 = shifted(h1, "section", 1)
     (rest,) = call(

time: 136 us -> 136 us (level)
  waiting for transfers between devices: 53.1 us -> 51.2 us
    ppermute x31, waiting for transfers between devices: 53.1 us -> 51.2 us  [shifted(): lax.ppermute(block, axis, [((i - distance) % size, i) for i in range(size)])]
  transfers between devices with their start and end apart: 31 -> 31, of which waited for: 20 -> 20; matrix products, arithmetic and copies ran while one was open for 0% -> 0% of each run, Pallas kernels for 31% -> 32%
where the time goes in v15:
time: 136 us
  waiting for transfers between devices  51.2 us (38%)
  Pallas kernels  44.5 us (33%)
  starting transfers between devices  37.7 us (28%)
    ppermute x31, waiting for transfers between devices, shifted(): lax.ppermute(block, axis, [((i - distance) % size, i) for i in range(size)])  51.2 us
    ppermute x31, starting transfers between devices, shifted(): lax.ppermute(block, axis, [((i - distance) % size, i) for i in range(size)])  37.7 us
    pallas_call x17, Pallas kernels, call(): pl.pallas_call(kernel, out_shape=outs, in_specs=[anywhere if i in any_arg...  31.1 us
    pallas_call x3, Pallas kernels, chunked_call(): pl.pallas_call(kernel, grid=(steps,), out_shape=[jax.ShapeDtypeStruct(s,...  13.4 us
  transfers between devices with their start and end apart: 31, of which 20 were waited for; matrix products, arithmetic and copies ran while one was open for 0% of the time, Pallas kernels for 32%

profile of v15, /device:TPU:0, one launch (start us, length us, event | category | flops | bytes accessed | tf_op | source)
XLA Modules:
  0.0 135.7 jit_solution(466070394524696920)
XLA Ops:
  0.6 5.1 %collective-permute-start.8 = (bf16[128,5120]{1,0:T(8,128)(2,1)}, bf16[128,5120]{1,0:T(8,128)(2,1)S(1)}, u32[]{:S(2)}, u32[]{:S(2)}) collective-permute-start(bf16[128,5120]{1,0:T(8,128)(2,1)} %param.8), channel_id=1, source_target_pairs={{8,0},{16,8},{24,16},{0,24},{9,1},{17,9},{25,17},{1,25},{10,2},{18... | collective-permute-start | bytes 3932168 | tf_op jit(solution)/shard_map/ppermute | solution.py:27
  5.7 3.5 %shard_map.110 = (bf16[80,640]{1,0:T(8,128)(2,1)S(1)}, bf16[80,640]{1,0:T(8,128)(2,1)S(1)}, bf16[128,640]{1,0:T(8,128)(2,1)}, bf16[80,128]{1,0:T(8,128)(2,1)S(1)}, f32[80,128]{1,0:T(8,128)S(1)}) custom-call(bf16[128,5120]{1,0:T(8,128)(2,1)} %tokens.3, s32[2,4,128]{2,1,0:T(4,128)} %bitcast.8, f32[2,4,128]{2,1,0:T(4,128)} %bitcast.15), custom_call_target="tpu_custom_call" | custom-call | bytes 1024 | tf_op jit(solution)/shard_map/pallas_call | solution.py:40
  9.3 0.6 copy-done.3
  9.9 0.6 copy-done.5
  10.5 1.6 %collective-permute-start.1 = (bf16[80,640]{1,0:T(8,128)(2,1)S(1)}, bf16[80,640]{1,0:T(8,128)(2,1)S(1)}, u32[]{:S(2)}, u32[]{:S(2)}) collective-permute-start(bf16[80,640]{1,0:T(8,128)(2,1)S(1)} %get-tuple-element.48.refs_0_), channel_id=1, source_target_pairs={{4,0},{6,2},{0,4},{2,6},{5,1},{7,3},{1,5},{3,7},{12,8},{14,10},{8,... | collective-permute-start | bytes 307208 | tf_op jit(solution)/shard_map/ppermute | solution.py:27
  12.1 1.4 %collective-permute-start.2 = (bf16[80,640]{1,0:T(8,128)(2,1)S(1)}, bf16[80,640]{1,0:T(8,128)(2,1)S(1)}, u32[]{:S(2)}, u32[]{:S(2)}) collective-permute-start(bf16[80,640]{1,0:T(8,128)(2,1)S(1)} %get-tuple-element.48.refs_0_), channel_id=1, source_target_pairs={{2,0},{4,2},{6,4},{0,6},{3,1},{5,3},{7,5},{1,7},{10,8},{12,10},{14... | collective-permute-start | bytes 307208 | tf_op jit(solution)/shard_map/ppermute | solution.py:27
  13.5 1.6 %collective-permute-done.refs_1_ = bf16[80,640]{1,0:T(8,128)(2,1)S(1)} collective-permute-done((bf16[80,640]{1,0:T(8,128)(2,1)S(1)}, bf16[80,640]{1,0:T(8,128)(2,1)S(1)}, u32[]{:S(2)}, u32[]{:S(2)}) %collective-permute-start) | collective-permute-done | bytes 102432 | tf_op jit(solution)/shard_map/ppermute | solution.py:27
  15.1 1.1 collective-permute-done.1.refs_2_
  16.2 0.7 collective-permute-done.2.refs_3_
  16.9 6.5 %shard_map.111 = (bf16[48,5120]{1,0:T(8,128)(2,1)S(1)}, f32[48,512]{1,0:T(8,128)S(1)}, f32[48,512]{1,0:T(8,128)S(1)}, bf16[48,512]{1,0:T(8,128)(2,1)S(1)}, bf16[...) custom-call(bf16[80,640]{1,0:T(8,128)(2,1)S(1)} %get-tuple-element.4, ...), custom_call_target="tpu_custom_call" | custom-call | bytes 1024 | tf_op jit(solution)/shard_map/pallas_call | solution.py:40
  23.5 2.3 %collective-permute-start.3 = (bf16[80,640]{1,0:T(8,128)(2,1)S(1)}, bf16[80,640]{1,0:T(8,128)(2,1)S(1)}, u32[]{:S(2)}, u32[]{:S(2)}) collective-permute-start(bf16[80,640]{1,0:T(8,128)(2,1)S(1)} %get-tuple-element.50), channel_id=1, source_target_pairs={{2,0},{4,2},{6,4},{0,6},{3,1},{5,3},{7,5},{1,7},{10,8},{12,10},{14... | collective-permute-start | bytes 307208 | tf_op jit(solution)/shard_map/ppermute | solution.py:27
  25.8 0.5 collective-permute-start.4
  26.3 0.5 collective-permute-start.6
  26.8 7.3 %collective-permute-done.6.refs_8_.next_routes = s32[1,4,128]{2,1,0:T(4,128)S(1)} collective-permute-done((s32[1,4,128]{2,1,0:T(4,128)S(1)}, s32[1,4,128]{2,1,0:T(4,128)S(1)}, u32[]{:S(2)}, u32[]{:S(2)}) %collective-permute-start.6) | collective-permute-done | bytes 2080 | tf_op jit(solution)/shard_map/ppermute | solution.py:27
  34.1 1.4 %collective-permute-start.16 = (bf16[128,640]{1,0:T(8,128)(2,1)S(1)}, bf16[128,640]{1,0:T(8,128)(2,1)S(1)}, u32[]{:S(2)}, u32[]{:S(2)}) collective-permute-start(bf16[128,640]{1,0:T(8,128)(2,1)S(1)} %copy-done.7), channel_id=1, source_target_pairs={{16,0},{24,8},{0,16},{8,24},{17,1},{25,9},{1,17},{9,25},{18,2},{26... | collective-permute-start | bytes 491528 | tf_op jit(solution)/shard_map/ppermute | solution.py:27
  35.5 0.7 shard_map.112
  36.2 3.4 %collective-permute-start.7 = (bf16[80,640]{1,0:T(8,128)(2,1)S(1)}, bf16[80,640]{1,0:T(8,128)(2,1)S(1)}, u32[]{:S(2)}, u32[]{:S(2)}) collective-permute-start(bf16[80,640]{1,0:T(8,128)(2,1)S(1)} %get-tuple-element.56), channel_id=1, source_target_pairs={{24,0},{0,8},{8,16},{16,24},{25,1},{1,9},{9,17},{17,25},{26,2},{2,... | collective-permute-start | bytes 307208 | tf_op jit(solution)/shard_map/ppermute | solution.py:27
  39.6 0.5 shard_map.113
  40.2 5.6 %collective-permute-done.16.__3_.early = bf16[128,640]{1,0:T(8,128)(2,1)S(1)} collective-permute-done((bf16[128,640]{1,0:T(8,128)(2,1)S(1)}, bf16[128,640]{1,0:T(8,128)(2,1)S(1)}, u32[]{:S(2)}, u32[]{:S(2)}) %collective-permute-start.16) | collective-permute-done | bytes 163872 | tf_op jit(solution)/shard_map/ppermute | solution.py:27
  45.8 1.3 collective-permute-start.17
  47.1 0.3 shard_map.114.refs_0_
  47.5 1.6 %collective-permute-start.10 = (bf16[160,640]{1,0:T(8,128)(2,1)S(1)}, bf16[160,640]{1,0:T(8,128)(2,1)S(1)}, u32[]{:S(2)}, u32[]{:S(2)}) collective-permute-start(bf16[160,640]{1,0:T(8,128)(2,1)S(1)} %shard_map.114.refs_0_), channel_id=1, source_target_pairs={{4,0},{6,2},{0,4},{2,6},{5,1},{7,3},{1,5},{3,7},{12,8},{14,10},{8,... | collective-permute-start | bytes 614408 | tf_op jit(solution)/shard_map/ppermute | solution.py:27
  49.1 1.4 %collective-permute-start.11 = (bf16[160,640]{1,0:T(8,128)(2,1)S(1)}, bf16[160,640]{1,0:T(8,128)(2,1)S(1)}, u32[]{:S(2)}, u32[]{:S(2)}) collective-permute-start(bf16[160,640]{1,0:T(8,128)(2,1)S(1)} %shard_map.114.refs_0_), channel_id=1, source_target_pairs={{2,0},{4,2},{6,4},{0,6},{3,1},{5,3},{7,5},{1,7},{10,8},{12,10},{14... | collective-permute-start | bytes 614408 | tf_op jit(solution)/shard_map/ppermute | solution.py:27
  50.4 3.8 %collective-permute-done.9.refs_1_ = bf16[160,640]{1,0:T(8,128)(2,1)S(1)} collective-permute-done((bf16[160,640]{1,0:T(8,128)(2,1)S(1)}, bf16[160,640]{1,0:T(8,128)(2,1)S(1)}, u32[]{:S(2)}, u32[]{:S(2)}) %collective-permute-start.9) | collective-permute-done | bytes 204832 | tf_op jit(solution)/shard_map/ppermute | solution.py:27
  54.2 1.2 collective-permute-done.10.refs_2_
  55.4 2.8 %collective-permute-done.11.refs_3_ = bf16[160,640]{1,0:T(8,128)(2,1)S(1)} collective-permute-done((bf16[160,640]{1,0:T(8,128)(2,1)S(1)}, bf16[160,640]{1,0:T(8,128)(2,1)S(1)}, u32[]{:S(2)}, u32[]{:S(2)}) %collective-permute-start.11) | collective-permute-done | bytes 204832 | tf_op jit(solution)/shard_map/ppermute | solution.py:27
  58.3 6.9 %shard_map.115 = (bf16[48,17408]{1,0:T(8,128)(2,1)S(1)}, bf16[80,640]{1,0:T(8,128)(2,1)S(1)}, bf16[80,640]{1,0:T(8,128)(2,1)S(1)}, bf16[80,640]{1,0:T(8,128)(2,1)S(1)}, bf16[80,640]{1,0:T(8,128)(2,1)S(1)}) custom-call(bf16[160,640]{1,0:T(8,128)(2,1)S(1)} %shard_map.114.refs_0_, bf16[160,640]{1,0:T(8,128)(2,1)S(1)} %collective-permute-done.9.refs_1_, ...), custom_call_target="tpu_custom_call" | custom-call | bytes 1024 | tf_op jit(solution)/shard_map/pallas_call | solution.py:40
  65.1 1.6 %collective-permute-start.29 = (bf16[48,17408]{1,0:T(8,128)(2,1)S(1)}, bf16[48,17408]{1,0:T(8,128)(2,1)S(1)}, u32[]{:S(2)}, u32[]{:S(2)}) collective-permute-start(bf16[48,17408]{1,0:T(8,128)(2,1)S(1)} %get-tuple-element.81.act.refs_0_.refs_2_.refs_4_.refs_6_), channel_id=1, source_target_pairs={{1,0},{0,1},{3,2},{2,3},{5,4},{4,5},{7,6},{6,7},{9,8},{8,9},{11,10... | collective-permute-start | bytes 5013512 | tf_op jit(solution)/shard_map/ppermute | solution.py:27
  66.7 1.9 %collective-permute-start.12 = (bf16[80,640]{1,0:T(8,128)(2,1)S(1)}, bf16[80,640]{1,0:T(8,128)(2,1)S(1)}, u32[]{:S(2)}, u32[]{:S(2)}) collective-permute-start(bf16[80,640]{1,0:T(8,128)(2,1)S(1)} %get-tuple-element.64), channel_id=1, source_target_pairs={{2,0},{4,2},{6,4},{0,6},{3,1},{5,3},{7,5},{1,7},{10,8},{12,10},{14... | collective-permute-start | bytes 307208 | tf_op jit(solution)/shard_map/ppermute | solution.py:27
  68.6 0.5 collective-permute-start.13
  69.1 2.4 %collective-permute-done.12.refs_1_ = bf16[80,640]{1,0:T(8,128)(2,1)S(1)} collective-permute-done((bf16[80,640]{1,0:T(8,128)(2,1)S(1)}, bf16[80,640]{1,0:T(8,128)(2,1)S(1)}, u32[]{:S(2)}, u32[]{:S(2)}) %collective-permute-start.12) | collective-permute-done | bytes 102432 | tf_op jit(solution)/shard_map/ppermute | solution.py:27
  71.5 3.0 %collective-permute-done.13.refs_2_ = bf16[80,640]{1,0:T(8,128)(2,1)S(1)} collective-permute-done((bf16[80,640]{1,0:T(8,128)(2,1)S(1)}, bf16[80,640]{1,0:T(8,128)(2,1)S(1)}, u32[]{:S(2)}, u32[]{:S(2)}) %collective-permute-start.13) | collective-permute-done | bytes 102432 | tf_op jit(solution)/shard_map/ppermute | solution.py:27
  74.5 0.4 shard_map.116
  75.0 1.8 %collective-permute-start.15 = (bf16[80,640]{1,0:T(8,128)(2,1)S(1)}, bf16[80,640]{1,0:T(8,128)(2,1)S(1)}, u32[]{:S(2)}, u32[]{:S(2)}) collective-permute-start(bf16[80,640]{1,0:T(8,128)(2,1)S(1)} %shard_map.116), channel_id=1, source_target_pairs={{8,0},{16,8},{24,16},{0,24},{9,1},{17,9},{25,17},{1,25},{10,2},{18... | collective-permute-start | bytes 307208 | tf_op jit(solution)/shard_map/ppermute | solution.py:27
  76.8 0.7 shard_map.118.__0_
  77.5 2.2 %collective-permute-done.15.__2_.upd1.refs_7_ = bf16[80,640]{1,0:T(8,128)(2,1)S(1)} collective-permute-done((bf16[80,640]{1,0:T(8,128)(2,1)S(1)}, bf16[80,640]{1,0:T(8,128)(2,1)S(1)}, u32[]{:S(2)}, u32[]{:S(2)}) %collective-permute-start.15) | collective-permute-done | bytes 102432 | tf_op jit(solution)/shard_map/ppermute | solution.py:27
  79.7 0.4 collective-permute-start.24
  80.1 0.8 shard_map.120
  80.9 0.1 collective-permute-start.18
  81.0 1.6 %collective-permute-start.19 = (bf16[80,640]{1,0:T(8,128)(2,1)S(1)}, bf16[80,640]{1,0:T(8,128)(2,1)S(1)}, u32[]{:S(2)}, u32[]{:S(2)}) collective-permute-start(bf16[80,640]{1,0:T(8,128)(2,1)S(1)} %get-tuple-element.70.refs_0_), channel_id=1, source_target_pairs={{4,0},{6,2},{0,4},{2,6},{5,1},{7,3},{1,5},{3,7},{12,8},{14,10},{8,... | collective-permute-start | bytes 307208 | tf_op jit(solution)/shard_map/ppermute | solution.py:27
  82.6 1.4 %collective-permute-start.20 = (bf16[80,640]{1,0:T(8,128)(2,1)S(1)}, bf16[80,640]{1,0:T(8,128)(2,1)S(1)}, u32[]{:S(2)}, u32[]{:S(2)}) collective-permute-start(bf16[80,640]{1,0:T(8,128)(2,1)S(1)} %get-tuple-element.70.refs_0_), channel_id=1, source_target_pairs={{2,0},{4,2},{6,4},{0,6},{3,1},{5,3},{7,5},{1,7},{10,8},{12,10},{14... | collective-permute-start | bytes 307208 | tf_op jit(solution)/shard_map/ppermute | solution.py:27
  83.9 1.6 %collective-permute-done.18.refs_1_ = bf16[80,640]{1,0:T(8,128)(2,1)S(1)} collective-permute-done((bf16[80,640]{1,0:T(8,128)(2,1)S(1)}, bf16[80,640]{1,0:T(8,128)(2,1)S(1)}, u32[]{:S(2)}, u32[]{:S(2)}) %collective-permute-start.18) | collective-permute-done | bytes 102432 | tf_op jit(solution)/shard_map/ppermute | solution.py:27
  85.5 1.2 collective-permute-done.19.refs_2_
  86.7 0.6 collective-permute-done.20.refs_3_
  87.4 5.0 %shard_map.121 = (bf16[48,6144]{1,0:T(8,128)(2,1)S(1)}, bf16[80,640]{1,0:T(8,128)(2,1)S(1)}, bf16[80,640]{1,0:T(8,128)(2,1)S(1)}, bf16[80,640]{1,0:T(8,128)(2,1)S(1)}, bf16[80,640]{1,0:T(8,128)(2,1)S(1)}) custom-call(bf16[80,640]{1,0:T(8,128)(2,1)S(1)} %get-tuple-element.70.refs_0_, bf16[80,640]{1,0:T(8,128)(2,1)S(1)} %collective-permute-done.18.refs_1_, ...), custom_call_target="tpu_custom_call" | custom-call | bytes 1024 | tf_op jit(solution)/shard_map/pallas_call | solution.py:40
  92.4 1.6 %collective-permute-start.30 = (bf16[48,6144]{1,0:T(8,128)(2,1)S(1)}, bf16[48,6144]{1,0:T(8,128)(2,1)S(1)}, u32[]{:S(2)}, u32[]{:S(2)}) collective-permute-start(bf16[48,6144]{1,0:T(8,128)(2,1)S(1)} %get-tuple-element.82._.refs_0_.refs_2_), channel_id=1, source_target_pairs={{1,0},{0,1},{3,2},{2,3},{5,4},{4,5},{7,6},{6,7},{9,8},{8,9},{11,10... | collective-permute-start | bytes 1769480 | tf_op jit(solution)/shard_map/ppermute | solution.py:27
  94.0 1.9 %collective-permute-start.21 = (bf16[80,640]{1,0:T(8,128)(2,1)S(1)}, bf16[80,640]{1,0:T(8,128)(2,1)S(1)}, u32[]{:S(2)}, u32[]{:S(2)}) collective-permute-start(bf16[80,640]{1,0:T(8,128)(2,1)S(1)} %get-tuple-element.74), channel_id=1, source_target_pairs={{2,0},{4,2},{6,4},{0,6},{3,1},{5,3},{7,5},{1,7},{10,8},{12,10},{14... | collective-permute-start | bytes 307208 | tf_op jit(solution)/shard_map/ppermute | solution.py:27
  95.9 1.1 shard_map.124
  97.1 1.1 collective-permute-done.21.refs_1_
  98.2 0.5 collective-permute-start.26
  98.7 0.6 collective-permute-done.25.refs_1_
  99.3 1.1 collective-permute-start.27
  100.4 3.5 %collective-permute-done.26.refs_2_ = bf16[80,640]{1,0:T(8,128)(2,1)S(1)} collective-permute-done((bf16[80,640]{1,0:T(8,128)(2,1)S(1)}, bf16[80,640]{1,0:T(8,128)(2,1)S(1)}, u32[]{:S(2)}, u32[]{:S(2)}) %collective-permute-start.26) | collective-permute-done | bytes 102432 | tf_op jit(solution)/shard_map/ppermute | solution.py:27
  103.9 1.1 collective-permute-done.27.refs_3_
  105.0 0.2 shard_map.125
  105.3 4.3 %collective-permute-done.22.refs_2_ = bf16[80,640]{1,0:T(8,128)(2,1)S(1)} collective-permute-done((bf16[80,640]{1,0:T(8,128)(2,1)S(1)}, bf16[80,640]{1,0:T(8,128)(2,1)S(1)}, u32[]{:S(2)}, u32[]{:S(2)}) %collective-permute-start.22) | collective-permute-done | bytes 102432 | tf_op jit(solution)/shard_map/ppermute | solution.py:27
  109.6 2.7 %collective-permute-start.28 = (bf16[80,640]{1,0:T(8,128)(2,1)S(1)}, bf16[80,640]{1,0:T(8,128)(2,1)S(1)}, u32[]{:S(2)}, u32[]{:S(2)}) collective-permute-start(bf16[80,640]{1,0:T(8,128)(2,1)S(1)} %shard_map.125), channel_id=1, source_target_pairs={{24,0},{0,8},{8,16},{16,24},{25,1},{1,9},{9,17},{17,25},{26,2},{2,... | collective-permute-start | bytes 307208 | tf_op jit(solution)/shard_map/ppermute | solution.py:27
  112.3 2.4 %shard_map.122 = bf16[128,5120]{1,0:T(8,128)(2,1)} custom-call(bf16[80,640]{1,0:T(8,128)(2,1)S(1)} %get-tuple-element.73.refs_0_, bf16[80,640]{1,0:T(8,128)(2,1)S(1)} %collective-permute-done.21.refs_1_, bf16[80,640]{1,0:T(8,128)(2,1)S(1)} %collective-permute-done.22.refs_2_, bf16[80,640]{1,0:T(8,128)(2,1)S(1)} %collective-permute-done.23.refs_3_, ...), custom_call_target="tpu_custom_call" | custom-call | bytes 1024 | tf_op jit(solution)/shard_map/pallas_call | solution.py:40
  114.7 3.1 %shard_map.127 = (bf16[5120,192]{1,0:T(8,128)(2,1)S(1)}, bf16[512,192]{1,0:T(8,128)(2,1)S(1)}) custom-call(bf16[48,17408]{1,0:T(8,128)(2,1)S(1)} %get-tuple-element.81.act.refs_0_.refs_2_.refs_4_.refs_6_, bf16[48,17408]{1,0:T(8,128)(2,1)S(1)} %collective-permute-done.29.refs_1_.refs_3_.refs_5_.refs_7_, ...), custom_call_target="tpu_custom_call" | custom-call | bytes 1024 | tf_op jit(solution)/shard_map/pallas_call | solution.py:461
  117.8 6.2 %shard_map.128 = (bf16[5120,512]{1,0:T(8,128)(2,1)}, bf16[5120,512]{1,0:T(8,128)(2,1)}) custom-call(bf16[5120,192]{1,0:T(8,128)(2,1)S(1)} %get-tuple-element.87.x_t, bf16[48,6144]{1,0:T(8,128)(2,1)S(1)} %get-tuple-element.82._.refs_0_.refs_2_, bf16[48,6144]{1,0:T(8,128)(2,1)S(1)} %collective-permute-done.30.refs_1_.refs_3_, ...), custom_call_target="tpu_custom_call" | custom-call | bytes 1024 | tf_op jit(solution)/shard_map/pallas_call | solution.py:461
  124.1 4.1 %shard_map.129 = bf16[512,5120]{1,0:T(8,128)(2,1)} custom-call(bf16[512,192]{1,0:T(8,128)(2,1)S(1)} %get-tuple-element.90.act_t, bf16[48,6144]{1,0:T(8,128)(2,1)S(1)} %get-tuple-element.82._.refs_0_.refs_2_, bf16[48,6144]{1,0:T(8,128)(2,1)S(1)} %collective-permute-done.30.refs_1_.refs_3_, ...), custom_call_target="tpu_custom_call" | custom-call | bytes 1024 | tf_op jit(solution)/shard_map/pallas_call | solution.py:461
  128.2 5.4 %collective-permute-done.24.rest = bf16[912,640]{1,0:T(8,128)(2,1)S(1)} collective-permute-done((bf16[912,640]{1,0:T(8,128)(2,1)S(1)}, bf16[912,640]{1,0:T(8,128)(2,1)S(1)}, u32[]{:S(2)}, u32[]{:S(2)}) %collective-permute-start.24) | collective-permute-done | bytes 1167392 | tf_op jit(solution)/shard_map/ppermute | solution.py:27
  133.6 0.5 shard_map.123
  134.1 1.4 %shard_map.126 = bf16[128,5120]{1,0:T(8,128)(2,1)} custom-call(bf16[128,5120]{1,0:T(8,128)(2,1)S(1)} %get-tuple-element.78.base, f32[128,80]{1,0:T(8,128)S(1)} %get-tuple-element.79.turned_select, f32[128,128]{1,0:T(8,128)S(1)} %get-tuple-element.80.hit, bf16[80,640]{1,0:T(8,128)(2,1)S(1)} %collective-permute-done.28.upd1), custom_call_target="tpu_custom_call" | custom-call | bytes 1024 | tf_op jit(solution)/shard_map/pallas_call | solution.py:40
  (35 shorter events, 0.2 us)
Async XLA Ops:
  0.6 39.0 %collective-permute-start.8 = (bf16[128,5120]{1,0:T(8,128)(2,1)}, bf16[128,5120]{1,0:T(8,128)(2,1)S(1)}, u32[]{:S(2)}, u32[]{:S(2)}) collective-permute-start(bf16[128,5120]{1,0:T(8,128)(2,1)} %param.8), channel_id=1, source_target_pairs={{8,0},{16,8},{24,16},{0,24},{9,1},{17,9},{25,17},{1,25},{10,2},{18... | collective-permute-start | bytes 3932168 | tf_op jit(solution)/shard_map/ppermute | solution.py:27
  9.3 0.6 copy-start.3
  9.9 0.6 copy-start.5
  10.5 4.6 %collective-permute-start = (bf16[80,640]{1,0:T(8,128)(2,1)S(1)}, bf16[80,640]{1,0:T(8,128)(2,1)S(1)}, u32[]{:S(2)}, u32[]{:S(2)}) collective-permute-start(bf16[80,640]{1,0:T(8,128)(2,1)S(1)} %get-tuple-element.48.refs_0_), channel_id=1, source_target_pairs={{6,0},{0,2},{2,4},{4,6},{7,1},{1,3},{3,5},{5,7},{14,8},{8,10},{10,... | collective-permute-start | bytes 307208 | tf_op jit(solution)/shard_map/ppermute | solution.py:27
  10.5 5.7 %collective-permute-start.1 = (bf16[80,640]{1,0:T(8,128)(2,1)S(1)}, bf16[80,640]{1,0:T(8,128)(2,1)S(1)}, u32[]{:S(2)}, u32[]{:S(2)}) collective-permute-start(bf16[80,640]{1,0:T(8,128)(2,1)S(1)} %get-tuple-element.48.refs_0_), channel_id=1, source_target_pairs={{4,0},{6,2},{0,4},{2,6},{5,1},{7,3},{1,5},{3,7},{12,8},{14,10},{8,... | collective-permute-start | bytes 307208 | tf_op jit(solution)/shard_map/ppermute | solution.py:27
  12.1 4.9 %collective-permute-start.2 = (bf16[80,640]{1,0:T(8,128)(2,1)S(1)}, bf16[80,640]{1,0:T(8,128)(2,1)S(1)}, u32[]{:S(2)}, u32[]{:S(2)}) collective-permute-start(bf16[80,640]{1,0:T(8,128)(2,1)S(1)} %get-tuple-element.48.refs_0_), channel_id=1, source_target_pairs={{2,0},{4,2},{6,4},{0,6},{3,1},{5,3},{7,5},{1,7},{10,8},{12,10},{14... | collective-permute-start | bytes 307208 | tf_op jit(solution)/shard_map/ppermute | solution.py:27
  16.9 9.4 %copy-start.1 = (s32[2,128,4]{1,2,0:T(4,128)S(1)}, s32[2,128,4]{1,2,0:T(4,128)}, u32[]{:S(2)}) copy-start(s32[2,128,4]{1,2,0:T(4,128)} %param.12) | copy-start | bytes 12292
  16.9 17.2 %copy-start.7 = (bf16[128,640]{1,0:T(8,128)(2,1)S(1)}, bf16[128,640]{1,0:T(8,128)(2,1)}, u32[]{:S(2)}) copy-start(bf16[128,640]{1,0:T(8,128)(2,1)} %get-tuple-element.68) | copy-start | bytes 491524
  16.9 18.6 %copy-start = (bf16[128,5120]{1,0:T(8,128)(2,1)S(1)}, bf16[128,5120]{1,0:T(8,128)(2,1)}, u32[]{:S(2)}) copy-start(bf16[128,5120]{1,0:T(8,128)(2,1)} %tokens.3) | copy-start | bytes 3932164
  16.9 18.6 %copy-start.4 = (f32[80,128]{1,0:T(8,128)S(1)}, f32[80,128]{1,0:T(8,128)}, u32[]{:S(2)}) copy-start(f32[80,128]{1,0:T(8,128)} %copy-done.3) | copy-start | bytes 122884
  16.9 18.6 %copy-start.6 = (bf16[80,128]{1,0:T(8,128)(2,1)S(1)}, bf16[80,128]{1,0:T(8,128)(2,1)}, u32[]{:S(2)}) copy-start(bf16[80,128]{1,0:T(8,128)(2,1)} %copy-done.5) | copy-start | bytes 61444
  23.5 16.1 %copy-start.2 = (f32[2,128,4]{1,2,0:T(4,128)S(1)}, f32[2,128,4]{1,2,0:T(4,128)}, u32[]{:S(2)}) copy-start(f32[2,128,4]{1,2,0:T(4,128)} %param.13) | copy-start | bytes 12292
  23.5 12.0 %collective-permute-start.3 = (bf16[80,640]{1,0:T(8,128)(2,1)S(1)}, bf16[80,640]{1,0:T(8,128)(2,1)S(1)}, u32[]{:S(2)}, u32[]{:S(2)}) collective-permute-start(bf16[80,640]{1,0:T(8,128)(2,1)S(1)} %get-tuple-element.50), channel_id=1, source_target_pairs={{2,0},{4,2},{6,4},{0,6},{3,1},{5,3},{7,5},{1,7},{10,8},{12,10},{14... | collective-permute-start | bytes 307208 | tf_op jit(solution)/shard_map/ppermute | solution.py:27
  25.8 9.7 %collective-permute-start.4 = (bf16[80,640]{1,0:T(8,128)(2,1)S(1)}, bf16[80,640]{1,0:T(8,128)(2,1)S(1)}, u32[]{:S(2)}, u32[]{:S(2)}) collective-permute-start(bf16[80,640]{1,0:T(8,128)(2,1)S(1)} %get-tuple-element.51), channel_id=1, source_target_pairs={{4,0},{6,2},{0,4},{2,6},{5,1},{7,3},{1,5},{3,7},{12,8},{14,10},{8,... | collective-permute-start | bytes 307208 | tf_op jit(solution)/shard_map/ppermute | solution.py:27
  26.3 9.2 %collective-permute-start.5 = (bf16[80,640]{1,0:T(8,128)(2,1)S(1)}, bf16[80,640]{1,0:T(8,128)(2,1)S(1)}, u32[]{:S(2)}, u32[]{:S(2)}) collective-permute-start(bf16[80,640]{1,0:T(8,128)(2,1)S(1)} %get-tuple-element.52), channel_id=1, source_target_pairs={{6,0},{0,2},{2,4},{4,6},{7,1},{1,3},{3,5},{5,7},{14,8},{8,10},{10,... | collective-permute-start | bytes 307208 | tf_op jit(solution)/shard_map/ppermute | solution.py:27
  26.3 7.8 %collective-permute-start.6 = (s32[1,4,128]{2,1,0:T(4,128)S(1)}, s32[1,4,128]{2,1,0:T(4,128)S(1)}, u32[]{:S(2)}, u32[]{:S(2)}) collective-permute-start(s32[1,4,128]{2,1,0:T(4,128)S(1)} %slice.4), channel_id=1, source_target_pairs={{8,0},{16,8},{24,16},{0,24},{9,1},{17,9},{25,17},{1,25},{10,2},{18... | collective-permute-start | bytes 6152 | tf_op jit(solution)/shard_map/ppermute | solution.py:27
  34.1 11.7 %collective-permute-start.16 = (bf16[128,640]{1,0:T(8,128)(2,1)S(1)}, bf16[128,640]{1,0:T(8,128)(2,1)S(1)}, u32[]{:S(2)}, u32[]{:S(2)}) collective-permute-start(bf16[128,640]{1,0:T(8,128)(2,1)S(1)} %copy-done.7), channel_id=1, source_target_pairs={{16,0},{24,8},{0,16},{8,24},{17,1},{25,9},{1,17},{9,25},{18,2},{26... | collective-permute-start | bytes 491528 | tf_op jit(solution)/shard_map/ppermute | solution.py:27
  36.2 9.6 %collective-permute-start.7 = (bf16[80,640]{1,0:T(8,128)(2,1)S(1)}, bf16[80,640]{1,0:T(8,128)(2,1)S(1)}, u32[]{:S(2)}, u32[]{:S(2)}) collective-permute-start(bf16[80,640]{1,0:T(8,128)(2,1)S(1)} %get-tuple-element.56), channel_id=1, source_target_pairs={{24,0},{0,8},{8,16},{16,24},{25,1},{1,9},{9,17},{17,25},{26,2},{2,... | collective-permute-start | bytes 307208 | tf_op jit(solution)/shard_map/ppermute | solution.py:27
  45.8 33.9 %collective-permute-start.17 = (bf16[128,5120]{1,0:T(8,128)(2,1)S(1)}, bf16[128,5120]{1,0:T(8,128)(2,1)S(1)}, u32[]{:S(2)}, u32[]{:S(2)}) collective-permute-start(bf16[128,5120]{1,0:T(8,128)(2,1)S(1)} %shard_map.117), channel_id=1, source_target_pairs={{8,0},{16,8},{24,16},{0,24},{9,1},{17,9},{25,17},{1,25},{10,2},{18... | collective-permute-start | bytes 3932168 | tf_op jit(solution)/shard_map/ppermute | solution.py:27
  47.4 6.8 %collective-permute-start.9 = (bf16[160,640]{1,0:T(8,128)(2,1)S(1)}, bf16[160,640]{1,0:T(8,128)(2,1)S(1)}, u32[]{:S(2)}, u32[]{:S(2)}) collective-permute-start(bf16[160,640]{1,0:T(8,128)(2,1)S(1)} %shard_map.114.refs_0_), channel_id=1, source_target_pairs={{6,0},{0,2},{2,4},{4,6},{7,1},{1,3},{3,5},{5,7},{14,8},{8,10},{10,... | collective-permute-start | bytes 614408 | tf_op jit(solution)/shard_map/ppermute | solution.py:27
  47.5 8.0 %collective-permute-start.10 = (bf16[160,640]{1,0:T(8,128)(2,1)S(1)}, bf16[160,640]{1,0:T(8,128)(2,1)S(1)}, u32[]{:S(2)}, u32[]{:S(2)}) collective-permute-start(bf16[160,640]{1,0:T(8,128)(2,1)S(1)} %shard_map.114.refs_0_), channel_id=1, source_target_pairs={{4,0},{6,2},{0,4},{2,6},{5,1},{7,3},{1,5},{3,7},{12,8},{14,10},{8,... | collective-permute-start | bytes 614408 | tf_op jit(solution)/shard_map/ppermute | solution.py:27
  49.1 9.2 %collective-permute-start.11 = (bf16[160,640]{1,0:T(8,128)(2,1)S(1)}, bf16[160,640]{1,0:T(8,128)(2,1)S(1)}, u32[]{:S(2)}, u32[]{:S(2)}) collective-permute-start(bf16[160,640]{1,0:T(8,128)(2,1)S(1)} %shard_map.114.refs_0_), channel_id=1, source_target_pairs={{2,0},{4,2},{6,4},{0,6},{3,1},{5,3},{7,5},{1,7},{10,8},{12,10},{14... | collective-permute-start | bytes 614408 | tf_op jit(solution)/shard_map/ppermute | solution.py:27
  65.1 49.6 %collective-permute-start.29 = (bf16[48,17408]{1,0:T(8,128)(2,1)S(1)}, bf16[48,17408]{1,0:T(8,128)(2,1)S(1)}, u32[]{:S(2)}, u32[]{:S(2)}) collective-permute-start(bf16[48,17408]{1,0:T(8,128)(2,1)S(1)} %get-tuple-element.81.act.refs_0_.refs_2_.refs_4_.refs_6_), channel_id=1, source_target_pairs={{1,0},{0,1},{3,2},{2,3},{5,4},{4,5},{7,6},{6,7},{9,8},{8,9},{11,10... | collective-permute-start | bytes 5013512 | tf_op jit(solution)/shard_map/ppermute | solution.py:27
  66.7 4.8 %collective-permute-start.12 = (bf16[80,640]{1,0:T(8,128)(2,1)S(1)}, bf16[80,640]{1,0:T(8,128)(2,1)S(1)}, u32[]{:S(2)}, u32[]{:S(2)}) collective-permute-start(bf16[80,640]{1,0:T(8,128)(2,1)S(1)} %get-tuple-element.64), channel_id=1, source_target_pairs={{2,0},{4,2},{6,4},{0,6},{3,1},{5,3},{7,5},{1,7},{10,8},{12,10},{14... | collective-permute-start | bytes 307208 | tf_op jit(solution)/shard_map/ppermute | solution.py:27
  68.6 5.9 %collective-permute-start.13 = (bf16[80,640]{1,0:T(8,128)(2,1)S(1)}, bf16[80,640]{1,0:T(8,128)(2,1)S(1)}, u32[]{:S(2)}, u32[]{:S(2)}) collective-permute-start(bf16[80,640]{1,0:T(8,128)(2,1)S(1)} %get-tuple-element.65), channel_id=1, source_target_pairs={{4,0},{6,2},{0,4},{2,6},{5,1},{7,3},{1,5},{3,7},{12,8},{14,10},{8,... | collective-permute-start | bytes 307208 | tf_op jit(solution)/shard_map/ppermute | solution.py:27
  69.1 5.4 %collective-permute-start.14 = (bf16[80,640]{1,0:T(8,128)(2,1)S(1)}, bf16[80,640]{1,0:T(8,128)(2,1)S(1)}, u32[]{:S(2)}, u32[]{:S(2)}) collective-permute-start(bf16[80,640]{1,0:T(8,128)(2,1)S(1)} %get-tuple-element.66), channel_id=1, source_target_pairs={{6,0},{0,2},{2,4},{4,6},{7,1},{1,3},{3,5},{5,7},{14,8},{8,10},{10,... | collective-permute-start | bytes 307208 | tf_op jit(solution)/shard_map/ppermute | solution.py:27
  75.0 4.7 %collective-permute-start.15 = (bf16[80,640]{1,0:T(8,128)(2,1)S(1)}, bf16[80,640]{1,0:T(8,128)(2,1)S(1)}, u32[]{:S(2)}, u32[]{:S(2)}) collective-permute-start(bf16[80,640]{1,0:T(8,128)(2,1)S(1)} %shard_map.116), channel_id=1, source_target_pairs={{8,0},{16,8},{24,16},{0,24},{9,1},{17,9},{25,17},{1,25},{10,2},{18... | collective-permute-start | bytes 307208 | tf_op jit(solution)/shard_map/ppermute | solution.py:27
  79.7 53.9 %collective-permute-start.24 = (bf16[912,640]{1,0:T(8,128)(2,1)S(1)}, bf16[912,640]{1,0:T(8,128)(2,1)S(1)}, u32[]{:S(2)}, u32[]{:S(2)}) collective-permute-start(bf16[912,640]{1,0:T(8,128)(2,1)S(1)} %shard_map.119._), channel_id=1, source_target_pairs={{16,0},{24,8},{0,16},{8,24},{17,1},{25,9},{1,17},{9,25},{18,2},{26... | collective-permute-start | bytes 3502088 | tf_op jit(solution)/shard_map/ppermute | solution.py:27
  80.9 4.6 %collective-permute-start.18 = (bf16[80,640]{1,0:T(8,128)(2,1)S(1)}, bf16[80,640]{1,0:T(8,128)(2,1)S(1)}, u32[]{:S(2)}, u32[]{:S(2)}) collective-permute-start(bf16[80,640]{1,0:T(8,128)(2,1)S(1)} %get-tuple-element.70.refs_0_), channel_id=1, source_target_pairs={{6,0},{0,2},{2,4},{4,6},{7,1},{1,3},{3,5},{5,7},{14,8},{8,10},{10,... | collective-permute-start | bytes 307208 | tf_op jit(solution)/shard_map/ppermute | solution.py:27
  81.0 5.8 %collective-permute-start.19 = (bf16[80,640]{1,0:T(8,128)(2,1)S(1)}, bf16[80,640]{1,0:T(8,128)(2,1)S(1)}, u32[]{:S(2)}, u32[]{:S(2)}) collective-permute-start(bf16[80,640]{1,0:T(8,128)(2,1)S(1)} %get-tuple-element.70.refs_0_), channel_id=1, source_target_pairs={{4,0},{6,2},{0,4},{2,6},{5,1},{7,3},{1,5},{3,7},{12,8},{14,10},{8,... | collective-permute-start | bytes 307208 | tf_op jit(solution)/shard_map/ppermute | solution.py:27
  82.6 4.8 %collective-permute-start.20 = (bf16[80,640]{1,0:T(8,128)(2,1)S(1)}, bf16[80,640]{1,0:T(8,128)(2,1)S(1)}, u32[]{:S(2)}, u32[]{:S(2)}) collective-permute-start(bf16[80,640]{1,0:T(8,128)(2,1)S(1)} %get-tuple-element.70.refs_0_), channel_id=1, source_target_pairs={{2,0},{4,2},{6,4},{0,6},{3,1},{5,3},{7,5},{1,7},{10,8},{12,10},{14... | collective-permute-start | bytes 307208 | tf_op jit(solution)/shard_map/ppermute | solution.py:27
  92.4 25.4 %collective-permute-start.30 = (bf16[48,6144]{1,0:T(8,128)(2,1)S(1)}, bf16[48,6144]{1,0:T(8,128)(2,1)S(1)}, u32[]{:S(2)}, u32[]{:S(2)}) collective-permute-start(bf16[48,6144]{1,0:T(8,128)(2,1)S(1)} %get-tuple-element.82._.refs_0_.refs_2_), channel_id=1, source_target_pairs={{1,0},{0,1},{3,2},{2,3},{5,4},{4,5},{7,6},{6,7},{9,8},{8,9},{11,10... | collective-permute-start | bytes 1769480 | tf_op jit(solution)/shard_map/ppermute | solution.py:27
  94.0 4.2 %collective-permute-start.21 = (bf16[80,640]{1,0:T(8,128)(2,1)S(1)}, bf16[80,640]{1,0:T(8,128)(2,1)S(1)}, u32[]{:S(2)}, u32[]{:S(2)}) collective-permute-start(bf16[80,640]{1,0:T(8,128)(2,1)S(1)} %get-tuple-element.74), channel_id=1, source_target_pairs={{2,0},{4,2},{6,4},{0,6},{3,1},{5,3},{7,5},{1,7},{10,8},{12,10},{14... | collective-permute-start | bytes 307208 | tf_op jit(solution)/shard_map/ppermute | solution.py:27
  97.0 2.3 %collective-permute-start.25 = (bf16[80,640]{1,0:T(8,128)(2,1)S(1)}, bf16[80,640]{1,0:T(8,128)(2,1)S(1)}, u32[]{:S(2)}, u32[]{:S(2)}) collective-permute-start(bf16[80,640]{1,0:T(8,128)(2,1)S(1)} %get-tuple-element.84), channel_id=1, source_target_pairs={{2,0},{4,2},{6,4},{0,6},{3,1},{5,3},{7,5},{1,7},{10,8},{12,10},{14... | collective-permute-start | bytes 307208 | tf_op jit(solution)/shard_map/ppermute | solution.py:27
  98.2 5.7 %collective-permute-start.26 = (bf16[80,640]{1,0:T(8,128)(2,1)S(1)}, bf16[80,640]{1,0:T(8,128)(2,1)S(1)}, u32[]{:S(2)}, u32[]{:S(2)}) collective-permute-start(bf16[80,640]{1,0:T(8,128)(2,1)S(1)} %get-tuple-element.85), channel_id=1, source_target_pairs={{4,0},{6,2},{0,4},{2,6},{5,1},{7,3},{1,5},{3,7},{12,8},{14,10},{8,... | collective-permute-start | bytes 307208 | tf_op jit(solution)/shard_map/ppermute | solution.py:27
  99.3 5.7 %collective-permute-start.27 = (bf16[80,640]{1,0:T(8,128)(2,1)S(1)}, bf16[80,640]{1,0:T(8,128)(2,1)S(1)}, u32[]{:S(2)}, u32[]{:S(2)}) collective-permute-start(bf16[80,640]{1,0:T(8,128)(2,1)S(1)} %get-tuple-element.86), channel_id=1, source_target_pairs={{6,0},{0,2},{2,4},{4,6},{7,1},{1,3},{3,5},{5,7},{14,8},{8,10},{10,... | collective-permute-start | bytes 307208 | tf_op jit(solution)/shard_map/ppermute | solution.py:27
  103.9 5.7 %collective-permute-start.22 = (bf16[80,640]{1,0:T(8,128)(2,1)S(1)}, bf16[80,640]{1,0:T(8,128)(2,1)S(1)}, u32[]{:S(2)}, u32[]{:S(2)}) collective-permute-start(bf16[80,640]{1,0:T(8,128)(2,1)S(1)} %get-tuple-element.75), channel_id=1, source_target_pairs={{4,0},{6,2},{0,4},{2,6},{5,1},{7,3},{1,5},{3,7},{12,8},{14,10},{8,... | collective-permute-start | bytes 307208 | tf_op jit(solution)/shard_map/ppermute | solution.py:27
  105.0 7.3 %collective-permute-start.23 = (bf16[80,640]{1,0:T(8,128)(2,1)S(1)}, bf16[80,640]{1,0:T(8,128)(2,1)S(1)}, u32[]{:S(2)}, u32[]{:S(2)}) collective-permute-start(bf16[80,640]{1,0:T(8,128)(2,1)S(1)} %get-tuple-element.76), channel_id=1, source_target_pairs={{6,0},{0,2},{2,4},{4,6},{7,1},{1,3},{3,5},{5,7},{14,8},{8,10},{10,... | collective-permute-start | bytes 307208 | tf_op jit(solution)/shard_map/ppermute | solution.py:27
  109.6 24.5 %collective-permute-start.28 = (bf16[80,640]{1,0:T(8,128)(2,1)S(1)}, bf16[80,640]{1,0:T(8,128)(2,1)S(1)}, u32[]{:S(2)}, u32[]{:S(2)}) collective-permute-start(bf16[80,640]{1,0:T(8,128)(2,1)S(1)} %shard_map.125), channel_id=1, source_target_pairs={{24,0},{0,8},{8,16},{16,24},{25,1},{1,9},{9,17},{17,25},{26,2},{2,... | collective-permute-start | bytes 307208 | tf_op jit(solution)/shard_map/ppermute | solution.py:27
